TPU v7x, 32 devices: a whole 2x2x4 slice. The times are simulated.
32 devices in a mesh: grp: 4 (over x, core), fsdp: 8 (over z, y).
Axes of the slice: x: 2, y: 2, z: 4, core: 2. Of those that a mesh axis runs over, the one named last changes fastest.
Arguments:
- caption_states: bfloat16 [8, 128, 4096], P('fsdp'), may hold values from -6 to 6
- caption_lens: int32 [8], replicated, may hold values from 4 to 128
- text_gain: float32 [4096], replicated, may hold values from 0.25 to 1.75
- text_query: bfloat16 [4096, 2048], P(None, 'grp'), may hold values from -0.01171875 to 0.01171875
- text_key: bfloat16 [4096, 2048], P(None, 'grp'), may hold values from -0.09375 to 0.09375
- text_value: bfloat16 [4096, 2048], P(None, 'grp'), may hold values from -0.09375 to 0.09375
- text_bias: float32 [32, 128, 128], P('grp'), may hold values from -4 to 4
- text_out: bfloat16 [2048, 4096], P('grp'), may hold values from -0.125 to 0.125
- final_gain: float32 [4096], replicated, may hold values from 0.25 to 1.75
- cross_key: bfloat16 [4096, 1536], P('fsdp', 'grp'), may hold values from -0.09375 to 0.09375
- cross_value: bfloat16 [4096, 1536], P('fsdp', 'grp'), may hold values from -0.09375 to 0.09375
- video_states: bfloat16 [2048, 3072], P('fsdp'), may hold values from -6 to 6
- video_counts: int32 [8], replicated, may hold values from 128 to 1024, as said below
- sample_caption: int32 [8], replicated, may hold values from 0 to 7, each once
- cross_query: bfloat16 [3072, 1536], P('fsdp', 'grp'), may hold values from -0.109375 to 0.109375
- cross_out: bfloat16 [1536, 3072], P('grp', 'fsdp'), may hold values from -0.15625 to 0.15625
- out_grad: bfloat16 [2048, 3072], P('fsdp'), may hold values from -6 to 6
Outputs:
- updated: bfloat16 [2048, 3072], P('fsdp', 'grp')
- input_grad: bfloat16 [2048, 3072], P('fsdp', 'grp')
- query_grad: float32 [3072, 1536], P('fsdp', 'grp')
- out_weight_grad: float32 [1536, 3072], P('grp', 'fsdp')
- key_grad: bfloat16 [8, 128, 1536], P('fsdp', None, 'grp')
- value_grad: bfloat16 [8, 128, 1536], P('fsdp', None, 'grp')
Inputs may be any that keep to these rules, and one draw needn't show every extreme that they name: `video_counts`: counts of the samples in order, summing to 2048. `sample_caption`: each caption belongs to exactly one sample.
All inputs are finite; a program needn't handle non-finite values.
Results may differ from a plain program's by a relative error of at most 0.04.
Values may be sent and summed in bfloat16 or wider, within the bound.
No kernel may reach another device: no remote copies, remote signals or barrier semaphores. Data moves between devices by JAX's collectives and lax.ppermute only.
A program may use at most 128 MiB of HBM per device.

v0:
```python
import math

import jax
import jax.numpy as jnp
from jax import lax
from jax.sharding import PartitionSpec as P

HEAD_SIZE = 128


def rms_scale(values, gain):
    mean_square = jnp.mean(values * values, axis=-1, keepdims=True)
    return values * lax.rsqrt(mean_square + 1e-06) * gain


def contract_last(left, right):
    return lax.dot_general(
        left, right, (((1,), (1,)), ((), ())), preferred_element_type=jnp.float32
    )


def contract_first(left, right):
    return lax.dot_general(
        left, right, (((0,), (0,)), ((), ())), preferred_element_type=jnp.float32
    )


def local(
    caption_states,
    caption_lens,
    text_gain,
    text_query,
    text_key,
    text_value,
    text_bias,
    text_out,
    final_gain,
    cross_key,
    cross_value,
    video_states,
    video_counts,
    sample_caption,
    cross_query,
    cross_out,
    out_grad,
):
    column = lax.axis_index("fsdp")
    caps_local, cap_len, text_width = caption_states.shape
    local_lens = lax.dynamic_slice_in_dim(caption_lens, column * caps_local, caps_local)
    flat_states = caption_states.reshape(caps_local * cap_len, text_width).astype(jnp.float32)
    text_normed = rms_scale(flat_states, text_gain).astype(jnp.bfloat16)
    local_heads = text_bias.shape[0]
    head_width = text_query.shape[1] // local_heads

    def heads_of(weight):
        product = jnp.dot(text_normed, weight, preferred_element_type=jnp.float32).astype(
            jnp.bfloat16
        )
        return product.reshape(caps_local, cap_len, local_heads, head_width)

    text_queries = heads_of(text_query)
    text_keys = heads_of(text_key)
    text_values = heads_of(text_value)
    text_scores = (
        jnp.einsum("cihd,cjhd->chij", text_queries, text_keys, preferred_element_type=jnp.float32)
        + text_bias[None]
    )
    key_valid = jnp.arange(cap_len, dtype=jnp.int32)[None, :] < local_lens[:, None]
    exp_scores = jnp.where(key_valid[:, None, None, :], jnp.exp(text_scores), 0.0)
    text_weights = (exp_scores / jnp.sum(exp_scores, axis=-1, keepdims=True)).astype(jnp.bfloat16)
    text_mixed = jnp.einsum(
        "chij,cjhd->cihd", text_weights, text_values, preferred_element_type=jnp.float32
    )
    text_mixed = text_mixed.astype(jnp.bfloat16).reshape(
        caps_local * cap_len, local_heads * head_width
    )
    partial_value = jnp.dot(text_mixed, text_out, preferred_element_type=jnp.float32)
    summed = lax.psum(partial_value.astype(jnp.bfloat16), "grp").astype(jnp.float32)
    encoded = rms_scale(flat_states + summed, final_gain).astype(jnp.bfloat16)
    width_local = cross_key.shape[1]
    columns_in = encoded
    key_sum = jnp.dot(
        columns_in,
        lax.all_gather(cross_key, "fsdp", axis=0, tiled=True),
        preferred_element_type=jnp.float32,
    )
    value_sum = jnp.dot(
        columns_in,
        lax.all_gather(cross_value, "fsdp", axis=0, tiled=True),
        preferred_element_type=jnp.float32,
    )
    cap_keys = key_sum.astype(jnp.bfloat16).reshape(caps_local, cap_len, width_local)
    cap_values = value_sum.astype(jnp.bfloat16).reshape(caps_local, cap_len, width_local)
    all_keys, all_values = (
        lax.all_gather(cap_keys, "fsdp", axis=0, tiled=True),
        lax.all_gather(cap_values, "fsdp", axis=0, tiled=True),
    )
    caption_total = all_keys.shape[0]
    tokens, model_width = video_states.shape
    positions = column * tokens + jnp.arange(tokens, dtype=jnp.int32)
    sample_end = jnp.cumsum(video_counts)
    token_sample = jnp.sum((sample_end[None, :] <= positions[:, None]).astype(jnp.int32), axis=1)
    slot_count = 3
    slot_sample = token_sample[0] + jnp.arange(slot_count, dtype=jnp.int32)
    slot_valid = slot_sample < caption_total
    slot_clipped = jnp.minimum(slot_sample, caption_total - 1)
    numbers = jnp.arange(caption_total, dtype=jnp.int32)
    slot_pick = slot_clipped[:, None] == numbers[None, :]
    slot_caption = jnp.sum(jnp.where(slot_pick, sample_caption[None, :], 0), axis=1)
    caption_pick = slot_caption[:, None] == numbers[None, :]
    slot_lens = jnp.sum(jnp.where(caption_pick, caption_lens[None, :], 0), axis=1)
    slot_member = token_sample[None, :] == slot_sample[:, None]
    member_float = slot_member.astype(jnp.float32)
    member_half = slot_member.astype(jnp.bfloat16)
    cross_local = width_local // HEAD_SIZE
    slot_keys = jnp.take(all_keys, slot_caption, axis=0).reshape(
        slot_count, cap_len, cross_local, HEAD_SIZE
    )
    slot_values = jnp.take(all_values, slot_caption, axis=0).reshape(
        slot_count, cap_len, cross_local, HEAD_SIZE
    )
    token_lens = jnp.sum(jnp.where(slot_member, slot_lens[:, None], 0), axis=0)
    video = video_states.astype(jnp.float32)
    center = video - jnp.mean(video, axis=-1, keepdims=True)
    inverse = lax.rsqrt(jnp.mean(center * center, axis=-1, keepdims=True) + 1e-06)
    video_hat = center * inverse
    video_normed = video_hat.astype(jnp.bfloat16)
    columns_in = video_normed
    queries = jnp.dot(
        columns_in,
        lax.all_gather(cross_query, "fsdp", axis=0, tiled=True),
        preferred_element_type=jnp.float32,
    ).astype(jnp.bfloat16)
    score_scale = 1.0 / math.sqrt(HEAD_SIZE)
    query_heads = queries.reshape(tokens, cross_local, HEAD_SIZE)
    slot_scores = jnp.einsum(
        "thd,kjhd->kthj", query_heads, slot_keys, preferred_element_type=jnp.float32
    )
    scores = jnp.sum(member_float[:, :, None, None] * slot_scores, axis=0) * score_scale
    token_valid = (jnp.arange(cap_len, dtype=jnp.int32)[None, :] < token_lens[:, None])[:, None, :]
    exp_video = jnp.where(token_valid, jnp.exp(scores), 0.0)
    weights = exp_video / jnp.sum(exp_video, axis=-1, keepdims=True)
    probs = weights.astype(jnp.bfloat16)
    masked_probs = member_half[:, :, None, None] * probs[None]
    attended = jnp.einsum(
        "kthj,kjhd->thd", masked_probs, slot_values, preferred_element_type=jnp.float32
    )
    attended = attended.astype(jnp.bfloat16).reshape(tokens, width_local)
    partial_out = jnp.dot(
        attended,
        lax.all_gather(cross_out, "fsdp", axis=1, tiled=True),
        preferred_element_type=jnp.float32,
    )
    out_share = lax.psum_scatter(
        partial_out.astype(jnp.bfloat16), "grp", scatter_dimension=1, tiled=True
    ).astype(jnp.float32)
    slice_width = out_share.shape[1]
    feature_start = lax.axis_index("grp") * slice_width
    updated = (lax.dynamic_slice_in_dim(video, feature_start, slice_width, 1) + out_share).astype(
        jnp.bfloat16
    )
    d_attended = contract_last(out_grad, lax.all_gather(cross_out, "fsdp", axis=1, tiled=True))
    d_attended = d_attended.astype(jnp.bfloat16).reshape(tokens, cross_local, HEAD_SIZE)
    slot_dprobs = jnp.einsum(
        "thd,kjhd->kthj", d_attended, slot_values, preferred_element_type=jnp.float32
    )
    d_probs = jnp.sum(member_float[:, :, None, None] * slot_dprobs, axis=0)
    d_scores = (
        weights * (d_probs - jnp.sum(weights * d_probs, axis=-1, keepdims=True)) * score_scale
    ).astype(jnp.bfloat16)
    masked_scores = member_half[:, :, None, None] * d_scores[None]
    d_queries = jnp.einsum(
        "kthj,kjhd->thd", masked_scores, slot_keys, preferred_element_type=jnp.float32
    )
    d_queries = d_queries.astype(jnp.bfloat16).reshape(tokens, width_local)
    key_slots = jnp.einsum(
        "kthj,thd->kjhd", masked_scores, query_heads, preferred_element_type=jnp.float32
    )
    value_slots = jnp.einsum(
        "kthj,thd->kjhd", masked_probs, d_attended, preferred_element_type=jnp.float32
    )
    slot_terms = jnp.concatenate(
        [
            key_slots.reshape(slot_count, cap_len, width_local),
            value_slots.reshape(slot_count, cap_len, width_local),
        ],
        axis=-1,
    )
    wanted = jnp.arange(caps_local * lax.axis_size("fsdp"), dtype=jnp.int32)
    placing = ((slot_caption[None, :] == wanted[:, None]) & slot_valid[None, :]).astype(jnp.float32)
    kv_grads = lax.psum_scatter(
        jnp.einsum("ck,kjw->cjw", placing, slot_terms).astype(jnp.bfloat16),
        "fsdp",
        scatter_dimension=0,
        tiled=True,
    ).astype(jnp.float32)
    key_grad = kv_grads[:, :, :width_local].astype(jnp.bfloat16)
    value_grad = kv_grads[:, :, width_local:].astype(jnp.bfloat16)
    query_grad = lax.psum_scatter(
        contract_first(video_normed, d_queries).astype(jnp.bfloat16),
        "fsdp",
        scatter_dimension=0,
        tiled=True,
    ).astype(jnp.float32)
    out_weight_grad = lax.psum_scatter(
        contract_first(attended, out_grad).astype(jnp.bfloat16),
        "fsdp",
        scatter_dimension=1,
        tiled=True,
    ).astype(jnp.float32)
    d_normed = contract_last(d_queries, lax.all_gather(cross_query, "fsdp", axis=0, tiled=True))
    d_full = lax.psum(d_normed.astype(jnp.bfloat16), "grp").astype(jnp.float32)
    first_mean = jnp.mean(d_full, axis=-1, keepdims=True)
    second_mean = jnp.mean(d_full * video_hat, axis=-1, keepdims=True)
    full_grad = out_grad.astype(jnp.float32) + inverse * (
        d_full - first_mean - video_hat * second_mean
    )
    input_grad = lax.dynamic_slice_in_dim(full_grad, feature_start, slice_width, 1).astype(
        jnp.bfloat16
    )
    return (updated, input_grad, query_grad, out_weight_grad, key_grad, value_grad)


def solution(mesh):
    in_specs = (
        P("fsdp", None, None),
        P(),
        P(),
        P(None, "grp"),
        P(None, "grp"),
        P(None, "grp"),
        P("grp", None, None),
        P("grp", None),
        P(),
        P("fsdp", "grp"),
        P("fsdp", "grp"),
        P("fsdp", None),
        P(),
        P(),
        P("fsdp", "grp"),
        P("grp", "fsdp"),
        P("fsdp", None),
    )
    out_specs = (
        P("fsdp", "grp"),
        P("fsdp", "grp"),
        P("fsdp", "grp"),
        P("grp", "fsdp"),
        P("fsdp", None, "grp"),
        P("fsdp", None, "grp"),
    )
    return jax.shard_map(local, mesh=mesh, in_specs=in_specs, out_specs=out_specs, check_vma=False)
```

profile of v0, /device:TPU:0, one launch (start us, length us, event | category | flops | bytes accessed | tf_op | source)
XLA Modules:
  0.0 560.4 jit_solution(6229628708613981955)
XLA Ops:
  8.0 1.5 fusion.1
  9.6 3.4 convolution_convert_fusion.11
  13.4 2.9 convolution_convert_fusion.10
  16.5 3.0 convolution_convert_fusion.9
  19.6 0.6 dynamic_slice.10
  20.2 0.6 iota_compare_fusion.4
  20.8 0.3 fusion.10
  21.3 3.9 convolution_convert_fusion
  25.4 0.5 all-gather.11.cloned.1.call-update
  25.9 0.5 all-gather.13.cloned.1.call-update
  26.5 0.5 all-gather.9.cloned.1.call-update
  27.1 0.7 all-gather.7.cloned.1.call-update
  28.1 0.5 slice.11
  28.6 0.6 iota_add_fusion.1
  29.8 0.3 convert_reduce_fusion
  30.1 0.6 multiply_reduce_fusion.1
  30.8 33.5 %all-reduce.3.cloned.1.call-done = bf16[128,4096]{1,0:T(8,128)(2,1)} async-done(((bf16[128,4096]{1,0:T(8,128)(2,1)}), bf16[128,4096]{1,0:T(8,128)(2,1)}) %all-reduce.3.cloned.1.call-update) | async-done | bytes 1048592 | tf_op jit(solution)/shard_map/psum | solution.py:78
  64.3 1.6 multiply_reduce_fusion.2
  65.9 16.5 %all-gather.11.cloned.1.call-done = bf16[3072,384]{1,0:T(8,128)(2,1)} async-done(((bf16[384,384]{1,0:T(8,128)(2,1)}), bf16[3072,384]{1,0:T(8,128)(2,1)}) %all-gather.11.cloned.1.call-update) | async-done | bytes 2359312 | tf_op jit(solution)/shard_map/all_gather | solution.py:131
  82.4 2.7 convolution_convert_fusion.7
  85.2 0.8 copy.105
  86.0 50.6 %all-gather.13.cloned.1.call-done = bf16[384,3072]{1,0:T(8,128)(2,1)} async-done(((bf16[384,384]{1,0:T(8,128)(2,1)}), bf16[384,3072]{1,0:T(8,128)(2,1)}) %all-gather.13.cloned.1.call-update) | async-done | bytes 2359312 | tf_op jit(solution)/shard_map/all_gather | solution.py:151
  136.6 3.1 convolution_convert_fusion.6
  139.7 0.8 copy.110
  140.6 56.6 %all-gather.9.cloned.1.call-done = bf16[4096,384]{1,0:T(8,128)(2,1)} async-done(((bf16[512,384]{1,0:T(8,128)(2,1)}), bf16[4096,384]{1,0:T(8,128)(2,1)}) %all-gather.9.cloned.1.call-update) | async-done | bytes 3145744 | tf_op jit(solution)/shard_map/all_gather | solution.py:84
  197.2 3.0 convolution_convert_fusion.12
  200.1 33.8 %all-gather.1 = bf16[1024,384]{1,0:T(8,128)(2,1)S(1)} all-gather(bf16[128,384]{1,0:T(8,128)(2,1)S(1)} %convolution_convert_fusion.12), channel_id=3, replica_groups=mesh['grp'=4,'fsdp'=8] {'fsdp'}, dimensions={0}, use_global_device_ids=true | all-gather | bytes 884736 | tf_op jit(solution)/shard_map/all_gather | solution.py:95
  233.9 29.1 %all-gather.7.cloned.1.call-done = bf16[4096,384]{1,0:T(8,128)(2,1)} async-done(((bf16[512,384]{1,0:T(8,128)(2,1)}), bf16[4096,384]{1,0:T(8,128)(2,1)}) %all-gather.7.cloned.1.call-update) | async-done | bytes 3145744 | tf_op jit(solution)/shard_map/all_gather | solution.py:89
  263.0 3.0 convolution_convert_fusion.13
  266.0 32.4 %all-gather = bf16[1024,384]{1,0:T(8,128)(2,1)S(1)} all-gather(bf16[128,384]{1,0:T(8,128)(2,1)S(1)} %convolution_convert_fusion.13), channel_id=2, replica_groups=mesh['grp'=4,'fsdp'=8] {'fsdp'}, dimensions={0}, use_global_device_ids=true | all-gather | bytes 884736 | tf_op jit(solution)/shard_map/all_gather | solution.py:96
  298.4 1.3 gather_fusion.1
  299.7 0.6 gather_fusion
  300.4 1.1 broadcast_select_fusion
  301.9 1.3 fusion.7
  303.5 0.4 fusion.8
  304.5 0.3 fusion.16
  304.8 0.7 copy-done.8
  305.5 0.5 copy-done.4
  306.0 2.2 convolution_convert_fusion.3
  308.3 0.7 broadcast_compare_fusion
  309.0 0.4 convolution_bitcast_fusion
  309.6 0.4 convolution_bitcast_fusion.1
  310.3 0.8 convolution_convert_fusion.5
  311.1 1.5 copy.119
  312.6 0.3 fusion.15
  313.0 3.9 convolution_convert_fusion.4
  317.0 2.2 convolution_convert_fusion.1
  319.2 4.4 copy.133
  323.7 0.8 copy-done.9
  324.5 2.6 convolution_convert_fusion.2
  327.1 2.0 convert_element_type.141
  329.2 20.5 %all-reduce.5.cloned.1.call-done = bf16[256,3072]{1,0:T(8,128)(2,1)} async-done(((bf16[256,3072]{1,0:T(8,128)(2,1)}), bf16[256,3072]{1,0:T(8,128)(2,1)}) %all-reduce.5.cloned.1.call-update) | async-done | bytes 1572880 | tf_op jit(solution)/shard_map/psum | solution.py:212
  349.7 1.9 convert_element_type.174
  351.6 1.1 convert_reduce_fusion.1
  352.7 1.0 fusion.20
  353.7 22.6 %reduce-scatter.11.cloned.1.call-done = bf16[1,128,768]{2,1,0:T(8,128)(2,1)} async-done(((bf16[8,128,768]{2,1,0:T(8,128)(2,1)}), bf16[1,128,768]{2,1,0:T(8,128)(2,1)}) %reduce-scatter.11.cloned.1.call-update) | async-done | bytes 196624 | tf_op jit(solution)/shard_map/reduce_scatter | solution.py:191
  376.3 1.6 fusion.59
  378.0 27.9 %reduce-scatter.7.cloned.1.call-done = bf16[256,768]{1,0:T(8,128)(2,1)} async-done(((bf16[256,3072]{1,0:T(8,128)(2,1)}), bf16[256,768]{1,0:T(8,128)(2,1)}) %reduce-scatter.7.cloned.1.call-update) | async-done | bytes 393232 | tf_op jit(solution)/shard_map/reduce_scatter | solution.py:154
  405.8 2.1 add_convert_fusion
  407.9 71.0 %reduce-scatter.13.cloned.1.call-done = bf16[384,384]{1,0:T(8,128)(2,1)} async-done(((bf16[3072,384]{1,0:T(8,128)(2,1)}), bf16[384,384]{1,0:T(8,128)(2,1)}) %reduce-scatter.13.cloned.1.call-update) | async-done | bytes 294928
  478.9 1.2 copy.134
  480.1 0.9 convert_element_type.179
  480.9 70.2 %reduce-scatter.9.cloned.1.call-done = bf16[384,384]{1,0:T(8,128)(2,1)} async-done(((bf16[3072,384]{1,0:T(8,128)(2,1)}), bf16[384,384]{1,0:T(8,128)(2,1)}) %reduce-scatter.9.cloned.1.call-update) | async-done | bytes 294928 | tf_op jit(solution)/shard_map/reduce_scatter | solution.py:199
  551.1 1.8 convert_element_type.177
  (80 shorter events, 4.0 us)
Async XLA Ops:
  8.0 56.3 %all-reduce.3.cloned.1.call-start = ((), (), s32[]{:S(2)}) async-start(), calls=%async_computation.4 | async-start | bytes 2097152 | tf_op jit(solution)/shard_map/psum | solution.py:78
  9.6 3.6 copy-start.5
  9.6 3.8 copy-start.2
  9.6 3.8 copy-start.12
  16.5 3.1 copy-start.16
  25.3 2.6 copy-start.14
  25.3 4.0 copy-start.15
  25.3 4.5 copy-start
  25.3 57.1 %all-gather.11.cloned.1.call-start = ((), (), s32[]{:S(2)}) async-start(), calls=%async_computation.7 | async-start | bytes 2654208 | tf_op jit(solution)/shard_map/all_gather | solution.py:131
  25.9 110.7 %all-gather.13.cloned.1.call-start = ((), (), s32[]{:S(2)}) async-start(), calls=%async_computation.8 | async-start | bytes 2654208 | tf_op jit(solution)/shard_map/all_gather | solution.py:151
  26.5 170.7 %all-gather.9.cloned.1.call-start = ((), (), s32[]{:S(2)}) async-start(), calls=%async_computation.6 | async-start | bytes 3538944 | tf_op jit(solution)/shard_map/all_gather | solution.py:84
  27.1 236.0 %all-gather.7.cloned.1.call-start = ((), (), s32[]{:S(2)}) async-start(), calls=%async_computation.5 | async-start | bytes 3538944 | tf_op jit(solution)/shard_map/all_gather | solution.py:89
  27.8 321.9 %all-reduce.5.cloned.1.call-start = ((), (), s32[]{:S(2)}) async-start(), calls=%async_computation.10 | async-start | bytes 3145728 | tf_op jit(solution)/shard_map/psum | solution.py:212
  86.0 111.2 %copy-start.13 = (f32[4096]{0:T(1024)S(1)}, f32[4096]{0:T(1024)}, u32[]{:S(2)}) copy-start(f32[4096]{0:T(1024)} %param.27) | copy-start | bytes 49156
  301.7 2.2 copy-start.6
  301.7 1.8 copy-start.11
  304.3 1.7 copy-start.4
  304.8 0.7 copy-start.8
  308.2 1.5 copy-start.10
  308.2 68.1 %reduce-scatter.11.cloned.1.call-start = ((), (), s32[]{:S(2)}) async-start(), calls=%async_computation.12 | async-start | bytes 1769472 | tf_op jit(solution)/shard_map/reduce_scatter | solution.py:191
  311.1 1.6 copy-start.7
  312.6 93.2 %reduce-scatter.7.cloned.1.call-start = ((), (), s32[]{:S(2)}) async-start(), calls=%async_computation.9 | async-start | bytes 1966080 | tf_op jit(solution)/shard_map/reduce_scatter | solution.py:154
  313.0 4.0 copy-start.3
  316.9 161.9 %reduce-scatter.13.cloned.1.call-start = ((), (), s32[]{:S(2)}) async-start(), calls=%async_computation.13 | async-start | bytes 2654208
  323.6 0.9 copy-start.9
  323.6 227.5 %reduce-scatter.9.cloned.1.call-start = ((), (), s32[]{:S(2)}) async-start(), calls=%async_computation.11 | async-start | bytes 2654208 | tf_op jit(solution)/shard_map/reduce_scatter | solution.py:199
  349.7 1.9 copy-start.1
Sparse Core Ops, SparseCore 0:
  25.4 38.8 all-reduce.2
  308.3 41.3 all-reduce.4
Sparse Core Ops, SparseCore 1:
  28.0 54.4 all-gather.10
  84.4 52.2 all-gather.12
  138.7 58.4 all-gather.8
  199.4 63.6 all-gather.6
  312.8 63.4 reduce-scatter.10
  378.9 26.9 reduce-scatter.6
  409.6 69.3 reduce-scatter.12
  482.7 68.4 reduce-scatter.8
where the time goes:
time: 561 us; the launch traced here: 560 us
  waiting for transfers between devices  401 us (71%)
  blocking collectives  66.2 us (12%)
  matrix products  40.3 us (7%)
  other arithmetic  19.2 us (3%)
  local copies, waits for them, and re-layouts  17.3 us (3%)
  between operations  16 us (3%)
    unnamed x11, waiting for transfers between devices  73.4 us
    reduce_scatter x1, waiting for transfers between devices, local(): lax.psum_scatter(contract_first(video_normed, d_queries).astype(jnp.bfloa...  70.2 us
    all_gather x1, waiting for transfers between devices, local(): lax.all_gather(cross_key, 'fsdp', axis=0, tiled=True)  56.6 us
    all_gather x1, waiting for transfers between devices, local(): lax.all_gather(cross_out, 'fsdp', axis=1, tiled=True)  50.6 us
    all_gather x1, blocking collectives, local(): lax.all_gather(cap_keys, 'fsdp', axis=0, tiled=True)  33.8 us
    psum x1, waiting for transfers between devices, local(): lax.psum(partial_value.astype(jnp.bfloat16), 'grp').astype(jnp.float32)  33.5 us
    all_gather x1, blocking collectives, local(): lax.all_gather(cap_values, 'fsdp', axis=0, tiled=True)  32.4 us
    all_gather x1, waiting for transfers between devices, local(): lax.all_gather(cross_value, 'fsdp', axis=0, tiled=True)  29.1 us
  transfers between devices with their start and end apart: 10, of which 10 were waited for; matrix products, arithmetic and copies ran while one was open for 8% of the time, Pallas kernels for 0%

commit v1 on v0

v1 whole, which is shorter than its diff:
```python
import math

import jax
import jax.numpy as jnp
from jax import lax
from jax.sharding import PartitionSpec as P

HEAD_SIZE = 128
BF = jnp.bfloat16
F32 = jnp.float32


def rms_scale(values, gain):
    mean_square = jnp.mean(values * values, axis=-1, keepdims=True)
    return values * lax.rsqrt(mean_square + 1e-06) * gain


def mm(left, right):
    return jnp.dot(left, right, preferred_element_type=F32)


def contract_last(left, right):
    return lax.dot_general(left, right, (((1,), (1,)), ((), ())), preferred_element_type=F32)


def contract_first(left, right):
    return lax.dot_general(left, right, (((0,), (0,)), ((), ())), preferred_element_type=F32)


def fsend(block, far, side):
    size = lax.axis_size("fsdp")
    pairs = size // 2
    perm = [(s, ((s // 2 + far) % pairs) * 2 + ((s % 2) ^ side)) for s in range(size)]
    return lax.ppermute(block, "fsdp", perm)


def gsend(block, flip):
    return lax.ppermute(block, "grp", [(s, s ^ flip) for s in range(lax.axis_size("grp"))])


def gather_ring(block):
    blocks = []
    current = block
    for far in range(lax.axis_size("fsdp") // 2):
        if far:
            current = fsend(current, 1, 0)
        blocks += [current, fsend(current, 0, 1)]
    return blocks


def gather_direct(block):
    blocks = []
    for far in range(lax.axis_size("fsdp") // 2):
        current = fsend(block, far, 0) if far else block
        blocks += [current, fsend(current, 0, 1)]
    return blocks


def quarter(array, index, axis=0):
    size = array.shape[axis] // 4
    return lax.dynamic_slice_in_dim(array, index * size, size, axis)


def grp_scatter(partial, g, axis):
    away = [quarter(partial, g ^ 1, axis), quarter(partial, g ^ 3, axis)]
    kept = [quarter(partial, g, axis), quarter(partial, g ^ 2, axis)]
    got = gsend(jnp.stack(away).astype(BF), 1)
    far = gsend((kept[1] + got[1].astype(F32)).astype(BF), 2)
    return kept[0] + got[0].astype(F32) + far.astype(F32)


def local(
    caption_states,
    caption_lens,
    text_gain,
    text_query,
    text_key,
    text_value,
    text_bias,
    text_out,
    final_gain,
    cross_key,
    cross_value,
    video_states,
    video_counts,
    sample_caption,
    cross_query,
    cross_out,
    out_grad,
):
    column = lax.axis_index("fsdp")
    g = lax.axis_index("grp")
    fsdp = lax.axis_size("fsdp")
    pairs = fsdp // 2
    z, y = column // 2, column % 2
    caps_local, cap_len, text_width = caption_states.shape
    tokens, model_width = video_states.shape
    width_local = cross_key.shape[1]
    cross_local = width_local // HEAD_SIZE
    query_rows = cross_query.shape[0]

    def source(far, side):
        return ((z - far) % pairs) * 2 + (y ^ side)

    def target(far, side):
        return ((z + far) % pairs) * 2 + (y ^ side)

    query_blocks = gather_ring(cross_query)
    out_blocks = gather_ring(cross_out)
    full_query = jnp.zeros((model_width, width_local), BF)
    full_out = jnp.zeros((width_local, model_width), BF)
    for far in range(pairs):
        for side in range(2):
            start = source(far, side) * query_rows
            full_query = lax.dynamic_update_slice(
                full_query, query_blocks[2 * far + side], (start, jnp.int32(0))
            )
            full_out = lax.dynamic_update_slice(
                full_out, out_blocks[2 * far + side], (jnp.int32(0), start)
            )

    own_kv = jnp.concatenate([cross_key, cross_value], axis=1)
    other_kv = fsend(own_kv, 0, 1)
    pair_kv = jnp.concatenate(
        [jnp.where(y == 0, own_kv, other_kv), jnp.where(y == 0, other_kv, own_kv)], axis=0
    )

    local_lens = lax.dynamic_slice_in_dim(caption_lens, column * caps_local, caps_local)
    flat_states = caption_states.reshape(caps_local * cap_len, text_width).astype(F32)
    text_normed = rms_scale(flat_states, text_gain).astype(BF)
    local_heads = text_bias.shape[0]
    head_width = text_query.shape[1] // local_heads

    def heads_of(weight):
        return mm(text_normed, weight).astype(BF).reshape(
            caps_local, cap_len, local_heads, head_width
        )

    text_queries = heads_of(text_query)
    text_keys = heads_of(text_key)
    text_values = heads_of(text_value)
    text_scores = (
        jnp.einsum("cihd,cjhd->chij", text_queries, text_keys, preferred_element_type=F32)
        + text_bias[None]
    )
    key_valid = jnp.arange(cap_len, dtype=jnp.int32)[None, :] < local_lens[:, None]
    exp_scores = jnp.where(key_valid[:, None, None, :], jnp.exp(text_scores), 0.0)
    text_weights = (exp_scores / jnp.sum(exp_scores, axis=-1, keepdims=True)).astype(BF)
    text_mixed = jnp.einsum(
        "chij,cjhd->cihd", text_weights, text_values, preferred_element_type=F32
    )
    text_mixed = text_mixed.astype(BF).reshape(caps_local * cap_len, local_heads * head_width)
    partial_text = mm(text_mixed, text_out)
    text_rows = grp_scatter(partial_text, g, 0)
    encoded = rms_scale(quarter(flat_states, g) + text_rows, final_gain).astype(BF)

    part = text_width // pairs
    pieces = [
        lax.dynamic_slice_in_dim(encoded, ((z + far) % pairs) * part, part, 1)
        for far in range(pairs)
    ]
    mine = jnp.stack([fsend(p, far, 0) if far else p for far, p in enumerate(pieces)])
    over_x = jnp.concatenate([mine[:, None], gsend(mine, 2)[:, None]], axis=1)
    over_core = jnp.stack([over_x, gsend(over_x, 1)], axis=2)
    kv_partial = mm(over_core.reshape(-1, part), pair_kv).reshape(pairs, cap_len, 2 * width_local)
    kv_sum = kv_partial[0]
    for far in range(1, pairs):
        kv_sum += fsend(kv_partial[far].astype(BF), pairs - far, 0).astype(F32)
    kv_rows = kv_sum.astype(BF).reshape(4, cap_len // 4, 2 * width_local)
    order = jnp.arange(4, dtype=jnp.int32) ^ g
    cap_kv = jnp.concatenate(
        [lax.dynamic_slice_in_dim(kv_rows, order[k], 1, 0) for k in range(4)], axis=0
    ).reshape(cap_len, 2 * width_local)
    all_kv = jnp.stack(gather_direct(cap_kv))

    video = video_states.astype(F32)
    center = video - jnp.mean(video, axis=-1, keepdims=True)
    inverse = lax.rsqrt(jnp.mean(center * center, axis=-1, keepdims=True) + 1e-06)
    video_hat = center * inverse
    video_normed = video_hat.astype(BF)

    both = jnp.stack([quarter(video_normed, g), quarter(out_grad, g)])
    tiles = []
    for far in range(pairs):
        for side in range(2):
            tile = lax.dynamic_slice_in_dim(both, target(far, side) * query_rows, query_rows, 2)
            tiles.append(fsend(tile, far, side) if far or side else tile)
    tiles = jnp.stack(tiles)
    tiles_x = jnp.stack([tiles, gsend(tiles, 2)], axis=2)
    tiles_all = jnp.stack([tiles_x, gsend(tiles_x, 1)], axis=3)
    normed_tile = tiles_all[:, 0].reshape(-1, query_rows)
    grad_tile = tiles_all[:, 1].reshape(-1, query_rows)

    caption_total = all_kv.shape[0]
    positions = column * tokens + jnp.arange(tokens, dtype=jnp.int32)
    sample_end = jnp.cumsum(video_counts)
    token_sample = jnp.sum((sample_end[None, :] <= positions[:, None]).astype(jnp.int32), axis=1)
    slot_count = 3
    slot_sample = token_sample[0] + jnp.arange(slot_count, dtype=jnp.int32)
    slot_valid = slot_sample < caption_total
    slot_clipped = jnp.minimum(slot_sample, caption_total - 1)
    numbers = jnp.arange(caption_total, dtype=jnp.int32)
    slot_pick = slot_clipped[:, None] == numbers[None, :]
    slot_caption = jnp.sum(jnp.where(slot_pick, sample_caption[None, :], 0), axis=1)
    caption_pick = slot_caption[:, None] == numbers[None, :]
    slot_lens = jnp.sum(jnp.where(caption_pick, caption_lens[None, :], 0), axis=1)
    slot_member = token_sample[None, :] == slot_sample[:, None]
    member_float = slot_member.astype(F32)
    member_half = slot_member.astype(BF)
    slot_entry = ((z - slot_caption // 2) % pairs) * 2 + ((slot_caption % 2) ^ y)
    slot_kv = jnp.take(all_kv, slot_entry, axis=0)
    slot_keys = slot_kv[..., :width_local].reshape(slot_count, cap_len, cross_local, HEAD_SIZE)
    slot_values = slot_kv[..., width_local:].reshape(slot_count, cap_len, cross_local, HEAD_SIZE)
    token_lens = jnp.sum(jnp.where(slot_member, slot_lens[:, None], 0), axis=0)

    query_sum = mm(video_normed, full_query)
    queries = query_sum.astype(BF)
    d_attended = contract_last(out_grad, full_out).astype(BF).reshape(
        tokens, cross_local, HEAD_SIZE
    )
    score_scale = 1.0 / math.sqrt(HEAD_SIZE)
    query_heads = queries.reshape(tokens, cross_local, HEAD_SIZE)
    slot_scores = jnp.einsum("thd,kjhd->kthj", query_heads, slot_keys, preferred_element_type=F32)
    scores = jnp.sum(member_float[:, :, None, None] * slot_scores, axis=0) * score_scale
    token_valid = (jnp.arange(cap_len, dtype=jnp.int32)[None, :] < token_lens[:, None])[:, None, :]
    exp_video = jnp.where(token_valid, jnp.exp(scores), 0.0)
    weights = exp_video / jnp.sum(exp_video, axis=-1, keepdims=True)
    probs = weights.astype(BF)
    masked_probs = member_half[:, :, None, None] * probs[None]
    attended = jnp.einsum("kthj,kjhd->thd", masked_probs, slot_values, preferred_element_type=F32)
    attended = attended.astype(BF).reshape(tokens, width_local)

    def reorder(array):
        return jnp.concatenate([quarter(array, order[k]) for k in range(4)], axis=0)

    all_attended = jnp.concatenate(gather_direct(reorder(attended)), axis=0)
    out_weight_grad = contract_first(all_attended, grad_tile)

    out_share = grp_scatter(mm(attended, full_out), g, 1)
    updated = (quarter(video, g, 1) + out_share).astype(BF)

    slot_dprobs = jnp.einsum("thd,kjhd->kthj", d_attended, slot_values, preferred_element_type=F32)
    d_probs = jnp.sum(member_float[:, :, None, None] * slot_dprobs, axis=0)
    d_scores = (
        weights * (d_probs - jnp.sum(weights * d_probs, axis=-1, keepdims=True)) * score_scale
    ).astype(BF)
    masked_scores = member_half[:, :, None, None] * d_scores[None]
    d_queries = jnp.einsum("kthj,kjhd->thd", masked_scores, slot_keys, preferred_element_type=F32)
    d_queries = d_queries.astype(BF).reshape(tokens, width_local)
    all_d_queries = jnp.concatenate(gather_direct(reorder(d_queries)), axis=0)
    query_grad = contract_first(normed_tile, all_d_queries)

    key_slots = jnp.einsum("kthj,thd->kjhd", masked_scores, query_heads, preferred_element_type=F32)
    value_slots = jnp.einsum("kthj,thd->kjhd", masked_probs, d_attended, preferred_element_type=F32)
    slot_terms = jnp.concatenate(
        [
            key_slots.reshape(slot_count, cap_len, width_local),
            value_slots.reshape(slot_count, cap_len, width_local),
        ],
        axis=-1,
    )

    def caption_terms(far, side):
        picked = (slot_caption == target(far, side)) & slot_valid
        return jnp.sum(jnp.where(picked[:, None, None], slot_terms, 0.0), axis=0)

    away = jnp.stack([caption_terms(far, 1).astype(BF) for far in range(pairs)])
    got = fsend(away, 0, 1).astype(F32)
    kv_grads = caption_terms(0, 0) + got[0]
    for far in range(1, pairs):
        kv_grads += fsend((caption_terms(far, 0) + got[far]).astype(BF), far, 0).astype(F32)
    kv_grads = kv_grads.astype(BF)[None]
    key_grad = kv_grads[:, :, :width_local]
    value_grad = kv_grads[:, :, width_local:]

    d_wide = d_queries.astype(F32)
    column_sum = jnp.sum(full_query.astype(F32), axis=0)
    row_sums = jnp.stack(
        [jnp.sum(d_wide * column_sum, axis=-1), jnp.sum(d_wide * query_sum, axis=-1)]
    )
    row_sums = row_sums + gsend(row_sums, 1)
    row_sums = (row_sums + gsend(row_sums, 2)) / model_width
    d_share = grp_scatter(contract_last(d_queries, full_query), g, 1)
    input_grad = (
        quarter(out_grad, g, 1).astype(F32)
        + inverse
        * (d_share - row_sums[0][:, None] - quarter(video_hat, g, 1) * row_sums[1][:, None])
    ).astype(BF)
    return (updated, input_grad, query_grad, out_weight_grad, key_grad, value_grad)


def solution(mesh):
    in_specs = (
        P("fsdp", None, None),
        P(),
        P(),
        P(None, "grp"),
        P(None, "grp"),
        P(None, "grp"),
        P("grp", None, None),
        P("grp", None),
        P(),
        P("fsdp", "grp"),
        P("fsdp", "grp"),
        P("fsdp", None),
        P(),
        P(),
        P("fsdp", "grp"),
        P("grp", "fsdp"),
        P("fsdp", None),
    )
    out_specs = (
        P("fsdp", "grp"),
        P("fsdp", "grp"),
        P("fsdp", "grp"),
        P("grp", "fsdp"),
        P("fsdp", None, "grp"),
        P("fsdp", None, "grp"),
    )
    return jax.shard_map(local, mesh=mesh, in_specs=in_specs, out_specs=out_specs, check_vma=False)
```

time: 561 us -> 363 us (0.65)
  waiting for transfers between devices: 401 us -> 138 us
  starting transfers between devices: 0.42 us -> 79.9 us
  blocking collectives: 66.2 us -> 0 us
  local copies, waits for them, and re-layouts: 17.3 us -> 49.9 us
  other arithmetic: 19.2 us -> 48.4 us
  matrix products: 40.3 us -> 32.7 us
    all_gather x4 -> x0, waiting for transfers between devices: 153 us -> none  [the longest x1 56.6 us: local(): lax.all_gather(cross_key, 'fsdp', axis=0, tiled=True)]
    ppermute x0 -> x65, waiting for transfers between devices: none -> 138 us  [the longest x53 135 us: fsend(): return lax.ppermute(block, 'fsdp', perm)]
    reduce_scatter x3 -> x0, waiting for transfers between devices: 121 us -> none  [the longest x1 70.2 us: local(): lax.psum_scatter(contract_first(video_normed, d_queries).astype(jnp.bfloa...]
    ppermute x0 -> x65, starting transfers between devices: none -> 79.9 us  [the longest x53 71.1 us: fsend(): return lax.ppermute(block, 'fsdp', perm)]
    unnamed x11 -> x0, waiting for transfers between devices: 73.4 us -> none
    all_gather x2 -> x0, blocking collectives: 66.2 us -> none  [the longest x1 33.8 us: local(): lax.all_gather(cap_keys, 'fsdp', axis=0, tiled=True)]
    psum x2 -> x0, waiting for transfers between devices: 54 us -> none  [the longest x1 33.5 us: local(): lax.psum(partial_value.astype(jnp.bfloat16), 'grp').astype(jnp.float32)]
    unnamed x37 -> x143, local copies, waits for them, and re-layouts: 7.9 us -> 21.8 us
  transfers between devices with their start and end apart: 10 -> 65, of which waited for: 10 -> 29; matrix products, arithmetic and copies ran while one was open for 8% -> 34% of each run, Pallas kernels for 0% -> 0%
where the time goes in v1:
time: 363 us; the launch traced here: 361 us
  waiting for transfers between devices  138 us (38%)
  starting transfers between devices  79.9 us (22%)
  local copies, waits for them, and re-layouts  49.9 us (14%)
  other arithmetic  48.4 us (13%)
  matrix products  32.7 us (9%)
  between operations  11.9 us (3%)
    ppermute x53, waiting for transfers between devices, fsend(): return lax.ppermute(block, 'fsdp', perm)  135 us
    ppermute x53, starting transfers between devices, fsend(): return lax.ppermute(block, 'fsdp', perm)  71.1 us
    unnamed x143, local copies, waits for them, and re-layouts  21.8 us
    dot_general x7, matrix products, mm(): return jnp.dot(left, right, preferred_element_type=F32)  16.3 us
    ppermute x12, starting transfers between devices, gsend(): lax.ppermute(block, 'grp', [(s, s ^ flip) for s in range(lax.axis_size('g...  8.78 us
  transfers between devices with their start and end apart: 65, of which 29 were waited for; matrix products, arithmetic and copies ran while one was open for 34% of the time, Pallas kernels for 0%

profile of v1, /device:TPU:0, one launch (start us, length us, event | category | flops | bytes accessed | tf_op | source)
XLA Modules:
  0.0 360.8 jit_solution(6896239514893539147)
XLA Ops:
  0.6 3.0 collective-permute-start.25
  7.3 1.7 convert_reduce_fusion.1
  9.6 2.4 subtract_multiply_fusion
  17.9 2.7 convert_element_type.260
  26.4 2.1 convert_element_type.258
  35.0 3.0 convolution_convert_fusion.4
  39.8 3.0 convolution_convert_fusion.3
  43.0 3.0 convolution_convert_fusion.2
  55.2 4.2 %fusion.116 = f32[128,4096]{1,0:T(8,128)} fusion(bf16[128,512]{0,1:T(8,128)(2,1)S(1)} %bitcast.337, bf16[512,4096]{1,0:T(8,128)(2,1)} %param.24), kind=kOutput, calls=%fused_computation.311 | convolution fusion | flops 536870912 | bytes 6422528 | tf_op jit(solution)/shard_map/dot_general | solution.py:19
  65.1 1.6 collective-permute-start.39
  68.2 3.5 collective-permute-done.39
  72.4 6.9 %collective-permute-done.40 = bf16[2,64,384]{2,1,0:T(8,128)(2,1)S(1)} collective-permute-done((bf16[2,64,384]{2,1,0:T(8,128)(2,1)}, bf16[2,64,384]{2,1,0:T(8,128)(2,1)S(1)}, u32[]{:S(2)}, u32[]{:S(2)}) %collective-permute-start.40) | collective-permute-done | bytes 98336 | tf_op jit(solution)/shard_map/ppermute | solution.py:34
  79.9 6.0 %collective-permute-done.41 = bf16[2,64,384]{2,1,0:T(8,128)(2,1)S(1)} collective-permute-done((bf16[2,64,384]{2,1,0:T(8,128)(2,1)}, bf16[2,64,384]{2,1,0:T(8,128)(2,1)S(1)}, u32[]{:S(2)}, u32[]{:S(2)}) %collective-permute-start.41) | collective-permute-done | bytes 98336 | tf_op jit(solution)/shard_map/ppermute | solution.py:34
  86.6 6.0 %collective-permute-done.42 = bf16[2,64,384]{2,1,0:T(8,128)(2,1)S(1)} collective-permute-done((bf16[2,64,384]{2,1,0:T(8,128)(2,1)}, bf16[2,64,384]{2,1,0:T(8,128)(2,1)S(1)}, u32[]{:S(2)}, u32[]{:S(2)}) %collective-permute-start.42) | collective-permute-done | bytes 98336 | tf_op jit(solution)/shard_map/ppermute | solution.py:34
  93.2 4.2 %collective-permute-done.43 = bf16[2,64,384]{2,1,0:T(8,128)(2,1)S(1)} collective-permute-done((bf16[2,64,384]{2,1,0:T(8,128)(2,1)}, bf16[2,64,384]{2,1,0:T(8,128)(2,1)S(1)}, u32[]{:S(2)}, u32[]{:S(2)}) %collective-permute-start.43) | collective-permute-done | bytes 98336 | tf_op jit(solution)/shard_map/ppermute | solution.py:34
  97.4 4.8 %collective-permute-start.44 = (bf16[2,64,384]{2,1,0:T(8,128)(2,1)}, bf16[2,64,384]{2,1,0:T(8,128)(2,1)S(1)}, u32[]{:S(2)}, u32[]{:S(2)}) collective-permute-start(bf16[2,64,384]{2,1,0:T(8,128)(2,1)} %get-tuple-element.47), channel_id=1, source_target_pairs={{0,7},{1,6},{2,1},{3,0},{4,3},{5,2},{6,5},{7,4},{8,15},{9,14},{10,... | collective-permute-start | bytes 294920 | tf_op jit(solution)/shard_map/ppermute | solution.py:34
  102.8 1.9 collective-permute-done.44
  105.4 1.8 constant_dynamic-update-slice_fusion.8
  108.7 1.7 constant_dynamic-update-slice_fusion.7
  110.4 2.0 collective-permute-start.27
  114.7 17.3 %collective-permute-done.27 = bf16[384,384]{1,0:T(8,128)(2,1)S(1)} collective-permute-done((bf16[384,384]{1,0:T(8,128)(2,1)}, bf16[384,384]{1,0:T(8,128)(2,1)S(1)}, u32[]{:S(2)}, u32[]{:S(2)}) %collective-permute-start.27) | collective-permute-done | bytes 294944 | tf_op jit(solution)/shard_map/ppermute | solution.py:34
  135.2 2.8 collective-permute-done.20
  141.1 4.1 %collective-permute-start.4 = (bf16[32,1024]{1,0:T(8,128)(2,1)S(1)}, bf16[32,1024]{1,0:T(8,128)(2,1)S(1)}, u32[]{:S(2)}, u32[]{:S(2)}) collective-permute-start(bf16[32,1024]{1,0:T(8,128)(2,1)S(1)} %get-tuple-element.63), channel_id=1, source_target_pairs={{0,6},{1,7},{2,0},{3,1},{4,2},{5,3},{6,4},{7,5},{8,14},{9,15},{10,... | collective-permute-start | bytes 196616 | tf_op jit(solution)/shard_map/ppermute | solution.py:34
  145.2 2.0 collective-permute-start.30
  148.8 13.8 %collective-permute-done.3 = bf16[32,1024]{1,0:T(8,128)(2,1)S(1)} collective-permute-done((bf16[32,1024]{1,0:T(8,128)(2,1)S(1)}, bf16[32,1024]{1,0:T(8,128)(2,1)S(1)}, u32[]{:S(2)}, u32[]{:S(2)}) %collective-permute-start.3) | collective-permute-done | bytes 65568 | tf_op jit(solution)/shard_map/ppermute | solution.py:34
  162.7 6.0 %collective-permute-done.2 = bf16[32,1024]{1,0:T(8,128)(2,1)S(1)} collective-permute-done((bf16[32,1024]{1,0:T(8,128)(2,1)S(1)}, bf16[32,1024]{1,0:T(8,128)(2,1)S(1)}, u32[]{:S(2)}, u32[]{:S(2)}) %collective-permute-start.2) | collective-permute-done | bytes 65568 | tf_op jit(solution)/shard_map/ppermute | solution.py:34
  171.5 2.0 pad_maximum_fusion.1
  176.9 6.4 %collective-permute-done.31 = bf16[384,384]{1,0:T(8,128)(2,1)S(1)} collective-permute-done((bf16[384,384]{1,0:T(8,128)(2,1)S(1)}, bf16[384,384]{1,0:T(8,128)(2,1)S(1)}, u32[]{:S(2)}, u32[]{:S(2)}) %collective-permute-start.31) | collective-permute-done | bytes 294944 | tf_op jit(solution)/shard_map/ppermute | solution.py:34
  183.3 5.9 %collective-permute-done.24 = bf16[384,384]{1,0:T(8,128)(2,1)S(1)} collective-permute-done((bf16[384,384]{1,0:T(8,128)(2,1)S(1)}, bf16[384,384]{1,0:T(8,128)(2,1)S(1)}, u32[]{:S(2)}, u32[]{:S(2)}) %collective-permute-start.24) | collective-permute-done | bytes 294944 | tf_op jit(solution)/shard_map/ppermute | solution.py:34
  191.9 3.6 collective-permute-start.8
  197.0 4.4 %collective-permute-done.10 = bf16[128,768]{1,0:T(8,128)(2,1)S(1)} collective-permute-done((bf16[128,768]{1,0:T(8,128)(2,1)S(1)}, bf16[128,768]{1,0:T(8,128)(2,1)S(1)}, u32[]{:S(2)}, u32[]{:S(2)}) %collective-permute-start.10) | collective-permute-done | bytes 196640 | tf_op jit(solution)/shard_map/ppermute | solution.py:34
  201.4 7.1 %collective-permute-done.9 = bf16[128,768]{1,0:T(8,128)(2,1)S(1)} collective-permute-done((bf16[128,768]{1,0:T(8,128)(2,1)S(1)}, bf16[128,768]{1,0:T(8,128)(2,1)S(1)}, u32[]{:S(2)}, u32[]{:S(2)}) %collective-permute-start.9) | collective-permute-done | bytes 196640 | tf_op jit(solution)/shard_map/ppermute | solution.py:34
  209.3 5.4 %collective-permute-start.12 = (bf16[128,768]{1,0:T(8,128)(2,1)S(1)}, bf16[128,768]{1,0:T(8,128)(2,1)}, u32[]{:S(2)}, u32[]{:S(2)}) collective-permute-start(bf16[128,768]{1,0:T(8,128)(2,1)S(1)} %bitcast.317), channel_id=1, source_target_pairs={{0,2},{1,3},{2,4},{3,5},{4,6},{5,7},{6,0},{7,1},{8,10},{9,11},{10,... | collective-permute-start | bytes 589832 | tf_op jit(solution)/shard_map/ppermute | solution.py:34
  214.8 2.4 collective-permute-start.16
  220.1 2.0 collective-permute-start.13
  222.1 3.4 collective-permute-done.14
  225.4 2.0 collective-permute-start.15
  227.5 1.6 bitcast_dynamic-update-slice_fusion.6
  229.1 1.6 bitcast_dynamic-update-slice_fusion.5
  231.4 1.6 bitcast_dynamic-update-slice_fusion.3
  234.8 1.7 collective-permute-done.17
  237.3 2.0 gather_fusion
  242.3 1.7 fusion.115
  248.0 2.7 fusion.118
  252.3 3.4 collective-permute-start.48
  255.7 2.5 collective-permute-start.50
  265.4 1.8 select_reduce_fusion.7
  275.9 1.7 collective-permute-start.59
  277.6 5.5 %collective-permute-done.52 = bf16[256,384]{0,1:T(8,128)(2,1)S(1)} collective-permute-done((bf16[256,384]{0,1:T(8,128)(2,1)S(1)}, bf16[256,384]{0,1:T(8,128)(2,1)S(1)}, u32[]{:S(2)}, u32[]{:S(2)}) %collective-permute-start.52) | collective-permute-done | bytes 196640 | tf_op jit(solution)/shard_map/ppermute | solution.py:34
  285.2 4.7 %collective-permute-done.57 = bf16[256,384]{0,1:T(8,128)(2,1)} collective-permute-done((bf16[256,384]{0,1:T(8,128)(2,1)}, bf16[256,384]{0,1:T(8,128)(2,1)}, u32[]{:S(2)}, u32[]{:S(2)}) %collective-permute-start.57) | collective-permute-done | bytes 196640 | tf_op jit(solution)/shard_map/ppermute | solution.py:34
  295.2 7.0 %collective-permute-done.53 = bf16[256,384]{0,1:T(8,128)(2,1)S(1)} collective-permute-done((bf16[256,384]{0,1:T(8,128)(2,1)S(1)}, bf16[256,384]{0,1:T(8,128)(2,1)S(1)}, u32[]{:S(2)}, u32[]{:S(2)}) %collective-permute-start.53) | collective-permute-done | bytes 196640 | tf_op jit(solution)/shard_map/ppermute | solution.py:34
  302.9 3.4 pad_maximum_fusion
  306.2 3.7 %concatenate.34 = bf16[2048,384]{0,1:T(8,128)(2,1)} concatenate(bf16[64,384]{0,1:T(8,128)(2,1)} %copy-done.25, bf16[64,384]{0,1:T(8,128)(2,1)} %copy-done.24, bf16[64,384]{0,1:T(8,128)(2,1)} %copy-done.23, bf16[64,384]{0,1:T(8,128)(2,1)} %copy-done.22, bf16[256,384]{0,1:T(8,128)(2,1)} %copy-done.40, bf16[256,384]{0,1:T(8,128)(2,1)} %copy-done.41, bf16[256,384]{0,1:T(8,128)(2,1)} %copy-done.44, ...), dimensions={0} | concatenate | bytes 3145728 | tf_op jit(solution)/shard_map/concatenate | solution.py:250
  312.1 3.7 %concatenate.36 = bf16[2048,384]{0,1:T(8,128)(2,1)} concatenate(bf16[64,384]{0,1:T(8,128)(2,1)} %copy-done.29, bf16[64,384]{0,1:T(8,128)(2,1)} %copy-done.28, bf16[64,384]{0,1:T(8,128)(2,1)} %copy-done.27, bf16[64,384]{0,1:T(8,128)(2,1)} %copy-done.26, bf16[256,384]{0,1:T(8,128)(2,1)} %collective-permute-done.54, bf16[256,384]{0,1:T(8,128)(2,1)} %collective-permute-done.55, ...), dimensions={0} | concatenate | bytes 3145728 | tf_op jit(solution)/shard_map/concatenate | solution.py:236
  315.9 3.9 %fusion.119 = f32[384,384]{1,0:T(8,128)} fusion(bf16[2048,384]{1,0:T(8,128)(2,1)} %bitcast.311, bf16[2048,384]{0,1:T(8,128)(2,1)} %concatenate.34), kind=kOutput, calls=%fused_computation.314 | convolution fusion | flops 603979776 | bytes 3735552 | tf_op jit(solution)/shard_map/dot_general | solution.py:27
  319.8 1.8 fusion.120
  321.6 2.1 fusion.26
  325.2 5.1 %collective-permute-done.61 = bf16[4,128,768]{1,2,0:T(8,128)(2,1)} collective-permute-done((bf16[4,128,768]{1,2,0:T(8,128)(2,1)}, bf16[4,128,768]{1,2,0:T(8,128)(2,1)}, u32[]{:S(2)}, u32[]{:S(2)}) %collective-permute-start.61) | collective-permute-done | bytes 786464 | tf_op jit(solution)/shard_map/ppermute | solution.py:34
  331.7 4.4 %collective-permute-start.64 = (bf16[128,768]{0,1:T(8,128)(2,1)S(1)}, bf16[128,768]{0,1:T(8,128)(2,1)S(1)}, u32[]{:S(2)}, u32[]{:S(2)}) collective-permute-start(bf16[128,768]{0,1:T(8,128)(2,1)S(1)} %get-tuple-element.39), channel_id=1, source_target_pairs={{0,6},{1,7},{2,0},{3,1},{4,2},{5,3},{6,4},{7,5},{8,14},{9,15},{10,... | collective-permute-start | bytes 589832 | tf_op jit(solution)/shard_map/ppermute | solution.py:34
  336.9 1.9 collective-permute-start.62
  338.9 1.8 fusion.19
  342.2 11.9 %collective-permute-done.63 = bf16[128,768]{0,1:T(8,128)(2,1)S(1)} collective-permute-done((bf16[128,768]{0,1:T(8,128)(2,1)S(1)}, bf16[128,768]{0,1:T(8,128)(2,1)S(1)}, u32[]{:S(2)}, u32[]{:S(2)}) %collective-permute-start.63) | collective-permute-done | bytes 196640 | tf_op jit(solution)/shard_map/ppermute | solution.py:34
  355.8 2.5 fusion.29
  358.3 2.5 fusion.25
  (339 shorter events, 104.5 us)
Async XLA Ops:
  0.6 104.8 %collective-permute-start.25 = (bf16[384,384]{1,0:T(8,128)(2,1)}, bf16[384,384]{1,0:T(8,128)(2,1)}, u32[]{:S(2)}, u32[]{:S(2)}) collective-permute-start(bf16[384,384]{1,0:T(8,128)(2,1)} %param.32), channel_id=1, source_target_pairs={{0,1},{1,0},{2,3},{3,2},{4,5},{5,4},{6,7},{7,6},{8,9},{9,8},{10,11... | collective-permute-start | bytes 884744 | tf_op jit(solution)/shard_map/ppermute | solution.py:34
  3.7 103.5 %collective-permute-start.26 = (bf16[384,384]{1,0:T(8,128)(2,1)}, bf16[384,384]{1,0:T(8,128)(2,1)}, u32[]{:S(2)}, u32[]{:S(2)}) collective-permute-start(bf16[384,384]{1,0:T(8,128)(2,1)} %param.32), channel_id=1, source_target_pairs={{0,2},{1,3},{2,4},{3,5},{4,6},{5,7},{6,0},{7,1},{8,10},{9,11},{10,... | collective-permute-start | bytes 884744 | tf_op jit(solution)/shard_map/ppermute | solution.py:34
  5.3 105.2 %collective-permute-start.18 = (bf16[384,384]{1,0:T(8,128)(2,1)}, bf16[384,384]{1,0:T(8,128)(2,1)}, u32[]{:S(2)}, u32[]{:S(2)}) collective-permute-start(bf16[384,384]{1,0:T(8,128)(2,1)} %param.31), channel_id=1, source_target_pairs={{0,1},{1,0},{2,3},{3,2},{4,5},{5,4},{6,7},{7,6},{8,9},{9,8},{10,11... | collective-permute-start | bytes 884744 | tf_op jit(solution)/shard_map/ppermute | solution.py:34
  5.8 107.7 %collective-permute-start.19 = (bf16[384,384]{1,0:T(8,128)(2,1)}, bf16[384,384]{1,0:T(8,128)(2,1)}, u32[]{:S(2)}, u32[]{:S(2)}) collective-permute-start(bf16[384,384]{1,0:T(8,128)(2,1)} %param.31), channel_id=1, source_target_pairs={{0,2},{1,3},{2,4},{3,5},{4,6},{5,7},{6,0},{7,1},{8,10},{9,11},{10,... | collective-permute-start | bytes 884744 | tf_op jit(solution)/shard_map/ppermute | solution.py:34
  14.8 50.3 %collective-permute-start.38 = (bf16[2,64,384]{2,1,0:T(8,128)(2,1)}, bf16[2,64,384]{2,1,0:T(8,128)(2,1)}, u32[]{:S(2)}, u32[]{:S(2)}) collective-permute-start(bf16[2,64,384]{2,1,0:T(8,128)(2,1)} %get-tuple-element.48), channel_id=1, source_target_pairs={{0,1},{1,0},{2,3},{3,2},{4,5},{5,4},{6,7},{7,6},{8,9},{9,8},{10,11... | collective-permute-start | bytes 294920 | tf_op jit(solution)/shard_map/ppermute | solution.py:34
  65.1 6.6 %collective-permute-start.39 = (bf16[2,64,384]{2,1,0:T(8,128)(2,1)}, bf16[2,64,384]{2,1,0:T(8,128)(2,1)S(1)}, u32[]{:S(2)}, u32[]{:S(2)}) collective-permute-start(bf16[2,64,384]{2,1,0:T(8,128)(2,1)} %get-tuple-element.49), channel_id=1, source_target_pairs={{0,2},{1,3},{2,4},{3,5},{4,6},{5,7},{6,0},{7,1},{8,10},{9,11},{10,... | collective-permute-start | bytes 294920 | tf_op jit(solution)/shard_map/ppermute | solution.py:34
  71.7 7.5 %collective-permute-start.40 = (bf16[2,64,384]{2,1,0:T(8,128)(2,1)}, bf16[2,64,384]{2,1,0:T(8,128)(2,1)S(1)}, u32[]{:S(2)}, u32[]{:S(2)}) collective-permute-start(bf16[2,64,384]{2,1,0:T(8,128)(2,1)} %get-tuple-element.50), channel_id=1, source_target_pairs={{0,3},{1,2},{2,5},{3,4},{4,7},{5,6},{6,1},{7,0},{8,11},{9,10},{10,... | collective-permute-start | bytes 294920 | tf_op jit(solution)/shard_map/ppermute | solution.py:34
  79.3 6.7 %collective-permute-start.41 = (bf16[2,64,384]{2,1,0:T(8,128)(2,1)}, bf16[2,64,384]{2,1,0:T(8,128)(2,1)S(1)}, u32[]{:S(2)}, u32[]{:S(2)}) collective-permute-start(bf16[2,64,384]{2,1,0:T(8,128)(2,1)} %get-tuple-element.51), channel_id=1, source_target_pairs={{0,4},{1,5},{2,6},{3,7},{4,0},{5,1},{6,2},{7,3},{8,12},{9,13},{10,... | collective-permute-start | bytes 294920 | tf_op jit(solution)/shard_map/ppermute | solution.py:34
  85.9 6.6 %collective-permute-start.42 = (bf16[2,64,384]{2,1,0:T(8,128)(2,1)}, bf16[2,64,384]{2,1,0:T(8,128)(2,1)S(1)}, u32[]{:S(2)}, u32[]{:S(2)}) collective-permute-start(bf16[2,64,384]{2,1,0:T(8,128)(2,1)} %get-tuple-element.52), channel_id=1, source_target_pairs={{0,5},{1,4},{2,7},{3,6},{4,1},{5,0},{6,3},{7,2},{8,13},{9,12},{10,... | collective-permute-start | bytes 294920 | tf_op jit(solution)/shard_map/ppermute | solution.py:34
  92.6 4.8 %collective-permute-start.43 = (bf16[2,64,384]{2,1,0:T(8,128)(2,1)}, bf16[2,64,384]{2,1,0:T(8,128)(2,1)S(1)}, u32[]{:S(2)}, u32[]{:S(2)}) collective-permute-start(bf16[2,64,384]{2,1,0:T(8,128)(2,1)} %fusion.75), channel_id=1, source_target_pairs={{0,6},{1,7},{2,0},{3,1},{4,2},{5,3},{6,4},{7,5},{8,14},{9,15},{10,... | collective-permute-start | bytes 294920 | tf_op jit(solution)/shard_map/ppermute | solution.py:34
  97.4 7.3 %collective-permute-start.44 = (bf16[2,64,384]{2,1,0:T(8,128)(2,1)}, bf16[2,64,384]{2,1,0:T(8,128)(2,1)S(1)}, u32[]{:S(2)}, u32[]{:S(2)}) collective-permute-start(bf16[2,64,384]{2,1,0:T(8,128)(2,1)} %get-tuple-element.47), channel_id=1, source_target_pairs={{0,7},{1,6},{2,1},{3,0},{4,3},{5,2},{6,5},{7,4},{8,15},{9,14},{10,... | collective-permute-start | bytes 294920 | tf_op jit(solution)/shard_map/ppermute | solution.py:34
  104.7 9.8 %collective-permute-start = (bf16[2,32,4096]{2,1,0:T(8,128)(2,1)}, bf16[2,32,4096]{2,1,0:T(8,128)(2,1)S(1)}, u32[]{:S(2)}, u32[]{:S(2)}) collective-permute-start(bf16[2,32,4096]{2,1,0:T(8,128)(2,1)} %pad_maximum_fusion.7), channel_id=1, source_target_pairs={{0,8},{8,0},{16,24},{24,16},{1,9},{9,1},{17,25},{25,17},{2,10},{10... | collective-permute-start | bytes 1572872 | tf_op jit(solution)/shard_map/ppermute | solution.py:38
  105.4 39.8 %collective-permute-start.7 = (bf16[512,768]{1,0:T(8,128)(2,1)S(1)}, bf16[512,768]{1,0:T(8,128)(2,1)S(1)}, u32[]{:S(2)}, u32[]{:S(2)}) collective-permute-start(bf16[512,768]{1,0:T(8,128)(2,1)S(1)} %constant_dynamic-update-slice_fusion), channel_id=1, source_target_pairs={{0,1},{1,0},{2,3},{3,2},{4,5},{5,4},{6,7},{7,6},{8,9},{9,8},{10,11... | collective-permute-start | bytes 2359304 | tf_op jit(solution)/shard_map/ppermute | solution.py:34
  107.2 63.0 %collective-permute-start.45 = (bf16[8,2,64,384]{3,2,0,1:T(8,128)(2,1)}, bf16[8,2,64,384]{3,2,0,1:T(8,128)(2,1)S(1)}, u32[]{:S(2)}, u32[]{:S(2)}) collective-permute-start(bf16[8,2,64,384]{3,2,0,1:T(8,128)(2,1)} %bitcast_dynamic-update-slice_fusion.14), channel_id=1, source_target_pairs={{0,16},{8,24},{16,0},{24,8},{1,17},{9,25},{17,1},{25,9},{2,18},{10... | collective-permute-start | bytes 2359304 | tf_op jit(solution)/shard_map/ppermute | solution.py:38
  110.4 21.6 %collective-permute-start.27 = (bf16[384,384]{1,0:T(8,128)(2,1)}, bf16[384,384]{1,0:T(8,128)(2,1)S(1)}, u32[]{:S(2)}, u32[]{:S(2)}) collective-permute-start(bf16[384,384]{1,0:T(8,128)(2,1)} %collective-permute-done.26), channel_id=1, source_target_pairs={{0,1},{1,0},{2,3},{3,2},{4,5},{5,4},{6,7},{7,6},{8,9},{9,8},{10,11... | collective-permute-start | bytes 884744 | tf_op jit(solution)/shard_map/ppermute | solution.py:34
  113.5 20.9 %collective-permute-start.28 = (bf16[384,384]{1,0:T(8,128)(2,1)}, bf16[384,384]{1,0:T(8,128)(2,1)S(1)}, u32[]{:S(2)}, u32[]{:S(2)}) collective-permute-start(bf16[384,384]{1,0:T(8,128)(2,1)} %collective-permute-done.26), channel_id=1, source_target_pairs={{0,2},{1,3},{2,4},{3,5},{4,6},{5,7},{6,0},{7,1},{8,10},{9,11},{10,... | collective-permute-start | bytes 884744 | tf_op jit(solution)/shard_map/ppermute | solution.py:34
  114.6 23.4 %collective-permute-start.20 = (bf16[384,384]{1,0:T(8,128)(2,1)}, bf16[384,384]{1,0:T(8,128)(2,1)S(1)}, u32[]{:S(2)}, u32[]{:S(2)}) collective-permute-start(bf16[384,384]{1,0:T(8,128)(2,1)} %collective-permute-done.19), channel_id=1, source_target_pairs={{0,1},{1,0},{2,3},{3,2},{4,5},{5,4},{6,7},{7,6},{8,9},{9,8},{10,11... | collective-permute-start | bytes 884744 | tf_op jit(solution)/shard_map/ppermute | solution.py:34
  132.1 7.6 %collective-permute-start.1 = (bf16[32,4096]{1,0:T(8,128)(2,1)S(1)}, bf16[32,4096]{1,0:T(8,128)(2,1)S(1)}, u32[]{:S(2)}, u32[]{:S(2)}) collective-permute-start(bf16[32,4096]{1,0:T(8,128)(2,1)S(1)} %fusion.32), channel_id=1, source_target_pairs={{0,16},{8,24},{16,0},{24,8},{1,17},{9,25},{17,1},{25,9},{2,18},{10... | collective-permute-start | bytes 786440 | tf_op jit(solution)/shard_map/ppermute | solution.py:38
  134.4 10.8 %collective-permute-start.21 = (bf16[384,384]{1,0:T(8,128)(2,1)}, bf16[384,384]{1,0:T(8,128)(2,1)S(1)}, u32[]{:S(2)}, u32[]{:S(2)}) collective-permute-start(bf16[384,384]{1,0:T(8,128)(2,1)} %collective-permute-done.19), channel_id=1, source_target_pairs={{0,2},{1,3},{2,4},{3,5},{4,6},{5,7},{6,0},{7,1},{8,10},{9,11},{10,... | collective-permute-start | bytes 884744 | tf_op jit(solution)/shard_map/ppermute | solution.py:34
  138.0 35.5 %collective-permute-start.29 = (bf16[384,384]{1,0:T(8,128)(2,1)S(1)}, bf16[384,384]{1,0:T(8,128)(2,1)S(1)}, u32[]{:S(2)}, u32[]{:S(2)}) collective-permute-start(bf16[384,384]{1,0:T(8,128)(2,1)S(1)} %collective-permute-done.28), channel_id=1, source_target_pairs={{0,1},{1,0},{2,3},{3,2},{4,5},{5,4},{6,7},{7,6},{8,9},{9,8},{10,11... | collective-permute-start | bytes 884744 | tf_op jit(solution)/shard_map/ppermute | solution.py:34
  141.1 6.6 %collective-permute-start.4 = (bf16[32,1024]{1,0:T(8,128)(2,1)S(1)}, bf16[32,1024]{1,0:T(8,128)(2,1)S(1)}, u32[]{:S(2)}, u32[]{:S(2)}) collective-permute-start(bf16[32,1024]{1,0:T(8,128)(2,1)S(1)} %get-tuple-element.63), channel_id=1, source_target_pairs={{0,6},{1,7},{2,0},{3,1},{4,2},{5,3},{6,4},{7,5},{8,14},{9,15},{10,... | collective-permute-start | bytes 196616 | tf_op jit(solution)/shard_map/ppermute | solution.py:34
  145.2 17.4 %collective-permute-start.3 = (bf16[32,1024]{1,0:T(8,128)(2,1)S(1)}, bf16[32,1024]{1,0:T(8,128)(2,1)S(1)}, u32[]{:S(2)}, u32[]{:S(2)}) collective-permute-start(bf16[32,1024]{1,0:T(8,128)(2,1)S(1)} %get-tuple-element.64), channel_id=1, source_target_pairs={{0,4},{1,5},{2,6},{3,7},{4,0},{5,1},{6,2},{7,3},{8,12},{9,13},{10,... | collective-permute-start | bytes 196616 | tf_op jit(solution)/shard_map/ppermute | solution.py:34
  145.2 28.2 %collective-permute-start.30 = (bf16[384,384]{1,0:T(8,128)(2,1)S(1)}, bf16[384,384]{1,0:T(8,128)(2,1)S(1)}, u32[]{:S(2)}, u32[]{:S(2)}) collective-permute-start(bf16[384,384]{1,0:T(8,128)(2,1)S(1)} %collective-permute-done.28), channel_id=1, source_target_pairs={{0,2},{1,3},{2,4},{3,5},{4,6},{5,7},{6,0},{7,1},{8,10},{9,11},{10,... | collective-permute-start | bytes 884744 | tf_op jit(solution)/shard_map/ppermute | solution.py:34
  147.7 26.4 %collective-permute-start.23 = (bf16[384,384]{1,0:T(8,128)(2,1)S(1)}, bf16[384,384]{1,0:T(8,128)(2,1)S(1)}, u32[]{:S(2)}, u32[]{:S(2)}) collective-permute-start(bf16[384,384]{1,0:T(8,128)(2,1)S(1)} %collective-permute-done.21), channel_id=1, source_target_pairs={{0,2},{1,3},{2,4},{3,5},{4,6},{5,7},{6,0},{7,1},{8,10},{9,11},{10,... | collective-permute-start | bytes 884744 | tf_op jit(solution)/shard_map/ppermute | solution.py:34
  162.6 6.1 %collective-permute-start.2 = (bf16[32,1024]{1,0:T(8,128)(2,1)S(1)}, bf16[32,1024]{1,0:T(8,128)(2,1)S(1)}, u32[]{:S(2)}, u32[]{:S(2)}) collective-permute-start(bf16[32,1024]{1,0:T(8,128)(2,1)S(1)} %get-tuple-element.65), channel_id=1, source_target_pairs={{0,2},{1,3},{2,4},{3,5},{4,6},{5,7},{6,0},{7,1},{8,10},{9,11},{10,... | collective-permute-start | bytes 196616 | tf_op jit(solution)/shard_map/ppermute | solution.py:34
  168.6 7.4 %collective-permute-start.22 = (bf16[384,384]{1,0:T(8,128)(2,1)S(1)}, bf16[384,384]{1,0:T(8,128)(2,1)S(1)}, u32[]{:S(2)}, u32[]{:S(2)}) collective-permute-start(bf16[384,384]{1,0:T(8,128)(2,1)S(1)} %collective-permute-done.21), channel_id=1, source_target_pairs={{0,1},{1,0},{2,3},{3,2},{4,5},{5,4},{6,7},{7,6},{8,9},{9,8},{10,11... | collective-permute-start | bytes 884744 | tf_op jit(solution)/shard_map/ppermute | solution.py:34
  170.2 6.4 %collective-permute-start.5 = (bf16[4,32,1024]{2,1,0:T(8,128)(2,1)S(1)}, bf16[4,32,1024]{2,1,0:T(8,128)(2,1)S(1)}, u32[]{:S(2)}, u32[]{:S(2)}) collective-permute-start(bf16[4,32,1024]{2,1,0:T(8,128)(2,1)S(1)} %get-tuple-element.61), channel_id=1, source_target_pairs={{0,16},{8,24},{16,0},{24,8},{1,17},{9,25},{17,1},{25,9},{2,18},{10... | collective-permute-start | bytes 786440 | tf_op jit(solution)/shard_map/ppermute | solution.py:38
  173.4 118.5 %collective-permute-start.46 = (bf16[8,2,2,64,384]{4,3,2,0,1:T(8,128)(2,1)}, bf16[8,2,2,64,384]{4,3,2,0,1:T(8,128)(2,1)}, u32[]{:S(2)}, u32[]{:S(2)}) collective-permute-start(bf16[8,2,2,64,384]{4,3,2,0,1:T(8,128)(2,1)} %get-tuple-element.41), channel_id=1, source_target_pairs={{0,8},{8,0},{16,24},{24,16},{1,9},{9,1},{17,25},{25,17},{2,10},{10... | collective-permute-start | bytes 4718600 | tf_op jit(solution)/shard_map/ppermute | solution.py:38
  173.5 9.9 %collective-permute-start.31 = (bf16[384,384]{1,0:T(8,128)(2,1)S(1)}, bf16[384,384]{1,0:T(8,128)(2,1)S(1)}, u32[]{:S(2)}, u32[]{:S(2)}) collective-permute-start(bf16[384,384]{1,0:T(8,128)(2,1)S(1)} %collective-permute-done.30), channel_id=1, source_target_pairs={{0,1},{1,0},{2,3},{3,2},{4,5},{5,4},{6,7},{7,6},{8,9},{9,8},{10,11... | collective-permute-start | bytes 884744 | tf_op jit(solution)/shard_map/ppermute | solution.py:34
  174.1 15.1 %collective-permute-start.24 = (bf16[384,384]{1,0:T(8,128)(2,1)S(1)}, bf16[384,384]{1,0:T(8,128)(2,1)S(1)}, u32[]{:S(2)}, u32[]{:S(2)}) collective-permute-start(bf16[384,384]{1,0:T(8,128)(2,1)S(1)} %collective-permute-done.23), channel_id=1, source_target_pairs={{0,1},{1,0},{2,3},{3,2},{4,5},{5,4},{6,7},{7,6},{8,9},{9,8},{10,11... | collective-permute-start | bytes 884744 | tf_op jit(solution)/shard_map/ppermute | solution.py:34
  176.7 13.6 %collective-permute-start.6 = (bf16[4,2,32,1024]{3,2,0,1:T(8,128)(2,1)S(1)}, bf16[4,2,32,1024]{3,2,0,1:T(8,128)(2,1)S(1)}, u32[]{:S(2)}, u32[]{:S(2)}) collective-permute-start(bf16[4,2,32,1024]{3,2,0,1:T(8,128)(2,1)S(1)} %get-tuple-element.59), channel_id=1, source_target_pairs={{0,8},{8,0},{16,24},{24,16},{1,9},{9,1},{17,25},{25,17},{2,10},{10... | collective-permute-start | bytes 1572872 | tf_op jit(solution)/shard_map/ppermute | solution.py:38
  191.6 9.8 %collective-permute-start.10 = (bf16[128,768]{1,0:T(8,128)(2,1)S(1)}, bf16[128,768]{1,0:T(8,128)(2,1)S(1)}, u32[]{:S(2)}, u32[]{:S(2)}) collective-permute-start(bf16[128,768]{1,0:T(8,128)(2,1)S(1)} %get-tuple-element.54), channel_id=1, source_target_pairs={{0,2},{1,3},{2,4},{3,5},{4,6},{5,7},{6,0},{7,1},{8,10},{9,11},{10,... | collective-permute-start | bytes 589832 | tf_op jit(solution)/shard_map/ppermute | solution.py:34
  191.7 16.9 %collective-permute-start.9 = (bf16[128,768]{1,0:T(8,128)(2,1)S(1)}, bf16[128,768]{1,0:T(8,128)(2,1)S(1)}, u32[]{:S(2)}, u32[]{:S(2)}) collective-permute-start(bf16[128,768]{1,0:T(8,128)(2,1)S(1)} %get-tuple-element.55), channel_id=1, source_target_pairs={{0,4},{1,5},{2,6},{3,7},{4,0},{5,1},{6,2},{7,3},{8,12},{9,13},{10,... | collective-permute-start | bytes 589832 | tf_op jit(solution)/shard_map/ppermute | solution.py:34
  191.9 16.6 %collective-permute-start.8 = (bf16[128,768]{1,0:T(8,128)(2,1)S(1)}, bf16[128,768]{1,0:T(8,128)(2,1)S(1)}, u32[]{:S(2)}, u32[]{:S(2)}) collective-permute-start(bf16[128,768]{1,0:T(8,128)(2,1)S(1)} %get-tuple-element.53), channel_id=1, source_target_pairs={{0,6},{1,7},{2,0},{3,1},{4,2},{5,3},{6,4},{7,5},{8,14},{9,15},{10,... | collective-permute-start | bytes 589832 | tf_op jit(solution)/shard_map/ppermute | solution.py:34
  208.7 18.8 %collective-permute-start.11 = (bf16[128,768]{1,0:T(8,128)(2,1)S(1)}, bf16[128,768]{1,0:T(8,128)(2,1)}, u32[]{:S(2)}, u32[]{:S(2)}) collective-permute-start(bf16[128,768]{1,0:T(8,128)(2,1)S(1)} %bitcast.316), channel_id=1, source_target_pairs={{0,1},{1,0},{2,3},{3,2},{4,5},{5,4},{6,7},{7,6},{8,9},{9,8},{10,11... | collective-permute-start | bytes 589832 | tf_op jit(solution)/shard_map/ppermute | solution.py:34
  209.3 10.8 %collective-permute-start.12 = (bf16[128,768]{1,0:T(8,128)(2,1)S(1)}, bf16[128,768]{1,0:T(8,128)(2,1)}, u32[]{:S(2)}, u32[]{:S(2)}) collective-permute-start(bf16[128,768]{1,0:T(8,128)(2,1)S(1)} %bitcast.317), channel_id=1, source_target_pairs={{0,2},{1,3},{2,4},{3,5},{4,6},{5,7},{6,0},{7,1},{8,10},{9,11},{10,... | collective-permute-start | bytes 589832 | tf_op jit(solution)/shard_map/ppermute | solution.py:34
  214.8 10.7 %collective-permute-start.14 = (bf16[128,768]{1,0:T(8,128)(2,1)S(1)}, bf16[128,768]{1,0:T(8,128)(2,1)}, u32[]{:S(2)}, u32[]{:S(2)}) collective-permute-start(bf16[128,768]{1,0:T(8,128)(2,1)S(1)} %bitcast.318), channel_id=1, source_target_pairs={{0,4},{1,5},{2,6},{3,7},{4,0},{5,1},{6,2},{7,3},{8,12},{9,13},{10,... | collective-permute-start | bytes 589832 | tf_op jit(solution)/shard_map/ppermute | solution.py:34
  214.8 12.7 %collective-permute-start.16 = (bf16[128,768]{1,0:T(8,128)(2,1)S(1)}, bf16[128,768]{1,0:T(8,128)(2,1)S(1)}, u32[]{:S(2)}, u32[]{:S(2)}) collective-permute-start(bf16[128,768]{1,0:T(8,128)(2,1)S(1)} %bitcast.319), channel_id=1, source_target_pairs={{0,6},{1,7},{2,0},{3,1},{4,2},{5,3},{6,4},{7,5},{8,14},{9,15},{10,... | collective-permute-start | bytes 589832 | tf_op jit(solution)/shard_map/ppermute | solution.py:34
  220.1 10.6 %collective-permute-start.13 = (bf16[128,768]{1,0:T(8,128)(2,1)}, bf16[128,768]{1,0:T(8,128)(2,1)S(1)}, u32[]{:S(2)}, u32[]{:S(2)}) collective-permute-start(bf16[128,768]{1,0:T(8,128)(2,1)} %collective-permute-done.12), channel_id=1, source_target_pairs={{0,1},{1,0},{2,3},{3,2},{4,5},{5,4},{6,7},{7,6},{8,9},{9,8},{10,11... | collective-permute-start | bytes 589832 | tf_op jit(solution)/shard_map/ppermute | solution.py:34
  225.4 8.0 %collective-permute-start.15 = (bf16[128,768]{1,0:T(8,128)(2,1)}, bf16[128,768]{1,0:T(8,128)(2,1)S(1)}, u32[]{:S(2)}, u32[]{:S(2)}) collective-permute-start(bf16[128,768]{1,0:T(8,128)(2,1)} %collective-permute-done.14), channel_id=1, source_target_pairs={{0,1},{1,0},{2,3},{3,2},{4,5},{5,4},{6,7},{7,6},{8,9},{9,8},{10,11... | collective-permute-start | bytes 589832 | tf_op jit(solution)/shard_map/ppermute | solution.py:34
  227.4 9.1 %collective-permute-start.17 = (bf16[128,768]{1,0:T(8,128)(2,1)S(1)}, bf16[128,768]{1,0:T(8,128)(2,1)S(1)}, u32[]{:S(2)}, u32[]{:S(2)}) collective-permute-start(bf16[128,768]{1,0:T(8,128)(2,1)S(1)} %collective-permute-done.16), channel_id=1, source_target_pairs={{0,1},{1,0},{2,3},{3,2},{4,5},{5,4},{6,7},{7,6},{8,9},{9,8},{10,11... | collective-permute-start | bytes 589832 | tf_op jit(solution)/shard_map/ppermute | solution.py:34
  251.3 20.4 %collective-permute-start.47 = (bf16[256,384]{0,1:T(8,128)(2,1)S(1)}, bf16[256,384]{0,1:T(8,128)(2,1)S(1)}, u32[]{:S(2)}, u32[]{:S(2)}) collective-permute-start(bf16[256,384]{0,1:T(8,128)(2,1)S(1)} %pad_maximum_fusion.11), channel_id=1, source_target_pairs={{0,1},{1,0},{2,3},{3,2},{4,5},{5,4},{6,7},{7,6},{8,9},{9,8},{10,11... | collective-permute-start | bytes 589832 | tf_op jit(solution)/shard_map/ppermute | solution.py:34
  252.3 22.8 %collective-permute-start.48 = (bf16[256,384]{0,1:T(8,128)(2,1)S(1)}, bf16[256,384]{0,1:T(8,128)(2,1)S(1)}, u32[]{:S(2)}, u32[]{:S(2)}) collective-permute-start(bf16[256,384]{0,1:T(8,128)(2,1)S(1)} %pad_maximum_fusion.11), channel_id=1, source_target_pairs={{0,2},{1,3},{2,4},{3,5},{4,6},{5,7},{6,0},{7,1},{8,10},{9,11},{10,... | collective-permute-start | bytes 589832 | tf_op jit(solution)/shard_map/ppermute | solution.py:34
  255.7 20.3 %collective-permute-start.50 = (bf16[256,384]{0,1:T(8,128)(2,1)S(1)}, bf16[256,384]{0,1:T(8,128)(2,1)S(1)}, u32[]{:S(2)}, u32[]{:S(2)}) collective-permute-start(bf16[256,384]{0,1:T(8,128)(2,1)S(1)} %pad_maximum_fusion.11), channel_id=1, source_target_pairs={{0,4},{1,5},{2,6},{3,7},{4,0},{5,1},{6,2},{7,3},{8,12},{9,13},{10,... | collective-permute-start | bytes 589832 | tf_op jit(solution)/shard_map/ppermute | solution.py:34
  261.4 6.0 %collective-permute-start.36 = (f32[2,256]{1,0:T(2,128)S(1)}, f32[2,256]{1,0:T(2,128)S(1)}, u32[]{:S(2)}, u32[]{:S(2)}) collective-permute-start(f32[2,256]{1,0:T(2,128)S(1)} %pad_maximum_fusion.13), channel_id=1, source_target_pairs={{0,8},{8,0},{16,24},{24,16},{1,9},{9,1},{17,25},{25,17},{2,10},{10... | collective-permute-start | bytes 6152 | tf_op jit(solution)/shard_map/ppermute | solution.py:38
  271.1 12.1 %collective-permute-start.52 = (bf16[256,384]{0,1:T(8,128)(2,1)S(1)}, bf16[256,384]{0,1:T(8,128)(2,1)S(1)}, u32[]{:S(2)}, u32[]{:S(2)}) collective-permute-start(bf16[256,384]{0,1:T(8,128)(2,1)S(1)} %pad_maximum_fusion.11), channel_id=1, source_target_pairs={{0,6},{1,7},{2,0},{3,1},{4,2},{5,3},{6,4},{7,5},{8,14},{9,15},{10,... | collective-permute-start | bytes 589832 | tf_op jit(solution)/shard_map/ppermute | solution.py:34
  271.6 12.6 %collective-permute-start.55 = (bf16[256,384]{0,1:T(8,128)(2,1)}, bf16[256,384]{0,1:T(8,128)(2,1)}, u32[]{:S(2)}, u32[]{:S(2)}) collective-permute-start(bf16[256,384]{0,1:T(8,128)(2,1)} %pad_maximum_fusion.12), channel_id=1, source_target_pairs={{0,2},{1,3},{2,4},{3,5},{4,6},{5,7},{6,0},{7,1},{8,10},{9,11},{10,... | collective-permute-start | bytes 589832 | tf_op jit(solution)/shard_map/ppermute | solution.py:34
  275.1 14.8 %collective-permute-start.57 = (bf16[256,384]{0,1:T(8,128)(2,1)}, bf16[256,384]{0,1:T(8,128)(2,1)}, u32[]{:S(2)}, u32[]{:S(2)}) collective-permute-start(bf16[256,384]{0,1:T(8,128)(2,1)} %pad_maximum_fusion.12), channel_id=1, source_target_pairs={{0,4},{1,5},{2,6},{3,7},{4,0},{5,1},{6,2},{7,3},{8,12},{9,13},{10,... | collective-permute-start | bytes 589832 | tf_op jit(solution)/shard_map/ppermute | solution.py:34
  275.9 15.0 %collective-permute-start.59 = (bf16[256,384]{0,1:T(8,128)(2,1)}, bf16[256,384]{0,1:T(8,128)(2,1)}, u32[]{:S(2)}, u32[]{:S(2)}) collective-permute-start(bf16[256,384]{0,1:T(8,128)(2,1)} %pad_maximum_fusion.12), channel_id=1, source_target_pairs={{0,6},{1,7},{2,0},{3,1},{4,2},{5,3},{6,4},{7,5},{8,14},{9,15},{10,... | collective-permute-start | bytes 589832 | tf_op jit(solution)/shard_map/ppermute | solution.py:34
  283.2 9.8 %collective-permute-start.49 = (bf16[256,384]{0,1:T(8,128)(2,1)S(1)}, bf16[256,384]{0,1:T(8,128)(2,1)S(1)}, u32[]{:S(2)}, u32[]{:S(2)}) collective-permute-start(bf16[256,384]{0,1:T(8,128)(2,1)S(1)} %collective-permute-done.48), channel_id=1, source_target_pairs={{0,1},{1,0},{2,3},{3,2},{4,5},{5,4},{6,7},{7,6},{8,9},{9,8},{10,11... | collective-permute-start | bytes 589832 | tf_op jit(solution)/shard_map/ppermute | solution.py:34
  284.2 9.8 %collective-permute-start.51 = (bf16[256,384]{0,1:T(8,128)(2,1)S(1)}, bf16[256,384]{0,1:T(8,128)(2,1)S(1)}, u32[]{:S(2)}, u32[]{:S(2)}) collective-permute-start(bf16[256,384]{0,1:T(8,128)(2,1)S(1)} %collective-permute-done.50), channel_id=1, source_target_pairs={{0,1},{1,0},{2,3},{3,2},{4,5},{5,4},{6,7},{7,6},{8,9},{9,8},{10,11... | collective-permute-start | bytes 589832 | tf_op jit(solution)/shard_map/ppermute | solution.py:34
  289.9 20.1 %collective-permute-start.54 = (bf16[256,384]{0,1:T(8,128)(2,1)}, bf16[256,384]{0,1:T(8,128)(2,1)}, u32[]{:S(2)}, u32[]{:S(2)}) collective-permute-start(bf16[256,384]{0,1:T(8,128)(2,1)} %pad_maximum_fusion.12), channel_id=1, source_target_pairs={{0,1},{1,0},{2,3},{3,2},{4,5},{5,4},{6,7},{7,6},{8,9},{9,8},{10,11... | collective-permute-start | bytes 589832 | tf_op jit(solution)/shard_map/ppermute | solution.py:34
  291.0 11.2 %collective-permute-start.53 = (bf16[256,384]{0,1:T(8,128)(2,1)S(1)}, bf16[256,384]{0,1:T(8,128)(2,1)S(1)}, u32[]{:S(2)}, u32[]{:S(2)}) collective-permute-start(bf16[256,384]{0,1:T(8,128)(2,1)S(1)} %collective-permute-done.52), channel_id=1, source_target_pairs={{0,1},{1,0},{2,3},{3,2},{4,5},{5,4},{6,7},{7,6},{8,9},{9,8},{10,11... | collective-permute-start | bytes 589832 | tf_op jit(solution)/shard_map/ppermute | solution.py:34
  291.9 18.1 %collective-permute-start.56 = (bf16[256,384]{0,1:T(8,128)(2,1)}, bf16[256,384]{0,1:T(8,128)(2,1)}, u32[]{:S(2)}, u32[]{:S(2)}) collective-permute-start(bf16[256,384]{0,1:T(8,128)(2,1)} %collective-permute-done.55), channel_id=1, source_target_pairs={{0,1},{1,0},{2,3},{3,2},{4,5},{5,4},{6,7},{7,6},{8,9},{9,8},{10,11... | collective-permute-start | bytes 589832 | tf_op jit(solution)/shard_map/ppermute | solution.py:34
  293.0 18.2 %collective-permute-start.58 = (bf16[256,384]{0,1:T(8,128)(2,1)}, bf16[256,384]{0,1:T(8,128)(2,1)}, u32[]{:S(2)}, u32[]{:S(2)}) collective-permute-start(bf16[256,384]{0,1:T(8,128)(2,1)} %collective-permute-done.57), channel_id=1, source_target_pairs={{0,1},{1,0},{2,3},{3,2},{4,5},{5,4},{6,7},{7,6},{8,9},{9,8},{10,11... | collective-permute-start | bytes 589832 | tf_op jit(solution)/shard_map/ppermute | solution.py:34
  294.1 18.1 %collective-permute-start.60 = (bf16[256,384]{0,1:T(8,128)(2,1)}, bf16[256,384]{0,1:T(8,128)(2,1)}, u32[]{:S(2)}, u32[]{:S(2)}) collective-permute-start(bf16[256,384]{0,1:T(8,128)(2,1)} %collective-permute-done.59), channel_id=1, source_target_pairs={{0,1},{1,0},{2,3},{3,2},{4,5},{5,4},{6,7},{7,6},{8,9},{9,8},{10,11... | collective-permute-start | bytes 589832 | tf_op jit(solution)/shard_map/ppermute | solution.py:34
  302.2 19.4 %collective-permute-start.32 = (bf16[2,256,768]{2,1,0:T(8,128)(2,1)}, bf16[2,256,768]{2,1,0:T(8,128)(2,1)}, u32[]{:S(2)}, u32[]{:S(2)}) collective-permute-start(bf16[2,256,768]{2,1,0:T(8,128)(2,1)} %pad_maximum_fusion.4), channel_id=1, source_target_pairs={{0,8},{8,0},{16,24},{24,16},{1,9},{9,1},{17,25},{25,17},{2,10},{10... | collective-permute-start | bytes 2359304 | tf_op jit(solution)/shard_map/ppermute | solution.py:38
  310.0 28.9 %collective-permute-start.34 = (bf16[2,256,768]{2,1,0:T(8,128)(2,1)}, bf16[2,256,768]{2,1,0:T(8,128)(2,1)}, u32[]{:S(2)}, u32[]{:S(2)}) collective-permute-start(bf16[2,256,768]{2,1,0:T(8,128)(2,1)} %pad_maximum_fusion.5), channel_id=1, source_target_pairs={{0,8},{8,0},{16,24},{24,16},{1,9},{9,1},{17,25},{25,17},{2,10},{10... | collective-permute-start | bytes 2359304 | tf_op jit(solution)/shard_map/ppermute | solution.py:38
  310.1 20.3 %collective-permute-start.61 = (bf16[4,128,768]{1,2,0:T(8,128)(2,1)}, bf16[4,128,768]{1,2,0:T(8,128)(2,1)}, u32[]{:S(2)}, u32[]{:S(2)}) collective-permute-start(bf16[4,128,768]{1,2,0:T(8,128)(2,1)} %pad_maximum_fusion.6), channel_id=1, source_target_pairs={{0,1},{1,0},{2,3},{3,2},{4,5},{5,4},{6,7},{7,6},{8,9},{9,8},{10,11... | collective-permute-start | bytes 2359304 | tf_op jit(solution)/shard_map/ppermute | solution.py:34
  323.7 32.1 %collective-permute-start.33 = (bf16[256,768]{1,0:T(8,128)(2,1)}, bf16[256,768]{1,0:T(8,128)(2,1)}, u32[]{:S(2)}, u32[]{:S(2)}) collective-permute-start(bf16[256,768]{1,0:T(8,128)(2,1)} %fusion.26), channel_id=1, source_target_pairs={{0,16},{8,24},{16,0},{24,8},{1,17},{9,25},{17,1},{25,9},{2,18},{10... | collective-permute-start | bytes 1179656 | tf_op jit(solution)/shard_map/ppermute | solution.py:38
  331.7 10.5 %collective-permute-start.64 = (bf16[128,768]{0,1:T(8,128)(2,1)S(1)}, bf16[128,768]{0,1:T(8,128)(2,1)S(1)}, u32[]{:S(2)}, u32[]{:S(2)}) collective-permute-start(bf16[128,768]{0,1:T(8,128)(2,1)S(1)} %get-tuple-element.39), channel_id=1, source_target_pairs={{0,6},{1,7},{2,0},{3,1},{4,2},{5,3},{6,4},{7,5},{8,14},{9,15},{10,... | collective-permute-start | bytes 589832 | tf_op jit(solution)/shard_map/ppermute | solution.py:34
  336.2 18.0 %collective-permute-start.63 = (bf16[128,768]{0,1:T(8,128)(2,1)S(1)}, bf16[128,768]{0,1:T(8,128)(2,1)S(1)}, u32[]{:S(2)}, u32[]{:S(2)}) collective-permute-start(bf16[128,768]{0,1:T(8,128)(2,1)S(1)} %get-tuple-element.40), channel_id=1, source_target_pairs={{0,4},{1,5},{2,6},{3,7},{4,0},{5,1},{6,2},{7,3},{8,12},{9,13},{10,... | collective-permute-start | bytes 589832 | tf_op jit(solution)/shard_map/ppermute | solution.py:34
  336.9 17.3 %collective-permute-start.62 = (bf16[128,768]{0,1:T(8,128)(2,1)S(1)}, bf16[128,768]{0,1:T(8,128)(2,1)S(1)}, u32[]{:S(2)}, u32[]{:S(2)}) collective-permute-start(bf16[128,768]{0,1:T(8,128)(2,1)S(1)} %get-tuple-element.38), channel_id=1, source_target_pairs={{0,2},{1,3},{2,4},{3,5},{4,6},{5,7},{6,0},{7,1},{8,10},{9,11},{10,... | collective-permute-start | bytes 589832 | tf_op jit(solution)/shard_map/ppermute | solution.py:34
  340.7 17.6 %collective-permute-start.35 = (bf16[256,768]{1,0:T(8,128)(2,1)}, bf16[256,768]{1,0:T(8,128)(2,1)}, u32[]{:S(2)}, u32[]{:S(2)}) collective-permute-start(bf16[256,768]{1,0:T(8,128)(2,1)} %fusion.19), channel_id=1, source_target_pairs={{0,16},{8,24},{16,0},{24,8},{1,17},{9,25},{17,1},{25,9},{2,18},{10... | collective-permute-start | bytes 1179656 | tf_op jit(solution)/shard_map/ppermute | solution.py:38
  (64 other events, 470.5 us)

commit v2 on v1

--- a/solution.py
+++ b/solution.py
@@ -3,11 +3,15 @@
 import jax
 import jax.numpy as jnp
 from jax import lax
+from jax.experimental import pallas as pl
+from jax.experimental.pallas import tpu as pltpu
 from jax.sharding import PartitionSpec as P
 
 HEAD_SIZE = 128
 BF = jnp.bfloat16
 F32 = jnp.float32
+SLOTS = 3
+VMEM_BYTES = 50 * 1024 * 1024
 
 
 def rms_scale(values, gain):
@@ -69,7 +73,7 @@
     return kept[0] + got[0].astype(F32) + far.astype(F32)
 
 
-def local(
+def local_general(
     caption_states,
     caption_lens,
     text_gain,
@@ -289,6 +293,445 @@
     return (updated, input_grad, query_grad, out_weight_grad, key_grad, value_grad)
 
 
+def after(value, *others):
+    return lax.optimization_barrier((value, *others))[0]
+
+
+def call(body, out_shape, operands, scalars, scratch=(), flops=0):
+    shapes = jax.tree.leaves(out_shape)
+    moved = sum(math.prod(a.shape) * a.dtype.itemsize for a in (*operands, *shapes))
+    specs = [pl.BlockSpec(memory_space=pltpu.SMEM)] * scalars
+    specs += [pl.BlockSpec(memory_space=pltpu.VMEM)] * (len(operands) - scalars)
+    return pl.pallas_call(
+        body,
+        out_shape=out_shape,
+        in_specs=specs,
+        out_specs=jax.tree.map(lambda _: pl.BlockSpec(memory_space=pltpu.VMEM), out_shape),
+        scratch_shapes=list(scratch),
+        compiler_params=pltpu.CompilerParams(vmem_limit_bytes=VMEM_BYTES),
+        cost_estimate=pl.CostEstimate(flops=flops, bytes_accessed=moved, transcendentals=0),
+    )(*operands)
+
+
+def shaped(shape, dtype=BF):
+    return jax.ShapeDtypeStruct(shape, dtype)
+
+
+def aligned(start, unit):
+    return pl.multiple_of(start, unit)
+
+
+def prepare_video(video_states, out_grad, place, pairs, part):
+    tokens, model_width = video_states.shape
+    rows = tokens // 4
+
+    def body(place_ref, video_ref, grad_ref, normed_ref, mean_ref, inverse_ref, *tile_refs):
+        @pl.loop(0, tokens // 32)
+        def _(step):
+            here = pl.ds(aligned(step * 32, 32), 32)
+            values = video_ref[here, :].astype(F32)
+            mean = jnp.mean(values, axis=-1, keepdims=True)
+            center = values - mean
+            inverse = lax.rsqrt(jnp.mean(center * center, axis=-1, keepdims=True) + 1e-06)
+            normed_ref[here, :] = (center * inverse).astype(BF)
+            mean_ref[here, :] = mean
+            inverse_ref[here, :] = inverse
+
+        z, y, g = place_ref[0], place_ref[1], place_ref[2]
+        mine = pl.ds(aligned(g * rows, rows), rows)
+        for far in range(pairs):
+            for side in range(2):
+                to = lax.rem(z + far, pairs) * 2 + (y ^ side)
+                columns = pl.ds(aligned(to * part, 128), part)
+                tile_refs[far][side, 0] = normed_ref[mine, columns]
+                tile_refs[far][side, 1] = grad_ref[mine, columns]
+
+    out = [shaped((tokens, model_width)), shaped((tokens, 1), F32), shaped((tokens, 1), F32)]
+    out += [shaped((2, 2, rows, part))] * pairs
+    normed, mean, inverse, *tiles = call(body, out, (place, video_states, out_grad), 1)
+    return normed, mean, inverse, tiles
+
+
+def project_rows(normed, out_grad, blocks, place, pairs, part):
+    tokens = normed.shape[0]
+    width = blocks[0].shape[1]
+
+    def body(place_ref, normed_ref, grad_ref, *refs):
+        block_refs, (query_ref, d_ref, sum_ref) = refs[:-3], refs[-3:]
+        z, y = place_ref[0], place_ref[1]
+        query = jnp.zeros((tokens, width), F32)
+        d_attended = jnp.zeros((tokens, width), F32)
+        total = jnp.zeros((1, width), F32)
+        for far in range(pairs):
+            for side in range(2):
+                block = block_refs[2 * far + side]
+                origin = lax.rem(z - far + pairs, pairs) * 2 + (y ^ side)
+                columns = pl.ds(aligned(origin * part, 128), part)
+                weight = block[:part, :]
+                query += mm(normed_ref[:, columns], weight)
+                d_attended += contract_last(grad_ref[:, columns], block[part : part + width, :])
+                total += jnp.sum(weight.astype(F32), axis=0, keepdims=True)
+        query_ref[...] = query.astype(BF)
+        d_ref[...] = d_attended.astype(BF)
+        sum_ref[...] = total
+
+    out = [shaped((tokens, width)), shaped((tokens, width)), shaped((1, width), F32)]
+    flops = 4 * tokens * width * normed.shape[1]
+    return call(body, out, (place, normed, out_grad, *blocks), 1, flops=flops)
+
+
+def project_captions(parts, own_key, own_value, side_block, place, pairs, skip):
+    quarter_rows, depth = parts[0].shape[1:]
+    half = depth // 2
+    width = own_key.shape[1]
+
+    def body(place_ref, *refs):
+        part_refs = refs[:4]
+        key_ref, value_ref, side_ref = refs[4:7]
+        out_refs = refs[7:]
+        y = place_ref[1]
+        mine = pl.ds(aligned(y * half, 128), half)
+        theirs = pl.ds(aligned((1 - y) * half, 128), half)
+        own = jnp.concatenate([r[far, :, mine] for far in range(pairs) for r in part_refs], 0)
+        other = jnp.concatenate([r[far, :, theirs] for far in range(pairs) for r in part_refs], 0)
+        keys = mm(own, key_ref[...]) + mm(other, side_ref[skip : skip + half, :])
+        values = mm(own, value_ref[...]) + mm(other, side_ref[skip + half : skip + 2 * half, :])
+        for far in range(pairs):
+            rows = slice(far * 4 * quarter_rows, (far + 1) * 4 * quarter_rows)
+            out_refs[far][:, :width] = keys[rows].astype(BF)
+            out_refs[far][:, width:] = values[rows].astype(BF)
+
+    out = [shaped((4 * quarter_rows, 2 * width))] * pairs
+    flops = 4 * pairs * 4 * quarter_rows * depth * width
+    operands = (place, *parts, own_key, own_value, side_block)
+    return call(body, out, operands, 1, flops=flops)
+
+
+def attend(queries, d_attended, column_sum, kv_blocks, place, counts, sample_caption, lens, pairs):
+    tokens, width = queries.shape
+    cap_len = kv_blocks[0].shape[0]
+    heads = width // HEAD_SIZE
+    captions = counts.shape[0]
+    keys_wide = SLOTS * cap_len
+    cap_quarter, row_quarter = cap_len // 4, tokens // 4
+    scale = 1.0 / math.sqrt(HEAD_SIZE)
+
+    def body(place_ref, count_ref, caption_ref, len_ref, q_ref, da_ref, sum_ref, *refs):
+        block_refs = refs[: len(kv_blocks)]
+        both_ref, att_ref, dq_ref, rows_ref, own_ref, away_ref, kv_ref = refs[len(kv_blocks) :]
+        z, y, g = place_ref[0], place_ref[1], place_ref[2]
+        base = (z * 2 + y) * tokens
+
+        def find(sample, carry):
+            total, first, start = carry
+            total = total + count_ref[sample]
+            past = total <= base
+            return total, first + past.astype(jnp.int32), jnp.where(past, total, start)
+
+        zero = jnp.int32(0)
+        _, first, start = lax.fori_loop(0, captions, find, (zero, zero, zero))
+        low, high, length, far_to, side_to, valid = [], [], [], [], [], []
+        edge = start - base
+        for slot in range(SLOTS):
+            ok = first + slot < captions
+            sample = jnp.minimum(first + slot, captions - 1)
+            caption = caption_ref[sample]
+            low.append(edge)
+            edge = edge + jnp.where(ok, count_ref[sample], 0)
+            high.append(edge)
+            length.append(len_ref[caption])
+            far_to.append(lax.rem(caption // 2 - z + pairs, pairs))
+            side_to.append(lax.rem(caption, 2) ^ y)
+            valid.append(ok)
+            entry = lax.rem(z - caption // 2 + pairs, pairs) * 2 + side_to[slot]
+            for number, block in enumerate(block_refs):
+
+                @pl.when(entry == number)
+                def _(slot=slot, block=block):
+                    kv_ref[slot * cap_len : (slot + 1) * cap_len, :] = block[...]
+
+        token = lax.broadcasted_iota(jnp.int32, (tokens, keys_wide), 0)
+        column = lax.broadcasted_iota(jnp.int32, (tokens, keys_wide), 1)
+        slot_of = column // cap_len
+        inside = column % cap_len
+        key = ((inside // cap_quarter) ^ g) * cap_quarter + inside % cap_quarter
+
+        def of_slot(values):
+            return jnp.where(slot_of == 0, values[0], jnp.where(slot_of == 1, values[1], values[2]))
+
+        live = (token >= of_slot(low)) & (token < of_slot(high)) & (key < of_slot(length))
+        own_ref[...] = jnp.zeros_like(own_ref)
+        away_ref[...] = jnp.zeros_like(away_ref)
+        first_sum = jnp.zeros((tokens, 1), F32)
+        second_sum = jnp.zeros((tokens, 1), F32)
+        for head in range(heads):
+            at = slice(head * HEAD_SIZE, (head + 1) * HEAD_SIZE)
+            at_value = slice(width + head * HEAD_SIZE, width + (head + 1) * HEAD_SIZE)
+            query, d_att = q_ref[:, at], da_ref[:, at]
+            keys, values = kv_ref[:, at], kv_ref[:, at_value]
+            grown = jnp.where(live, jnp.exp(contract_last(query, keys) * scale), 0.0)
+            weights = grown * (1.0 / jnp.sum(grown, axis=-1, keepdims=True))
+            probs = weights.astype(BF)
+            d_probs = contract_last(d_att, values)
+            mixed = jnp.sum(weights * d_probs, axis=-1, keepdims=True)
+            d_scores = (weights * (d_probs - mixed) * scale).astype(BF)
+            att_ref[:, at] = mm(probs, values).astype(BF)
+            d_query = mm(d_scores, keys).astype(BF)
+            dq_ref[:, at] = d_query
+            d_wide = d_query.astype(F32)
+            first_sum += jnp.sum(d_wide * sum_ref[:, at], axis=-1, keepdims=True)
+            second_sum += jnp.sum(d_wide * query.astype(F32), axis=-1, keepdims=True)
+            key_grad = contract_first(d_scores, query).astype(BF)
+            value_grad = contract_first(probs, d_att).astype(BF)
+            for slot in range(SLOTS):
+                for part in range(4):
+                    held = slice(
+                        slot * cap_len + part * cap_quarter, slot * cap_len + (part + 1) * cap_quarter
+                    )
+                    to = pl.ds(aligned((part ^ g) * cap_quarter, cap_quarter), cap_quarter)
+                    for side, target_ref in enumerate((own_ref, away_ref)):
+
+                        @pl.when(valid[slot] & (side_to[slot] == side))
+                        def _(slot=slot, held=held, to=to, target_ref=target_ref):
+                            target_ref[far_to[slot], to, at] = key_grad[held]
+                            target_ref[far_to[slot], to, at_value] = value_grad[held]
+
+        rows_ref[:, 0:1] = first_sum
+        rows_ref[:, 1:2] = second_sum
+        for part in range(4):
+            rows = pl.ds(aligned((part ^ g) * row_quarter, row_quarter), row_quarter)
+            to = slice(part * row_quarter, (part + 1) * row_quarter)
+            both_ref[0, to, :] = att_ref[rows, :]
+            both_ref[1, to, :] = dq_ref[rows, :]
+
+    out = [
+        shaped((2, tokens, width)),
+        shaped((tokens, width)),
+        shaped((tokens, width)),
+        shaped((tokens, 2), F32),
+        shaped((pairs, cap_len, 2 * width)),
+        shaped((pairs, cap_len, 2 * width)),
+    ]
+    operands = (place, counts, sample_caption, lens, queries, d_attended, column_sum, *kv_blocks)
+    scratch = [pltpu.VMEM((keys_wide, 2 * width), BF)]
+    return call(body, out, operands, 4, scratch, flops=12 * tokens * keys_wide * width)
+
+
+def project_back(attended, d_queries, blocks, place, pairs, part):
+    tokens, width = attended.shape
+    model_width = 2 * pairs * part
+    per_piece = 2 * pairs // 4
+
+    def body(place_ref, att_ref, dq_ref, *refs):
+        block_refs = refs[: len(blocks)]
+        halves = (refs[len(blocks) : len(blocks) + 2], refs[len(blocks) + 2 :])
+        z, y, g = place_ref[0], place_ref[1], place_ref[2]
+        att, d_query = att_ref[...], dq_ref[...]
+        for far in range(pairs):
+            for side in range(2):
+                block = block_refs[2 * far + side]
+                origin = lax.rem(z - far + pairs, pairs) * 2 + (y ^ side)
+                flip = (origin // per_piece) ^ g
+                start = ((flip // 2) * per_piece + lax.rem(origin, per_piece)) * part
+                columns = pl.ds(aligned(start, 128), part)
+                added = mm(att, block[part : part + width, :]).astype(BF)
+                d_normed = contract_last(d_query, block[:part, :]).astype(BF)
+                for number, (out_ref, d_ref) in enumerate(halves):
+
+                    @pl.when(lax.rem(flip, 2) == number)
+                    def _(out_ref=out_ref, d_ref=d_ref, added=added, d_normed=d_normed):
+                        out_ref[:, columns] = added
+                        d_ref[:, columns] = d_normed
+
+    out = [shaped((tokens, model_width // 2))] * 4
+    flops = 4 * tokens * width * model_width
+    return call(body, out, (place, attended, d_queries, *blocks), 1, flops=flops)
+
+
+def weight_grads(tiles, both_blocks, pairs):
+    part = tiles[0].shape[-1]
+    width = both_blocks[0].shape[-1]
+
+    def body(*refs):
+        tile_refs, block_refs, (query_ref, out_ref) = refs[:4], refs[4:-2], refs[-2:]
+        query_grad = jnp.zeros((part, width), F32)
+        out_grad = jnp.zeros((width, part), F32)
+        for far in range(pairs):
+            for side in range(2):
+                block = block_refs[2 * far + side]
+                normed, grad = (
+                    jnp.concatenate([r[far, side, which] for r in tile_refs], axis=0)
+                    for which in range(2)
+                )
+                out_grad += contract_first(block[0], grad)
+                query_grad += contract_first(normed, block[1])
+        query_ref[...] = query_grad
+        out_ref[...] = out_grad
+
+    out = [shaped((part, width), F32), shaped((width, part), F32)]
+    flops = 4 * 2 * pairs * both_blocks[0].shape[1] * part * width
+    return call(body, out, (*tiles, *both_blocks), 0, flops=flops)
+
+
+def local(
+    caption_states,
+    caption_lens,
+    text_gain,
+    text_query,
+    text_key,
+    text_value,
+    text_bias,
+    text_out,
+    final_gain,
+    cross_key,
+    cross_value,
+    video_states,
+    video_counts,
+    sample_caption,
+    cross_query,
+    cross_out,
+    out_grad,
+):
+    column = lax.axis_index("fsdp")
+    g = lax.axis_index("grp")
+    pairs = lax.axis_size("fsdp") // 2
+    z, y = column // 2, column % 2
+    place = jnp.stack([z, y, g]).astype(jnp.int32)
+    caps_local, cap_len, text_width = caption_states.shape
+    tokens, model_width = video_states.shape
+    width_local = cross_key.shape[1]
+    part = cross_query.shape[0]
+
+    own_weights = jnp.concatenate([cross_query, cross_out], axis=0)
+    ring = [own_weights, fsend(own_weights, 1, 0)]
+    side_block = fsend(jnp.concatenate([own_weights, cross_key, cross_value], axis=0), 0, 1)
+
+    local_lens = lax.dynamic_slice_in_dim(caption_lens, column * caps_local, caps_local)
+    flat_states = caption_states.reshape(caps_local * cap_len, text_width).astype(F32)
+    text_normed = rms_scale(flat_states, text_gain).astype(BF)
+    local_heads = text_bias.shape[0]
+    head_width = text_query.shape[1] // local_heads
+
+    def heads_of(weight):
+        return mm(text_normed, weight).astype(BF).reshape(
+            caps_local, cap_len, local_heads, head_width
+        )
+
+    text_queries = heads_of(text_query)
+    text_keys = heads_of(text_key)
+    text_values = heads_of(text_value)
+    text_scores = (
+        jnp.einsum("cihd,cjhd->chij", text_queries, text_keys, preferred_element_type=F32)
+        + text_bias[None]
+    )
+    key_valid = jnp.arange(cap_len, dtype=jnp.int32)[None, :] < local_lens[:, None]
+    exp_scores = jnp.where(key_valid[:, None, None, :], jnp.exp(text_scores), 0.0)
+    text_weights = (exp_scores / jnp.sum(exp_scores, axis=-1, keepdims=True)).astype(BF)
+    text_mixed = jnp.einsum(
+        "chij,cjhd->cihd", text_weights, text_values, preferred_element_type=F32
+    )
+    text_mixed = text_mixed.astype(BF).reshape(caps_local * cap_len, local_heads * head_width)
+    text_mixed = jnp.concatenate([quarter(text_mixed, g ^ k) for k in (0, 2, 1, 3)], axis=0)
+    partial_text = mm(text_mixed, text_out).astype(BF)
+    partial_text = after(partial_text, ring[1])
+    half_rows = partial_text.shape[0] // 2
+    quarter_rows = half_rows // 2
+    got = gsend(partial_text[half_rows:], 1).astype(F32)
+    normed, mean, inverse, tiles = prepare_video(
+        after(video_states, partial_text), out_grad, place, pairs, part
+    )
+    ring.append(fsend(after(ring[1], partial_text), 1, 0))
+    kept = partial_text[:half_rows].astype(F32) + got
+    text_rows = kept[:quarter_rows] + gsend(kept[quarter_rows:].astype(BF), 2).astype(F32)
+    encoded = rms_scale(quarter(flat_states, g) + text_rows, final_gain).astype(BF)
+    encoded = after(encoded, ring[2], normed)
+
+    depth = text_width // pairs
+    pieces = [
+        lax.dynamic_slice_in_dim(encoded, ((z + far) % pairs) * depth, depth, 1)
+        for far in range(pairs)
+    ]
+    mine = jnp.stack([fsend(p, far, 0) if far else p for far, p in enumerate(pieces)])
+    over_x = gsend(mine, 2)
+    parts = [mine, gsend(mine, 1), over_x, gsend(over_x, 1)]
+    current = after(ring[2], mine)
+    for far in range(3, pairs):
+        current = fsend(current, 1, 0)
+        ring.append(current)
+    blocks = [own_weights, side_block]
+    for block in ring[1:]:
+        blocks += [block, fsend(block, 0, 1)]
+
+    kv_partial = project_captions(
+        parts, cross_key, cross_value, side_block, place, pairs, own_weights.shape[0]
+    )
+    kv_partial = after(tuple(kv_partial), ring[-1])
+    kv_sum = kv_partial[0].astype(F32)
+    for far in range(1, pairs):
+        kv_sum += fsend(kv_partial[far], pairs - far, 0).astype(F32)
+    kv_blocks = gather_direct(kv_sum.astype(BF))
+
+    queries, d_attended, column_sum = project_rows(normed, out_grad, blocks, place, pairs, part)
+
+    tiles = after(tuple(tiles), kv_blocks[-2])
+    over_z = [fsend(t, far, 0) if far else t for far, t in enumerate(tiles)]
+    over_y = fsend(jnp.stack([t[1] for t in over_z]), 0, 1)
+    tiles = jnp.stack([jnp.stack([t[0] for t in over_z]), over_y], axis=1)
+    tiles_x = gsend(tiles, 2)
+    tiles = [tiles, gsend(tiles, 1), tiles_x, gsend(tiles_x, 1)]
+
+    both, attended, d_queries, row_sums, kv_own, kv_away = attend(
+        queries,
+        d_attended,
+        column_sum,
+        kv_blocks,
+        place,
+        video_counts,
+        sample_caption,
+        caption_lens,
+        pairs,
+    )
+    kv_side = fsend(kv_away, 0, 1)
+    both_blocks = gather_ring(both)
+    row_sums = row_sums + gsend(row_sums, 1)
+    row_sums = (row_sums + gsend(row_sums, 2)) / model_width
+
+    out_kept, d_kept, out_away, d_away = project_back(
+        attended, d_queries, blocks, place, pairs, part
+    )
+    slice_width = model_width // 4
+
+    def finish(kept, away):
+        kept = kept.astype(F32) + gsend(away, 1).astype(F32)
+        sent = gsend(kept[:, slice_width:].astype(BF), 2)
+        return kept[:, :slice_width] + sent.astype(F32)
+
+    video = quarter(video_states, g, 1).astype(F32)
+    updated = (video + finish(out_kept, out_away)).astype(BF)
+    video_hat = (video - mean) * inverse
+    d_share = finish(d_kept, d_away)
+    input_grad = (
+        quarter(out_grad, g, 1).astype(F32)
+        + inverse * (d_share - row_sums[:, 0:1] - video_hat * row_sums[:, 1:2])
+    ).astype(BF)
+
+    kv_terms = kv_own.astype(F32) + kv_side.astype(F32)
+    kv_grads = kv_terms[0]
+    for far in range(1, pairs):
+        kv_grads += fsend(kv_terms[far].astype(BF), far, 0).astype(F32)
+    kv_grads = kv_grads.astype(BF)[None]
+    key_grad = kv_grads[:, :, :width_local]
+    value_grad = kv_grads[:, :, width_local:]
+
+    query_grad, out_weight_grad = weight_grads(tiles, both_blocks, pairs)
+    return (updated, input_grad, query_grad, out_weight_grad, key_grad, value_grad)
+
+
+def local_of(*arrays):
+    cross_query = arrays[14]
+    return local_general(*arrays) if cross_query.shape[0] % 128 else local(*arrays)
+
+
 def solution(mesh):
     in_specs = (
         P("fsdp", None, None),
@@ -317,4 +760,6 @@
         P("fsdp", None, "grp"),
         P("fsdp", None, "grp"),
     )
-    return jax.shard_map(local, mesh=mesh, in_specs=in_specs, out_specs=out_specs, check_vma=False)
+    return jax.shard_map(
+        local_of, mesh=mesh, in_specs=in_specs, out_specs=out_specs, check_vma=False
+    )

time: 363 us -> 241 us (0.66)
  local copies, waits for them, and re-layouts: 49.9 us -> 10.5 us
  starting transfers between devices: 79.9 us -> 45.1 us
  other arithmetic: 48.4 us -> 17.6 us
  Pallas kernels: 0 us -> 26.5 us
  matrix products: 32.7 us -> 12.5 us
  waiting for transfers between devices: 138 us -> 127 us
  between operations: 11.9 us -> 1.2 us
    ppermute x53 -> x35, starting transfers between devices: 71.1 us -> 38.1 us  [fsend(): return lax.ppermute(block, 'fsdp', perm)]
    pallas_call x0 -> x6, Pallas kernels: none -> 26.5 us  [call(): pl.pallas_call(body, out_shape=out_shape, in_specs=specs, out_specs=jax.t...]
    ppermute x53 -> x35, waiting for transfers between devices: 135 us -> 116 us  [fsend(): return lax.ppermute(block, 'fsdp', perm)]
    unnamed x143 -> x50, local copies, waits for them, and re-layouts: 21.8 us -> 3.25 us
    dot_general x10 -> x0, matrix products: 13.9 us -> none  [the longest x2 5.66 us: contract_first(): lax.dot_general(left, right, (((0,), (0,)), ((), ())), preferred_element_...]
    convert_element_type x9 -> x1, other arithmetic: 10.1 us -> 0.1 us  [local(): kv_blocks = gather_direct(kv_sum.astype(BF))]
    another operation x12 -> x5, other arithmetic: 11 us -> 3.1 us  [the longest x2 2.18 us: local(): tiles = jnp.stack([jnp.stack([t[0] for t in over_z]), over_y], axis=1)]
    dynamic_update_slice x15 -> x0, local copies, waits for them, and re-layouts: 7.75 us -> none  [the longest x8 5.48 us: local(): lax.dynamic_update_slice(full_out, out_blocks[2 * far + side], (jnp.int32...]
  transfers between devices with their start and end apart: 65 -> 49, of which waited for: 29 -> 25; matrix products, arithmetic and copies ran while one was open for 34% -> 15% of each run, Pallas kernels for 0% -> 9%
where the time goes in v2:
time: 241 us; the launch traced here: 240 us
  waiting for transfers between devices  127 us (53%)
  starting transfers between devices  45.1 us (19%)
  Pallas kernels  26.5 us (11%)
  other arithmetic  17.6 us (7%)
  matrix products  12.5 us (5%)
  local copies, waits for them, and re-layouts  10.5 us (4%)
    ppermute x35, waiting for transfers between devices, fsend(): return lax.ppermute(block, 'fsdp', perm)  116 us
    ppermute x35, starting transfers between devices, fsend(): return lax.ppermute(block, 'fsdp', perm)  38.1 us
    pallas_call x6, Pallas kernels, call(): pl.pallas_call(body, out_shape=out_shape, in_specs=specs, out_specs=jax.t...  26.5 us
    dot_general x4, matrix products, mm(): return jnp.dot(left, right, preferred_element_type=F32)  12 us
    ppermute x14, waiting for transfers between devices, gsend(): lax.ppermute(block, 'grp', [(s, s ^ flip) for s in range(lax.axis_size('g...  10.9 us
    ppermute x14, starting transfers between devices, gsend(): lax.ppermute(block, 'grp', [(s, s ^ flip) for s in range(lax.axis_size('g...  6.95 us
  transfers between devices with their start and end apart: 49, of which 25 were waited for; matrix products, arithmetic and copies ran while one was open for 15% of the time, Pallas kernels for 9%

profile of v2, /device:TPU:0, one launch (start us, length us, event | category | flops | bytes accessed | tf_op | source)
XLA Modules:
  0.0 240.1 jit_solution(10852656448260502231)
XLA Ops:
  0.7 1.1 constant_dynamic-update-slice_fusion.1
  2.8 3.1 %collective-permute-start = (bf16[768,384]{1,0:T(8,128)(2,1)S(1)}, bf16[768,384]{1,0:T(8,128)(2,1)S(1)}, u32[]{:S(2)}, u32[]{:S(2)}) collective-permute-start(bf16[768,384]{1,0:T(8,128)(2,1)S(1)} %constant_dynamic-update-slice_fusion.refs_0_), channel_id=1, source_target_pairs={{0,2},{1,3},{2,4},{3,5},{4,6},{5,7},{6,0},{7,1},{8,10},{9,11},{10,... | collective-permute-start | bytes 1769480 | tf_op jit(solution)/shard_map/ppermute | solution.py:38
  5.8 1.2 dynamic_slice.39
  7.7 1.5 fusion
  9.3 2.9 %convolution_convert_fusion.3 = bf16[128,512]{1,0:T(8,128)(2,1)S(1)} fusion(bf16[4096,512]{1,0:T(8,128)(2,1)} %param.20, f32[4096]{0:T(1024)S(1)} %copy-done.23, f32[128]{0:T(128)S(1)} %add_rsqrt_fusion.1, bf16[1,128,4096]{2,1,0:T(8,128)(2,1)S(1)} %copy-done.12), kind=kOutput, calls=%fused_computation.15 | convolution fusion | flops 539033600 | bytes 5390848 | tf_op jit(solution)/shard_map/dot_general | solution.py:23
  12.3 3.0 %convolution_convert_fusion.2 = bf16[128,512]{1,0:T(8,128)(2,1)S(1)} fusion(bf16[4096,512]{1,0:T(8,128)(2,1)} %param.21, f32[4096]{0:T(1024)S(1)} %copy-done.23, f32[128]{0:T(128)S(1)} %add_rsqrt_fusion.1, bf16[1,128,4096]{2,1,0:T(8,128)(2,1)S(1)} %copy-done.12), kind=kOutput, calls=%fused_computation.14 | convolution fusion | flops 539033600 | bytes 5390848 | tf_op jit(solution)/shard_map/dot_general | solution.py:23
  15.4 3.0 %convolution_convert_fusion.4 = bf16[128,512]{1,0:T(8,128)(2,1)S(1)} fusion(bf16[4096,512]{1,0:T(8,128)(2,1)} %param.22, f32[4096]{0:T(1024)S(1)} %copy-done.23, f32[128]{0:T(128)S(1)} %add_rsqrt_fusion.1, bf16[1,128,4096]{2,1,0:T(8,128)(2,1)S(1)} %copy-done.12), kind=kOutput, calls=%fused_computation.16 | convolution fusion | flops 539033600 | bytes 5390848 | tf_op jit(solution)/shard_map/dot_general | solution.py:23
  19.6 3.1 %convolution_convert_fusion = bf16[128,4096]{1,0:T(8,128)(2,1)S(1)} fusion(bf16[512,4096]{1,0:T(8,128)(2,1)} %param.24, bf16[32,512]{0,1:T(8,128)(2,1)S(1)} %get-tuple-element.108, bf16[32,512]{0,1:T(8,128)(2,1)S(1)} %get-tuple-element.109, bf16[32,512]{0,1:T(8,128)(2,1)S(1)} %get-tuple-element.110, bf16[32,512]{0,1:T(8,128)(2,1)S(1)} %get-tuple-element.107), kind=kOutput, calls=%fused_computation | convolution fusion | flops 537919488 | bytes 5373952 | tf_op jit(solution)/shard_map/dot_general | solution.py:23
  22.8 1.9 collective-permute-done.5
  26.5 1.5 collective-permute-start.6
  28.0 1.3 pad_maximum_fusion
  29.3 1.5 collective-permute-start.1
  30.8 2.8 %convert_element_type.125 = f32[1,128,4096]{2,1,0:T(8,128)} convert(bf16[1,128,4096]{2,1,0:T(8,128)(2,1)} %param.17) | non-fusion elementwise | flops 524288 | bytes 3145728 | tf_op jit(solution)/shard_map/convert_element_type | solution.py:610
  33.7 1.6 collective-permute-start.3
  35.2 4.1 %shard_map.208 = (bf16[256,3072]{1,0:T(8,128)(2,1)S(1)}, f32[256,1]{1,0:T(8,128)S(1)}, f32[256,1]{1,0:T(8,128)S(1)}, bf16[2,2,64,384]{3,2,1,0:T(8,128)(2,1)S(1)}...) custom-call(s32[3]{0:T(128)S(1)} %pad_add_fusion.place_ref, ...), custom_call_target="tpu_custom_call" | custom-call | bytes 5507084 | tf_op jit(solution)/shard_map/pallas_call | solution.py:305
  39.4 1.4 multiply_reduce_fusion
  40.8 1.1 multiply_convert_fusion
  41.8 8.4 %collective-permute-done.3.refs_4_ = bf16[768,384]{1,0:T(8,128)(2,1)S(1)} collective-permute-done((bf16[768,384]{1,0:T(8,128)(2,1)S(1)}, bf16[768,384]{1,0:T(8,128)(2,1)S(1)}, u32[]{:S(2)}, u32[]{:S(2)}) %collective-permute-start.3) | collective-permute-done | bytes 589856 | tf_op jit(solution)/shard_map/ppermute | solution.py:38
  51.6 1.6 collective-permute-start.7
  53.2 1.5 collective-permute-done.9
  54.7 3.1 %collective-permute-done.8 = bf16[32,1024]{1,0:T(8,128)(2,1)S(1)} collective-permute-done((bf16[32,1024]{1,0:T(8,128)(2,1)S(1)}, bf16[32,1024]{1,0:T(8,128)(2,1)S(1)}, u32[]{:S(2)}, u32[]{:S(2)}) %collective-permute-start.8) | collective-permute-done | bytes 65568 | tf_op jit(solution)/shard_map/ppermute | solution.py:38
  58.5 5.8 %collective-permute-done.13.refs_2_ = bf16[4,32,1024]{2,1,0:T(8,128)(2,1)S(1)} collective-permute-done((bf16[4,32,1024]{2,1,0:T(8,128)(2,1)S(1)}, bf16[4,32,1024]{2,1,0:T(8,128)(2,1)S(1)}, u32[]{:S(2)}, u32[]{:S(2)}) %collective-permute-start.13) | collective-permute-done | bytes 262176 | tf_op jit(solution)/shard_map/ppermute | solution.py:42
  64.3 1.5 collective-permute-done.14.refs_3_
  65.8 1.8 shard_map.210
  67.7 5.5 %collective-permute-done.10.refs_6_ = bf16[768,384]{1,0:T(8,128)(2,1)S(1)} collective-permute-done((bf16[768,384]{1,0:T(8,128)(2,1)S(1)}, bf16[768,384]{1,0:T(8,128)(2,1)S(1)}, u32[]{:S(2)}, u32[]{:S(2)}) %collective-permute-start.10) | collective-permute-done | bytes 589856 | tf_op jit(solution)/shard_map/ppermute | solution.py:38
  73.3 2.0 collective-permute-start.17
  76.4 1.0 collective-permute-start.4
  77.4 3.6 %collective-permute-done.15 = bf16[128,768]{1,0:T(8,128)(2,1)S(1)} collective-permute-done((bf16[128,768]{1,0:T(8,128)(2,1)S(1)}, bf16[128,768]{1,0:T(8,128)(2,1)S(1)}, u32[]{:S(2)}, u32[]{:S(2)}) %collective-permute-start.15) | collective-permute-done | bytes 196640 | tf_op jit(solution)/shard_map/ppermute | solution.py:38
  81.0 8.8 %collective-permute-done.16 = bf16[128,768]{1,0:T(8,128)(2,1)S(1)} collective-permute-done((bf16[128,768]{1,0:T(8,128)(2,1)S(1)}, bf16[128,768]{1,0:T(8,128)(2,1)S(1)}, u32[]{:S(2)}, u32[]{:S(2)}) %collective-permute-start.16) | collective-permute-done | bytes 196640 | tf_op jit(solution)/shard_map/ppermute | solution.py:38
  90.6 5.7 %collective-permute-done.23.refs_6_ = bf16[128,768]{1,0:T(8,128)(2,1)S(1)} collective-permute-done((bf16[128,768]{1,0:T(8,128)(2,1)S(1)}, bf16[128,768]{1,0:T(8,128)(2,1)S(1)}, u32[]{:S(2)}, u32[]{:S(2)}) %collective-permute-start.23) | collective-permute-done | bytes 196640 | tf_op jit(solution)/shard_map/ppermute | solution.py:38
  96.4 1.4 collective-permute-start.19
  98.5 5.8 %collective-permute-done.4.refs_5_ = bf16[768,384]{1,0:T(8,128)(2,1)S(1)} collective-permute-done((bf16[768,384]{1,0:T(8,128)(2,1)S(1)}, bf16[768,384]{1,0:T(8,128)(2,1)S(1)}, u32[]{:S(2)}, u32[]{:S(2)}) %collective-permute-start.4) | collective-permute-done | bytes 589856 | tf_op jit(solution)/shard_map/ppermute | solution.py:38
  104.3 1.3 collective-permute-start.31
  105.5 6.7 %collective-permute-done.21.refs_4_ = bf16[128,768]{1,0:T(8,128)(2,1)S(1)} collective-permute-done((bf16[128,768]{1,0:T(8,128)(2,1)S(1)}, bf16[128,768]{1,0:T(8,128)(2,1)S(1)}, u32[]{:S(2)}, u32[]{:S(2)}) %collective-permute-start.21) | collective-permute-done | bytes 196640 | tf_op jit(solution)/shard_map/ppermute | solution.py:38
  112.3 1.5 collective-permute-start.24
  114.3 1.5 collective-permute-done.11.refs_7_
  117.2 4.7 %shard_map.209 = (bf16[256,384]{1,0:T(8,128)(2,1)S(1)}, bf16[256,384]{1,0:T(8,128)(2,1)S(1)}, f32[1,384]{1,0:T(1,128)S(1)}) custom-call(s32[3]{0:T(128)S(1)} %pad_add_fusion.place_ref, bf16[256,3072]{1,0:T(8,128)(2,1)} %copy-done.1, bf16[256,3072]{1,0:T(8,128)(2,1)} %grad_ref.3, bf16[768,384]{1,0:T(8,128)(2,1)S(1)} %constant_dynamic-update-slice_fusion.refs_0_, ...), custom_call_target="tpu_custom_call" | custom-call | flops 1207959552 | bytes 9045516 | tf_op jit(solution)/shard_map/pallas_call | solution.py:305
  121.9 3.8 %collective-permute-start.32 = (bf16[2,2,64,384]{3,2,1,0:T(8,128)(2,1)S(1)}, bf16[2,2,64,384]{3,2,1,0:T(8,128)(2,1)S(1)}, u32[]{:S(2)}, u32[]{:S(2)}) collective-permute-start(bf16[2,2,64,384]{3,2,1,0:T(8,128)(2,1)S(1)} %get-tuple-element.77), channel_id=1, source_target_pairs={{0,4},{1,5},{2,6},{3,7},{4,0},{5,1},{6,2},{7,3},{8,12},{9,13},{10,... | collective-permute-start | bytes 589832 | tf_op jit(solution)/shard_map/ppermute | solution.py:38
  125.6 1.9 collective-permute-start.33
  127.6 2.1 collective-permute-done.20.refs_3_
  129.7 4.6 %shard_map.211 = (bf16[2,256,384]{2,1,0:T(8,128)(2,1)S(1)}, bf16[256,384]{1,0:T(8,128)(2,1)S(1)}, bf16[256,384]{1,0:T(8,128)(2,1)S(1)}, f32[256,2]{1,0:T(8,128)S...) custom-call(s32[3]{0:T(128)S(1)} %pad_add_fusion.place_ref, s32[8]{0:T(128)S(1)} %copy-done.6, ...), custom_call_target="tpu_custom_call" | custom-call | flops 452984832 | bytes 4329068 | tf_op jit(solution)/shard_map/pallas_call | solution.py:305
  134.4 1.2 collective-permute-start.45
  139.2 6.9 %shard_map.212 = (bf16[256,1536]{1,0:T(8,128)(2,1)}, bf16[256,1536]{1,0:T(8,128)(2,1)}, bf16[256,1536]{1,0:T(8,128)(2,1)}, bf16[256,1536]{1,0:T(8,128)(2,1)}) custom-call(s32[3]{0:T(128)S(1)} %pad_add_fusion.place_ref, bf16[256,384]{1,0:T(8,128)(2,1)S(1)} %get-tuple-element.62.att_ref, bf16[256,384]{1,0:T(8,128)(2,1)S(1)} %get-tuple-element.63.dq_ref, ...), custom_call_target="tpu_custom_call" | custom-call | flops 1207959552 | bytes 9043980 | tf_op jit(solution)/shard_map/pallas_call | solution.py:305
  147.3 1.1 maximum_bitcast_fusion
  148.6 1.2 collective-permute-start.38
  149.9 13.7 %collective-permute-done.34 = bf16[4,2,64,384]{3,2,1,0:T(8,128)(2,1)} collective-permute-done((bf16[4,2,64,384]{3,2,1,0:T(8,128)(2,1)}, bf16[4,2,64,384]{3,2,1,0:T(8,128)(2,1)}, u32[]{:S(2)}, u32[]{:S(2)}) %collective-permute-start.34) | collective-permute-done | bytes 393248 | tf_op jit(solution)/shard_map/ppermute | solution.py:38
  163.6 1.1 pad_maximum_fusion.1.refs_0_
  165.5 1.3 convert_add_fusion
  166.9 1.3 collective-permute-start.36
  168.2 1.4 convert_add_fusion.2
  169.7 1.4 collective-permute-done.30
  171.1 3.8 %collective-permute-start.48 = (bf16[128,768]{1,0:T(8,128)(2,1)S(1)}, bf16[128,768]{1,0:T(8,128)(2,1)S(1)}, u32[]{:S(2)}, u32[]{:S(2)}) collective-permute-start(bf16[128,768]{1,0:T(8,128)(2,1)S(1)} %get-tuple-element.91), channel_id=1, source_target_pairs={{0,6},{1,7},{2,0},{3,1},{4,2},{5,3},{6,4},{7,5},{8,14},{9,15},{10,... | collective-permute-start | bytes 589832 | tf_op jit(solution)/shard_map/ppermute | solution.py:38
  176.0 6.1 %collective-permute-done.41.refs_8_ = bf16[2,256,384]{2,1,0:T(8,128)(2,1)S(1)} collective-permute-done((bf16[2,256,384]{2,1,0:T(8,128)(2,1)S(1)}, bf16[2,256,384]{2,1,0:T(8,128)(2,1)S(1)}, u32[]{:S(2)}, u32[]{:S(2)}) %collective-permute-start.41) | collective-permute-done | bytes 393248 | tf_op jit(solution)/shard_map/ppermute | solution.py:38
  182.9 3.4 %collective-permute-done.46 = bf16[128,768]{1,0:T(8,128)(2,1)S(1)} collective-permute-done((bf16[128,768]{1,0:T(8,128)(2,1)S(1)}, bf16[128,768]{1,0:T(8,128)(2,1)S(1)}, u32[]{:S(2)}, u32[]{:S(2)}) %collective-permute-start.46) | collective-permute-done | bytes 196640 | tf_op jit(solution)/shard_map/ppermute | solution.py:38
  186.3 3.1 %collective-permute-done.48 = bf16[128,768]{1,0:T(8,128)(2,1)S(1)} collective-permute-done((bf16[128,768]{1,0:T(8,128)(2,1)S(1)}, bf16[128,768]{1,0:T(8,128)(2,1)S(1)}, u32[]{:S(2)}, u32[]{:S(2)}) %collective-permute-start.48) | collective-permute-done | bytes 196640 | tf_op jit(solution)/shard_map/ppermute | solution.py:38
  189.4 1.7 collective-permute-start.43
  191.3 14.9 %collective-permute-done.47 = bf16[128,768]{1,0:T(8,128)(2,1)S(1)} collective-permute-done((bf16[128,768]{1,0:T(8,128)(2,1)S(1)}, bf16[128,768]{1,0:T(8,128)(2,1)S(1)}, u32[]{:S(2)}, u32[]{:S(2)}) %collective-permute-start.47) | collective-permute-done | bytes 196640 | tf_op jit(solution)/shard_map/ppermute | solution.py:38
  206.9 1.3 collective-permute-start.40
  209.0 1.2 collective-permute-start.44
  210.9 2.3 fusion.11
  213.2 5.7 %collective-permute-done.40.refs_7_ = bf16[2,256,384]{2,1,0:T(8,128)(2,1)S(1)} collective-permute-done((bf16[2,256,384]{2,1,0:T(8,128)(2,1)S(1)}, bf16[2,256,384]{2,1,0:T(8,128)(2,1)S(1)}, u32[]{:S(2)}, u32[]{:S(2)}) %collective-permute-start.40) | collective-permute-done | bytes 393248 | tf_op jit(solution)/shard_map/ppermute | solution.py:38
  218.9 8.4 %collective-permute-done.42.refs_9_ = bf16[2,256,384]{2,1,0:T(8,128)(2,1)S(1)} collective-permute-done((bf16[2,256,384]{2,1,0:T(8,128)(2,1)S(1)}, bf16[2,256,384]{2,1,0:T(8,128)(2,1)S(1)}, u32[]{:S(2)}, u32[]{:S(2)}) %collective-permute-start.42) | collective-permute-done | bytes 393248 | tf_op jit(solution)/shard_map/ppermute | solution.py:38
  227.3 7.5 %collective-permute-done.44.refs_11_ = bf16[2,256,384]{2,1,0:T(8,128)(2,1)S(1)} collective-permute-done((bf16[2,256,384]{2,1,0:T(8,128)(2,1)S(1)}, bf16[2,256,384]{2,1,0:T(8,128)(2,1)S(1)}, u32[]{:S(2)}, u32[]{:S(2)}) %collective-permute-start.44) | collective-permute-done | bytes 393248 | tf_op jit(solution)/shard_map/ppermute | solution.py:38
  235.8 4.3 %shard_map.213 = (f32[384,384]{1,0:T(8,128)}, f32[384,384]{1,0:T(8,128)}) custom-call(bf16[4,2,2,64,384]{4,3,2,1,0:T(8,128)(2,1)S(1)} %pad_maximum_fusion.1.refs_0_, bf16[4,2,2,64,384]{4,3,2,1,0:T(8,128)(2,1)} %copy-done.17, bf16[4,2,2,64,384]{4,3,2,1,0:T(8,128)(2,1)} %copy-done.16, bf16[4,2,2,64,384]{4,3,2,1,0:T(8,128)(2,1)} %copy-done.18, ...), custom_call_target="tpu_custom_call" | custom-call | flops 1207959552 | bytes 7471104 | tf_op jit(solution)/shard_map/pallas_call | solution.py:305
  (138 shorter events, 22.7 us)
Async XLA Ops:
  0.6 8.6 %copy-start.12 = (bf16[1,128,4096]{2,1,0:T(8,128)(2,1)S(1)}, bf16[1,128,4096]{2,1,0:T(8,128)(2,1)}, u32[]{:S(2)}) copy-start(bf16[1,128,4096]{2,1,0:T(8,128)(2,1)} %param.17) | copy-start | bytes 3145732
  0.6 8.6 %copy-start.23 = (f32[4096]{0:T(1024)S(1)}, f32[4096]{0:T(1024)}, u32[]{:S(2)}) copy-start(f32[4096]{0:T(1024)} %param.19) | copy-start | bytes 49156
  2.8 19.9 %collective-permute-start = (bf16[768,384]{1,0:T(8,128)(2,1)S(1)}, bf16[768,384]{1,0:T(8,128)(2,1)S(1)}, u32[]{:S(2)}, u32[]{:S(2)}) collective-permute-start(bf16[768,384]{1,0:T(8,128)(2,1)S(1)} %constant_dynamic-update-slice_fusion.refs_0_), channel_id=1, source_target_pairs={{0,2},{1,3},{2,4},{3,5},{4,6},{5,7},{6,0},{7,1},{8,10},{9,11},{10,... | collective-permute-start | bytes 1769480 | tf_op jit(solution)/shard_map/ppermute | solution.py:38
  22.7 2.0 collective-permute-start.5
  26.5 12.8 %collective-permute-start.6 = (bf16[32,4096]{1,0:T(8,128)(2,1)}, bf16[32,4096]{1,0:T(8,128)(2,1)}, u32[]{:S(2)}, u32[]{:S(2)}) collective-permute-start(bf16[32,4096]{1,0:T(8,128)(2,1)} %slice.159), channel_id=1, source_target_pairs={{0,16},{8,24},{16,0},{24,8},{1,17},{9,25},{17,1},{25,9},{2,18},{10... | collective-permute-start | bytes 786440 | tf_op jit(solution)/shard_map/ppermute | solution.py:42
  29.3 35.0 %collective-permute-start.1 = (bf16[1792,384]{1,0:T(8,128)(2,1)}, bf16[1792,384]{1,0:T(8,128)(2,1)S(1)}, u32[]{:S(2)}, u32[]{:S(2)}) collective-permute-start(bf16[1792,384]{1,0:T(8,128)(2,1)} %pad_maximum_fusion), channel_id=1, source_target_pairs={{0,1},{1,0},{2,3},{3,2},{4,5},{5,4},{6,7},{7,6},{8,9},{9,8},{10,11... | collective-permute-start | bytes 4128776 | tf_op jit(solution)/shard_map/ppermute | solution.py:38
  33.6 5.8 %copy-start.10 = (f32[64,4096]{1,0:T(8,128)S(1)}, f32[64,4096]{1,0:T(8,128)}, u32[]{:S(2)}) copy-start(f32[64,4096]{1,0:T(8,128)} %copy-done.9) | copy-start | bytes 3145732
  33.6 5.8 %copy-start.11 = (f32[1,128,4096]{2,1,0:T(8,128)S(1)}, f32[1,128,4096]{2,1,0:T(8,128)}, u32[]{:S(2)}) copy-start(f32[1,128,4096]{2,1,0:T(8,128)} %convert_element_type.125) | copy-start | bytes 6291460
  33.7 7.1 %copy-start.22 = (f32[4096]{0:T(1024)S(1)}, f32[4096]{0:T(1024)}, u32[]{:S(2)}) copy-start(f32[4096]{0:T(1024)} %param.25) | copy-start | bytes 49156
  33.7 16.6 %collective-permute-start.3 = (bf16[768,384]{1,0:T(8,128)(2,1)S(1)}, bf16[768,384]{1,0:T(8,128)(2,1)S(1)}, u32[]{:S(2)}, u32[]{:S(2)}) collective-permute-start(bf16[768,384]{1,0:T(8,128)(2,1)S(1)} %collective-permute-done.refs_2_), channel_id=1, source_target_pairs={{0,2},{1,3},{2,4},{3,5},{4,6},{5,7},{6,0},{7,1},{8,10},{9,11},{10,... | collective-permute-start | bytes 1769480 | tf_op jit(solution)/shard_map/ppermute | solution.py:38
  39.3 25.0 %copy-start.1 = (bf16[256,3072]{1,0:T(8,128)(2,1)}, bf16[256,3072]{1,0:T(8,128)(2,1)S(1)}, u32[]{:S(2)}) copy-start(bf16[256,3072]{1,0:T(8,128)(2,1)S(1)} %get-tuple-element.47.normed_ref) | copy-start | bytes 4718596
  39.3 28.3 %copy-start.4 = (f32[256,1]{1,0:T(8,128)}, f32[256,1]{1,0:T(8,128)S(1)}, u32[]{:S(2)}) copy-start(f32[256,1]{1,0:T(8,128)S(1)} %get-tuple-element.66) | copy-start | bytes 3076
  50.3 4.4 %collective-permute-start.9 = (bf16[32,1024]{1,0:T(8,128)(2,1)S(1)}, bf16[32,1024]{1,0:T(8,128)(2,1)S(1)}, u32[]{:S(2)}, u32[]{:S(2)}) collective-permute-start(bf16[32,1024]{1,0:T(8,128)(2,1)S(1)} %get-tuple-element.94), channel_id=1, source_target_pairs={{0,6},{1,7},{2,0},{3,1},{4,2},{5,3},{6,4},{7,5},{8,14},{9,15},{10,... | collective-permute-start | bytes 196616 | tf_op jit(solution)/shard_map/ppermute | solution.py:38
  50.9 7.0 %collective-permute-start.8 = (bf16[32,1024]{1,0:T(8,128)(2,1)S(1)}, bf16[32,1024]{1,0:T(8,128)(2,1)S(1)}, u32[]{:S(2)}, u32[]{:S(2)}) collective-permute-start(bf16[32,1024]{1,0:T(8,128)(2,1)S(1)} %get-tuple-element.95), channel_id=1, source_target_pairs={{0,4},{1,5},{2,6},{3,7},{4,0},{5,1},{6,2},{7,3},{8,12},{9,13},{10,... | collective-permute-start | bytes 196616 | tf_op jit(solution)/shard_map/ppermute | solution.py:38
  51.6 6.2 %collective-permute-start.7 = (bf16[32,1024]{1,0:T(8,128)(2,1)S(1)}, bf16[32,1024]{1,0:T(8,128)(2,1)S(1)}, u32[]{:S(2)}, u32[]{:S(2)}) collective-permute-start(bf16[32,1024]{1,0:T(8,128)(2,1)S(1)} %get-tuple-element.96), channel_id=1, source_target_pairs={{0,2},{1,3},{2,4},{3,5},{4,6},{5,7},{6,0},{7,1},{8,10},{9,11},{10,... | collective-permute-start | bytes 196616 | tf_op jit(solution)/shard_map/ppermute | solution.py:38
  57.9 6.4 %collective-permute-start.13 = (bf16[4,32,1024]{2,1,0:T(8,128)(2,1)S(1)}, bf16[4,32,1024]{2,1,0:T(8,128)(2,1)S(1)}, u32[]{:S(2)}, u32[]{:S(2)}) collective-permute-start(bf16[4,32,1024]{2,1,0:T(8,128)(2,1)S(1)} %pad_maximum_fusion.3.refs_0_), channel_id=1, source_target_pairs={{0,16},{8,24},{16,0},{24,8},{1,17},{9,25},{17,1},{25,9},{2,18},{10... | collective-permute-start | bytes 786440 | tf_op jit(solution)/shard_map/ppermute | solution.py:42
  58.5 14.6 %collective-permute-start.10 = (bf16[768,384]{1,0:T(8,128)(2,1)S(1)}, bf16[768,384]{1,0:T(8,128)(2,1)S(1)}, u32[]{:S(2)}, u32[]{:S(2)}) collective-permute-start(bf16[768,384]{1,0:T(8,128)(2,1)S(1)} %collective-permute-done.3.refs_4_), channel_id=1, source_target_pairs={{0,2},{1,3},{2,4},{3,5},{4,6},{5,7},{6,0},{7,1},{8,10},{9,11},{10,... | collective-permute-start | bytes 1769480 | tf_op jit(solution)/shard_map/ppermute | solution.py:38
  58.5 5.9 %collective-permute-start.12 = (bf16[4,32,1024]{2,1,0:T(8,128)(2,1)S(1)}, bf16[4,32,1024]{2,1,0:T(8,128)(2,1)S(1)}, u32[]{:S(2)}, u32[]{:S(2)}) collective-permute-start(bf16[4,32,1024]{2,1,0:T(8,128)(2,1)S(1)} %pad_maximum_fusion.3.refs_0_), channel_id=1, source_target_pairs={{0,8},{8,0},{16,24},{24,16},{1,9},{9,1},{17,25},{25,17},{2,10},{10... | collective-permute-start | bytes 786440 | tf_op jit(solution)/shard_map/ppermute | solution.py:42
  64.3 1.5 collective-permute-start.14
  64.3 25.7 %copy-start = (bf16[1792,384]{1,0:T(8,128)(2,1)}, bf16[1792,384]{1,0:T(8,128)(2,1)S(1)}, u32[]{:S(2)}) copy-start(bf16[1792,384]{1,0:T(8,128)(2,1)S(1)} %collective-permute-done.1.refs_1_.refs_6_) | copy-start | bytes 4128772
  73.1 7.9 %collective-permute-start.15 = (bf16[128,768]{1,0:T(8,128)(2,1)S(1)}, bf16[128,768]{1,0:T(8,128)(2,1)S(1)}, u32[]{:S(2)}, u32[]{:S(2)}) collective-permute-start(bf16[128,768]{1,0:T(8,128)(2,1)S(1)} %get-tuple-element.59), channel_id=1, source_target_pairs={{0,6},{1,7},{2,0},{3,1},{4,2},{5,3},{6,4},{7,5},{8,14},{9,15},{10,... | collective-permute-start | bytes 589832 | tf_op jit(solution)/shard_map/ppermute | solution.py:38
  73.2 16.7 %collective-permute-start.16 = (bf16[128,768]{1,0:T(8,128)(2,1)S(1)}, bf16[128,768]{1,0:T(8,128)(2,1)S(1)}, u32[]{:S(2)}, u32[]{:S(2)}) collective-permute-start(bf16[128,768]{1,0:T(8,128)(2,1)S(1)} %get-tuple-element.60), channel_id=1, source_target_pairs={{0,4},{1,5},{2,6},{3,7},{4,0},{5,1},{6,2},{7,3},{8,12},{9,13},{10,... | collective-permute-start | bytes 589832 | tf_op jit(solution)/shard_map/ppermute | solution.py:38
  73.3 16.5 %collective-permute-start.17 = (bf16[128,768]{1,0:T(8,128)(2,1)S(1)}, bf16[128,768]{1,0:T(8,128)(2,1)S(1)}, u32[]{:S(2)}, u32[]{:S(2)}) collective-permute-start(bf16[128,768]{1,0:T(8,128)(2,1)S(1)} %get-tuple-element.61), channel_id=1, source_target_pairs={{0,2},{1,3},{2,4},{3,5},{4,6},{5,7},{6,0},{7,1},{8,10},{9,11},{10,... | collective-permute-start | bytes 589832 | tf_op jit(solution)/shard_map/ppermute | solution.py:38
  75.4 22.3 %collective-permute-start.2 = (bf16[768,384]{1,0:T(8,128)(2,1)S(1)}, bf16[768,384]{1,0:T(8,128)(2,1)S(1)}, u32[]{:S(2)}, u32[]{:S(2)}) collective-permute-start(bf16[768,384]{1,0:T(8,128)(2,1)S(1)} %collective-permute-done.refs_2_), channel_id=1, source_target_pairs={{0,1},{1,0},{2,3},{3,2},{4,5},{5,4},{6,7},{7,6},{8,9},{9,8},{10,11... | collective-permute-start | bytes 1769480 | tf_op jit(solution)/shard_map/ppermute | solution.py:38
  76.4 27.9 %collective-permute-start.4 = (bf16[768,384]{1,0:T(8,128)(2,1)S(1)}, bf16[768,384]{1,0:T(8,128)(2,1)S(1)}, u32[]{:S(2)}, u32[]{:S(2)}) collective-permute-start(bf16[768,384]{1,0:T(8,128)(2,1)S(1)} %collective-permute-done.3.refs_4_), channel_id=1, source_target_pairs={{0,1},{1,0},{2,3},{3,2},{4,5},{5,4},{6,7},{7,6},{8,9},{9,8},{10,11... | collective-permute-start | bytes 1769480 | tf_op jit(solution)/shard_map/ppermute | solution.py:38
  81.0 34.8 %collective-permute-start.11 = (bf16[768,384]{1,0:T(8,128)(2,1)S(1)}, bf16[768,384]{1,0:T(8,128)(2,1)S(1)}, u32[]{:S(2)}, u32[]{:S(2)}) collective-permute-start(bf16[768,384]{1,0:T(8,128)(2,1)S(1)} %collective-permute-done.10.refs_6_), channel_id=1, source_target_pairs={{0,1},{1,0},{2,3},{3,2},{4,5},{5,4},{6,7},{7,6},{8,9},{9,8},{10,11... | collective-permute-start | bytes 1769480 | tf_op jit(solution)/shard_map/ppermute | solution.py:38
  90.0 6.4 %collective-permute-start.23 = (bf16[128,768]{1,0:T(8,128)(2,1)S(1)}, bf16[128,768]{1,0:T(8,128)(2,1)S(1)}, u32[]{:S(2)}, u32[]{:S(2)}) collective-permute-start(bf16[128,768]{1,0:T(8,128)(2,1)S(1)} %add_convert_fusion.refs_0_), channel_id=1, source_target_pairs={{0,6},{1,7},{2,0},{3,1},{4,2},{5,3},{6,4},{7,5},{8,14},{9,15},{10,... | collective-permute-start | bytes 589832 | tf_op jit(solution)/shard_map/ppermute | solution.py:38
  90.0 22.2 %collective-permute-start.21 = (bf16[128,768]{1,0:T(8,128)(2,1)S(1)}, bf16[128,768]{1,0:T(8,128)(2,1)S(1)}, u32[]{:S(2)}, u32[]{:S(2)}) collective-permute-start(bf16[128,768]{1,0:T(8,128)(2,1)S(1)} %add_convert_fusion.refs_0_), channel_id=1, source_target_pairs={{0,4},{1,5},{2,6},{3,7},{4,0},{5,1},{6,2},{7,3},{8,12},{9,13},{10,... | collective-permute-start | bytes 589832 | tf_op jit(solution)/shard_map/ppermute | solution.py:38
  96.4 17.4 %collective-permute-start.19 = (bf16[128,768]{1,0:T(8,128)(2,1)S(1)}, bf16[128,768]{1,0:T(8,128)(2,1)S(1)}, u32[]{:S(2)}, u32[]{:S(2)}) collective-permute-start(bf16[128,768]{1,0:T(8,128)(2,1)S(1)} %add_convert_fusion.refs_0_), channel_id=1, source_target_pairs={{0,2},{1,3},{2,4},{3,5},{4,6},{5,7},{6,0},{7,1},{8,10},{9,11},{10,... | collective-permute-start | bytes 589832 | tf_op jit(solution)/shard_map/ppermute | solution.py:38
  97.7 24.1 %collective-permute-start.18 = (bf16[128,768]{1,0:T(8,128)(2,1)S(1)}, bf16[128,768]{1,0:T(8,128)(2,1)S(1)}, u32[]{:S(2)}, u32[]{:S(2)}) collective-permute-start(bf16[128,768]{1,0:T(8,128)(2,1)S(1)} %add_convert_fusion.refs_0_), channel_id=1, source_target_pairs={{0,1},{1,0},{2,3},{3,2},{4,5},{5,4},{6,7},{7,6},{8,9},{9,8},{10,11... | collective-permute-start | bytes 589832 | tf_op jit(solution)/shard_map/ppermute | solution.py:38
  104.3 31.3 %collective-permute-start.31 = (bf16[2,2,64,384]{3,2,1,0:T(8,128)(2,1)S(1)}, bf16[2,2,64,384]{3,2,1,0:T(8,128)(2,1)S(1)}, u32[]{:S(2)}, u32[]{:S(2)}) collective-permute-start(bf16[2,2,64,384]{3,2,1,0:T(8,128)(2,1)S(1)} %get-tuple-element.76), channel_id=1, source_target_pairs={{0,2},{1,3},{2,4},{3,5},{4,6},{5,7},{6,0},{7,1},{8,10},{9,11},{10,... | collective-permute-start | bytes 589832 | tf_op jit(solution)/shard_map/ppermute | solution.py:38
  112.3 13.3 %collective-permute-start.24 = (bf16[128,768]{1,0:T(8,128)(2,1)S(1)}, bf16[128,768]{1,0:T(8,128)(2,1)S(1)}, u32[]{:S(2)}, u32[]{:S(2)}) collective-permute-start(bf16[128,768]{1,0:T(8,128)(2,1)S(1)} %collective-permute-done.23.refs_6_), channel_id=1, source_target_pairs={{0,1},{1,0},{2,3},{3,2},{4,5},{5,4},{6,7},{7,6},{8,9},{9,8},{10,11... | collective-permute-start | bytes 589832 | tf_op jit(solution)/shard_map/ppermute | solution.py:38
  113.8 13.8 %collective-permute-start.22 = (bf16[128,768]{1,0:T(8,128)(2,1)S(1)}, bf16[128,768]{1,0:T(8,128)(2,1)S(1)}, u32[]{:S(2)}, u32[]{:S(2)}) collective-permute-start(bf16[128,768]{1,0:T(8,128)(2,1)S(1)} %collective-permute-done.21.refs_4_), channel_id=1, source_target_pairs={{0,1},{1,0},{2,3},{3,2},{4,5},{5,4},{6,7},{7,6},{8,9},{9,8},{10,11... | collective-permute-start | bytes 589832 | tf_op jit(solution)/shard_map/ppermute | solution.py:38
  115.8 14.0 %collective-permute-start.20 = (bf16[128,768]{1,0:T(8,128)(2,1)S(1)}, bf16[128,768]{1,0:T(8,128)(2,1)S(1)}, u32[]{:S(2)}, u32[]{:S(2)}) collective-permute-start(bf16[128,768]{1,0:T(8,128)(2,1)S(1)} %collective-permute-done.19.refs_2_), channel_id=1, source_target_pairs={{0,1},{1,0},{2,3},{3,2},{4,5},{5,4},{6,7},{7,6},{8,9},{9,8},{10,11... | collective-permute-start | bytes 589832 | tf_op jit(solution)/shard_map/ppermute | solution.py:38
  117.1 12.6 %copy-start.6 = (s32[8]{0:T(128)S(1)}, s32[8]{0:T(128)}, u32[]{:S(2)}) copy-start(s32[8]{0:T(128)} %count_ref.1) | copy-start | bytes 100
  117.1 12.6 %copy-start.7 = (s32[8]{0:T(128)S(1)}, s32[8]{0:T(128)}, u32[]{:S(2)}) copy-start(s32[8]{0:T(128)} %caption_ref.1) | copy-start | bytes 100
  117.1 12.6 %copy-start.8 = (s32[8]{0:T(128)S(1)}, s32[8]{0:T(128)}, u32[]{:S(2)}) copy-start(s32[8]{0:T(128)} %len_ref.1) | copy-start | bytes 100
  121.9 14.4 %collective-permute-start.32 = (bf16[2,2,64,384]{3,2,1,0:T(8,128)(2,1)S(1)}, bf16[2,2,64,384]{3,2,1,0:T(8,128)(2,1)S(1)}, u32[]{:S(2)}, u32[]{:S(2)}) collective-permute-start(bf16[2,2,64,384]{3,2,1,0:T(8,128)(2,1)S(1)} %get-tuple-element.77), channel_id=1, source_target_pairs={{0,4},{1,5},{2,6},{3,7},{4,0},{5,1},{6,2},{7,3},{8,12},{9,13},{10,... | collective-permute-start | bytes 589832 | tf_op jit(solution)/shard_map/ppermute | solution.py:38
  125.6 11.3 %collective-permute-start.33 = (bf16[2,2,64,384]{3,2,1,0:T(8,128)(2,1)S(1)}, bf16[2,2,64,384]{3,2,1,0:T(8,128)(2,1)S(1)}, u32[]{:S(2)}, u32[]{:S(2)}) collective-permute-start(bf16[2,2,64,384]{3,2,1,0:T(8,128)(2,1)S(1)} %get-tuple-element.78), channel_id=1, source_target_pairs={{0,6},{1,7},{2,0},{3,1},{4,2},{5,3},{6,4},{7,5},{8,14},{9,15},{10,... | collective-permute-start | bytes 589832 | tf_op jit(solution)/shard_map/ppermute | solution.py:38
  134.4 30.3 %collective-permute-start.45 = (bf16[4,128,768]{2,1,0:T(8,128)(2,1)}, bf16[4,128,768]{2,1,0:T(8,128)(2,1)}, u32[]{:S(2)}, u32[]{:S(2)}) collective-permute-start(bf16[4,128,768]{2,1,0:T(8,128)(2,1)} %get-tuple-element.83), channel_id=1, source_target_pairs={{0,1},{1,0},{2,3},{3,2},{4,5},{5,4},{6,7},{7,6},{8,9},{9,8},{10,11... | collective-permute-start | bytes 2359304 | tf_op jit(solution)/shard_map/ppermute | solution.py:38
  138.4 25.2 %collective-permute-start.34 = (bf16[4,2,64,384]{3,2,1,0:T(8,128)(2,1)}, bf16[4,2,64,384]{3,2,1,0:T(8,128)(2,1)}, u32[]{:S(2)}, u32[]{:S(2)}) collective-permute-start(bf16[4,2,64,384]{3,2,1,0:T(8,128)(2,1)} %pad_maximum_fusion.2), channel_id=1, source_target_pairs={{0,1},{1,0},{2,3},{3,2},{4,5},{5,4},{6,7},{7,6},{8,9},{9,8},{10,11... | collective-permute-start | bytes 1179656 | tf_op jit(solution)/shard_map/ppermute | solution.py:38
  139.2 7.0 %copy-start.5 = (f32[256,1]{1,0:T(8,128)S(1)}, f32[256,1]{1,0:T(8,128)}, u32[]{:S(2)}) copy-start(f32[256,1]{1,0:T(8,128)} %copy-done.4) | copy-start | bytes 3076
  146.1 22.1 %collective-permute-start.25 = (bf16[256,1536]{1,0:T(8,128)(2,1)}, bf16[256,1536]{1,0:T(8,128)(2,1)}, u32[]{:S(2)}, u32[]{:S(2)}) collective-permute-start(bf16[256,1536]{1,0:T(8,128)(2,1)} %get-tuple-element.65), channel_id=1, source_target_pairs={{0,8},{8,0},{16,24},{24,16},{1,9},{9,1},{17,25},{25,17},{2,10},{10... | collective-permute-start | bytes 2359304 | tf_op jit(solution)/shard_map/ppermute | solution.py:42
  146.4 2.2 collective-permute-start.29
  147.0 19.9 %collective-permute-start.39 = (bf16[2,256,384]{2,1,0:T(8,128)(2,1)S(1)}, bf16[2,256,384]{2,1,0:T(8,128)(2,1)S(1)}, u32[]{:S(2)}, u32[]{:S(2)}) collective-permute-start(bf16[2,256,384]{2,1,0:T(8,128)(2,1)S(1)} %get-tuple-element.79.refs_4_), channel_id=1, source_target_pairs={{0,2},{1,3},{2,4},{3,5},{4,6},{5,7},{6,0},{7,1},{8,10},{9,11},{10,... | collective-permute-start | bytes 1179656 | tf_op jit(solution)/shard_map/ppermute | solution.py:38
  148.6 26.6 %collective-permute-start.38 = (bf16[2,256,384]{2,1,0:T(8,128)(2,1)S(1)}, bf16[2,256,384]{2,1,0:T(8,128)(2,1)S(1)}, u32[]{:S(2)}, u32[]{:S(2)}) collective-permute-start(bf16[2,256,384]{2,1,0:T(8,128)(2,1)S(1)} %get-tuple-element.79.refs_4_), channel_id=1, source_target_pairs={{0,1},{1,0},{2,3},{3,2},{4,5},{5,4},{6,7},{7,6},{8,9},{9,8},{10,11... | collective-permute-start | bytes 1179656 | tf_op jit(solution)/shard_map/ppermute | solution.py:38
  163.6 7.5 %collective-permute-start.27 = (bf16[256,1536]{1,0:T(8,128)(2,1)}, bf16[256,1536]{1,0:T(8,128)(2,1)S(1)}, u32[]{:S(2)}, u32[]{:S(2)}) collective-permute-start(bf16[256,1536]{1,0:T(8,128)(2,1)} %get-tuple-element.68), channel_id=1, source_target_pairs={{0,8},{8,0},{16,24},{24,16},{1,9},{9,1},{17,25},{25,17},{2,10},{10... | collective-permute-start | bytes 2359304 | tf_op jit(solution)/shard_map/ppermute | solution.py:42
  164.7 6.4 %collective-permute-start.30 = (f32[256,2]{1,0:T(8,128)S(1)}, f32[256,2]{1,0:T(8,128)S(1)}, u32[]{:S(2)}, u32[]{:S(2)}) collective-permute-start(f32[256,2]{1,0:T(8,128)S(1)} %add.172), channel_id=1, source_target_pairs={{0,16},{8,24},{16,0},{24,8},{1,17},{9,25},{17,1},{25,9},{2,18},{10... | collective-permute-start | bytes 6152 | tf_op jit(solution)/shard_map/ppermute | solution.py:42
  166.9 39.4 %collective-permute-start.36 = (bf16[4,2,2,64,384]{4,3,2,1,0:T(8,128)(2,1)S(1)}, bf16[4,2,2,64,384]{4,3,2,1,0:T(8,128)(2,1)S(1)}, u32[]{:S(2)}, u32[]{:S(2)}) collective-permute-start(bf16[4,2,2,64,384]{4,3,2,1,0:T(8,128)(2,1)S(1)} %pad_maximum_fusion.1.refs_0_), channel_id=1, source_target_pairs={{0,16},{8,24},{16,0},{24,8},{1,17},{9,25},{17,1},{25,9},{2,18},{10... | collective-permute-start | bytes 2359304 | tf_op jit(solution)/shard_map/ppermute | solution.py:42
  168.2 13.9 %collective-permute-start.41 = (bf16[2,256,384]{2,1,0:T(8,128)(2,1)S(1)}, bf16[2,256,384]{2,1,0:T(8,128)(2,1)S(1)}, u32[]{:S(2)}, u32[]{:S(2)}) collective-permute-start(bf16[2,256,384]{2,1,0:T(8,128)(2,1)S(1)} %collective-permute-done.39.refs_6_), channel_id=1, source_target_pairs={{0,2},{1,3},{2,4},{3,5},{4,6},{5,7},{6,0},{7,1},{8,10},{9,11},{10,... | collective-permute-start | bytes 1179656 | tf_op jit(solution)/shard_map/ppermute | solution.py:38
  168.2 6.7 %copy-start.19 = (bf16[256,1536]{1,0:T(8,128)(2,1)S(1)}, bf16[256,1536]{1,0:T(8,128)(2,1)}, u32[]{:S(2)}) copy-start(bf16[256,1536]{1,0:T(8,128)(2,1)} %get-tuple-element.67) | copy-start | bytes 2359300
  171.1 15.2 %collective-permute-start.46 = (bf16[128,768]{1,0:T(8,128)(2,1)S(1)}, bf16[128,768]{1,0:T(8,128)(2,1)S(1)}, u32[]{:S(2)}, u32[]{:S(2)}) collective-permute-start(bf16[128,768]{1,0:T(8,128)(2,1)S(1)} %get-tuple-element.90), channel_id=1, source_target_pairs={{0,2},{1,3},{2,4},{3,5},{4,6},{5,7},{6,0},{7,1},{8,10},{9,11},{10,... | collective-permute-start | bytes 589832 | tf_op jit(solution)/shard_map/ppermute | solution.py:38
  171.1 18.3 %collective-permute-start.48 = (bf16[128,768]{1,0:T(8,128)(2,1)S(1)}, bf16[128,768]{1,0:T(8,128)(2,1)S(1)}, u32[]{:S(2)}, u32[]{:S(2)}) collective-permute-start(bf16[128,768]{1,0:T(8,128)(2,1)S(1)} %get-tuple-element.91), channel_id=1, source_target_pairs={{0,6},{1,7},{2,0},{3,1},{4,2},{5,3},{6,4},{7,5},{8,14},{9,15},{10,... | collective-permute-start | bytes 589832 | tf_op jit(solution)/shard_map/ppermute | solution.py:38
  175.2 32.9 %collective-permute-start.26 = (bf16[256,768]{1,0:T(8,128)(2,1)S(1)}, bf16[256,768]{1,0:T(8,128)(2,1)S(1)}, u32[]{:S(2)}, u32[]{:S(2)}) collective-permute-start(bf16[256,768]{1,0:T(8,128)(2,1)S(1)} %slice.158), channel_id=1, source_target_pairs={{0,16},{8,24},{16,0},{24,8},{1,17},{9,25},{17,1},{25,9},{2,18},{10... | collective-permute-start | bytes 1179656 | tf_op jit(solution)/shard_map/ppermute | solution.py:42
  182.2 26.8 %collective-permute-start.28 = (bf16[256,768]{1,0:T(8,128)(2,1)S(1)}, bf16[256,768]{1,0:T(8,128)(2,1)S(1)}, u32[]{:S(2)}, u32[]{:S(2)}) collective-permute-start(bf16[256,768]{1,0:T(8,128)(2,1)S(1)} %slice.157), channel_id=1, source_target_pairs={{0,16},{8,24},{16,0},{24,8},{1,17},{9,25},{17,1},{25,9},{2,18},{10... | collective-permute-start | bytes 1179656 | tf_op jit(solution)/shard_map/ppermute | solution.py:42
  186.3 20.0 %collective-permute-start.47 = (bf16[128,768]{1,0:T(8,128)(2,1)S(1)}, bf16[128,768]{1,0:T(8,128)(2,1)S(1)}, u32[]{:S(2)}, u32[]{:S(2)}) collective-permute-start(bf16[128,768]{1,0:T(8,128)(2,1)S(1)} %get-tuple-element.92), channel_id=1, source_target_pairs={{0,4},{1,5},{2,6},{3,7},{4,0},{5,1},{6,2},{7,3},{8,12},{9,13},{10,... | collective-permute-start | bytes 589832 | tf_op jit(solution)/shard_map/ppermute | solution.py:38
  189.4 17.5 %collective-permute-start.43 = (bf16[2,256,384]{2,1,0:T(8,128)(2,1)S(1)}, bf16[2,256,384]{2,1,0:T(8,128)(2,1)S(1)}, u32[]{:S(2)}, u32[]{:S(2)}) collective-permute-start(bf16[2,256,384]{2,1,0:T(8,128)(2,1)S(1)} %collective-permute-done.41.refs_8_), channel_id=1, source_target_pairs={{0,2},{1,3},{2,4},{3,5},{4,6},{5,7},{6,0},{7,1},{8,10},{9,11},{10,... | collective-permute-start | bytes 1179656 | tf_op jit(solution)/shard_map/ppermute | solution.py:38
  206.3 21.1 %collective-permute-start.35 = (bf16[4,2,2,64,384]{4,3,2,1,0:T(8,128)(2,1)S(1)}, bf16[4,2,2,64,384]{4,3,2,1,0:T(8,128)(2,1)S(1)}, u32[]{:S(2)}, u32[]{:S(2)}) collective-permute-start(bf16[4,2,2,64,384]{4,3,2,1,0:T(8,128)(2,1)S(1)} %pad_maximum_fusion.1.refs_0_), channel_id=1, source_target_pairs={{0,8},{8,0},{16,24},{24,16},{1,9},{9,1},{17,25},{25,17},{2,10},{10... | collective-permute-start | bytes 2359304 | tf_op jit(solution)/shard_map/ppermute | solution.py:42
  206.3 7.0 %copy-start.16 = (bf16[4,2,2,64,384]{4,3,2,1,0:T(8,128)(2,1)}, bf16[4,2,2,64,384]{4,3,2,1,0:T(8,128)(2,1)S(1)}, u32[]{:S(2)}) copy-start(bf16[4,2,2,64,384]{4,3,2,1,0:T(8,128)(2,1)S(1)} %collective-permute-done.36.refs_2_) | copy-start | bytes 2359300
  206.3 28.6 %collective-permute-start.37 = (bf16[4,2,2,64,384]{4,3,2,1,0:T(8,128)(2,1)S(1)}, bf16[4,2,2,64,384]{4,3,2,1,0:T(8,128)(2,1)S(1)}, u32[]{:S(2)}, u32[]{:S(2)}) collective-permute-start(bf16[4,2,2,64,384]{4,3,2,1,0:T(8,128)(2,1)S(1)} %collective-permute-done.36.refs_2_), channel_id=1, source_target_pairs={{0,8},{8,0},{16,24},{24,16},{1,9},{9,1},{17,25},{25,17},{2,10},{10... | collective-permute-start | bytes 2359304 | tf_op jit(solution)/shard_map/ppermute | solution.py:42
  206.9 12.0 %collective-permute-start.40 = (bf16[2,256,384]{2,1,0:T(8,128)(2,1)S(1)}, bf16[2,256,384]{2,1,0:T(8,128)(2,1)S(1)}, u32[]{:S(2)}, u32[]{:S(2)}) collective-permute-start(bf16[2,256,384]{2,1,0:T(8,128)(2,1)S(1)} %collective-permute-done.39.refs_6_), channel_id=1, source_target_pairs={{0,1},{1,0},{2,3},{3,2},{4,5},{5,4},{6,7},{7,6},{8,9},{9,8},{10,11... | collective-permute-start | bytes 1179656 | tf_op jit(solution)/shard_map/ppermute | solution.py:38
  208.2 19.2 %collective-permute-start.42 = (bf16[2,256,384]{2,1,0:T(8,128)(2,1)S(1)}, bf16[2,256,384]{2,1,0:T(8,128)(2,1)S(1)}, u32[]{:S(2)}, u32[]{:S(2)}) collective-permute-start(bf16[2,256,384]{2,1,0:T(8,128)(2,1)S(1)} %collective-permute-done.41.refs_8_), channel_id=1, source_target_pairs={{0,1},{1,0},{2,3},{3,2},{4,5},{5,4},{6,7},{7,6},{8,9},{9,8},{10,11... | collective-permute-start | bytes 1179656 | tf_op jit(solution)/shard_map/ppermute | solution.py:38
  209.0 25.9 %collective-permute-start.44 = (bf16[2,256,384]{2,1,0:T(8,128)(2,1)S(1)}, bf16[2,256,384]{2,1,0:T(8,128)(2,1)S(1)}, u32[]{:S(2)}, u32[]{:S(2)}) collective-permute-start(bf16[2,256,384]{2,1,0:T(8,128)(2,1)S(1)} %collective-permute-done.43.refs_10_), channel_id=1, source_target_pairs={{0,1},{1,0},{2,3},{3,2},{4,5},{5,4},{6,7},{7,6},{8,9},{9,8},{10,11... | collective-permute-start | bytes 1179656 | tf_op jit(solution)/shard_map/ppermute | solution.py:38
  227.3 7.5 %copy-start.17 = (bf16[4,2,2,64,384]{4,3,2,1,0:T(8,128)(2,1)}, bf16[4,2,2,64,384]{4,3,2,1,0:T(8,128)(2,1)S(1)}, u32[]{:S(2)}) copy-start(bf16[4,2,2,64,384]{4,3,2,1,0:T(8,128)(2,1)S(1)} %collective-permute-done.35.refs_1_) | copy-start | bytes 2359300
  (9 other events, 31.4 us)

commit v3 on v2

--- a/solution.py
+++ b/solution.py
@@ -12,6 +12,7 @@
 F32 = jnp.float32
 SLOTS = 3
 VMEM_BYTES = 50 * 1024 * 1024
+SMALL = pl.CostEstimate(flops=1, bytes_accessed=1, transcendentals=0)
 
 
 def rms_scale(values, gain):
@@ -297,9 +298,7 @@
     return lax.optimization_barrier((value, *others))[0]
 
 
-def call(body, out_shape, operands, scalars, scratch=(), flops=0):
-    shapes = jax.tree.leaves(out_shape)
-    moved = sum(math.prod(a.shape) * a.dtype.itemsize for a in (*operands, *shapes))
+def call(body, out_shape, operands, scalars, scratch=()):
     specs = [pl.BlockSpec(memory_space=pltpu.SMEM)] * scalars
     specs += [pl.BlockSpec(memory_space=pltpu.VMEM)] * (len(operands) - scalars)
     return pl.pallas_call(
@@ -309,7 +308,7 @@
         out_specs=jax.tree.map(lambda _: pl.BlockSpec(memory_space=pltpu.VMEM), out_shape),
         scratch_shapes=list(scratch),
         compiler_params=pltpu.CompilerParams(vmem_limit_bytes=VMEM_BYTES),
-        cost_estimate=pl.CostEstimate(flops=flops, bytes_accessed=moved, transcendentals=0),
+        cost_estimate=SMALL,
     )(*operands)
 
 
@@ -319,6 +318,134 @@
 
 def aligned(start, unit):
     return pl.multiple_of(start, unit)
+
+
+def project_text(states, gain, weights, sent, steps=4):
+    rows, depth = states.shape
+    width = weights[0].shape[1]
+    chunk = depth // steps
+    starts = [sum(a.shape[0] for a in sent[:k]) for k in range(len(sent) + 1)]
+
+    def body(states_ref, gain_ref, wq_ref, wk_ref, wv_ref, *refs):
+        sent_refs = refs[: len(sent)]
+        out_ref, few_ref, all_ref, normed_ref, total_ref, sems = refs[len(sent) :]
+        step = pl.program_id(0)
+
+        def copies():
+            made = []
+            for k, source in enumerate(sent_refs):
+                to = slice(starts[k], starts[k + 1])
+                made.append(pltpu.make_async_copy(source, all_ref.at[to], sems.at[k]))
+                if k < 2:
+                    made.append(
+                        pltpu.make_async_copy(source, few_ref.at[to], sems.at[len(sent) + k])
+                    )
+            return made
+
+        @pl.when(step == 0)
+        def _():
+            for copy in copies():
+                copy.start()
+            for at in range(0, rows, 16):
+                values = states_ref[at : at + 16, :].astype(F32)
+                normed_ref[at : at + 16, :] = rms_scale(values, gain_ref[...]).astype(BF)
+            total_ref[...] = jnp.zeros_like(total_ref)
+
+        here = normed_ref[:, pl.ds(aligned(step * chunk, chunk), chunk)]
+        for k, weight_ref in enumerate((wq_ref, wk_ref, wv_ref)):
+            total_ref[:, k * width : (k + 1) * width] += mm(here, weight_ref[...])
+
+        @pl.when(step == steps - 1)
+        def _():
+            out_ref[...] = total_ref[...].astype(BF)
+            for copy in copies():
+                copy.wait()
+
+    whole = lambda shape: pl.BlockSpec(shape, lambda i: (0,) * len(shape))
+    wide = sent[0].shape[1]
+    out = [shaped((rows, 3 * width)), shaped((starts[2], wide)), shaped((starts[-1], wide))]
+    return pl.pallas_call(
+        body,
+        grid=(steps,),
+        out_shape=out,
+        in_specs=[whole((rows, depth)), whole((1, depth))]
+        + [pl.BlockSpec((chunk, width), lambda i: (i, 0))] * 3
+        + [pl.BlockSpec(memory_space=pl.ANY)] * len(sent),
+        out_specs=[whole(out[0].shape)] + [pl.BlockSpec(memory_space=pl.ANY)] * 2,
+        scratch_shapes=[
+            pltpu.VMEM((rows, depth), BF),
+            pltpu.VMEM((rows, 3 * width), F32),
+            pltpu.SemaphoreType.DMA((len(sent) + 2,)),
+        ],
+        compiler_params=pltpu.CompilerParams(vmem_limit_bytes=VMEM_BYTES),
+        cost_estimate=SMALL,
+    )(states, gain.reshape(1, -1), *weights, *sent)
+
+
+def attend_text(projected, bias, text_out, place, lens, steps=4):
+    rows = projected.shape[0]
+    heads = bias.shape[0]
+    inner, depth = text_out.shape
+    size = inner // heads
+    quarter_rows = rows // 4
+    chunk = depth // steps
+
+    def body(place_ref, len_ref, qkv_ref, bias_ref, out_ref, kept_ref, away_ref, held_ref, mixed_ref):
+        @pl.when(pl.program_id(0) == 0)
+        def _():
+            g = place_ref[2]
+            length = len_ref[place_ref[0] * 2 + place_ref[1]]
+            live = lax.broadcasted_iota(jnp.int32, (rows, rows), 1) < length
+            for head in range(heads):
+                query, key, value = (
+                    qkv_ref[:, k * inner + head * size : k * inner + (head + 1) * size]
+                    for k in range(3)
+                )
+                grown = jnp.where(live, jnp.exp(contract_last(query, key) + bias_ref[head]), 0.0)
+                weights = grown * (1.0 / jnp.sum(grown, axis=-1, keepdims=True))
+                held_ref[:, head * size : (head + 1) * size] = mm(weights.astype(BF), value).astype(BF)
+            for k, to in ((0, 0), (2, 1), (1, 2), (3, 3)):
+                rows_from = pl.ds(aligned((g ^ k) * quarter_rows, quarter_rows), quarter_rows)
+                mixed_ref[to * quarter_rows : (to + 1) * quarter_rows, :] = held_ref[rows_from, :]
+
+        product = mm(mixed_ref[...], out_ref[...]).astype(BF)
+        kept_ref[...] = product[: rows // 2]
+        away_ref[...] = product[rows // 2 :]
+
+    whole = lambda shape: pl.BlockSpec(shape, lambda i: (0,) * len(shape))
+    return pl.pallas_call(
+        body,
+        grid=(steps,),
+        out_shape=[shaped((rows // 2, depth))] * 2,
+        in_specs=[pl.BlockSpec(memory_space=pltpu.SMEM)] * 2
+        + [whole(projected.shape), whole(bias.shape)]
+        + [pl.BlockSpec((inner, chunk), lambda i: (0, i))],
+        out_specs=[pl.BlockSpec((rows // 2, chunk), lambda i: (0, i))] * 2,
+        scratch_shapes=[pltpu.VMEM((rows, inner), BF), pltpu.VMEM((rows, inner), BF)],
+        compiler_params=pltpu.CompilerParams(vmem_limit_bytes=VMEM_BYTES),
+        cost_estimate=SMALL,
+    )(place, lens, projected, bias, text_out)
+
+
+def encode_rows(states, kept, got, far, gain, place, pairs):
+    quarter_rows = states.shape[0] // 4
+    width = states.shape[1]
+    depth = width // pairs
+
+    def body(place_ref, states_ref, kept_ref, got_ref, far_ref, gain_ref, *refs):
+        piece_refs, encoded_ref = refs[:-1], refs[-1]
+        z, g = place_ref[0], place_ref[2]
+        mine = pl.ds(aligned(g * quarter_rows, quarter_rows), quarter_rows)
+        total = states_ref[mine, :].astype(F32) + far_ref[...].astype(F32)
+        total += kept_ref[:quarter_rows, :].astype(F32) + got_ref[:quarter_rows, :].astype(F32)
+        encoded_ref[...] = rms_scale(total, gain_ref[...]).astype(BF)
+        for far_by, piece in enumerate(piece_refs):
+            to = lax.rem(z + far_by, pairs)
+            piece[...] = encoded_ref[:, pl.ds(aligned(to * depth, 128), depth)]
+
+    out = [shaped((quarter_rows, depth))] * pairs
+    operands = (place, states, kept, got, far, gain.reshape(1, -1))
+    return call(body, out, operands, 1, [pltpu.VMEM((quarter_rows, width), BF)])
 
 
 def prepare_video(video_states, out_grad, place, pairs, part):
@@ -343,13 +470,12 @@
             for side in range(2):
                 to = lax.rem(z + far, pairs) * 2 + (y ^ side)
                 columns = pl.ds(aligned(to * part, 128), part)
-                tile_refs[far][side, 0] = normed_ref[mine, columns]
-                tile_refs[far][side, 1] = grad_ref[mine, columns]
+                tile_refs[side][far, 0] = normed_ref[mine, columns]
+                tile_refs[side][far, 1] = grad_ref[mine, columns]
 
     out = [shaped((tokens, model_width)), shaped((tokens, 1), F32), shaped((tokens, 1), F32)]
-    out += [shaped((2, 2, rows, part))] * pairs
-    normed, mean, inverse, *tiles = call(body, out, (place, video_states, out_grad), 1)
-    return normed, mean, inverse, tiles
+    out += [shaped((pairs, 2, rows, part))] * 2
+    return call(body, out, (place, video_states, out_grad), 1)
 
 
 def project_rows(normed, out_grad, blocks, place, pairs, part):
@@ -376,8 +502,7 @@
         sum_ref[...] = total
 
     out = [shaped((tokens, width)), shaped((tokens, width)), shaped((1, width), F32)]
-    flops = 4 * tokens * width * normed.shape[1]
-    return call(body, out, (place, normed, out_grad, *blocks), 1, flops=flops)
+    return call(body, out, (place, normed, out_grad, *blocks), 1)
 
 
 def project_captions(parts, own_key, own_value, side_block, place, pairs, skip):
@@ -402,9 +527,8 @@
             out_refs[far][:, width:] = values[rows].astype(BF)
 
     out = [shaped((4 * quarter_rows, 2 * width))] * pairs
-    flops = 4 * pairs * 4 * quarter_rows * depth * width
     operands = (place, *parts, own_key, own_value, side_block)
-    return call(body, out, operands, 1, flops=flops)
+    return call(body, out, operands, 1)
 
 
 def attend(queries, d_attended, column_sum, kv_blocks, place, counts, sample_caption, lens, pairs):
@@ -514,17 +638,18 @@
     ]
     operands = (place, counts, sample_caption, lens, queries, d_attended, column_sum, *kv_blocks)
     scratch = [pltpu.VMEM((keys_wide, 2 * width), BF)]
-    return call(body, out, operands, 4, scratch, flops=12 * tokens * keys_wide * width)
+    return call(body, out, operands, 4, scratch)
 
 
 def project_back(attended, d_queries, blocks, place, pairs, part):
     tokens, width = attended.shape
     model_width = 2 * pairs * part
     per_piece = 2 * pairs // 4
+    piece = model_width // 4
 
     def body(place_ref, att_ref, dq_ref, *refs):
         block_refs = refs[: len(blocks)]
-        halves = (refs[len(blocks) : len(blocks) + 2], refs[len(blocks) + 2 :])
+        own_ref, far_ref, away_ref = refs[len(blocks) :]
         z, y, g = place_ref[0], place_ref[1], place_ref[2]
         att, d_query = att_ref[...], dq_ref[...]
         for far in range(pairs):
@@ -532,20 +657,21 @@
                 block = block_refs[2 * far + side]
                 origin = lax.rem(z - far + pairs, pairs) * 2 + (y ^ side)
                 flip = (origin // per_piece) ^ g
-                start = ((flip // 2) * per_piece + lax.rem(origin, per_piece)) * part
+                start = lax.rem(origin, per_piece) * part
                 columns = pl.ds(aligned(start, 128), part)
+                beyond = pl.ds(aligned(start + piece, 128), part)
                 added = mm(att, block[part : part + width, :]).astype(BF)
                 d_normed = contract_last(d_query, block[:part, :]).astype(BF)
-                for number, (out_ref, d_ref) in enumerate(halves):
-
-                    @pl.when(lax.rem(flip, 2) == number)
-                    def _(out_ref=out_ref, d_ref=d_ref, added=added, d_normed=d_normed):
-                        out_ref[:, columns] = added
-                        d_ref[:, columns] = d_normed
-
-    out = [shaped((tokens, model_width // 2))] * 4
-    flops = 4 * tokens * width * model_width
-    return call(body, out, (place, attended, d_queries, *blocks), 1, flops=flops)
+                places = ((own_ref, columns), (away_ref, columns), (far_ref, columns), (away_ref, beyond))
+                for number, (target_ref, to) in enumerate(places):
+
+                    @pl.when(flip == number)
+                    def _(target_ref=target_ref, to=to, added=added, d_normed=d_normed):
+                        target_ref[0, :, to] = added
+                        target_ref[1, :, to] = d_normed
+
+    out = [shaped((2, tokens, piece)), shaped((2, tokens, piece)), shaped((2, tokens, 2 * piece))]
+    return call(body, out, (place, attended, d_queries, *blocks), 1)
 
 
 def weight_grads(tiles, both_blocks, pairs):
@@ -569,8 +695,7 @@
         out_ref[...] = out_grad
 
     out = [shaped((part, width), F32), shaped((width, part), F32)]
-    flops = 4 * 2 * pairs * both_blocks[0].shape[1] * part * width
-    return call(body, out, (*tiles, *both_blocks), 0, flops=flops)
+    return call(body, out, (*tiles, *both_blocks), 0)
 
 
 def local(
@@ -602,83 +727,59 @@
     width_local = cross_key.shape[1]
     part = cross_query.shape[0]
 
-    own_weights = jnp.concatenate([cross_query, cross_out], axis=0)
+    weights = (cross_query, cross_out, cross_key, cross_value)
+    states = caption_states.reshape(cap_len, text_width)
+
+    projected, own_weights, own_blocks = project_text(
+        states, text_gain, (text_query, text_key, text_value), weights
+    )
     ring = [own_weights, fsend(own_weights, 1, 0)]
-    side_block = fsend(jnp.concatenate([own_weights, cross_key, cross_value], axis=0), 0, 1)
-
-    local_lens = lax.dynamic_slice_in_dim(caption_lens, column * caps_local, caps_local)
-    flat_states = caption_states.reshape(caps_local * cap_len, text_width).astype(F32)
-    text_normed = rms_scale(flat_states, text_gain).astype(BF)
-    local_heads = text_bias.shape[0]
-    head_width = text_query.shape[1] // local_heads
-
-    def heads_of(weight):
-        return mm(text_normed, weight).astype(BF).reshape(
-            caps_local, cap_len, local_heads, head_width
-        )
-
-    text_queries = heads_of(text_query)
-    text_keys = heads_of(text_key)
-    text_values = heads_of(text_value)
-    text_scores = (
-        jnp.einsum("cihd,cjhd->chij", text_queries, text_keys, preferred_element_type=F32)
-        + text_bias[None]
-    )
-    key_valid = jnp.arange(cap_len, dtype=jnp.int32)[None, :] < local_lens[:, None]
-    exp_scores = jnp.where(key_valid[:, None, None, :], jnp.exp(text_scores), 0.0)
-    text_weights = (exp_scores / jnp.sum(exp_scores, axis=-1, keepdims=True)).astype(BF)
-    text_mixed = jnp.einsum(
-        "chij,cjhd->cihd", text_weights, text_values, preferred_element_type=F32
-    )
-    text_mixed = text_mixed.astype(BF).reshape(caps_local * cap_len, local_heads * head_width)
-    text_mixed = jnp.concatenate([quarter(text_mixed, g ^ k) for k in (0, 2, 1, 3)], axis=0)
-    partial_text = mm(text_mixed, text_out).astype(BF)
-    partial_text = after(partial_text, ring[1])
-    half_rows = partial_text.shape[0] // 2
-    quarter_rows = half_rows // 2
-    got = gsend(partial_text[half_rows:], 1).astype(F32)
-    normed, mean, inverse, tiles = prepare_video(
-        after(video_states, partial_text), out_grad, place, pairs, part
-    )
-    ring.append(fsend(after(ring[1], partial_text), 1, 0))
-    kept = partial_text[:half_rows].astype(F32) + got
-    text_rows = kept[:quarter_rows] + gsend(kept[quarter_rows:].astype(BF), 2).astype(F32)
-    encoded = rms_scale(quarter(flat_states, g) + text_rows, final_gain).astype(BF)
-    encoded = after(encoded, ring[2], normed)
-
-    depth = text_width // pairs
-    pieces = [
-        lax.dynamic_slice_in_dim(encoded, ((z + far) % pairs) * depth, depth, 1)
-        for far in range(pairs)
-    ]
+    side_block = fsend(own_blocks, 0, 1)
+    kept, away = attend_text(projected, text_bias, text_out, place, caption_lens)
+    quarter_rows = cap_len // 4
+    got = gsend(away, 1)
+    normed, mean, inverse, own_tiles, other_tiles = prepare_video(
+        after(video_states, kept), out_grad, place, pairs, part
+    )
+    over_core = after(got, ring[1], normed)
+    sent = (kept[quarter_rows:].astype(F32) + over_core[quarter_rows:].astype(F32)).astype(BF)
+    ring.append(fsend(after(ring[1], over_core), 1, 0))
+    over_x = gsend(sent, 2)
+    pieces = encode_rows(
+        states, kept, over_core, after(over_x, ring[2]), final_gain, place, pairs
+    )
+
     mine = jnp.stack([fsend(p, far, 0) if far else p for far, p in enumerate(pieces)])
     over_x = gsend(mine, 2)
     parts = [mine, gsend(mine, 1), over_x, gsend(over_x, 1)]
-    current = after(ring[2], mine)
+    current = after(ring[2], pieces[0])
     for far in range(3, pairs):
         current = fsend(current, 1, 0)
         ring.append(current)
     blocks = [own_weights, side_block]
     for block in ring[1:]:
         blocks += [block, fsend(block, 0, 1)]
-
+    other_tiles = fsend(other_tiles, 0, 1)
+
+    parts[3] = after(parts[3], ring[-1], blocks[3])
     kv_partial = project_captions(
         parts, cross_key, cross_value, side_block, place, pairs, own_weights.shape[0]
     )
-    kv_partial = after(tuple(kv_partial), ring[-1])
     kv_sum = kv_partial[0].astype(F32)
     for far in range(1, pairs):
         kv_sum += fsend(kv_partial[far], pairs - far, 0).astype(F32)
-    kv_blocks = gather_direct(kv_sum.astype(BF))
-
-    queries, d_attended, column_sum = project_rows(normed, out_grad, blocks, place, pairs, part)
-
-    tiles = after(tuple(tiles), kv_blocks[-2])
-    over_z = [fsend(t, far, 0) if far else t for far, t in enumerate(tiles)]
-    over_y = fsend(jnp.stack([t[1] for t in over_z]), 0, 1)
-    tiles = jnp.stack([jnp.stack([t[0] for t in over_z]), over_y], axis=1)
-    tiles_x = gsend(tiles, 2)
-    tiles = [tiles, gsend(tiles, 1), tiles_x, gsend(tiles_x, 1)]
+    kv_sum = after(kv_sum.astype(BF), blocks[5], other_tiles)
+    kv_blocks = gather_direct(kv_sum)
+    for k in range(7, len(blocks), 2):
+        kv_blocks[2] = after(kv_blocks[2], blocks[k])
+
+    queries, d_attended, column_sum = project_rows(
+        normed, after(out_grad, kv_blocks[2]), blocks, place, pairs, part
+    )
+
+    tiles = jnp.stack([own_tiles, other_tiles], axis=1)
+    over_z = [fsend(after(tiles[far], kv_blocks[4]), far, 0) for far in range(1, pairs)]
+    over_z = [tiles[0]] + over_z
 
     both, attended, d_queries, row_sums, kv_own, kv_away = attend(
         queries,
@@ -691,45 +792,55 @@
         caption_lens,
         pairs,
     )
+    kv_away, both = after((kv_away, both), over_z[1:-1])
     kv_side = fsend(kv_away, 0, 1)
-    both_blocks = gather_ring(both)
+    both_blocks = [both, fsend(both, 0, 1)]
+    waits = [kv_side, both_blocks[1]]
+    current = after(both, over_z[-1])
+    for far in range(1, pairs):
+        current = fsend(current, 1, 0)
+        side = fsend(after(current, waits[far - 1]), 0, 1)
+        both_blocks += [current, side]
+        waits.append(side)
+    tiles = jnp.stack(over_z)
+    tiles_x = gsend(tiles, 2)
+    tiles_core = gsend(tiles, 1)
     row_sums = row_sums + gsend(row_sums, 1)
     row_sums = (row_sums + gsend(row_sums, 2)) / model_width
 
-    out_kept, d_kept, out_away, d_away = project_back(
-        attended, d_queries, blocks, place, pairs, part
-    )
-    slice_width = model_width // 4
-
-    def finish(kept, away):
-        kept = kept.astype(F32) + gsend(away, 1).astype(F32)
-        sent = gsend(kept[:, slice_width:].astype(BF), 2)
-        return kept[:, :slice_width] + sent.astype(F32)
-
+    attended = after(attended, kv_side, tiles_x, both_blocks[1], both_blocks[4])
+    own, far_piece, away = project_back(attended, d_queries, blocks, place, pairs, part)
+    width = model_width // 4
+    got = gsend(away, 1)
+    sent = (far_piece.astype(F32) + got[:, :, width:].astype(F32)).astype(BF)
+    far_sum = gsend(sent, 2)
+    total = own.astype(F32) + got[:, :, :width].astype(F32) + far_sum.astype(F32)
     video = quarter(video_states, g, 1).astype(F32)
-    updated = (video + finish(out_kept, out_away)).astype(BF)
+    updated = (video + total[0]).astype(BF)
     video_hat = (video - mean) * inverse
-    d_share = finish(d_kept, d_away)
     input_grad = (
         quarter(out_grad, g, 1).astype(F32)
-        + inverse * (d_share - row_sums[:, 0:1] - video_hat * row_sums[:, 1:2])
+        + inverse * (total[1] - row_sums[:, 0:1] - video_hat * row_sums[:, 1:2])
     ).astype(BF)
 
-    kv_terms = kv_own.astype(F32) + kv_side.astype(F32)
-    kv_grads = kv_terms[0]
+    def kv_term(far):
+        return kv_own[far].astype(F32) + kv_side[far].astype(F32)
+
+    kv_grads = kv_term(0)
     for far in range(1, pairs):
-        kv_grads += fsend(kv_terms[far].astype(BF), far, 0).astype(F32)
+        kv_grads += fsend(kv_term(far).astype(BF), far, 0).astype(F32)
     kv_grads = kv_grads.astype(BF)[None]
     key_grad = kv_grads[:, :, :width_local]
     value_grad = kv_grads[:, :, width_local:]
 
+    tiles = [tiles, tiles_core, tiles_x, gsend(tiles_x, 1)]
     query_grad, out_weight_grad = weight_grads(tiles, both_blocks, pairs)
     return (updated, input_grad, query_grad, out_weight_grad, key_grad, value_grad)
 
 
 def local_of(*arrays):
-    cross_query = arrays[14]
-    return local_general(*arrays) if cross_query.shape[0] % 128 else local(*arrays)
+    whole_tiles = arrays[14].shape[0] % 128 == 0 and arrays[0].shape[0] == 1
+    return local(*arrays) if whole_tiles else local_general(*arrays)
 
 
 def solution(mesh):

time: 241 us -> 238 us (0.988)
  Pallas kernels: 26.5 us -> 40.2 us
  matrix products: 12.5 us -> 0 us
  other arithmetic: 17.6 us -> 10.9 us
  starting transfers between devices: 45.1 us -> 51.1 us
  waiting for transfers between devices: 127 us -> 124 us
    pallas_call x0 -> x2, Pallas kernels: none -> 12.8 us  [the longest x1 6.82 us: project_text(): pl.pallas_call(body, grid=(steps,), out_shape=out, in_specs=[whole((rows,...]
    dot_general x6 -> x0, matrix products: 12.5 us -> none  [the longest x4 12 us: mm(): return jnp.dot(left, right, preferred_element_type=F32)]
    unnamed x50 -> x62, local copies, waits for them, and re-layouts: 3.25 us -> 9.17 us
    ppermute x35, starting transfers between devices: 38.1 us -> 43 us  [fsend(): return lax.ppermute(block, 'fsdp', perm)]
    ppermute x35, waiting for transfers between devices: 116 us -> 111 us  [fsend(): return lax.ppermute(block, 'fsdp', perm)]
    slice x8 -> x0, local copies, waits for them, and re-layouts: 3.49 us -> none  [the longest x4 2.64 us: local(): tiles = jnp.stack([jnp.stack([t[0] for t in over_z]), over_y], axis=1)]
    reduce_sum x2 -> x0, other arithmetic: 2.87 us -> none  [rms_scale(): mean_square = jnp.mean(values * values, axis=-1, keepdims=True)]
    another operation x3 -> x2, other arithmetic: 2.99 us -> 0.23 us  [the longest x1 0.12 us: local(): tiles = jnp.stack(over_z)]
  transfers between devices with their start and end apart: 49 -> 47, of which waited for: 25 -> 22; matrix products, arithmetic and copies ran while one was open for 15% -> 3% of each run, Pallas kernels for 9% -> 11%
where the time goes in v3:
time: 238 us; the launch traced here: 237 us
  waiting for transfers between devices  124 us (52%)
  starting transfers between devices  51.1 us (21%)
  Pallas kernels  40.2 us (17%)
  other arithmetic  10.9 us (5%)
  local copies, waits for them, and re-layouts  10.1 us (4%)
    ppermute x35, waiting for transfers between devices, fsend(): return lax.ppermute(block, 'fsdp', perm)  111 us
    ppermute x35, starting transfers between devices, fsend(): return lax.ppermute(block, 'fsdp', perm)  43 us
    pallas_call x7, Pallas kernels, call(): pl.pallas_call(body, out_shape=out_shape, in_specs=specs, out_specs=jax.t...  27.4 us
    ppermute x12, waiting for transfers between devices, gsend(): lax.ppermute(block, 'grp', [(s, s ^ flip) for s in range(lax.axis_size('g...  12.7 us
    unnamed x62, local copies, waits for them, and re-layouts  9.17 us
    ppermute x12, starting transfers between devices, gsend(): lax.ppermute(block, 'grp', [(s, s ^ flip) for s in range(lax.axis_size('g...  8.07 us
    pallas_call x1, Pallas kernels, project_text(): pl.pallas_call(body, grid=(steps,), out_shape=out, in_specs=[whole((rows,...  6.82 us
    pallas_call x1, Pallas kernels, attend_text(): pl.pallas_call(body, grid=(steps,), out_shape=[shaped((rows // 2, depth))...  5.98 us
  transfers between devices with their start and end apart: 47, of which 22 were waited for; matrix products, arithmetic and copies ran while one was open for 3% of the time, Pallas kernels for 11%

profile of v3, /device:TPU:0, one launch (start us, length us, event | category | flops | bytes accessed | tf_op | source)
XLA Modules:
  0.0 237.2 jit_solution(9675930739520045405)
XLA Ops:
  0.6 1.2 copy-done.1
  1.9 1.0 copy-done.4
  2.9 1.0 copy-done.6
  3.9 1.0 copy-done.13
  4.8 1.0 copy-done.14
  6.5 6.8 %shard_map.208 = (bf16[128,1536]{1,0:T(8,128)(2,1)S(1)}, bf16[768,384]{1,0:T(8,128)(2,1)S(1)}, bf16[1792,384]{1,0:T(8,128)(2,1)}) custom-call(bf16[128,4096]{1,0:T(8,128)(2,1)S(1)} %bitcast.49, f32[1,4096]{1,0:T(1,128)S(1)} %bitcast.54, bf16[4096,512]{1,0:T(8,128)(2,1)} %wq_ref.1, bf16[4096,512]{1,0:T(8,128)(2,1)} %wk_ref.1, bf16[4096,512]{1,0:T(8,128)(2,1)} %wv_ref.1, ...), custom_call_target="tpu_custom_call" | custom-call | flops 1 | bytes 1 | tf_op jit(solution)/shard_map/pallas_call | solution.py:367
  13.3 3.1 %collective-permute-start.1 = (bf16[768,384]{1,0:T(8,128)(2,1)S(1)}, bf16[768,384]{1,0:T(8,128)(2,1)S(1)}, u32[]{:S(2)}, u32[]{:S(2)}) collective-permute-start(bf16[768,384]{1,0:T(8,128)(2,1)S(1)} %get-tuple-element.62.refs_0_), channel_id=1, source_target_pairs={{0,2},{1,3},{2,4},{3,5},{4,6},{5,7},{6,0},{7,1},{8,10},{9,11},{10,... | collective-permute-start | bytes 1769480 | tf_op jit(solution)/shard_map/ppermute | solution.py:39
  16.5 6.0 %shard_map.209 = (bf16[64,4096]{1,0:T(8,128)(2,1)S(1)}, bf16[64,4096]{1,0:T(8,128)(2,1)S(1)}) custom-call(s32[3]{0:T(128)S(1)} %pad_add_fusion.place_ref, s32[8]{0:T(128)S(1)} %copy-done.19, bf16[128,1536]{1,0:T(8,128)(2,1)S(1)} %get-tuple-element.57.qkv_ref, f32[8,128,128]{2,1,0:T(8,128)S(1)} %copy-done.8, bf16[512,4096]{1,0:T(8,128)(2,1)} %out_ref.1), custom_call_target="tpu_custom_call" | custom-call | flops 1 | bytes 1 | tf_op jit(solution)/shard_map/pallas_call | solution.py:416
  22.6 1.6 collective-permute-start.12
  24.2 4.2 %shard_map.210 = (bf16[256,3072]{1,0:T(8,128)(2,1)S(1)}, f32[256,1]{1,0:T(8,128)S(1)}, f32[256,1]{1,0:T(8,128)S(1)}, bf16[4,2,64,384]{3,2,1,0:T(8,128)(2,1)S(1)}, bf16[4,2,64,384]{3,2,1,0:T(8,128)(2,1)S(1)}) custom-call(s32[3]{0:T(128)S(1)} %pad_add_fusion.place_ref, bf16[256,3072]{1,0:T(8,128)(2,1)} %video_ref, bf16[256,3072]{1,0:T(8,128)(2,1)} %grad_ref.2), custom_call_target="tpu_custom_call" | custom-call | flops 1 | bytes 1 | tf_op jit(solution)/shard_map/pallas_call | solution.py:304
  28.3 1.1 copy-done.3
  30.8 1.0 collective-permute-done.1.refs_2_
  32.5 1.5 collective-permute-start.2
  34.0 0.9 collective-permute-start.11
  34.9 5.7 %collective-permute-done.2.far_ref = bf16[32,4096]{1,0:T(8,128)(2,1)S(1)} collective-permute-done((bf16[32,4096]{1,0:T(8,128)(2,1)S(1)}, bf16[32,4096]{1,0:T(8,128)(2,1)S(1)}, u32[]{:S(2)}, u32[]{:S(2)}) %collective-permute-start.2) | collective-permute-done | bytes 262176 | tf_op jit(solution)/shard_map/ppermute | solution.py:43
  40.6 7.4 %collective-permute-done.3.refs_4_ = bf16[768,384]{1,0:T(8,128)(2,1)S(1)} collective-permute-done((bf16[768,384]{1,0:T(8,128)(2,1)S(1)}, bf16[768,384]{1,0:T(8,128)(2,1)S(1)}, u32[]{:S(2)}, u32[]{:S(2)}) %collective-permute-start.3) | collective-permute-done | bytes 589856 | tf_op jit(solution)/shard_map/ppermute | solution.py:39
  48.1 0.8 shard_map.211
  49.4 0.7 collective-permute-start.5
  50.1 1.6 collective-permute-start.4
  51.7 2.5 %collective-permute-done.6 = bf16[32,1024]{1,0:T(8,128)(2,1)S(1)} collective-permute-done((bf16[32,1024]{1,0:T(8,128)(2,1)S(1)}, bf16[32,1024]{1,0:T(8,128)(2,1)S(1)}, u32[]{:S(2)}, u32[]{:S(2)}) %collective-permute-start.6) | collective-permute-done | bytes 65568 | tf_op jit(solution)/shard_map/ppermute | solution.py:39
  54.9 14.2 %collective-permute-done.5 = bf16[32,1024]{1,0:T(8,128)(2,1)S(1)} collective-permute-done((bf16[32,1024]{1,0:T(8,128)(2,1)S(1)}, bf16[32,1024]{1,0:T(8,128)(2,1)S(1)}, u32[]{:S(2)}, u32[]{:S(2)}) %collective-permute-start.5) | collective-permute-done | bytes 65568 | tf_op jit(solution)/shard_map/ppermute | solution.py:39
  69.1 1.5 collective-permute-start.8
  70.6 4.9 %collective-permute-done.8.refs_2_ = bf16[4,32,1024]{2,1,0:T(8,128)(2,1)S(1)} collective-permute-done((bf16[4,32,1024]{2,1,0:T(8,128)(2,1)S(1)}, bf16[4,32,1024]{2,1,0:T(8,128)(2,1)S(1)}, u32[]{:S(2)}, u32[]{:S(2)}) %collective-permute-start.8) | collective-permute-done | bytes 262176 | tf_op jit(solution)/shard_map/ppermute | solution.py:43
  76.0 1.0 collective-permute-done.9.refs_3_
  77.4 1.8 shard_map.212
  79.4 3.7 %collective-permute-start.13 = (bf16[128,768]{1,0:T(8,128)(2,1)S(1)}, bf16[128,768]{1,0:T(8,128)(2,1)S(1)}, u32[]{:S(2)}, u32[]{:S(2)}) collective-permute-start(bf16[128,768]{1,0:T(8,128)(2,1)S(1)} %get-tuple-element.74), channel_id=1, source_target_pairs={{0,6},{1,7},{2,0},{3,1},{4,2},{5,3},{6,4},{7,5},{8,14},{9,15},{10,... | collective-permute-start | bytes 589832 | tf_op jit(solution)/shard_map/ppermute | solution.py:39
  83.8 5.2 %collective-permute-done.15 = bf16[128,768]{1,0:T(8,128)(2,1)S(1)} collective-permute-done((bf16[128,768]{1,0:T(8,128)(2,1)S(1)}, bf16[128,768]{1,0:T(8,128)(2,1)S(1)}, u32[]{:S(2)}, u32[]{:S(2)}) %collective-permute-start.15) | collective-permute-done | bytes 196640 | tf_op jit(solution)/shard_map/ppermute | solution.py:39
  89.7 6.8 %collective-permute-done.14 = bf16[128,768]{1,0:T(8,128)(2,1)S(1)} collective-permute-done((bf16[128,768]{1,0:T(8,128)(2,1)S(1)}, bf16[128,768]{1,0:T(8,128)(2,1)S(1)}, u32[]{:S(2)}, u32[]{:S(2)}) %collective-permute-start.14) | collective-permute-done | bytes 196640 | tf_op jit(solution)/shard_map/ppermute | solution.py:39
  96.6 4.1 %collective-permute-done.17 = bf16[4,2,64,384]{3,2,1,0:T(8,128)(2,1)S(1)} collective-permute-done((bf16[4,2,64,384]{3,2,1,0:T(8,128)(2,1)S(1)}, bf16[4,2,64,384]{3,2,1,0:T(8,128)(2,1)S(1)}, u32[]{:S(2)}, u32[]{:S(2)}) %collective-permute-start.17) | collective-permute-done | bytes 393248 | tf_op jit(solution)/shard_map/ppermute | solution.py:39
  100.7 3.8 %collective-permute-start.24 = (bf16[128,768]{1,0:T(8,128)(2,1)S(1)}, bf16[128,768]{1,0:T(8,128)(2,1)S(1)}, u32[]{:S(2)}, u32[]{:S(2)}) collective-permute-start(bf16[128,768]{1,0:T(8,128)(2,1)S(1)} %add_convert_fusion.5.refs_0_), channel_id=1, source_target_pairs={{0,6},{1,7},{2,0},{3,1},{4,2},{5,3},{6,4},{7,5},{8,14},{9,15},{10,... | collective-permute-start | bytes 589832 | tf_op jit(solution)/shard_map/ppermute | solution.py:39
  104.5 5.9 %collective-permute-done.18.refs_2_ = bf16[128,768]{1,0:T(8,128)(2,1)S(1)} collective-permute-done((bf16[128,768]{1,0:T(8,128)(2,1)S(1)}, bf16[128,768]{1,0:T(8,128)(2,1)S(1)}, u32[]{:S(2)}, u32[]{:S(2)}) %collective-permute-start.18) | collective-permute-done | bytes 196640 | tf_op jit(solution)/shard_map/ppermute | solution.py:39
  110.5 5.6 %collective-permute-done.22.refs_4_ = bf16[128,768]{1,0:T(8,128)(2,1)S(1)} collective-permute-done((bf16[128,768]{1,0:T(8,128)(2,1)S(1)}, bf16[128,768]{1,0:T(8,128)(2,1)S(1)}, u32[]{:S(2)}, u32[]{:S(2)}) %collective-permute-start.22) | collective-permute-done | bytes 196640 | tf_op jit(solution)/shard_map/ppermute | solution.py:39
  116.7 1.4 collective-permute-start.25
  118.1 2.6 %collective-permute-start.26 = (bf16[2,2,64,384]{3,2,1,0:T(8,128)(2,1)S(1)}, bf16[2,2,64,384]{3,2,1,0:T(8,128)(2,1)S(1)}, u32[]{:S(2)}, u32[]{:S(2)}) collective-permute-start(bf16[2,2,64,384]{3,2,1,0:T(8,128)(2,1)S(1)} %get-tuple-element.88), channel_id=1, source_target_pairs={{0,2},{1,3},{2,4},{3,5},{4,6},{5,7},{6,0},{7,1},{8,10},{9,11},{10,... | collective-permute-start | bytes 589832 | tf_op jit(solution)/shard_map/ppermute | solution.py:39
  120.8 1.9 collective-permute-start.27
  123.2 4.7 %shard_map.213 = (bf16[256,384]{1,0:T(8,128)(2,1)S(1)}, bf16[256,384]{1,0:T(8,128)(2,1)S(1)}, f32[1,384]{1,0:T(1,128)S(1)}) custom-call(s32[3]{0:T(128)S(1)} %pad_add_fusion.place_ref, bf16[256,3072]{1,0:T(8,128)(2,1)} %copy-done.3, bf16[256,3072]{1,0:T(8,128)(2,1)} %grad_ref.2, bf16[768,384]{1,0:T(8,128)(2,1)S(1)} %get-tuple-element.62.refs_0_, ...), custom_call_target="tpu_custom_call" | custom-call | flops 1 | bytes 1 | tf_op jit(solution)/shard_map/pallas_call | solution.py:304
  127.9 1.3 collective-permute-done.25.refs_7_
  129.2 4.7 %shard_map.214 = (bf16[2,256,384]{2,1,0:T(8,128)(2,1)S(1)}, bf16[256,384]{1,0:T(8,128)(2,1)S(1)}, bf16[256,384]{1,0:T(8,128)(2,1)S(1)}, f32[256,2]{1,0:T(8,128)}...) custom-call(s32[3]{0:T(128)S(1)} %pad_add_fusion.place_ref, s32[8]{0:T(128)S(1)} %copy-done.20, ...), custom_call_target="tpu_custom_call" | custom-call | flops 1 | bytes 1 | tf_op jit(solution)/shard_map/pallas_call | solution.py:304
  134.8 4.8 %collective-permute-start.32 = (bf16[2,256,384]{2,1,0:T(8,128)(2,1)S(1)}, bf16[2,256,384]{2,1,0:T(8,128)(2,1)S(1)}, u32[]{:S(2)}, u32[]{:S(2)}) collective-permute-start(bf16[2,256,384]{2,1,0:T(8,128)(2,1)S(1)} %get-tuple-element.93.refs_4_), channel_id=1, source_target_pairs={{0,2},{1,3},{2,4},{3,5},{4,6},{5,7},{6,0},{7,1},{8,10},{9,11},{10,... | collective-permute-start | bytes 1179656 | tf_op jit(solution)/shard_map/ppermute | solution.py:39
  139.8 1.5 collective-permute-start.30
  141.6 9.0 %collective-permute-done.32.refs_6_ = bf16[2,256,384]{2,1,0:T(8,128)(2,1)S(1)} collective-permute-done((bf16[2,256,384]{2,1,0:T(8,128)(2,1)S(1)}, bf16[2,256,384]{2,1,0:T(8,128)(2,1)S(1)}, u32[]{:S(2)}, u32[]{:S(2)}) %collective-permute-start.32) | collective-permute-done | bytes 393248 | tf_op jit(solution)/shard_map/ppermute | solution.py:39
  150.6 11.9 %collective-permute-done.31.refs_5_ = bf16[2,256,384]{2,1,0:T(8,128)(2,1)S(1)} collective-permute-done((bf16[2,256,384]{2,1,0:T(8,128)(2,1)S(1)}, bf16[2,256,384]{2,1,0:T(8,128)(2,1)S(1)}, u32[]{:S(2)}, u32[]{:S(2)}) %collective-permute-start.31) | collective-permute-done | bytes 393248 | tf_op jit(solution)/shard_map/ppermute | solution.py:39
  162.5 0.8 copy-done.11
  163.3 6.9 %shard_map.215 = (bf16[2,256,768]{2,1,0:T(8,128)(2,1)}, bf16[2,256,768]{2,1,0:T(8,128)(2,1)}, bf16[2,256,1536]{2,1,0:T(8,128)(2,1)}) custom-call(s32[3]{0:T(128)S(1)} %pad_add_fusion.place_ref, bf16[256,384]{1,0:T(8,128)(2,1)S(1)} %get-tuple-element.94.att_ref, bf16[256,384]{1,0:T(8,128)(2,1)S(1)} %get-tuple-element.95.dq_ref, ...), custom_call_target="tpu_custom_call" | custom-call | flops 1 | bytes 1 | tf_op jit(solution)/shard_map/pallas_call | solution.py:304
  170.8 1.0 reduce.2
  171.8 1.0 reduce
  173.0 0.7 collective-permute-done.36
  173.8 0.9 add.79
  174.7 1.5 collective-permute-start.37
  176.6 4.0 %collective-permute-start.42 = (bf16[2,256,384]{2,1,0:T(8,128)(2,1)}, bf16[2,256,384]{2,1,0:T(8,128)(2,1)S(1)}, u32[]{:S(2)}, u32[]{:S(2)}) collective-permute-start(bf16[2,256,384]{2,1,0:T(8,128)(2,1)} %copy-done.11), channel_id=1, source_target_pairs={{0,2},{1,3},{2,4},{3,5},{4,6},{5,7},{6,0},{7,1},{8,10},{9,11},{10,... | collective-permute-start | bytes 1179656 | tf_op jit(solution)/shard_map/ppermute | solution.py:39
  180.6 1.3 fusion.11
  181.9 2.9 %collective-permute-start.46 = (bf16[128,768]{1,0:T(8,128)(2,1)S(1)}, bf16[128,768]{1,0:T(8,128)(2,1)S(1)}, u32[]{:S(2)}, u32[]{:S(2)}) collective-permute-start(bf16[128,768]{1,0:T(8,128)(2,1)S(1)} %get-tuple-element.113), channel_id=1, source_target_pairs={{0,6},{1,7},{2,0},{3,1},{4,2},{5,3},{6,4},{7,5},{8,14},{9,15},{10,... | collective-permute-start | bytes 589832 | tf_op jit(solution)/shard_map/ppermute | solution.py:39
  184.8 1.3 add_convert_fusion
  186.1 0.7 collective-permute-start.45
  186.8 9.9 %collective-permute-done.46 = bf16[128,768]{1,0:T(8,128)(2,1)S(1)} collective-permute-done((bf16[128,768]{1,0:T(8,128)(2,1)S(1)}, bf16[128,768]{1,0:T(8,128)(2,1)S(1)}, u32[]{:S(2)}, u32[]{:S(2)}) %collective-permute-start.46) | collective-permute-done | bytes 196640 | tf_op jit(solution)/shard_map/ppermute | solution.py:39
  196.7 1.8 collective-permute-start.44
  199.4 10.2 %collective-permute-done.45 = bf16[128,768]{1,0:T(8,128)(2,1)S(1)} collective-permute-done((bf16[128,768]{1,0:T(8,128)(2,1)S(1)}, bf16[128,768]{1,0:T(8,128)(2,1)S(1)}, u32[]{:S(2)}, u32[]{:S(2)}) %collective-permute-start.45) | collective-permute-done | bytes 196640 | tf_op jit(solution)/shard_map/ppermute | solution.py:39
  210.1 1.5 collective-permute-start.43
  211.6 1.1 fusion.14
  213.4 8.2 %collective-permute-done.41.refs_9_ = bf16[2,256,384]{2,1,0:T(8,128)(2,1)S(1)} collective-permute-done((bf16[2,256,384]{2,1,0:T(8,128)(2,1)S(1)}, bf16[2,256,384]{2,1,0:T(8,128)(2,1)S(1)}, u32[]{:S(2)}, u32[]{:S(2)}) %collective-permute-start.41) | collective-permute-done | bytes 393248 | tf_op jit(solution)/shard_map/ppermute | solution.py:39
  221.6 7.5 %collective-permute-done.43.refs_11_ = bf16[2,256,384]{2,1,0:T(8,128)(2,1)S(1)} collective-permute-done((bf16[2,256,384]{2,1,0:T(8,128)(2,1)S(1)}, bf16[2,256,384]{2,1,0:T(8,128)(2,1)S(1)}, u32[]{:S(2)}, u32[]{:S(2)}) %collective-permute-start.43) | collective-permute-done | bytes 393248 | tf_op jit(solution)/shard_map/ppermute | solution.py:39
  229.1 4.3 %shard_map.216 = (f32[384,384]{1,0:T(8,128)}, f32[384,384]{1,0:T(8,128)}) custom-call(bf16[4,2,2,64,384]{4,3,2,1,0:T(8,128)(2,1)S(1)} %pad_maximum_fusion.refs_0_, bf16[4,2,2,64,384]{4,3,2,1,0:T(8,128)(2,1)} %copy-done.26, bf16[4,2,2,64,384]{4,3,2,1,0:T(8,128)(2,1)} %copy-done.23, bf16[4,2,2,64,384]{4,3,2,1,0:T(8,128)(2,1)} %copy-done.27, ...), custom_call_target="tpu_custom_call" | custom-call | flops 1 | bytes 1 | tf_op jit(solution)/shard_map/pallas_call | solution.py:304
  233.4 1.4 convert_add_fusion
  234.8 2.3 fusion.6
  (118 shorter events, 12.4 us)
Async XLA Ops:
  6.5 10.0 %copy-start.8 = (f32[8,128,128]{2,1,0:T(8,128)S(1)}, f32[8,128,128]{2,1,0:T(8,128)}, u32[]{:S(2)}) copy-start(f32[8,128,128]{2,1,0:T(8,128)} %bias_ref.1) | copy-start | bytes 1572868
  6.5 10.0 %copy-start.19 = (s32[8]{0:T(128)S(1)}, s32[8]{0:T(128)}, u32[]{:S(2)}) copy-start(s32[8]{0:T(128)} %len_ref.3) | copy-start | bytes 100
  13.3 18.4 %collective-permute-start.1 = (bf16[768,384]{1,0:T(8,128)(2,1)S(1)}, bf16[768,384]{1,0:T(8,128)(2,1)S(1)}, u32[]{:S(2)}, u32[]{:S(2)}) collective-permute-start(bf16[768,384]{1,0:T(8,128)(2,1)S(1)} %get-tuple-element.62.refs_0_), channel_id=1, source_target_pairs={{0,2},{1,3},{2,4},{3,5},{4,6},{5,7},{6,0},{7,1},{8,10},{9,11},{10,... | collective-permute-start | bytes 1769480 | tf_op jit(solution)/shard_map/ppermute | solution.py:39
  22.5 8.3 %collective-permute-start = (bf16[64,4096]{1,0:T(8,128)(2,1)S(1)}, bf16[64,4096]{1,0:T(8,128)(2,1)S(1)}, u32[]{:S(2)}, u32[]{:S(2)}) collective-permute-start(bf16[64,4096]{1,0:T(8,128)(2,1)S(1)} %get-tuple-element.61), channel_id=1, source_target_pairs={{0,8},{8,0},{16,24},{24,16},{1,9},{9,1},{17,25},{25,17},{2,10},{10... | collective-permute-start | bytes 1572872 | tf_op jit(solution)/shard_map/ppermute | solution.py:43
  22.6 54.5 %collective-permute-start.12 = (bf16[1792,384]{1,0:T(8,128)(2,1)S(1)}, bf16[1792,384]{1,0:T(8,128)(2,1)S(1)}, u32[]{:S(2)}, u32[]{:S(2)}) collective-permute-start(bf16[1792,384]{1,0:T(8,128)(2,1)S(1)} %copy-done.30), channel_id=1, source_target_pairs={{0,1},{1,0},{2,3},{3,2},{4,5},{5,4},{6,7},{7,6},{8,9},{9,8},{10,11... | collective-permute-start | bytes 4128776 | tf_op jit(solution)/shard_map/ppermute | solution.py:39
  24.1 23.9 %copy-start.2 = (bf16[1,128,4096]{2,1,0:T(8,128)(2,1)S(1)}, bf16[1,128,4096]{2,1,0:T(8,128)(2,1)}, u32[]{:S(2)}) copy-start(bf16[1,128,4096]{2,1,0:T(8,128)(2,1)} %param.17) | copy-start | bytes 3145732
  24.2 23.9 %copy-start.17 = (f32[4096]{0:T(1024)S(1)}, f32[4096]{0:T(1024)}, u32[]{:S(2)}) copy-start(f32[4096]{0:T(1024)} %param.25) | copy-start | bytes 49156
  31.8 16.3 %collective-permute-start.3 = (bf16[768,384]{1,0:T(8,128)(2,1)S(1)}, bf16[768,384]{1,0:T(8,128)(2,1)S(1)}, u32[]{:S(2)}, u32[]{:S(2)}) collective-permute-start(bf16[768,384]{1,0:T(8,128)(2,1)S(1)} %collective-permute-done.1.refs_2_), channel_id=1, source_target_pairs={{0,2},{1,3},{2,4},{3,5},{4,6},{5,7},{6,0},{7,1},{8,10},{9,11},{10,... | collective-permute-start | bytes 1769480 | tf_op jit(solution)/shard_map/ppermute | solution.py:39
  32.4 45.0 %copy-start.5 = (bf16[512,384]{1,0:T(8,128)(2,1)S(1)}, bf16[512,384]{1,0:T(8,128)(2,1)}, u32[]{:S(2)}) copy-start(bf16[512,384]{1,0:T(8,128)(2,1)} %refs_4_.1) | copy-start | bytes 1179652
  32.5 45.0 %copy-start.7 = (bf16[512,384]{1,0:T(8,128)(2,1)S(1)}, bf16[512,384]{1,0:T(8,128)(2,1)}, u32[]{:S(2)}) copy-start(bf16[512,384]{1,0:T(8,128)(2,1)} %refs_5_.1) | copy-start | bytes 1179652
  32.5 8.2 %collective-permute-start.2 = (bf16[32,4096]{1,0:T(8,128)(2,1)S(1)}, bf16[32,4096]{1,0:T(8,128)(2,1)S(1)}, u32[]{:S(2)}, u32[]{:S(2)}) collective-permute-start(bf16[32,4096]{1,0:T(8,128)(2,1)S(1)} %add_convert_fusion.1), channel_id=1, source_target_pairs={{0,16},{8,24},{16,0},{24,8},{1,17},{9,25},{17,1},{25,9},{2,18},{10... | collective-permute-start | bytes 786440 | tf_op jit(solution)/shard_map/ppermute | solution.py:43
  34.0 42.0 %collective-permute-start.11 = (bf16[768,384]{1,0:T(8,128)(2,1)S(1)}, bf16[768,384]{1,0:T(8,128)(2,1)S(1)}, u32[]{:S(2)}, u32[]{:S(2)}) collective-permute-start(bf16[768,384]{1,0:T(8,128)(2,1)S(1)} %collective-permute-done.1.refs_2_), channel_id=1, source_target_pairs={{0,1},{1,0},{2,3},{3,2},{4,5},{5,4},{6,7},{7,6},{8,9},{9,8},{10,11... | collective-permute-start | bytes 1769480 | tf_op jit(solution)/shard_map/ppermute | solution.py:39
  48.9 5.3 %collective-permute-start.6 = (bf16[32,1024]{1,0:T(8,128)(2,1)S(1)}, bf16[32,1024]{1,0:T(8,128)(2,1)S(1)}, u32[]{:S(2)}, u32[]{:S(2)}) collective-permute-start(bf16[32,1024]{1,0:T(8,128)(2,1)S(1)} %get-tuple-element.69), channel_id=1, source_target_pairs={{0,6},{1,7},{2,0},{3,1},{4,2},{5,3},{6,4},{7,5},{8,14},{9,15},{10,... | collective-permute-start | bytes 196616 | tf_op jit(solution)/shard_map/ppermute | solution.py:39
  49.4 19.7 %collective-permute-start.5 = (bf16[32,1024]{1,0:T(8,128)(2,1)S(1)}, bf16[32,1024]{1,0:T(8,128)(2,1)S(1)}, u32[]{:S(2)}, u32[]{:S(2)}) collective-permute-start(bf16[32,1024]{1,0:T(8,128)(2,1)S(1)} %get-tuple-element.68), channel_id=1, source_target_pairs={{0,4},{1,5},{2,6},{3,7},{4,0},{5,1},{6,2},{7,3},{8,12},{9,13},{10,... | collective-permute-start | bytes 196616 | tf_op jit(solution)/shard_map/ppermute | solution.py:39
  50.1 18.9 %collective-permute-start.4 = (bf16[32,1024]{1,0:T(8,128)(2,1)S(1)}, bf16[32,1024]{1,0:T(8,128)(2,1)S(1)}, u32[]{:S(2)}, u32[]{:S(2)}) collective-permute-start(bf16[32,1024]{1,0:T(8,128)(2,1)S(1)} %get-tuple-element.67), channel_id=1, source_target_pairs={{0,2},{1,3},{2,4},{3,5},{4,6},{5,7},{6,0},{7,1},{8,10},{9,11},{10,... | collective-permute-start | bytes 196616 | tf_op jit(solution)/shard_map/ppermute | solution.py:39
  54.2 22.8 %collective-permute-start.10 = (bf16[768,384]{1,0:T(8,128)(2,1)S(1)}, bf16[768,384]{1,0:T(8,128)(2,1)S(1)}, u32[]{:S(2)}, u32[]{:S(2)}) collective-permute-start(bf16[768,384]{1,0:T(8,128)(2,1)S(1)} %collective-permute-done.3.refs_4_), channel_id=1, source_target_pairs={{0,2},{1,3},{2,4},{3,5},{4,6},{5,7},{6,0},{7,1},{8,10},{9,11},{10,... | collective-permute-start | bytes 1769480 | tf_op jit(solution)/shard_map/ppermute | solution.py:39
  69.1 6.4 %collective-permute-start.8 = (bf16[4,32,1024]{2,1,0:T(8,128)(2,1)S(1)}, bf16[4,32,1024]{2,1,0:T(8,128)(2,1)S(1)}, u32[]{:S(2)}, u32[]{:S(2)}) collective-permute-start(bf16[4,32,1024]{2,1,0:T(8,128)(2,1)S(1)} %pad_maximum_fusion.1.refs_0_), channel_id=1, source_target_pairs={{0,16},{8,24},{16,0},{24,8},{1,17},{9,25},{17,1},{25,9},{2,18},{10... | collective-permute-start | bytes 786440 | tf_op jit(solution)/shard_map/ppermute | solution.py:43
  75.5 1.5 collective-permute-start.9
  75.5 1.9 collective-permute-start.7
  76.0 24.6 %collective-permute-start.16 = (bf16[768,384]{1,0:T(8,128)(2,1)S(1)}, bf16[768,384]{1,0:T(8,128)(2,1)S(1)}, u32[]{:S(2)}, u32[]{:S(2)}) collective-permute-start(bf16[768,384]{1,0:T(8,128)(2,1)S(1)} %collective-permute-done.3.refs_4_), channel_id=1, source_target_pairs={{0,1},{1,0},{2,3},{3,2},{4,5},{5,4},{6,7},{7,6},{8,9},{9,8},{10,11... | collective-permute-start | bytes 1769480 | tf_op jit(solution)/shard_map/ppermute | solution.py:39
  79.3 9.7 %collective-permute-start.15 = (bf16[128,768]{1,0:T(8,128)(2,1)S(1)}, bf16[128,768]{1,0:T(8,128)(2,1)S(1)}, u32[]{:S(2)}, u32[]{:S(2)}) collective-permute-start(bf16[128,768]{1,0:T(8,128)(2,1)S(1)} %get-tuple-element.76), channel_id=1, source_target_pairs={{0,2},{1,3},{2,4},{3,5},{4,6},{5,7},{6,0},{7,1},{8,10},{9,11},{10,... | collective-permute-start | bytes 589832 | tf_op jit(solution)/shard_map/ppermute | solution.py:39
  79.3 17.2 %collective-permute-start.14 = (bf16[128,768]{1,0:T(8,128)(2,1)S(1)}, bf16[128,768]{1,0:T(8,128)(2,1)S(1)}, u32[]{:S(2)}, u32[]{:S(2)}) collective-permute-start(bf16[128,768]{1,0:T(8,128)(2,1)S(1)} %get-tuple-element.75), channel_id=1, source_target_pairs={{0,4},{1,5},{2,6},{3,7},{4,0},{5,1},{6,2},{7,3},{8,12},{9,13},{10,... | collective-permute-start | bytes 589832 | tf_op jit(solution)/shard_map/ppermute | solution.py:39
  79.4 17.1 %collective-permute-start.13 = (bf16[128,768]{1,0:T(8,128)(2,1)S(1)}, bf16[128,768]{1,0:T(8,128)(2,1)S(1)}, u32[]{:S(2)}, u32[]{:S(2)}) collective-permute-start(bf16[128,768]{1,0:T(8,128)(2,1)S(1)} %get-tuple-element.74), channel_id=1, source_target_pairs={{0,6},{1,7},{2,0},{3,1},{4,2},{5,3},{6,4},{7,5},{8,14},{9,15},{10,... | collective-permute-start | bytes 589832 | tf_op jit(solution)/shard_map/ppermute | solution.py:39
  83.1 17.5 %collective-permute-start.17 = (bf16[4,2,64,384]{3,2,1,0:T(8,128)(2,1)S(1)}, bf16[4,2,64,384]{3,2,1,0:T(8,128)(2,1)S(1)}, u32[]{:S(2)}, u32[]{:S(2)}) collective-permute-start(bf16[4,2,64,384]{3,2,1,0:T(8,128)(2,1)S(1)} %get-tuple-element.77), channel_id=1, source_target_pairs={{0,1},{1,0},{2,3},{3,2},{4,5},{5,4},{6,7},{7,6},{8,9},{9,8},{10,11... | collective-permute-start | bytes 1179656 | tf_op jit(solution)/shard_map/ppermute | solution.py:39
  89.0 31.8 %collective-permute-start.19 = (bf16[768,384]{1,0:T(8,128)(2,1)S(1)}, bf16[768,384]{1,0:T(8,128)(2,1)S(1)}, u32[]{:S(2)}, u32[]{:S(2)}) collective-permute-start(bf16[768,384]{1,0:T(8,128)(2,1)S(1)} %collective-permute-done.10.refs_6_), channel_id=1, source_target_pairs={{0,1},{1,0},{2,3},{3,2},{4,5},{5,4},{6,7},{7,6},{8,9},{9,8},{10,11... | collective-permute-start | bytes 1769480 | tf_op jit(solution)/shard_map/ppermute | solution.py:39
  100.7 9.7 %collective-permute-start.18 = (bf16[128,768]{1,0:T(8,128)(2,1)S(1)}, bf16[128,768]{1,0:T(8,128)(2,1)S(1)}, u32[]{:S(2)}, u32[]{:S(2)}) collective-permute-start(bf16[128,768]{1,0:T(8,128)(2,1)S(1)} %add_convert_fusion.5.refs_0_), channel_id=1, source_target_pairs={{0,2},{1,3},{2,4},{3,5},{4,6},{5,7},{6,0},{7,1},{8,10},{9,11},{10,... | collective-permute-start | bytes 589832 | tf_op jit(solution)/shard_map/ppermute | solution.py:39
  100.7 15.4 %collective-permute-start.22 = (bf16[128,768]{1,0:T(8,128)(2,1)S(1)}, bf16[128,768]{1,0:T(8,128)(2,1)S(1)}, u32[]{:S(2)}, u32[]{:S(2)}) collective-permute-start(bf16[128,768]{1,0:T(8,128)(2,1)S(1)} %add_convert_fusion.5.refs_0_), channel_id=1, source_target_pairs={{0,4},{1,5},{2,6},{3,7},{4,0},{5,1},{6,2},{7,3},{8,12},{9,13},{10,... | collective-permute-start | bytes 589832 | tf_op jit(solution)/shard_map/ppermute | solution.py:39
  100.7 16.0 %collective-permute-start.24 = (bf16[128,768]{1,0:T(8,128)(2,1)S(1)}, bf16[128,768]{1,0:T(8,128)(2,1)S(1)}, u32[]{:S(2)}, u32[]{:S(2)}) collective-permute-start(bf16[128,768]{1,0:T(8,128)(2,1)S(1)} %add_convert_fusion.5.refs_0_), channel_id=1, source_target_pairs={{0,6},{1,7},{2,0},{3,1},{4,2},{5,3},{6,4},{7,5},{8,14},{9,15},{10,... | collective-permute-start | bytes 589832 | tf_op jit(solution)/shard_map/ppermute | solution.py:39
  104.5 13.6 %collective-permute-start.20 = (bf16[128,768]{1,0:T(8,128)(2,1)S(1)}, bf16[128,768]{1,0:T(8,128)(2,1)S(1)}, u32[]{:S(2)}, u32[]{:S(2)}) collective-permute-start(bf16[128,768]{1,0:T(8,128)(2,1)S(1)} %add_convert_fusion.5.refs_0_), channel_id=1, source_target_pairs={{0,1},{1,0},{2,3},{3,2},{4,5},{5,4},{6,7},{7,6},{8,9},{9,8},{10,11... | collective-permute-start | bytes 589832 | tf_op jit(solution)/shard_map/ppermute | solution.py:39
  110.4 12.3 %collective-permute-start.21 = (bf16[128,768]{1,0:T(8,128)(2,1)S(1)}, bf16[128,768]{1,0:T(8,128)(2,1)S(1)}, u32[]{:S(2)}, u32[]{:S(2)}) collective-permute-start(bf16[128,768]{1,0:T(8,128)(2,1)S(1)} %collective-permute-done.18.refs_2_), channel_id=1, source_target_pairs={{0,1},{1,0},{2,3},{3,2},{4,5},{5,4},{6,7},{7,6},{8,9},{9,8},{10,11... | collective-permute-start | bytes 589832 | tf_op jit(solution)/shard_map/ppermute | solution.py:39
  116.1 11.8 %collective-permute-start.23 = (bf16[128,768]{1,0:T(8,128)(2,1)S(1)}, bf16[128,768]{1,0:T(8,128)(2,1)S(1)}, u32[]{:S(2)}, u32[]{:S(2)}) collective-permute-start(bf16[128,768]{1,0:T(8,128)(2,1)S(1)} %collective-permute-done.22.refs_4_), channel_id=1, source_target_pairs={{0,1},{1,0},{2,3},{3,2},{4,5},{5,4},{6,7},{7,6},{8,9},{9,8},{10,11... | collective-permute-start | bytes 589832 | tf_op jit(solution)/shard_map/ppermute | solution.py:39
  116.7 12.5 %collective-permute-start.25 = (bf16[128,768]{1,0:T(8,128)(2,1)S(1)}, bf16[128,768]{1,0:T(8,128)(2,1)S(1)}, u32[]{:S(2)}, u32[]{:S(2)}) collective-permute-start(bf16[128,768]{1,0:T(8,128)(2,1)S(1)} %collective-permute-done.24.refs_6_), channel_id=1, source_target_pairs={{0,1},{1,0},{2,3},{3,2},{4,5},{5,4},{6,7},{7,6},{8,9},{9,8},{10,11... | collective-permute-start | bytes 589832 | tf_op jit(solution)/shard_map/ppermute | solution.py:39
  118.1 15.8 %collective-permute-start.26 = (bf16[2,2,64,384]{3,2,1,0:T(8,128)(2,1)S(1)}, bf16[2,2,64,384]{3,2,1,0:T(8,128)(2,1)S(1)}, u32[]{:S(2)}, u32[]{:S(2)}) collective-permute-start(bf16[2,2,64,384]{3,2,1,0:T(8,128)(2,1)S(1)} %get-tuple-element.88), channel_id=1, source_target_pairs={{0,2},{1,3},{2,4},{3,5},{4,6},{5,7},{6,0},{7,1},{8,10},{9,11},{10,... | collective-permute-start | bytes 589832 | tf_op jit(solution)/shard_map/ppermute | solution.py:39
  120.8 13.7 %collective-permute-start.27 = (bf16[2,2,64,384]{3,2,1,0:T(8,128)(2,1)S(1)}, bf16[2,2,64,384]{3,2,1,0:T(8,128)(2,1)S(1)}, u32[]{:S(2)}, u32[]{:S(2)}) collective-permute-start(bf16[2,2,64,384]{3,2,1,0:T(8,128)(2,1)S(1)} %get-tuple-element.89), channel_id=1, source_target_pairs={{0,4},{1,5},{2,6},{3,7},{4,0},{5,1},{6,2},{7,3},{8,12},{9,13},{10,... | collective-permute-start | bytes 589832 | tf_op jit(solution)/shard_map/ppermute | solution.py:39
  122.7 6.6 %copy-start.21 = (s32[8]{0:T(128)S(1)}, s32[8]{0:T(128)}, u32[]{:S(2)}) copy-start(s32[8]{0:T(128)} %caption_ref.1) | copy-start | bytes 100
  122.7 12.2 %collective-permute-start.29 = (bf16[2,2,64,384]{3,2,1,0:T(8,128)(2,1)S(1)}, bf16[2,2,64,384]{3,2,1,0:T(8,128)(2,1)S(1)}, u32[]{:S(2)}, u32[]{:S(2)}) collective-permute-start(bf16[2,2,64,384]{3,2,1,0:T(8,128)(2,1)S(1)} %get-tuple-element.91), channel_id=1, source_target_pairs={{0,6},{1,7},{2,0},{3,1},{4,2},{5,3},{6,4},{7,5},{8,14},{9,15},{10,... | collective-permute-start | bytes 589832 | tf_op jit(solution)/shard_map/ppermute | solution.py:39
  134.5 28.0 %collective-permute-start.28 = (bf16[4,128,768]{2,1,0:T(8,128)(2,1)}, bf16[4,128,768]{2,1,0:T(8,128)(2,1)S(1)}, u32[]{:S(2)}, u32[]{:S(2)}) collective-permute-start(bf16[4,128,768]{2,1,0:T(8,128)(2,1)} %get-tuple-element.90), channel_id=1, source_target_pairs={{0,1},{1,0},{2,3},{3,2},{4,5},{5,4},{6,7},{7,6},{8,9},{9,8},{10,11... | collective-permute-start | bytes 2359304 | tf_op jit(solution)/shard_map/ppermute | solution.py:39
  134.8 15.7 %collective-permute-start.32 = (bf16[2,256,384]{2,1,0:T(8,128)(2,1)S(1)}, bf16[2,256,384]{2,1,0:T(8,128)(2,1)S(1)}, u32[]{:S(2)}, u32[]{:S(2)}) collective-permute-start(bf16[2,256,384]{2,1,0:T(8,128)(2,1)S(1)} %get-tuple-element.93.refs_4_), channel_id=1, source_target_pairs={{0,2},{1,3},{2,4},{3,5},{4,6},{5,7},{6,0},{7,1},{8,10},{9,11},{10,... | collective-permute-start | bytes 1179656 | tf_op jit(solution)/shard_map/ppermute | solution.py:39
  139.8 22.7 %collective-permute-start.30 = (bf16[4,2,2,64,384]{4,3,2,1,0:T(8,128)(2,1)S(1)}, bf16[4,2,2,64,384]{4,3,2,1,0:T(8,128)(2,1)S(1)}, u32[]{:S(2)}, u32[]{:S(2)}) collective-permute-start(bf16[4,2,2,64,384]{4,3,2,1,0:T(8,128)(2,1)S(1)} %pad_maximum_fusion.refs_0_), channel_id=1, source_target_pairs={{0,16},{8,24},{16,0},{24,8},{1,17},{9,25},{17,1},{25,9},{2,18},{10... | collective-permute-start | bytes 2359304 | tf_op jit(solution)/shard_map/ppermute | solution.py:43
  141.3 21.2 %collective-permute-start.31 = (bf16[2,256,384]{2,1,0:T(8,128)(2,1)S(1)}, bf16[2,256,384]{2,1,0:T(8,128)(2,1)S(1)}, u32[]{:S(2)}, u32[]{:S(2)}) collective-permute-start(bf16[2,256,384]{2,1,0:T(8,128)(2,1)S(1)} %get-tuple-element.93.refs_4_), channel_id=1, source_target_pairs={{0,1},{1,0},{2,3},{3,2},{4,5},{5,4},{6,7},{7,6},{8,9},{9,8},{10,11... | collective-permute-start | bytes 1179656 | tf_op jit(solution)/shard_map/ppermute | solution.py:39
  150.6 11.9 %collective-permute-start.33 = (bf16[2,256,384]{2,1,0:T(8,128)(2,1)S(1)}, bf16[2,256,384]{2,1,0:T(8,128)(2,1)S(1)}, u32[]{:S(2)}, u32[]{:S(2)}) collective-permute-start(bf16[2,256,384]{2,1,0:T(8,128)(2,1)S(1)} %collective-permute-done.32.refs_6_), channel_id=1, source_target_pairs={{0,2},{1,3},{2,4},{3,5},{4,6},{5,7},{6,0},{7,1},{8,10},{9,11},{10,... | collective-permute-start | bytes 1179656 | tf_op jit(solution)/shard_map/ppermute | solution.py:39
  162.5 7.8 %copy-start.9 = (bf16[2,256,384]{2,1,0:T(8,128)(2,1)}, bf16[2,256,384]{2,1,0:T(8,128)(2,1)S(1)}, u32[]{:S(2)}) copy-start(bf16[2,256,384]{2,1,0:T(8,128)(2,1)S(1)} %collective-permute-done.31.refs_5_) | copy-start | bytes 1179652
  162.5 7.9 %copy-start.25 = (bf16[4,128,768]{2,1,0:T(8,128)(2,1)}, bf16[4,128,768]{2,1,0:T(8,128)(2,1)S(1)}, u32[]{:S(2)}) copy-start(bf16[4,128,768]{2,1,0:T(8,128)(2,1)S(1)} %collective-permute-done.28) | copy-start | bytes 2359300
  162.5 7.8 %copy-start.23 = (bf16[4,2,2,64,384]{4,3,2,1,0:T(8,128)(2,1)}, bf16[4,2,2,64,384]{4,3,2,1,0:T(8,128)(2,1)S(1)}, u32[]{:S(2)}) copy-start(bf16[4,2,2,64,384]{4,3,2,1,0:T(8,128)(2,1)S(1)} %collective-permute-done.30.refs_2_) | copy-start | bytes 2359300
  170.2 14.5 %copy-start.28 = (bf16[2,256,768]{2,1,0:T(8,128)(2,1)S(1)}, bf16[2,256,768]{2,1,0:T(8,128)(2,1)}, u32[]{:S(2)}) copy-start(bf16[2,256,768]{2,1,0:T(8,128)(2,1)} %get-tuple-element.98) | copy-start | bytes 2359300
  170.2 11.6 %collective-permute-start.34 = (bf16[2,256,1536]{2,1,0:T(8,128)(2,1)}, bf16[2,256,1536]{2,1,0:T(8,128)(2,1)}, u32[]{:S(2)}, u32[]{:S(2)}) collective-permute-start(bf16[2,256,1536]{2,1,0:T(8,128)(2,1)} %get-tuple-element.97), channel_id=1, source_target_pairs={{0,8},{8,0},{16,24},{24,16},{1,9},{9,1},{17,25},{25,17},{2,10},{10... | collective-permute-start | bytes 4718600 | tf_op jit(solution)/shard_map/ppermute | solution.py:43
  170.3 3.4 %collective-permute-start.36 = (f32[256,2]{1,0:T(8,128)}, f32[256,2]{1,0:T(8,128)S(1)}, u32[]{:S(2)}, u32[]{:S(2)}) collective-permute-start(f32[256,2]{1,0:T(8,128)} %get-tuple-element.100), channel_id=1, source_target_pairs={{0,8},{8,0},{16,24},{24,16},{1,9},{9,1},{17,25},{25,17},{2,10},{10... | collective-permute-start | bytes 6152 | tf_op jit(solution)/shard_map/ppermute | solution.py:43
  172.9 40.5 %collective-permute-start.38 = (bf16[4,2,2,64,384]{4,3,2,1,0:T(8,128)(2,1)S(1)}, bf16[4,2,2,64,384]{4,3,2,1,0:T(8,128)(2,1)S(1)}, u32[]{:S(2)}, u32[]{:S(2)}) collective-permute-start(bf16[4,2,2,64,384]{4,3,2,1,0:T(8,128)(2,1)S(1)} %pad_maximum_fusion.refs_0_), channel_id=1, source_target_pairs={{0,8},{8,0},{16,24},{24,16},{1,9},{9,1},{17,25},{25,17},{2,10},{10... | collective-permute-start | bytes 2359304 | tf_op jit(solution)/shard_map/ppermute | solution.py:43
  174.7 11.4 %collective-permute-start.37 = (f32[256,2]{1,0:T(8,128)S(1)}, f32[256,2]{1,0:T(8,128)S(1)}, u32[]{:S(2)}, u32[]{:S(2)}) collective-permute-start(f32[256,2]{1,0:T(8,128)S(1)} %add.79), channel_id=1, source_target_pairs={{0,16},{8,24},{16,0},{24,8},{1,17},{9,25},{17,1},{25,9},{2,18},{10... | collective-permute-start | bytes 6152 | tf_op jit(solution)/shard_map/ppermute | solution.py:43
  176.2 22.3 %collective-permute-start.40 = (bf16[2,256,384]{2,1,0:T(8,128)(2,1)S(1)}, bf16[2,256,384]{2,1,0:T(8,128)(2,1)S(1)}, u32[]{:S(2)}, u32[]{:S(2)}) collective-permute-start(bf16[2,256,384]{2,1,0:T(8,128)(2,1)S(1)} %collective-permute-done.32.refs_6_), channel_id=1, source_target_pairs={{0,1},{1,0},{2,3},{3,2},{4,5},{5,4},{6,7},{7,6},{8,9},{9,8},{10,11... | collective-permute-start | bytes 1179656 | tf_op jit(solution)/shard_map/ppermute | solution.py:39
  176.6 21.9 %collective-permute-start.42 = (bf16[2,256,384]{2,1,0:T(8,128)(2,1)}, bf16[2,256,384]{2,1,0:T(8,128)(2,1)S(1)}, u32[]{:S(2)}, u32[]{:S(2)}) collective-permute-start(bf16[2,256,384]{2,1,0:T(8,128)(2,1)} %copy-done.11), channel_id=1, source_target_pairs={{0,2},{1,3},{2,4},{3,5},{4,6},{5,7},{6,0},{7,1},{8,10},{9,11},{10,... | collective-permute-start | bytes 1179656 | tf_op jit(solution)/shard_map/ppermute | solution.py:39
  181.9 16.6 %copy-start.24 = (bf16[4,2,2,64,384]{4,3,2,1,0:T(8,128)(2,1)S(1)}, bf16[4,2,2,64,384]{4,3,2,1,0:T(8,128)(2,1)}, u32[]{:S(2)}) copy-start(bf16[4,2,2,64,384]{4,3,2,1,0:T(8,128)(2,1)} %copy-done.23) | copy-start | bytes 2359300
  181.9 27.7 %copy-start.12 = (bf16[2,256,384]{2,1,0:T(8,128)(2,1)S(1)}, bf16[2,256,384]{2,1,0:T(8,128)(2,1)}, u32[]{:S(2)}) copy-start(bf16[2,256,384]{2,1,0:T(8,128)(2,1)} %copy-done.11) | copy-start | bytes 1179652
  181.9 14.8 %collective-permute-start.46 = (bf16[128,768]{1,0:T(8,128)(2,1)S(1)}, bf16[128,768]{1,0:T(8,128)(2,1)S(1)}, u32[]{:S(2)}, u32[]{:S(2)}) collective-permute-start(bf16[128,768]{1,0:T(8,128)(2,1)S(1)} %get-tuple-element.113), channel_id=1, source_target_pairs={{0,6},{1,7},{2,0},{3,1},{4,2},{5,3},{6,4},{7,5},{8,14},{9,15},{10,... | collective-permute-start | bytes 589832 | tf_op jit(solution)/shard_map/ppermute | solution.py:39
  186.1 43.0 %copy-start.10 = (bf16[2,256,384]{2,1,0:T(8,128)(2,1)S(1)}, bf16[2,256,384]{2,1,0:T(8,128)(2,1)}, u32[]{:S(2)}) copy-start(bf16[2,256,384]{2,1,0:T(8,128)(2,1)} %copy-done.9) | copy-start | bytes 1179652
  186.1 23.5 %collective-permute-start.45 = (bf16[128,768]{1,0:T(8,128)(2,1)S(1)}, bf16[128,768]{1,0:T(8,128)(2,1)S(1)}, u32[]{:S(2)}, u32[]{:S(2)}) collective-permute-start(bf16[128,768]{1,0:T(8,128)(2,1)S(1)} %get-tuple-element.114), channel_id=1, source_target_pairs={{0,4},{1,5},{2,6},{3,7},{4,0},{5,1},{6,2},{7,3},{8,12},{9,13},{10,... | collective-permute-start | bytes 589832 | tf_op jit(solution)/shard_map/ppermute | solution.py:39
  196.7 13.4 %collective-permute-start.44 = (bf16[128,768]{1,0:T(8,128)(2,1)S(1)}, bf16[128,768]{1,0:T(8,128)(2,1)S(1)}, u32[]{:S(2)}, u32[]{:S(2)}) collective-permute-start(bf16[128,768]{1,0:T(8,128)(2,1)S(1)} %get-tuple-element.112), channel_id=1, source_target_pairs={{0,2},{1,3},{2,4},{3,5},{4,6},{5,7},{6,0},{7,1},{8,10},{9,11},{10,... | collective-permute-start | bytes 589832 | tf_op jit(solution)/shard_map/ppermute | solution.py:39
  198.5 23.1 %collective-permute-start.39 = (bf16[4,2,2,64,384]{4,3,2,1,0:T(8,128)(2,1)S(1)}, bf16[4,2,2,64,384]{4,3,2,1,0:T(8,128)(2,1)S(1)}, u32[]{:S(2)}, u32[]{:S(2)}) collective-permute-start(bf16[4,2,2,64,384]{4,3,2,1,0:T(8,128)(2,1)S(1)} %copy-done.24), channel_id=1, source_target_pairs={{0,8},{8,0},{16,24},{24,16},{1,9},{9,1},{17,25},{25,17},{2,10},{10... | collective-permute-start | bytes 2359304 | tf_op jit(solution)/shard_map/ppermute | solution.py:43
  198.5 34.9 %collective-permute-start.35 = (bf16[2,256,768]{2,1,0:T(8,128)(2,1)S(1)}, bf16[2,256,768]{2,1,0:T(8,128)(2,1)S(1)}, u32[]{:S(2)}, u32[]{:S(2)}) collective-permute-start(bf16[2,256,768]{2,1,0:T(8,128)(2,1)S(1)} %add_convert_fusion), channel_id=1, source_target_pairs={{0,16},{8,24},{16,0},{24,8},{1,17},{9,25},{17,1},{25,9},{2,18},{10... | collective-permute-start | bytes 2359304 | tf_op jit(solution)/shard_map/ppermute | solution.py:43
  209.6 12.0 %collective-permute-start.41 = (bf16[2,256,384]{2,1,0:T(8,128)(2,1)S(1)}, bf16[2,256,384]{2,1,0:T(8,128)(2,1)S(1)}, u32[]{:S(2)}, u32[]{:S(2)}) collective-permute-start(bf16[2,256,384]{2,1,0:T(8,128)(2,1)S(1)} %copy-done.12), channel_id=1, source_target_pairs={{0,1},{1,0},{2,3},{3,2},{4,5},{5,4},{6,7},{7,6},{8,9},{9,8},{10,11... | collective-permute-start | bytes 1179656 | tf_op jit(solution)/shard_map/ppermute | solution.py:39
  210.1 18.9 %collective-permute-start.43 = (bf16[2,256,384]{2,1,0:T(8,128)(2,1)S(1)}, bf16[2,256,384]{2,1,0:T(8,128)(2,1)S(1)}, u32[]{:S(2)}, u32[]{:S(2)}) collective-permute-start(bf16[2,256,384]{2,1,0:T(8,128)(2,1)S(1)} %collective-permute-done.42.refs_10_), channel_id=1, source_target_pairs={{0,1},{1,0},{2,3},{3,2},{4,5},{5,4},{6,7},{7,6},{8,9},{9,8},{10,11... | collective-permute-start | bytes 1179656 | tf_op jit(solution)/shard_map/ppermute | solution.py:39
  213.4 20.0 %copy-start.29 = (bf16[2,256,768]{2,1,0:T(8,128)(2,1)S(1)}, bf16[2,256,768]{2,1,0:T(8,128)(2,1)}, u32[]{:S(2)}) copy-start(bf16[2,256,768]{2,1,0:T(8,128)(2,1)} %get-tuple-element.96) | copy-start | bytes 2359300
  213.4 15.7 %copy-start.26 = (bf16[4,2,2,64,384]{4,3,2,1,0:T(8,128)(2,1)}, bf16[4,2,2,64,384]{4,3,2,1,0:T(8,128)(2,1)S(1)}, u32[]{:S(2)}) copy-start(bf16[4,2,2,64,384]{4,3,2,1,0:T(8,128)(2,1)S(1)} %collective-permute-done.38.refs_1_) | copy-start | bytes 2359300
  221.6 7.5 %copy-start.27 = (bf16[4,2,2,64,384]{4,3,2,1,0:T(8,128)(2,1)}, bf16[4,2,2,64,384]{4,3,2,1,0:T(8,128)(2,1)S(1)}, u32[]{:S(2)}) copy-start(bf16[4,2,2,64,384]{4,3,2,1,0:T(8,128)(2,1)S(1)} %collective-permute-done.39.refs_3_) | copy-start | bytes 2359300
  (14 other events, 26.4 us)

commit v4 on v3

--- a/solution.py
+++ b/solution.py
@@ -11,7 +11,7 @@
 BF = jnp.bfloat16
 F32 = jnp.float32
 SLOTS = 3
-VMEM_BYTES = 50 * 1024 * 1024
+VMEM_BYTES = 60 * 1024 * 1024
 SMALL = pl.CostEstimate(flops=1, bytes_accessed=1, transcendentals=0)
 
 
@@ -320,32 +320,16 @@
     return pl.multiple_of(start, unit)
 
 
-def project_text(states, gain, weights, sent, steps=4):
+def project_text(states, gain, weights, steps=4):
     rows, depth = states.shape
     width = weights[0].shape[1]
     chunk = depth // steps
-    starts = [sum(a.shape[0] for a in sent[:k]) for k in range(len(sent) + 1)]
-
-    def body(states_ref, gain_ref, wq_ref, wk_ref, wv_ref, *refs):
-        sent_refs = refs[: len(sent)]
-        out_ref, few_ref, all_ref, normed_ref, total_ref, sems = refs[len(sent) :]
+
+    def body(states_ref, gain_ref, wq_ref, wk_ref, wv_ref, out_ref, normed_ref, total_ref):
         step = pl.program_id(0)
-
-        def copies():
-            made = []
-            for k, source in enumerate(sent_refs):
-                to = slice(starts[k], starts[k + 1])
-                made.append(pltpu.make_async_copy(source, all_ref.at[to], sems.at[k]))
-                if k < 2:
-                    made.append(
-                        pltpu.make_async_copy(source, few_ref.at[to], sems.at[len(sent) + k])
-                    )
-            return made
 
         @pl.when(step == 0)
         def _():
-            for copy in copies():
-                copy.start()
             for at in range(0, rows, 16):
                 values = states_ref[at : at + 16, :].astype(F32)
                 normed_ref[at : at + 16, :] = rms_scale(values, gain_ref[...]).astype(BF)
@@ -358,28 +342,19 @@
         @pl.when(step == steps - 1)
         def _():
             out_ref[...] = total_ref[...].astype(BF)
-            for copy in copies():
-                copy.wait()
 
     whole = lambda shape: pl.BlockSpec(shape, lambda i: (0,) * len(shape))
-    wide = sent[0].shape[1]
-    out = [shaped((rows, 3 * width)), shaped((starts[2], wide)), shaped((starts[-1], wide))]
     return pl.pallas_call(
         body,
         grid=(steps,),
-        out_shape=out,
+        out_shape=shaped((rows, 3 * width)),
         in_specs=[whole((rows, depth)), whole((1, depth))]
-        + [pl.BlockSpec((chunk, width), lambda i: (i, 0))] * 3
-        + [pl.BlockSpec(memory_space=pl.ANY)] * len(sent),
-        out_specs=[whole(out[0].shape)] + [pl.BlockSpec(memory_space=pl.ANY)] * 2,
-        scratch_shapes=[
-            pltpu.VMEM((rows, depth), BF),
-            pltpu.VMEM((rows, 3 * width), F32),
-            pltpu.SemaphoreType.DMA((len(sent) + 2,)),
-        ],
+        + [pl.BlockSpec((chunk, width), lambda i: (i, 0))] * 3,
+        out_specs=whole((rows, 3 * width)),
+        scratch_shapes=[pltpu.VMEM((rows, depth), BF), pltpu.VMEM((rows, 3 * width), F32)],
         compiler_params=pltpu.CompilerParams(vmem_limit_bytes=VMEM_BYTES),
         cost_estimate=SMALL,
-    )(states, gain.reshape(1, -1), *weights, *sent)
+    )(states, gain.reshape(1, -1), *weights)
 
 
 def attend_text(projected, bias, text_out, place, lens, steps=4):
@@ -448,6 +423,18 @@
     return call(body, out, operands, 1, [pltpu.VMEM((quarter_rows, width), BF)])
 
 
+def pieces_of(pairs_of_blocks):
+    arrays, listed = [], []
+    for entry in pairs_of_blocks:
+        numbers = []
+        for array, start in entry:
+            if not any(array is held for held in arrays):
+                arrays.append(array)
+            numbers.append((next(k for k, held in enumerate(arrays) if held is array), start))
+        listed.append(numbers)
+    return arrays, listed
+
+
 def prepare_video(video_states, out_grad, place, pairs, part):
     tokens, model_width = video_states.shape
     rows = tokens // 4
@@ -480,7 +467,8 @@
 
 def project_rows(normed, out_grad, blocks, place, pairs, part):
     tokens = normed.shape[0]
-    width = blocks[0].shape[1]
+    arrays, blocks = pieces_of(blocks)
+    width = arrays[0].shape[1]
 
     def body(place_ref, normed_ref, grad_ref, *refs):
         block_refs, (query_ref, d_ref, sum_ref) = refs[:-3], refs[-3:]
@@ -490,44 +478,45 @@
         total = jnp.zeros((1, width), F32)
         for far in range(pairs):
             for side in range(2):
-                block = block_refs[2 * far + side]
+                (of_query, query_at), (of_out, out_at) = blocks[2 * far + side]
                 origin = lax.rem(z - far + pairs, pairs) * 2 + (y ^ side)
                 columns = pl.ds(aligned(origin * part, 128), part)
-                weight = block[:part, :]
+                weight = block_refs[of_query][query_at : query_at + part, :]
+                out_weight = block_refs[of_out][out_at : out_at + width, :]
                 query += mm(normed_ref[:, columns], weight)
-                d_attended += contract_last(grad_ref[:, columns], block[part : part + width, :])
+                d_attended += contract_last(grad_ref[:, columns], out_weight)
                 total += jnp.sum(weight.astype(F32), axis=0, keepdims=True)
         query_ref[...] = query.astype(BF)
         d_ref[...] = d_attended.astype(BF)
         sum_ref[...] = total
 
     out = [shaped((tokens, width)), shaped((tokens, width)), shaped((1, width), F32)]
-    return call(body, out, (place, normed, out_grad, *blocks), 1)
-
-
-def project_captions(parts, own_key, own_value, side_block, place, pairs, skip):
+    return call(body, out, (place, normed, out_grad, *arrays), 1)
+
+
+def project_captions(parts, own_key, own_value, side_key, side_value, place, pairs):
     quarter_rows, depth = parts[0].shape[1:]
     half = depth // 2
     width = own_key.shape[1]
 
     def body(place_ref, *refs):
         part_refs = refs[:4]
-        key_ref, value_ref, side_ref = refs[4:7]
-        out_refs = refs[7:]
+        key_ref, value_ref, side_key_ref, side_value_ref = refs[4:8]
+        out_refs = refs[8:]
         y = place_ref[1]
         mine = pl.ds(aligned(y * half, 128), half)
         theirs = pl.ds(aligned((1 - y) * half, 128), half)
         own = jnp.concatenate([r[far, :, mine] for far in range(pairs) for r in part_refs], 0)
         other = jnp.concatenate([r[far, :, theirs] for far in range(pairs) for r in part_refs], 0)
-        keys = mm(own, key_ref[...]) + mm(other, side_ref[skip : skip + half, :])
-        values = mm(own, value_ref[...]) + mm(other, side_ref[skip + half : skip + 2 * half, :])
+        keys = mm(own, key_ref[...]) + mm(other, side_key_ref[...])
+        values = mm(own, value_ref[...]) + mm(other, side_value_ref[...])
         for far in range(pairs):
             rows = slice(far * 4 * quarter_rows, (far + 1) * 4 * quarter_rows)
             out_refs[far][:, :width] = keys[rows].astype(BF)
             out_refs[far][:, width:] = values[rows].astype(BF)
 
     out = [shaped((4 * quarter_rows, 2 * width))] * pairs
-    operands = (place, *parts, own_key, own_value, side_block)
+    operands = (place, *parts, own_key, own_value, side_key, side_value)
     return call(body, out, operands, 1)
 
 
@@ -643,25 +632,28 @@
 
 def project_back(attended, d_queries, blocks, place, pairs, part):
     tokens, width = attended.shape
+    arrays, blocks = pieces_of(blocks)
     model_width = 2 * pairs * part
     per_piece = 2 * pairs // 4
     piece = model_width // 4
 
     def body(place_ref, att_ref, dq_ref, *refs):
-        block_refs = refs[: len(blocks)]
-        own_ref, far_ref, away_ref = refs[len(blocks) :]
+        block_refs = refs[: len(arrays)]
+        own_ref, far_ref, away_ref = refs[len(arrays) :]
         z, y, g = place_ref[0], place_ref[1], place_ref[2]
         att, d_query = att_ref[...], dq_ref[...]
         for far in range(pairs):
             for side in range(2):
-                block = block_refs[2 * far + side]
+                (of_query, query_at), (of_out, out_at) = blocks[2 * far + side]
+                weight = block_refs[of_query][query_at : query_at + part, :]
+                out_weight = block_refs[of_out][out_at : out_at + width, :]
                 origin = lax.rem(z - far + pairs, pairs) * 2 + (y ^ side)
                 flip = (origin // per_piece) ^ g
                 start = lax.rem(origin, per_piece) * part
                 columns = pl.ds(aligned(start, 128), part)
                 beyond = pl.ds(aligned(start + piece, 128), part)
-                added = mm(att, block[part : part + width, :]).astype(BF)
-                d_normed = contract_last(d_query, block[:part, :]).astype(BF)
+                added = mm(att, out_weight).astype(BF)
+                d_normed = contract_last(d_query, weight).astype(BF)
                 places = ((own_ref, columns), (away_ref, columns), (far_ref, columns), (away_ref, beyond))
                 for number, (target_ref, to) in enumerate(places):
 
@@ -671,12 +663,13 @@
                         target_ref[1, :, to] = d_normed
 
     out = [shaped((2, tokens, piece)), shaped((2, tokens, piece)), shaped((2, tokens, 2 * piece))]
-    return call(body, out, (place, attended, d_queries, *blocks), 1)
+    return call(body, out, (place, attended, d_queries, *arrays), 1)
 
 
 def weight_grads(tiles, both_blocks, pairs):
     part = tiles[0].shape[-1]
-    width = both_blocks[0].shape[-1]
+    arrays, blocks = pieces_of(both_blocks)
+    width = arrays[0].shape[-1]
 
     def body(*refs):
         tile_refs, block_refs, (query_ref, out_ref) = refs[:4], refs[4:-2], refs[-2:]
@@ -684,18 +677,19 @@
         out_grad = jnp.zeros((width, part), F32)
         for far in range(pairs):
             for side in range(2):
-                block = block_refs[2 * far + side]
+                ((number, at),) = blocks[2 * far + side]
+                block = block_refs[number]
                 normed, grad = (
                     jnp.concatenate([r[far, side, which] for r in tile_refs], axis=0)
                     for which in range(2)
                 )
-                out_grad += contract_first(block[0], grad)
-                query_grad += contract_first(normed, block[1])
+                out_grad += contract_first(block[at], grad)
+                query_grad += contract_first(normed, block[at + 1])
         query_ref[...] = query_grad
         out_ref[...] = out_grad
 
     out = [shaped((part, width), F32), shaped((width, part), F32)]
-    return call(body, out, (*tiles, *both_blocks), 0)
+    return call(body, out, (*tiles, *arrays), 0)
 
 
 def local(
@@ -727,54 +721,55 @@
     width_local = cross_key.shape[1]
     part = cross_query.shape[0]
 
-    weights = (cross_query, cross_out, cross_key, cross_value)
     states = caption_states.reshape(cap_len, text_width)
-
-    projected, own_weights, own_blocks = project_text(
-        states, text_gain, (text_query, text_key, text_value), weights
-    )
-    ring = [own_weights, fsend(own_weights, 1, 0)]
-    side_block = fsend(own_blocks, 0, 1)
+    quarter_rows = cap_len // 4
+
+    first = [fsend(cross_query, 1, 0), fsend(cross_out, 1, 0)]
+    side_key, side_value = fsend(cross_key, 0, 1), fsend(cross_value, 0, 1)
+    projected = project_text(states, text_gain, (text_query, text_key, text_value))
     kept, away = attend_text(projected, text_bias, text_out, place, caption_lens)
-    quarter_rows = cap_len // 4
+    kept, away = after((kept, away), first, side_key, side_value)
     got = gsend(away, 1)
+    ring = [None, jnp.concatenate(first, axis=0)]
+    side_first = fsend(jnp.concatenate([cross_query, cross_out, *first], axis=0), 0, 1)
+    ring.append(fsend(ring[1], 1, 0))
+    sent = (kept[quarter_rows:].astype(F32) + got[quarter_rows:].astype(F32)).astype(BF)
+    over_x = gsend(sent, 2)
     normed, mean, inverse, own_tiles, other_tiles = prepare_video(
-        after(video_states, kept), out_grad, place, pairs, part
-    )
-    over_core = after(got, ring[1], normed)
-    sent = (kept[quarter_rows:].astype(F32) + over_core[quarter_rows:].astype(F32)).astype(BF)
-    ring.append(fsend(after(ring[1], over_core), 1, 0))
-    over_x = gsend(sent, 2)
-    pieces = encode_rows(
-        states, kept, over_core, after(over_x, ring[2]), final_gain, place, pairs
-    )
+        after(video_states, sent), out_grad, place, pairs, part
+    )
+    pieces = encode_rows(states, kept, got, over_x, final_gain, place, pairs)
 
     mine = jnp.stack([fsend(p, far, 0) if far else p for far, p in enumerate(pieces)])
+    mine = after(mine, ring[2])
     over_x = gsend(mine, 2)
     parts = [mine, gsend(mine, 1), over_x, gsend(over_x, 1)]
-    current = after(ring[2], pieces[0])
+    current = after(ring[2], mine)
     for far in range(3, pairs):
         current = fsend(current, 1, 0)
         ring.append(current)
-    blocks = [own_weights, side_block]
-    for block in ring[1:]:
-        blocks += [block, fsend(block, 0, 1)]
-    other_tiles = fsend(other_tiles, 0, 1)
-
-    parts[3] = after(parts[3], ring[-1], blocks[3])
+    parts[3] = after(parts[3], side_first)
     kv_partial = project_captions(
-        parts, cross_key, cross_value, side_block, place, pairs, own_weights.shape[0]
-    )
+        parts, cross_key, cross_value, side_key, side_value, place, pairs
+    )
+    kv_partial = after(tuple(kv_partial), ring[-1])
     kv_sum = kv_partial[0].astype(F32)
     for far in range(1, pairs):
         kv_sum += fsend(kv_partial[far], pairs - far, 0).astype(F32)
-    kv_sum = after(kv_sum.astype(BF), blocks[5], other_tiles)
+    side_later = [fsend(w, 0, 1) for w in ring[2:]]
+    other_tiles = fsend(other_tiles, 0, 1)
+    kv_sum = after(kv_sum.astype(BF), side_later[0])
     kv_blocks = gather_direct(kv_sum)
-    for k in range(7, len(blocks), 2):
-        kv_blocks[2] = after(kv_blocks[2], blocks[k])
-
+    kv_blocks[4] = after(kv_blocks[4], side_later, other_tiles)
+
+    step = part + width_local
+    blocks = []
+    for far, held in enumerate(ring):
+        side, start = (side_first, far * step) if far < 2 else (side_later[far - 2], 0)
+        here = ((held, 0), (held, part)) if far else ((cross_query, 0), (cross_out, 0))
+        blocks += [here, ((side, start), (side, start + part))]
     queries, d_attended, column_sum = project_rows(
-        normed, after(out_grad, kv_blocks[2]), blocks, place, pairs, part
+        normed, after(out_grad, kv_blocks[4]), blocks, place, pairs, part
     )
 
     tiles = jnp.stack([own_tiles, other_tiles], axis=1)
@@ -792,29 +787,39 @@
         caption_lens,
         pairs,
     )
-    kv_away, both = after((kv_away, both), over_z[1:-1])
+    kv_away, both, row_sums = after((kv_away, both, row_sums), over_z[1:-1])
+
     kv_side = fsend(kv_away, 0, 1)
-    both_blocks = [both, fsend(both, 0, 1)]
-    waits = [kv_side, both_blocks[1]]
-    current = after(both, over_z[-1])
-    for far in range(1, pairs):
-        current = fsend(current, 1, 0)
-        side = fsend(after(current, waits[far - 1]), 0, 1)
-        both_blocks += [current, side]
-        waits.append(side)
+    late = [both, fsend(both, 1, 0)]
+    sums_core = gsend(row_sums, 1)
     tiles = jnp.stack(over_z)
+    attended = after(attended, late[1])
+    own, far_piece, away = project_back(attended, d_queries, blocks, place, pairs, part)
+    kv_side, late, sums_core, tiles, away = after((kv_side, late, sums_core, tiles, away))
+
+    sides = [fsend(jnp.stack(late[:2]).reshape(4, tokens, width_local), 0, 1)]
+    late = list(late)
+    for far in range(2, pairs):
+        late.append(fsend(late[-1], 1, 0))
     tiles_x = gsend(tiles, 2)
     tiles_core = gsend(tiles, 1)
-    row_sums = row_sums + gsend(row_sums, 1)
-    row_sums = (row_sums + gsend(row_sums, 2)) / model_width
-
-    attended = after(attended, kv_side, tiles_x, both_blocks[1], both_blocks[4])
-    own, far_piece, away = project_back(attended, d_queries, blocks, place, pairs, part)
+    row_sums = row_sums + sums_core
+    sums_x = gsend(row_sums, 2)
+    got = gsend(away, 1)
+    done = after((sides[0], late, tiles_x, tiles_core, sums_x, got, kv_side))
+    sides[0], late, tiles_x, tiles_core, sums_x, got, kv_side = done
+
+    for far in range(2, pairs, 2):
+        stacked = jnp.stack(late[far : far + 2])
+        sides.append(fsend(stacked.reshape(-1, tokens, width_local), 0, 1))
+    both_blocks = []
+    for far in range(pairs):
+        both_blocks += [((late[far], 0),), ((sides[far // 2], far % 2 * 2),)]
     width = model_width // 4
-    got = gsend(away, 1)
     sent = (far_piece.astype(F32) + got[:, :, width:].astype(F32)).astype(BF)
     far_sum = gsend(sent, 2)
     total = own.astype(F32) + got[:, :, :width].astype(F32) + far_sum.astype(F32)
+    row_sums = (row_sums + sums_x) / model_width
     video = quarter(video_states, g, 1).astype(F32)
     updated = (video + total[0]).astype(BF)
     video_hat = (video - mean) * inverse

time: 238 us -> 205 us (0.86)
  waiting for transfers between devices: 124 us -> 82.7 us
  Pallas kernels: 40.2 us -> 53 us
  local copies, waits for them, and re-layouts: 10.1 us -> 6.18 us
    ppermute x35, waiting for transfers between devices: 111 us -> 64.5 us  [fsend(): return lax.ppermute(block, 'fsdp', perm)]
    pallas_call x7, Pallas kernels: 27.4 us -> 37.9 us  [call(): pl.pallas_call(body, out_shape=out_shape, in_specs=specs, out_specs=jax.t...]
    ppermute x12, waiting for transfers between devices: 12.7 us -> 18.2 us  [gsend(): lax.ppermute(block, 'grp', [(s, s ^ flip) for s in range(lax.axis_size('g...]
    unnamed x62 -> x81, local copies, waits for them, and re-layouts: 9.17 us -> 5.24 us
  transfers between devices with their start and end apart: 47 -> 47, of which waited for: 22 -> 19; matrix products, arithmetic and copies ran while one was open for 3% -> 6% of each run, Pallas kernels for 11% -> 23%
where the time goes in v4:
time: 205 us; the launch traced here: 204 us
  waiting for transfers between devices  82.7 us (40%)
  Pallas kernels  53 us (26%)
  starting transfers between devices  49 us (24%)
  other arithmetic  12.5 us (6%)
  local copies, waits for them, and re-layouts  6.18 us (3%)
    ppermute x35, waiting for transfers between devices, fsend(): return lax.ppermute(block, 'fsdp', perm)  64.5 us
    ppermute x35, starting transfers between devices, fsend(): return lax.ppermute(block, 'fsdp', perm)  41.7 us
    pallas_call x7, Pallas kernels, call(): pl.pallas_call(body, out_shape=out_shape, in_specs=specs, out_specs=jax.t...  37.9 us
    ppermute x12, waiting for transfers between devices, gsend(): lax.ppermute(block, 'grp', [(s, s ^ flip) for s in range(lax.axis_size('g...  18.2 us
    pallas_call x1, Pallas kernels, project_text(): pl.pallas_call(body, grid=(steps,), out_shape=shaped((rows, 3 * width)),...  7.96 us
    ppermute x12, starting transfers between devices, gsend(): lax.ppermute(block, 'grp', [(s, s ^ flip) for s in range(lax.axis_size('g...  7.29 us
    pallas_call x1, Pallas kernels, attend_text(): pl.pallas_call(body, grid=(steps,), out_shape=[shaped((rows // 2, depth))...  7.16 us
    unnamed x81, local copies, waits for them, and re-layouts  5.24 us
  transfers between devices with their start and end apart: 47, of which 19 were waited for; matrix products, arithmetic and copies ran while one was open for 6% of the time, Pallas kernels for 23%

profile of v4, /device:TPU:0, one launch (start us, length us, event | category | flops | bytes accessed | tf_op | source)
XLA Modules:
  0.0 204.5 jit_solution(5561593386918546038)
XLA Ops:
  0.6 3.0 %collective-permute-start.2 = (bf16[512,384]{1,0:T(8,128)(2,1)}, bf16[512,384]{1,0:T(8,128)(2,1)S(1)}, u32[]{:S(2)}, u32[]{:S(2)}) collective-permute-start(bf16[512,384]{1,0:T(8,128)(2,1)} %refs_4_.1), channel_id=1, source_target_pairs={{0,1},{1,0},{2,3},{3,2},{4,5},{5,4},{6,7},{7,6},{8,9},{9,8},{10,11... | collective-permute-start | bytes 1179656 | tf_op jit(solution)/shard_map/ppermute | solution.py:39
  3.7 2.0 collective-permute-start
  5.7 1.6 collective-permute-start.1
  7.3 8.0 %shard_map.208.qkv_ref = bf16[128,1536]{1,0:T(8,128)(2,1)} custom-call(bf16[128,4096]{1,0:T(8,128)(2,1)} %bitcast.55, f32[1,4096]{1,0:T(1,128)} %bitcast.71, bf16[4096,512]{1,0:T(8,128)(2,1)} %wq_ref.1, bf16[4096,512]{1,0:T(8,128)(2,1)} %wk_ref.1, bf16[4096,512]{1,0:T(8,128)(2,1)} %wv_ref.1), custom_call_target="tpu_custom_call" | custom-call | flops 1 | bytes 1 | tf_op jit(solution)/shard_map/pallas_call | solution.py:347
  15.9 7.2 %shard_map.209 = (bf16[64,4096]{1,0:T(8,128)(2,1)}, bf16[64,4096]{1,0:T(8,128)(2,1)}) custom-call(s32[3]{0:T(128)} %pad_add_fusion.place_ref, s32[8]{0:T(128)} %len_ref.3, bf16[128,1536]{1,0:T(8,128)(2,1)} %shard_map.208.qkv_ref, f32[8,128,128]{2,1,0:T(8,128)} %bias_ref.1, bf16[512,4096]{1,0:T(8,128)(2,1)} %out_ref.1), custom_call_target="tpu_custom_call" | custom-call | flops 1 | bytes 1 | tf_op jit(solution)/shard_map/pallas_call | solution.py:391
  23.3 1.6 collective-permute-start.9
  24.9 1.1 pad_maximum_fusion
  26.1 1.5 collective-permute-start.13
  27.7 1.6 collective-permute-start.5
  29.2 6.7 %collective-permute-done.5.far_ref = bf16[32,4096]{1,0:T(8,128)(2,1)S(1)} collective-permute-done((bf16[32,4096]{1,0:T(8,128)(2,1)S(1)}, bf16[32,4096]{1,0:T(8,128)(2,1)S(1)}, u32[]{:S(2)}, u32[]{:S(2)}) %collective-permute-start.5) | collective-permute-done | bytes 262176 | tf_op jit(solution)/shard_map/ppermute | solution.py:43
  35.9 0.7 copy-done.30
  36.6 2.6 %shard_map.211 = (bf16[32,1024]{1,0:T(8,128)(2,1)}, bf16[32,1024]{1,0:T(8,128)(2,1)}, bf16[32,1024]{1,0:T(8,128)(2,1)}, bf16[32,1024]{1,0:T(8,128)(2,1)}) custom-call(s32[3]{0:T(128)} %pad_add_fusion.place_ref, bf16[128,4096]{1,0:T(8,128)(2,1)} %bitcast.56, bf16[64,4096]{1,0:T(8,128)(2,1)} %get-tuple-element.73.kept_ref, bf16[64,4096]{1,0:T(8,128)(2,1)} %copy-done.14, ...), custom_call_target="tpu_custom_call" | custom-call | flops 1 | bytes 1 | tf_op jit(solution)/shard_map/pallas_call | solution.py:304
  39.5 2.5 %collective-permute-start.7 = (bf16[32,1024]{1,0:T(8,128)(2,1)}, bf16[32,1024]{1,0:T(8,128)(2,1)S(1)}, u32[]{:S(2)}, u32[]{:S(2)}) collective-permute-start(bf16[32,1024]{1,0:T(8,128)(2,1)} %get-tuple-element.79), channel_id=1, source_target_pairs={{0,4},{1,5},{2,6},{3,7},{4,0},{5,1},{6,2},{7,3},{8,12},{9,13},{10,... | collective-permute-start | bytes 196616 | tf_op jit(solution)/shard_map/ppermute | solution.py:39
  42.0 1.4 collective-permute-start.8
  43.3 2.4 %collective-permute-done.6 = bf16[32,1024]{1,0:T(8,128)(2,1)S(1)} collective-permute-done((bf16[32,1024]{1,0:T(8,128)(2,1)}, bf16[32,1024]{1,0:T(8,128)(2,1)S(1)}, u32[]{:S(2)}, u32[]{:S(2)}) %collective-permute-start.6) | collective-permute-done | bytes 65568 | tf_op jit(solution)/shard_map/ppermute | solution.py:39
  45.7 1.2 collective-permute-done.7
  47.0 0.9 pad_maximum_fusion.4.refs_0_
  47.9 1.4 collective-permute-start.14
  49.3 1.5 collective-permute-start.11
  50.8 5.9 %collective-permute-done.11.refs_2_ = bf16[4,32,1024]{2,1,0:T(8,128)(2,1)S(1)} collective-permute-done((bf16[4,32,1024]{2,1,0:T(8,128)(2,1)S(1)}, bf16[4,32,1024]{2,1,0:T(8,128)(2,1)S(1)}, u32[]{:S(2)}, u32[]{:S(2)}) %collective-permute-start.11) | collective-permute-done | bytes 262176 | tf_op jit(solution)/shard_map/ppermute | solution.py:43
  58.9 0.7 copy-done.29
  59.6 3.7 %shard_map.212 = (bf16[128,768]{1,0:T(8,128)(2,1)}, bf16[128,768]{1,0:T(8,128)(2,1)}, bf16[128,768]{1,0:T(8,128)(2,1)}, bf16[128,768]{1,0:T(8,128)(2,1)}) custom-call(s32[3]{0:T(128)} %pad_add_fusion.place_ref, bf16[4,32,1024]{2,1,0:T(8,128)(2,1)} %copy-done.15, bf16[4,32,1024]{2,1,0:T(8,128)(2,1)} %copy-done.29, bf16[4,32,1024]{2,1,0:T(8,128)(2,1)} %copy-done.27, ...), custom_call_target="tpu_custom_call" | custom-call | flops 1 | bytes 1 | tf_op jit(solution)/shard_map/pallas_call | solution.py:304
  63.4 1.7 collective-permute-start.15
  65.5 1.7 collective-permute-start.17
  67.2 1.0 collective-permute-start.20
  68.2 5.5 %shard_map.210 = (bf16[256,3072]{1,0:T(8,128)(2,1)}, f32[256,1]{1,0:T(8,128)}, f32[256,1]{1,0:T(8,128)}, bf16[4,2,64,384]{3,2,1,0:T(8,128)(2,1)}, bf16[4,2,64,384]{3,2,1,0:T(8,128)(2,1)}) custom-call(s32[3]{0:T(128)} %pad_add_fusion.place_ref, bf16[256,3072]{1,0:T(8,128)(2,1)} %video_ref, bf16[256,3072]{1,0:T(8,128)(2,1)} %grad_ref.2), custom_call_target="tpu_custom_call" | custom-call | flops 1 | bytes 1 | tf_op jit(solution)/shard_map/pallas_call | solution.py:304
  73.8 1.0 collective-permute-start.21
  74.8 8.4 %collective-permute-done.16 = bf16[128,768]{1,0:T(8,128)(2,1)S(1)} collective-permute-done((bf16[128,768]{1,0:T(8,128)(2,1)}, bf16[128,768]{1,0:T(8,128)(2,1)S(1)}, u32[]{:S(2)}, u32[]{:S(2)}) %collective-permute-start.16) | collective-permute-done | bytes 196640 | tf_op jit(solution)/shard_map/ppermute | solution.py:39
  83.2 1.0 add_convert_fusion.5.refs_0_
  84.4 2.0 collective-permute-start.23
  86.4 2.6 %collective-permute-start.19 = (bf16[128,768]{1,0:T(8,128)(2,1)S(1)}, bf16[128,768]{1,0:T(8,128)(2,1)S(1)}, u32[]{:S(2)}, u32[]{:S(2)}) collective-permute-start(bf16[128,768]{1,0:T(8,128)(2,1)S(1)} %add_convert_fusion.5.refs_0_), channel_id=1, source_target_pairs={{0,4},{1,5},{2,6},{3,7},{4,0},{5,1},{6,2},{7,3},{8,12},{9,13},{10,... | collective-permute-start | bytes 589832 | tf_op jit(solution)/shard_map/ppermute | solution.py:39
  88.9 4.6 %collective-permute-done.21 = bf16[4,2,64,384]{3,2,1,0:T(8,128)(2,1)S(1)} collective-permute-done((bf16[4,2,64,384]{3,2,1,0:T(8,128)(2,1)}, bf16[4,2,64,384]{3,2,1,0:T(8,128)(2,1)S(1)}, u32[]{:S(2)}, u32[]{:S(2)}) %collective-permute-start.21) | collective-permute-done | bytes 393248 | tf_op jit(solution)/shard_map/ppermute | solution.py:39
  94.0 1.1 fusion.15
  95.2 1.6 collective-permute-start.27
  96.8 1.7 collective-permute-done.23.refs_2_
  99.1 5.6 %collective-permute-done.19.refs_4_ = bf16[128,768]{1,0:T(8,128)(2,1)S(1)} collective-permute-done((bf16[128,768]{1,0:T(8,128)(2,1)S(1)}, bf16[128,768]{1,0:T(8,128)(2,1)S(1)}, u32[]{:S(2)}, u32[]{:S(2)}) %collective-permute-start.19) | collective-permute-done | bytes 196640 | tf_op jit(solution)/shard_map/ppermute | solution.py:39
  105.3 0.9 collective-permute-start.28
  106.2 6.1 %shard_map.213 = (bf16[256,384]{1,0:T(8,128)(2,1)}, bf16[256,384]{1,0:T(8,128)(2,1)}, f32[1,384]{1,0:T(1,128)}) custom-call(s32[3]{0:T(128)} %pad_add_fusion.place_ref, bf16[256,3072]{1,0:T(8,128)(2,1)} %get-tuple-element.76.normed_ref, bf16[256,3072]{1,0:T(8,128)(2,1)} %grad_ref.2, bf16[384,384]{1,0:T(8,128)(2,1)} %refs_0_.3, bf16[384,384]{1,0:T(8,128)(2,1)} %refs_1_.3, ...), custom_call_target="tpu_custom_call" | custom-call | flops 1 | bytes 1 | tf_op jit(solution)/shard_map/pallas_call | solution.py:304
  113.0 6.2 %shard_map.214 = (bf16[2,256,384]{2,1,0:T(8,128)(2,1)}, bf16[256,384]{1,0:T(8,128)(2,1)}, bf16[256,384]{1,0:T(8,128)(2,1)}, f32[256,2]{1,0:T(8,128)}, bf16[4,128...) custom-call(s32[3]{0:T(128)} %pad_add_fusion.place_ref, s32[8]{0:T(128)} %count_ref.1, s32[8]{0:T(128)} %caption_ref.1, ...), custom_call_target="tpu_custom_call" | custom-call | flops 1 | bytes 1 | tf_op jit(solution)/shard_map/pallas_call | solution.py:304
  119.2 1.7 collective-permute-start.31
  120.8 2.4 %collective-permute-start.30 = (bf16[2,256,384]{2,1,0:T(8,128)(2,1)}, bf16[2,256,384]{2,1,0:T(8,128)(2,1)S(1)}, u32[]{:S(2)}, u32[]{:S(2)}) collective-permute-start(bf16[2,256,384]{2,1,0:T(8,128)(2,1)} %get-tuple-element.127.refs_4_), channel_id=1, source_target_pairs={{0,2},{1,3},{2,4},{3,5},{4,6},{5,7},{6,0},{7,1},{8,10},{9,11},{10,... | collective-permute-start | bytes 1179656 | tf_op jit(solution)/shard_map/ppermute | solution.py:39
  123.2 1.4 collective-permute-start.33
  124.7 11.9 %collective-permute-done.33 = bf16[2,2,64,384]{3,2,1,0:T(8,128)(2,1)S(1)} collective-permute-done((bf16[2,2,64,384]{3,2,1,0:T(8,128)(2,1)S(1)}, bf16[2,2,64,384]{3,2,1,0:T(8,128)(2,1)S(1)}, u32[]{:S(2)}, u32[]{:S(2)}) %collective-permute-start.33) | collective-permute-done | bytes 196640 | tf_op jit(solution)/shard_map/ppermute | solution.py:39
  136.7 8.3 %shard_map.215 = (bf16[2,256,768]{2,1,0:T(8,128)(2,1)}, bf16[2,256,768]{2,1,0:T(8,128)(2,1)}, bf16[2,256,1536]{2,1,0:T(8,128)(2,1)}) custom-call(s32[3]{0:T(128)} %pad_add_fusion.place_ref, bf16[256,384]{1,0:T(8,128)(2,1)} %get-tuple-element.107.att_ref, bf16[256,384]{1,0:T(8,128)(2,1)} %get-tuple-element.108.dq_ref, bf16[384,384]{1,0:T(8,128)(2,1)} %refs_0_.3, ...), custom_call_target="tpu_custom_call" | custom-call | flops 1 | bytes 1 | tf_op jit(solution)/shard_map/pallas_call | solution.py:304
  145.1 0.9 copy-done.17
  146.1 1.6 collective-permute-start.39
  148.3 1.0 pad_maximum_fusion.2
  149.6 2.5 %collective-permute-done.39 = f32[256,2]{1,0:T(8,128)S(1)} collective-permute-done((f32[256,2]{1,0:T(8,128)S(1)}, f32[256,2]{1,0:T(8,128)S(1)}, u32[]{:S(2)}, u32[]{:S(2)}) %collective-permute-start.39) | collective-permute-done | bytes 2080 | tf_op jit(solution)/shard_map/ppermute | solution.py:43
  152.1 1.5 collective-permute-start.37
  153.6 7.1 %collective-permute-done.35.refs_7_ = bf16[2,256,384]{2,1,0:T(8,128)(2,1)S(1)} collective-permute-done((bf16[2,256,384]{2,1,0:T(8,128)(2,1)S(1)}, bf16[2,256,384]{2,1,0:T(8,128)(2,1)S(1)}, u32[]{:S(2)}, u32[]{:S(2)}) %collective-permute-start.35) | collective-permute-done | bytes 393248 | tf_op jit(solution)/shard_map/ppermute | solution.py:39
  160.8 1.1 reduce
  161.9 1.0 reduce.2
  162.9 6.1 %collective-permute-done.34.refs_5_ = bf16[4,256,384]{2,1,0:T(8,128)(2,1)} collective-permute-done((bf16[4,256,384]{2,1,0:T(8,128)(2,1)}, bf16[4,256,384]{2,1,0:T(8,128)(2,1)}, u32[]{:S(2)}, u32[]{:S(2)}) %collective-permute-start.34) | collective-permute-done | bytes 786464 | tf_op jit(solution)/shard_map/ppermute | solution.py:39
  169.0 2.3 %collective-permute-done.37.refs_2_ = bf16[4,2,2,64,384]{4,3,2,1,0:T(8,128)(2,1)} collective-permute-done((bf16[4,2,2,64,384]{4,3,2,1,0:T(8,128)(2,1)S(1)}, bf16[4,2,2,64,384]{4,3,2,1,0:T(8,128)(2,1)}, u32[]{:S(2)}, u32[]{:S(2)}) %collective-permute-start.37) | collective-permute-done | bytes 786464 | tf_op jit(solution)/shard_map/ppermute | solution.py:43
  171.3 1.6 collective-permute-done.36.refs_9_
  173.0 1.5 add_convert_fusion
  175.4 3.8 %collective-permute-start.46 = (bf16[128,768]{1,0:T(8,128)(2,1)S(1)}, bf16[128,768]{1,0:T(8,128)(2,1)S(1)}, u32[]{:S(2)}, u32[]{:S(2)}) collective-permute-start(bf16[128,768]{1,0:T(8,128)(2,1)S(1)} %get-tuple-element.141), channel_id=1, source_target_pairs={{0,6},{1,7},{2,0},{3,1},{4,2},{5,3},{6,4},{7,5},{8,14},{9,15},{10,... | collective-permute-start | bytes 589832 | tf_op jit(solution)/shard_map/ppermute | solution.py:39
  180.1 4.9 %collective-permute-done.44 = bf16[128,768]{1,0:T(8,128)(2,1)S(1)} collective-permute-done((bf16[128,768]{1,0:T(8,128)(2,1)S(1)}, bf16[128,768]{1,0:T(8,128)(2,1)S(1)}, u32[]{:S(2)}, u32[]{:S(2)}) %collective-permute-start.44) | collective-permute-done | bytes 196640 | tf_op jit(solution)/shard_map/ppermute | solution.py:39
  185.0 8.8 %collective-permute-done.45 = bf16[128,768]{1,0:T(8,128)(2,1)S(1)} collective-permute-done((bf16[128,768]{1,0:T(8,128)(2,1)S(1)}, bf16[128,768]{1,0:T(8,128)(2,1)S(1)}, u32[]{:S(2)}, u32[]{:S(2)}) %collective-permute-start.45) | collective-permute-done | bytes 196640 | tf_op jit(solution)/shard_map/ppermute | solution.py:39
  194.0 0.7 fusion.21
  194.9 2.3 %fusion.6 = (bf16[256,768]{1,0:T(8,128)(2,1)}, bf16[256,768]{1,0:T(8,128)(2,1)}) fusion(f32[2,256,768]{2,1,0:T(8,128)S(1)} %convert_add_fusion, f32[256]{0:T(256)S(1)} %get-tuple-element.137, f32[256]{0:T(256)S(1)} %reduce.2, f32[256]{0:T(256)S(1)} %get-tuple-element.136, f32[256]{0:T(256)S(1)} %reduce, bf16[256,3072]{1,0:T(8,128)(2,1)} %grad_ref.2, ...), kind=kLoop, calls=%fused_computation.17 | loop fusion | flops 2359296 | bytes 3149828 | tf_op jit(solution)/shard_map/convert_element_type | solution.py:829
  197.2 0.9 copy-done.19
  198.1 0.9 copy-done.20
  199.0 5.5 %shard_map.216 = (f32[384,384]{1,0:T(8,128)}, f32[384,384]{1,0:T(8,128)}) custom-call(bf16[4,2,2,64,384]{4,3,2,1,0:T(8,128)(2,1)} %copy-done.2, bf16[4,2,2,64,384]{4,3,2,1,0:T(8,128)(2,1)} %collective-permute-done.38.refs_1_, bf16[4,2,2,64,384]{4,3,2,1,0:T(8,128)(2,1)} %collective-permute-done.37.refs_2_, bf16[4,2,2,64,384]{4,3,2,1,0:T(8,128)(2,1)} %copy-done.20, ...), custom_call_target="tpu_custom_call" | custom-call | flops 1 | bytes 1 | tf_op jit(solution)/shard_map/pallas_call | solution.py:304
  (141 shorter events, 9.8 us)
Async XLA Ops:
  0.6 22.4 %collective-permute-start.2 = (bf16[512,384]{1,0:T(8,128)(2,1)}, bf16[512,384]{1,0:T(8,128)(2,1)S(1)}, u32[]{:S(2)}, u32[]{:S(2)}) collective-permute-start(bf16[512,384]{1,0:T(8,128)(2,1)} %refs_4_.1), channel_id=1, source_target_pairs={{0,1},{1,0},{2,3},{3,2},{4,5},{5,4},{6,7},{7,6},{8,9},{9,8},{10,11... | collective-permute-start | bytes 1179656 | tf_op jit(solution)/shard_map/ppermute | solution.py:39
  3.7 19.4 %collective-permute-start.3 = (bf16[512,384]{1,0:T(8,128)(2,1)}, bf16[512,384]{1,0:T(8,128)(2,1)S(1)}, u32[]{:S(2)}, u32[]{:S(2)}) collective-permute-start(bf16[512,384]{1,0:T(8,128)(2,1)} %refs_5_.1), channel_id=1, source_target_pairs={{0,1},{1,0},{2,3},{3,2},{4,5},{5,4},{6,7},{7,6},{8,9},{9,8},{10,11... | collective-permute-start | bytes 1179656 | tf_op jit(solution)/shard_map/ppermute | solution.py:39
  3.7 19.3 %collective-permute-start = (bf16[384,384]{1,0:T(8,128)(2,1)}, bf16[384,384]{1,0:T(8,128)(2,1)S(1)}, u32[]{:S(2)}, u32[]{:S(2)}) collective-permute-start(bf16[384,384]{1,0:T(8,128)(2,1)} %refs_0_.3), channel_id=1, source_target_pairs={{0,2},{1,3},{2,4},{3,5},{4,6},{5,7},{6,0},{7,1},{8,10},{9,11},{10,... | collective-permute-start | bytes 884744 | tf_op jit(solution)/shard_map/ppermute | solution.py:39
  5.7 17.3 %collective-permute-start.1 = (bf16[384,384]{1,0:T(8,128)(2,1)}, bf16[384,384]{1,0:T(8,128)(2,1)S(1)}, u32[]{:S(2)}, u32[]{:S(2)}) collective-permute-start(bf16[384,384]{1,0:T(8,128)(2,1)} %refs_1_.3), channel_id=1, source_target_pairs={{0,2},{1,3},{2,4},{3,5},{4,6},{5,7},{6,0},{7,1},{8,10},{9,11},{10,... | collective-permute-start | bytes 884744 | tf_op jit(solution)/shard_map/ppermute | solution.py:39
  23.1 4.5 %collective-permute-start.4 = (bf16[64,4096]{1,0:T(8,128)(2,1)}, bf16[64,4096]{1,0:T(8,128)(2,1)S(1)}, u32[]{:S(2)}, u32[]{:S(2)}) collective-permute-start(bf16[64,4096]{1,0:T(8,128)(2,1)} %get-tuple-element.74), channel_id=1, source_target_pairs={{0,8},{8,0},{16,24},{24,16},{1,9},{9,1},{17,25},{25,17},{2,10},{10... | collective-permute-start | bytes 1572872 | tf_op jit(solution)/shard_map/ppermute | solution.py:43
  23.3 24.6 %collective-permute-start.9 = (bf16[768,384]{1,0:T(8,128)(2,1)S(1)}, bf16[768,384]{1,0:T(8,128)(2,1)S(1)}, u32[]{:S(2)}, u32[]{:S(2)}) collective-permute-start(bf16[768,384]{1,0:T(8,128)(2,1)S(1)} %constant_dynamic-update-slice_fusion.refs_3_), channel_id=1, source_target_pairs={{0,2},{1,3},{2,4},{3,5},{4,6},{5,7},{6,0},{7,1},{8,10},{9,11},{10,... | collective-permute-start | bytes 1769480 | tf_op jit(solution)/shard_map/ppermute | solution.py:39
  26.1 31.6 %collective-permute-start.13 = (bf16[1536,384]{1,0:T(8,128)(2,1)}, bf16[1536,384]{1,0:T(8,128)(2,1)S(1)}, u32[]{:S(2)}, u32[]{:S(2)}) collective-permute-start(bf16[1536,384]{1,0:T(8,128)(2,1)} %pad_maximum_fusion), channel_id=1, source_target_pairs={{0,1},{1,0},{2,3},{3,2},{4,5},{5,4},{6,7},{7,6},{8,9},{9,8},{10,11... | collective-permute-start | bytes 3538952 | tf_op jit(solution)/shard_map/ppermute | solution.py:39
  27.7 8.2 %collective-permute-start.5 = (bf16[32,4096]{1,0:T(8,128)(2,1)S(1)}, bf16[32,4096]{1,0:T(8,128)(2,1)S(1)}, u32[]{:S(2)}, u32[]{:S(2)}) collective-permute-start(bf16[32,4096]{1,0:T(8,128)(2,1)S(1)} %add_convert_fusion.1), channel_id=1, source_target_pairs={{0,16},{8,24},{16,0},{24,8},{1,17},{9,25},{17,1},{25,9},{2,18},{10... | collective-permute-start | bytes 786440 | tf_op jit(solution)/shard_map/ppermute | solution.py:43
  39.2 6.6 %collective-permute-start.6 = (bf16[32,1024]{1,0:T(8,128)(2,1)}, bf16[32,1024]{1,0:T(8,128)(2,1)S(1)}, u32[]{:S(2)}, u32[]{:S(2)}) collective-permute-start(bf16[32,1024]{1,0:T(8,128)(2,1)} %get-tuple-element.78), channel_id=1, source_target_pairs={{0,2},{1,3},{2,4},{3,5},{4,6},{5,7},{6,0},{7,1},{8,10},{9,11},{10,... | collective-permute-start | bytes 196616 | tf_op jit(solution)/shard_map/ppermute | solution.py:39
  39.5 7.5 %collective-permute-start.7 = (bf16[32,1024]{1,0:T(8,128)(2,1)}, bf16[32,1024]{1,0:T(8,128)(2,1)S(1)}, u32[]{:S(2)}, u32[]{:S(2)}) collective-permute-start(bf16[32,1024]{1,0:T(8,128)(2,1)} %get-tuple-element.79), channel_id=1, source_target_pairs={{0,4},{1,5},{2,6},{3,7},{4,0},{5,1},{6,2},{7,3},{8,12},{9,13},{10,... | collective-permute-start | bytes 196616 | tf_op jit(solution)/shard_map/ppermute | solution.py:39
  42.0 5.0 %collective-permute-start.8 = (bf16[32,1024]{1,0:T(8,128)(2,1)}, bf16[32,1024]{1,0:T(8,128)(2,1)S(1)}, u32[]{:S(2)}, u32[]{:S(2)}) collective-permute-start(bf16[32,1024]{1,0:T(8,128)(2,1)} %get-tuple-element.80), channel_id=1, source_target_pairs={{0,6},{1,7},{2,0},{3,1},{4,2},{5,3},{6,4},{7,5},{8,14},{9,15},{10,... | collective-permute-start | bytes 196616 | tf_op jit(solution)/shard_map/ppermute | solution.py:39
  47.9 10.7 %copy-start.15 = (bf16[4,32,1024]{2,1,0:T(8,128)(2,1)}, bf16[4,32,1024]{2,1,0:T(8,128)(2,1)S(1)}, u32[]{:S(2)}) copy-start(bf16[4,32,1024]{2,1,0:T(8,128)(2,1)S(1)} %pad_maximum_fusion.4.refs_0_) | copy-start | bytes 786436
  47.9 25.9 %copy-start.5 = (bf16[768,384]{1,0:T(8,128)(2,1)}, bf16[768,384]{1,0:T(8,128)(2,1)S(1)}, u32[]{:S(2)}) copy-start(bf16[768,384]{1,0:T(8,128)(2,1)S(1)} %collective-permute-done.9.refs_4_) | copy-start | bytes 1769476
  47.9 15.5 %collective-permute-start.14 = (bf16[768,384]{1,0:T(8,128)(2,1)S(1)}, bf16[768,384]{1,0:T(8,128)(2,1)S(1)}, u32[]{:S(2)}, u32[]{:S(2)}) collective-permute-start(bf16[768,384]{1,0:T(8,128)(2,1)S(1)} %collective-permute-done.9.refs_4_), channel_id=1, source_target_pairs={{0,2},{1,3},{2,4},{3,5},{4,6},{5,7},{6,0},{7,1},{8,10},{9,11},{10,... | collective-permute-start | bytes 1769480 | tf_op jit(solution)/shard_map/ppermute | solution.py:39
  49.3 7.4 %collective-permute-start.11 = (bf16[4,32,1024]{2,1,0:T(8,128)(2,1)S(1)}, bf16[4,32,1024]{2,1,0:T(8,128)(2,1)S(1)}, u32[]{:S(2)}, u32[]{:S(2)}) collective-permute-start(bf16[4,32,1024]{2,1,0:T(8,128)(2,1)S(1)} %pad_maximum_fusion.4.refs_0_), channel_id=1, source_target_pairs={{0,16},{8,24},{16,0},{24,8},{1,17},{9,25},{17,1},{25,9},{2,18},{10... | collective-permute-start | bytes 786440 | tf_op jit(solution)/shard_map/ppermute | solution.py:43
  56.7 1.5 collective-permute-start.12
  56.7 1.9 collective-permute-start.10
  57.2 27.1 %collective-permute-start.18 = (bf16[768,384]{1,0:T(8,128)(2,1)S(1)}, bf16[768,384]{1,0:T(8,128)(2,1)S(1)}, u32[]{:S(2)}, u32[]{:S(2)}) collective-permute-start(bf16[768,384]{1,0:T(8,128)(2,1)S(1)} %collective-permute-done.9.refs_4_), channel_id=1, source_target_pairs={{0,1},{1,0},{2,3},{3,2},{4,5},{5,4},{6,7},{7,6},{8,9},{9,8},{10,11... | collective-permute-start | bytes 1769480 | tf_op jit(solution)/shard_map/ppermute | solution.py:39
  57.7 16.1 %copy-start = (bf16[1536,384]{1,0:T(8,128)(2,1)}, bf16[1536,384]{1,0:T(8,128)(2,1)S(1)}, u32[]{:S(2)}) copy-start(bf16[1536,384]{1,0:T(8,128)(2,1)S(1)} %collective-permute-done.13.refs_2_) | copy-start | bytes 3538948
  63.4 10.3 %copy-start.6 = (bf16[768,384]{1,0:T(8,128)(2,1)}, bf16[768,384]{1,0:T(8,128)(2,1)S(1)}, u32[]{:S(2)}) copy-start(bf16[768,384]{1,0:T(8,128)(2,1)S(1)} %collective-permute-done.14.refs_6_) | copy-start | bytes 1769476
  63.4 19.8 %copy-start.36 = (bf16[128,768]{1,0:T(8,128)(2,1)S(1)}, bf16[128,768]{1,0:T(8,128)(2,1)}, u32[]{:S(2)}) copy-start(bf16[128,768]{1,0:T(8,128)(2,1)} %get-tuple-element.88) | copy-start | bytes 589828
  63.4 10.3 %collective-permute-start.15 = (bf16[128,768]{1,0:T(8,128)(2,1)}, bf16[128,768]{1,0:T(8,128)(2,1)S(1)}, u32[]{:S(2)}, u32[]{:S(2)}) collective-permute-start(bf16[128,768]{1,0:T(8,128)(2,1)} %get-tuple-element.89), channel_id=1, source_target_pairs={{0,6},{1,7},{2,0},{3,1},{4,2},{5,3},{6,4},{7,5},{8,14},{9,15},{10,... | collective-permute-start | bytes 589832 | tf_op jit(solution)/shard_map/ppermute | solution.py:39
  65.2 18.0 %collective-permute-start.16 = (bf16[128,768]{1,0:T(8,128)(2,1)}, bf16[128,768]{1,0:T(8,128)(2,1)S(1)}, u32[]{:S(2)}, u32[]{:S(2)}) collective-permute-start(bf16[128,768]{1,0:T(8,128)(2,1)} %get-tuple-element.90), channel_id=1, source_target_pairs={{0,4},{1,5},{2,6},{3,7},{4,0},{5,1},{6,2},{7,3},{8,12},{9,13},{10,... | collective-permute-start | bytes 589832 | tf_op jit(solution)/shard_map/ppermute | solution.py:39
  65.5 17.8 %collective-permute-start.17 = (bf16[128,768]{1,0:T(8,128)(2,1)}, bf16[128,768]{1,0:T(8,128)(2,1)}, u32[]{:S(2)}, u32[]{:S(2)}) collective-permute-start(bf16[128,768]{1,0:T(8,128)(2,1)} %get-tuple-element.91), channel_id=1, source_target_pairs={{0,2},{1,3},{2,4},{3,5},{4,6},{5,7},{6,0},{7,1},{8,10},{9,11},{10,... | collective-permute-start | bytes 589832 | tf_op jit(solution)/shard_map/ppermute | solution.py:39
  67.2 38.1 %collective-permute-start.20 = (bf16[768,384]{1,0:T(8,128)(2,1)S(1)}, bf16[768,384]{1,0:T(8,128)(2,1)S(1)}, u32[]{:S(2)}, u32[]{:S(2)}) collective-permute-start(bf16[768,384]{1,0:T(8,128)(2,1)S(1)} %collective-permute-done.14.refs_6_), channel_id=1, source_target_pairs={{0,1},{1,0},{2,3},{3,2},{4,5},{5,4},{6,7},{7,6},{8,9},{9,8},{10,11... | collective-permute-start | bytes 1769480 | tf_op jit(solution)/shard_map/ppermute | solution.py:39
  73.8 19.7 %collective-permute-start.21 = (bf16[4,2,64,384]{3,2,1,0:T(8,128)(2,1)}, bf16[4,2,64,384]{3,2,1,0:T(8,128)(2,1)S(1)}, u32[]{:S(2)}, u32[]{:S(2)}) collective-permute-start(bf16[4,2,64,384]{3,2,1,0:T(8,128)(2,1)} %get-tuple-element.93), channel_id=1, source_target_pairs={{0,1},{1,0},{2,3},{3,2},{4,5},{5,4},{6,7},{7,6},{8,9},{9,8},{10,11... | collective-permute-start | bytes 1179656 | tf_op jit(solution)/shard_map/ppermute | solution.py:39
  84.3 28.0 %copy-start.21 = (bf16[128,768]{1,0:T(8,128)(2,1)}, bf16[128,768]{1,0:T(8,128)(2,1)S(1)}, u32[]{:S(2)}) copy-start(bf16[128,768]{1,0:T(8,128)(2,1)S(1)} %add_convert_fusion.5.refs_0_) | copy-start | bytes 589828
  84.3 21.9 %copy-start.7 = (bf16[768,384]{1,0:T(8,128)(2,1)}, bf16[768,384]{1,0:T(8,128)(2,1)S(1)}, u32[]{:S(2)}) copy-start(bf16[768,384]{1,0:T(8,128)(2,1)S(1)} %collective-permute-done.18.refs_5_) | copy-start | bytes 1769476
  84.3 10.8 %collective-permute-start.26 = (bf16[128,768]{1,0:T(8,128)(2,1)S(1)}, bf16[128,768]{1,0:T(8,128)(2,1)S(1)}, u32[]{:S(2)}, u32[]{:S(2)}) collective-permute-start(bf16[128,768]{1,0:T(8,128)(2,1)S(1)} %add_convert_fusion.5.refs_0_), channel_id=1, source_target_pairs={{0,6},{1,7},{2,0},{3,1},{4,2},{5,3},{6,4},{7,5},{8,14},{9,15},{10,... | collective-permute-start | bytes 589832 | tf_op jit(solution)/shard_map/ppermute | solution.py:39
  84.4 14.1 %collective-permute-start.23 = (bf16[128,768]{1,0:T(8,128)(2,1)S(1)}, bf16[128,768]{1,0:T(8,128)(2,1)S(1)}, u32[]{:S(2)}, u32[]{:S(2)}) collective-permute-start(bf16[128,768]{1,0:T(8,128)(2,1)S(1)} %add_convert_fusion.5.refs_0_), channel_id=1, source_target_pairs={{0,2},{1,3},{2,4},{3,5},{4,6},{5,7},{6,0},{7,1},{8,10},{9,11},{10,... | collective-permute-start | bytes 589832 | tf_op jit(solution)/shard_map/ppermute | solution.py:39
  86.4 18.3 %collective-permute-start.19 = (bf16[128,768]{1,0:T(8,128)(2,1)S(1)}, bf16[128,768]{1,0:T(8,128)(2,1)S(1)}, u32[]{:S(2)}, u32[]{:S(2)}) collective-permute-start(bf16[128,768]{1,0:T(8,128)(2,1)S(1)} %add_convert_fusion.5.refs_0_), channel_id=1, source_target_pairs={{0,4},{1,5},{2,6},{3,7},{4,0},{5,1},{6,2},{7,3},{8,12},{9,13},{10,... | collective-permute-start | bytes 589832 | tf_op jit(solution)/shard_map/ppermute | solution.py:39
  93.5 11.8 %collective-permute-start.22 = (bf16[128,768]{1,0:T(8,128)(2,1)S(1)}, bf16[128,768]{1,0:T(8,128)(2,1)S(1)}, u32[]{:S(2)}, u32[]{:S(2)}) collective-permute-start(bf16[128,768]{1,0:T(8,128)(2,1)S(1)} %add_convert_fusion.5.refs_0_), channel_id=1, source_target_pairs={{0,1},{1,0},{2,3},{3,2},{4,5},{5,4},{6,7},{7,6},{8,9},{9,8},{10,11... | collective-permute-start | bytes 589832 | tf_op jit(solution)/shard_map/ppermute | solution.py:39
  95.1 17.2 %copy-start.31 = (bf16[128,768]{1,0:T(8,128)(2,1)}, bf16[128,768]{1,0:T(8,128)(2,1)S(1)}, u32[]{:S(2)}) copy-start(bf16[128,768]{1,0:T(8,128)(2,1)S(1)} %collective-permute-done.26.refs_6_) | copy-start | bytes 589828
  95.2 17.2 %collective-permute-start.27 = (bf16[128,768]{1,0:T(8,128)(2,1)S(1)}, bf16[128,768]{1,0:T(8,128)(2,1)S(1)}, u32[]{:S(2)}, u32[]{:S(2)}) collective-permute-start(bf16[128,768]{1,0:T(8,128)(2,1)S(1)} %collective-permute-done.26.refs_6_), channel_id=1, source_target_pairs={{0,1},{1,0},{2,3},{3,2},{4,5},{5,4},{6,7},{7,6},{8,9},{9,8},{10,11... | collective-permute-start | bytes 589832 | tf_op jit(solution)/shard_map/ppermute | solution.py:39
  98.4 13.9 %copy-start.32 = (bf16[128,768]{1,0:T(8,128)(2,1)}, bf16[128,768]{1,0:T(8,128)(2,1)S(1)}, u32[]{:S(2)}) copy-start(bf16[128,768]{1,0:T(8,128)(2,1)S(1)} %collective-permute-done.23.refs_2_) | copy-start | bytes 589828
  98.4 13.9 %collective-permute-start.24 = (bf16[128,768]{1,0:T(8,128)(2,1)S(1)}, bf16[128,768]{1,0:T(8,128)(2,1)}, u32[]{:S(2)}, u32[]{:S(2)}) collective-permute-start(bf16[128,768]{1,0:T(8,128)(2,1)S(1)} %collective-permute-done.23.refs_2_), channel_id=1, source_target_pairs={{0,1},{1,0},{2,3},{3,2},{4,5},{5,4},{6,7},{7,6},{8,9},{9,8},{10,11... | collective-permute-start | bytes 589832 | tf_op jit(solution)/shard_map/ppermute | solution.py:39
  104.6 7.7 %collective-permute-start.25 = (bf16[128,768]{1,0:T(8,128)(2,1)S(1)}, bf16[128,768]{1,0:T(8,128)(2,1)}, u32[]{:S(2)}, u32[]{:S(2)}) collective-permute-start(bf16[128,768]{1,0:T(8,128)(2,1)S(1)} %collective-permute-done.19.refs_4_), channel_id=1, source_target_pairs={{0,1},{1,0},{2,3},{3,2},{4,5},{5,4},{6,7},{7,6},{8,9},{9,8},{10,11... | collective-permute-start | bytes 589832 | tf_op jit(solution)/shard_map/ppermute | solution.py:39
  105.3 13.9 %collective-permute-start.29 = (bf16[2,2,64,384]{3,2,1,0:T(8,128)(2,1)S(1)}, bf16[2,2,64,384]{3,2,1,0:T(8,128)(2,1)S(1)}, u32[]{:S(2)}, u32[]{:S(2)}) collective-permute-start(bf16[2,2,64,384]{3,2,1,0:T(8,128)(2,1)S(1)} %get-tuple-element.105), channel_id=1, source_target_pairs={{0,4},{1,5},{2,6},{3,7},{4,0},{5,1},{6,2},{7,3},{8,12},{9,13},{10,... | collective-permute-start | bytes 589832 | tf_op jit(solution)/shard_map/ppermute | solution.py:39
  105.3 13.8 %collective-permute-start.28 = (bf16[2,2,64,384]{3,2,1,0:T(8,128)(2,1)S(1)}, bf16[2,2,64,384]{3,2,1,0:T(8,128)(2,1)S(1)}, u32[]{:S(2)}, u32[]{:S(2)}) collective-permute-start(bf16[2,2,64,384]{3,2,1,0:T(8,128)(2,1)S(1)} %get-tuple-element.104), channel_id=1, source_target_pairs={{0,2},{1,3},{2,4},{3,5},{4,6},{5,7},{6,0},{7,1},{8,10},{9,11},{10,... | collective-permute-start | bytes 589832 | tf_op jit(solution)/shard_map/ppermute | solution.py:39
  119.2 25.9 %collective-permute-start.31 = (bf16[4,128,768]{2,1,0:T(8,128)(2,1)}, bf16[4,128,768]{2,1,0:T(8,128)(2,1)S(1)}, u32[]{:S(2)}, u32[]{:S(2)}) collective-permute-start(bf16[4,128,768]{2,1,0:T(8,128)(2,1)} %get-tuple-element.110), channel_id=1, source_target_pairs={{0,1},{1,0},{2,3},{3,2},{4,5},{5,4},{6,7},{7,6},{8,9},{9,8},{10,11... | collective-permute-start | bytes 2359304 | tf_op jit(solution)/shard_map/ppermute | solution.py:39
  120.8 15.9 %collective-permute-start.30 = (bf16[2,256,384]{2,1,0:T(8,128)(2,1)}, bf16[2,256,384]{2,1,0:T(8,128)(2,1)S(1)}, u32[]{:S(2)}, u32[]{:S(2)}) collective-permute-start(bf16[2,256,384]{2,1,0:T(8,128)(2,1)} %get-tuple-element.127.refs_4_), channel_id=1, source_target_pairs={{0,2},{1,3},{2,4},{3,5},{4,6},{5,7},{6,0},{7,1},{8,10},{9,11},{10,... | collective-permute-start | bytes 1179656 | tf_op jit(solution)/shard_map/ppermute | solution.py:39
  123.2 13.3 %collective-permute-start.33 = (bf16[2,2,64,384]{3,2,1,0:T(8,128)(2,1)S(1)}, bf16[2,2,64,384]{3,2,1,0:T(8,128)(2,1)S(1)}, u32[]{:S(2)}, u32[]{:S(2)}) collective-permute-start(bf16[2,2,64,384]{3,2,1,0:T(8,128)(2,1)S(1)} %get-tuple-element.112), channel_id=1, source_target_pairs={{0,6},{1,7},{2,0},{3,1},{4,2},{5,3},{6,4},{7,5},{8,14},{9,15},{10,... | collective-permute-start | bytes 589832 | tf_op jit(solution)/shard_map/ppermute | solution.py:39
  124.7 20.4 %collective-permute-start.32 = (f32[256,2]{1,0:T(8,128)}, f32[256,2]{1,0:T(8,128)S(1)}, u32[]{:S(2)}, u32[]{:S(2)}) collective-permute-start(f32[256,2]{1,0:T(8,128)} %get-tuple-element.111), channel_id=1, source_target_pairs={{0,8},{8,0},{16,24},{24,16},{1,9},{9,1},{17,25},{25,17},{2,10},{10... | collective-permute-start | bytes 6152 | tf_op jit(solution)/shard_map/ppermute | solution.py:43
  136.7 15.4 %copy-start.2 = (bf16[4,2,2,64,384]{4,3,2,1,0:T(8,128)(2,1)}, bf16[4,2,2,64,384]{4,3,2,1,0:T(8,128)(2,1)S(1)}, u32[]{:S(2)}) copy-start(bf16[4,2,2,64,384]{4,3,2,1,0:T(8,128)(2,1)S(1)} %pad_maximum_fusion.1.refs_0_) | copy-start | bytes 2359300
  136.7 11.6 %copy-start.10 = (bf16[2,256,384]{2,1,0:T(8,128)(2,1)}, bf16[2,256,384]{2,1,0:T(8,128)(2,1)S(1)}, u32[]{:S(2)}) copy-start(bf16[2,256,384]{2,1,0:T(8,128)(2,1)S(1)} %collective-permute-done.30.refs_6_) | copy-start | bytes 1179652
  136.7 11.6 %copy-start.9 = (bf16[2,256,384]{2,1,0:T(8,128)(2,1)S(1)}, bf16[2,256,384]{2,1,0:T(8,128)(2,1)}, u32[]{:S(2)}) copy-start(bf16[2,256,384]{2,1,0:T(8,128)(2,1)} %get-tuple-element.127.refs_4_) | copy-start | bytes 1179652
  146.0 26.9 %collective-permute-start.40 = (bf16[2,256,1536]{2,1,0:T(8,128)(2,1)}, bf16[2,256,1536]{2,1,0:T(8,128)(2,1)S(1)}, u32[]{:S(2)}, u32[]{:S(2)}) collective-permute-start(bf16[2,256,1536]{2,1,0:T(8,128)(2,1)} %get-tuple-element.118), channel_id=1, source_target_pairs={{0,8},{8,0},{16,24},{24,16},{1,9},{9,1},{17,25},{25,17},{2,10},{10... | collective-permute-start | bytes 4718600 | tf_op jit(solution)/shard_map/ppermute | solution.py:43
  146.1 14.6 %copy-start.23 = (f32[256,2]{1,0:T(8,128)}, f32[256,2]{1,0:T(8,128)S(1)}, u32[]{:S(2)}) copy-start(f32[256,2]{1,0:T(8,128)S(1)} %add.75) | copy-start | bytes 6148
  146.1 6.0 %collective-permute-start.39 = (f32[256,2]{1,0:T(8,128)S(1)}, f32[256,2]{1,0:T(8,128)S(1)}, u32[]{:S(2)}, u32[]{:S(2)}) collective-permute-start(f32[256,2]{1,0:T(8,128)S(1)} %add.75), channel_id=1, source_target_pairs={{0,16},{8,24},{16,0},{24,8},{1,17},{9,25},{17,1},{25,9},{2,18},{10... | collective-permute-start | bytes 6152 | tf_op jit(solution)/shard_map/ppermute | solution.py:43
  147.6 13.0 %collective-permute-start.35 = (bf16[2,256,384]{2,1,0:T(8,128)(2,1)S(1)}, bf16[2,256,384]{2,1,0:T(8,128)(2,1)S(1)}, u32[]{:S(2)}, u32[]{:S(2)}) collective-permute-start(bf16[2,256,384]{2,1,0:T(8,128)(2,1)S(1)} %collective-permute-done.30.refs_6_), channel_id=1, source_target_pairs={{0,2},{1,3},{2,4},{3,5},{4,6},{5,7},{6,0},{7,1},{8,10},{9,11},{10,... | collective-permute-start | bytes 1179656 | tf_op jit(solution)/shard_map/ppermute | solution.py:39
  149.3 19.7 %collective-permute-start.34 = (bf16[4,256,384]{2,1,0:T(8,128)(2,1)}, bf16[4,256,384]{2,1,0:T(8,128)(2,1)}, u32[]{:S(2)}, u32[]{:S(2)}) collective-permute-start(bf16[4,256,384]{2,1,0:T(8,128)(2,1)} %bitcast.20), channel_id=1, source_target_pairs={{0,1},{1,0},{2,3},{3,2},{4,5},{5,4},{6,7},{7,6},{8,9},{9,8},{10,11... | collective-permute-start | bytes 2359304 | tf_op jit(solution)/shard_map/ppermute | solution.py:39
  149.6 19.4 %collective-permute-start.38 = (bf16[4,2,2,64,384]{4,3,2,1,0:T(8,128)(2,1)S(1)}, bf16[4,2,2,64,384]{4,3,2,1,0:T(8,128)(2,1)}, u32[]{:S(2)}, u32[]{:S(2)}) collective-permute-start(bf16[4,2,2,64,384]{4,3,2,1,0:T(8,128)(2,1)S(1)} %pad_maximum_fusion.1.refs_0_), channel_id=1, source_target_pairs={{0,8},{8,0},{16,24},{24,16},{1,9},{9,1},{17,25},{25,17},{2,10},{10... | collective-permute-start | bytes 2359304 | tf_op jit(solution)/shard_map/ppermute | solution.py:43
  152.1 19.3 %collective-permute-start.37 = (bf16[4,2,2,64,384]{4,3,2,1,0:T(8,128)(2,1)S(1)}, bf16[4,2,2,64,384]{4,3,2,1,0:T(8,128)(2,1)}, u32[]{:S(2)}, u32[]{:S(2)}) collective-permute-start(bf16[4,2,2,64,384]{4,3,2,1,0:T(8,128)(2,1)S(1)} %pad_maximum_fusion.1.refs_0_), channel_id=1, source_target_pairs={{0,16},{8,24},{16,0},{24,8},{1,17},{9,25},{17,1},{25,9},{2,18},{10... | collective-permute-start | bytes 2359304 | tf_op jit(solution)/shard_map/ppermute | solution.py:43
  160.7 18.4 %copy-start.11 = (bf16[2,256,384]{2,1,0:T(8,128)(2,1)}, bf16[2,256,384]{2,1,0:T(8,128)(2,1)S(1)}, u32[]{:S(2)}) copy-start(bf16[2,256,384]{2,1,0:T(8,128)(2,1)S(1)} %collective-permute-done.35.refs_7_) | copy-start | bytes 1179652
  160.7 12.3 %collective-permute-start.36 = (bf16[2,256,384]{2,1,0:T(8,128)(2,1)S(1)}, bf16[2,256,384]{2,1,0:T(8,128)(2,1)S(1)}, u32[]{:S(2)}, u32[]{:S(2)}) collective-permute-start(bf16[2,256,384]{2,1,0:T(8,128)(2,1)S(1)} %collective-permute-done.35.refs_7_), channel_id=1, source_target_pairs={{0,2},{1,3},{2,4},{3,5},{4,6},{5,7},{6,0},{7,1},{8,10},{9,11},{10,... | collective-permute-start | bytes 1179656 | tf_op jit(solution)/shard_map/ppermute | solution.py:39
  162.9 12.2 %copy-start.16 = (bf16[4,128,768]{2,1,0:T(8,128)(2,1)S(1)}, bf16[4,128,768]{2,1,0:T(8,128)(2,1)}, u32[]{:S(2)}) copy-start(bf16[4,128,768]{2,1,0:T(8,128)(2,1)} %get-tuple-element.134) | copy-start | bytes 2359300
  162.9 12.2 %copy-start.18 = (bf16[4,128,768]{2,1,0:T(8,128)(2,1)S(1)}, bf16[4,128,768]{2,1,0:T(8,128)(2,1)}, u32[]{:S(2)}) copy-start(bf16[4,128,768]{2,1,0:T(8,128)(2,1)} %copy-done.17) | copy-start | bytes 2359300
  174.5 20.2 %collective-permute-start.41 = (bf16[2,256,768]{2,1,0:T(8,128)(2,1)S(1)}, bf16[2,256,768]{2,1,0:T(8,128)(2,1)S(1)}, u32[]{:S(2)}, u32[]{:S(2)}) collective-permute-start(bf16[2,256,768]{2,1,0:T(8,128)(2,1)S(1)} %add_convert_fusion), channel_id=1, source_target_pairs={{0,16},{8,24},{16,0},{24,8},{1,17},{9,25},{17,1},{25,9},{2,18},{10... | collective-permute-start | bytes 2359304 | tf_op jit(solution)/shard_map/ppermute | solution.py:43
  175.2 9.8 %collective-permute-start.44 = (bf16[128,768]{1,0:T(8,128)(2,1)S(1)}, bf16[128,768]{1,0:T(8,128)(2,1)S(1)}, u32[]{:S(2)}, u32[]{:S(2)}) collective-permute-start(bf16[128,768]{1,0:T(8,128)(2,1)S(1)} %get-tuple-element.140), channel_id=1, source_target_pairs={{0,2},{1,3},{2,4},{3,5},{4,6},{5,7},{6,0},{7,1},{8,10},{9,11},{10,... | collective-permute-start | bytes 589832 | tf_op jit(solution)/shard_map/ppermute | solution.py:39
  175.4 9.7 %collective-permute-start.46 = (bf16[128,768]{1,0:T(8,128)(2,1)S(1)}, bf16[128,768]{1,0:T(8,128)(2,1)S(1)}, u32[]{:S(2)}, u32[]{:S(2)}) collective-permute-start(bf16[128,768]{1,0:T(8,128)(2,1)S(1)} %get-tuple-element.141), channel_id=1, source_target_pairs={{0,6},{1,7},{2,0},{3,1},{4,2},{5,3},{6,4},{7,5},{8,14},{9,15},{10,... | collective-permute-start | bytes 589832 | tf_op jit(solution)/shard_map/ppermute | solution.py:39
  179.1 14.7 %collective-permute-start.45 = (bf16[128,768]{1,0:T(8,128)(2,1)S(1)}, bf16[128,768]{1,0:T(8,128)(2,1)S(1)}, u32[]{:S(2)}, u32[]{:S(2)}) collective-permute-start(bf16[128,768]{1,0:T(8,128)(2,1)S(1)} %get-tuple-element.142), channel_id=1, source_target_pairs={{0,4},{1,5},{2,6},{3,7},{4,0},{5,1},{6,2},{7,3},{8,12},{9,13},{10,... | collective-permute-start | bytes 589832 | tf_op jit(solution)/shard_map/ppermute | solution.py:39
  179.1 15.5 %copy-start.22 = (bf16[2,256,768]{2,1,0:T(8,128)(2,1)S(1)}, bf16[2,256,768]{2,1,0:T(8,128)(2,1)}, u32[]{:S(2)}) copy-start(bf16[2,256,768]{2,1,0:T(8,128)(2,1)} %get-tuple-element.109) | copy-start | bytes 2359300
  179.2 18.0 %collective-permute-start.43 = (bf16[4,256,384]{2,1,0:T(8,128)(2,1)S(1)}, bf16[4,256,384]{2,1,0:T(8,128)(2,1)S(1)}, u32[]{:S(2)}, u32[]{:S(2)}) collective-permute-start(bf16[4,256,384]{2,1,0:T(8,128)(2,1)S(1)} %bitcast.61), channel_id=1, source_target_pairs={{0,1},{1,0},{2,3},{3,2},{4,5},{5,4},{6,7},{7,6},{8,9},{9,8},{10,11... | collective-permute-start | bytes 2359304 | tf_op jit(solution)/shard_map/ppermute | solution.py:39
  185.0 12.2 %collective-permute-start.42 = (bf16[4,2,2,64,384]{4,3,2,1,0:T(8,128)(2,1)}, bf16[4,2,2,64,384]{4,3,2,1,0:T(8,128)(2,1)S(1)}, u32[]{:S(2)}, u32[]{:S(2)}) collective-permute-start(bf16[4,2,2,64,384]{4,3,2,1,0:T(8,128)(2,1)} %collective-permute-done.37.refs_2_), channel_id=1, source_target_pairs={{0,8},{8,0},{16,24},{24,16},{1,9},{9,1},{17,25},{25,17},{2,10},{10... | collective-permute-start | bytes 2359304 | tf_op jit(solution)/shard_map/ppermute | solution.py:43
  (23 other events, 91.7 us)

commit v5 on v4

--- a/solution.py
+++ b/solution.py
@@ -11,7 +11,8 @@
 BF = jnp.bfloat16
 F32 = jnp.float32
 SLOTS = 3
-VMEM_BYTES = 60 * 1024 * 1024
+VMEM_BYTES = 20 * 1024 * 1024
+SPARE_BYTES = 8 * 1024 * 1024
 SMALL = pl.CostEstimate(flops=1, bytes_accessed=1, transcendentals=0)
 
 
@@ -301,13 +302,15 @@
 def call(body, out_shape, operands, scalars, scratch=()):
     specs = [pl.BlockSpec(memory_space=pltpu.SMEM)] * scalars
     specs += [pl.BlockSpec(memory_space=pltpu.VMEM)] * (len(operands) - scalars)
+    held = (*operands[scalars:], *jax.tree.leaves(out_shape), *scratch)
+    held_bytes = sum(math.prod(a.shape) * jnp.dtype(a.dtype).itemsize for a in held)
     return pl.pallas_call(
         body,
         out_shape=out_shape,
         in_specs=specs,
         out_specs=jax.tree.map(lambda _: pl.BlockSpec(memory_space=pltpu.VMEM), out_shape),
         scratch_shapes=list(scratch),
-        compiler_params=pltpu.CompilerParams(vmem_limit_bytes=VMEM_BYTES),
+        compiler_params=pltpu.CompilerParams(vmem_limit_bytes=held_bytes + SPARE_BYTES),
         cost_estimate=SMALL,
     )(*operands)
 
@@ -666,30 +669,32 @@
     return call(body, out, (place, attended, d_queries, *arrays), 1)
 
 
-def weight_grads(tiles, both_blocks, pairs):
+def weight_grads(tiles, both_blocks, known, pairs):
     part = tiles[0].shape[-1]
-    arrays, blocks = pieces_of(both_blocks)
+    given = [k for k, block in enumerate(both_blocks) if block is not None]
+    arrays, blocks = pieces_of([both_blocks[k] for k in given])
     width = arrays[0].shape[-1]
+    known = known or []
 
     def body(*refs):
-        tile_refs, block_refs, (query_ref, out_ref) = refs[:4], refs[4:-2], refs[-2:]
-        query_grad = jnp.zeros((part, width), F32)
-        out_grad = jnp.zeros((width, part), F32)
-        for far in range(pairs):
-            for side in range(2):
-                ((number, at),) = blocks[2 * far + side]
-                block = block_refs[number]
-                normed, grad = (
-                    jnp.concatenate([r[far, side, which] for r in tile_refs], axis=0)
-                    for which in range(2)
-                )
-                out_grad += contract_first(block[at], grad)
-                query_grad += contract_first(normed, block[at + 1])
+        tile_refs, known_refs = refs[:4], refs[4 : 4 + len(known)]
+        block_refs, (query_ref, out_ref) = refs[4 + len(known) : -2], refs[-2:]
+        query_grad = known_refs[0][...] if known else jnp.zeros((part, width), F32)
+        out_grad = known_refs[1][...] if known else jnp.zeros((width, part), F32)
+        for k, ((number, at),) in zip(given, blocks):
+            side, far = divmod(k, pairs)
+            block = block_refs[number]
+            normed, grad = (
+                jnp.concatenate([r[far, side, which] for r in tile_refs], axis=0)
+                for which in range(2)
+            )
+            out_grad += contract_first(block[at], grad)
+            query_grad += contract_first(normed, block[at + 1])
         query_ref[...] = query_grad
         out_ref[...] = out_grad
 
     out = [shaped((part, width), F32), shaped((width, part), F32)]
-    return call(body, out, (*tiles, *arrays), 0)
+    return call(body, out, (*tiles, *known, *arrays), 0)
 
 
 def local(
@@ -738,7 +743,10 @@
     normed, mean, inverse, own_tiles, other_tiles = prepare_video(
         after(video_states, sent), out_grad, place, pairs, part
     )
-    pieces = encode_rows(states, kept, got, over_x, final_gain, place, pairs)
+    other_tiles = fsend(other_tiles, 0, 1)
+    pieces = encode_rows(
+        states, kept, got, after(over_x, normed), final_gain, place, pairs
+    )
 
     mine = jnp.stack([fsend(p, far, 0) if far else p for far, p in enumerate(pieces)])
     mine = after(mine, ring[2])
@@ -748,7 +756,7 @@
     for far in range(3, pairs):
         current = fsend(current, 1, 0)
         ring.append(current)
-    parts[3] = after(parts[3], side_first)
+    parts[3] = after(parts[3], side_first, other_tiles)
     kv_partial = project_captions(
         parts, cross_key, cross_value, side_key, side_value, place, pairs
     )
@@ -757,10 +765,8 @@
     for far in range(1, pairs):
         kv_sum += fsend(kv_partial[far], pairs - far, 0).astype(F32)
     side_later = [fsend(w, 0, 1) for w in ring[2:]]
-    other_tiles = fsend(other_tiles, 0, 1)
-    kv_sum = after(kv_sum.astype(BF), side_later[0])
+    kv_sum = after(kv_sum.astype(BF), side_later)
     kv_blocks = gather_direct(kv_sum)
-    kv_blocks[4] = after(kv_blocks[4], side_later, other_tiles)
 
     step = part + width_local
     blocks = []
@@ -787,37 +793,52 @@
         caption_lens,
         pairs,
     )
-    kv_away, both, row_sums = after((kv_away, both, row_sums), over_z[1:-1])
+    kv_away, both, row_sums, over_z = after((kv_away, both, row_sums, over_z))
+    tiles = jnp.stack(over_z)
+
+    def chain(blocks, steps):
+        for _ in range(steps):
+            blocks.append(fsend(blocks[-1], 1, 0))
+        return blocks
+
+    def joined(two):
+        return jnp.stack(two).reshape(-1, tokens, width_local)
 
     kv_side = fsend(kv_away, 0, 1)
-    late = [both, fsend(both, 1, 0)]
+    late = chain([both], pairs // 2)
     sums_core = gsend(row_sums, 1)
-    tiles = jnp.stack(over_z)
-    attended = after(attended, late[1])
-    own, far_piece, away = project_back(attended, d_queries, blocks, place, pairs, part)
-    kv_side, late, sums_core, tiles, away = after((kv_side, late, sums_core, tiles, away))
-
-    sides = [fsend(jnp.stack(late[:2]).reshape(4, tokens, width_local), 0, 1)]
-    late = list(late)
-    for far in range(2, pairs):
-        late.append(fsend(late[-1], 1, 0))
+    attended, tiles = after((attended, tiles), sums_core)
     tiles_x = gsend(tiles, 2)
     tiles_core = gsend(tiles, 1)
+    own, far_piece, away = project_back(attended, d_queries, blocks, place, pairs, part)
+    stage = (kv_side, late, sums_core, tiles_x, tiles_core, joined(late[:2]), away)
+    kv_side, late, sums_core, tiles_x, tiles_core, first_two, away = after(stage)
+
+    sides = [fsend(first_two, 0, 1)]
+    late = chain(list(late), pairs - 1 - pairs // 2)
     row_sums = row_sums + sums_core
     sums_x = gsend(row_sums, 2)
     got = gsend(away, 1)
-    done = after((sides[0], late, tiles_x, tiles_core, sums_x, got, kv_side))
-    sides[0], late, tiles_x, tiles_core, sums_x, got, kv_side = done
-
-    for far in range(2, pairs, 2):
-        stacked = jnp.stack(late[far : far + 2])
-        sides.append(fsend(stacked.reshape(-1, tokens, width_local), 0, 1))
-    both_blocks = []
-    for far in range(pairs):
-        both_blocks += [((late[far], 0),), ((sides[far // 2], far % 2 * 2),)]
     width = model_width // 4
     sent = (far_piece.astype(F32) + got[:, :, width:].astype(F32)).astype(BF)
     far_sum = gsend(sent, 2)
+    tiles = [tiles, tiles_core, tiles_x, gsend(tiles_x, 1)]
+
+    def kv_term(far):
+        return kv_own[far].astype(F32) + kv_side[far].astype(F32)
+
+    kv_grads = kv_term(0)
+    for far in range(1, pairs, 2):
+        kv_grads += fsend(kv_term(far).astype(BF), far, 0).astype(F32)
+    kv_rest = [kv_term(far).astype(BF) for far in range(2, pairs, 2)]
+    others = [joined(late[far : far + 2]) for far in range(2, pairs, 2)]
+    stage = (sides[0], late, sums_x, sent, tiles, kv_grads, kv_rest, others)
+    sides[0], late, sums_x, _, tiles, kv_grads, kv_rest, others = after(stage)
+
+    sides += [fsend(two, 0, 1) for two in others]
+    here = [((block, 0),) for block in late]
+    there = [((sides[far // 2], far % 2 * 2),) for far in range(pairs)]
+    known = weight_grads(tiles, here + there[:2], None, pairs)
     total = own.astype(F32) + got[:, :, :width].astype(F32) + far_sum.astype(F32)
     row_sums = (row_sums + sums_x) / model_width
     video = quarter(video_states, g, 1).astype(F32)
@@ -827,19 +848,12 @@
         quarter(out_grad, g, 1).astype(F32)
         + inverse * (total[1] - row_sums[:, 0:1] - video_hat * row_sums[:, 1:2])
     ).astype(BF)
-
-    def kv_term(far):
-        return kv_own[far].astype(F32) + kv_side[far].astype(F32)
-
-    kv_grads = kv_term(0)
-    for far in range(1, pairs):
-        kv_grads += fsend(kv_term(far).astype(BF), far, 0).astype(F32)
+    for far in range(2, pairs, 2):
+        kv_grads += fsend(kv_rest[far // 2 - 1], far, 0).astype(F32)
     kv_grads = kv_grads.astype(BF)[None]
     key_grad = kv_grads[:, :, :width_local]
     value_grad = kv_grads[:, :, width_local:]
-
-    tiles = [tiles, tiles_core, tiles_x, gsend(tiles_x, 1)]
-    query_grad, out_weight_grad = weight_grads(tiles, both_blocks, pairs)
+    query_grad, out_weight_grad = weight_grads(tiles, [None] * (pairs + 2) + there[2:], known, pairs)
     return (updated, input_grad, query_grad, out_weight_grad, key_grad, value_grad)
 
 

time: 205 us -> 212 us (1.034)
  Pallas kernels: 53 us -> 31 us
  waiting for transfers between devices: 82.7 us -> 103 us
  local copies, waits for them, and re-layouts: 6.18 us -> 12.4 us
    ppermute x35, waiting for transfers between devices: 64.5 us -> 88 us  [fsend(): return lax.ppermute(block, 'fsdp', perm)]
    pallas_call x7 -> x8, Pallas kernels: 37.9 us -> 23.6 us  [call(): pl.pallas_call(body, out_shape=out_shape, in_specs=specs, out_specs=jax.t...]
    unnamed x81 -> x63, local copies, waits for them, and re-layouts: 5.24 us -> 11.5 us
    pallas_call x1, Pallas kernels: 7.96 us -> 2.95 us  [project_text(): pl.pallas_call(body, grid=(steps,), out_shape=shaped((rows, 3 * width)),...]
    ppermute x12, waiting for transfers between devices: 18.2 us -> 14.7 us  [gsend(): lax.ppermute(block, 'grp', [(s, s ^ flip) for s in range(lax.axis_size('g...]
    pallas_call x1, Pallas kernels: 7.16 us -> 4.43 us  [attend_text(): pl.pallas_call(body, grid=(steps,), out_shape=[shaped((rows // 2, depth))...]
    ppermute x35, starting transfers between devices: 41.7 us -> 43.8 us  [fsend(): return lax.ppermute(block, 'fsdp', perm)]
  transfers between devices with their start and end apart: 47 -> 47, of which waited for: 19 -> 18; matrix products, arithmetic and copies ran while one was open for 6% -> 7% of each run, Pallas kernels for 23% -> 13%
where the time goes in v5:
time: 212 us; the launch traced here: 211 us
  waiting for transfers between devices  103 us (49%)
  starting transfers between devices  50.4 us (24%)
  Pallas kernels  31 us (15%)
  other arithmetic  13.2 us (6%)
  local copies, waits for them, and re-layouts  12.4 us (6%)
    ppermute x35, waiting for transfers between devices, fsend(): return lax.ppermute(block, 'fsdp', perm)  88 us
    ppermute x35, starting transfers between devices, fsend(): return lax.ppermute(block, 'fsdp', perm)  43.8 us
    pallas_call x8, Pallas kernels, call(): pl.pallas_call(body, out_shape=out_shape, in_specs=specs, out_specs=jax.t...  23.6 us
    ppermute x12, waiting for transfers between devices, gsend(): lax.ppermute(block, 'grp', [(s, s ^ flip) for s in range(lax.axis_size('g...  14.7 us
    unnamed x63, local copies, waits for them, and re-layouts  11.5 us
    ppermute x12, starting transfers between devices, gsend(): lax.ppermute(block, 'grp', [(s, s ^ flip) for s in range(lax.axis_size('g...  6.53 us
    pallas_call x1, Pallas kernels, attend_text(): pl.pallas_call(body, grid=(steps,), out_shape=[shaped((rows // 2, depth))...  4.43 us
  transfers between devices with their start and end apart: 47, of which 18 were waited for; matrix products, arithmetic and copies ran while one was open for 7% of the time, Pallas kernels for 13%

profile of v5, /device:TPU:0, one launch (start us, length us, event | category | flops | bytes accessed | tf_op | source)
XLA Modules:
  0.0 210.9 jit_solution(7220299331487373116)
XLA Ops:
  0.6 3.0 %collective-permute-start.2 = (bf16[512,384]{1,0:T(8,128)(2,1)}, bf16[512,384]{1,0:T(8,128)(2,1)S(1)}, u32[]{:S(2)}, u32[]{:S(2)}) collective-permute-start(bf16[512,384]{1,0:T(8,128)(2,1)} %refs_4_.1), channel_id=1, source_target_pairs={{0,1},{1,0},{2,3},{3,2},{4,5},{5,4},{6,7},{7,6},{8,9},{9,8},{10,11... | collective-permute-start | bytes 1179656 | tf_op jit(solution)/shard_map/ppermute | solution.py:40
  3.7 2.0 collective-permute-start
  5.8 1.6 collective-permute-start.1
  7.3 2.2 %copy-done.2 = bf16[4096,512]{1,0:T(8,128)(2,1)S(1)} copy-done((bf16[4096,512]{1,0:T(8,128)(2,1)S(1)}, bf16[4096,512]{1,0:T(8,128)(2,1)}, u32[]{:S(2)}) %copy-start.2) | copy-done | bytes 4194328
  9.5 2.2 %copy-done.3 = bf16[4096,512]{1,0:T(8,128)(2,1)S(1)} copy-done((bf16[4096,512]{1,0:T(8,128)(2,1)S(1)}, bf16[4096,512]{1,0:T(8,128)(2,1)}, u32[]{:S(2)}) %copy-start.3) | copy-done | bytes 4194328
  11.7 2.2 %copy-done.4 = bf16[4096,512]{1,0:T(8,128)(2,1)S(1)} copy-done((bf16[4096,512]{1,0:T(8,128)(2,1)S(1)}, bf16[4096,512]{1,0:T(8,128)(2,1)}, u32[]{:S(2)}) %copy-start.4) | copy-done | bytes 4194328
  13.9 1.2 copy-done.5
  15.8 3.0 %shard_map.208.qkv_ref = bf16[128,1536]{1,0:T(8,128)(2,1)S(1)} custom-call(bf16[128,4096]{1,0:T(8,128)(2,1)S(1)} %bitcast.52, f32[1,4096]{1,0:T(1,128)S(1)} %bitcast.58, bf16[4096,512]{1,0:T(8,128)(2,1)S(1)} %copy-done.2, bf16[4096,512]{1,0:T(8,128)(2,1)S(1)} %copy-done.3, bf16[4096,512]{1,0:T(8,128)(2,1)S(1)} %copy-done.4), custom_call_target="tpu_custom_call" | custom-call | flops 1 | bytes 1 | tf_op jit(solution)/shard_map/pallas_call | solution.py:350
  18.9 2.2 %copy-done.1 = bf16[512,4096]{1,0:T(8,128)(2,1)S(1)} copy-done((bf16[512,4096]{1,0:T(8,128)(2,1)S(1)}, bf16[512,4096]{1,0:T(8,128)(2,1)}, u32[]{:S(2)}) %copy-start.1) | copy-done | bytes 4194328
  21.1 4.4 %shard_map.209 = (bf16[64,4096]{1,0:T(8,128)(2,1)S(1)}, bf16[64,4096]{1,0:T(8,128)(2,1)S(1)}) custom-call(s32[3]{0:T(128)S(1)} %pad_add_fusion.place_ref, s32[8]{0:T(128)S(1)} %copy-done.25, bf16[128,1536]{1,0:T(8,128)(2,1)S(1)} %shard_map.208.qkv_ref, f32[8,128,128]{2,1,0:T(8,128)S(1)} %copy-done.17, bf16[512,4096]{1,0:T(8,128)(2,1)S(1)} %copy-done.1), custom_call_target="tpu_custom_call" | custom-call | flops 1 | bytes 1 | tf_op jit(solution)/shard_map/pallas_call | solution.py:394
  25.8 1.6 collective-permute-start.9
  27.6 1.6 collective-permute-start.5
  29.4 1.6 collective-permute-start.13
  30.9 2.7 %shard_map.210 = (bf16[256,3072]{1,0:T(8,128)(2,1)S(1)}, f32[256,1]{1,0:T(8,128)S(1)}, f32[256,1]{1,0:T(8,128)S(1)}, bf16[4,2,64,384]{3,2,1,0:T(8,128)(2,1)S(1)}, bf16[4,2,64,384]{3,2,1,0:T(8,128)(2,1)S(1)}) custom-call(s32[3]{0:T(128)S(1)} %pad_add_fusion.place_ref, bf16[256,3072]{1,0:T(8,128)(2,1)S(1)} %copy-done.9, bf16[256,3072]{1,0:T(8,128)(2,1)S(1)} %copy-done), custom_call_target="tpu_custom_call" | custom-call | flops 1 | bytes 1 | tf_op jit(solution)/shard_map/pallas_call | solution.py:307
  34.3 1.7 collective-permute-done.5.far_ref
  36.9 1.6 collective-permute-start.6
  38.5 1.2 collective-permute-start.7
  39.8 1.3 collective-permute-start.8
  41.0 4.3 %collective-permute-done.6 = bf16[32,1024]{1,0:T(8,128)(2,1)S(1)} collective-permute-done((bf16[32,1024]{1,0:T(8,128)(2,1)S(1)}, bf16[32,1024]{1,0:T(8,128)(2,1)S(1)}, u32[]{:S(2)}, u32[]{:S(2)}) %collective-permute-start.6) | collective-permute-done | bytes 65568 | tf_op jit(solution)/shard_map/ppermute | solution.py:40
  45.3 2.4 %collective-permute-done.7 = bf16[32,1024]{1,0:T(8,128)(2,1)S(1)} collective-permute-done((bf16[32,1024]{1,0:T(8,128)(2,1)S(1)}, bf16[32,1024]{1,0:T(8,128)(2,1)S(1)}, u32[]{:S(2)}, u32[]{:S(2)}) %collective-permute-start.7) | collective-permute-done | bytes 65568 | tf_op jit(solution)/shard_map/ppermute | solution.py:40
  47.8 1.9 collective-permute-start.15
  49.7 1.5 collective-permute-start.14
  51.2 1.5 collective-permute-start.11
  52.7 6.2 %collective-permute-done.11.refs_2_ = bf16[4,32,1024]{2,1,0:T(8,128)(2,1)S(1)} collective-permute-done((bf16[4,32,1024]{2,1,0:T(8,128)(2,1)S(1)}, bf16[4,32,1024]{2,1,0:T(8,128)(2,1)S(1)}, u32[]{:S(2)}, u32[]{:S(2)}) %collective-permute-start.11) | collective-permute-done | bytes 262176 | tf_op jit(solution)/shard_map/ppermute | solution.py:44
  59.4 6.2 %collective-permute-done.14 = bf16[4,2,64,384]{3,2,1,0:T(8,128)(2,1)S(1)} collective-permute-done((bf16[4,2,64,384]{3,2,1,0:T(8,128)(2,1)S(1)}, bf16[4,2,64,384]{3,2,1,0:T(8,128)(2,1)S(1)}, u32[]{:S(2)}, u32[]{:S(2)}) %collective-permute-start.14) | collective-permute-done | bytes 393248 | tf_op jit(solution)/shard_map/ppermute | solution.py:40
  65.6 1.5 collective-permute-start.19
  67.6 1.8 shard_map.212
  69.4 2.3 %collective-permute-start.16 = (bf16[128,768]{1,0:T(8,128)(2,1)S(1)}, bf16[128,768]{1,0:T(8,128)(2,1)S(1)}, u32[]{:S(2)}, u32[]{:S(2)}) collective-permute-start(bf16[128,768]{1,0:T(8,128)(2,1)S(1)} %get-tuple-element.104), channel_id=1, source_target_pairs={{0,6},{1,7},{2,0},{3,1},{4,2},{5,3},{6,4},{7,5},{8,14},{9,15},{10,... | collective-permute-start | bytes 589832 | tf_op jit(solution)/shard_map/ppermute | solution.py:40
  72.8 4.4 %collective-permute-done.16 = bf16[128,768]{1,0:T(8,128)(2,1)S(1)} collective-permute-done((bf16[128,768]{1,0:T(8,128)(2,1)S(1)}, bf16[128,768]{1,0:T(8,128)(2,1)S(1)}, u32[]{:S(2)}, u32[]{:S(2)}) %collective-permute-start.16) | collective-permute-done | bytes 196640 | tf_op jit(solution)/shard_map/ppermute | solution.py:40
  77.1 11.2 %collective-permute-done.17 = bf16[128,768]{1,0:T(8,128)(2,1)S(1)} collective-permute-done((bf16[128,768]{1,0:T(8,128)(2,1)S(1)}, bf16[128,768]{1,0:T(8,128)(2,1)S(1)}, u32[]{:S(2)}, u32[]{:S(2)}) %collective-permute-start.17) | collective-permute-done | bytes 196640 | tf_op jit(solution)/shard_map/ppermute | solution.py:40
  88.5 3.9 %collective-permute-done.20.refs_7_ = bf16[768,384]{1,0:T(8,128)(2,1)S(1)} collective-permute-done((bf16[768,384]{1,0:T(8,128)(2,1)S(1)}, bf16[768,384]{1,0:T(8,128)(2,1)S(1)}, u32[]{:S(2)}, u32[]{:S(2)}) %collective-permute-start.20) | collective-permute-done | bytes 589856 | tf_op jit(solution)/shard_map/ppermute | solution.py:40
  92.4 2.2 %collective-permute-start.26 = (bf16[128,768]{1,0:T(8,128)(2,1)S(1)}, bf16[128,768]{1,0:T(8,128)(2,1)S(1)}, u32[]{:S(2)}, u32[]{:S(2)}) collective-permute-start(bf16[128,768]{1,0:T(8,128)(2,1)S(1)} %add_convert_fusion.6.refs_0_), channel_id=1, source_target_pairs={{0,6},{1,7},{2,0},{3,1},{4,2},{5,3},{6,4},{7,5},{8,14},{9,15},{10,... | collective-permute-start | bytes 589832 | tf_op jit(solution)/shard_map/ppermute | solution.py:40
  95.7 1.5 collective-permute-start.22
  97.2 2.8 %collective-permute-done.26.refs_6_ = bf16[128,768]{1,0:T(8,128)(2,1)S(1)} collective-permute-done((bf16[128,768]{1,0:T(8,128)(2,1)S(1)}, bf16[128,768]{1,0:T(8,128)(2,1)S(1)}, u32[]{:S(2)}, u32[]{:S(2)}) %collective-permute-start.26) | collective-permute-done | bytes 196640 | tf_op jit(solution)/shard_map/ppermute | solution.py:40
  100.1 1.5 collective-permute-start.27
  101.7 9.3 %collective-permute-done.21.refs_4_ = bf16[128,768]{1,0:T(8,128)(2,1)S(1)} collective-permute-done((bf16[128,768]{1,0:T(8,128)(2,1)S(1)}, bf16[128,768]{1,0:T(8,128)(2,1)S(1)}, u32[]{:S(2)}, u32[]{:S(2)}) %collective-permute-start.21) | collective-permute-done | bytes 196640 | tf_op jit(solution)/shard_map/ppermute | solution.py:40
  111.0 1.5 collective-permute-start.25
  113.0 1.0 collective-permute-start.29
  114.1 2.9 %collective-permute-start.30 = (bf16[2,2,64,384]{3,2,1,0:T(8,128)(2,1)S(1)}, bf16[2,2,64,384]{3,2,1,0:T(8,128)(2,1)S(1)}, u32[]{:S(2)}, u32[]{:S(2)}) collective-permute-start(bf16[2,2,64,384]{3,2,1,0:T(8,128)(2,1)S(1)} %get-tuple-element.119), channel_id=1, source_target_pairs={{0,6},{1,7},{2,0},{3,1},{4,2},{5,3},{6,4},{7,5},{8,14},{9,15},{10,... | collective-permute-start | bytes 589832 | tf_op jit(solution)/shard_map/ppermute | solution.py:40
  116.9 2.8 %shard_map.213 = (bf16[256,384]{1,0:T(8,128)(2,1)S(1)}, bf16[256,384]{1,0:T(8,128)(2,1)S(1)}, f32[1,384]{1,0:T(1,128)S(1)}) custom-call(s32[3]{0:T(128)S(1)} %pad_add_fusion.place_ref, bf16[256,3072]{1,0:T(8,128)(2,1)S(1)} %get-tuple-element.89.normed_ref, bf16[256,3072]{1,0:T(8,128)(2,1)S(1)} %copy-done, bf16[384,384]{1,0:T(8,128)(2,1)S(1)} %copy-done.7, ...), custom_call_target="tpu_custom_call" | custom-call | flops 1 | bytes 1 | tf_op jit(solution)/shard_map/pallas_call | solution.py:307
  120.1 3.8 %shard_map.214 = (bf16[2,256,384]{2,1,0:T(8,128)(2,1)S(1)}, bf16[256,384]{1,0:T(8,128)(2,1)S(1)}, bf16[256,384]{1,0:T(8,128)(2,1)S(1)}, f32[256,2]{1,0:T(8,128)S...) custom-call(s32[3]{0:T(128)S(1)} %pad_add_fusion.place_ref, s32[8]{0:T(128)S(1)} %copy-done.26, ...), custom_call_target="tpu_custom_call" | custom-call | flops 1 | bytes 1 | tf_op jit(solution)/shard_map/pallas_call | solution.py:307
  123.9 3.9 %collective-permute-done.29 = bf16[2,2,64,384]{3,2,1,0:T(8,128)(2,1)S(1)} collective-permute-done((bf16[2,2,64,384]{3,2,1,0:T(8,128)(2,1)S(1)}, bf16[2,2,64,384]{3,2,1,0:T(8,128)(2,1)S(1)}, u32[]{:S(2)}, u32[]{:S(2)}) %collective-permute-start.29) | collective-permute-done | bytes 196640 | tf_op jit(solution)/shard_map/ppermute | solution.py:40
  127.9 3.8 %collective-permute-start.33 = (bf16[2,256,384]{2,1,0:T(8,128)(2,1)S(1)}, bf16[2,256,384]{2,1,0:T(8,128)(2,1)S(1)}, u32[]{:S(2)}, u32[]{:S(2)}) collective-permute-start(bf16[2,256,384]{2,1,0:T(8,128)(2,1)S(1)} %get-tuple-element.150.refs_4_), channel_id=1, source_target_pairs={{0,2},{1,3},{2,4},{3,5},{4,6},{5,7},{6,0},{7,1},{8,10},{9,11},{10,... | collective-permute-start | bytes 1179656 | tf_op jit(solution)/shard_map/ppermute | solution.py:40
  131.7 1.5 collective-permute-start.32
  134.0 9.1 %collective-permute-done.33.refs_5_ = bf16[2,256,384]{2,1,0:T(8,128)(2,1)S(1)} collective-permute-done((bf16[2,256,384]{2,1,0:T(8,128)(2,1)S(1)}, bf16[2,256,384]{2,1,0:T(8,128)(2,1)S(1)}, u32[]{:S(2)}, u32[]{:S(2)}) %collective-permute-start.33) | collective-permute-done | bytes 393248 | tf_op jit(solution)/shard_map/ppermute | solution.py:40
  143.2 5.5 %shard_map.215 = (bf16[2,256,768]{2,1,0:T(8,128)(2,1)S(1)}, bf16[2,256,768]{2,1,0:T(8,128)(2,1)S(1)}, bf16[2,256,1536]{2,1,0:T(8,128)(2,1)}) custom-call(s32[3]{0:T(128)S(1)} %pad_add_fusion.place_ref, bf16[256,384]{1,0:T(8,128)(2,1)S(1)} %get-tuple-element.125.att_ref, bf16[256,384]{1,0:T(8,128)(2,1)S(1)} %get-tuple-element.126.dq_ref, ...), custom_call_target="tpu_custom_call" | custom-call | flops 1 | bytes 1 | tf_op jit(solution)/shard_map/pallas_call | solution.py:307
  148.8 1.1 pad_maximum_fusion.2
  149.9 6.0 %collective-permute-done.34.refs_6_ = bf16[2,256,384]{2,1,0:T(8,128)(2,1)} collective-permute-done((bf16[2,256,384]{2,1,0:T(8,128)(2,1)S(1)}, bf16[2,256,384]{2,1,0:T(8,128)(2,1)}, u32[]{:S(2)}, u32[]{:S(2)}) %collective-permute-start.34) | collective-permute-done | bytes 393248 | tf_op jit(solution)/shard_map/ppermute | solution.py:40
  156.0 0.9 fusion.11
  157.0 2.0 collective-permute-start.43
  159.6 17.5 %collective-permute-done.44 = bf16[128,768]{1,0:T(8,128)(2,1)} collective-permute-done((bf16[128,768]{1,0:T(8,128)(2,1)S(1)}, bf16[128,768]{1,0:T(8,128)(2,1)}, u32[]{:S(2)}, u32[]{:S(2)}) %collective-permute-start.44) | collective-permute-done | bytes 196640 | tf_op jit(solution)/shard_map/ppermute | solution.py:40
  177.0 1.0 reduce
  178.0 1.0 reduce.2
  179.1 1.1 add.79
  180.7 1.3 fusion.8
  182.1 1.2 pad_maximum_fusion.3
  183.3 1.4 add_convert_fusion
  184.7 1.5 collective-permute-start.38
  186.9 3.3 %shard_map.216 = (f32[384,384]{1,0:T(8,128)S(1)}, f32[384,384]{1,0:T(8,128)S(1)}) custom-call(bf16[4,2,2,64,384]{4,3,2,1,0:T(8,128)(2,1)S(1)} %pad_maximum_fusion.1.refs_0_, bf16[4,2,2,64,384]{4,3,2,1,0:T(8,128)(2,1)S(1)} %collective-permute-done.36.refs_1_, bf16[4,2,2,64,384]{4,3,2,1,0:T(8,128)(2,1)} %collective-permute-done.35.refs_2_, ...), custom_call_target="tpu_custom_call" | custom-call | flops 1 | bytes 1 | tf_op jit(solution)/shard_map/pallas_call | solution.py:307
  190.4 6.7 %collective-permute-done.46 = bf16[128,768]{1,0:T(8,128)(2,1)S(1)} collective-permute-done((bf16[128,768]{1,0:T(8,128)(2,1)S(1)}, bf16[128,768]{1,0:T(8,128)(2,1)S(1)}, u32[]{:S(2)}, u32[]{:S(2)}) %collective-permute-start.46) | collective-permute-done | bytes 196640 | tf_op jit(solution)/shard_map/ppermute | solution.py:40
  197.8 6.6 %collective-permute-done.38 = bf16[2,256,768]{2,1,0:T(8,128)(2,1)S(1)} collective-permute-done((bf16[2,256,768]{2,1,0:T(8,128)(2,1)S(1)}, bf16[2,256,768]{2,1,0:T(8,128)(2,1)S(1)}, u32[]{:S(2)}, u32[]{:S(2)}) %collective-permute-start.38) | collective-permute-done | bytes 786464 | tf_op jit(solution)/shard_map/ppermute | solution.py:44
  204.4 1.4 convert_add_fusion
  205.8 2.2 %fusion.6 = (bf16[256,768]{1,0:T(8,128)(2,1)}, bf16[256,768]{1,0:T(8,128)(2,1)}) fusion(f32[2,256,768]{2,1,0:T(8,128)S(1)} %convert_add_fusion, f32[256]{0:T(256)S(1)} %get-tuple-element.163, f32[256]{0:T(256)S(1)} %reduce.2, f32[256]{0:T(256)S(1)} %get-tuple-element.162, f32[256]{0:T(256)S(1)} %reduce, bf16[256,3072]{1,0:T(8,128)(2,1)S(1)} %copy-done, ...), kind=kLoop, calls=%fused_computation.17 | loop fusion | flops 2359296 | bytes 3149828 | tf_op jit(solution)/shard_map/convert_element_type | solution.py:850
  208.0 2.9 %shard_map.217 = (f32[384,384]{1,0:T(8,128)}, f32[384,384]{1,0:T(8,128)}) custom-call(bf16[4,2,2,64,384]{4,3,2,1,0:T(8,128)(2,1)S(1)} %pad_maximum_fusion.1.refs_0_, bf16[4,2,2,64,384]{4,3,2,1,0:T(8,128)(2,1)S(1)} %collective-permute-done.36.refs_1_, bf16[4,2,2,64,384]{4,3,2,1,0:T(8,128)(2,1)} %collective-permute-done.35.refs_2_, ...), custom_call_target="tpu_custom_call" | custom-call | flops 1 | bytes 1 | tf_op jit(solution)/shard_map/pallas_call | solution.py:307
  (125 shorter events, 11.1 us)
Async XLA Ops:
  0.6 24.9 %collective-permute-start.2 = (bf16[512,384]{1,0:T(8,128)(2,1)}, bf16[512,384]{1,0:T(8,128)(2,1)S(1)}, u32[]{:S(2)}, u32[]{:S(2)}) collective-permute-start(bf16[512,384]{1,0:T(8,128)(2,1)} %refs_4_.1), channel_id=1, source_target_pairs={{0,1},{1,0},{2,3},{3,2},{4,5},{5,4},{6,7},{7,6},{8,9},{9,8},{10,11... | collective-permute-start | bytes 1179656 | tf_op jit(solution)/shard_map/ppermute | solution.py:40
  3.7 21.9 %collective-permute-start.3 = (bf16[512,384]{1,0:T(8,128)(2,1)}, bf16[512,384]{1,0:T(8,128)(2,1)S(1)}, u32[]{:S(2)}, u32[]{:S(2)}) collective-permute-start(bf16[512,384]{1,0:T(8,128)(2,1)} %refs_5_.1), channel_id=1, source_target_pairs={{0,1},{1,0},{2,3},{3,2},{4,5},{5,4},{6,7},{7,6},{8,9},{9,8},{10,11... | collective-permute-start | bytes 1179656 | tf_op jit(solution)/shard_map/ppermute | solution.py:40
  3.7 21.8 %collective-permute-start = (bf16[384,384]{1,0:T(8,128)(2,1)}, bf16[384,384]{1,0:T(8,128)(2,1)S(1)}, u32[]{:S(2)}, u32[]{:S(2)}) collective-permute-start(bf16[384,384]{1,0:T(8,128)(2,1)} %refs_0_.3), channel_id=1, source_target_pairs={{0,2},{1,3},{2,4},{3,5},{4,6},{5,7},{6,0},{7,1},{8,10},{9,11},{10,... | collective-permute-start | bytes 884744 | tf_op jit(solution)/shard_map/ppermute | solution.py:40
  5.8 19.8 %collective-permute-start.1 = (bf16[384,384]{1,0:T(8,128)(2,1)}, bf16[384,384]{1,0:T(8,128)(2,1)S(1)}, u32[]{:S(2)}, u32[]{:S(2)}) collective-permute-start(bf16[384,384]{1,0:T(8,128)(2,1)} %refs_1_.3), channel_id=1, source_target_pairs={{0,2},{1,3},{2,4},{3,5},{4,6},{5,7},{6,0},{7,1},{8,10},{9,11},{10,... | collective-permute-start | bytes 884744 | tf_op jit(solution)/shard_map/ppermute | solution.py:40
  25.6 2.0 collective-permute-start.4
  25.8 5.2 %copy-start = (bf16[256,3072]{1,0:T(8,128)(2,1)S(1)}, bf16[256,3072]{1,0:T(8,128)(2,1)}, u32[]{:S(2)}) copy-start(bf16[256,3072]{1,0:T(8,128)(2,1)} %grad_ref.2) | copy-start | bytes 4718596
  25.8 5.2 %copy-start.9 = (bf16[256,3072]{1,0:T(8,128)(2,1)S(1)}, bf16[256,3072]{1,0:T(8,128)(2,1)}, u32[]{:S(2)}) copy-start(bf16[256,3072]{1,0:T(8,128)(2,1)} %video_ref) | copy-start | bytes 4718596
  25.8 22.0 %collective-permute-start.9 = (bf16[768,384]{1,0:T(8,128)(2,1)S(1)}, bf16[768,384]{1,0:T(8,128)(2,1)S(1)}, u32[]{:S(2)}, u32[]{:S(2)}) collective-permute-start(bf16[768,384]{1,0:T(8,128)(2,1)S(1)} %constant_dynamic-update-slice_fusion.refs_3_), channel_id=1, source_target_pairs={{0,2},{1,3},{2,4},{3,5},{4,6},{5,7},{6,0},{7,1},{8,10},{9,11},{10,... | collective-permute-start | bytes 1769480 | tf_op jit(solution)/shard_map/ppermute | solution.py:40
  27.6 8.4 %collective-permute-start.5 = (bf16[32,4096]{1,0:T(8,128)(2,1)S(1)}, bf16[32,4096]{1,0:T(8,128)(2,1)S(1)}, u32[]{:S(2)}, u32[]{:S(2)}) collective-permute-start(bf16[32,4096]{1,0:T(8,128)(2,1)S(1)} %add_convert_fusion.1), channel_id=1, source_target_pairs={{0,16},{8,24},{16,0},{24,8},{1,17},{9,25},{17,1},{25,9},{2,18},{10... | collective-permute-start | bytes 786440 | tf_op jit(solution)/shard_map/ppermute | solution.py:44
  29.3 6.7 %copy-start.6 = (bf16[1,128,4096]{2,1,0:T(8,128)(2,1)S(1)}, bf16[1,128,4096]{2,1,0:T(8,128)(2,1)}, u32[]{:S(2)}) copy-start(bf16[1,128,4096]{2,1,0:T(8,128)(2,1)} %param.17) | copy-start | bytes 3145732
  29.3 6.7 %copy-start.24 = (f32[4096]{0:T(1024)S(1)}, f32[4096]{0:T(1024)}, u32[]{:S(2)}) copy-start(f32[4096]{0:T(1024)} %param.25) | copy-start | bytes 49156
  29.4 38.3 %collective-permute-start.13 = (bf16[1536,384]{1,0:T(8,128)(2,1)S(1)}, bf16[1536,384]{1,0:T(8,128)(2,1)S(1)}, u32[]{:S(2)}, u32[]{:S(2)}) collective-permute-start(bf16[1536,384]{1,0:T(8,128)(2,1)S(1)} %pad_maximum_fusion), channel_id=1, source_target_pairs={{0,1},{1,0},{2,3},{3,2},{4,5},{5,4},{6,7},{7,6},{8,9},{9,8},{10,11... | collective-permute-start | bytes 3538952 | tf_op jit(solution)/shard_map/ppermute | solution.py:40
  34.3 13.4 %copy-start.21 = (f32[256,1]{1,0:T(8,128)}, f32[256,1]{1,0:T(8,128)S(1)}, u32[]{:S(2)}) copy-start(f32[256,1]{1,0:T(8,128)S(1)} %get-tuple-element.145) | copy-start | bytes 3076
  34.3 33.3 %copy-start.18 = (bf16[512,384]{1,0:T(8,128)(2,1)S(1)}, bf16[512,384]{1,0:T(8,128)(2,1)}, u32[]{:S(2)}) copy-start(bf16[512,384]{1,0:T(8,128)(2,1)} %refs_4_.1) | copy-start | bytes 1179652
  34.3 33.3 %copy-start.19 = (bf16[512,384]{1,0:T(8,128)(2,1)S(1)}, bf16[512,384]{1,0:T(8,128)(2,1)}, u32[]{:S(2)}) copy-start(bf16[512,384]{1,0:T(8,128)(2,1)} %refs_5_.1) | copy-start | bytes 1179652
  36.9 8.4 %collective-permute-start.6 = (bf16[32,1024]{1,0:T(8,128)(2,1)S(1)}, bf16[32,1024]{1,0:T(8,128)(2,1)S(1)}, u32[]{:S(2)}, u32[]{:S(2)}) collective-permute-start(bf16[32,1024]{1,0:T(8,128)(2,1)S(1)} %get-tuple-element.92), channel_id=1, source_target_pairs={{0,2},{1,3},{2,4},{3,5},{4,6},{5,7},{6,0},{7,1},{8,10},{9,11},{10,... | collective-permute-start | bytes 196616 | tf_op jit(solution)/shard_map/ppermute | solution.py:40
  38.5 9.2 %collective-permute-start.7 = (bf16[32,1024]{1,0:T(8,128)(2,1)S(1)}, bf16[32,1024]{1,0:T(8,128)(2,1)S(1)}, u32[]{:S(2)}, u32[]{:S(2)}) collective-permute-start(bf16[32,1024]{1,0:T(8,128)(2,1)S(1)} %get-tuple-element.93), channel_id=1, source_target_pairs={{0,4},{1,5},{2,6},{3,7},{4,0},{5,1},{6,2},{7,3},{8,12},{9,13},{10,... | collective-permute-start | bytes 196616 | tf_op jit(solution)/shard_map/ppermute | solution.py:40
  39.8 8.0 %collective-permute-start.8 = (bf16[32,1024]{1,0:T(8,128)(2,1)S(1)}, bf16[32,1024]{1,0:T(8,128)(2,1)S(1)}, u32[]{:S(2)}, u32[]{:S(2)}) collective-permute-start(bf16[32,1024]{1,0:T(8,128)(2,1)S(1)} %get-tuple-element.94), channel_id=1, source_target_pairs={{0,6},{1,7},{2,0},{3,1},{4,2},{5,3},{6,4},{7,5},{8,14},{9,15},{10,... | collective-permute-start | bytes 196616 | tf_op jit(solution)/shard_map/ppermute | solution.py:40
  47.8 19.3 %collective-permute-start.15 = (bf16[768,384]{1,0:T(8,128)(2,1)S(1)}, bf16[768,384]{1,0:T(8,128)(2,1)S(1)}, u32[]{:S(2)}, u32[]{:S(2)}) collective-permute-start(bf16[768,384]{1,0:T(8,128)(2,1)S(1)} %collective-permute-done.9.refs_4_), channel_id=1, source_target_pairs={{0,2},{1,3},{2,4},{3,5},{4,6},{5,7},{6,0},{7,1},{8,10},{9,11},{10,... | collective-permute-start | bytes 1769480 | tf_op jit(solution)/shard_map/ppermute | solution.py:40
  49.7 15.9 %collective-permute-start.14 = (bf16[4,2,64,384]{3,2,1,0:T(8,128)(2,1)S(1)}, bf16[4,2,64,384]{3,2,1,0:T(8,128)(2,1)S(1)}, u32[]{:S(2)}, u32[]{:S(2)}) collective-permute-start(bf16[4,2,64,384]{3,2,1,0:T(8,128)(2,1)S(1)} %get-tuple-element.96), channel_id=1, source_target_pairs={{0,1},{1,0},{2,3},{3,2},{4,5},{5,4},{6,7},{7,6},{8,9},{9,8},{10,11... | collective-permute-start | bytes 1179656 | tf_op jit(solution)/shard_map/ppermute | solution.py:40
  51.2 7.7 %collective-permute-start.11 = (bf16[4,32,1024]{2,1,0:T(8,128)(2,1)S(1)}, bf16[4,32,1024]{2,1,0:T(8,128)(2,1)S(1)}, u32[]{:S(2)}, u32[]{:S(2)}) collective-permute-start(bf16[4,32,1024]{2,1,0:T(8,128)(2,1)S(1)} %pad_maximum_fusion.4.refs_0_), channel_id=1, source_target_pairs={{0,16},{8,24},{16,0},{24,8},{1,17},{9,25},{17,1},{25,9},{2,18},{10... | collective-permute-start | bytes 786440 | tf_op jit(solution)/shard_map/ppermute | solution.py:44
  58.9 8.7 %collective-permute-start.12 = (bf16[4,32,1024]{2,1,0:T(8,128)(2,1)S(1)}, bf16[4,32,1024]{2,1,0:T(8,128)(2,1)S(1)}, u32[]{:S(2)}, u32[]{:S(2)}) collective-permute-start(bf16[4,32,1024]{2,1,0:T(8,128)(2,1)S(1)} %collective-permute-done.11.refs_2_), channel_id=1, source_target_pairs={{0,8},{8,0},{16,24},{24,16},{1,9},{9,1},{17,25},{25,17},{2,10},{10... | collective-permute-start | bytes 786440 | tf_op jit(solution)/shard_map/ppermute | solution.py:44
  58.9 8.7 %collective-permute-start.10 = (bf16[4,32,1024]{2,1,0:T(8,128)(2,1)S(1)}, bf16[4,32,1024]{2,1,0:T(8,128)(2,1)S(1)}, u32[]{:S(2)}, u32[]{:S(2)}) collective-permute-start(bf16[4,32,1024]{2,1,0:T(8,128)(2,1)S(1)} %pad_maximum_fusion.4.refs_0_), channel_id=1, source_target_pairs={{0,8},{8,0},{16,24},{24,16},{1,9},{9,1},{17,25},{25,17},{2,10},{10... | collective-permute-start | bytes 786440 | tf_op jit(solution)/shard_map/ppermute | solution.py:44
  65.6 22.9 %collective-permute-start.19 = (bf16[768,384]{1,0:T(8,128)(2,1)S(1)}, bf16[768,384]{1,0:T(8,128)(2,1)S(1)}, u32[]{:S(2)}, u32[]{:S(2)}) collective-permute-start(bf16[768,384]{1,0:T(8,128)(2,1)S(1)} %collective-permute-done.9.refs_4_), channel_id=1, source_target_pairs={{0,1},{1,0},{2,3},{3,2},{4,5},{5,4},{6,7},{7,6},{8,9},{9,8},{10,11... | collective-permute-start | bytes 1769480 | tf_op jit(solution)/shard_map/ppermute | solution.py:40
  67.1 25.3 %collective-permute-start.20 = (bf16[768,384]{1,0:T(8,128)(2,1)S(1)}, bf16[768,384]{1,0:T(8,128)(2,1)S(1)}, u32[]{:S(2)}, u32[]{:S(2)}) collective-permute-start(bf16[768,384]{1,0:T(8,128)(2,1)S(1)} %collective-permute-done.15.refs_6_), channel_id=1, source_target_pairs={{0,1},{1,0},{2,3},{3,2},{4,5},{5,4},{6,7},{7,6},{8,9},{9,8},{10,11... | collective-permute-start | bytes 1769480 | tf_op jit(solution)/shard_map/ppermute | solution.py:40
  69.4 7.7 %collective-permute-start.16 = (bf16[128,768]{1,0:T(8,128)(2,1)S(1)}, bf16[128,768]{1,0:T(8,128)(2,1)S(1)}, u32[]{:S(2)}, u32[]{:S(2)}) collective-permute-start(bf16[128,768]{1,0:T(8,128)(2,1)S(1)} %get-tuple-element.104), channel_id=1, source_target_pairs={{0,6},{1,7},{2,0},{3,1},{4,2},{5,3},{6,4},{7,5},{8,14},{9,15},{10,... | collective-permute-start | bytes 589832 | tf_op jit(solution)/shard_map/ppermute | solution.py:40
  71.7 16.6 %collective-permute-start.17 = (bf16[128,768]{1,0:T(8,128)(2,1)S(1)}, bf16[128,768]{1,0:T(8,128)(2,1)S(1)}, u32[]{:S(2)}, u32[]{:S(2)}) collective-permute-start(bf16[128,768]{1,0:T(8,128)(2,1)S(1)} %get-tuple-element.105), channel_id=1, source_target_pairs={{0,4},{1,5},{2,6},{3,7},{4,0},{5,1},{6,2},{7,3},{8,12},{9,13},{10,... | collective-permute-start | bytes 589832 | tf_op jit(solution)/shard_map/ppermute | solution.py:40
  72.5 15.8 %collective-permute-start.18 = (bf16[128,768]{1,0:T(8,128)(2,1)S(1)}, bf16[128,768]{1,0:T(8,128)(2,1)S(1)}, u32[]{:S(2)}, u32[]{:S(2)}) collective-permute-start(bf16[128,768]{1,0:T(8,128)(2,1)S(1)} %get-tuple-element.106), channel_id=1, source_target_pairs={{0,2},{1,3},{2,4},{3,5},{4,6},{5,7},{6,0},{7,1},{8,10},{9,11},{10,... | collective-permute-start | bytes 589832 | tf_op jit(solution)/shard_map/ppermute | solution.py:40
  92.4 7.6 %collective-permute-start.26 = (bf16[128,768]{1,0:T(8,128)(2,1)S(1)}, bf16[128,768]{1,0:T(8,128)(2,1)S(1)}, u32[]{:S(2)}, u32[]{:S(2)}) collective-permute-start(bf16[128,768]{1,0:T(8,128)(2,1)S(1)} %add_convert_fusion.6.refs_0_), channel_id=1, source_target_pairs={{0,6},{1,7},{2,0},{3,1},{4,2},{5,3},{6,4},{7,5},{8,14},{9,15},{10,... | collective-permute-start | bytes 589832 | tf_op jit(solution)/shard_map/ppermute | solution.py:40
  94.7 16.3 %collective-permute-start.21 = (bf16[128,768]{1,0:T(8,128)(2,1)S(1)}, bf16[128,768]{1,0:T(8,128)(2,1)S(1)}, u32[]{:S(2)}, u32[]{:S(2)}) collective-permute-start(bf16[128,768]{1,0:T(8,128)(2,1)S(1)} %add_convert_fusion.6.refs_0_), channel_id=1, source_target_pairs={{0,4},{1,5},{2,6},{3,7},{4,0},{5,1},{6,2},{7,3},{8,12},{9,13},{10,... | collective-permute-start | bytes 589832 | tf_op jit(solution)/shard_map/ppermute | solution.py:40
  95.5 17.0 %collective-permute-start.23 = (bf16[128,768]{1,0:T(8,128)(2,1)S(1)}, bf16[128,768]{1,0:T(8,128)(2,1)S(1)}, u32[]{:S(2)}, u32[]{:S(2)}) collective-permute-start(bf16[128,768]{1,0:T(8,128)(2,1)S(1)} %add_convert_fusion.6.refs_0_), channel_id=1, source_target_pairs={{0,2},{1,3},{2,4},{3,5},{4,6},{5,7},{6,0},{7,1},{8,10},{9,11},{10,... | collective-permute-start | bytes 589832 | tf_op jit(solution)/shard_map/ppermute | solution.py:40
  95.7 17.3 %collective-permute-start.22 = (bf16[128,768]{1,0:T(8,128)(2,1)S(1)}, bf16[128,768]{1,0:T(8,128)(2,1)S(1)}, u32[]{:S(2)}, u32[]{:S(2)}) collective-permute-start(bf16[128,768]{1,0:T(8,128)(2,1)S(1)} %add_convert_fusion.6.refs_0_), channel_id=1, source_target_pairs={{0,1},{1,0},{2,3},{3,2},{4,5},{5,4},{6,7},{7,6},{8,9},{9,8},{10,11... | collective-permute-start | bytes 589832 | tf_op jit(solution)/shard_map/ppermute | solution.py:40
  100.1 14.0 %collective-permute-start.27 = (bf16[128,768]{1,0:T(8,128)(2,1)S(1)}, bf16[128,768]{1,0:T(8,128)(2,1)S(1)}, u32[]{:S(2)}, u32[]{:S(2)}) collective-permute-start(bf16[128,768]{1,0:T(8,128)(2,1)S(1)} %collective-permute-done.26.refs_6_), channel_id=1, source_target_pairs={{0,1},{1,0},{2,3},{3,2},{4,5},{5,4},{6,7},{7,6},{8,9},{9,8},{10,11... | collective-permute-start | bytes 589832 | tf_op jit(solution)/shard_map/ppermute | solution.py:40
  111.0 9.2 %collective-permute-start.25 = (bf16[128,768]{1,0:T(8,128)(2,1)S(1)}, bf16[128,768]{1,0:T(8,128)(2,1)S(1)}, u32[]{:S(2)}, u32[]{:S(2)}) collective-permute-start(bf16[128,768]{1,0:T(8,128)(2,1)S(1)} %collective-permute-done.21.refs_4_), channel_id=1, source_target_pairs={{0,1},{1,0},{2,3},{3,2},{4,5},{5,4},{6,7},{7,6},{8,9},{9,8},{10,11... | collective-permute-start | bytes 589832 | tf_op jit(solution)/shard_map/ppermute | solution.py:40
  112.5 7.6 %collective-permute-start.24 = (bf16[128,768]{1,0:T(8,128)(2,1)S(1)}, bf16[128,768]{1,0:T(8,128)(2,1)S(1)}, u32[]{:S(2)}, u32[]{:S(2)}) collective-permute-start(bf16[128,768]{1,0:T(8,128)(2,1)S(1)} %collective-permute-done.23.refs_2_), channel_id=1, source_target_pairs={{0,1},{1,0},{2,3},{3,2},{4,5},{5,4},{6,7},{7,6},{8,9},{9,8},{10,11... | collective-permute-start | bytes 589832 | tf_op jit(solution)/shard_map/ppermute | solution.py:40
  113.0 7.1 %copy-start.26 = (s32[8]{0:T(128)S(1)}, s32[8]{0:T(128)}, u32[]{:S(2)}) copy-start(s32[8]{0:T(128)} %count_ref.1) | copy-start | bytes 100
  113.0 7.1 %copy-start.27 = (s32[8]{0:T(128)S(1)}, s32[8]{0:T(128)}, u32[]{:S(2)}) copy-start(s32[8]{0:T(128)} %caption_ref.1) | copy-start | bytes 100
  113.0 10.9 %collective-permute-start.28 = (bf16[2,2,64,384]{3,2,1,0:T(8,128)(2,1)S(1)}, bf16[2,2,64,384]{3,2,1,0:T(8,128)(2,1)S(1)}, u32[]{:S(2)}, u32[]{:S(2)}) collective-permute-start(bf16[2,2,64,384]{3,2,1,0:T(8,128)(2,1)S(1)} %get-tuple-element.117), channel_id=1, source_target_pairs={{0,2},{1,3},{2,4},{3,5},{4,6},{5,7},{6,0},{7,1},{8,10},{9,11},{10,... | collective-permute-start | bytes 589832 | tf_op jit(solution)/shard_map/ppermute | solution.py:40
  113.0 14.8 %collective-permute-start.29 = (bf16[2,2,64,384]{3,2,1,0:T(8,128)(2,1)S(1)}, bf16[2,2,64,384]{3,2,1,0:T(8,128)(2,1)S(1)}, u32[]{:S(2)}, u32[]{:S(2)}) collective-permute-start(bf16[2,2,64,384]{3,2,1,0:T(8,128)(2,1)S(1)} %get-tuple-element.118), channel_id=1, source_target_pairs={{0,4},{1,5},{2,6},{3,7},{4,0},{5,1},{6,2},{7,3},{8,12},{9,13},{10,... | collective-permute-start | bytes 589832 | tf_op jit(solution)/shard_map/ppermute | solution.py:40
  114.1 13.8 %collective-permute-start.30 = (bf16[2,2,64,384]{3,2,1,0:T(8,128)(2,1)S(1)}, bf16[2,2,64,384]{3,2,1,0:T(8,128)(2,1)S(1)}, u32[]{:S(2)}, u32[]{:S(2)}) collective-permute-start(bf16[2,2,64,384]{3,2,1,0:T(8,128)(2,1)S(1)} %get-tuple-element.119), channel_id=1, source_target_pairs={{0,6},{1,7},{2,0},{3,1},{4,2},{5,3},{6,4},{7,5},{8,14},{9,15},{10,... | collective-permute-start | bytes 589832 | tf_op jit(solution)/shard_map/ppermute | solution.py:40
  123.9 19.3 %copy-start.20 = (f32[256,2]{1,0:T(8,128)}, f32[256,2]{1,0:T(8,128)S(1)}, u32[]{:S(2)}) copy-start(f32[256,2]{1,0:T(8,128)S(1)} %get-tuple-element.124) | copy-start | bytes 6148
  123.9 32.1 %copy-start.12 = (bf16[4,128,768]{2,1,0:T(8,128)(2,1)}, bf16[4,128,768]{2,1,0:T(8,128)(2,1)S(1)}, u32[]{:S(2)}) copy-start(bf16[4,128,768]{2,1,0:T(8,128)(2,1)S(1)} %get-tuple-element.142) | copy-start | bytes 2359300
  127.9 5.4 %collective-permute-start.31 = (f32[256,2]{1,0:T(8,128)S(1)}, f32[256,2]{1,0:T(8,128)S(1)}, u32[]{:S(2)}, u32[]{:S(2)}) collective-permute-start(f32[256,2]{1,0:T(8,128)S(1)} %get-tuple-element.124), channel_id=1, source_target_pairs={{0,8},{8,0},{16,24},{24,16},{1,9},{9,1},{17,25},{25,17},{2,10},{10... | collective-permute-start | bytes 6152 | tf_op jit(solution)/shard_map/ppermute | solution.py:44
  127.9 15.2 %collective-permute-start.33 = (bf16[2,256,384]{2,1,0:T(8,128)(2,1)S(1)}, bf16[2,256,384]{2,1,0:T(8,128)(2,1)S(1)}, u32[]{:S(2)}, u32[]{:S(2)}) collective-permute-start(bf16[2,256,384]{2,1,0:T(8,128)(2,1)S(1)} %get-tuple-element.150.refs_4_), channel_id=1, source_target_pairs={{0,2},{1,3},{2,4},{3,5},{4,6},{5,7},{6,0},{7,1},{8,10},{9,11},{10,... | collective-permute-start | bytes 1179656 | tf_op jit(solution)/shard_map/ppermute | solution.py:40
  131.7 24.2 %collective-permute-start.32 = (bf16[4,128,768]{2,1,0:T(8,128)(2,1)S(1)}, bf16[4,128,768]{2,1,0:T(8,128)(2,1)S(1)}, u32[]{:S(2)}, u32[]{:S(2)}) collective-permute-start(bf16[4,128,768]{2,1,0:T(8,128)(2,1)S(1)} %get-tuple-element.128), channel_id=1, source_target_pairs={{0,1},{1,0},{2,3},{3,2},{4,5},{5,4},{6,7},{7,6},{8,9},{9,8},{10,11... | collective-permute-start | bytes 2359304 | tf_op jit(solution)/shard_map/ppermute | solution.py:40
  133.3 15.5 %copy-start.30 = (f32[256,2]{1,0:T(8,128)}, f32[256,2]{1,0:T(8,128)S(1)}, u32[]{:S(2)}) copy-start(f32[256,2]{1,0:T(8,128)S(1)} %collective-permute-done.31) | copy-start | bytes 6148
  133.3 22.6 %collective-permute-start.36 = (bf16[4,2,2,64,384]{4,3,2,1,0:T(8,128)(2,1)S(1)}, bf16[4,2,2,64,384]{4,3,2,1,0:T(8,128)(2,1)S(1)}, u32[]{:S(2)}, u32[]{:S(2)}) collective-permute-start(bf16[4,2,2,64,384]{4,3,2,1,0:T(8,128)(2,1)S(1)} %pad_maximum_fusion.1.refs_0_), channel_id=1, source_target_pairs={{0,8},{8,0},{16,24},{24,16},{1,9},{9,1},{17,25},{25,17},{2,10},{10... | collective-permute-start | bytes 2359304 | tf_op jit(solution)/shard_map/ppermute | solution.py:44
  133.4 22.5 %collective-permute-start.35 = (bf16[4,2,2,64,384]{4,3,2,1,0:T(8,128)(2,1)S(1)}, bf16[4,2,2,64,384]{4,3,2,1,0:T(8,128)(2,1)}, u32[]{:S(2)}, u32[]{:S(2)}) collective-permute-start(bf16[4,2,2,64,384]{4,3,2,1,0:T(8,128)(2,1)S(1)} %pad_maximum_fusion.1.refs_0_), channel_id=1, source_target_pairs={{0,16},{8,24},{16,0},{24,8},{1,17},{9,25},{17,1},{25,9},{2,18},{10... | collective-permute-start | bytes 2359304 | tf_op jit(solution)/shard_map/ppermute | solution.py:44
  143.0 5.8 %copy-start.10 = (bf16[2,256,384]{2,1,0:T(8,128)(2,1)}, bf16[2,256,384]{2,1,0:T(8,128)(2,1)S(1)}, u32[]{:S(2)}) copy-start(bf16[2,256,384]{2,1,0:T(8,128)(2,1)S(1)} %collective-permute-done.33.refs_5_) | copy-start | bytes 1179652
  143.0 12.9 %collective-permute-start.34 = (bf16[2,256,384]{2,1,0:T(8,128)(2,1)S(1)}, bf16[2,256,384]{2,1,0:T(8,128)(2,1)}, u32[]{:S(2)}, u32[]{:S(2)}) collective-permute-start(bf16[2,256,384]{2,1,0:T(8,128)(2,1)S(1)} %collective-permute-done.33.refs_5_), channel_id=1, source_target_pairs={{0,2},{1,3},{2,4},{3,5},{4,6},{5,7},{6,0},{7,1},{8,10},{9,11},{10,... | collective-permute-start | bytes 1179656 | tf_op jit(solution)/shard_map/ppermute | solution.py:40
  148.8 8.1 %copy-start.13 = (bf16[2,256,768]{2,1,0:T(8,128)(2,1)}, bf16[2,256,768]{2,1,0:T(8,128)(2,1)S(1)}, u32[]{:S(2)}) copy-start(bf16[2,256,768]{2,1,0:T(8,128)(2,1)S(1)} %get-tuple-element.133) | copy-start | bytes 2359300
  148.8 8.1 %copy-start.15 = (bf16[2,256,768]{2,1,0:T(8,128)(2,1)}, bf16[2,256,768]{2,1,0:T(8,128)(2,1)S(1)}, u32[]{:S(2)}) copy-start(bf16[2,256,768]{2,1,0:T(8,128)(2,1)S(1)} %get-tuple-element.127) | copy-start | bytes 2359300
  155.9 27.4 %collective-permute-start.37 = (bf16[2,256,1536]{2,1,0:T(8,128)(2,1)}, bf16[2,256,1536]{2,1,0:T(8,128)(2,1)}, u32[]{:S(2)}, u32[]{:S(2)}) collective-permute-start(bf16[2,256,1536]{2,1,0:T(8,128)(2,1)} %get-tuple-element.132), channel_id=1, source_target_pairs={{0,8},{8,0},{16,24},{24,16},{1,9},{9,1},{17,25},{25,17},{2,10},{10... | collective-permute-start | bytes 4718600 | tf_op jit(solution)/shard_map/ppermute | solution.py:44
  156.9 20.1 %collective-permute-start.44 = (bf16[128,768]{1,0:T(8,128)(2,1)S(1)}, bf16[128,768]{1,0:T(8,128)(2,1)}, u32[]{:S(2)}, u32[]{:S(2)}) collective-permute-start(bf16[128,768]{1,0:T(8,128)(2,1)S(1)} %get-tuple-element.167), channel_id=1, source_target_pairs={{0,6},{1,7},{2,0},{3,1},{4,2},{5,3},{6,4},{7,5},{8,14},{9,15},{10,... | collective-permute-start | bytes 589832 | tf_op jit(solution)/shard_map/ppermute | solution.py:40
  157.0 23.1 %collective-permute-start.43 = (bf16[128,768]{1,0:T(8,128)(2,1)}, bf16[128,768]{1,0:T(8,128)(2,1)}, u32[]{:S(2)}, u32[]{:S(2)}) collective-permute-start(bf16[128,768]{1,0:T(8,128)(2,1)} %get-tuple-element.168), channel_id=1, source_target_pairs={{0,2},{1,3},{2,4},{3,5},{4,6},{5,7},{6,0},{7,1},{8,10},{9,11},{10,... | collective-permute-start | bytes 589832 | tf_op jit(solution)/shard_map/ppermute | solution.py:40
  159.0 23.0 %collective-permute-start.40 = (bf16[2,256,384]{2,1,0:T(8,128)(2,1)}, bf16[2,256,384]{2,1,0:T(8,128)(2,1)}, u32[]{:S(2)}, u32[]{:S(2)}) collective-permute-start(bf16[2,256,384]{2,1,0:T(8,128)(2,1)} %collective-permute-done.34.refs_6_), channel_id=1, source_target_pairs={{0,2},{1,3},{2,4},{3,5},{4,6},{5,7},{6,0},{7,1},{8,10},{9,11},{10,... | collective-permute-start | bytes 1179656 | tf_op jit(solution)/shard_map/ppermute | solution.py:40
  159.0 27.2 %collective-permute-start.39 = (bf16[4,256,384]{2,1,0:T(8,128)(2,1)}, bf16[4,256,384]{2,1,0:T(8,128)(2,1)}, u32[]{:S(2)}, u32[]{:S(2)}) collective-permute-start(bf16[4,256,384]{2,1,0:T(8,128)(2,1)} %bitcast.22), channel_id=1, source_target_pairs={{0,1},{1,0},{2,3},{3,2},{4,5},{5,4},{6,7},{7,6},{8,9},{9,8},{10,11... | collective-permute-start | bytes 2359304 | tf_op jit(solution)/shard_map/ppermute | solution.py:40
  177.0 9.2 %collective-permute-start.42 = (bf16[4,2,2,64,384]{4,3,2,1,0:T(8,128)(2,1)}, bf16[4,2,2,64,384]{4,3,2,1,0:T(8,128)(2,1)}, u32[]{:S(2)}, u32[]{:S(2)}) collective-permute-start(bf16[4,2,2,64,384]{4,3,2,1,0:T(8,128)(2,1)} %collective-permute-done.35.refs_2_), channel_id=1, source_target_pairs={{0,8},{8,0},{16,24},{24,16},{1,9},{9,1},{17,25},{25,17},{2,10},{10... | collective-permute-start | bytes 2359304 | tf_op jit(solution)/shard_map/ppermute | solution.py:44
  179.1 4.3 %copy-start.14 = (bf16[2,256,768]{2,1,0:T(8,128)(2,1)S(1)}, bf16[2,256,768]{2,1,0:T(8,128)(2,1)}, u32[]{:S(2)}) copy-start(bf16[2,256,768]{2,1,0:T(8,128)(2,1)} %copy-done.13) | copy-start | bytes 2359300
  180.1 6.1 %collective-permute-start.41 = (f32[256,2]{1,0:T(8,128)S(1)}, f32[256,2]{1,0:T(8,128)S(1)}, u32[]{:S(2)}, u32[]{:S(2)}) collective-permute-start(f32[256,2]{1,0:T(8,128)S(1)} %add.79), channel_id=1, source_target_pairs={{0,16},{8,24},{16,0},{24,8},{1,17},{9,25},{17,1},{25,9},{2,18},{10... | collective-permute-start | bytes 6152 | tf_op jit(solution)/shard_map/ppermute | solution.py:44
  184.7 19.7 %collective-permute-start.38 = (bf16[2,256,768]{2,1,0:T(8,128)(2,1)S(1)}, bf16[2,256,768]{2,1,0:T(8,128)(2,1)S(1)}, u32[]{:S(2)}, u32[]{:S(2)}) collective-permute-start(bf16[2,256,768]{2,1,0:T(8,128)(2,1)S(1)} %add_convert_fusion), channel_id=1, source_target_pairs={{0,16},{8,24},{16,0},{24,8},{1,17},{9,25},{17,1},{25,9},{2,18},{10... | collective-permute-start | bytes 2359304 | tf_op jit(solution)/shard_map/ppermute | solution.py:44
  186.3 10.8 %collective-permute-start.46 = (bf16[128,768]{1,0:T(8,128)(2,1)S(1)}, bf16[128,768]{1,0:T(8,128)(2,1)S(1)}, u32[]{:S(2)}, u32[]{:S(2)}) collective-permute-start(bf16[128,768]{1,0:T(8,128)(2,1)S(1)} %copy-done.29), channel_id=1, source_target_pairs={{0,4},{1,5},{2,6},{3,7},{4,0},{5,1},{6,2},{7,3},{8,12},{9,13},{10,... | collective-permute-start | bytes 589832 | tf_op jit(solution)/shard_map/ppermute | solution.py:40
  186.4 21.6 %collective-permute-start.45 = (bf16[4,256,384]{2,1,0:T(8,128)(2,1)S(1)}, bf16[4,256,384]{2,1,0:T(8,128)(2,1)S(1)}, u32[]{:S(2)}, u32[]{:S(2)}) collective-permute-start(bf16[4,256,384]{2,1,0:T(8,128)(2,1)S(1)} %bitcast.61), channel_id=1, source_target_pairs={{0,1},{1,0},{2,3},{3,2},{4,5},{5,4},{6,7},{7,6},{8,9},{9,8},{10,11... | collective-permute-start | bytes 2359304 | tf_op jit(solution)/shard_map/ppermute | solution.py:40
  190.2 14.2 %copy-start.16 = (bf16[2,256,768]{2,1,0:T(8,128)(2,1)S(1)}, bf16[2,256,768]{2,1,0:T(8,128)(2,1)}, u32[]{:S(2)}) copy-start(bf16[2,256,768]{2,1,0:T(8,128)(2,1)} %copy-done.15) | copy-start | bytes 2359300
  (14 other events, 32.5 us)

commit v6 on v5

--- a/solution.py
+++ b/solution.py
@@ -11,7 +11,7 @@
 BF = jnp.bfloat16
 F32 = jnp.float32
 SLOTS = 3
-VMEM_BYTES = 20 * 1024 * 1024
+VMEM_BYTES = 60 * 1024 * 1024
 SPARE_BYTES = 8 * 1024 * 1024
 SMALL = pl.CostEstimate(flops=1, bytes_accessed=1, transcendentals=0)
 
@@ -523,6 +523,25 @@
     return call(body, out, operands, 1)
 
 
+def slots_of(count_ref, caption_ref, base, captions):
+    def find(sample, carry):
+        total, first, start = carry
+        total = total + count_ref[sample]
+        past = total <= base
+        return total, first + past.astype(jnp.int32), jnp.where(past, total, start)
+
+    zero = jnp.int32(0)
+    _, first, start = lax.fori_loop(0, captions, find, (zero, zero, zero))
+    found, edge = [], start - base
+    for slot in range(SLOTS):
+        valid = first + slot < captions
+        sample = jnp.minimum(first + slot, captions - 1)
+        end = edge + jnp.where(valid, count_ref[sample], 0)
+        found.append((edge, end, caption_ref[sample], valid))
+        edge = end
+    return found
+
+
 def attend(queries, d_attended, column_sum, kv_blocks, place, counts, sample_caption, lens, pairs):
     tokens, width = queries.shape
     cap_len = kv_blocks[0].shape[0]
@@ -534,32 +553,15 @@
 
     def body(place_ref, count_ref, caption_ref, len_ref, q_ref, da_ref, sum_ref, *refs):
         block_refs = refs[: len(kv_blocks)]
-        both_ref, att_ref, dq_ref, rows_ref, own_ref, away_ref, kv_ref = refs[len(kv_blocks) :]
+        both_ref, att_ref, dq_ref, rows_ref, slot_ref, kv_ref = refs[len(kv_blocks) :]
         z, y, g = place_ref[0], place_ref[1], place_ref[2]
-        base = (z * 2 + y) * tokens
-
-        def find(sample, carry):
-            total, first, start = carry
-            total = total + count_ref[sample]
-            past = total <= base
-            return total, first + past.astype(jnp.int32), jnp.where(past, total, start)
-
-        zero = jnp.int32(0)
-        _, first, start = lax.fori_loop(0, captions, find, (zero, zero, zero))
-        low, high, length, far_to, side_to, valid = [], [], [], [], [], []
-        edge = start - base
-        for slot in range(SLOTS):
-            ok = first + slot < captions
-            sample = jnp.minimum(first + slot, captions - 1)
-            caption = caption_ref[sample]
-            low.append(edge)
-            edge = edge + jnp.where(ok, count_ref[sample], 0)
-            high.append(edge)
+        low, high, length = [], [], []
+        found = slots_of(count_ref, caption_ref, (z * 2 + y) * tokens, captions)
+        for slot, (start, end, caption, _) in enumerate(found):
+            low.append(start)
+            high.append(end)
             length.append(len_ref[caption])
-            far_to.append(lax.rem(caption // 2 - z + pairs, pairs))
-            side_to.append(lax.rem(caption, 2) ^ y)
-            valid.append(ok)
-            entry = lax.rem(z - caption // 2 + pairs, pairs) * 2 + side_to[slot]
+            entry = lax.rem(z - caption // 2 + pairs, pairs) * 2 + (lax.rem(caption, 2) ^ y)
             for number, block in enumerate(block_refs):
 
                 @pl.when(entry == number)
@@ -576,8 +578,6 @@
             return jnp.where(slot_of == 0, values[0], jnp.where(slot_of == 1, values[1], values[2]))
 
         live = (token >= of_slot(low)) & (token < of_slot(high)) & (key < of_slot(length))
-        own_ref[...] = jnp.zeros_like(own_ref)
-        away_ref[...] = jnp.zeros_like(away_ref)
         first_sum = jnp.zeros((tokens, 1), F32)
         second_sum = jnp.zeros((tokens, 1), F32)
         for head in range(heads):
@@ -605,12 +605,8 @@
                         slot * cap_len + part * cap_quarter, slot * cap_len + (part + 1) * cap_quarter
                     )
                     to = pl.ds(aligned((part ^ g) * cap_quarter, cap_quarter), cap_quarter)
-                    for side, target_ref in enumerate((own_ref, away_ref)):
-
-                        @pl.when(valid[slot] & (side_to[slot] == side))
-                        def _(slot=slot, held=held, to=to, target_ref=target_ref):
-                            target_ref[far_to[slot], to, at] = key_grad[held]
-                            target_ref[far_to[slot], to, at_value] = value_grad[held]
+                    slot_ref[slot, to, at] = key_grad[held]
+                    slot_ref[slot, to, at_value] = value_grad[held]
 
         rows_ref[:, 0:1] = first_sum
         rows_ref[:, 1:2] = second_sum
@@ -625,12 +621,38 @@
         shaped((tokens, width)),
         shaped((tokens, width)),
         shaped((tokens, 2), F32),
-        shaped((pairs, cap_len, 2 * width)),
-        shaped((pairs, cap_len, 2 * width)),
+        shaped((SLOTS, cap_len, 2 * width)),
     ]
     operands = (place, counts, sample_caption, lens, queries, d_attended, column_sum, *kv_blocks)
     scratch = [pltpu.VMEM((keys_wide, 2 * width), BF)]
     return call(body, out, operands, 4, scratch)
+
+
+def caption_terms(slots, side_slots, place, counts, sample_caption, tokens, pairs):
+    captions = counts.shape[0]
+    shape = slots.shape[1:]
+
+    def body(place_ref, count_ref, caption_ref, own_ref, side_ref, *refs):
+        term_refs, total_ref = refs[:-1], refs[-1]
+        z, y = place_ref[0], place_ref[1]
+        total_ref[...] = jnp.zeros_like(total_ref)
+        for side, slot_ref in enumerate((own_ref, side_ref)):
+            base = (z * 2 + (y ^ side)) * tokens
+            for slot, (_, _, caption, valid) in enumerate(
+                slots_of(count_ref, caption_ref, base, captions)
+            ):
+                far = lax.rem(caption // 2 - z + pairs, pairs)
+
+                @pl.when(valid & (lax.rem(caption, 2) == y))
+                def _(slot=slot, far=far, slot_ref=slot_ref):
+                    total_ref[far] += slot_ref[slot].astype(F32)
+
+        for far, term_ref in enumerate(term_refs):
+            term_ref[...] = total_ref[far].astype(term_ref.dtype)
+
+    out = [shaped(shape, F32 if far == 0 else BF) for far in range(pairs)]
+    operands = (place, counts, sample_caption, slots, side_slots)
+    return call(body, out, operands, 3, [pltpu.VMEM((pairs, *shape), F32)])
 
 
 def project_back(attended, d_queries, blocks, place, pairs, part):
@@ -743,7 +765,6 @@
     normed, mean, inverse, own_tiles, other_tiles = prepare_video(
         after(video_states, sent), out_grad, place, pairs, part
     )
-    other_tiles = fsend(other_tiles, 0, 1)
     pieces = encode_rows(
         states, kept, got, after(over_x, normed), final_gain, place, pairs
     )
@@ -756,7 +777,7 @@
     for far in range(3, pairs):
         current = fsend(current, 1, 0)
         ring.append(current)
-    parts[3] = after(parts[3], side_first, other_tiles)
+    parts[3] = after(parts[3], side_first)
     kv_partial = project_captions(
         parts, cross_key, cross_value, side_key, side_value, place, pairs
     )
@@ -765,8 +786,10 @@
     for far in range(1, pairs):
         kv_sum += fsend(kv_partial[far], pairs - far, 0).astype(F32)
     side_later = [fsend(w, 0, 1) for w in ring[2:]]
-    kv_sum = after(kv_sum.astype(BF), side_later)
+    other_tiles = fsend(other_tiles, 0, 1)
+    kv_sum = after(kv_sum.astype(BF), side_later[0])
     kv_blocks = gather_direct(kv_sum)
+    kv_blocks[4] = after(kv_blocks[4], side_later, other_tiles)
 
     step = part + width_local
     blocks = []
@@ -782,7 +805,7 @@
     over_z = [fsend(after(tiles[far], kv_blocks[4]), far, 0) for far in range(1, pairs)]
     over_z = [tiles[0]] + over_z
 
-    both, attended, d_queries, row_sums, kv_own, kv_away = attend(
+    both, attended, d_queries, row_sums, slots = attend(
         queries,
         d_attended,
         column_sum,
@@ -793,7 +816,7 @@
         caption_lens,
         pairs,
     )
-    kv_away, both, row_sums, over_z = after((kv_away, both, row_sums, over_z))
+    slots, both, row_sums, over_z = after((slots, both, row_sums, over_z))
     tiles = jnp.stack(over_z)
 
     def chain(blocks, steps):
@@ -804,41 +827,38 @@
     def joined(two):
         return jnp.stack(two).reshape(-1, tokens, width_local)
 
-    kv_side = fsend(kv_away, 0, 1)
-    late = chain([both], pairs // 2)
+    side_slots = fsend(slots, 0, 1)
+    side_own = fsend(both, 0, 1)
+    late = chain([both], 2)
     sums_core = gsend(row_sums, 1)
     attended, tiles = after((attended, tiles), sums_core)
     tiles_x = gsend(tiles, 2)
-    tiles_core = gsend(tiles, 1)
     own, far_piece, away = project_back(attended, d_queries, blocks, place, pairs, part)
-    stage = (kv_side, late, sums_core, tiles_x, tiles_core, joined(late[:2]), away)
-    kv_side, late, sums_core, tiles_x, tiles_core, first_two, away = after(stage)
-
-    sides = [fsend(first_two, 0, 1)]
-    late = chain(list(late), pairs - 1 - pairs // 2)
+    two = joined(late[1:3])
+    stage = (side_slots, side_own, late, sums_core, tiles_x, two, away)
+    side_slots, side_own, late, sums_core, tiles_x, two, away = after(stage)
+
+    side_two = fsend(two, 0, 1)
+    late = chain(list(late), pairs - 3)
     row_sums = row_sums + sums_core
     sums_x = gsend(row_sums, 2)
     got = gsend(away, 1)
+    tiles_core = gsend(tiles, 1)
     width = model_width // 4
     sent = (far_piece.astype(F32) + got[:, :, width:].astype(F32)).astype(BF)
     far_sum = gsend(sent, 2)
     tiles = [tiles, tiles_core, tiles_x, gsend(tiles_x, 1)]
-
-    def kv_term(far):
-        return kv_own[far].astype(F32) + kv_side[far].astype(F32)
-
-    kv_grads = kv_term(0)
-    for far in range(1, pairs, 2):
-        kv_grads += fsend(kv_term(far).astype(BF), far, 0).astype(F32)
-    kv_rest = [kv_term(far).astype(BF) for far in range(2, pairs, 2)]
-    others = [joined(late[far : far + 2]) for far in range(2, pairs, 2)]
-    stage = (sides[0], late, sums_x, sent, tiles, kv_grads, kv_rest, others)
-    sides[0], late, sums_x, _, tiles, kv_grads, kv_rest, others = after(stage)
-
-    sides += [fsend(two, 0, 1) for two in others]
+    terms = caption_terms(
+        slots, side_slots, place, video_counts, sample_caption, tokens, pairs
+    )
+    kv_parts = [fsend(terms[far], far, 0) for far in range(1, pairs, 2)]
+    stage = (side_two, late, sums_x, sent, tiles, kv_parts, terms)
+    side_two, late, sums_x, _, tiles, kv_parts, terms = after(stage)
+
     here = [((block, 0),) for block in late]
-    there = [((sides[far // 2], far % 2 * 2),) for far in range(pairs)]
-    known = weight_grads(tiles, here + there[:2], None, pairs)
+    there = [((side_own, 0),), ((side_two, 0),), ((side_two, 2),)]
+    there += [((fsend(block, 0, 1), 0),) for block in late[3:]]
+    known = weight_grads(tiles, here + there[:3], None, pairs)
     total = own.astype(F32) + got[:, :, :width].astype(F32) + far_sum.astype(F32)
     row_sums = (row_sums + sums_x) / model_width
     video = quarter(video_states, g, 1).astype(F32)
@@ -848,12 +868,13 @@
         quarter(out_grad, g, 1).astype(F32)
         + inverse * (total[1] - row_sums[:, 0:1] - video_hat * row_sums[:, 1:2])
     ).astype(BF)
-    for far in range(2, pairs, 2):
-        kv_grads += fsend(kv_rest[far // 2 - 1], far, 0).astype(F32)
-    kv_grads = kv_grads.astype(BF)[None]
+    kv_parts += [fsend(terms[far], far, 0) for far in range(2, pairs, 2)]
+    kv_grads = (terms[0] + sum(p.astype(F32) for p in kv_parts)).astype(BF)[None]
     key_grad = kv_grads[:, :, :width_local]
     value_grad = kv_grads[:, :, width_local:]
-    query_grad, out_weight_grad = weight_grads(tiles, [None] * (pairs + 2) + there[2:], known, pairs)
+    query_grad, out_weight_grad = weight_grads(
+        tiles, [None] * (pairs + 3) + there[3:], known, pairs
+    )
     return (updated, input_grad, query_grad, out_weight_grad, key_grad, value_grad)
 
 

time: 212 us -> 196 us (0.925)
  waiting for transfers between devices: 103 us -> 69.2 us
  starting transfers between devices: 50.4 us -> 64.2 us
  Pallas kernels: 31 us -> 38.2 us
  local copies, waits for them, and re-layouts: 12.4 us -> 9.17 us
    ppermute x35 -> x36, waiting for transfers between devices: 88 us -> 55.3 us  [fsend(): return lax.ppermute(block, 'fsdp', perm)]
    ppermute x35 -> x36, starting transfers between devices: 43.8 us -> 56.5 us  [fsend(): return lax.ppermute(block, 'fsdp', perm)]
    pallas_call x1, Pallas kernels: 2.95 us -> 7.96 us  [project_text(): pl.pallas_call(body, grid=(steps,), out_shape=shaped((rows, 3 * width)),...]
    unnamed x63 -> x73, local copies, waits for them, and re-layouts: 11.5 us -> 7.21 us
    pallas_call x1, Pallas kernels: 4.43 us -> 7.14 us  [attend_text(): pl.pallas_call(body, grid=(steps,), out_shape=[shaped((rows // 2, depth))...]
    pallas_call x8 -> x9, Pallas kernels: 23.6 us -> 23.1 us  [call(): pl.pallas_call(body, out_shape=out_shape, in_specs=specs, out_specs=jax.t...]
  transfers between devices with their start and end apart: 47 -> 48, of which waited for: 18 -> 18; matrix products, arithmetic and copies ran while one was open for 7% -> 7% of each run, Pallas kernels for 13% -> 20%
where the time goes in v6:
time: 196 us; the launch traced here: 195 us
  waiting for transfers between devices  69.2 us (35%)
  starting transfers between devices  64.2 us (33%)
  Pallas kernels  38.2 us (19%)
  other arithmetic  13.5 us (7%)
  local copies, waits for them, and re-layouts  9.17 us (5%)
    ppermute x36, starting transfers between devices, fsend(): return lax.ppermute(block, 'fsdp', perm)  56.5 us
    ppermute x36, waiting for transfers between devices, fsend(): return lax.ppermute(block, 'fsdp', perm)  55.3 us
    pallas_call x9, Pallas kernels, call(): pl.pallas_call(body, out_shape=out_shape, in_specs=specs, out_specs=jax.t...  23.1 us
    ppermute x12, waiting for transfers between devices, gsend(): lax.ppermute(block, 'grp', [(s, s ^ flip) for s in range(lax.axis_size('g...  13.9 us
    pallas_call x1, Pallas kernels, project_text(): pl.pallas_call(body, grid=(steps,), out_shape=shaped((rows, 3 * width)),...  7.96 us
    ppermute x12, starting transfers between devices, gsend(): lax.ppermute(block, 'grp', [(s, s ^ flip) for s in range(lax.axis_size('g...  7.73 us
    unnamed x73, local copies, waits for them, and re-layouts  7.21 us
    pallas_call x1, Pallas kernels, attend_text(): pl.pallas_call(body, grid=(steps,), out_shape=[shaped((rows // 2, depth))...  7.14 us
  transfers between devices with their start and end apart: 48, of which 18 were waited for; matrix products, arithmetic and copies ran while one was open for 7% of the time, Pallas kernels for 20%

profile of v6, /device:TPU:0, one launch (start us, length us, event | category | flops | bytes accessed | tf_op | source)
XLA Modules:
  0.0 195.4 jit_solution(15087835207361819162)
XLA Ops:
  0.6 3.0 %collective-permute-start.2 = (bf16[512,384]{1,0:T(8,128)(2,1)}, bf16[512,384]{1,0:T(8,128)(2,1)S(1)}, u32[]{:S(2)}, u32[]{:S(2)}) collective-permute-start(bf16[512,384]{1,0:T(8,128)(2,1)} %refs_4_.1), channel_id=1, source_target_pairs={{0,1},{1,0},{2,3},{3,2},{4,5},{5,4},{6,7},{7,6},{8,9},{9,8},{10,11... | collective-permute-start | bytes 1179656 | tf_op jit(solution)/shard_map/ppermute | solution.py:40
  3.7 2.0 %collective-permute-start = (bf16[384,384]{1,0:T(8,128)(2,1)}, bf16[384,384]{1,0:T(8,128)(2,1)}, u32[]{:S(2)}, u32[]{:S(2)}) collective-permute-start(bf16[384,384]{1,0:T(8,128)(2,1)} %refs_0_.3), channel_id=1, source_target_pairs={{0,2},{1,3},{2,4},{3,5},{4,6},{5,7},{6,0},{7,1},{8,10},{9,11},{10,... | collective-permute-start | bytes 884744 | tf_op jit(solution)/shard_map/ppermute | solution.py:40
  5.7 1.6 collective-permute-start.1
  7.3 8.0 %shard_map.208.qkv_ref = bf16[128,1536]{1,0:T(8,128)(2,1)} custom-call(bf16[128,4096]{1,0:T(8,128)(2,1)} %bitcast.39, f32[1,4096]{1,0:T(1,128)} %bitcast.53, bf16[4096,512]{1,0:T(8,128)(2,1)} %wq_ref.1, bf16[4096,512]{1,0:T(8,128)(2,1)} %wk_ref.1, bf16[4096,512]{1,0:T(8,128)(2,1)} %wv_ref.1), custom_call_target="tpu_custom_call" | custom-call | flops 1 | bytes 1 | tf_op jit(solution)/shard_map/pallas_call | solution.py:350
  15.9 7.1 %shard_map.209 = (bf16[64,4096]{1,0:T(8,128)(2,1)}, bf16[64,4096]{1,0:T(8,128)(2,1)}) custom-call(s32[3]{0:T(128)} %pad_add_fusion.place_ref, s32[8]{0:T(128)} %len_ref.3, bf16[128,1536]{1,0:T(8,128)(2,1)} %shard_map.208.qkv_ref, f32[8,128,128]{2,1,0:T(8,128)} %bias_ref.1, bf16[512,4096]{1,0:T(8,128)(2,1)} %out_ref.1), custom_call_target="tpu_custom_call" | custom-call | flops 1 | bytes 1 | tf_op jit(solution)/shard_map/pallas_call | solution.py:394
  23.9 1.0 constant_dynamic-update-slice_fusion.1
  25.0 1.1 constant_dynamic-update-slice_fusion.refs_3_
  26.1 1.6 collective-permute-start.9
  27.7 1.2 pad_maximum_fusion
  28.9 1.6 collective-permute-start.13
  30.6 1.6 collective-permute-start.5
  32.1 2.7 %shard_map.210 = (bf16[256,3072]{1,0:T(8,128)(2,1)S(1)}, f32[256,1]{1,0:T(8,128)S(1)}, f32[256,1]{1,0:T(8,128)S(1)}, bf16[4,2,64,384]{3,2,1,0:T(8,128)(2,1)S(1)}, bf16[4,2,64,384]{3,2,1,0:T(8,128)(2,1)S(1)}) custom-call(s32[3]{0:T(128)S(1)} %copy-done.30, bf16[256,3072]{1,0:T(8,128)(2,1)S(1)} %copy-done.6, bf16[256,3072]{1,0:T(8,128)(2,1)S(1)} %copy-done), custom_call_target="tpu_custom_call" | custom-call | flops 1 | bytes 1 | tf_op jit(solution)/shard_map/pallas_call | solution.py:307
  35.5 3.2 %collective-permute-done.5.far_ref = bf16[32,4096]{1,0:T(8,128)(2,1)S(1)} collective-permute-done((bf16[32,4096]{1,0:T(8,128)(2,1)S(1)}, bf16[32,4096]{1,0:T(8,128)(2,1)S(1)}, u32[]{:S(2)}, u32[]{:S(2)}) %collective-permute-start.5) | collective-permute-done | bytes 262176 | tf_op jit(solution)/shard_map/ppermute | solution.py:44
  39.6 2.3 %collective-permute-start.8 = (bf16[32,1024]{1,0:T(8,128)(2,1)S(1)}, bf16[32,1024]{1,0:T(8,128)(2,1)S(1)}, u32[]{:S(2)}, u32[]{:S(2)}) collective-permute-start(bf16[32,1024]{1,0:T(8,128)(2,1)S(1)} %get-tuple-element.99), channel_id=1, source_target_pairs={{0,6},{1,7},{2,0},{3,1},{4,2},{5,3},{6,4},{7,5},{8,14},{9,15},{10,... | collective-permute-start | bytes 196616 | tf_op jit(solution)/shard_map/ppermute | solution.py:40
  41.9 1.0 collective-permute-start.6
  42.9 2.1 %collective-permute-done.8 = bf16[32,1024]{1,0:T(8,128)(2,1)S(1)} collective-permute-done((bf16[32,1024]{1,0:T(8,128)(2,1)S(1)}, bf16[32,1024]{1,0:T(8,128)(2,1)S(1)}, u32[]{:S(2)}, u32[]{:S(2)}) %collective-permute-start.8) | collective-permute-done | bytes 65568 | tf_op jit(solution)/shard_map/ppermute | solution.py:40
  45.1 4.2 %collective-permute-done.7 = bf16[32,1024]{1,0:T(8,128)(2,1)S(1)} collective-permute-done((bf16[32,1024]{1,0:T(8,128)(2,1)S(1)}, bf16[32,1024]{1,0:T(8,128)(2,1)S(1)}, u32[]{:S(2)}, u32[]{:S(2)}) %collective-permute-start.7) | collective-permute-done | bytes 65568 | tf_op jit(solution)/shard_map/ppermute | solution.py:40
  49.4 1.6 collective-permute-start.11
  50.9 6.6 %collective-permute-done.11.refs_2_ = bf16[4,32,1024]{2,1,0:T(8,128)(2,1)S(1)} collective-permute-done((bf16[4,32,1024]{2,1,0:T(8,128)(2,1)S(1)}, bf16[4,32,1024]{2,1,0:T(8,128)(2,1)S(1)}, u32[]{:S(2)}, u32[]{:S(2)}) %collective-permute-start.11) | collective-permute-done | bytes 262176 | tf_op jit(solution)/shard_map/ppermute | solution.py:44
  58.1 1.6 collective-permute-start.18
  59.8 1.8 shard_map.212
  61.6 4.7 %collective-permute-done.14.refs_6_ = bf16[768,384]{1,0:T(8,128)(2,1)S(1)} collective-permute-done((bf16[768,384]{1,0:T(8,128)(2,1)S(1)}, bf16[768,384]{1,0:T(8,128)(2,1)S(1)}, u32[]{:S(2)}, u32[]{:S(2)}) %collective-permute-start.14) | collective-permute-done | bytes 589856 | tf_op jit(solution)/shard_map/ppermute | solution.py:40
  66.4 3.7 %collective-permute-start.15 = (bf16[128,768]{1,0:T(8,128)(2,1)S(1)}, bf16[128,768]{1,0:T(8,128)(2,1)S(1)}, u32[]{:S(2)}, u32[]{:S(2)}) collective-permute-start(bf16[128,768]{1,0:T(8,128)(2,1)S(1)} %get-tuple-element.108), channel_id=1, source_target_pairs={{0,6},{1,7},{2,0},{3,1},{4,2},{5,3},{6,4},{7,5},{8,14},{9,15},{10,... | collective-permute-start | bytes 589832 | tf_op jit(solution)/shard_map/ppermute | solution.py:40
  70.1 1.6 collective-permute-start.21
  71.8 4.3 %collective-permute-done.17 = bf16[128,768]{1,0:T(8,128)(2,1)S(1)} collective-permute-done((bf16[128,768]{1,0:T(8,128)(2,1)S(1)}, bf16[128,768]{1,0:T(8,128)(2,1)S(1)}, u32[]{:S(2)}, u32[]{:S(2)}) %collective-permute-start.17) | collective-permute-done | bytes 196640 | tf_op jit(solution)/shard_map/ppermute | solution.py:40
  76.1 1.6 collective-permute-start.20
  77.7 4.9 %collective-permute-done.16 = bf16[128,768]{1,0:T(8,128)(2,1)S(1)} collective-permute-done((bf16[128,768]{1,0:T(8,128)(2,1)S(1)}, bf16[128,768]{1,0:T(8,128)(2,1)S(1)}, u32[]{:S(2)}, u32[]{:S(2)}) %collective-permute-start.16) | collective-permute-done | bytes 196640 | tf_op jit(solution)/shard_map/ppermute | solution.py:40
  82.7 5.9 %collective-permute-start.23 = (bf16[128,768]{1,0:T(8,128)(2,1)S(1)}, bf16[128,768]{1,0:T(8,128)(2,1)S(1)}, u32[]{:S(2)}, u32[]{:S(2)}) collective-permute-start(bf16[128,768]{1,0:T(8,128)(2,1)S(1)} %add_convert_fusion.3.refs_0_), channel_id=1, source_target_pairs={{0,2},{1,3},{2,4},{3,5},{4,6},{5,7},{6,0},{7,1},{8,10},{9,11},{10,... | collective-permute-start | bytes 589832 | tf_op jit(solution)/shard_map/ppermute | solution.py:40
  88.6 2.4 %collective-permute-start.26 = (bf16[128,768]{1,0:T(8,128)(2,1)S(1)}, bf16[128,768]{1,0:T(8,128)(2,1)S(1)}, u32[]{:S(2)}, u32[]{:S(2)}) collective-permute-start(bf16[128,768]{1,0:T(8,128)(2,1)S(1)} %add_convert_fusion.3.refs_0_), channel_id=1, source_target_pairs={{0,6},{1,7},{2,0},{3,1},{4,2},{5,3},{6,4},{7,5},{8,14},{9,15},{10,... | collective-permute-start | bytes 589832 | tf_op jit(solution)/shard_map/ppermute | solution.py:40
  91.1 1.8 collective-permute-start.22
  92.8 1.2 collective-permute-done.23.refs_2_
  94.0 1.8 collective-permute-start.24
  95.8 3.4 %collective-permute-done.19.refs_4_ = bf16[128,768]{1,0:T(8,128)(2,1)S(1)} collective-permute-done((bf16[128,768]{1,0:T(8,128)(2,1)S(1)}, bf16[128,768]{1,0:T(8,128)(2,1)S(1)}, u32[]{:S(2)}, u32[]{:S(2)}) %collective-permute-start.19) | collective-permute-done | bytes 196640 | tf_op jit(solution)/shard_map/ppermute | solution.py:40
  99.2 1.8 collective-permute-start.25
  101.3 3.9 %collective-permute-start.28 = (bf16[2,2,64,384]{3,2,1,0:T(8,128)(2,1)S(1)}, bf16[2,2,64,384]{3,2,1,0:T(8,128)(2,1)S(1)}, u32[]{:S(2)}, u32[]{:S(2)}) collective-permute-start(bf16[2,2,64,384]{3,2,1,0:T(8,128)(2,1)S(1)} %get-tuple-element.123), channel_id=1, source_target_pairs={{0,2},{1,3},{2,4},{3,5},{4,6},{5,7},{6,0},{7,1},{8,10},{9,11},{10,... | collective-permute-start | bytes 589832 | tf_op jit(solution)/shard_map/ppermute | solution.py:40
  105.2 3.1 %collective-permute-start.29 = (bf16[2,2,64,384]{3,2,1,0:T(8,128)(2,1)S(1)}, bf16[2,2,64,384]{3,2,1,0:T(8,128)(2,1)S(1)}, u32[]{:S(2)}, u32[]{:S(2)}) collective-permute-start(bf16[2,2,64,384]{3,2,1,0:T(8,128)(2,1)S(1)} %get-tuple-element.124), channel_id=1, source_target_pairs={{0,4},{1,5},{2,6},{3,7},{4,0},{5,1},{6,2},{7,3},{8,12},{9,13},{10,... | collective-permute-start | bytes 589832 | tf_op jit(solution)/shard_map/ppermute | solution.py:40
  108.3 1.3 collective-permute-start.30
  109.6 2.8 %shard_map.213 = (bf16[256,384]{1,0:T(8,128)(2,1)S(1)}, bf16[256,384]{1,0:T(8,128)(2,1)S(1)}, f32[1,384]{1,0:T(1,128)S(1)}) custom-call(s32[3]{0:T(128)S(1)} %copy-done.30, bf16[256,3072]{1,0:T(8,128)(2,1)S(1)} %get-tuple-element.94.normed_ref, bf16[256,3072]{1,0:T(8,128)(2,1)S(1)} %copy-done, bf16[384,384]{1,0:T(8,128)(2,1)S(1)} %copy-done.4, ...), custom_call_target="tpu_custom_call" | custom-call | flops 1 | bytes 1 | tf_op jit(solution)/shard_map/pallas_call | solution.py:307
  112.5 2.8 %shard_map.214 = (bf16[2,256,384]{2,1,0:T(8,128)(2,1)S(1)}, bf16[256,384]{1,0:T(8,128)(2,1)S(1)}, bf16[256,384]{1,0:T(8,128)(2,1)S(1)}, f32[256,2]{1,0:T(8,128)S(1)}, bf16[3,128,768]{2,1,0:T(8,128)(2,1)S(1)}) custom-call(s32[3]{0:T(128)S(1)} %copy-done.30, s32[8]{0:T(128)S(1)} %copy-done.32, s32[8]{0:T(128)S(1)} %copy-done.33, s32[8]{0:T(128)S(1)} %copy-done.34, ...), custom_call_target="tpu_custom_call" | custom-call | flops 1 | bytes 1 | tf_op jit(solution)/shard_map/pallas_call | solution.py:307
  115.3 2.8 %collective-permute-done.29 = bf16[2,2,64,384]{3,2,1,0:T(8,128)(2,1)S(1)} collective-permute-done((bf16[2,2,64,384]{3,2,1,0:T(8,128)(2,1)S(1)}, bf16[2,2,64,384]{3,2,1,0:T(8,128)(2,1)S(1)}, u32[]{:S(2)}, u32[]{:S(2)}) %collective-permute-start.29) | collective-permute-done | bytes 196640 | tf_op jit(solution)/shard_map/ppermute | solution.py:40
  118.2 4.7 %collective-permute-start.34 = (bf16[2,256,384]{2,1,0:T(8,128)(2,1)S(1)}, bf16[2,256,384]{2,1,0:T(8,128)(2,1)S(1)}, u32[]{:S(2)}, u32[]{:S(2)}) collective-permute-start(bf16[2,256,384]{2,1,0:T(8,128)(2,1)S(1)} %get-tuple-element.158.refs_4_), channel_id=1, source_target_pairs={{0,2},{1,3},{2,4},{3,5},{4,6},{5,7},{6,0},{7,1},{8,10},{9,11},{10,... | collective-permute-start | bytes 1179656 | tf_op jit(solution)/shard_map/ppermute | solution.py:40
  123.0 1.6 collective-permute-start.36
  125.0 9.4 %collective-permute-done.34.refs_5_ = bf16[2,256,384]{2,1,0:T(8,128)(2,1)S(1)} collective-permute-done((bf16[2,256,384]{2,1,0:T(8,128)(2,1)S(1)}, bf16[2,256,384]{2,1,0:T(8,128)(2,1)S(1)}, u32[]{:S(2)}, u32[]{:S(2)}) %collective-permute-start.34) | collective-permute-done | bytes 393248 | tf_op jit(solution)/shard_map/ppermute | solution.py:40
  134.8 5.5 %shard_map.215 = (bf16[2,256,768]{2,1,0:T(8,128)(2,1)S(1)}, bf16[2,256,768]{2,1,0:T(8,128)(2,1)S(1)}, bf16[2,256,1536]{2,1,0:T(8,128)(2,1)}) custom-call(s32[3]{0:T(128)S(1)} %copy-done.30, bf16[256,384]{1,0:T(8,128)(2,1)S(1)} %get-tuple-element.131.att_ref, bf16[256,384]{1,0:T(8,128)(2,1)S(1)} %get-tuple-element.132.dq_ref, bf16[384,384]{1,0:T(8,128)(2,1)S(1)} %copy-done.4, ...), custom_call_target="tpu_custom_call" | custom-call | flops 1 | bytes 1 | tf_op jit(solution)/shard_map/pallas_call | solution.py:307
  140.3 6.9 %collective-permute-done.35.refs_6_ = bf16[2,256,384]{2,1,0:T(8,128)(2,1)} collective-permute-done((bf16[2,256,384]{2,1,0:T(8,128)(2,1)S(1)}, bf16[2,256,384]{2,1,0:T(8,128)(2,1)}, u32[]{:S(2)}, u32[]{:S(2)}) %collective-permute-start.35) | collective-permute-done | bytes 393248 | tf_op jit(solution)/shard_map/ppermute | solution.py:40
  147.2 2.0 %pad_maximum_fusion.2 = bf16[2,2,256,384]{3,2,1,0:T(8,128)(2,1)} fusion(bf16[1,2,256,384]{3,2,1,0:T(8,128)(2,1)} %bitcast.21, bf16[1,2,256,384]{3,2,1,0:T(8,128)(2,1)S(1)} %bitcast.41), kind=kLoop, calls=%fused_computation.22 | loop fusion | flops 393216 | bytes 1572864 | tf_op jit(solution)/shard_map/stack | solution.py:828
  152.4 3.7 %collective-permute-done.42.refs_1_ = bf16[4,2,2,64,384]{4,3,2,1,0:T(8,128)(2,1)S(1)} collective-permute-done((bf16[4,2,2,64,384]{4,3,2,1,0:T(8,128)(2,1)S(1)}, bf16[4,2,2,64,384]{4,3,2,1,0:T(8,128)(2,1)S(1)}, u32[]{:S(2)}, u32[]{:S(2)}) %collective-permute-start.42) | collective-permute-done | bytes 786464 | tf_op jit(solution)/shard_map/ppermute | solution.py:44
  157.0 1.5 collective-permute-start.41
  158.5 1.0 reduce.2
  159.5 1.6 reduce
  161.2 1.1 copy-done.15
  162.2 1.1 copy-done.17
  163.3 1.0 shard_map.216
  164.4 3.8 %collective-permute-start.45 = (bf16[128,768]{1,0:T(8,128)(2,1)S(1)}, bf16[128,768]{1,0:T(8,128)(2,1)S(1)}, u32[]{:S(2)}, u32[]{:S(2)}) collective-permute-start(bf16[128,768]{1,0:T(8,128)(2,1)S(1)} %get-tuple-element.149), channel_id=1, source_target_pairs={{0,6},{1,7},{2,0},{3,1},{4,2},{5,3},{6,4},{7,5},{8,14},{9,15},{10,... | collective-permute-start | bytes 589832 | tf_op jit(solution)/shard_map/ppermute | solution.py:40
  168.2 1.3 add_convert_fusion
  169.6 4.5 %collective-permute-done.44 = bf16[128,768]{1,0:T(8,128)(2,1)S(1)} collective-permute-done((bf16[128,768]{1,0:T(8,128)(2,1)S(1)}, bf16[128,768]{1,0:T(8,128)(2,1)S(1)}, u32[]{:S(2)}, u32[]{:S(2)}) %collective-permute-start.44) | collective-permute-done | bytes 196640 | tf_op jit(solution)/shard_map/ppermute | solution.py:40
  174.6 1.0 collective-permute-done.45
  175.6 2.4 %collective-permute-start.47 = (bf16[128,768]{1,0:T(8,128)(2,1)S(1)}, bf16[128,768]{1,0:T(8,128)(2,1)S(1)}, u32[]{:S(2)}, u32[]{:S(2)}) collective-permute-start(bf16[128,768]{1,0:T(8,128)(2,1)S(1)} %get-tuple-element.171), channel_id=1, source_target_pairs={{0,4},{1,5},{2,6},{3,7},{4,0},{5,1},{6,2},{7,3},{8,12},{9,13},{10,... | collective-permute-start | bytes 589832 | tf_op jit(solution)/shard_map/ppermute | solution.py:40
  179.1 3.1 %shard_map.217 = (f32[384,384]{1,0:T(8,128)S(1)}, f32[384,384]{1,0:T(8,128)S(1)}) custom-call(bf16[4,2,2,64,384]{4,3,2,1,0:T(8,128)(2,1)S(1)} %pad_maximum_fusion.1.refs_0_, bf16[4,2,2,64,384]{4,3,2,1,0:T(8,128)(2,1)S(1)} %copy-done.3, bf16[4,2,2,64,384]{4,3,2,1,0:T(8,128)(2,1)S(1)} %collective-permute-done.36.refs_2_, ...), custom_call_target="tpu_custom_call" | custom-call | flops 1 | bytes 1 | tf_op jit(solution)/shard_map/pallas_call | solution.py:307
  182.4 4.1 %collective-permute-done.47 = bf16[128,768]{1,0:T(8,128)(2,1)S(1)} collective-permute-done((bf16[128,768]{1,0:T(8,128)(2,1)S(1)}, bf16[128,768]{1,0:T(8,128)(2,1)S(1)}, u32[]{:S(2)}, u32[]{:S(2)}) %collective-permute-start.47) | collective-permute-done | bytes 196640 | tf_op jit(solution)/shard_map/ppermute | solution.py:40
  187.3 1.7 collective-permute-done.46.refs_6_
  189.0 2.5 %shard_map.218 = (f32[384,384]{1,0:T(8,128)}, f32[384,384]{1,0:T(8,128)}) custom-call(bf16[4,2,2,64,384]{4,3,2,1,0:T(8,128)(2,1)S(1)} %pad_maximum_fusion.1.refs_0_, bf16[4,2,2,64,384]{4,3,2,1,0:T(8,128)(2,1)S(1)} %copy-done.3, bf16[4,2,2,64,384]{4,3,2,1,0:T(8,128)(2,1)S(1)} %collective-permute-done.36.refs_2_, ...), custom_call_target="tpu_custom_call" | custom-call | flops 1 | bytes 1 | tf_op jit(solution)/shard_map/pallas_call | solution.py:307
  191.8 1.4 convert_add_fusion
  193.2 2.2 %fusion.6 = (bf16[256,768]{1,0:T(8,128)(2,1)}, bf16[256,768]{1,0:T(8,128)(2,1)}) fusion(f32[2,256,768]{2,1,0:T(8,128)S(1)} %convert_add_fusion, f32[256]{0:T(256)S(1)} %get-tuple-element.173, f32[256]{0:T(256)S(1)} %reduce.2, f32[256]{0:T(256)S(1)} %get-tuple-element.172, f32[256]{0:T(256)S(1)} %copy-done.35, bf16[256,3072]{1,0:T(8,128)(2,1)S(1)} %copy-done, ...), kind=kLoop, calls=%fused_computation.17 | loop fusion | flops 2359296 | bytes 3149828 | tf_op jit(solution)/shard_map/convert_element_type | solution.py:870
  (135 shorter events, 12.5 us)
Async XLA Ops:
  0.6 22.5 %collective-permute-start.2 = (bf16[512,384]{1,0:T(8,128)(2,1)}, bf16[512,384]{1,0:T(8,128)(2,1)S(1)}, u32[]{:S(2)}, u32[]{:S(2)}) collective-permute-start(bf16[512,384]{1,0:T(8,128)(2,1)} %refs_4_.1), channel_id=1, source_target_pairs={{0,1},{1,0},{2,3},{3,2},{4,5},{5,4},{6,7},{7,6},{8,9},{9,8},{10,11... | collective-permute-start | bytes 1179656 | tf_op jit(solution)/shard_map/ppermute | solution.py:40
  3.7 19.5 %collective-permute-start.3 = (bf16[512,384]{1,0:T(8,128)(2,1)}, bf16[512,384]{1,0:T(8,128)(2,1)S(1)}, u32[]{:S(2)}, u32[]{:S(2)}) collective-permute-start(bf16[512,384]{1,0:T(8,128)(2,1)} %refs_5_.1), channel_id=1, source_target_pairs={{0,1},{1,0},{2,3},{3,2},{4,5},{5,4},{6,7},{7,6},{8,9},{9,8},{10,11... | collective-permute-start | bytes 1179656 | tf_op jit(solution)/shard_map/ppermute | solution.py:40
  3.7 19.3 %collective-permute-start = (bf16[384,384]{1,0:T(8,128)(2,1)}, bf16[384,384]{1,0:T(8,128)(2,1)}, u32[]{:S(2)}, u32[]{:S(2)}) collective-permute-start(bf16[384,384]{1,0:T(8,128)(2,1)} %refs_0_.3), channel_id=1, source_target_pairs={{0,2},{1,3},{2,4},{3,5},{4,6},{5,7},{6,0},{7,1},{8,10},{9,11},{10,... | collective-permute-start | bytes 884744 | tf_op jit(solution)/shard_map/ppermute | solution.py:40
  5.7 17.3 %collective-permute-start.1 = (bf16[384,384]{1,0:T(8,128)(2,1)}, bf16[384,384]{1,0:T(8,128)(2,1)}, u32[]{:S(2)}, u32[]{:S(2)}) collective-permute-start(bf16[384,384]{1,0:T(8,128)(2,1)} %refs_1_.3), channel_id=1, source_target_pairs={{0,2},{1,3},{2,4},{3,5},{4,6},{5,7},{6,0},{7,1},{8,10},{9,11},{10,... | collective-permute-start | bytes 884744 | tf_op jit(solution)/shard_map/ppermute | solution.py:40
  15.9 11.8 %copy-start.4 = (bf16[384,384]{1,0:T(8,128)(2,1)S(1)}, bf16[384,384]{1,0:T(8,128)(2,1)}, u32[]{:S(2)}) copy-start(bf16[384,384]{1,0:T(8,128)(2,1)} %refs_0_.3) | copy-start | bytes 884740
  15.9 11.8 %copy-start.5 = (bf16[384,384]{1,0:T(8,128)(2,1)S(1)}, bf16[384,384]{1,0:T(8,128)(2,1)}, u32[]{:S(2)}) copy-start(bf16[384,384]{1,0:T(8,128)(2,1)} %refs_1_.3) | copy-start | bytes 884740
  23.9 6.5 %collective-permute-start.4 = (bf16[64,4096]{1,0:T(8,128)(2,1)}, bf16[64,4096]{1,0:T(8,128)(2,1)S(1)}, u32[]{:S(2)}, u32[]{:S(2)}) collective-permute-start(bf16[64,4096]{1,0:T(8,128)(2,1)} %get-tuple-element.92), channel_id=1, source_target_pairs={{0,8},{8,0},{16,24},{24,16},{1,9},{9,1},{17,25},{25,17},{2,10},{10... | collective-permute-start | bytes 1572872 | tf_op jit(solution)/shard_map/ppermute | solution.py:44
  26.1 23.3 %collective-permute-start.9 = (bf16[768,384]{1,0:T(8,128)(2,1)S(1)}, bf16[768,384]{1,0:T(8,128)(2,1)S(1)}, u32[]{:S(2)}, u32[]{:S(2)}) collective-permute-start(bf16[768,384]{1,0:T(8,128)(2,1)S(1)} %constant_dynamic-update-slice_fusion.refs_3_), channel_id=1, source_target_pairs={{0,2},{1,3},{2,4},{3,5},{4,6},{5,7},{6,0},{7,1},{8,10},{9,11},{10,... | collective-permute-start | bytes 1769480 | tf_op jit(solution)/shard_map/ppermute | solution.py:40
  28.9 30.8 %collective-permute-start.13 = (bf16[1536,384]{1,0:T(8,128)(2,1)S(1)}, bf16[1536,384]{1,0:T(8,128)(2,1)S(1)}, u32[]{:S(2)}, u32[]{:S(2)}) collective-permute-start(bf16[1536,384]{1,0:T(8,128)(2,1)S(1)} %pad_maximum_fusion), channel_id=1, source_target_pairs={{0,1},{1,0},{2,3},{3,2},{4,5},{5,4},{6,7},{7,6},{8,9},{9,8},{10,11... | collective-permute-start | bytes 3538952 | tf_op jit(solution)/shard_map/ppermute | solution.py:40
  30.6 8.2 %collective-permute-start.5 = (bf16[32,4096]{1,0:T(8,128)(2,1)S(1)}, bf16[32,4096]{1,0:T(8,128)(2,1)S(1)}, u32[]{:S(2)}, u32[]{:S(2)}) collective-permute-start(bf16[32,4096]{1,0:T(8,128)(2,1)S(1)} %add_convert_fusion.1), channel_id=1, source_target_pairs={{0,16},{8,24},{16,0},{24,8},{1,17},{9,25},{17,1},{25,9},{2,18},{10... | collective-permute-start | bytes 786440 | tf_op jit(solution)/shard_map/ppermute | solution.py:44
  35.5 47.2 %copy-start.28 = (f32[256,1]{1,0:T(8,128)}, f32[256,1]{1,0:T(8,128)S(1)}, u32[]{:S(2)}) copy-start(f32[256,1]{1,0:T(8,128)S(1)} %get-tuple-element.140) | copy-start | bytes 3076
  35.5 24.2 %copy-start.22 = (bf16[512,384]{1,0:T(8,128)(2,1)S(1)}, bf16[512,384]{1,0:T(8,128)(2,1)}, u32[]{:S(2)}) copy-start(bf16[512,384]{1,0:T(8,128)(2,1)} %refs_4_.1) | copy-start | bytes 1179652
  35.5 24.2 %copy-start.23 = (bf16[512,384]{1,0:T(8,128)(2,1)S(1)}, bf16[512,384]{1,0:T(8,128)(2,1)}, u32[]{:S(2)}) copy-start(bf16[512,384]{1,0:T(8,128)(2,1)} %refs_5_.1) | copy-start | bytes 1179652
  35.5 24.2 %copy-start.25 = (bf16[512,384]{1,0:T(8,128)(2,1)S(1)}, bf16[512,384]{1,0:T(8,128)(2,1)}, u32[]{:S(2)}) copy-start(bf16[512,384]{1,0:T(8,128)(2,1)} %copy-done.24) | copy-start | bytes 1179652
  35.5 24.2 %copy-start.27 = (bf16[512,384]{1,0:T(8,128)(2,1)S(1)}, bf16[512,384]{1,0:T(8,128)(2,1)}, u32[]{:S(2)}) copy-start(bf16[512,384]{1,0:T(8,128)(2,1)} %copy-done.26) | copy-start | bytes 1179652
  39.6 5.4 %collective-permute-start.8 = (bf16[32,1024]{1,0:T(8,128)(2,1)S(1)}, bf16[32,1024]{1,0:T(8,128)(2,1)S(1)}, u32[]{:S(2)}, u32[]{:S(2)}) collective-permute-start(bf16[32,1024]{1,0:T(8,128)(2,1)S(1)} %get-tuple-element.99), channel_id=1, source_target_pairs={{0,6},{1,7},{2,0},{3,1},{4,2},{5,3},{6,4},{7,5},{8,14},{9,15},{10,... | collective-permute-start | bytes 196616 | tf_op jit(solution)/shard_map/ppermute | solution.py:40
  41.9 7.4 %collective-permute-start.7 = (bf16[32,1024]{1,0:T(8,128)(2,1)S(1)}, bf16[32,1024]{1,0:T(8,128)(2,1)S(1)}, u32[]{:S(2)}, u32[]{:S(2)}) collective-permute-start(bf16[32,1024]{1,0:T(8,128)(2,1)S(1)} %get-tuple-element.98), channel_id=1, source_target_pairs={{0,4},{1,5},{2,6},{3,7},{4,0},{5,1},{6,2},{7,3},{8,12},{9,13},{10,... | collective-permute-start | bytes 196616 | tf_op jit(solution)/shard_map/ppermute | solution.py:40
  41.9 7.4 %collective-permute-start.6 = (bf16[32,1024]{1,0:T(8,128)(2,1)S(1)}, bf16[32,1024]{1,0:T(8,128)(2,1)S(1)}, u32[]{:S(2)}, u32[]{:S(2)}) collective-permute-start(bf16[32,1024]{1,0:T(8,128)(2,1)S(1)} %get-tuple-element.97), channel_id=1, source_target_pairs={{0,2},{1,3},{2,4},{3,5},{4,6},{5,7},{6,0},{7,1},{8,10},{9,11},{10,... | collective-permute-start | bytes 196616 | tf_op jit(solution)/shard_map/ppermute | solution.py:40
  49.3 17.0 %collective-permute-start.14 = (bf16[768,384]{1,0:T(8,128)(2,1)S(1)}, bf16[768,384]{1,0:T(8,128)(2,1)S(1)}, u32[]{:S(2)}, u32[]{:S(2)}) collective-permute-start(bf16[768,384]{1,0:T(8,128)(2,1)S(1)} %collective-permute-done.9.refs_4_), channel_id=1, source_target_pairs={{0,2},{1,3},{2,4},{3,5},{4,6},{5,7},{6,0},{7,1},{8,10},{9,11},{10,... | collective-permute-start | bytes 1769480 | tf_op jit(solution)/shard_map/ppermute | solution.py:40
  49.4 8.2 %collective-permute-start.11 = (bf16[4,32,1024]{2,1,0:T(8,128)(2,1)S(1)}, bf16[4,32,1024]{2,1,0:T(8,128)(2,1)S(1)}, u32[]{:S(2)}, u32[]{:S(2)}) collective-permute-start(bf16[4,32,1024]{2,1,0:T(8,128)(2,1)S(1)} %pad_maximum_fusion.3.refs_0_), channel_id=1, source_target_pairs={{0,16},{8,24},{16,0},{24,8},{1,17},{9,25},{17,1},{25,9},{2,18},{10... | collective-permute-start | bytes 786440 | tf_op jit(solution)/shard_map/ppermute | solution.py:44
  57.6 2.1 %collective-permute-start.12 = (bf16[4,32,1024]{2,1,0:T(8,128)(2,1)S(1)}, bf16[4,32,1024]{2,1,0:T(8,128)(2,1)S(1)}, u32[]{:S(2)}, u32[]{:S(2)}) collective-permute-start(bf16[4,32,1024]{2,1,0:T(8,128)(2,1)S(1)} %collective-permute-done.11.refs_2_), channel_id=1, source_target_pairs={{0,8},{8,0},{16,24},{24,16},{1,9},{9,1},{17,25},{25,17},{2,10},{10... | collective-permute-start | bytes 786440 | tf_op jit(solution)/shard_map/ppermute | solution.py:44
  57.6 2.1 %collective-permute-start.10 = (bf16[4,32,1024]{2,1,0:T(8,128)(2,1)S(1)}, bf16[4,32,1024]{2,1,0:T(8,128)(2,1)S(1)}, u32[]{:S(2)}, u32[]{:S(2)}) collective-permute-start(bf16[4,32,1024]{2,1,0:T(8,128)(2,1)S(1)} %pad_maximum_fusion.3.refs_0_), channel_id=1, source_target_pairs={{0,8},{8,0},{16,24},{24,16},{1,9},{9,1},{17,25},{25,17},{2,10},{10... | collective-permute-start | bytes 786440 | tf_op jit(solution)/shard_map/ppermute | solution.py:44
  58.1 24.6 %collective-permute-start.18 = (bf16[768,384]{1,0:T(8,128)(2,1)S(1)}, bf16[768,384]{1,0:T(8,128)(2,1)S(1)}, u32[]{:S(2)}, u32[]{:S(2)}) collective-permute-start(bf16[768,384]{1,0:T(8,128)(2,1)S(1)} %collective-permute-done.9.refs_4_), channel_id=1, source_target_pairs={{0,1},{1,0},{2,3},{3,2},{4,5},{5,4},{6,7},{7,6},{8,9},{9,8},{10,11... | collective-permute-start | bytes 1769480 | tf_op jit(solution)/shard_map/ppermute | solution.py:40
  66.3 9.7 %collective-permute-start.17 = (bf16[128,768]{1,0:T(8,128)(2,1)S(1)}, bf16[128,768]{1,0:T(8,128)(2,1)S(1)}, u32[]{:S(2)}, u32[]{:S(2)}) collective-permute-start(bf16[128,768]{1,0:T(8,128)(2,1)S(1)} %get-tuple-element.110), channel_id=1, source_target_pairs={{0,2},{1,3},{2,4},{3,5},{4,6},{5,7},{6,0},{7,1},{8,10},{9,11},{10,... | collective-permute-start | bytes 589832 | tf_op jit(solution)/shard_map/ppermute | solution.py:40
  66.3 16.3 %collective-permute-start.16 = (bf16[128,768]{1,0:T(8,128)(2,1)S(1)}, bf16[128,768]{1,0:T(8,128)(2,1)S(1)}, u32[]{:S(2)}, u32[]{:S(2)}) collective-permute-start(bf16[128,768]{1,0:T(8,128)(2,1)S(1)} %get-tuple-element.109), channel_id=1, source_target_pairs={{0,4},{1,5},{2,6},{3,7},{4,0},{5,1},{6,2},{7,3},{8,12},{9,13},{10,... | collective-permute-start | bytes 589832 | tf_op jit(solution)/shard_map/ppermute | solution.py:40
  66.4 16.2 %collective-permute-start.15 = (bf16[128,768]{1,0:T(8,128)(2,1)S(1)}, bf16[128,768]{1,0:T(8,128)(2,1)S(1)}, u32[]{:S(2)}, u32[]{:S(2)}) collective-permute-start(bf16[128,768]{1,0:T(8,128)(2,1)S(1)} %get-tuple-element.108), channel_id=1, source_target_pairs={{0,6},{1,7},{2,0},{3,1},{4,2},{5,3},{6,4},{7,5},{8,14},{9,15},{10,... | collective-permute-start | bytes 589832 | tf_op jit(solution)/shard_map/ppermute | solution.py:40
  70.1 20.9 %collective-permute-start.21 = (bf16[4,2,64,384]{3,2,1,0:T(8,128)(2,1)S(1)}, bf16[4,2,64,384]{3,2,1,0:T(8,128)(2,1)S(1)}, u32[]{:S(2)}, u32[]{:S(2)}) collective-permute-start(bf16[4,2,64,384]{3,2,1,0:T(8,128)(2,1)S(1)} %get-tuple-element.112), channel_id=1, source_target_pairs={{0,1},{1,0},{2,3},{3,2},{4,5},{5,4},{6,7},{7,6},{8,9},{9,8},{10,11... | collective-permute-start | bytes 1179656 | tf_op jit(solution)/shard_map/ppermute | solution.py:40
  76.1 25.2 %collective-permute-start.20 = (bf16[768,384]{1,0:T(8,128)(2,1)S(1)}, bf16[768,384]{1,0:T(8,128)(2,1)S(1)}, u32[]{:S(2)}, u32[]{:S(2)}) collective-permute-start(bf16[768,384]{1,0:T(8,128)(2,1)S(1)} %collective-permute-done.14.refs_6_), channel_id=1, source_target_pairs={{0,1},{1,0},{2,3},{3,2},{4,5},{5,4},{6,7},{7,6},{8,9},{9,8},{10,11... | collective-permute-start | bytes 1769480 | tf_op jit(solution)/shard_map/ppermute | solution.py:40
  82.7 11.2 %collective-permute-start.23 = (bf16[128,768]{1,0:T(8,128)(2,1)S(1)}, bf16[128,768]{1,0:T(8,128)(2,1)S(1)}, u32[]{:S(2)}, u32[]{:S(2)}) collective-permute-start(bf16[128,768]{1,0:T(8,128)(2,1)S(1)} %add_convert_fusion.3.refs_0_), channel_id=1, source_target_pairs={{0,2},{1,3},{2,4},{3,5},{4,6},{5,7},{6,0},{7,1},{8,10},{9,11},{10,... | collective-permute-start | bytes 589832 | tf_op jit(solution)/shard_map/ppermute | solution.py:40
  88.6 10.6 %collective-permute-start.19 = (bf16[128,768]{1,0:T(8,128)(2,1)S(1)}, bf16[128,768]{1,0:T(8,128)(2,1)S(1)}, u32[]{:S(2)}, u32[]{:S(2)}) collective-permute-start(bf16[128,768]{1,0:T(8,128)(2,1)S(1)} %add_convert_fusion.3.refs_0_), channel_id=1, source_target_pairs={{0,4},{1,5},{2,6},{3,7},{4,0},{5,1},{6,2},{7,3},{8,12},{9,13},{10,... | collective-permute-start | bytes 589832 | tf_op jit(solution)/shard_map/ppermute | solution.py:40
  88.6 12.4 %collective-permute-start.26 = (bf16[128,768]{1,0:T(8,128)(2,1)S(1)}, bf16[128,768]{1,0:T(8,128)(2,1)S(1)}, u32[]{:S(2)}, u32[]{:S(2)}) collective-permute-start(bf16[128,768]{1,0:T(8,128)(2,1)S(1)} %add_convert_fusion.3.refs_0_), channel_id=1, source_target_pairs={{0,6},{1,7},{2,0},{3,1},{4,2},{5,3},{6,4},{7,5},{8,14},{9,15},{10,... | collective-permute-start | bytes 589832 | tf_op jit(solution)/shard_map/ppermute | solution.py:40
  91.1 14.2 %collective-permute-start.22 = (bf16[128,768]{1,0:T(8,128)(2,1)S(1)}, bf16[128,768]{1,0:T(8,128)(2,1)S(1)}, u32[]{:S(2)}, u32[]{:S(2)}) collective-permute-start(bf16[128,768]{1,0:T(8,128)(2,1)S(1)} %add_convert_fusion.3.refs_0_), channel_id=1, source_target_pairs={{0,1},{1,0},{2,3},{3,2},{4,5},{5,4},{6,7},{7,6},{8,9},{9,8},{10,11... | collective-permute-start | bytes 589832 | tf_op jit(solution)/shard_map/ppermute | solution.py:40
  94.0 14.4 %collective-permute-start.24 = (bf16[128,768]{1,0:T(8,128)(2,1)S(1)}, bf16[128,768]{1,0:T(8,128)(2,1)S(1)}, u32[]{:S(2)}, u32[]{:S(2)}) collective-permute-start(bf16[128,768]{1,0:T(8,128)(2,1)S(1)} %collective-permute-done.23.refs_2_), channel_id=1, source_target_pairs={{0,1},{1,0},{2,3},{3,2},{4,5},{5,4},{6,7},{7,6},{8,9},{9,8},{10,11... | collective-permute-start | bytes 589832 | tf_op jit(solution)/shard_map/ppermute | solution.py:40
  99.2 13.2 %collective-permute-start.25 = (bf16[128,768]{1,0:T(8,128)(2,1)S(1)}, bf16[128,768]{1,0:T(8,128)(2,1)S(1)}, u32[]{:S(2)}, u32[]{:S(2)}) collective-permute-start(bf16[128,768]{1,0:T(8,128)(2,1)S(1)} %collective-permute-done.19.refs_4_), channel_id=1, source_target_pairs={{0,1},{1,0},{2,3},{3,2},{4,5},{5,4},{6,7},{7,6},{8,9},{9,8},{10,11... | collective-permute-start | bytes 589832 | tf_op jit(solution)/shard_map/ppermute | solution.py:40
  101.0 11.5 %collective-permute-start.27 = (bf16[128,768]{1,0:T(8,128)(2,1)S(1)}, bf16[128,768]{1,0:T(8,128)(2,1)S(1)}, u32[]{:S(2)}, u32[]{:S(2)}) collective-permute-start(bf16[128,768]{1,0:T(8,128)(2,1)S(1)} %collective-permute-done.26.refs_6_), channel_id=1, source_target_pairs={{0,1},{1,0},{2,3},{3,2},{4,5},{5,4},{6,7},{7,6},{8,9},{9,8},{10,11... | collective-permute-start | bytes 589832 | tf_op jit(solution)/shard_map/ppermute | solution.py:40
  101.3 14.1 %collective-permute-start.28 = (bf16[2,2,64,384]{3,2,1,0:T(8,128)(2,1)S(1)}, bf16[2,2,64,384]{3,2,1,0:T(8,128)(2,1)S(1)}, u32[]{:S(2)}, u32[]{:S(2)}) collective-permute-start(bf16[2,2,64,384]{3,2,1,0:T(8,128)(2,1)S(1)} %get-tuple-element.123), channel_id=1, source_target_pairs={{0,2},{1,3},{2,4},{3,5},{4,6},{5,7},{6,0},{7,1},{8,10},{9,11},{10,... | collective-permute-start | bytes 589832 | tf_op jit(solution)/shard_map/ppermute | solution.py:40
  105.2 12.9 %collective-permute-start.29 = (bf16[2,2,64,384]{3,2,1,0:T(8,128)(2,1)S(1)}, bf16[2,2,64,384]{3,2,1,0:T(8,128)(2,1)S(1)}, u32[]{:S(2)}, u32[]{:S(2)}) collective-permute-start(bf16[2,2,64,384]{3,2,1,0:T(8,128)(2,1)S(1)} %get-tuple-element.124), channel_id=1, source_target_pairs={{0,4},{1,5},{2,6},{3,7},{4,0},{5,1},{6,2},{7,3},{8,12},{9,13},{10,... | collective-permute-start | bytes 589832 | tf_op jit(solution)/shard_map/ppermute | solution.py:40
  108.3 9.8 %collective-permute-start.30 = (bf16[2,2,64,384]{3,2,1,0:T(8,128)(2,1)S(1)}, bf16[2,2,64,384]{3,2,1,0:T(8,128)(2,1)S(1)}, u32[]{:S(2)}, u32[]{:S(2)}) collective-permute-start(bf16[2,2,64,384]{3,2,1,0:T(8,128)(2,1)S(1)} %get-tuple-element.125), channel_id=1, source_target_pairs={{0,6},{1,7},{2,0},{3,1},{4,2},{5,3},{6,4},{7,5},{8,14},{9,15},{10,... | collective-permute-start | bytes 589832 | tf_op jit(solution)/shard_map/ppermute | solution.py:40
  115.3 25.0 %copy-start.14 = (bf16[3,128,768]{2,1,0:T(8,128)(2,1)}, bf16[3,128,768]{2,1,0:T(8,128)(2,1)S(1)}, u32[]{:S(2)}) copy-start(bf16[3,128,768]{2,1,0:T(8,128)(2,1)S(1)} %get-tuple-element.134.own_ref) | copy-start | bytes 1769476
  115.3 25.0 %copy-start.18 = (bf16[2,256,384]{2,1,0:T(8,128)(2,1)}, bf16[2,256,384]{2,1,0:T(8,128)(2,1)S(1)}, u32[]{:S(2)}) copy-start(bf16[2,256,384]{2,1,0:T(8,128)(2,1)S(1)} %get-tuple-element.158.refs_4_) | copy-start | bytes 1179652
  118.2 4.8 %collective-permute-start.31 = (f32[256,2]{1,0:T(8,128)S(1)}, f32[256,2]{1,0:T(8,128)S(1)}, u32[]{:S(2)}, u32[]{:S(2)}) collective-permute-start(f32[256,2]{1,0:T(8,128)S(1)} %get-tuple-element.130), channel_id=1, source_target_pairs={{0,8},{8,0},{16,24},{24,16},{1,9},{9,1},{17,25},{25,17},{2,10},{10... | collective-permute-start | bytes 6152 | tf_op jit(solution)/shard_map/ppermute | solution.py:44
  118.2 16.2 %collective-permute-start.34 = (bf16[2,256,384]{2,1,0:T(8,128)(2,1)S(1)}, bf16[2,256,384]{2,1,0:T(8,128)(2,1)S(1)}, u32[]{:S(2)}, u32[]{:S(2)}) collective-permute-start(bf16[2,256,384]{2,1,0:T(8,128)(2,1)S(1)} %get-tuple-element.158.refs_4_), channel_id=1, source_target_pairs={{0,2},{1,3},{2,4},{3,5},{4,6},{5,7},{6,0},{7,1},{8,10},{9,11},{10,... | collective-permute-start | bytes 1179656 | tf_op jit(solution)/shard_map/ppermute | solution.py:40
  123.0 27.8 %collective-permute-start.36 = (bf16[4,2,2,64,384]{4,3,2,1,0:T(8,128)(2,1)S(1)}, bf16[4,2,2,64,384]{4,3,2,1,0:T(8,128)(2,1)S(1)}, u32[]{:S(2)}, u32[]{:S(2)}) collective-permute-start(bf16[4,2,2,64,384]{4,3,2,1,0:T(8,128)(2,1)S(1)} %pad_maximum_fusion.1.refs_0_), channel_id=1, source_target_pairs={{0,16},{8,24},{16,0},{24,8},{1,17},{9,25},{17,1},{25,9},{2,18},{10... | collective-permute-start | bytes 2359304 | tf_op jit(solution)/shard_map/ppermute | solution.py:44
  124.6 25.4 %collective-permute-start.32 = (bf16[3,128,768]{2,1,0:T(8,128)(2,1)S(1)}, bf16[3,128,768]{2,1,0:T(8,128)(2,1)S(1)}, u32[]{:S(2)}, u32[]{:S(2)}) collective-permute-start(bf16[3,128,768]{2,1,0:T(8,128)(2,1)S(1)} %get-tuple-element.134.own_ref), channel_id=1, source_target_pairs={{0,1},{1,0},{2,3},{3,2},{4,5},{5,4},{6,7},{7,6},{8,9},{9,8},{10,11... | collective-permute-start | bytes 1769480 | tf_op jit(solution)/shard_map/ppermute | solution.py:40
  134.3 12.9 %copy-start.7 = (bf16[2,256,384]{2,1,0:T(8,128)(2,1)}, bf16[2,256,384]{2,1,0:T(8,128)(2,1)S(1)}, u32[]{:S(2)}) copy-start(bf16[2,256,384]{2,1,0:T(8,128)(2,1)S(1)} %collective-permute-done.34.refs_5_) | copy-start | bytes 1179652
  134.3 12.9 %collective-permute-start.35 = (bf16[2,256,384]{2,1,0:T(8,128)(2,1)S(1)}, bf16[2,256,384]{2,1,0:T(8,128)(2,1)}, u32[]{:S(2)}, u32[]{:S(2)}) collective-permute-start(bf16[2,256,384]{2,1,0:T(8,128)(2,1)S(1)} %collective-permute-done.34.refs_5_), channel_id=1, source_target_pairs={{0,2},{1,3},{2,4},{3,5},{4,6},{5,7},{6,0},{7,1},{8,10},{9,11},{10,... | collective-permute-start | bytes 1179656 | tf_op jit(solution)/shard_map/ppermute | solution.py:40
  134.4 14.8 %collective-permute-start.33 = (bf16[2,256,384]{2,1,0:T(8,128)(2,1)S(1)}, bf16[2,256,384]{2,1,0:T(8,128)(2,1)S(1)}, u32[]{:S(2)}, u32[]{:S(2)}) collective-permute-start(bf16[2,256,384]{2,1,0:T(8,128)(2,1)S(1)} %get-tuple-element.158.refs_4_), channel_id=1, source_target_pairs={{0,1},{1,0},{2,3},{3,2},{4,5},{5,4},{6,7},{7,6},{8,9},{9,8},{10,11... | collective-permute-start | bytes 1179656 | tf_op jit(solution)/shard_map/ppermute | solution.py:40
  140.3 15.8 %copy-start.10 = (bf16[2,256,768]{2,1,0:T(8,128)(2,1)}, bf16[2,256,768]{2,1,0:T(8,128)(2,1)S(1)}, u32[]{:S(2)}) copy-start(bf16[2,256,768]{2,1,0:T(8,128)(2,1)S(1)} %get-tuple-element.139) | copy-start | bytes 2359300
  140.3 15.8 %copy-start.12 = (bf16[2,256,768]{2,1,0:T(8,128)(2,1)}, bf16[2,256,768]{2,1,0:T(8,128)(2,1)S(1)}, u32[]{:S(2)}) copy-start(bf16[2,256,768]{2,1,0:T(8,128)(2,1)S(1)} %get-tuple-element.133) | copy-start | bytes 2359300
  150.8 13.6 %collective-permute-start.37 = (bf16[2,256,1536]{2,1,0:T(8,128)(2,1)}, bf16[2,256,1536]{2,1,0:T(8,128)(2,1)}, u32[]{:S(2)}, u32[]{:S(2)}) collective-permute-start(bf16[2,256,1536]{2,1,0:T(8,128)(2,1)} %get-tuple-element.138), channel_id=1, source_target_pairs={{0,8},{8,0},{16,24},{24,16},{1,9},{9,1},{17,25},{25,17},{2,10},{10... | collective-permute-start | bytes 4718600 | tf_op jit(solution)/shard_map/ppermute | solution.py:44
  150.8 5.3 %collective-permute-start.42 = (bf16[4,2,2,64,384]{4,3,2,1,0:T(8,128)(2,1)S(1)}, bf16[4,2,2,64,384]{4,3,2,1,0:T(8,128)(2,1)S(1)}, u32[]{:S(2)}, u32[]{:S(2)}) collective-permute-start(bf16[4,2,2,64,384]{4,3,2,1,0:T(8,128)(2,1)S(1)} %pad_maximum_fusion.1.refs_0_), channel_id=1, source_target_pairs={{0,8},{8,0},{16,24},{24,16},{1,9},{9,1},{17,25},{25,17},{2,10},{10... | collective-permute-start | bytes 2359304 | tf_op jit(solution)/shard_map/ppermute | solution.py:44
  151.3 24.3 %collective-permute-start.39 = (bf16[4,256,384]{2,1,0:T(8,128)(2,1)}, bf16[4,256,384]{2,1,0:T(8,128)(2,1)}, u32[]{:S(2)}, u32[]{:S(2)}) collective-permute-start(bf16[4,256,384]{2,1,0:T(8,128)(2,1)} %bitcast.22), channel_id=1, source_target_pairs={{0,1},{1,0},{2,3},{3,2},{4,5},{5,4},{6,7},{7,6},{8,9},{9,8},{10,11... | collective-permute-start | bytes 2359304 | tf_op jit(solution)/shard_map/ppermute | solution.py:40
  151.6 24.0 %collective-permute-start.43 = (bf16[4,2,2,64,384]{4,3,2,1,0:T(8,128)(2,1)S(1)}, bf16[4,2,2,64,384]{4,3,2,1,0:T(8,128)(2,1)}, u32[]{:S(2)}, u32[]{:S(2)}) collective-permute-start(bf16[4,2,2,64,384]{4,3,2,1,0:T(8,128)(2,1)S(1)} %collective-permute-done.36.refs_2_), channel_id=1, source_target_pairs={{0,8},{8,0},{16,24},{24,16},{1,9},{9,1},{17,25},{25,17},{2,10},{10... | collective-permute-start | bytes 2359304 | tf_op jit(solution)/shard_map/ppermute | solution.py:44
  151.6 24.0 %collective-permute-start.40 = (bf16[2,256,384]{2,1,0:T(8,128)(2,1)}, bf16[2,256,384]{2,1,0:T(8,128)(2,1)S(1)}, u32[]{:S(2)}, u32[]{:S(2)}) collective-permute-start(bf16[2,256,384]{2,1,0:T(8,128)(2,1)} %collective-permute-done.35.refs_6_), channel_id=1, source_target_pairs={{0,2},{1,3},{2,4},{3,5},{4,6},{5,7},{6,0},{7,1},{8,10},{9,11},{10,... | collective-permute-start | bytes 1179656 | tf_op jit(solution)/shard_map/ppermute | solution.py:40
  157.0 7.3 %collective-permute-start.41 = (f32[256,2]{1,0:T(8,128)}, f32[256,2]{1,0:T(8,128)}, u32[]{:S(2)}, u32[]{:S(2)}) collective-permute-start(f32[256,2]{1,0:T(8,128)} %add.61), channel_id=1, source_target_pairs={{0,16},{8,24},{16,0},{24,8},{1,17},{9,25},{17,1},{25,9},{2,18},{10... | collective-permute-start | bytes 6152 | tf_op jit(solution)/shard_map/ppermute | solution.py:44
  164.3 14.8 %copy-start.3 = (bf16[4,2,2,64,384]{4,3,2,1,0:T(8,128)(2,1)S(1)}, bf16[4,2,2,64,384]{4,3,2,1,0:T(8,128)(2,1)}, u32[]{:S(2)}) copy-start(bf16[4,2,2,64,384]{4,3,2,1,0:T(8,128)(2,1)} %copy-done.2) | copy-start | bytes 2359300
  164.3 14.8 %copy-start.8 = (bf16[2,256,384]{2,1,0:T(8,128)(2,1)S(1)}, bf16[2,256,384]{2,1,0:T(8,128)(2,1)}, u32[]{:S(2)}) copy-start(bf16[2,256,384]{2,1,0:T(8,128)(2,1)} %copy-done.7) | copy-start | bytes 1179652
  164.3 14.8 %copy-start.19 = (bf16[2,256,384]{2,1,0:T(8,128)(2,1)S(1)}, bf16[2,256,384]{2,1,0:T(8,128)(2,1)}, u32[]{:S(2)}) copy-start(bf16[2,256,384]{2,1,0:T(8,128)(2,1)} %copy-done.18) | copy-start | bytes 1179652
  164.3 14.8 %copy-start.21 = (bf16[2,256,384]{2,1,0:T(8,128)(2,1)S(1)}, bf16[2,256,384]{2,1,0:T(8,128)(2,1)}, u32[]{:S(2)}) copy-start(bf16[2,256,384]{2,1,0:T(8,128)(2,1)} %copy-done.20) | copy-start | bytes 1179652
  164.4 9.7 %collective-permute-start.44 = (bf16[128,768]{1,0:T(8,128)(2,1)S(1)}, bf16[128,768]{1,0:T(8,128)(2,1)S(1)}, u32[]{:S(2)}, u32[]{:S(2)}) collective-permute-start(bf16[128,768]{1,0:T(8,128)(2,1)S(1)} %get-tuple-element.148), channel_id=1, source_target_pairs={{0,2},{1,3},{2,4},{3,5},{4,6},{5,7},{6,0},{7,1},{8,10},{9,11},{10,... | collective-permute-start | bytes 589832 | tf_op jit(solution)/shard_map/ppermute | solution.py:40
  164.4 11.2 %collective-permute-start.45 = (bf16[128,768]{1,0:T(8,128)(2,1)S(1)}, bf16[128,768]{1,0:T(8,128)(2,1)S(1)}, u32[]{:S(2)}, u32[]{:S(2)}) collective-permute-start(bf16[128,768]{1,0:T(8,128)(2,1)S(1)} %get-tuple-element.149), channel_id=1, source_target_pairs={{0,6},{1,7},{2,0},{3,1},{4,2},{5,3},{6,4},{7,5},{8,14},{9,15},{10,... | collective-permute-start | bytes 589832 | tf_op jit(solution)/shard_map/ppermute | solution.py:40
  174.0 17.8 %collective-permute-start.38 = (bf16[2,256,768]{2,1,0:T(8,128)(2,1)S(1)}, bf16[2,256,768]{2,1,0:T(8,128)(2,1)S(1)}, u32[]{:S(2)}, u32[]{:S(2)}) collective-permute-start(bf16[2,256,768]{2,1,0:T(8,128)(2,1)S(1)} %add_convert_fusion), channel_id=1, source_target_pairs={{0,16},{8,24},{16,0},{24,8},{1,17},{9,25},{17,1},{25,9},{2,18},{10... | collective-permute-start | bytes 2359304 | tf_op jit(solution)/shard_map/ppermute | solution.py:44
  175.6 10.9 %collective-permute-start.47 = (bf16[128,768]{1,0:T(8,128)(2,1)S(1)}, bf16[128,768]{1,0:T(8,128)(2,1)S(1)}, u32[]{:S(2)}, u32[]{:S(2)}) collective-permute-start(bf16[128,768]{1,0:T(8,128)(2,1)S(1)} %get-tuple-element.171), channel_id=1, source_target_pairs={{0,4},{1,5},{2,6},{3,7},{4,0},{5,1},{6,2},{7,3},{8,12},{9,13},{10,... | collective-permute-start | bytes 589832 | tf_op jit(solution)/shard_map/ppermute | solution.py:40
  179.0 10.0 %collective-permute-start.46 = (bf16[2,256,384]{2,1,0:T(8,128)(2,1)S(1)}, bf16[2,256,384]{2,1,0:T(8,128)(2,1)S(1)}, u32[]{:S(2)}, u32[]{:S(2)}) collective-permute-start(bf16[2,256,384]{2,1,0:T(8,128)(2,1)S(1)} %collective-permute-done.40.refs_7_), channel_id=1, source_target_pairs={{0,1},{1,0},{2,3},{3,2},{4,5},{5,4},{6,7},{7,6},{8,9},{9,8},{10,11... | collective-permute-start | bytes 1179656 | tf_op jit(solution)/shard_map/ppermute | solution.py:40
  (20 other events, 80.2 us)

commit v7 on v6

--- a/solution.py
+++ b/solution.py
@@ -323,38 +323,41 @@
     return pl.multiple_of(start, unit)
 
 
-def project_text(states, gain, weights, steps=4):
+def project_text(states, gain, weights, steps=8):
     rows, depth = states.shape
     width = weights[0].shape[1]
     chunk = depth // steps
 
-    def body(states_ref, gain_ref, wq_ref, wk_ref, wv_ref, out_ref, normed_ref, total_ref):
+    def body(states_ref, gain_ref, wq_ref, wk_ref, wv_ref, out_ref, square_ref, total_ref):
         step = pl.program_id(0)
 
         @pl.when(step == 0)
         def _():
-            for at in range(0, rows, 16):
-                values = states_ref[at : at + 16, :].astype(F32)
-                normed_ref[at : at + 16, :] = rms_scale(values, gain_ref[...]).astype(BF)
+            square_ref[...] = jnp.zeros_like(square_ref)
             total_ref[...] = jnp.zeros_like(total_ref)
 
-        here = normed_ref[:, pl.ds(aligned(step * chunk, chunk), chunk)]
+        values = states_ref[...].astype(F32)
+        square_ref[...] += jnp.sum(values * values, axis=-1, keepdims=True)
+        here = (values * gain_ref[...]).astype(BF)
         for k, weight_ref in enumerate((wq_ref, wk_ref, wv_ref)):
             total_ref[:, k * width : (k + 1) * width] += mm(here, weight_ref[...])
 
         @pl.when(step == steps - 1)
         def _():
-            out_ref[...] = total_ref[...].astype(BF)
-
-    whole = lambda shape: pl.BlockSpec(shape, lambda i: (0,) * len(shape))
+            scale = lax.rsqrt(square_ref[...] / depth + 1e-06)
+            out_ref[...] = (total_ref[...] * scale).astype(BF)
+
     return pl.pallas_call(
         body,
         grid=(steps,),
         out_shape=shaped((rows, 3 * width)),
-        in_specs=[whole((rows, depth)), whole((1, depth))]
+        in_specs=[
+            pl.BlockSpec((rows, chunk), lambda i: (0, i)),
+            pl.BlockSpec((1, chunk), lambda i: (0, i)),
+        ]
         + [pl.BlockSpec((chunk, width), lambda i: (i, 0))] * 3,
-        out_specs=whole((rows, 3 * width)),
-        scratch_shapes=[pltpu.VMEM((rows, depth), BF), pltpu.VMEM((rows, 3 * width), F32)],
+        out_specs=pl.BlockSpec((rows, 3 * width), lambda i: (0, 0)),
+        scratch_shapes=[pltpu.VMEM((rows, 1), F32), pltpu.VMEM((rows, 3 * width), F32)],
         compiler_params=pltpu.CompilerParams(vmem_limit_bytes=VMEM_BYTES),
         cost_estimate=SMALL,
     )(states, gain.reshape(1, -1), *weights)
@@ -497,29 +500,29 @@
     return call(body, out, (place, normed, out_grad, *arrays), 1)
 
 
-def project_captions(parts, own_key, own_value, side_key, side_value, place, pairs):
+def project_captions(parts, own_key, own_value, side_both, place, pairs):
     quarter_rows, depth = parts[0].shape[1:]
     half = depth // 2
     width = own_key.shape[1]
 
     def body(place_ref, *refs):
         part_refs = refs[:4]
-        key_ref, value_ref, side_key_ref, side_value_ref = refs[4:8]
-        out_refs = refs[8:]
+        key_ref, value_ref, side_ref = refs[4:7]
+        out_refs = refs[7:]
         y = place_ref[1]
         mine = pl.ds(aligned(y * half, 128), half)
         theirs = pl.ds(aligned((1 - y) * half, 128), half)
         own = jnp.concatenate([r[far, :, mine] for far in range(pairs) for r in part_refs], 0)
         other = jnp.concatenate([r[far, :, theirs] for far in range(pairs) for r in part_refs], 0)
-        keys = mm(own, key_ref[...]) + mm(other, side_key_ref[...])
-        values = mm(own, value_ref[...]) + mm(other, side_value_ref[...])
+        keys = mm(own, key_ref[...]) + mm(other, side_ref[:half, :])
+        values = mm(own, value_ref[...]) + mm(other, side_ref[half:, :])
         for far in range(pairs):
             rows = slice(far * 4 * quarter_rows, (far + 1) * 4 * quarter_rows)
             out_refs[far][:, :width] = keys[rows].astype(BF)
             out_refs[far][:, width:] = values[rows].astype(BF)
 
     out = [shaped((4 * quarter_rows, 2 * width))] * pairs
-    operands = (place, *parts, own_key, own_value, side_key, side_value)
+    operands = (place, *parts, own_key, own_value, side_both)
     return call(body, out, operands, 1)
 
 
@@ -751,26 +754,29 @@
     states = caption_states.reshape(cap_len, text_width)
     quarter_rows = cap_len // 4
 
-    first = [fsend(cross_query, 1, 0), fsend(cross_out, 1, 0)]
-    side_key, side_value = fsend(cross_key, 0, 1), fsend(cross_value, 0, 1)
+    ring = [(cross_query, cross_out)]
+    ring.append(tuple(fsend(w, 1, 0) for w in ring[0]))
+    side_both = fsend(jnp.concatenate([cross_key, cross_value], axis=0), 0, 1)
+    side_own = tuple(fsend(w, 0, 1) for w in ring[0])
     projected = project_text(states, text_gain, (text_query, text_key, text_value))
     kept, away = attend_text(projected, text_bias, text_out, place, caption_lens)
-    kept, away = after((kept, away), first, side_key, side_value)
+    kept, away = after((kept, away), ring[1], side_both)
     got = gsend(away, 1)
-    ring = [None, jnp.concatenate(first, axis=0)]
-    side_first = fsend(jnp.concatenate([cross_query, cross_out, *first], axis=0), 0, 1)
-    ring.append(fsend(ring[1], 1, 0))
     sent = (kept[quarter_rows:].astype(F32) + got[quarter_rows:].astype(F32)).astype(BF)
+    sent = after(sent, side_own[0])
     over_x = gsend(sent, 2)
+    joint = jnp.concatenate(ring[1], axis=0)
+    ring = [ring[0], joint, fsend(joint, 1, 0)]
+    side_first = fsend(joint, 0, 1)
     normed, mean, inverse, own_tiles, other_tiles = prepare_video(
         after(video_states, sent), out_grad, place, pairs, part
     )
     pieces = encode_rows(
-        states, kept, got, after(over_x, normed), final_gain, place, pairs
+        states, kept, got, after(over_x, normed, side_own[1]), final_gain, place, pairs
     )
 
     mine = jnp.stack([fsend(p, far, 0) if far else p for far, p in enumerate(pieces)])
-    mine = after(mine, ring[2])
+    mine = after(mine, ring[2], side_first)
     over_x = gsend(mine, 2)
     parts = [mine, gsend(mine, 1), over_x, gsend(over_x, 1)]
     current = after(ring[2], mine)
@@ -779,7 +785,7 @@
         ring.append(current)
     parts[3] = after(parts[3], side_first)
     kv_partial = project_captions(
-        parts, cross_key, cross_value, side_key, side_value, place, pairs
+        parts, cross_key, cross_value, side_both, place, pairs
     )
     kv_partial = after(tuple(kv_partial), ring[-1])
     kv_sum = kv_partial[0].astype(F32)
@@ -791,12 +797,9 @@
     kv_blocks = gather_direct(kv_sum)
     kv_blocks[4] = after(kv_blocks[4], side_later, other_tiles)
 
-    step = part + width_local
-    blocks = []
-    for far, held in enumerate(ring):
-        side, start = (side_first, far * step) if far < 2 else (side_later[far - 2], 0)
-        here = ((held, 0), (held, part)) if far else ((cross_query, 0), (cross_out, 0))
-        blocks += [here, ((side, start), (side, start + part))]
+    blocks = [((cross_query, 0), (cross_out, 0)), ((side_own[0], 0), (side_own[1], 0))]
+    for held, side in zip(ring[1:], [side_first, *side_later]):
+        blocks += [((held, 0), (held, part)), ((side, 0), (side, part))]
     queries, d_attended, column_sum = project_rows(
         normed, after(out_grad, kv_blocks[4]), blocks, place, pairs, part
     )
@@ -824,42 +827,43 @@
             blocks.append(fsend(blocks[-1], 1, 0))
         return blocks
 
-    def joined(two):
-        return jnp.stack(two).reshape(-1, tokens, width_local)
-
     side_slots = fsend(slots, 0, 1)
-    side_own = fsend(both, 0, 1)
+    side_mine = fsend(both, 0, 1)
     late = chain([both], 2)
     sums_core = gsend(row_sums, 1)
     attended, tiles = after((attended, tiles), sums_core)
     tiles_x = gsend(tiles, 2)
     own, far_piece, away = project_back(attended, d_queries, blocks, place, pairs, part)
-    two = joined(late[1:3])
-    stage = (side_slots, side_own, late, sums_core, tiles_x, two, away)
-    side_slots, side_own, late, sums_core, tiles_x, two, away = after(stage)
-
-    side_two = fsend(two, 0, 1)
+    tiles_core = gsend(tiles, 1)
+    stage = (side_slots, side_mine, late, sums_core, tiles_x, tiles_core, away)
+    side_slots, side_mine, late, sums_core, tiles_x, tiles_core, away = after(stage)
+
+    sides = [fsend(block, 0, 1) for block in late[1:3]]
     late = chain(list(late), pairs - 3)
     row_sums = row_sums + sums_core
     sums_x = gsend(row_sums, 2)
     got = gsend(away, 1)
-    tiles_core = gsend(tiles, 1)
     width = model_width // 4
-    sent = (far_piece.astype(F32) + got[:, :, width:].astype(F32)).astype(BF)
-    far_sum = gsend(sent, 2)
+    sent = [
+        (far_piece[k].astype(F32) + got[k, :, width:].astype(F32)).astype(BF) for k in range(2)
+    ]
+    far_out = gsend(sent[0], 2)
+    terms = caption_terms(
+        after(slots, sent[0]), side_slots, place, video_counts, sample_caption, tokens, pairs
+    )
+    kv_parts = [fsend(terms[far], far, 0) for far in range(1, pairs, 2)]
+    stage = (sides, late, sums_x, tiles_x, kv_parts, terms, far_out, sent[1])
+    sides, late, sums_x, tiles_x, kv_parts, terms, far_out, sent_d = after(stage)
+
+    here = [((block, 0),) for block in late]
     tiles = [tiles, tiles_core, tiles_x, gsend(tiles_x, 1)]
-    terms = caption_terms(
-        slots, side_slots, place, video_counts, sample_caption, tokens, pairs
-    )
-    kv_parts = [fsend(terms[far], far, 0) for far in range(1, pairs, 2)]
-    stage = (side_two, late, sums_x, sent, tiles, kv_parts, terms)
-    side_two, late, sums_x, _, tiles, kv_parts, terms = after(stage)
-
-    here = [((block, 0),) for block in late]
-    there = [((side_own, 0),), ((side_two, 0),), ((side_two, 2),)]
+    there = [((block, 0),) for block in (side_mine, *sides)]
     there += [((fsend(block, 0, 1), 0),) for block in late[3:]]
     known = weight_grads(tiles, here + there[:3], None, pairs)
-    total = own.astype(F32) + got[:, :, :width].astype(F32) + far_sum.astype(F32)
+    total = [
+        own[k].astype(F32) + got[k, :, :width].astype(F32) + far.astype(F32)
+        for k, far in enumerate((far_out, gsend(sent_d, 2)))
+    ]
     row_sums = (row_sums + sums_x) / model_width
     video = quarter(video_states, g, 1).astype(F32)
     updated = (video + total[0]).astype(BF)

time: 196 us -> 208 us (1.061)
  waiting for transfers between devices: 69.2 us -> 94.8 us
  starting transfers between devices: 64.2 us -> 56.5 us
  local copies, waits for them, and re-layouts: 9.17 us -> 3.78 us
    ppermute x36 -> x38, waiting for transfers between devices: 55.3 us -> 76.9 us  [fsend(): return lax.ppermute(block, 'fsdp', perm)]
    ppermute x36 -> x38, starting transfers between devices: 56.5 us -> 48.6 us  [fsend(): return lax.ppermute(block, 'fsdp', perm)]
    unnamed x73 -> x63, local copies, waits for them, and re-layouts: 7.21 us -> 1.88 us
    ppermute x12 -> x13, waiting for transfers between devices: 13.9 us -> 17.9 us  [gsend(): lax.ppermute(block, 'grp', [(s, s ^ flip) for s in range(lax.axis_size('g...]
    ppermute x12 -> x13, starting transfers between devices: 7.73 us -> 7.88 us  [gsend(): lax.ppermute(block, 'grp', [(s, s ^ flip) for s in range(lax.axis_size('g...]
  transfers between devices with their start and end apart: 48 -> 51, of which waited for: 18 -> 22; matrix products, arithmetic and copies ran while one was open for 7% -> 6% of each run, Pallas kernels for 20% -> 18%
where the time goes in v7:
time: 208 us
  waiting for transfers between devices  94.8 us (46%)
  starting transfers between devices  56.5 us (27%)
  Pallas kernels  39 us (19%)
  other arithmetic  12.4 us (6%)
  local copies, waits for them, and re-layouts  3.78 us (2%)
    ppermute x38, waiting for transfers between devices, fsend(): return lax.ppermute(block, 'fsdp', perm)  76.9 us
    ppermute x38, starting transfers between devices, fsend(): return lax.ppermute(block, 'fsdp', perm)  48.6 us
    pallas_call x9, Pallas kernels, call(): pl.pallas_call(body, out_shape=out_shape, in_specs=specs, out_specs=jax.t...  22.7 us
    ppermute x13, waiting for transfers between devices, gsend(): lax.ppermute(block, 'grp', [(s, s ^ flip) for s in range(lax.axis_size('g...  17.9 us
    pallas_call x1, Pallas kernels, project_text(): pl.pallas_call(body, grid=(steps,), out_shape=shaped((rows, 3 * width)),...  9.04 us
    ppermute x13, starting transfers between devices, gsend(): lax.ppermute(block, 'grp', [(s, s ^ flip) for s in range(lax.axis_size('g...  7.88 us
    pallas_call x1, Pallas kernels, attend_text(): pl.pallas_call(body, grid=(steps,), out_shape=[shaped((rows // 2, depth))...  7.19 us
  transfers between devices with their start and end apart: 51, of which 22 were waited for; matrix products, arithmetic and copies ran while one was open for 6% of the time, Pallas kernels for 18%

profile of v7, /device:TPU:0, one launch (start us, length us, event | category | flops | bytes accessed | tf_op | source)
XLA Modules:
  0.0 207.5 jit_solution(2401937261164337565)
XLA Ops:
  0.6 2.1 %pad_maximum_fusion = bf16[1024,384]{1,0:T(8,128)(2,1)} fusion(bf16[512,384]{1,0:T(8,128)(2,1)} %refs_5_.1, bf16[512,384]{1,0:T(8,128)(2,1)} %refs_4_.1), kind=kLoop, calls=%fused_computation.15 | loop fusion | flops 1572864 | bytes 1572864 | tf_op jit(solution)/shard_map/concatenate | solution.py:759
  2.8 3.0 %collective-permute-start.2 = (bf16[1024,384]{1,0:T(8,128)(2,1)}, bf16[1024,384]{1,0:T(8,128)(2,1)}, u32[]{:S(2)}, u32[]{:S(2)}) collective-permute-start(bf16[1024,384]{1,0:T(8,128)(2,1)} %pad_maximum_fusion), channel_id=1, source_target_pairs={{0,1},{1,0},{2,3},{3,2},{4,5},{5,4},{6,7},{7,6},{8,9},{9,8},{10,11... | collective-permute-start | bytes 2359304 | tf_op jit(solution)/shard_map/ppermute | solution.py:40
  5.7 1.6 collective-permute-start
  7.3 1.6 collective-permute-start.1
  8.9 9.0 %shard_map.208.qkv_ref = bf16[128,1536]{1,0:T(8,128)(2,1)} custom-call(bf16[128,4096]{1,0:T(8,128)(2,1)} %bitcast.40, f32[1,4096]{1,0:T(1,128)} %bitcast.53, bf16[4096,512]{1,0:T(8,128)(2,1)} %wq_ref.1, bf16[4096,512]{1,0:T(8,128)(2,1)} %wk_ref.1, bf16[4096,512]{1,0:T(8,128)(2,1)} %wv_ref.1), custom_call_target="tpu_custom_call" | custom-call | flops 1 | bytes 1 | tf_op jit(solution)/shard_map/pallas_call | solution.py:350
  18.5 7.2 %shard_map.209 = (bf16[64,4096]{1,0:T(8,128)(2,1)}, bf16[64,4096]{1,0:T(8,128)(2,1)}) custom-call(s32[3]{0:T(128)} %pad_add_fusion.place_ref, s32[8]{0:T(128)} %len_ref.3, bf16[128,1536]{1,0:T(8,128)(2,1)} %shard_map.208.qkv_ref, f32[8,128,128]{2,1,0:T(8,128)} %bias_ref.1, bf16[512,4096]{1,0:T(8,128)(2,1)} %out_ref.1), custom_call_target="tpu_custom_call" | custom-call | flops 1 | bytes 1 | tf_op jit(solution)/shard_map/pallas_call | solution.py:397
  26.4 1.5 collective-permute-start.6
  27.9 1.0 constant_dynamic-update-slice_fusion.1
  28.9 1.0 constant_dynamic-update-slice_fusion.refs_4_
  29.9 1.6 collective-permute-start.10
  32.0 1.0 add_convert_fusion.2
  33.1 2.6 %collective-permute-done.4.refs_2_ = bf16[384,384]{1,0:T(8,128)(2,1)S(1)} collective-permute-done((bf16[384,384]{1,0:T(8,128)(2,1)S(1)}, bf16[384,384]{1,0:T(8,128)(2,1)S(1)}, u32[]{:S(2)}, u32[]{:S(2)}) %collective-permute-start.4) | collective-permute-done | bytes 294944 | tf_op jit(solution)/shard_map/ppermute | solution.py:40
  35.7 1.5 collective-permute-start.5
  37.2 2.7 %shard_map.210 = (bf16[256,3072]{1,0:T(8,128)(2,1)S(1)}, f32[256,1]{1,0:T(8,128)S(1)}, f32[256,1]{1,0:T(8,128)S(1)}, bf16[4,2,64,384]{3,2,1,0:T(8,128)(2,1)S(1)}, bf16[4,2,64,384]{3,2,1,0:T(8,128)(2,1)S(1)}) custom-call(s32[3]{0:T(128)S(1)} %copy-done.22, bf16[256,3072]{1,0:T(8,128)(2,1)S(1)} %copy-done.4, bf16[256,3072]{1,0:T(8,128)(2,1)S(1)} %copy-done), custom_call_target="tpu_custom_call" | custom-call | flops 1 | bytes 1 | tf_op jit(solution)/shard_map/pallas_call | solution.py:307
  40.0 2.0 collective-permute-done.6.refs_3_
  42.0 1.1 collective-permute-done.5.far_ref
  43.1 0.8 shard_map.211
  43.9 1.6 collective-permute-start.7
  45.6 1.2 collective-permute-start.8
  46.8 1.3 collective-permute-start.9
  48.1 2.0 collective-permute-done.7
  50.2 1.6 collective-permute-done.8
  51.8 2.3 %collective-permute-done.11.refs_5_ = bf16[768,384]{1,0:T(8,128)(2,1)S(1)} collective-permute-done((bf16[768,384]{1,0:T(8,128)(2,1)S(1)}, bf16[768,384]{1,0:T(8,128)(2,1)S(1)}, u32[]{:S(2)}, u32[]{:S(2)}) %collective-permute-start.11) | collective-permute-done | bytes 589856 | tf_op jit(solution)/shard_map/ppermute | solution.py:40
  54.2 1.6 collective-permute-start.15
  55.8 1.5 collective-permute-start.13
  57.2 6.1 %collective-permute-done.13.refs_2_ = bf16[4,32,1024]{2,1,0:T(8,128)(2,1)S(1)} collective-permute-done((bf16[4,32,1024]{2,1,0:T(8,128)(2,1)S(1)}, bf16[4,32,1024]{2,1,0:T(8,128)(2,1)S(1)}, u32[]{:S(2)}, u32[]{:S(2)}) %collective-permute-start.13) | collective-permute-done | bytes 262176 | tf_op jit(solution)/shard_map/ppermute | solution.py:44
  65.3 2.4 %shard_map.212 = (bf16[128,768]{1,0:T(8,128)(2,1)S(1)}, bf16[128,768]{1,0:T(8,128)(2,1)S(1)}, bf16[128,768]{1,0:T(8,128)(2,1)S(1)}, bf16[128,768]{1,0:T(8,128)(2,1)S(1)}) custom-call(s32[3]{0:T(128)S(1)} %copy-done.22, bf16[4,32,1024]{2,1,0:T(8,128)(2,1)S(1)} %pad_maximum_fusion.2.refs_0_, bf16[4,32,1024]{2,1,0:T(8,128)(2,1)S(1)} %collective-permute-done.12.refs_1_, ...), custom_call_target="tpu_custom_call" | custom-call | flops 1 | bytes 1 | tf_op jit(solution)/shard_map/pallas_call | solution.py:307
  67.7 3.2 %collective-permute-done.15.refs_8_ = bf16[768,384]{1,0:T(8,128)(2,1)S(1)} collective-permute-done((bf16[768,384]{1,0:T(8,128)(2,1)S(1)}, bf16[768,384]{1,0:T(8,128)(2,1)S(1)}, u32[]{:S(2)}, u32[]{:S(2)}) %collective-permute-start.15) | collective-permute-done | bytes 589856 | tf_op jit(solution)/shard_map/ppermute | solution.py:40
  71.3 0.8 collective-permute-start.17
  73.4 4.1 %collective-permute-done.16 = bf16[128,768]{1,0:T(8,128)(2,1)S(1)} collective-permute-done((bf16[128,768]{1,0:T(8,128)(2,1)S(1)}, bf16[128,768]{1,0:T(8,128)(2,1)S(1)}, u32[]{:S(2)}, u32[]{:S(2)}) %collective-permute-start.16) | collective-permute-done | bytes 196640 | tf_op jit(solution)/shard_map/ppermute | solution.py:40
  78.0 10.3 %collective-permute-done.17 = bf16[128,768]{1,0:T(8,128)(2,1)S(1)} collective-permute-done((bf16[128,768]{1,0:T(8,128)(2,1)S(1)}, bf16[128,768]{1,0:T(8,128)(2,1)S(1)}, u32[]{:S(2)}, u32[]{:S(2)}) %collective-permute-start.17) | collective-permute-done | bytes 196640 | tf_op jit(solution)/shard_map/ppermute | solution.py:40
  88.7 2.0 collective-permute-start.20
  90.7 2.8 %collective-permute-start.27 = (bf16[128,768]{1,0:T(8,128)(2,1)S(1)}, bf16[128,768]{1,0:T(8,128)(2,1)S(1)}, u32[]{:S(2)}, u32[]{:S(2)}) collective-permute-start(bf16[128,768]{1,0:T(8,128)(2,1)S(1)} %add_convert_fusion.4.refs_0_), channel_id=1, source_target_pairs={{0,6},{1,7},{2,0},{3,1},{4,2},{5,3},{6,4},{7,5},{8,14},{9,15},{10,... | collective-permute-start | bytes 589832 | tf_op jit(solution)/shard_map/ppermute | solution.py:40
  94.2 4.0 %collective-permute-done.24.refs_2_ = bf16[128,768]{1,0:T(8,128)(2,1)S(1)} collective-permute-done((bf16[128,768]{1,0:T(8,128)(2,1)S(1)}, bf16[128,768]{1,0:T(8,128)(2,1)S(1)}, u32[]{:S(2)}, u32[]{:S(2)}) %collective-permute-start.24) | collective-permute-done | bytes 196640 | tf_op jit(solution)/shard_map/ppermute | solution.py:40
  98.7 5.0 %collective-permute-done.20.refs_4_ = bf16[128,768]{1,0:T(8,128)(2,1)S(1)} collective-permute-done((bf16[128,768]{1,0:T(8,128)(2,1)S(1)}, bf16[128,768]{1,0:T(8,128)(2,1)S(1)}, u32[]{:S(2)}, u32[]{:S(2)}) %collective-permute-start.20) | collective-permute-done | bytes 196640 | tf_op jit(solution)/shard_map/ppermute | solution.py:40
  104.4 1.4 collective-permute-start.28
  105.8 7.3 %collective-permute-start.31 = (bf16[2,2,64,384]{3,2,1,0:T(8,128)(2,1)S(1)}, bf16[2,2,64,384]{3,2,1,0:T(8,128)(2,1)S(1)}, u32[]{:S(2)}, u32[]{:S(2)}) collective-permute-start(bf16[2,2,64,384]{3,2,1,0:T(8,128)(2,1)S(1)} %get-tuple-element.128), channel_id=1, source_target_pairs={{0,6},{1,7},{2,0},{3,1},{4,2},{5,3},{6,4},{7,5},{8,14},{9,15},{10,... | collective-permute-start | bytes 589832 | tf_op jit(solution)/shard_map/ppermute | solution.py:40
  113.7 3.2 %shard_map.213 = (bf16[256,384]{1,0:T(8,128)(2,1)S(1)}, bf16[256,384]{1,0:T(8,128)(2,1)S(1)}, f32[1,384]{1,0:T(1,128)S(1)}) custom-call(s32[3]{0:T(128)S(1)} %copy-done.22, bf16[256,3072]{1,0:T(8,128)(2,1)S(1)} %get-tuple-element.97.normed_ref, bf16[256,3072]{1,0:T(8,128)(2,1)S(1)} %copy-done, bf16[384,384]{1,0:T(8,128)(2,1)S(1)} %copy-done.8, ...), custom_call_target="tpu_custom_call" | custom-call | flops 1 | bytes 1 | tf_op jit(solution)/shard_map/pallas_call | solution.py:307
  117.0 2.8 %shard_map.214 = (bf16[2,256,384]{2,1,0:T(8,128)(2,1)S(1)}, bf16[256,384]{1,0:T(8,128)(2,1)S(1)}, bf16[256,384]{1,0:T(8,128)(2,1)S(1)}, f32[256,2]{1,0:T(8,128)S(1)}, bf16[3,128,768]{2,1,0:T(8,128)(2,1)S(1)}) custom-call(s32[3]{0:T(128)S(1)} %copy-done.22, s32[8]{0:T(128)S(1)} %copy-done.24, s32[8]{0:T(128)S(1)} %copy-done.25, s32[8]{0:T(128)S(1)} %copy-done.26, ...), custom_call_target="tpu_custom_call" | custom-call | flops 1 | bytes 1 | tf_op jit(solution)/shard_map/pallas_call | solution.py:307
  119.9 8.1 %collective-permute-done.30 = bf16[2,2,64,384]{3,2,1,0:T(8,128)(2,1)S(1)} collective-permute-done((bf16[2,2,64,384]{3,2,1,0:T(8,128)(2,1)S(1)}, bf16[2,2,64,384]{3,2,1,0:T(8,128)(2,1)S(1)}, u32[]{:S(2)}, u32[]{:S(2)}) %collective-permute-start.30) | collective-permute-done | bytes 196640 | tf_op jit(solution)/shard_map/ppermute | solution.py:40
  128.0 1.4 collective-permute-start.35
  129.5 1.6 collective-permute-start.37
  131.4 1.7 collective-permute-start.34
  133.0 8.2 %collective-permute-done.35.refs_5_ = bf16[2,256,384]{2,1,0:T(8,128)(2,1)S(1)} collective-permute-done((bf16[2,256,384]{2,1,0:T(8,128)(2,1)S(1)}, bf16[2,256,384]{2,1,0:T(8,128)(2,1)S(1)}, u32[]{:S(2)}, u32[]{:S(2)}) %collective-permute-start.35) | collective-permute-done | bytes 393248 | tf_op jit(solution)/shard_map/ppermute | solution.py:40
  141.3 4.9 %shard_map.215 = (bf16[2,256,768]{2,1,0:T(8,128)(2,1)S(1)}, bf16[2,256,768]{2,1,0:T(8,128)(2,1)S(1)}, bf16[2,256,1536]{2,1,0:T(8,128)(2,1)S(1)}) custom-call(s32[3]{0:T(128)S(1)} %copy-done.22, bf16[256,384]{1,0:T(8,128)(2,1)S(1)} %get-tuple-element.134.att_ref, bf16[256,384]{1,0:T(8,128)(2,1)S(1)} %get-tuple-element.135.dq_ref, ...), custom_call_target="tpu_custom_call" | custom-call | flops 1 | bytes 1 | tf_op jit(solution)/shard_map/pallas_call | solution.py:307
  146.3 8.9 %collective-permute-done.34.refs_8_ = bf16[2,256,384]{2,1,0:T(8,128)(2,1)S(1)} collective-permute-done((bf16[2,256,384]{2,1,0:T(8,128)(2,1)S(1)}, bf16[2,256,384]{2,1,0:T(8,128)(2,1)S(1)}, u32[]{:S(2)}, u32[]{:S(2)}) %collective-permute-start.34) | collective-permute-done | bytes 393248 | tf_op jit(solution)/shard_map/ppermute | solution.py:40
  155.7 2.5 %collective-permute-start.42 = (bf16[2,256,384]{2,1,0:T(8,128)(2,1)}, bf16[2,256,384]{2,1,0:T(8,128)(2,1)}, u32[]{:S(2)}, u32[]{:S(2)}) collective-permute-start(bf16[2,256,384]{2,1,0:T(8,128)(2,1)} %collective-permute-done.36.refs_6_), channel_id=1, source_target_pairs={{0,2},{1,3},{2,4},{3,5},{4,6},{5,7},{6,0},{7,1},{8,10},{9,11},{10,... | collective-permute-start | bytes 1179656 | tf_op jit(solution)/shard_map/ppermute | solution.py:40
  158.2 1.7 collective-permute-start.40
  159.9 1.2 fusion.9
  161.7 1.6 collective-permute-start.43
  163.2 1.8 shard_map.216
  165.0 9.7 %collective-permute-done.43 = f32[256,2]{1,0:T(8,128)S(1)} collective-permute-done((f32[256,2]{1,0:T(8,128)S(1)}, f32[256,2]{1,0:T(8,128)S(1)}, u32[]{:S(2)}, u32[]{:S(2)}) %collective-permute-start.43) | collective-permute-done | bytes 2080 | tf_op jit(solution)/shard_map/ppermute | solution.py:44
  174.7 1.8 collective-permute-start.44
  177.3 2.0 collective-permute-start.45
  179.4 1.0 reduce
  180.4 1.0 reduce.2
  181.4 2.3 %collective-permute-done.44 = bf16[128,768]{1,0:T(8,128)(2,1)} collective-permute-done((bf16[128,768]{1,0:T(8,128)(2,1)}, bf16[128,768]{1,0:T(8,128)(2,1)}, u32[]{:S(2)}, u32[]{:S(2)}) %collective-permute-start.44) | collective-permute-done | bytes 196640 | tf_op jit(solution)/shard_map/ppermute | solution.py:40
  183.7 3.0 %collective-permute-done.45 = bf16[128,768]{1,0:T(8,128)(2,1)} collective-permute-done((bf16[128,768]{1,0:T(8,128)(2,1)}, bf16[128,768]{1,0:T(8,128)(2,1)}, u32[]{:S(2)}, u32[]{:S(2)}) %collective-permute-start.45) | collective-permute-done | bytes 196640 | tf_op jit(solution)/shard_map/ppermute | solution.py:40
  187.7 1.0 add_multiply_fusion
  189.5 9.1 %collective-permute-done.50 = bf16[128,768]{1,0:T(8,128)(2,1)S(1)} collective-permute-done((bf16[128,768]{1,0:T(8,128)(2,1)}, bf16[128,768]{1,0:T(8,128)(2,1)S(1)}, u32[]{:S(2)}, u32[]{:S(2)}) %collective-permute-start.50) | collective-permute-done | bytes 196640 | tf_op jit(solution)/shard_map/ppermute | solution.py:40
  198.6 1.3 fusion.10
  200.6 2.9 %fusion.6 = (bf16[256,768]{1,0:T(8,128)(2,1)}, bf16[256,768]{1,0:T(8,128)(2,1)}) fusion(bf16[256,768]{1,0:T(8,128)(2,1)S(1)} %collective-permute-done.47, bf16[2,256,1536]{2,1,0:T(8,128)(2,1)} %copy-done.28, f32[256]{0:T(256)S(1)} %get-tuple-element.177, f32[256]{0:T(256)S(1)} %reduce.2, f32[256]{0:T(256)S(1)} %get-tuple-element.176, ...), kind=kLoop, calls=%fused_computation.14 | loop fusion | flops 4325376 | bytes 3936260 | tf_op jit(solution)/shard_map/convert_element_type | solution.py:874
  203.5 2.7 %shard_map.217 = (f32[384,384]{1,0:T(8,128)S(1)}, f32[384,384]{1,0:T(8,128)S(1)}) custom-call(bf16[4,2,2,64,384]{4,3,2,1,0:T(8,128)(2,1)S(1)} %pad_maximum_fusion.1.refs_0_, bf16[4,2,2,64,384]{4,3,2,1,0:T(8,128)(2,1)S(1)} %copy-done.3, bf16[4,2,2,64,384]{4,3,2,1,0:T(8,128)(2,1)S(1)} %collective-permute-done.37.refs_2_, ...), custom_call_target="tpu_custom_call" | custom-call | flops 1 | bytes 1 | tf_op jit(solution)/shard_map/pallas_call | solution.py:307
  206.2 1.3 shard_map.218
  (129 shorter events, 13.8 us)
Async XLA Ops:
  2.8 22.9 %collective-permute-start.2 = (bf16[1024,384]{1,0:T(8,128)(2,1)}, bf16[1024,384]{1,0:T(8,128)(2,1)}, u32[]{:S(2)}, u32[]{:S(2)}) collective-permute-start(bf16[1024,384]{1,0:T(8,128)(2,1)} %pad_maximum_fusion), channel_id=1, source_target_pairs={{0,1},{1,0},{2,3},{3,2},{4,5},{5,4},{6,7},{7,6},{8,9},{9,8},{10,11... | collective-permute-start | bytes 2359304 | tf_op jit(solution)/shard_map/ppermute | solution.py:40
  5.7 20.0 %collective-permute-start = (bf16[384,384]{1,0:T(8,128)(2,1)S(1)}, bf16[384,384]{1,0:T(8,128)(2,1)}, u32[]{:S(2)}, u32[]{:S(2)}) collective-permute-start(bf16[384,384]{1,0:T(8,128)(2,1)S(1)} %copy-done.8), channel_id=1, source_target_pairs={{0,2},{1,3},{2,4},{3,5},{4,6},{5,7},{6,0},{7,1},{8,10},{9,11},{10,... | collective-permute-start | bytes 884744 | tf_op jit(solution)/shard_map/ppermute | solution.py:40
  7.3 18.4 %collective-permute-start.1 = (bf16[384,384]{1,0:T(8,128)(2,1)}, bf16[384,384]{1,0:T(8,128)(2,1)}, u32[]{:S(2)}, u32[]{:S(2)}) collective-permute-start(bf16[384,384]{1,0:T(8,128)(2,1)} %refs_1_.3), channel_id=1, source_target_pairs={{0,2},{1,3},{2,4},{3,5},{4,6},{5,7},{6,0},{7,1},{8,10},{9,11},{10,... | collective-permute-start | bytes 884744 | tf_op jit(solution)/shard_map/ppermute | solution.py:40
  18.5 18.7 %copy-start.4 = (bf16[256,3072]{1,0:T(8,128)(2,1)S(1)}, bf16[256,3072]{1,0:T(8,128)(2,1)}, u32[]{:S(2)}) copy-start(bf16[256,3072]{1,0:T(8,128)(2,1)} %video_ref) | copy-start | bytes 4718596
  25.7 11.5 %copy-start.22 = (s32[3]{0:T(128)S(1)}, s32[3]{0:T(128)}, u32[]{:S(2)}) copy-start(s32[3]{0:T(128)} %pad_add_fusion.place_ref) | copy-start | bytes 40
  25.7 6.3 %collective-permute-start.3 = (bf16[64,4096]{1,0:T(8,128)(2,1)}, bf16[64,4096]{1,0:T(8,128)(2,1)S(1)}, u32[]{:S(2)}, u32[]{:S(2)}) collective-permute-start(bf16[64,4096]{1,0:T(8,128)(2,1)} %get-tuple-element.94), channel_id=1, source_target_pairs={{0,8},{8,0},{16,24},{24,16},{1,9},{9,1},{17,25},{25,17},{2,10},{10... | collective-permute-start | bytes 1572872 | tf_op jit(solution)/shard_map/ppermute | solution.py:44
  25.8 9.9 %collective-permute-start.4 = (bf16[384,384]{1,0:T(8,128)(2,1)S(1)}, bf16[384,384]{1,0:T(8,128)(2,1)S(1)}, u32[]{:S(2)}, u32[]{:S(2)}) collective-permute-start(bf16[384,384]{1,0:T(8,128)(2,1)S(1)} %copy-done.8), channel_id=1, source_target_pairs={{0,1},{1,0},{2,3},{3,2},{4,5},{5,4},{6,7},{7,6},{8,9},{9,8},{10,11... | collective-permute-start | bytes 884744 | tf_op jit(solution)/shard_map/ppermute | solution.py:40
  26.4 15.6 %collective-permute-start.6 = (bf16[384,384]{1,0:T(8,128)(2,1)}, bf16[384,384]{1,0:T(8,128)(2,1)S(1)}, u32[]{:S(2)}, u32[]{:S(2)}) collective-permute-start(bf16[384,384]{1,0:T(8,128)(2,1)} %refs_1_.3), channel_id=1, source_target_pairs={{0,1},{1,0},{2,3},{3,2},{4,5},{5,4},{6,7},{7,6},{8,9},{9,8},{10,11... | collective-permute-start | bytes 884744 | tf_op jit(solution)/shard_map/ppermute | solution.py:40
  29.9 21.9 %collective-permute-start.10 = (bf16[768,384]{1,0:T(8,128)(2,1)S(1)}, bf16[768,384]{1,0:T(8,128)(2,1)S(1)}, u32[]{:S(2)}, u32[]{:S(2)}) collective-permute-start(bf16[768,384]{1,0:T(8,128)(2,1)S(1)} %constant_dynamic-update-slice_fusion.refs_4_), channel_id=1, source_target_pairs={{0,2},{1,3},{2,4},{3,5},{4,6},{5,7},{6,0},{7,1},{8,10},{9,11},{10,... | collective-permute-start | bytes 1769480 | tf_op jit(solution)/shard_map/ppermute | solution.py:40
  31.5 22.7 %collective-permute-start.11 = (bf16[768,384]{1,0:T(8,128)(2,1)S(1)}, bf16[768,384]{1,0:T(8,128)(2,1)S(1)}, u32[]{:S(2)}, u32[]{:S(2)}) collective-permute-start(bf16[768,384]{1,0:T(8,128)(2,1)S(1)} %constant_dynamic-update-slice_fusion.refs_4_), channel_id=1, source_target_pairs={{0,1},{1,0},{2,3},{3,2},{4,5},{5,4},{6,7},{7,6},{8,9},{9,8},{10,11... | collective-permute-start | bytes 1769480 | tf_op jit(solution)/shard_map/ppermute | solution.py:40
  35.7 7.4 %collective-permute-start.5 = (bf16[32,4096]{1,0:T(8,128)(2,1)S(1)}, bf16[32,4096]{1,0:T(8,128)(2,1)S(1)}, u32[]{:S(2)}, u32[]{:S(2)}) collective-permute-start(bf16[32,4096]{1,0:T(8,128)(2,1)S(1)} %add_convert_fusion.2), channel_id=1, source_target_pairs={{0,16},{8,24},{16,0},{24,8},{1,17},{9,25},{17,1},{25,9},{2,18},{10... | collective-permute-start | bytes 786440 | tf_op jit(solution)/shard_map/ppermute | solution.py:44
  39.9 25.0 %copy-start.21 = (f32[256,1]{1,0:T(8,128)}, f32[256,1]{1,0:T(8,128)S(1)}, u32[]{:S(2)}) copy-start(f32[256,1]{1,0:T(8,128)S(1)} %get-tuple-element.155) | copy-start | bytes 3076
  39.9 73.2 %copy-start.20 = (f32[256,1]{1,0:T(8,128)}, f32[256,1]{1,0:T(8,128)S(1)}, u32[]{:S(2)}) copy-start(f32[256,1]{1,0:T(8,128)S(1)} %get-tuple-element.158) | copy-start | bytes 3076
  39.9 25.3 %copy-start.5 = (bf16[512,384]{1,0:T(8,128)(2,1)S(1)}, bf16[512,384]{1,0:T(8,128)(2,1)}, u32[]{:S(2)}) copy-start(bf16[512,384]{1,0:T(8,128)(2,1)} %refs_4_.1) | copy-start | bytes 1179652
  39.9 25.3 %copy-start.6 = (bf16[512,384]{1,0:T(8,128)(2,1)S(1)}, bf16[512,384]{1,0:T(8,128)(2,1)}, u32[]{:S(2)}) copy-start(bf16[512,384]{1,0:T(8,128)(2,1)} %refs_5_.1) | copy-start | bytes 1179652
  43.9 6.2 %collective-permute-start.7 = (bf16[32,1024]{1,0:T(8,128)(2,1)S(1)}, bf16[32,1024]{1,0:T(8,128)(2,1)S(1)}, u32[]{:S(2)}, u32[]{:S(2)}) collective-permute-start(bf16[32,1024]{1,0:T(8,128)(2,1)S(1)} %get-tuple-element.100), channel_id=1, source_target_pairs={{0,2},{1,3},{2,4},{3,5},{4,6},{5,7},{6,0},{7,1},{8,10},{9,11},{10,... | collective-permute-start | bytes 196616 | tf_op jit(solution)/shard_map/ppermute | solution.py:40
  45.6 6.2 %collective-permute-start.8 = (bf16[32,1024]{1,0:T(8,128)(2,1)S(1)}, bf16[32,1024]{1,0:T(8,128)(2,1)S(1)}, u32[]{:S(2)}, u32[]{:S(2)}) collective-permute-start(bf16[32,1024]{1,0:T(8,128)(2,1)S(1)} %get-tuple-element.101), channel_id=1, source_target_pairs={{0,4},{1,5},{2,6},{3,7},{4,0},{5,1},{6,2},{7,3},{8,12},{9,13},{10,... | collective-permute-start | bytes 196616 | tf_op jit(solution)/shard_map/ppermute | solution.py:40
  46.8 5.0 %collective-permute-start.9 = (bf16[32,1024]{1,0:T(8,128)(2,1)S(1)}, bf16[32,1024]{1,0:T(8,128)(2,1)S(1)}, u32[]{:S(2)}, u32[]{:S(2)}) collective-permute-start(bf16[32,1024]{1,0:T(8,128)(2,1)S(1)} %get-tuple-element.102), channel_id=1, source_target_pairs={{0,6},{1,7},{2,0},{3,1},{4,2},{5,3},{6,4},{7,5},{8,14},{9,15},{10,... | collective-permute-start | bytes 196616 | tf_op jit(solution)/shard_map/ppermute | solution.py:40
  54.2 16.7 %collective-permute-start.15 = (bf16[768,384]{1,0:T(8,128)(2,1)S(1)}, bf16[768,384]{1,0:T(8,128)(2,1)S(1)}, u32[]{:S(2)}, u32[]{:S(2)}) collective-permute-start(bf16[768,384]{1,0:T(8,128)(2,1)S(1)} %collective-permute-done.10.refs_6_), channel_id=1, source_target_pairs={{0,2},{1,3},{2,4},{3,5},{4,6},{5,7},{6,0},{7,1},{8,10},{9,11},{10,... | collective-permute-start | bytes 1769480 | tf_op jit(solution)/shard_map/ppermute | solution.py:40
  55.8 7.6 %collective-permute-start.13 = (bf16[4,32,1024]{2,1,0:T(8,128)(2,1)S(1)}, bf16[4,32,1024]{2,1,0:T(8,128)(2,1)S(1)}, u32[]{:S(2)}, u32[]{:S(2)}) collective-permute-start(bf16[4,32,1024]{2,1,0:T(8,128)(2,1)S(1)} %pad_maximum_fusion.2.refs_0_), channel_id=1, source_target_pairs={{0,16},{8,24},{16,0},{24,8},{1,17},{9,25},{17,1},{25,9},{2,18},{10... | collective-permute-start | bytes 786440 | tf_op jit(solution)/shard_map/ppermute | solution.py:44
  63.4 1.5 collective-permute-start.14
  63.4 1.9 collective-permute-start.12
  63.9 24.6 %collective-permute-start.19 = (bf16[768,384]{1,0:T(8,128)(2,1)S(1)}, bf16[768,384]{1,0:T(8,128)(2,1)S(1)}, u32[]{:S(2)}, u32[]{:S(2)}) collective-permute-start(bf16[768,384]{1,0:T(8,128)(2,1)S(1)} %collective-permute-done.10.refs_6_), channel_id=1, source_target_pairs={{0,1},{1,0},{2,3},{3,2},{4,5},{5,4},{6,7},{7,6},{8,9},{9,8},{10,11... | collective-permute-start | bytes 1769480 | tf_op jit(solution)/shard_map/ppermute | solution.py:40
  70.9 6.6 %collective-permute-start.16 = (bf16[128,768]{1,0:T(8,128)(2,1)S(1)}, bf16[128,768]{1,0:T(8,128)(2,1)S(1)}, u32[]{:S(2)}, u32[]{:S(2)}) collective-permute-start(bf16[128,768]{1,0:T(8,128)(2,1)S(1)} %get-tuple-element.111), channel_id=1, source_target_pairs={{0,6},{1,7},{2,0},{3,1},{4,2},{5,3},{6,4},{7,5},{8,14},{9,15},{10,... | collective-permute-start | bytes 589832 | tf_op jit(solution)/shard_map/ppermute | solution.py:40
  71.3 17.0 %collective-permute-start.17 = (bf16[128,768]{1,0:T(8,128)(2,1)S(1)}, bf16[128,768]{1,0:T(8,128)(2,1)S(1)}, u32[]{:S(2)}, u32[]{:S(2)}) collective-permute-start(bf16[128,768]{1,0:T(8,128)(2,1)S(1)} %get-tuple-element.112), channel_id=1, source_target_pairs={{0,4},{1,5},{2,6},{3,7},{4,0},{5,1},{6,2},{7,3},{8,12},{9,13},{10,... | collective-permute-start | bytes 589832 | tf_op jit(solution)/shard_map/ppermute | solution.py:40
  72.1 16.2 %collective-permute-start.18 = (bf16[128,768]{1,0:T(8,128)(2,1)S(1)}, bf16[128,768]{1,0:T(8,128)(2,1)S(1)}, u32[]{:S(2)}, u32[]{:S(2)}) collective-permute-start(bf16[128,768]{1,0:T(8,128)(2,1)S(1)} %get-tuple-element.113), channel_id=1, source_target_pairs={{0,2},{1,3},{2,4},{3,5},{4,6},{5,7},{6,0},{7,1},{8,10},{9,11},{10,... | collective-permute-start | bytes 589832 | tf_op jit(solution)/shard_map/ppermute | solution.py:40
  72.9 20.7 %collective-permute-start.22 = (bf16[4,2,64,384]{3,2,1,0:T(8,128)(2,1)S(1)}, bf16[4,2,64,384]{3,2,1,0:T(8,128)(2,1)S(1)}, u32[]{:S(2)}, u32[]{:S(2)}) collective-permute-start(bf16[4,2,64,384]{3,2,1,0:T(8,128)(2,1)S(1)} %get-tuple-element.115), channel_id=1, source_target_pairs={{0,1},{1,0},{2,3},{3,2},{4,5},{5,4},{6,7},{7,6},{8,9},{9,8},{10,11... | collective-permute-start | bytes 1179656 | tf_op jit(solution)/shard_map/ppermute | solution.py:40
  77.5 28.3 %collective-permute-start.21 = (bf16[768,384]{1,0:T(8,128)(2,1)S(1)}, bf16[768,384]{1,0:T(8,128)(2,1)S(1)}, u32[]{:S(2)}, u32[]{:S(2)}) collective-permute-start(bf16[768,384]{1,0:T(8,128)(2,1)S(1)} %collective-permute-done.15.refs_8_), channel_id=1, source_target_pairs={{0,1},{1,0},{2,3},{3,2},{4,5},{5,4},{6,7},{7,6},{8,9},{9,8},{10,11... | collective-permute-start | bytes 1769480 | tf_op jit(solution)/shard_map/ppermute | solution.py:40
  88.4 9.7 %collective-permute-start.24 = (bf16[128,768]{1,0:T(8,128)(2,1)S(1)}, bf16[128,768]{1,0:T(8,128)(2,1)S(1)}, u32[]{:S(2)}, u32[]{:S(2)}) collective-permute-start(bf16[128,768]{1,0:T(8,128)(2,1)S(1)} %add_convert_fusion.4.refs_0_), channel_id=1, source_target_pairs={{0,2},{1,3},{2,4},{3,5},{4,6},{5,7},{6,0},{7,1},{8,10},{9,11},{10,... | collective-permute-start | bytes 589832 | tf_op jit(solution)/shard_map/ppermute | solution.py:40
  88.7 15.0 %collective-permute-start.20 = (bf16[128,768]{1,0:T(8,128)(2,1)S(1)}, bf16[128,768]{1,0:T(8,128)(2,1)S(1)}, u32[]{:S(2)}, u32[]{:S(2)}) collective-permute-start(bf16[128,768]{1,0:T(8,128)(2,1)S(1)} %add_convert_fusion.4.refs_0_), channel_id=1, source_target_pairs={{0,4},{1,5},{2,6},{3,7},{4,0},{5,1},{6,2},{7,3},{8,12},{9,13},{10,... | collective-permute-start | bytes 589832 | tf_op jit(solution)/shard_map/ppermute | solution.py:40
  90.7 13.7 %collective-permute-start.27 = (bf16[128,768]{1,0:T(8,128)(2,1)S(1)}, bf16[128,768]{1,0:T(8,128)(2,1)S(1)}, u32[]{:S(2)}, u32[]{:S(2)}) collective-permute-start(bf16[128,768]{1,0:T(8,128)(2,1)S(1)} %add_convert_fusion.4.refs_0_), channel_id=1, source_target_pairs={{0,6},{1,7},{2,0},{3,1},{4,2},{5,3},{6,4},{7,5},{8,14},{9,15},{10,... | collective-permute-start | bytes 589832 | tf_op jit(solution)/shard_map/ppermute | solution.py:40
  93.6 19.5 %collective-permute-start.23 = (bf16[128,768]{1,0:T(8,128)(2,1)S(1)}, bf16[128,768]{1,0:T(8,128)(2,1)S(1)}, u32[]{:S(2)}, u32[]{:S(2)}) collective-permute-start(bf16[128,768]{1,0:T(8,128)(2,1)S(1)} %add_convert_fusion.4.refs_0_), channel_id=1, source_target_pairs={{0,1},{1,0},{2,3},{3,2},{4,5},{5,4},{6,7},{7,6},{8,9},{9,8},{10,11... | collective-permute-start | bytes 589832 | tf_op jit(solution)/shard_map/ppermute | solution.py:40
  98.1 15.0 %collective-permute-start.25 = (bf16[128,768]{1,0:T(8,128)(2,1)S(1)}, bf16[128,768]{1,0:T(8,128)(2,1)S(1)}, u32[]{:S(2)}, u32[]{:S(2)}) collective-permute-start(bf16[128,768]{1,0:T(8,128)(2,1)S(1)} %collective-permute-done.24.refs_2_), channel_id=1, source_target_pairs={{0,1},{1,0},{2,3},{3,2},{4,5},{5,4},{6,7},{7,6},{8,9},{9,8},{10,11... | collective-permute-start | bytes 589832 | tf_op jit(solution)/shard_map/ppermute | solution.py:40
  103.7 13.2 %collective-permute-start.26 = (bf16[128,768]{1,0:T(8,128)(2,1)S(1)}, bf16[128,768]{1,0:T(8,128)(2,1)S(1)}, u32[]{:S(2)}, u32[]{:S(2)}) collective-permute-start(bf16[128,768]{1,0:T(8,128)(2,1)S(1)} %collective-permute-done.20.refs_4_), channel_id=1, source_target_pairs={{0,1},{1,0},{2,3},{3,2},{4,5},{5,4},{6,7},{7,6},{8,9},{9,8},{10,11... | collective-permute-start | bytes 589832 | tf_op jit(solution)/shard_map/ppermute | solution.py:40
  104.4 12.6 %collective-permute-start.28 = (bf16[128,768]{1,0:T(8,128)(2,1)S(1)}, bf16[128,768]{1,0:T(8,128)(2,1)S(1)}, u32[]{:S(2)}, u32[]{:S(2)}) collective-permute-start(bf16[128,768]{1,0:T(8,128)(2,1)S(1)} %collective-permute-done.27.refs_6_), channel_id=1, source_target_pairs={{0,1},{1,0},{2,3},{3,2},{4,5},{5,4},{6,7},{7,6},{8,9},{9,8},{10,11... | collective-permute-start | bytes 589832 | tf_op jit(solution)/shard_map/ppermute | solution.py:40
  105.8 14.1 %collective-permute-start.31 = (bf16[2,2,64,384]{3,2,1,0:T(8,128)(2,1)S(1)}, bf16[2,2,64,384]{3,2,1,0:T(8,128)(2,1)S(1)}, u32[]{:S(2)}, u32[]{:S(2)}) collective-permute-start(bf16[2,2,64,384]{3,2,1,0:T(8,128)(2,1)S(1)} %get-tuple-element.128), channel_id=1, source_target_pairs={{0,6},{1,7},{2,0},{3,1},{4,2},{5,3},{6,4},{7,5},{8,14},{9,15},{10,... | collective-permute-start | bytes 589832 | tf_op jit(solution)/shard_map/ppermute | solution.py:40
  113.0 14.9 %collective-permute-start.30 = (bf16[2,2,64,384]{3,2,1,0:T(8,128)(2,1)S(1)}, bf16[2,2,64,384]{3,2,1,0:T(8,128)(2,1)S(1)}, u32[]{:S(2)}, u32[]{:S(2)}) collective-permute-start(bf16[2,2,64,384]{3,2,1,0:T(8,128)(2,1)S(1)} %get-tuple-element.127), channel_id=1, source_target_pairs={{0,4},{1,5},{2,6},{3,7},{4,0},{5,1},{6,2},{7,3},{8,12},{9,13},{10,... | collective-permute-start | bytes 589832 | tf_op jit(solution)/shard_map/ppermute | solution.py:40
  113.1 14.8 %collective-permute-start.29 = (bf16[2,2,64,384]{3,2,1,0:T(8,128)(2,1)S(1)}, bf16[2,2,64,384]{3,2,1,0:T(8,128)(2,1)S(1)}, u32[]{:S(2)}, u32[]{:S(2)}) collective-permute-start(bf16[2,2,64,384]{3,2,1,0:T(8,128)(2,1)S(1)} %get-tuple-element.126), channel_id=1, source_target_pairs={{0,2},{1,3},{2,4},{3,5},{4,6},{5,7},{6,0},{7,1},{8,10},{9,11},{10,... | collective-permute-start | bytes 589832 | tf_op jit(solution)/shard_map/ppermute | solution.py:40
  119.9 26.4 %copy-start.11 = (bf16[2,256,384]{2,1,0:T(8,128)(2,1)}, bf16[2,256,384]{2,1,0:T(8,128)(2,1)S(1)}, u32[]{:S(2)}) copy-start(bf16[2,256,384]{2,1,0:T(8,128)(2,1)S(1)} %get-tuple-element.161.refs_4_) | copy-start | bytes 1179652
  128.0 1.5 collective-permute-start.32
  128.0 13.3 %collective-permute-start.35 = (bf16[2,256,384]{2,1,0:T(8,128)(2,1)S(1)}, bf16[2,256,384]{2,1,0:T(8,128)(2,1)S(1)}, u32[]{:S(2)}, u32[]{:S(2)}) collective-permute-start(bf16[2,256,384]{2,1,0:T(8,128)(2,1)S(1)} %get-tuple-element.161.refs_4_), channel_id=1, source_target_pairs={{0,2},{1,3},{2,4},{3,5},{4,6},{5,7},{6,0},{7,1},{8,10},{9,11},{10,... | collective-permute-start | bytes 1179656 | tf_op jit(solution)/shard_map/ppermute | solution.py:40
  129.5 25.7 %collective-permute-start.37 = (bf16[4,2,2,64,384]{4,3,2,1,0:T(8,128)(2,1)S(1)}, bf16[4,2,2,64,384]{4,3,2,1,0:T(8,128)(2,1)S(1)}, u32[]{:S(2)}, u32[]{:S(2)}) collective-permute-start(bf16[4,2,2,64,384]{4,3,2,1,0:T(8,128)(2,1)S(1)} %pad_maximum_fusion.1.refs_0_), channel_id=1, source_target_pairs={{0,16},{8,24},{16,0},{24,8},{1,17},{9,25},{17,1},{25,9},{2,18},{10... | collective-permute-start | bytes 2359304 | tf_op jit(solution)/shard_map/ppermute | solution.py:44
  131.0 24.2 %collective-permute-start.38 = (bf16[4,2,2,64,384]{4,3,2,1,0:T(8,128)(2,1)S(1)}, bf16[4,2,2,64,384]{4,3,2,1,0:T(8,128)(2,1)S(1)}, u32[]{:S(2)}, u32[]{:S(2)}) collective-permute-start(bf16[4,2,2,64,384]{4,3,2,1,0:T(8,128)(2,1)S(1)} %pad_maximum_fusion.1.refs_0_), channel_id=1, source_target_pairs={{0,8},{8,0},{16,24},{24,16},{1,9},{9,1},{17,25},{25,17},{2,10},{10... | collective-permute-start | bytes 2359304 | tf_op jit(solution)/shard_map/ppermute | solution.py:44
  131.0 24.2 %collective-permute-start.33 = (bf16[3,128,768]{2,1,0:T(8,128)(2,1)S(1)}, bf16[3,128,768]{2,1,0:T(8,128)(2,1)S(1)}, u32[]{:S(2)}, u32[]{:S(2)}) collective-permute-start(bf16[3,128,768]{2,1,0:T(8,128)(2,1)S(1)} %get-tuple-element.148.own_ref), channel_id=1, source_target_pairs={{0,1},{1,0},{2,3},{3,2},{4,5},{5,4},{6,7},{7,6},{8,9},{9,8},{10,11... | collective-permute-start | bytes 1769480 | tf_op jit(solution)/shard_map/ppermute | solution.py:40
  131.4 23.8 %collective-permute-start.34 = (bf16[2,256,384]{2,1,0:T(8,128)(2,1)S(1)}, bf16[2,256,384]{2,1,0:T(8,128)(2,1)S(1)}, u32[]{:S(2)}, u32[]{:S(2)}) collective-permute-start(bf16[2,256,384]{2,1,0:T(8,128)(2,1)S(1)} %get-tuple-element.161.refs_4_), channel_id=1, source_target_pairs={{0,1},{1,0},{2,3},{3,2},{4,5},{5,4},{6,7},{7,6},{8,9},{9,8},{10,11... | collective-permute-start | bytes 1179656 | tf_op jit(solution)/shard_map/ppermute | solution.py:40
  141.3 16.9 %copy-start.13 = (bf16[2,256,384]{2,1,0:T(8,128)(2,1)}, bf16[2,256,384]{2,1,0:T(8,128)(2,1)S(1)}, u32[]{:S(2)}) copy-start(bf16[2,256,384]{2,1,0:T(8,128)(2,1)S(1)} %collective-permute-done.35.refs_5_) | copy-start | bytes 1179652
  141.3 13.9 %collective-permute-start.36 = (bf16[2,256,384]{2,1,0:T(8,128)(2,1)S(1)}, bf16[2,256,384]{2,1,0:T(8,128)(2,1)}, u32[]{:S(2)}, u32[]{:S(2)}) collective-permute-start(bf16[2,256,384]{2,1,0:T(8,128)(2,1)S(1)} %collective-permute-done.35.refs_5_), channel_id=1, source_target_pairs={{0,2},{1,3},{2,4},{3,5},{4,6},{5,7},{6,0},{7,1},{8,10},{9,11},{10,... | collective-permute-start | bytes 1179656 | tf_op jit(solution)/shard_map/ppermute | solution.py:40
  146.3 18.7 %copy-start.9 = (bf16[2,256,768]{2,1,0:T(8,128)(2,1)}, bf16[2,256,768]{2,1,0:T(8,128)(2,1)S(1)}, u32[]{:S(2)}) copy-start(bf16[2,256,768]{2,1,0:T(8,128)(2,1)S(1)} %get-tuple-element.136) | copy-start | bytes 2359300
  155.2 4.7 %collective-permute-start.39 = (bf16[2,256,1536]{2,1,0:T(8,128)(2,1)S(1)}, bf16[2,256,1536]{2,1,0:T(8,128)(2,1)S(1)}, u32[]{:S(2)}, u32[]{:S(2)}) collective-permute-start(bf16[2,256,1536]{2,1,0:T(8,128)(2,1)S(1)} %get-tuple-element.141), channel_id=1, source_target_pairs={{0,8},{8,0},{16,24},{24,16},{1,9},{9,1},{17,25},{25,17},{2,10},{10... | collective-permute-start | bytes 4718600 | tf_op jit(solution)/shard_map/ppermute | solution.py:44
  155.3 26.1 %collective-permute-start.41 = (bf16[2,256,384]{2,1,0:T(8,128)(2,1)}, bf16[2,256,384]{2,1,0:T(8,128)(2,1)S(1)}, u32[]{:S(2)}, u32[]{:S(2)}) collective-permute-start(bf16[2,256,384]{2,1,0:T(8,128)(2,1)} %collective-permute-done.36.refs_6_), channel_id=1, source_target_pairs={{0,1},{1,0},{2,3},{3,2},{4,5},{5,4},{6,7},{7,6},{8,9},{9,8},{10,11... | collective-permute-start | bytes 1179656 | tf_op jit(solution)/shard_map/ppermute | solution.py:40
  155.7 25.7 %collective-permute-start.42 = (bf16[2,256,384]{2,1,0:T(8,128)(2,1)}, bf16[2,256,384]{2,1,0:T(8,128)(2,1)}, u32[]{:S(2)}, u32[]{:S(2)}) collective-permute-start(bf16[2,256,384]{2,1,0:T(8,128)(2,1)} %collective-permute-done.36.refs_6_), channel_id=1, source_target_pairs={{0,2},{1,3},{2,4},{3,5},{4,6},{5,7},{6,0},{7,1},{8,10},{9,11},{10,... | collective-permute-start | bytes 1179656 | tf_op jit(solution)/shard_map/ppermute | solution.py:40
  158.2 18.4 %collective-permute-start.40 = (bf16[2,256,384]{2,1,0:T(8,128)(2,1)S(1)}, bf16[2,256,384]{2,1,0:T(8,128)(2,1)S(1)}, u32[]{:S(2)}, u32[]{:S(2)}) collective-permute-start(bf16[2,256,384]{2,1,0:T(8,128)(2,1)S(1)} %collective-permute-done.35.refs_5_), channel_id=1, source_target_pairs={{0,1},{1,0},{2,3},{3,2},{4,5},{5,4},{6,7},{7,6},{8,9},{9,8},{10,11... | collective-permute-start | bytes 1179656 | tf_op jit(solution)/shard_map/ppermute | solution.py:40
  161.1 25.6 %collective-permute-start.46 = (bf16[256,768]{1,0:T(8,128)(2,1)}, bf16[256,768]{1,0:T(8,128)(2,1)}, u32[]{:S(2)}, u32[]{:S(2)}) collective-permute-start(bf16[256,768]{1,0:T(8,128)(2,1)} %get-tuple-element.181), channel_id=1, source_target_pairs={{0,16},{8,24},{16,0},{24,8},{1,17},{9,25},{17,1},{25,9},{2,18},{10... | collective-permute-start | bytes 1179656 | tf_op jit(solution)/shard_map/ppermute | solution.py:44
  161.7 15.7 %copy-start.29 = (f32[256,2]{1,0:T(8,128)}, f32[256,2]{1,0:T(8,128)S(1)}, u32[]{:S(2)}) copy-start(f32[256,2]{1,0:T(8,128)S(1)} %add.76) | copy-start | bytes 6148
  161.7 13.1 %collective-permute-start.43 = (f32[256,2]{1,0:T(8,128)S(1)}, f32[256,2]{1,0:T(8,128)S(1)}, u32[]{:S(2)}, u32[]{:S(2)}) collective-permute-start(f32[256,2]{1,0:T(8,128)S(1)} %add.76), channel_id=1, source_target_pairs={{0,16},{8,24},{16,0},{24,8},{1,17},{9,25},{17,1},{25,9},{2,18},{10... | collective-permute-start | bytes 6152 | tf_op jit(solution)/shard_map/ppermute | solution.py:44
  165.0 11.6 %copy-start.19 = (f32[128,768]{1,0:T(8,128)}, f32[128,768]{1,0:T(8,128)S(1)}, u32[]{:S(2)}) copy-start(f32[128,768]{1,0:T(8,128)S(1)} %get-tuple-element.172) | copy-start | bytes 1179652
  165.0 12.3 %copy-start.27 = (bf16[128,768]{1,0:T(8,128)(2,1)}, bf16[128,768]{1,0:T(8,128)(2,1)S(1)}, u32[]{:S(2)}) copy-start(bf16[128,768]{1,0:T(8,128)(2,1)S(1)} %get-tuple-element.175) | copy-start | bytes 589828
  174.7 9.0 %collective-permute-start.44 = (bf16[128,768]{1,0:T(8,128)(2,1)}, bf16[128,768]{1,0:T(8,128)(2,1)}, u32[]{:S(2)}, u32[]{:S(2)}) collective-permute-start(bf16[128,768]{1,0:T(8,128)(2,1)} %get-tuple-element.150), channel_id=1, source_target_pairs={{0,2},{1,3},{2,4},{3,5},{4,6},{5,7},{6,0},{7,1},{8,10},{9,11},{10,... | collective-permute-start | bytes 589832 | tf_op jit(solution)/shard_map/ppermute | solution.py:40
  177.3 9.3 %collective-permute-start.45 = (bf16[128,768]{1,0:T(8,128)(2,1)}, bf16[128,768]{1,0:T(8,128)(2,1)}, u32[]{:S(2)}, u32[]{:S(2)}) collective-permute-start(bf16[128,768]{1,0:T(8,128)(2,1)} %get-tuple-element.151), channel_id=1, source_target_pairs={{0,6},{1,7},{2,0},{3,1},{4,2},{5,3},{6,4},{7,5},{8,14},{9,15},{10,... | collective-permute-start | bytes 589832 | tf_op jit(solution)/shard_map/ppermute | solution.py:40
  181.4 19.1 %copy-start.10 = (bf16[2,256,768]{2,1,0:T(8,128)(2,1)S(1)}, bf16[2,256,768]{2,1,0:T(8,128)(2,1)}, u32[]{:S(2)}) copy-start(bf16[2,256,768]{2,1,0:T(8,128)(2,1)} %copy-done.9) | copy-start | bytes 2359300
  186.7 11.9 %collective-permute-start.50 = (bf16[128,768]{1,0:T(8,128)(2,1)}, bf16[128,768]{1,0:T(8,128)(2,1)S(1)}, u32[]{:S(2)}, u32[]{:S(2)}) collective-permute-start(bf16[128,768]{1,0:T(8,128)(2,1)} %copy-done.27), channel_id=1, source_target_pairs={{0,4},{1,5},{2,6},{3,7},{4,0},{5,1},{6,2},{7,3},{8,12},{9,13},{10,... | collective-permute-start | bytes 589832 | tf_op jit(solution)/shard_map/ppermute | solution.py:40
  187.3 16.1 %collective-permute-start.48 = (bf16[4,2,2,64,384]{4,3,2,1,0:T(8,128)(2,1)S(1)}, bf16[4,2,2,64,384]{4,3,2,1,0:T(8,128)(2,1)S(1)}, u32[]{:S(2)}, u32[]{:S(2)}) collective-permute-start(bf16[4,2,2,64,384]{4,3,2,1,0:T(8,128)(2,1)S(1)} %collective-permute-done.37.refs_2_), channel_id=1, source_target_pairs={{0,8},{8,0},{16,24},{24,16},{1,9},{9,1},{17,25},{25,17},{2,10},{10... | collective-permute-start | bytes 2359304 | tf_op jit(solution)/shard_map/ppermute | solution.py:44
  187.3 18.9 %collective-permute-start.49 = (bf16[2,256,384]{2,1,0:T(8,128)(2,1)}, bf16[2,256,384]{2,1,0:T(8,128)(2,1)S(1)}, u32[]{:S(2)}, u32[]{:S(2)}) collective-permute-start(bf16[2,256,384]{2,1,0:T(8,128)(2,1)} %collective-permute-done.42.refs_7_), channel_id=1, source_target_pairs={{0,1},{1,0},{2,3},{3,2},{4,5},{5,4},{6,7},{7,6},{8,9},{9,8},{10,11... | collective-permute-start | bytes 1179656 | tf_op jit(solution)/shard_map/ppermute | solution.py:40
  188.9 11.7 %collective-permute-start.47 = (bf16[256,768]{1,0:T(8,128)(2,1)}, bf16[256,768]{1,0:T(8,128)(2,1)S(1)}, u32[]{:S(2)}, u32[]{:S(2)}) collective-permute-start(bf16[256,768]{1,0:T(8,128)(2,1)} %get-tuple-element.156), channel_id=1, source_target_pairs={{0,16},{8,24},{16,0},{24,8},{1,17},{9,25},{17,1},{25,9},{2,18},{10... | collective-permute-start | bytes 1179656 | tf_op jit(solution)/shard_map/ppermute | solution.py:44
  (18 other events, 101.2 us)

commit v8 on v6

--- a/solution.py
+++ b/solution.py
@@ -816,50 +816,51 @@
         caption_lens,
         pairs,
     )
-    slots, both, row_sums, over_z = after((slots, both, row_sums, over_z))
-    tiles = jnp.stack(over_z)
 
     def chain(blocks, steps):
         for _ in range(steps):
             blocks.append(fsend(blocks[-1], 1, 0))
         return blocks
 
-    def joined(two):
-        return jnp.stack(two).reshape(-1, tokens, width_local)
-
     side_slots = fsend(slots, 0, 1)
-    side_own = fsend(both, 0, 1)
-    late = chain([both], 2)
+    side_mine = fsend(both, 0, 1)
+    first, over_z = after((both, over_z))
+    tiles = jnp.stack(over_z)
+    late = chain([first], 2)
     sums_core = gsend(row_sums, 1)
-    attended, tiles = after((attended, tiles), sums_core)
+    row_sums = row_sums + sums_core
+    attended, tiles = after((attended, tiles), row_sums)
     tiles_x = gsend(tiles, 2)
     own, far_piece, away = project_back(attended, d_queries, blocks, place, pairs, part)
-    two = joined(late[1:3])
-    stage = (side_slots, side_own, late, sums_core, tiles_x, two, away)
-    side_slots, side_own, late, sums_core, tiles_x, two, away = after(stage)
-
-    side_two = fsend(two, 0, 1)
+    tiles_core = gsend(tiles, 1)
+    stage = (side_slots, side_mine, late, row_sums, tiles_x, tiles_core, away)
+    side_slots, side_mine, late, row_sums, tiles_x, tiles_core, away = after(stage)
+
+    sides = [fsend(block, 0, 1) for block in late[1:3]]
     late = chain(list(late), pairs - 3)
-    row_sums = row_sums + sums_core
+    got = gsend(away, 1)
+    width = model_width // 4
+    sent = [
+        (far_piece[k].astype(F32) + got[k, :, width:].astype(F32)).astype(BF) for k in range(2)
+    ]
     sums_x = gsend(row_sums, 2)
-    got = gsend(away, 1)
-    tiles_core = gsend(tiles, 1)
-    width = model_width // 4
-    sent = (far_piece.astype(F32) + got[:, :, width:].astype(F32)).astype(BF)
-    far_sum = gsend(sent, 2)
+    far_out = gsend(after(sent[0], sums_x), 2)
+    terms = caption_terms(
+        after(slots, sent[0]), side_slots, place, video_counts, sample_caption, tokens, pairs
+    )
+    kv_parts = [fsend(terms[far], far, 0) for far in range(1, pairs, 2)]
+    stage = (sides, late, tiles_x, kv_parts, terms, far_out, sent[1])
+    sides, late, tiles_x, kv_parts, terms, far_out, sent_d = after(stage)
+
+    here = [((block, 0),) for block in late]
     tiles = [tiles, tiles_core, tiles_x, gsend(tiles_x, 1)]
-    terms = caption_terms(
-        slots, side_slots, place, video_counts, sample_caption, tokens, pairs
-    )
-    kv_parts = [fsend(terms[far], far, 0) for far in range(1, pairs, 2)]
-    stage = (side_two, late, sums_x, sent, tiles, kv_parts, terms)
-    side_two, late, sums_x, _, tiles, kv_parts, terms = after(stage)
-
-    here = [((block, 0),) for block in late]
-    there = [((side_own, 0),), ((side_two, 0),), ((side_two, 2),)]
+    there = [((block, 0),) for block in (side_mine, *sides)]
     there += [((fsend(block, 0, 1), 0),) for block in late[3:]]
     known = weight_grads(tiles, here + there[:3], None, pairs)
-    total = own.astype(F32) + got[:, :, :width].astype(F32) + far_sum.astype(F32)
+    total = [
+        own[k].astype(F32) + got[k, :, :width].astype(F32) + far.astype(F32)
+        for k, far in enumerate((far_out, after(gsend(sent_d, 2), known)))
+    ]
     row_sums = (row_sums + sums_x) / model_width
     video = quarter(video_states, g, 1).astype(F32)
     updated = (video + total[0]).astype(BF)

time: 196 us -> 198 us (1.010)
  waiting for transfers between devices: 69.2 us -> 86.2 us
  starting transfers between devices: 64.2 us -> 59.1 us
  local copies, waits for them, and re-layouts: 9.17 us -> 4.21 us
  other arithmetic: 13.5 us -> 10.1 us
    ppermute x36 -> x37, waiting for transfers between devices: 55.3 us -> 72.2 us  [fsend(): return lax.ppermute(block, 'fsdp', perm)]
    ppermute x36 -> x37, starting transfers between devices: 56.5 us -> 52.2 us  [fsend(): return lax.ppermute(block, 'fsdp', perm)]
    unnamed x73 -> x79, local copies, waits for them, and re-layouts: 7.21 us -> 3.27 us
    another operation x1 -> x0, other arithmetic: 2.01 us -> none  [joined(): return jnp.stack(two).reshape(-1, tokens, width_local)]
    ppermute x12 -> x13, starting transfers between devices: 7.73 us -> 6.87 us  [gsend(): lax.ppermute(block, 'grp', [(s, s ^ flip) for s in range(lax.axis_size('g...]
    ppermute x12 -> x13, waiting for transfers between devices: 13.9 us -> 14 us  [gsend(): lax.ppermute(block, 'grp', [(s, s ^ flip) for s in range(lax.axis_size('g...]
  transfers between devices with their start and end apart: 48 -> 50, of which waited for: 18 -> 18; matrix products, arithmetic and copies ran while one was open for 7% -> 4% of each run, Pallas kernels for 20% -> 18%
where the time goes in v8:
time: 198 us; the launch traced here: 197 us
  waiting for transfers between devices  86.2 us (44%)
  starting transfers between devices  59.1 us (30%)
  Pallas kernels  36.3 us (18%)
  other arithmetic  10.1 us (5%)
  local copies, waits for them, and re-layouts  4.21 us (2%)
    ppermute x37, waiting for transfers between devices, fsend(): return lax.ppermute(block, 'fsdp', perm)  72.2 us
    ppermute x37, starting transfers between devices, fsend(): return lax.ppermute(block, 'fsdp', perm)  52.2 us
    pallas_call x9, Pallas kernels, call(): pl.pallas_call(body, out_shape=out_shape, in_specs=specs, out_specs=jax.t...  21.2 us
    ppermute x13, waiting for transfers between devices, gsend(): lax.ppermute(block, 'grp', [(s, s ^ flip) for s in range(lax.axis_size('g...  14 us
    pallas_call x1, Pallas kernels, project_text(): pl.pallas_call(body, grid=(steps,), out_shape=shaped((rows, 3 * width)),...  7.96 us
    pallas_call x1, Pallas kernels, attend_text(): pl.pallas_call(body, grid=(steps,), out_shape=[shaped((rows // 2, depth))...  7.14 us
    ppermute x13, starting transfers between devices, gsend(): lax.ppermute(block, 'grp', [(s, s ^ flip) for s in range(lax.axis_size('g...  6.87 us
  transfers between devices with their start and end apart: 50, of which 18 were waited for; matrix products, arithmetic and copies ran while one was open for 4% of the time, Pallas kernels for 18%

profile of v8, /device:TPU:0, one launch (start us, length us, event | category | flops | bytes accessed | tf_op | source)
XLA Modules:
  0.0 197.2 jit_solution(5944226614865320461)
XLA Ops:
  0.6 3.0 %collective-permute-start.2 = (bf16[512,384]{1,0:T(8,128)(2,1)}, bf16[512,384]{1,0:T(8,128)(2,1)S(1)}, u32[]{:S(2)}, u32[]{:S(2)}) collective-permute-start(bf16[512,384]{1,0:T(8,128)(2,1)} %refs_4_.1), channel_id=1, source_target_pairs={{0,1},{1,0},{2,3},{3,2},{4,5},{5,4},{6,7},{7,6},{8,9},{9,8},{10,11... | collective-permute-start | bytes 1179656 | tf_op jit(solution)/shard_map/ppermute | solution.py:40
  3.7 2.0 %collective-permute-start = (bf16[384,384]{1,0:T(8,128)(2,1)}, bf16[384,384]{1,0:T(8,128)(2,1)S(1)}, u32[]{:S(2)}, u32[]{:S(2)}) collective-permute-start(bf16[384,384]{1,0:T(8,128)(2,1)} %refs_0_.3), channel_id=1, source_target_pairs={{0,2},{1,3},{2,4},{3,5},{4,6},{5,7},{6,0},{7,1},{8,10},{9,11},{10,... | collective-permute-start | bytes 884744 | tf_op jit(solution)/shard_map/ppermute | solution.py:40
  5.7 1.6 collective-permute-start.1
  7.3 8.0 %shard_map.208.qkv_ref = bf16[128,1536]{1,0:T(8,128)(2,1)} custom-call(bf16[128,4096]{1,0:T(8,128)(2,1)} %bitcast.40, f32[1,4096]{1,0:T(1,128)} %bitcast.53, bf16[4096,512]{1,0:T(8,128)(2,1)} %wq_ref.1, bf16[4096,512]{1,0:T(8,128)(2,1)} %wk_ref.1, bf16[4096,512]{1,0:T(8,128)(2,1)} %wv_ref.1), custom_call_target="tpu_custom_call" | custom-call | flops 1 | bytes 1 | tf_op jit(solution)/shard_map/pallas_call | solution.py:350
  15.9 7.1 %shard_map.209 = (bf16[64,4096]{1,0:T(8,128)(2,1)}, bf16[64,4096]{1,0:T(8,128)(2,1)}) custom-call(s32[3]{0:T(128)} %pad_add_fusion.place_ref, s32[8]{0:T(128)} %len_ref.3, bf16[128,1536]{1,0:T(8,128)(2,1)} %shard_map.208.qkv_ref, f32[8,128,128]{2,1,0:T(8,128)} %bias_ref.1, bf16[512,4096]{1,0:T(8,128)(2,1)} %out_ref.1), custom_call_target="tpu_custom_call" | custom-call | flops 1 | bytes 1 | tf_op jit(solution)/shard_map/pallas_call | solution.py:394
  23.1 0.8 copy-done.23
  24.2 1.7 collective-permute-start.9
  25.9 1.2 pad_maximum_fusion
  27.0 1.6 collective-permute-start.13
  28.7 1.6 collective-permute-start.5
  30.3 2.7 %shard_map.210 = (bf16[256,3072]{1,0:T(8,128)(2,1)S(1)}, f32[256,1]{1,0:T(8,128)S(1)}, f32[256,1]{1,0:T(8,128)S(1)}, bf16[4,2,64,384]{3,2,1,0:T(8,128)(2,1)S(1)}, bf16[4,2,64,384]{3,2,1,0:T(8,128)(2,1)S(1)}) custom-call(s32[3]{0:T(128)S(1)} %copy-done.27, bf16[256,3072]{1,0:T(8,128)(2,1)S(1)} %copy-done.6, bf16[256,3072]{1,0:T(8,128)(2,1)S(1)} %copy-done), custom_call_target="tpu_custom_call" | custom-call | flops 1 | bytes 1 | tf_op jit(solution)/shard_map/pallas_call | solution.py:307
  33.7 3.1 %collective-permute-done.5.far_ref = bf16[32,4096]{1,0:T(8,128)(2,1)S(1)} collective-permute-done((bf16[32,4096]{1,0:T(8,128)(2,1)S(1)}, bf16[32,4096]{1,0:T(8,128)(2,1)S(1)}, u32[]{:S(2)}, u32[]{:S(2)}) %collective-permute-start.5) | collective-permute-done | bytes 262176 | tf_op jit(solution)/shard_map/ppermute | solution.py:44
  36.8 0.8 shard_map.211
  38.2 2.4 %collective-permute-start.7 = (bf16[32,1024]{1,0:T(8,128)(2,1)S(1)}, bf16[32,1024]{1,0:T(8,128)(2,1)S(1)}, u32[]{:S(2)}, u32[]{:S(2)}) collective-permute-start(bf16[32,1024]{1,0:T(8,128)(2,1)S(1)} %get-tuple-element.98), channel_id=1, source_target_pairs={{0,4},{1,5},{2,6},{3,7},{4,0},{5,1},{6,2},{7,3},{8,12},{9,13},{10,... | collective-permute-start | bytes 196616 | tf_op jit(solution)/shard_map/ppermute | solution.py:40
  40.5 1.3 collective-permute-start.8
  41.9 2.7 %collective-permute-done.6 = bf16[32,1024]{1,0:T(8,128)(2,1)S(1)} collective-permute-done((bf16[32,1024]{1,0:T(8,128)(2,1)S(1)}, bf16[32,1024]{1,0:T(8,128)(2,1)S(1)}, u32[]{:S(2)}, u32[]{:S(2)}) %collective-permute-start.6) | collective-permute-done | bytes 65568 | tf_op jit(solution)/shard_map/ppermute | solution.py:40
  44.6 1.4 collective-permute-done.7
  46.0 1.9 collective-permute-start.14
  48.0 1.5 collective-permute-start.11
  49.5 6.5 %collective-permute-done.11.refs_2_ = bf16[4,32,1024]{2,1,0:T(8,128)(2,1)S(1)} collective-permute-done((bf16[4,32,1024]{2,1,0:T(8,128)(2,1)S(1)}, bf16[4,32,1024]{2,1,0:T(8,128)(2,1)S(1)}, u32[]{:S(2)}, u32[]{:S(2)}) %collective-permute-start.11) | collective-permute-done | bytes 262176 | tf_op jit(solution)/shard_map/ppermute | solution.py:44
  56.4 1.6 collective-permute-start.18
  58.0 1.8 shard_map.212
  59.8 3.2 %collective-permute-done.14.refs_6_ = bf16[768,384]{1,0:T(8,128)(2,1)S(1)} collective-permute-done((bf16[768,384]{1,0:T(8,128)(2,1)S(1)}, bf16[768,384]{1,0:T(8,128)(2,1)S(1)}, u32[]{:S(2)}, u32[]{:S(2)}) %collective-permute-start.14) | collective-permute-done | bytes 589856 | tf_op jit(solution)/shard_map/ppermute | solution.py:40
  63.0 1.6 collective-permute-start.16
  65.1 1.6 collective-permute-start.21
  66.6 3.1 %collective-permute-done.15 = bf16[128,768]{1,0:T(8,128)(2,1)S(1)} collective-permute-done((bf16[128,768]{1,0:T(8,128)(2,1)S(1)}, bf16[128,768]{1,0:T(8,128)(2,1)S(1)}, u32[]{:S(2)}, u32[]{:S(2)}) %collective-permute-start.15) | collective-permute-done | bytes 196640 | tf_op jit(solution)/shard_map/ppermute | solution.py:40
  69.8 1.6 collective-permute-start.20
  71.3 10.0 %collective-permute-done.16 = bf16[128,768]{1,0:T(8,128)(2,1)S(1)} collective-permute-done((bf16[128,768]{1,0:T(8,128)(2,1)S(1)}, bf16[128,768]{1,0:T(8,128)(2,1)S(1)}, u32[]{:S(2)}, u32[]{:S(2)}) %collective-permute-start.16) | collective-permute-done | bytes 196640 | tf_op jit(solution)/shard_map/ppermute | solution.py:40
  81.5 1.5 collective-permute-start.19
  83.0 2.8 %collective-permute-start.26 = (bf16[128,768]{1,0:T(8,128)(2,1)S(1)}, bf16[128,768]{1,0:T(8,128)(2,1)S(1)}, u32[]{:S(2)}, u32[]{:S(2)}) collective-permute-start(bf16[128,768]{1,0:T(8,128)(2,1)S(1)} %add_convert_fusion.4.refs_0_), channel_id=1, source_target_pairs={{0,6},{1,7},{2,0},{3,1},{4,2},{5,3},{6,4},{7,5},{8,14},{9,15},{10,... | collective-permute-start | bytes 589832 | tf_op jit(solution)/shard_map/ppermute | solution.py:40
  85.8 1.6 collective-permute-start.22
  87.4 3.7 %collective-permute-done.23.refs_2_ = bf16[128,768]{1,0:T(8,128)(2,1)S(1)} collective-permute-done((bf16[128,768]{1,0:T(8,128)(2,1)S(1)}, bf16[128,768]{1,0:T(8,128)(2,1)S(1)}, u32[]{:S(2)}, u32[]{:S(2)}) %collective-permute-start.23) | collective-permute-done | bytes 196640 | tf_op jit(solution)/shard_map/ppermute | solution.py:40
  91.1 1.6 collective-permute-start.24
  92.7 4.2 %collective-permute-done.19.refs_4_ = bf16[128,768]{1,0:T(8,128)(2,1)S(1)} collective-permute-done((bf16[128,768]{1,0:T(8,128)(2,1)S(1)}, bf16[128,768]{1,0:T(8,128)(2,1)S(1)}, u32[]{:S(2)}, u32[]{:S(2)}) %collective-permute-start.19) | collective-permute-done | bytes 196640 | tf_op jit(solution)/shard_map/ppermute | solution.py:40
  96.9 1.6 collective-permute-start.25
  99.0 6.5 %collective-permute-start.30 = (bf16[2,2,64,384]{3,2,1,0:T(8,128)(2,1)S(1)}, bf16[2,2,64,384]{3,2,1,0:T(8,128)(2,1)S(1)}, u32[]{:S(2)}, u32[]{:S(2)}) collective-permute-start(bf16[2,2,64,384]{3,2,1,0:T(8,128)(2,1)S(1)} %get-tuple-element.123), channel_id=1, source_target_pairs={{0,6},{1,7},{2,0},{3,1},{4,2},{5,3},{6,4},{7,5},{8,14},{9,15},{10,... | collective-permute-start | bytes 589832 | tf_op jit(solution)/shard_map/ppermute | solution.py:40
  106.2 2.8 %shard_map.213 = (bf16[256,384]{1,0:T(8,128)(2,1)S(1)}, bf16[256,384]{1,0:T(8,128)(2,1)S(1)}, f32[1,384]{1,0:T(1,128)S(1)}) custom-call(s32[3]{0:T(128)S(1)} %copy-done.27, bf16[256,3072]{1,0:T(8,128)(2,1)S(1)} %get-tuple-element.94.normed_ref, bf16[256,3072]{1,0:T(8,128)(2,1)S(1)} %copy-done, bf16[384,384]{1,0:T(8,128)(2,1)S(1)} %copy-done.4, ...), custom_call_target="tpu_custom_call" | custom-call | flops 1 | bytes 1 | tf_op jit(solution)/shard_map/pallas_call | solution.py:307
  109.6 2.8 %shard_map.214 = (bf16[2,256,384]{2,1,0:T(8,128)(2,1)S(1)}, bf16[256,384]{1,0:T(8,128)(2,1)S(1)}, bf16[256,384]{1,0:T(8,128)(2,1)S(1)}, f32[256,2]{1,0:T(8,128)S(1)}, bf16[3,128,768]{2,1,0:T(8,128)(2,1)S(1)}) custom-call(s32[3]{0:T(128)S(1)} %copy-done.27, s32[8]{0:T(128)S(1)} %copy-done.29, s32[8]{0:T(128)S(1)} %copy-done.30, s32[8]{0:T(128)S(1)} %copy-done.31, ...), custom_call_target="tpu_custom_call" | custom-call | flops 1 | bytes 1 | tf_op jit(solution)/shard_map/pallas_call | solution.py:307
  112.5 1.3 collective-permute-done.31
  113.9 8.0 %collective-permute-done.29 = bf16[2,2,64,384]{3,2,1,0:T(8,128)(2,1)S(1)} collective-permute-done((bf16[2,2,64,384]{3,2,1,0:T(8,128)(2,1)S(1)}, bf16[2,2,64,384]{3,2,1,0:T(8,128)(2,1)S(1)}, u32[]{:S(2)}, u32[]{:S(2)}) %collective-permute-start.29) | collective-permute-done | bytes 196640 | tf_op jit(solution)/shard_map/ppermute | solution.py:40
  122.0 1.6 collective-permute-start.36
  123.6 1.4 collective-permute-start.32
  125.6 9.4 %collective-permute-done.34.refs_5_ = bf16[2,256,384]{2,1,0:T(8,128)(2,1)S(1)} collective-permute-done((bf16[2,256,384]{2,1,0:T(8,128)(2,1)S(1)}, bf16[2,256,384]{2,1,0:T(8,128)(2,1)S(1)}, u32[]{:S(2)}, u32[]{:S(2)}) %collective-permute-start.34) | collective-permute-done | bytes 393248 | tf_op jit(solution)/shard_map/ppermute | solution.py:40
  135.0 4.4 %shard_map.215 = (bf16[2,256,768]{2,1,0:T(8,128)(2,1)S(1)}, bf16[2,256,768]{2,1,0:T(8,128)(2,1)S(1)}, bf16[2,256,1536]{2,1,0:T(8,128)(2,1)S(1)}) custom-call(s32[3]{0:T(128)S(1)} %copy-done.27, bf16[256,384]{1,0:T(8,128)(2,1)S(1)} %get-tuple-element.129.att_ref, bf16[256,384]{1,0:T(8,128)(2,1)S(1)} %get-tuple-element.130.dq_ref, ...), custom_call_target="tpu_custom_call" | custom-call | flops 1 | bytes 1 | tf_op jit(solution)/shard_map/pallas_call | solution.py:307
  139.4 8.4 %collective-permute-done.33.refs_8_ = bf16[2,256,384]{2,1,0:T(8,128)(2,1)S(1)} collective-permute-done((bf16[2,256,384]{2,1,0:T(8,128)(2,1)S(1)}, bf16[2,256,384]{2,1,0:T(8,128)(2,1)S(1)}, u32[]{:S(2)}, u32[]{:S(2)}) %collective-permute-start.33) | collective-permute-done | bytes 393248 | tf_op jit(solution)/shard_map/ppermute | solution.py:40
  147.9 1.5 collective-permute-start.40
  149.4 2.5 %collective-permute-start.41 = (bf16[2,256,384]{2,1,0:T(8,128)(2,1)}, bf16[2,256,384]{2,1,0:T(8,128)(2,1)}, u32[]{:S(2)}, u32[]{:S(2)}) collective-permute-start(bf16[2,256,384]{2,1,0:T(8,128)(2,1)} %collective-permute-done.35.refs_6_), channel_id=1, source_target_pairs={{0,2},{1,3},{2,4},{3,5},{4,6},{5,7},{6,0},{7,1},{8,10},{9,11},{10,... | collective-permute-start | bytes 1179656 | tf_op jit(solution)/shard_map/ppermute | solution.py:40
  152.9 1.2 fusion.9
  154.1 3.1 %collective-permute-done.44 = f32[256,2]{1,0:T(8,128)S(1)} collective-permute-done((f32[256,2]{1,0:T(8,128)S(1)}, f32[256,2]{1,0:T(8,128)S(1)}, u32[]{:S(2)}, u32[]{:S(2)}) %collective-permute-start.44) | collective-permute-done | bytes 2080 | tf_op jit(solution)/shard_map/ppermute | solution.py:44
  157.7 1.7 shard_map.216
  159.8 8.2 %collective-permute-done.39.refs_9_ = bf16[2,256,384]{2,1,0:T(8,128)(2,1)S(1)} collective-permute-done((bf16[2,256,384]{2,1,0:T(8,128)(2,1)S(1)}, bf16[2,256,384]{2,1,0:T(8,128)(2,1)S(1)}, u32[]{:S(2)}, u32[]{:S(2)}) %collective-permute-start.39) | collective-permute-done | bytes 393248 | tf_op jit(solution)/shard_map/ppermute | solution.py:40
  168.0 0.8 copy-done.16
  168.8 3.8 %collective-permute-start.43 = (bf16[128,768]{1,0:T(8,128)(2,1)}, bf16[128,768]{1,0:T(8,128)(2,1)}, u32[]{:S(2)}, u32[]{:S(2)}) collective-permute-start(bf16[128,768]{1,0:T(8,128)(2,1)} %get-tuple-element.145), channel_id=1, source_target_pairs={{0,6},{1,7},{2,0},{3,1},{4,2},{5,3},{6,4},{7,5},{8,14},{9,15},{10,... | collective-permute-start | bytes 589832 | tf_op jit(solution)/shard_map/ppermute | solution.py:40
  172.6 1.0 reduce
  173.6 1.0 reduce.2
  174.7 2.2 %collective-permute-done.43 = bf16[128,768]{1,0:T(8,128)(2,1)} collective-permute-done((bf16[128,768]{1,0:T(8,128)(2,1)}, bf16[128,768]{1,0:T(8,128)(2,1)}, u32[]{:S(2)}, u32[]{:S(2)}) %collective-permute-start.43) | collective-permute-done | bytes 196640 | tf_op jit(solution)/shard_map/ppermute | solution.py:40
  176.9 1.3 collective-permute-start.49
  178.2 1.0 add_multiply_fusion
  179.4 0.8 collective-permute-start.48
  180.7 7.1 %collective-permute-done.49 = bf16[128,768]{1,0:T(8,128)(2,1)S(1)} collective-permute-done((bf16[128,768]{1,0:T(8,128)(2,1)}, bf16[128,768]{1,0:T(8,128)(2,1)S(1)}, u32[]{:S(2)}, u32[]{:S(2)}) %collective-permute-start.49) | collective-permute-done | bytes 196640 | tf_op jit(solution)/shard_map/ppermute | solution.py:40
  187.8 1.2 fusion.10
  189.8 2.8 %shard_map.217 = (f32[384,384]{1,0:T(8,128)S(1)}, f32[384,384]{1,0:T(8,128)S(1)}) custom-call(bf16[4,2,2,64,384]{4,3,2,1,0:T(8,128)(2,1)S(1)} %pad_maximum_fusion.1.refs_0_, bf16[4,2,2,64,384]{4,3,2,1,0:T(8,128)(2,1)S(1)} %copy-done.3, bf16[4,2,2,64,384]{4,3,2,1,0:T(8,128)(2,1)S(1)} %collective-permute-done.36.refs_2_, ...), custom_call_target="tpu_custom_call" | custom-call | flops 1 | bytes 1 | tf_op jit(solution)/shard_map/pallas_call | solution.py:307
  192.7 1.3 shard_map.218
  194.7 2.5 %fusion.6 = (bf16[256,768]{1,0:T(8,128)(2,1)}, bf16[256,768]{1,0:T(8,128)(2,1)}) fusion(bf16[256,768]{1,0:T(8,128)(2,1)S(1)} %collective-permute-done.46, bf16[2,256,1536]{2,1,0:T(8,128)(2,1)S(1)} %copy-done.34, f32[256]{0:T(256)S(1)} %get-tuple-element.173, f32[256]{0:T(256)S(1)} %reduce.2, f32[256]{0:T(256)S(1)} %get-tuple-element.172, ...), kind=kLoop, calls=%fused_computation.15 | loop fusion | flops 4325376 | bytes 3936260 | tf_op jit(solution)/shard_map/convert_element_type | solution.py:871
  (143 shorter events, 10.3 us)
Async XLA Ops:
  0.6 22.5 %collective-permute-start.2 = (bf16[512,384]{1,0:T(8,128)(2,1)}, bf16[512,384]{1,0:T(8,128)(2,1)S(1)}, u32[]{:S(2)}, u32[]{:S(2)}) collective-permute-start(bf16[512,384]{1,0:T(8,128)(2,1)} %refs_4_.1), channel_id=1, source_target_pairs={{0,1},{1,0},{2,3},{3,2},{4,5},{5,4},{6,7},{7,6},{8,9},{9,8},{10,11... | collective-permute-start | bytes 1179656 | tf_op jit(solution)/shard_map/ppermute | solution.py:40
  3.7 19.4 %collective-permute-start.3 = (bf16[512,384]{1,0:T(8,128)(2,1)}, bf16[512,384]{1,0:T(8,128)(2,1)S(1)}, u32[]{:S(2)}, u32[]{:S(2)}) collective-permute-start(bf16[512,384]{1,0:T(8,128)(2,1)} %refs_5_.1), channel_id=1, source_target_pairs={{0,1},{1,0},{2,3},{3,2},{4,5},{5,4},{6,7},{7,6},{8,9},{9,8},{10,11... | collective-permute-start | bytes 1179656 | tf_op jit(solution)/shard_map/ppermute | solution.py:40
  3.7 19.3 %collective-permute-start = (bf16[384,384]{1,0:T(8,128)(2,1)}, bf16[384,384]{1,0:T(8,128)(2,1)S(1)}, u32[]{:S(2)}, u32[]{:S(2)}) collective-permute-start(bf16[384,384]{1,0:T(8,128)(2,1)} %refs_0_.3), channel_id=1, source_target_pairs={{0,2},{1,3},{2,4},{3,5},{4,6},{5,7},{6,0},{7,1},{8,10},{9,11},{10,... | collective-permute-start | bytes 884744 | tf_op jit(solution)/shard_map/ppermute | solution.py:40
  5.7 17.3 %collective-permute-start.1 = (bf16[384,384]{1,0:T(8,128)(2,1)}, bf16[384,384]{1,0:T(8,128)(2,1)S(1)}, u32[]{:S(2)}, u32[]{:S(2)}) collective-permute-start(bf16[384,384]{1,0:T(8,128)(2,1)} %refs_1_.3), channel_id=1, source_target_pairs={{0,2},{1,3},{2,4},{3,5},{4,6},{5,7},{6,0},{7,1},{8,10},{9,11},{10,... | collective-permute-start | bytes 884744 | tf_op jit(solution)/shard_map/ppermute | solution.py:40
  23.9 4.7 %collective-permute-start.4 = (bf16[64,4096]{1,0:T(8,128)(2,1)}, bf16[64,4096]{1,0:T(8,128)(2,1)S(1)}, u32[]{:S(2)}, u32[]{:S(2)}) collective-permute-start(bf16[64,4096]{1,0:T(8,128)(2,1)} %get-tuple-element.92), channel_id=1, source_target_pairs={{0,8},{8,0},{16,24},{24,16},{1,9},{9,1},{17,25},{25,17},{2,10},{10... | collective-permute-start | bytes 1572872 | tf_op jit(solution)/shard_map/ppermute | solution.py:44
  24.2 21.8 %collective-permute-start.9 = (bf16[768,384]{1,0:T(8,128)(2,1)S(1)}, bf16[768,384]{1,0:T(8,128)(2,1)S(1)}, u32[]{:S(2)}, u32[]{:S(2)}) collective-permute-start(bf16[768,384]{1,0:T(8,128)(2,1)S(1)} %constant_dynamic-update-slice_fusion.refs_3_), channel_id=1, source_target_pairs={{0,2},{1,3},{2,4},{3,5},{4,6},{5,7},{6,0},{7,1},{8,10},{9,11},{10,... | collective-permute-start | bytes 1769480 | tf_op jit(solution)/shard_map/ppermute | solution.py:40
  27.0 30.9 %collective-permute-start.13 = (bf16[1536,384]{1,0:T(8,128)(2,1)S(1)}, bf16[1536,384]{1,0:T(8,128)(2,1)S(1)}, u32[]{:S(2)}, u32[]{:S(2)}) collective-permute-start(bf16[1536,384]{1,0:T(8,128)(2,1)S(1)} %pad_maximum_fusion), channel_id=1, source_target_pairs={{0,1},{1,0},{2,3},{3,2},{4,5},{5,4},{6,7},{7,6},{8,9},{9,8},{10,11... | collective-permute-start | bytes 3538952 | tf_op jit(solution)/shard_map/ppermute | solution.py:40
  28.7 8.1 %collective-permute-start.5 = (bf16[32,4096]{1,0:T(8,128)(2,1)S(1)}, bf16[32,4096]{1,0:T(8,128)(2,1)S(1)}, u32[]{:S(2)}, u32[]{:S(2)}) collective-permute-start(bf16[32,4096]{1,0:T(8,128)(2,1)S(1)} %add_convert_fusion.2), channel_id=1, source_target_pairs={{0,16},{8,24},{16,0},{24,8},{1,17},{9,25},{17,1},{25,9},{2,18},{10... | collective-permute-start | bytes 786440 | tf_op jit(solution)/shard_map/ppermute | solution.py:44
  33.7 71.9 %copy-start.25 = (f32[256,1]{1,0:T(8,128)}, f32[256,1]{1,0:T(8,128)S(1)}, u32[]{:S(2)}) copy-start(f32[256,1]{1,0:T(8,128)S(1)} %get-tuple-element.165) | copy-start | bytes 3076
  33.7 24.3 %copy-start.19 = (bf16[512,384]{1,0:T(8,128)(2,1)S(1)}, bf16[512,384]{1,0:T(8,128)(2,1)}, u32[]{:S(2)}) copy-start(bf16[512,384]{1,0:T(8,128)(2,1)} %refs_4_.1) | copy-start | bytes 1179652
  33.7 24.3 %copy-start.20 = (bf16[512,384]{1,0:T(8,128)(2,1)S(1)}, bf16[512,384]{1,0:T(8,128)(2,1)}, u32[]{:S(2)}) copy-start(bf16[512,384]{1,0:T(8,128)(2,1)} %refs_5_.1) | copy-start | bytes 1179652
  33.7 24.3 %copy-start.22 = (bf16[512,384]{1,0:T(8,128)(2,1)S(1)}, bf16[512,384]{1,0:T(8,128)(2,1)}, u32[]{:S(2)}) copy-start(bf16[512,384]{1,0:T(8,128)(2,1)} %copy-done.21) | copy-start | bytes 1179652
  33.7 24.3 %copy-start.24 = (bf16[512,384]{1,0:T(8,128)(2,1)S(1)}, bf16[512,384]{1,0:T(8,128)(2,1)}, u32[]{:S(2)}) copy-start(bf16[512,384]{1,0:T(8,128)(2,1)} %copy-done.23) | copy-start | bytes 1179652
  37.6 6.9 %collective-permute-start.6 = (bf16[32,1024]{1,0:T(8,128)(2,1)S(1)}, bf16[32,1024]{1,0:T(8,128)(2,1)S(1)}, u32[]{:S(2)}, u32[]{:S(2)}) collective-permute-start(bf16[32,1024]{1,0:T(8,128)(2,1)S(1)} %get-tuple-element.97), channel_id=1, source_target_pairs={{0,2},{1,3},{2,4},{3,5},{4,6},{5,7},{6,0},{7,1},{8,10},{9,11},{10,... | collective-permute-start | bytes 196616 | tf_op jit(solution)/shard_map/ppermute | solution.py:40
  38.2 7.8 %collective-permute-start.7 = (bf16[32,1024]{1,0:T(8,128)(2,1)S(1)}, bf16[32,1024]{1,0:T(8,128)(2,1)S(1)}, u32[]{:S(2)}, u32[]{:S(2)}) collective-permute-start(bf16[32,1024]{1,0:T(8,128)(2,1)S(1)} %get-tuple-element.98), channel_id=1, source_target_pairs={{0,4},{1,5},{2,6},{3,7},{4,0},{5,1},{6,2},{7,3},{8,12},{9,13},{10,... | collective-permute-start | bytes 196616 | tf_op jit(solution)/shard_map/ppermute | solution.py:40
  40.5 5.5 %collective-permute-start.8 = (bf16[32,1024]{1,0:T(8,128)(2,1)S(1)}, bf16[32,1024]{1,0:T(8,128)(2,1)S(1)}, u32[]{:S(2)}, u32[]{:S(2)}) collective-permute-start(bf16[32,1024]{1,0:T(8,128)(2,1)S(1)} %get-tuple-element.99), channel_id=1, source_target_pairs={{0,6},{1,7},{2,0},{3,1},{4,2},{5,3},{6,4},{7,5},{8,14},{9,15},{10,... | collective-permute-start | bytes 196616 | tf_op jit(solution)/shard_map/ppermute | solution.py:40
  46.0 17.0 %collective-permute-start.14 = (bf16[768,384]{1,0:T(8,128)(2,1)S(1)}, bf16[768,384]{1,0:T(8,128)(2,1)S(1)}, u32[]{:S(2)}, u32[]{:S(2)}) collective-permute-start(bf16[768,384]{1,0:T(8,128)(2,1)S(1)} %collective-permute-done.9.refs_4_), channel_id=1, source_target_pairs={{0,2},{1,3},{2,4},{3,5},{4,6},{5,7},{6,0},{7,1},{8,10},{9,11},{10,... | collective-permute-start | bytes 1769480 | tf_op jit(solution)/shard_map/ppermute | solution.py:40
  48.0 7.9 %collective-permute-start.11 = (bf16[4,32,1024]{2,1,0:T(8,128)(2,1)S(1)}, bf16[4,32,1024]{2,1,0:T(8,128)(2,1)S(1)}, u32[]{:S(2)}, u32[]{:S(2)}) collective-permute-start(bf16[4,32,1024]{2,1,0:T(8,128)(2,1)S(1)} %pad_maximum_fusion.2.refs_0_), channel_id=1, source_target_pairs={{0,16},{8,24},{16,0},{24,8},{1,17},{9,25},{17,1},{25,9},{2,18},{10... | collective-permute-start | bytes 786440 | tf_op jit(solution)/shard_map/ppermute | solution.py:44
  55.9 2.1 %collective-permute-start.12 = (bf16[4,32,1024]{2,1,0:T(8,128)(2,1)S(1)}, bf16[4,32,1024]{2,1,0:T(8,128)(2,1)S(1)}, u32[]{:S(2)}, u32[]{:S(2)}) collective-permute-start(bf16[4,32,1024]{2,1,0:T(8,128)(2,1)S(1)} %collective-permute-done.11.refs_2_), channel_id=1, source_target_pairs={{0,8},{8,0},{16,24},{24,16},{1,9},{9,1},{17,25},{25,17},{2,10},{10... | collective-permute-start | bytes 786440 | tf_op jit(solution)/shard_map/ppermute | solution.py:44
  55.9 2.1 %collective-permute-start.10 = (bf16[4,32,1024]{2,1,0:T(8,128)(2,1)S(1)}, bf16[4,32,1024]{2,1,0:T(8,128)(2,1)S(1)}, u32[]{:S(2)}, u32[]{:S(2)}) collective-permute-start(bf16[4,32,1024]{2,1,0:T(8,128)(2,1)S(1)} %pad_maximum_fusion.2.refs_0_), channel_id=1, source_target_pairs={{0,8},{8,0},{16,24},{24,16},{1,9},{9,1},{17,25},{25,17},{2,10},{10... | collective-permute-start | bytes 786440 | tf_op jit(solution)/shard_map/ppermute | solution.py:44
  56.4 25.0 %collective-permute-start.18 = (bf16[768,384]{1,0:T(8,128)(2,1)S(1)}, bf16[768,384]{1,0:T(8,128)(2,1)S(1)}, u32[]{:S(2)}, u32[]{:S(2)}) collective-permute-start(bf16[768,384]{1,0:T(8,128)(2,1)S(1)} %collective-permute-done.9.refs_4_), channel_id=1, source_target_pairs={{0,1},{1,0},{2,3},{3,2},{4,5},{5,4},{6,7},{7,6},{8,9},{9,8},{10,11... | collective-permute-start | bytes 1769480 | tf_op jit(solution)/shard_map/ppermute | solution.py:40
  63.0 6.7 %collective-permute-start.15 = (bf16[128,768]{1,0:T(8,128)(2,1)S(1)}, bf16[128,768]{1,0:T(8,128)(2,1)S(1)}, u32[]{:S(2)}, u32[]{:S(2)}) collective-permute-start(bf16[128,768]{1,0:T(8,128)(2,1)S(1)} %get-tuple-element.108), channel_id=1, source_target_pairs={{0,6},{1,7},{2,0},{3,1},{4,2},{5,3},{6,4},{7,5},{8,14},{9,15},{10,... | collective-permute-start | bytes 589832 | tf_op jit(solution)/shard_map/ppermute | solution.py:40
  63.0 18.2 %collective-permute-start.16 = (bf16[128,768]{1,0:T(8,128)(2,1)S(1)}, bf16[128,768]{1,0:T(8,128)(2,1)S(1)}, u32[]{:S(2)}, u32[]{:S(2)}) collective-permute-start(bf16[128,768]{1,0:T(8,128)(2,1)S(1)} %get-tuple-element.109), channel_id=1, source_target_pairs={{0,4},{1,5},{2,6},{3,7},{4,0},{5,1},{6,2},{7,3},{8,12},{9,13},{10,... | collective-permute-start | bytes 589832 | tf_op jit(solution)/shard_map/ppermute | solution.py:40
  64.7 16.6 %collective-permute-start.17 = (bf16[128,768]{1,0:T(8,128)(2,1)S(1)}, bf16[128,768]{1,0:T(8,128)(2,1)S(1)}, u32[]{:S(2)}, u32[]{:S(2)}) collective-permute-start(bf16[128,768]{1,0:T(8,128)(2,1)S(1)} %get-tuple-element.110), channel_id=1, source_target_pairs={{0,2},{1,3},{2,4},{3,5},{4,6},{5,7},{6,0},{7,1},{8,10},{9,11},{10,... | collective-permute-start | bytes 589832 | tf_op jit(solution)/shard_map/ppermute | solution.py:40
  65.1 20.8 %collective-permute-start.21 = (bf16[4,2,64,384]{3,2,1,0:T(8,128)(2,1)S(1)}, bf16[4,2,64,384]{3,2,1,0:T(8,128)(2,1)S(1)}, u32[]{:S(2)}, u32[]{:S(2)}) collective-permute-start(bf16[4,2,64,384]{3,2,1,0:T(8,128)(2,1)S(1)} %get-tuple-element.112), channel_id=1, source_target_pairs={{0,1},{1,0},{2,3},{3,2},{4,5},{5,4},{6,7},{7,6},{8,9},{9,8},{10,11... | collective-permute-start | bytes 1179656 | tf_op jit(solution)/shard_map/ppermute | solution.py:40
  69.8 29.2 %collective-permute-start.20 = (bf16[768,384]{1,0:T(8,128)(2,1)S(1)}, bf16[768,384]{1,0:T(8,128)(2,1)S(1)}, u32[]{:S(2)}, u32[]{:S(2)}) collective-permute-start(bf16[768,384]{1,0:T(8,128)(2,1)S(1)} %collective-permute-done.14.refs_6_), channel_id=1, source_target_pairs={{0,1},{1,0},{2,3},{3,2},{4,5},{5,4},{6,7},{7,6},{8,9},{9,8},{10,11... | collective-permute-start | bytes 1769480 | tf_op jit(solution)/shard_map/ppermute | solution.py:40
  81.4 9.7 %collective-permute-start.23 = (bf16[128,768]{1,0:T(8,128)(2,1)S(1)}, bf16[128,768]{1,0:T(8,128)(2,1)S(1)}, u32[]{:S(2)}, u32[]{:S(2)}) collective-permute-start(bf16[128,768]{1,0:T(8,128)(2,1)S(1)} %add_convert_fusion.4.refs_0_), channel_id=1, source_target_pairs={{0,2},{1,3},{2,4},{3,5},{4,6},{5,7},{6,0},{7,1},{8,10},{9,11},{10,... | collective-permute-start | bytes 589832 | tf_op jit(solution)/shard_map/ppermute | solution.py:40
  81.5 15.4 %collective-permute-start.19 = (bf16[128,768]{1,0:T(8,128)(2,1)S(1)}, bf16[128,768]{1,0:T(8,128)(2,1)S(1)}, u32[]{:S(2)}, u32[]{:S(2)}) collective-permute-start(bf16[128,768]{1,0:T(8,128)(2,1)S(1)} %add_convert_fusion.4.refs_0_), channel_id=1, source_target_pairs={{0,4},{1,5},{2,6},{3,7},{4,0},{5,1},{6,2},{7,3},{8,12},{9,13},{10,... | collective-permute-start | bytes 589832 | tf_op jit(solution)/shard_map/ppermute | solution.py:40
  83.0 15.4 %collective-permute-start.26 = (bf16[128,768]{1,0:T(8,128)(2,1)S(1)}, bf16[128,768]{1,0:T(8,128)(2,1)S(1)}, u32[]{:S(2)}, u32[]{:S(2)}) collective-permute-start(bf16[128,768]{1,0:T(8,128)(2,1)S(1)} %add_convert_fusion.4.refs_0_), channel_id=1, source_target_pairs={{0,6},{1,7},{2,0},{3,1},{4,2},{5,3},{6,4},{7,5},{8,14},{9,15},{10,... | collective-permute-start | bytes 589832 | tf_op jit(solution)/shard_map/ppermute | solution.py:40
  85.8 19.6 %collective-permute-start.22 = (bf16[128,768]{1,0:T(8,128)(2,1)S(1)}, bf16[128,768]{1,0:T(8,128)(2,1)S(1)}, u32[]{:S(2)}, u32[]{:S(2)}) collective-permute-start(bf16[128,768]{1,0:T(8,128)(2,1)S(1)} %add_convert_fusion.4.refs_0_), channel_id=1, source_target_pairs={{0,1},{1,0},{2,3},{3,2},{4,5},{5,4},{6,7},{7,6},{8,9},{9,8},{10,11... | collective-permute-start | bytes 589832 | tf_op jit(solution)/shard_map/ppermute | solution.py:40
  91.1 14.4 %collective-permute-start.24 = (bf16[128,768]{1,0:T(8,128)(2,1)S(1)}, bf16[128,768]{1,0:T(8,128)(2,1)S(1)}, u32[]{:S(2)}, u32[]{:S(2)}) collective-permute-start(bf16[128,768]{1,0:T(8,128)(2,1)S(1)} %collective-permute-done.23.refs_2_), channel_id=1, source_target_pairs={{0,1},{1,0},{2,3},{3,2},{4,5},{5,4},{6,7},{7,6},{8,9},{9,8},{10,11... | collective-permute-start | bytes 589832 | tf_op jit(solution)/shard_map/ppermute | solution.py:40
  96.9 12.1 %collective-permute-start.25 = (bf16[128,768]{1,0:T(8,128)(2,1)S(1)}, bf16[128,768]{1,0:T(8,128)(2,1)S(1)}, u32[]{:S(2)}, u32[]{:S(2)}) collective-permute-start(bf16[128,768]{1,0:T(8,128)(2,1)S(1)} %collective-permute-done.19.refs_4_), channel_id=1, source_target_pairs={{0,1},{1,0},{2,3},{3,2},{4,5},{5,4},{6,7},{7,6},{8,9},{9,8},{10,11... | collective-permute-start | bytes 589832 | tf_op jit(solution)/shard_map/ppermute | solution.py:40
  98.4 11.2 %collective-permute-start.27 = (bf16[128,768]{1,0:T(8,128)(2,1)S(1)}, bf16[128,768]{1,0:T(8,128)(2,1)S(1)}, u32[]{:S(2)}, u32[]{:S(2)}) collective-permute-start(bf16[128,768]{1,0:T(8,128)(2,1)S(1)} %collective-permute-done.26.refs_6_), channel_id=1, source_target_pairs={{0,1},{1,0},{2,3},{3,2},{4,5},{5,4},{6,7},{7,6},{8,9},{9,8},{10,11... | collective-permute-start | bytes 589832 | tf_op jit(solution)/shard_map/ppermute | solution.py:40
  99.0 14.9 %collective-permute-start.30 = (bf16[2,2,64,384]{3,2,1,0:T(8,128)(2,1)S(1)}, bf16[2,2,64,384]{3,2,1,0:T(8,128)(2,1)S(1)}, u32[]{:S(2)}, u32[]{:S(2)}) collective-permute-start(bf16[2,2,64,384]{3,2,1,0:T(8,128)(2,1)S(1)} %get-tuple-element.123), channel_id=1, source_target_pairs={{0,6},{1,7},{2,0},{3,1},{4,2},{5,3},{6,4},{7,5},{8,14},{9,15},{10,... | collective-permute-start | bytes 589832 | tf_op jit(solution)/shard_map/ppermute | solution.py:40
  105.5 16.4 %collective-permute-start.29 = (bf16[2,2,64,384]{3,2,1,0:T(8,128)(2,1)S(1)}, bf16[2,2,64,384]{3,2,1,0:T(8,128)(2,1)S(1)}, u32[]{:S(2)}, u32[]{:S(2)}) collective-permute-start(bf16[2,2,64,384]{3,2,1,0:T(8,128)(2,1)S(1)} %get-tuple-element.122), channel_id=1, source_target_pairs={{0,4},{1,5},{2,6},{3,7},{4,0},{5,1},{6,2},{7,3},{8,12},{9,13},{10,... | collective-permute-start | bytes 589832 | tf_op jit(solution)/shard_map/ppermute | solution.py:40
  105.6 16.3 %collective-permute-start.28 = (bf16[2,2,64,384]{3,2,1,0:T(8,128)(2,1)S(1)}, bf16[2,2,64,384]{3,2,1,0:T(8,128)(2,1)S(1)}, u32[]{:S(2)}, u32[]{:S(2)}) collective-permute-start(bf16[2,2,64,384]{3,2,1,0:T(8,128)(2,1)S(1)} %get-tuple-element.121), channel_id=1, source_target_pairs={{0,2},{1,3},{2,4},{3,5},{4,6},{5,7},{6,0},{7,1},{8,10},{9,11},{10,... | collective-permute-start | bytes 589832 | tf_op jit(solution)/shard_map/ppermute | solution.py:40
  112.4 26.9 %copy-start.10 = (bf16[2,256,384]{2,1,0:T(8,128)(2,1)}, bf16[2,256,384]{2,1,0:T(8,128)(2,1)S(1)}, u32[]{:S(2)}) copy-start(bf16[2,256,384]{2,1,0:T(8,128)(2,1)S(1)} %get-tuple-element.155.refs_4_) | copy-start | bytes 1179652
  112.4 1.4 collective-permute-start.31
  113.9 38.0 %copy-start.37 = (f32[256,2]{1,0:T(8,128)}, f32[256,2]{1,0:T(8,128)S(1)}, u32[]{:S(2)}) copy-start(f32[256,2]{1,0:T(8,128)S(1)} %add.74) | copy-start | bytes 6148
  122.0 25.7 %collective-permute-start.36 = (bf16[4,2,2,64,384]{4,3,2,1,0:T(8,128)(2,1)S(1)}, bf16[4,2,2,64,384]{4,3,2,1,0:T(8,128)(2,1)S(1)}, u32[]{:S(2)}, u32[]{:S(2)}) collective-permute-start(bf16[4,2,2,64,384]{4,3,2,1,0:T(8,128)(2,1)S(1)} %pad_maximum_fusion.1.refs_0_), channel_id=1, source_target_pairs={{0,16},{8,24},{16,0},{24,8},{1,17},{9,25},{17,1},{25,9},{2,18},{10... | collective-permute-start | bytes 2359304 | tf_op jit(solution)/shard_map/ppermute | solution.py:44
  123.6 11.4 %collective-permute-start.34 = (bf16[2,256,384]{2,1,0:T(8,128)(2,1)S(1)}, bf16[2,256,384]{2,1,0:T(8,128)(2,1)S(1)}, u32[]{:S(2)}, u32[]{:S(2)}) collective-permute-start(bf16[2,256,384]{2,1,0:T(8,128)(2,1)S(1)} %get-tuple-element.155.refs_4_), channel_id=1, source_target_pairs={{0,2},{1,3},{2,4},{3,5},{4,6},{5,7},{6,0},{7,1},{8,10},{9,11},{10,... | collective-permute-start | bytes 1179656 | tf_op jit(solution)/shard_map/ppermute | solution.py:40
  123.6 24.2 %collective-permute-start.37 = (bf16[4,2,2,64,384]{4,3,2,1,0:T(8,128)(2,1)S(1)}, bf16[4,2,2,64,384]{4,3,2,1,0:T(8,128)(2,1)S(1)}, u32[]{:S(2)}, u32[]{:S(2)}) collective-permute-start(bf16[4,2,2,64,384]{4,3,2,1,0:T(8,128)(2,1)S(1)} %pad_maximum_fusion.1.refs_0_), channel_id=1, source_target_pairs={{0,8},{8,0},{16,24},{24,16},{1,9},{9,1},{17,25},{25,17},{2,10},{10... | collective-permute-start | bytes 2359304 | tf_op jit(solution)/shard_map/ppermute | solution.py:44
  123.6 24.2 %collective-permute-start.32 = (bf16[3,128,768]{2,1,0:T(8,128)(2,1)S(1)}, bf16[3,128,768]{2,1,0:T(8,128)(2,1)S(1)}, u32[]{:S(2)}, u32[]{:S(2)}) collective-permute-start(bf16[3,128,768]{2,1,0:T(8,128)(2,1)S(1)} %get-tuple-element.142.own_ref), channel_id=1, source_target_pairs={{0,1},{1,0},{2,3},{3,2},{4,5},{5,4},{6,7},{7,6},{8,9},{9,8},{10,11... | collective-permute-start | bytes 1769480 | tf_op jit(solution)/shard_map/ppermute | solution.py:40
  125.0 22.7 %collective-permute-start.33 = (bf16[2,256,384]{2,1,0:T(8,128)(2,1)S(1)}, bf16[2,256,384]{2,1,0:T(8,128)(2,1)S(1)}, u32[]{:S(2)}, u32[]{:S(2)}) collective-permute-start(bf16[2,256,384]{2,1,0:T(8,128)(2,1)S(1)} %get-tuple-element.155.refs_4_), channel_id=1, source_target_pairs={{0,1},{1,0},{2,3},{3,2},{4,5},{5,4},{6,7},{7,6},{8,9},{9,8},{10,11... | collective-permute-start | bytes 1179656 | tf_op jit(solution)/shard_map/ppermute | solution.py:40
  135.0 17.4 %copy-start.12 = (bf16[2,256,384]{2,1,0:T(8,128)(2,1)}, bf16[2,256,384]{2,1,0:T(8,128)(2,1)S(1)}, u32[]{:S(2)}) copy-start(bf16[2,256,384]{2,1,0:T(8,128)(2,1)S(1)} %collective-permute-done.34.refs_5_) | copy-start | bytes 1179652
  135.0 12.8 %collective-permute-start.35 = (bf16[2,256,384]{2,1,0:T(8,128)(2,1)S(1)}, bf16[2,256,384]{2,1,0:T(8,128)(2,1)}, u32[]{:S(2)}, u32[]{:S(2)}) collective-permute-start(bf16[2,256,384]{2,1,0:T(8,128)(2,1)S(1)} %collective-permute-done.34.refs_5_), channel_id=1, source_target_pairs={{0,2},{1,3},{2,4},{3,5},{4,6},{5,7},{6,0},{7,1},{8,10},{9,11},{10,... | collective-permute-start | bytes 1179656 | tf_op jit(solution)/shard_map/ppermute | solution.py:40
  139.4 20.1 %copy-start.8 = (bf16[2,256,768]{2,1,0:T(8,128)(2,1)}, bf16[2,256,768]{2,1,0:T(8,128)(2,1)S(1)}, u32[]{:S(2)}) copy-start(bf16[2,256,768]{2,1,0:T(8,128)(2,1)S(1)} %get-tuple-element.131) | copy-start | bytes 2359300
  147.8 5.1 %collective-permute-start.38 = (bf16[2,256,1536]{2,1,0:T(8,128)(2,1)S(1)}, bf16[2,256,1536]{2,1,0:T(8,128)(2,1)S(1)}, u32[]{:S(2)}, u32[]{:S(2)}) collective-permute-start(bf16[2,256,1536]{2,1,0:T(8,128)(2,1)S(1)} %get-tuple-element.136), channel_id=1, source_target_pairs={{0,8},{8,0},{16,24},{24,16},{1,9},{9,1},{17,25},{25,17},{2,10},{10... | collective-permute-start | bytes 4718600 | tf_op jit(solution)/shard_map/ppermute | solution.py:44
  147.9 26.8 %collective-permute-start.40 = (bf16[2,256,384]{2,1,0:T(8,128)(2,1)}, bf16[2,256,384]{2,1,0:T(8,128)(2,1)}, u32[]{:S(2)}, u32[]{:S(2)}) collective-permute-start(bf16[2,256,384]{2,1,0:T(8,128)(2,1)} %collective-permute-done.35.refs_6_), channel_id=1, source_target_pairs={{0,1},{1,0},{2,3},{3,2},{4,5},{5,4},{6,7},{7,6},{8,9},{9,8},{10,11... | collective-permute-start | bytes 1179656 | tf_op jit(solution)/shard_map/ppermute | solution.py:40
  149.4 25.3 %collective-permute-start.41 = (bf16[2,256,384]{2,1,0:T(8,128)(2,1)}, bf16[2,256,384]{2,1,0:T(8,128)(2,1)}, u32[]{:S(2)}, u32[]{:S(2)}) collective-permute-start(bf16[2,256,384]{2,1,0:T(8,128)(2,1)} %collective-permute-done.35.refs_6_), channel_id=1, source_target_pairs={{0,2},{1,3},{2,4},{3,5},{4,6},{5,7},{6,0},{7,1},{8,10},{9,11},{10,... | collective-permute-start | bytes 1179656 | tf_op jit(solution)/shard_map/ppermute | solution.py:40
  151.9 5.3 %collective-permute-start.44 = (f32[256,2]{1,0:T(8,128)S(1)}, f32[256,2]{1,0:T(8,128)S(1)}, u32[]{:S(2)}, u32[]{:S(2)}) collective-permute-start(f32[256,2]{1,0:T(8,128)S(1)} %add.74), channel_id=1, source_target_pairs={{0,16},{8,24},{16,0},{24,8},{1,17},{9,25},{17,1},{25,9},{2,18},{10... | collective-permute-start | bytes 6152 | tf_op jit(solution)/shard_map/ppermute | solution.py:44
  152.4 15.6 %collective-permute-start.39 = (bf16[2,256,384]{2,1,0:T(8,128)(2,1)S(1)}, bf16[2,256,384]{2,1,0:T(8,128)(2,1)S(1)}, u32[]{:S(2)}, u32[]{:S(2)}) collective-permute-start(bf16[2,256,384]{2,1,0:T(8,128)(2,1)S(1)} %collective-permute-done.34.refs_5_), channel_id=1, source_target_pairs={{0,1},{1,0},{2,3},{3,2},{4,5},{5,4},{6,7},{7,6},{8,9},{9,8},{10,11... | collective-permute-start | bytes 1179656 | tf_op jit(solution)/shard_map/ppermute | solution.py:40
  157.1 32.6 %copy-start.11 = (bf16[2,256,384]{2,1,0:T(8,128)(2,1)S(1)}, bf16[2,256,384]{2,1,0:T(8,128)(2,1)}, u32[]{:S(2)}) copy-start(bf16[2,256,384]{2,1,0:T(8,128)(2,1)} %copy-done.10) | copy-start | bytes 1179652
  157.2 19.8 %collective-permute-start.45 = (bf16[256,768]{1,0:T(8,128)(2,1)}, bf16[256,768]{1,0:T(8,128)(2,1)}, u32[]{:S(2)}, u32[]{:S(2)}) collective-permute-start(bf16[256,768]{1,0:T(8,128)(2,1)} %get-tuple-element.149), channel_id=1, source_target_pairs={{0,16},{8,24},{16,0},{24,8},{1,17},{9,25},{17,1},{25,9},{2,18},{10... | collective-permute-start | bytes 1179656 | tf_op jit(solution)/shard_map/ppermute | solution.py:44
  159.5 15.3 %collective-permute-start.42 = (bf16[128,768]{1,0:T(8,128)(2,1)}, bf16[128,768]{1,0:T(8,128)(2,1)}, u32[]{:S(2)}, u32[]{:S(2)}) collective-permute-start(bf16[128,768]{1,0:T(8,128)(2,1)} %get-tuple-element.144), channel_id=1, source_target_pairs={{0,2},{1,3},{2,4},{3,5},{4,6},{5,7},{6,0},{7,1},{8,10},{9,11},{10,... | collective-permute-start | bytes 589832 | tf_op jit(solution)/shard_map/ppermute | solution.py:40
  168.8 8.1 %collective-permute-start.43 = (bf16[128,768]{1,0:T(8,128)(2,1)}, bf16[128,768]{1,0:T(8,128)(2,1)}, u32[]{:S(2)}, u32[]{:S(2)}) collective-permute-start(bf16[128,768]{1,0:T(8,128)(2,1)} %get-tuple-element.145), channel_id=1, source_target_pairs={{0,6},{1,7},{2,0},{3,1},{4,2},{5,3},{6,4},{7,5},{8,14},{9,15},{10,... | collective-permute-start | bytes 589832 | tf_op jit(solution)/shard_map/ppermute | solution.py:40
  174.7 15.1 %copy-start.3 = (bf16[4,2,2,64,384]{4,3,2,1,0:T(8,128)(2,1)S(1)}, bf16[4,2,2,64,384]{4,3,2,1,0:T(8,128)(2,1)}, u32[]{:S(2)}) copy-start(bf16[4,2,2,64,384]{4,3,2,1,0:T(8,128)(2,1)} %copy-done.2) | copy-start | bytes 2359300
  174.7 15.1 %copy-start.13 = (bf16[2,256,384]{2,1,0:T(8,128)(2,1)S(1)}, bf16[2,256,384]{2,1,0:T(8,128)(2,1)}, u32[]{:S(2)}) copy-start(bf16[2,256,384]{2,1,0:T(8,128)(2,1)} %copy-done.12) | copy-start | bytes 1179652
  174.7 15.1 %copy-start.15 = (bf16[2,256,384]{2,1,0:T(8,128)(2,1)S(1)}, bf16[2,256,384]{2,1,0:T(8,128)(2,1)}, u32[]{:S(2)}) copy-start(bf16[2,256,384]{2,1,0:T(8,128)(2,1)} %copy-done.14) | copy-start | bytes 1179652
  174.7 15.1 %copy-start.17 = (bf16[2,256,384]{2,1,0:T(8,128)(2,1)S(1)}, bf16[2,256,384]{2,1,0:T(8,128)(2,1)}, u32[]{:S(2)}) copy-start(bf16[2,256,384]{2,1,0:T(8,128)(2,1)} %copy-done.16) | copy-start | bytes 1179652
  176.9 10.9 %collective-permute-start.49 = (bf16[128,768]{1,0:T(8,128)(2,1)}, bf16[128,768]{1,0:T(8,128)(2,1)S(1)}, u32[]{:S(2)}, u32[]{:S(2)}) collective-permute-start(bf16[128,768]{1,0:T(8,128)(2,1)} %copy-done.32), channel_id=1, source_target_pairs={{0,4},{1,5},{2,6},{3,7},{4,0},{5,1},{6,2},{7,3},{8,12},{9,13},{10,... | collective-permute-start | bytes 589832 | tf_op jit(solution)/shard_map/ppermute | solution.py:40
  178.2 11.5 %collective-permute-start.47 = (bf16[4,2,2,64,384]{4,3,2,1,0:T(8,128)(2,1)S(1)}, bf16[4,2,2,64,384]{4,3,2,1,0:T(8,128)(2,1)S(1)}, u32[]{:S(2)}, u32[]{:S(2)}) collective-permute-start(bf16[4,2,2,64,384]{4,3,2,1,0:T(8,128)(2,1)S(1)} %collective-permute-done.36.refs_2_), channel_id=1, source_target_pairs={{0,8},{8,0},{16,24},{24,16},{1,9},{9,1},{17,25},{25,17},{2,10},{10... | collective-permute-start | bytes 2359304 | tf_op jit(solution)/shard_map/ppermute | solution.py:44
  179.4 13.3 %collective-permute-start.48 = (bf16[2,256,384]{2,1,0:T(8,128)(2,1)}, bf16[2,256,384]{2,1,0:T(8,128)(2,1)S(1)}, u32[]{:S(2)}, u32[]{:S(2)}) collective-permute-start(bf16[2,256,384]{2,1,0:T(8,128)(2,1)} %collective-permute-done.41.refs_7_), channel_id=1, source_target_pairs={{0,1},{1,0},{2,3},{3,2},{4,5},{5,4},{6,7},{7,6},{8,9},{9,8},{10,11... | collective-permute-start | bytes 1179656 | tf_op jit(solution)/shard_map/ppermute | solution.py:40
  180.2 12.4 %collective-permute-start.46 = (bf16[256,768]{1,0:T(8,128)(2,1)}, bf16[256,768]{1,0:T(8,128)(2,1)S(1)}, u32[]{:S(2)}, u32[]{:S(2)}) collective-permute-start(bf16[256,768]{1,0:T(8,128)(2,1)} %get-tuple-element.152), channel_id=1, source_target_pairs={{0,16},{8,24},{16,0},{24,8},{1,17},{9,25},{17,1},{25,9},{2,18},{10... | collective-permute-start | bytes 1179656 | tf_op jit(solution)/shard_map/ppermute | solution.py:44
  (25 other events, 139.3 us)

commit v9 on v6

--- a/solution.py
+++ b/solution.py
@@ -816,49 +816,45 @@
         caption_lens,
         pairs,
     )
-    slots, both, row_sums, over_z = after((slots, both, row_sums, over_z))
+
+    side_slots = fsend(slots, 0, 1)
+    sides = [fsend(both, 0, 1)]
+    first, over_z = after((both, over_z))
     tiles = jnp.stack(over_z)
-
-    def chain(blocks, steps):
-        for _ in range(steps):
-            blocks.append(fsend(blocks[-1], 1, 0))
-        return blocks
-
-    def joined(two):
-        return jnp.stack(two).reshape(-1, tokens, width_local)
-
-    side_slots = fsend(slots, 0, 1)
-    side_own = fsend(both, 0, 1)
-    late = chain([both], 2)
-    sums_core = gsend(row_sums, 1)
-    attended, tiles = after((attended, tiles), sums_core)
+    late = [both, fsend(first, 1, 0)]
+    sides.append(fsend(after(late[1], side_slots), 0, 1))
+    for far in range(2, pairs):
+        late.append(fsend(after(late[-1], sides[0]) if far == pairs - 1 else late[-1], 1, 0))
+    row_sums = row_sums + gsend(row_sums, 1)
+    tiles = after(tiles, row_sums)
     tiles_x = gsend(tiles, 2)
-    own, far_piece, away = project_back(attended, d_queries, blocks, place, pairs, part)
-    two = joined(late[1:3])
-    stage = (side_slots, side_own, late, sums_core, tiles_x, two, away)
-    side_slots, side_own, late, sums_core, tiles_x, two, away = after(stage)
-
-    side_two = fsend(two, 0, 1)
-    late = chain(list(late), pairs - 3)
-    row_sums = row_sums + sums_core
+    tiles_core = gsend(tiles, 1)
+    own, far_piece, away = project_back(
+        after(attended, row_sums), d_queries, blocks, place, pairs, part
+    )
+    tiles = [tiles, tiles_core, tiles_x, gsend(tiles_x, 1)]
+    stage = (side_slots, sides, late, tiles, row_sums, away)
+    side_slots, sides, late, tiles, row_sums, away = after(stage)
+
+    joint = jnp.stack(late[2:]).reshape(-1, tokens, width_local)
+    joint = fsend(joint, 0, 1)
+    got = gsend(away, 1)
     sums_x = gsend(row_sums, 2)
-    got = gsend(away, 1)
-    tiles_core = gsend(tiles, 1)
     width = model_width // 4
     sent = (far_piece.astype(F32) + got[:, :, width:].astype(F32)).astype(BF)
-    far_sum = gsend(sent, 2)
-    tiles = [tiles, tiles_core, tiles_x, gsend(tiles_x, 1)]
+    far_sum = gsend(after(sent, sums_x), 2)
     terms = caption_terms(
         slots, side_slots, place, video_counts, sample_caption, tokens, pairs
     )
-    kv_parts = [fsend(terms[far], far, 0) for far in range(1, pairs, 2)]
-    stage = (side_two, late, sums_x, sent, tiles, kv_parts, terms)
-    side_two, late, sums_x, _, tiles, kv_parts, terms = after(stage)
-
+    kv_parts = [fsend(terms[far], far, 0) for far in range(1, pairs)]
+    kv_grads = (terms[0] + sum(p.astype(F32) for p in kv_parts)).astype(BF)[None]
+    key_grad = kv_grads[:, :, :width_local]
+    value_grad = kv_grads[:, :, width_local:]
+    tiles = after(tiles, far_sum)
     here = [((block, 0),) for block in late]
-    there = [((side_own, 0),), ((side_two, 0),), ((side_two, 2),)]
-    there += [((fsend(block, 0, 1), 0),) for block in late[3:]]
-    known = weight_grads(tiles, here + there[:3], None, pairs)
+    there = [((block, 0),) for block in sides]
+    there += [((joint, 2 * k),) for k in range(pairs - 2)]
+    known = weight_grads(tiles, here + there[:2], None, pairs)
     total = own.astype(F32) + got[:, :, :width].astype(F32) + far_sum.astype(F32)
     row_sums = (row_sums + sums_x) / model_width
     video = quarter(video_states, g, 1).astype(F32)
@@ -868,12 +864,8 @@
         quarter(out_grad, g, 1).astype(F32)
         + inverse * (total[1] - row_sums[:, 0:1] - video_hat * row_sums[:, 1:2])
     ).astype(BF)
-    kv_parts += [fsend(terms[far], far, 0) for far in range(2, pairs, 2)]
-    kv_grads = (terms[0] + sum(p.astype(F32) for p in kv_parts)).astype(BF)[None]
-    key_grad = kv_grads[:, :, :width_local]
-    value_grad = kv_grads[:, :, width_local:]
     query_grad, out_weight_grad = weight_grads(
-        tiles, [None] * (pairs + 3) + there[3:], known, pairs
+        tiles, [None] * (pairs + 2) + there[2:], known, pairs
     )
     return (updated, input_grad, query_grad, out_weight_grad, key_grad, value_grad)
 

time: 196 us -> 202 us (1.031)
  waiting for transfers between devices: 69.2 us -> 75.4 us
    ppermute x12, waiting for transfers between devices: 13.9 us -> 18.7 us  [gsend(): lax.ppermute(block, 'grp', [(s, s ^ flip) for s in range(lax.axis_size('g...]
    unnamed x73 -> x89, local copies, waits for them, and re-layouts: 7.21 us -> 9.94 us
  transfers between devices with their start and end apart: 48 -> 48, of which waited for: 18 -> 20; matrix products, arithmetic and copies ran while one was open for 7% -> 7% of each run, Pallas kernels for 20% -> 17%
where the time goes in v9:
time: 202 us; the launch traced here: 201 us
  waiting for transfers between devices  75.4 us (37%)
  starting transfers between devices  65.8 us (33%)
  Pallas kernels  36.5 us (18%)
  other arithmetic  11.6 us (6%)
  local copies, waits for them, and re-layouts  10.9 us (5%)
    ppermute x36, starting transfers between devices, fsend(): return lax.ppermute(block, 'fsdp', perm)  58.1 us
    ppermute x36, waiting for transfers between devices, fsend(): return lax.ppermute(block, 'fsdp', perm)  56.7 us
    pallas_call x9, Pallas kernels, call(): pl.pallas_call(body, out_shape=out_shape, in_specs=specs, out_specs=jax.t...  21.4 us
    ppermute x12, waiting for transfers between devices, gsend(): lax.ppermute(block, 'grp', [(s, s ^ flip) for s in range(lax.axis_size('g...  18.7 us
    unnamed x89, local copies, waits for them, and re-layouts  9.94 us
    pallas_call x1, Pallas kernels, project_text(): pl.pallas_call(body, grid=(steps,), out_shape=shaped((rows, 3 * width)),...  7.96 us
    ppermute x12, starting transfers between devices, gsend(): lax.ppermute(block, 'grp', [(s, s ^ flip) for s in range(lax.axis_size('g...  7.71 us
    pallas_call x1, Pallas kernels, attend_text(): pl.pallas_call(body, grid=(steps,), out_shape=[shaped((rows // 2, depth))...  7.14 us
  transfers between devices with their start and end apart: 48, of which 20 were waited for; matrix products, arithmetic and copies ran while one was open for 7% of the time, Pallas kernels for 17%

profile of v9, /device:TPU:0, one launch (start us, length us, event | category | flops | bytes accessed | tf_op | source)
XLA Modules:
  0.0 201.5 jit_solution(14428431043295811345)
XLA Ops:
  0.6 3.0 %collective-permute-start.2 = (bf16[512,384]{1,0:T(8,128)(2,1)}, bf16[512,384]{1,0:T(8,128)(2,1)S(1)}, u32[]{:S(2)}, u32[]{:S(2)}) collective-permute-start(bf16[512,384]{1,0:T(8,128)(2,1)} %refs_4_.1), channel_id=1, source_target_pairs={{0,1},{1,0},{2,3},{3,2},{4,5},{5,4},{6,7},{7,6},{8,9},{9,8},{10,11... | collective-permute-start | bytes 1179656 | tf_op jit(solution)/shard_map/ppermute | solution.py:40
  3.7 2.0 collective-permute-start
  5.7 1.6 collective-permute-start.1
  7.3 8.0 %shard_map.208.qkv_ref = bf16[128,1536]{1,0:T(8,128)(2,1)} custom-call(bf16[128,4096]{1,0:T(8,128)(2,1)} %bitcast.39, f32[1,4096]{1,0:T(1,128)} %bitcast.54, bf16[4096,512]{1,0:T(8,128)(2,1)} %wq_ref.1, bf16[4096,512]{1,0:T(8,128)(2,1)} %wk_ref.1, bf16[4096,512]{1,0:T(8,128)(2,1)} %wv_ref.1), custom_call_target="tpu_custom_call" | custom-call | flops 1 | bytes 1 | tf_op jit(solution)/shard_map/pallas_call | solution.py:350
  15.8 7.1 %shard_map.209 = (bf16[64,4096]{1,0:T(8,128)(2,1)}, bf16[64,4096]{1,0:T(8,128)(2,1)}) custom-call(s32[3]{0:T(128)} %pad_add_fusion.place_ref, s32[8]{0:T(128)} %len_ref.3, bf16[128,1536]{1,0:T(8,128)(2,1)} %shard_map.208.qkv_ref, f32[8,128,128]{2,1,0:T(8,128)} %bias_ref.1, bf16[512,4096]{1,0:T(8,128)(2,1)} %out_ref.1), custom_call_target="tpu_custom_call" | custom-call | flops 1 | bytes 1 | tf_op jit(solution)/shard_map/pallas_call | solution.py:394
  23.9 1.0 constant_dynamic-update-slice_fusion.1
  25.0 1.6 collective-permute-start.9
  26.6 1.2 pad_maximum_fusion
  27.8 1.6 collective-permute-start.13
  29.5 1.6 collective-permute-start.5
  31.0 2.7 %shard_map.210 = (bf16[256,3072]{1,0:T(8,128)(2,1)S(1)}, f32[256,1]{1,0:T(8,128)S(1)}, f32[256,1]{1,0:T(8,128)S(1)}, bf16[4,2,64,384]{3,2,1,0:T(8,128)(2,1)S(1)}, bf16[4,2,64,384]{3,2,1,0:T(8,128)(2,1)S(1)}) custom-call(s32[3]{0:T(128)S(1)} %copy-done.36, bf16[256,3072]{1,0:T(8,128)(2,1)S(1)} %copy-done.8, bf16[256,3072]{1,0:T(8,128)(2,1)S(1)} %copy-done), custom_call_target="tpu_custom_call" | custom-call | flops 1 | bytes 1 | tf_op jit(solution)/shard_map/pallas_call | solution.py:307
  34.4 3.2 %collective-permute-done.5.far_ref = bf16[32,4096]{1,0:T(8,128)(2,1)S(1)} collective-permute-done((bf16[32,4096]{1,0:T(8,128)(2,1)S(1)}, bf16[32,4096]{1,0:T(8,128)(2,1)S(1)}, u32[]{:S(2)}, u32[]{:S(2)}) %collective-permute-start.5) | collective-permute-done | bytes 262176 | tf_op jit(solution)/shard_map/ppermute | solution.py:44
  39.0 2.4 %collective-permute-start.7 = (bf16[32,1024]{1,0:T(8,128)(2,1)S(1)}, bf16[32,1024]{1,0:T(8,128)(2,1)S(1)}, u32[]{:S(2)}, u32[]{:S(2)}) collective-permute-start(bf16[32,1024]{1,0:T(8,128)(2,1)S(1)} %get-tuple-element.93), channel_id=1, source_target_pairs={{0,4},{1,5},{2,6},{3,7},{4,0},{5,1},{6,2},{7,3},{8,12},{9,13},{10,... | collective-permute-start | bytes 196616 | tf_op jit(solution)/shard_map/ppermute | solution.py:40
  41.4 1.3 collective-permute-start.8
  42.7 2.7 %collective-permute-done.6 = bf16[32,1024]{1,0:T(8,128)(2,1)S(1)} collective-permute-done((bf16[32,1024]{1,0:T(8,128)(2,1)S(1)}, bf16[32,1024]{1,0:T(8,128)(2,1)S(1)}, u32[]{:S(2)}, u32[]{:S(2)}) %collective-permute-start.6) | collective-permute-done | bytes 65568 | tf_op jit(solution)/shard_map/ppermute | solution.py:40
  45.4 1.4 collective-permute-done.7
  46.9 1.9 collective-permute-start.14
  48.8 1.5 collective-permute-start.11
  50.3 6.5 %collective-permute-done.11.refs_2_ = bf16[4,32,1024]{2,1,0:T(8,128)(2,1)S(1)} collective-permute-done((bf16[4,32,1024]{2,1,0:T(8,128)(2,1)S(1)}, bf16[4,32,1024]{2,1,0:T(8,128)(2,1)S(1)}, u32[]{:S(2)}, u32[]{:S(2)}) %collective-permute-start.11) | collective-permute-done | bytes 262176 | tf_op jit(solution)/shard_map/ppermute | solution.py:44
  57.3 1.6 collective-permute-start.18
  58.9 1.8 shard_map.212
  60.7 3.2 %collective-permute-done.14.refs_6_ = bf16[768,384]{1,0:T(8,128)(2,1)S(1)} collective-permute-done((bf16[768,384]{1,0:T(8,128)(2,1)S(1)}, bf16[768,384]{1,0:T(8,128)(2,1)S(1)}, u32[]{:S(2)}, u32[]{:S(2)}) %collective-permute-start.14) | collective-permute-done | bytes 589856 | tf_op jit(solution)/shard_map/ppermute | solution.py:40
  63.9 1.6 collective-permute-start.16
  66.0 1.6 collective-permute-start.21
  67.5 3.1 %collective-permute-done.15 = bf16[128,768]{1,0:T(8,128)(2,1)S(1)} collective-permute-done((bf16[128,768]{1,0:T(8,128)(2,1)S(1)}, bf16[128,768]{1,0:T(8,128)(2,1)S(1)}, u32[]{:S(2)}, u32[]{:S(2)}) %collective-permute-start.15) | collective-permute-done | bytes 196640 | tf_op jit(solution)/shard_map/ppermute | solution.py:40
  70.6 1.6 collective-permute-start.20
  72.2 10.0 %collective-permute-done.16 = bf16[128,768]{1,0:T(8,128)(2,1)S(1)} collective-permute-done((bf16[128,768]{1,0:T(8,128)(2,1)S(1)}, bf16[128,768]{1,0:T(8,128)(2,1)S(1)}, u32[]{:S(2)}, u32[]{:S(2)}) %collective-permute-start.16) | collective-permute-done | bytes 196640 | tf_op jit(solution)/shard_map/ppermute | solution.py:40
  82.3 2.0 collective-permute-start.23
  84.3 1.5 collective-permute-start.19
  85.8 1.6 collective-permute-start.22
  88.0 1.6 collective-permute-start.27
  89.6 5.7 %collective-permute-done.23.refs_2_ = bf16[128,768]{1,0:T(8,128)(2,1)S(1)} collective-permute-done((bf16[128,768]{1,0:T(8,128)(2,1)S(1)}, bf16[128,768]{1,0:T(8,128)(2,1)S(1)}, u32[]{:S(2)}, u32[]{:S(2)}) %collective-permute-start.23) | collective-permute-done | bytes 196640 | tf_op jit(solution)/shard_map/ppermute | solution.py:40
  95.3 1.6 collective-permute-start.24
  96.9 4.6 %collective-permute-done.19.refs_4_ = bf16[128,768]{1,0:T(8,128)(2,1)S(1)} collective-permute-done((bf16[128,768]{1,0:T(8,128)(2,1)S(1)}, bf16[128,768]{1,0:T(8,128)(2,1)S(1)}, u32[]{:S(2)}, u32[]{:S(2)}) %collective-permute-start.19) | collective-permute-done | bytes 196640 | tf_op jit(solution)/shard_map/ppermute | solution.py:40
  101.5 1.6 collective-permute-start.25
  103.3 1.1 collective-permute-start.32
  104.5 2.7 %collective-permute-start.33 = (bf16[2,2,64,384]{3,2,1,0:T(8,128)(2,1)S(1)}, bf16[2,2,64,384]{3,2,1,0:T(8,128)(2,1)S(1)}, u32[]{:S(2)}, u32[]{:S(2)}) collective-permute-start(bf16[2,2,64,384]{3,2,1,0:T(8,128)(2,1)S(1)} %get-tuple-element.123), channel_id=1, source_target_pairs={{0,6},{1,7},{2,0},{3,1},{4,2},{5,3},{6,4},{7,5},{8,14},{9,15},{10,... | collective-permute-start | bytes 589832 | tf_op jit(solution)/shard_map/ppermute | solution.py:40
  107.2 2.8 %shard_map.213 = (bf16[256,384]{1,0:T(8,128)(2,1)S(1)}, bf16[256,384]{1,0:T(8,128)(2,1)S(1)}, f32[1,384]{1,0:T(1,128)S(1)}) custom-call(s32[3]{0:T(128)S(1)} %copy-done.36, bf16[256,3072]{1,0:T(8,128)(2,1)S(1)} %get-tuple-element.89.normed_ref, bf16[256,3072]{1,0:T(8,128)(2,1)S(1)} %copy-done, bf16[384,384]{1,0:T(8,128)(2,1)S(1)} %copy-done.6, ...), custom_call_target="tpu_custom_call" | custom-call | flops 1 | bytes 1 | tf_op jit(solution)/shard_map/pallas_call | solution.py:307
  110.5 2.8 %shard_map.214 = (bf16[2,256,384]{2,1,0:T(8,128)(2,1)S(1)}, bf16[256,384]{1,0:T(8,128)(2,1)S(1)}, bf16[256,384]{1,0:T(8,128)(2,1)S(1)}, f32[256,2]{1,0:T(8,128)S(1)}, bf16[3,128,768]{2,1,0:T(8,128)(2,1)S(1)}) custom-call(s32[3]{0:T(128)S(1)} %copy-done.36, s32[8]{0:T(128)S(1)} %copy-done.38, s32[8]{0:T(128)S(1)} %copy-done.39, s32[8]{0:T(128)S(1)} %copy-done.40, ...), custom_call_target="tpu_custom_call" | custom-call | flops 1 | bytes 1 | tf_op jit(solution)/shard_map/pallas_call | solution.py:307
  113.4 1.3 collective-permute-done.28
  115.4 4.3 %collective-permute-done.32 = bf16[2,2,64,384]{3,2,1,0:T(8,128)(2,1)S(1)} collective-permute-done((bf16[2,2,64,384]{3,2,1,0:T(8,128)(2,1)S(1)}, bf16[2,2,64,384]{3,2,1,0:T(8,128)(2,1)S(1)}, u32[]{:S(2)}, u32[]{:S(2)}) %collective-permute-start.32) | collective-permute-done | bytes 196640 | tf_op jit(solution)/shard_map/ppermute | solution.py:40
  119.9 1.6 collective-permute-start.39
  121.4 12.2 %collective-permute-start.34 = (bf16[2,256,384]{2,1,0:T(8,128)(2,1)S(1)}, bf16[2,256,384]{2,1,0:T(8,128)(2,1)S(1)}, u32[]{:S(2)}, u32[]{:S(2)}) collective-permute-start(bf16[2,256,384]{2,1,0:T(8,128)(2,1)S(1)} %get-tuple-element.147.refs_4_), channel_id=1, source_target_pairs={{0,2},{1,3},{2,4},{3,5},{4,6},{5,7},{6,0},{7,1},{8,10},{9,11},{10,... | collective-permute-start | bytes 1179656 | tf_op jit(solution)/shard_map/ppermute | solution.py:40
  134.1 1.6 collective-permute-start.30
  135.7 3.6 %collective-permute-done.34.refs_5_ = bf16[2,256,384]{2,1,0:T(8,128)(2,1)S(1)} collective-permute-done((bf16[2,256,384]{2,1,0:T(8,128)(2,1)S(1)}, bf16[2,256,384]{2,1,0:T(8,128)(2,1)S(1)}, u32[]{:S(2)}, u32[]{:S(2)}) %collective-permute-start.34) | collective-permute-done | bytes 393248 | tf_op jit(solution)/shard_map/ppermute | solution.py:40
  139.2 2.5 %collective-permute-start.36 = (bf16[2,256,384]{2,1,0:T(8,128)(2,1)S(1)}, bf16[2,256,384]{2,1,0:T(8,128)(2,1)S(1)}, u32[]{:S(2)}, u32[]{:S(2)}) collective-permute-start(bf16[2,256,384]{2,1,0:T(8,128)(2,1)S(1)} %collective-permute-done.34.refs_5_), channel_id=1, source_target_pairs={{0,2},{1,3},{2,4},{3,5},{4,6},{5,7},{6,0},{7,1},{8,10},{9,11},{10,... | collective-permute-start | bytes 1179656 | tf_op jit(solution)/shard_map/ppermute | solution.py:40
  142.2 1.3 collective-permute-done.29.side_ref
  144.0 6.5 %collective-permute-done.30.refs_8_ = bf16[2,256,384]{2,1,0:T(8,128)(2,1)S(1)} collective-permute-done((bf16[2,256,384]{2,1,0:T(8,128)(2,1)S(1)}, bf16[2,256,384]{2,1,0:T(8,128)(2,1)S(1)}, u32[]{:S(2)}, u32[]{:S(2)}) %collective-permute-start.30) | collective-permute-done | bytes 393248 | tf_op jit(solution)/shard_map/ppermute | solution.py:40
  151.3 5.5 %shard_map.215 = (bf16[2,256,768]{2,1,0:T(8,128)(2,1)S(1)}, bf16[2,256,768]{2,1,0:T(8,128)(2,1)S(1)}, bf16[2,256,1536]{2,1,0:T(8,128)(2,1)}) custom-call(s32[3]{0:T(128)S(1)} %copy-done.36, bf16[256,384]{1,0:T(8,128)(2,1)S(1)} %get-tuple-element.115.att_ref, bf16[256,384]{1,0:T(8,128)(2,1)S(1)} %get-tuple-element.116.dq_ref, bf16[384,384]{1,0:T(8,128)(2,1)S(1)} %copy-done.6, ...), custom_call_target="tpu_custom_call" | custom-call | flops 1 | bytes 1 | tf_op jit(solution)/shard_map/pallas_call | solution.py:307
  161.8 1.0 reduce
  162.9 1.6 reduce.2
  164.4 1.1 copy-done.17
  165.6 1.1 copy-done.19
  166.6 1.0 shard_map.218
  167.7 3.7 %collective-permute-start.46 = (bf16[128,768]{1,0:T(8,128)(2,1)S(1)}, bf16[128,768]{1,0:T(8,128)(2,1)S(1)}, u32[]{:S(2)}, u32[]{:S(2)}) collective-permute-start(bf16[128,768]{1,0:T(8,128)(2,1)S(1)} %get-tuple-element.160), channel_id=1, source_target_pairs={{0,4},{1,5},{2,6},{3,7},{4,0},{5,1},{6,2},{7,3},{8,12},{9,13},{10,... | collective-permute-start | bytes 589832 | tf_op jit(solution)/shard_map/ppermute | solution.py:40
  171.6 1.1 pad_maximum_fusion.2
  173.2 1.4 add_convert_fusion
  174.7 2.0 %collective-permute-start.43 = (bf16[2,256,768]{2,1,0:T(8,128)(2,1)S(1)}, bf16[2,256,768]{2,1,0:T(8,128)(2,1)S(1)}, u32[]{:S(2)}, u32[]{:S(2)}) collective-permute-start(bf16[2,256,768]{2,1,0:T(8,128)(2,1)S(1)} %add_convert_fusion), channel_id=1, source_target_pairs={{0,16},{8,24},{16,0},{24,8},{1,17},{9,25},{17,1},{25,9},{2,18},{10... | collective-permute-start | bytes 2359304 | tf_op jit(solution)/shard_map/ppermute | solution.py:44
  177.4 8.0 %collective-permute-done.46 = bf16[128,768]{1,0:T(8,128)(2,1)S(1)} collective-permute-done((bf16[128,768]{1,0:T(8,128)(2,1)S(1)}, bf16[128,768]{1,0:T(8,128)(2,1)S(1)}, u32[]{:S(2)}, u32[]{:S(2)}) %collective-permute-start.46) | collective-permute-done | bytes 196640 | tf_op jit(solution)/shard_map/ppermute | solution.py:40
  186.2 7.6 %collective-permute-done.43 = bf16[2,256,768]{2,1,0:T(8,128)(2,1)S(1)} collective-permute-done((bf16[2,256,768]{2,1,0:T(8,128)(2,1)S(1)}, bf16[2,256,768]{2,1,0:T(8,128)(2,1)S(1)}, u32[]{:S(2)}, u32[]{:S(2)}) %collective-permute-start.43) | collective-permute-done | bytes 786464 | tf_op jit(solution)/shard_map/ppermute | solution.py:44
  193.9 2.4 %shard_map.216 = (f32[384,384]{1,0:T(8,128)S(1)}, f32[384,384]{1,0:T(8,128)S(1)}) custom-call(bf16[4,2,2,64,384]{4,3,2,1,0:T(8,128)(2,1)S(1)} %pad_maximum_fusion.1.refs_0_, bf16[4,2,2,64,384]{4,3,2,1,0:T(8,128)(2,1)S(1)} %copy-done.3, bf16[4,2,2,64,384]{4,3,2,1,0:T(8,128)(2,1)S(1)} %collective-permute-done.39.refs_2_, ...), custom_call_target="tpu_custom_call" | custom-call | flops 1 | bytes 1 | tf_op jit(solution)/shard_map/pallas_call | solution.py:307
  196.3 1.4 convert_add_fusion
  197.8 2.2 %fusion.6 = (bf16[256,768]{1,0:T(8,128)(2,1)}, bf16[256,768]{1,0:T(8,128)(2,1)}) fusion(f32[2,256,768]{2,1,0:T(8,128)S(1)} %convert_add_fusion, f32[256]{0:T(256)S(1)} %get-tuple-element.163, f32[256]{0:T(256)S(1)} %copy-done.43, f32[256]{0:T(256)S(1)} %get-tuple-element.162, f32[256]{0:T(256)S(1)} %reduce, bf16[256,3072]{1,0:T(8,128)(2,1)S(1)} %copy-done, ...), kind=kLoop, calls=%fused_computation.17 | loop fusion | flops 2359296 | bytes 3149828 | tf_op jit(solution)/shard_map/convert_element_type | solution.py:866
  200.0 1.5 shard_map.217
  (151 shorter events, 16.4 us)
Async XLA Ops:
  0.6 22.4 %collective-permute-start.2 = (bf16[512,384]{1,0:T(8,128)(2,1)}, bf16[512,384]{1,0:T(8,128)(2,1)S(1)}, u32[]{:S(2)}, u32[]{:S(2)}) collective-permute-start(bf16[512,384]{1,0:T(8,128)(2,1)} %refs_4_.1), channel_id=1, source_target_pairs={{0,1},{1,0},{2,3},{3,2},{4,5},{5,4},{6,7},{7,6},{8,9},{9,8},{10,11... | collective-permute-start | bytes 1179656 | tf_op jit(solution)/shard_map/ppermute | solution.py:40
  3.7 19.4 %collective-permute-start.3 = (bf16[512,384]{1,0:T(8,128)(2,1)}, bf16[512,384]{1,0:T(8,128)(2,1)S(1)}, u32[]{:S(2)}, u32[]{:S(2)}) collective-permute-start(bf16[512,384]{1,0:T(8,128)(2,1)} %refs_5_.1), channel_id=1, source_target_pairs={{0,1},{1,0},{2,3},{3,2},{4,5},{5,4},{6,7},{7,6},{8,9},{9,8},{10,11... | collective-permute-start | bytes 1179656 | tf_op jit(solution)/shard_map/ppermute | solution.py:40
  3.7 19.2 %collective-permute-start = (bf16[384,384]{1,0:T(8,128)(2,1)}, bf16[384,384]{1,0:T(8,128)(2,1)}, u32[]{:S(2)}, u32[]{:S(2)}) collective-permute-start(bf16[384,384]{1,0:T(8,128)(2,1)} %refs_0_.3), channel_id=1, source_target_pairs={{0,2},{1,3},{2,4},{3,5},{4,6},{5,7},{6,0},{7,1},{8,10},{9,11},{10,... | collective-permute-start | bytes 884744 | tf_op jit(solution)/shard_map/ppermute | solution.py:40
  5.7 17.2 %collective-permute-start.1 = (bf16[384,384]{1,0:T(8,128)(2,1)}, bf16[384,384]{1,0:T(8,128)(2,1)S(1)}, u32[]{:S(2)}, u32[]{:S(2)}) collective-permute-start(bf16[384,384]{1,0:T(8,128)(2,1)} %refs_1_.3), channel_id=1, source_target_pairs={{0,2},{1,3},{2,4},{3,5},{4,6},{5,7},{6,0},{7,1},{8,10},{9,11},{10,... | collective-permute-start | bytes 884744 | tf_op jit(solution)/shard_map/ppermute | solution.py:40
  23.9 5.5 %collective-permute-start.4 = (bf16[64,4096]{1,0:T(8,128)(2,1)}, bf16[64,4096]{1,0:T(8,128)(2,1)S(1)}, u32[]{:S(2)}, u32[]{:S(2)}) collective-permute-start(bf16[64,4096]{1,0:T(8,128)(2,1)} %get-tuple-element.87), channel_id=1, source_target_pairs={{0,8},{8,0},{16,24},{24,16},{1,9},{9,1},{17,25},{25,17},{2,10},{10... | collective-permute-start | bytes 1572872 | tf_op jit(solution)/shard_map/ppermute | solution.py:44
  25.0 21.9 %collective-permute-start.9 = (bf16[768,384]{1,0:T(8,128)(2,1)S(1)}, bf16[768,384]{1,0:T(8,128)(2,1)S(1)}, u32[]{:S(2)}, u32[]{:S(2)}) collective-permute-start(bf16[768,384]{1,0:T(8,128)(2,1)S(1)} %constant_dynamic-update-slice_fusion.refs_3_), channel_id=1, source_target_pairs={{0,2},{1,3},{2,4},{3,5},{4,6},{5,7},{6,0},{7,1},{8,10},{9,11},{10,... | collective-permute-start | bytes 1769480 | tf_op jit(solution)/shard_map/ppermute | solution.py:40
  27.8 31.1 %collective-permute-start.13 = (bf16[1536,384]{1,0:T(8,128)(2,1)S(1)}, bf16[1536,384]{1,0:T(8,128)(2,1)S(1)}, u32[]{:S(2)}, u32[]{:S(2)}) collective-permute-start(bf16[1536,384]{1,0:T(8,128)(2,1)S(1)} %pad_maximum_fusion), channel_id=1, source_target_pairs={{0,1},{1,0},{2,3},{3,2},{4,5},{5,4},{6,7},{7,6},{8,9},{9,8},{10,11... | collective-permute-start | bytes 3538952 | tf_op jit(solution)/shard_map/ppermute | solution.py:40
  29.5 8.2 %collective-permute-start.5 = (bf16[32,4096]{1,0:T(8,128)(2,1)S(1)}, bf16[32,4096]{1,0:T(8,128)(2,1)S(1)}, u32[]{:S(2)}, u32[]{:S(2)}) collective-permute-start(bf16[32,4096]{1,0:T(8,128)(2,1)S(1)} %add_convert_fusion.1), channel_id=1, source_target_pairs={{0,16},{8,24},{16,0},{24,8},{1,17},{9,25},{17,1},{25,9},{2,18},{10... | collective-permute-start | bytes 786440 | tf_op jit(solution)/shard_map/ppermute | solution.py:44
  34.4 70.0 %copy-start.34 = (f32[256,1]{1,0:T(8,128)}, f32[256,1]{1,0:T(8,128)S(1)}, u32[]{:S(2)}) copy-start(f32[256,1]{1,0:T(8,128)S(1)} %get-tuple-element.138) | copy-start | bytes 3076
  34.4 24.5 %copy-start.20 = (bf16[512,384]{1,0:T(8,128)(2,1)S(1)}, bf16[512,384]{1,0:T(8,128)(2,1)}, u32[]{:S(2)}) copy-start(bf16[512,384]{1,0:T(8,128)(2,1)} %refs_4_.1) | copy-start | bytes 1179652
  34.4 24.5 %copy-start.21 = (bf16[512,384]{1,0:T(8,128)(2,1)S(1)}, bf16[512,384]{1,0:T(8,128)(2,1)}, u32[]{:S(2)}) copy-start(bf16[512,384]{1,0:T(8,128)(2,1)} %refs_5_.1) | copy-start | bytes 1179652
  34.4 24.5 %copy-start.23 = (bf16[512,384]{1,0:T(8,128)(2,1)S(1)}, bf16[512,384]{1,0:T(8,128)(2,1)}, u32[]{:S(2)}) copy-start(bf16[512,384]{1,0:T(8,128)(2,1)} %copy-done.22) | copy-start | bytes 1179652
  34.4 24.5 %copy-start.25 = (bf16[512,384]{1,0:T(8,128)(2,1)S(1)}, bf16[512,384]{1,0:T(8,128)(2,1)}, u32[]{:S(2)}) copy-start(bf16[512,384]{1,0:T(8,128)(2,1)} %copy-done.24) | copy-start | bytes 1179652
  38.5 6.9 %collective-permute-start.6 = (bf16[32,1024]{1,0:T(8,128)(2,1)S(1)}, bf16[32,1024]{1,0:T(8,128)(2,1)S(1)}, u32[]{:S(2)}, u32[]{:S(2)}) collective-permute-start(bf16[32,1024]{1,0:T(8,128)(2,1)S(1)} %get-tuple-element.92), channel_id=1, source_target_pairs={{0,2},{1,3},{2,4},{3,5},{4,6},{5,7},{6,0},{7,1},{8,10},{9,11},{10,... | collective-permute-start | bytes 196616 | tf_op jit(solution)/shard_map/ppermute | solution.py:40
  39.0 7.8 %collective-permute-start.7 = (bf16[32,1024]{1,0:T(8,128)(2,1)S(1)}, bf16[32,1024]{1,0:T(8,128)(2,1)S(1)}, u32[]{:S(2)}, u32[]{:S(2)}) collective-permute-start(bf16[32,1024]{1,0:T(8,128)(2,1)S(1)} %get-tuple-element.93), channel_id=1, source_target_pairs={{0,4},{1,5},{2,6},{3,7},{4,0},{5,1},{6,2},{7,3},{8,12},{9,13},{10,... | collective-permute-start | bytes 196616 | tf_op jit(solution)/shard_map/ppermute | solution.py:40
  41.4 5.5 %collective-permute-start.8 = (bf16[32,1024]{1,0:T(8,128)(2,1)S(1)}, bf16[32,1024]{1,0:T(8,128)(2,1)S(1)}, u32[]{:S(2)}, u32[]{:S(2)}) collective-permute-start(bf16[32,1024]{1,0:T(8,128)(2,1)S(1)} %get-tuple-element.94), channel_id=1, source_target_pairs={{0,6},{1,7},{2,0},{3,1},{4,2},{5,3},{6,4},{7,5},{8,14},{9,15},{10,... | collective-permute-start | bytes 196616 | tf_op jit(solution)/shard_map/ppermute | solution.py:40
  46.9 17.0 %collective-permute-start.14 = (bf16[768,384]{1,0:T(8,128)(2,1)S(1)}, bf16[768,384]{1,0:T(8,128)(2,1)S(1)}, u32[]{:S(2)}, u32[]{:S(2)}) collective-permute-start(bf16[768,384]{1,0:T(8,128)(2,1)S(1)} %collective-permute-done.9.refs_4_), channel_id=1, source_target_pairs={{0,2},{1,3},{2,4},{3,5},{4,6},{5,7},{6,0},{7,1},{8,10},{9,11},{10,... | collective-permute-start | bytes 1769480 | tf_op jit(solution)/shard_map/ppermute | solution.py:40
  48.8 7.9 %collective-permute-start.11 = (bf16[4,32,1024]{2,1,0:T(8,128)(2,1)S(1)}, bf16[4,32,1024]{2,1,0:T(8,128)(2,1)S(1)}, u32[]{:S(2)}, u32[]{:S(2)}) collective-permute-start(bf16[4,32,1024]{2,1,0:T(8,128)(2,1)S(1)} %pad_maximum_fusion.3.refs_0_), channel_id=1, source_target_pairs={{0,16},{8,24},{16,0},{24,8},{1,17},{9,25},{17,1},{25,9},{2,18},{10... | collective-permute-start | bytes 786440 | tf_op jit(solution)/shard_map/ppermute | solution.py:44
  56.8 2.1 %collective-permute-start.12 = (bf16[4,32,1024]{2,1,0:T(8,128)(2,1)S(1)}, bf16[4,32,1024]{2,1,0:T(8,128)(2,1)S(1)}, u32[]{:S(2)}, u32[]{:S(2)}) collective-permute-start(bf16[4,32,1024]{2,1,0:T(8,128)(2,1)S(1)} %collective-permute-done.11.refs_2_), channel_id=1, source_target_pairs={{0,8},{8,0},{16,24},{24,16},{1,9},{9,1},{17,25},{25,17},{2,10},{10... | collective-permute-start | bytes 786440 | tf_op jit(solution)/shard_map/ppermute | solution.py:44
  56.8 2.1 %collective-permute-start.10 = (bf16[4,32,1024]{2,1,0:T(8,128)(2,1)S(1)}, bf16[4,32,1024]{2,1,0:T(8,128)(2,1)S(1)}, u32[]{:S(2)}, u32[]{:S(2)}) collective-permute-start(bf16[4,32,1024]{2,1,0:T(8,128)(2,1)S(1)} %pad_maximum_fusion.3.refs_0_), channel_id=1, source_target_pairs={{0,8},{8,0},{16,24},{24,16},{1,9},{9,1},{17,25},{25,17},{2,10},{10... | collective-permute-start | bytes 786440 | tf_op jit(solution)/shard_map/ppermute | solution.py:44
  57.3 25.0 %collective-permute-start.18 = (bf16[768,384]{1,0:T(8,128)(2,1)S(1)}, bf16[768,384]{1,0:T(8,128)(2,1)S(1)}, u32[]{:S(2)}, u32[]{:S(2)}) collective-permute-start(bf16[768,384]{1,0:T(8,128)(2,1)S(1)} %collective-permute-done.9.refs_4_), channel_id=1, source_target_pairs={{0,1},{1,0},{2,3},{3,2},{4,5},{5,4},{6,7},{7,6},{8,9},{9,8},{10,11... | collective-permute-start | bytes 1769480 | tf_op jit(solution)/shard_map/ppermute | solution.py:40
  63.9 6.7 %collective-permute-start.15 = (bf16[128,768]{1,0:T(8,128)(2,1)S(1)}, bf16[128,768]{1,0:T(8,128)(2,1)S(1)}, u32[]{:S(2)}, u32[]{:S(2)}) collective-permute-start(bf16[128,768]{1,0:T(8,128)(2,1)S(1)} %get-tuple-element.103), channel_id=1, source_target_pairs={{0,6},{1,7},{2,0},{3,1},{4,2},{5,3},{6,4},{7,5},{8,14},{9,15},{10,... | collective-permute-start | bytes 589832 | tf_op jit(solution)/shard_map/ppermute | solution.py:40
  63.9 18.2 %collective-permute-start.16 = (bf16[128,768]{1,0:T(8,128)(2,1)S(1)}, bf16[128,768]{1,0:T(8,128)(2,1)S(1)}, u32[]{:S(2)}, u32[]{:S(2)}) collective-permute-start(bf16[128,768]{1,0:T(8,128)(2,1)S(1)} %get-tuple-element.104), channel_id=1, source_target_pairs={{0,4},{1,5},{2,6},{3,7},{4,0},{5,1},{6,2},{7,3},{8,12},{9,13},{10,... | collective-permute-start | bytes 589832 | tf_op jit(solution)/shard_map/ppermute | solution.py:40
  65.6 16.6 %collective-permute-start.17 = (bf16[128,768]{1,0:T(8,128)(2,1)S(1)}, bf16[128,768]{1,0:T(8,128)(2,1)S(1)}, u32[]{:S(2)}, u32[]{:S(2)}) collective-permute-start(bf16[128,768]{1,0:T(8,128)(2,1)S(1)} %get-tuple-element.105), channel_id=1, source_target_pairs={{0,2},{1,3},{2,4},{3,5},{4,6},{5,7},{6,0},{7,1},{8,10},{9,11},{10,... | collective-permute-start | bytes 589832 | tf_op jit(solution)/shard_map/ppermute | solution.py:40
  66.0 19.9 %collective-permute-start.21 = (bf16[4,2,64,384]{3,2,1,0:T(8,128)(2,1)S(1)}, bf16[4,2,64,384]{3,2,1,0:T(8,128)(2,1)S(1)}, u32[]{:S(2)}, u32[]{:S(2)}) collective-permute-start(bf16[4,2,64,384]{3,2,1,0:T(8,128)(2,1)S(1)} %get-tuple-element.107), channel_id=1, source_target_pairs={{0,1},{1,0},{2,3},{3,2},{4,5},{5,4},{6,7},{7,6},{8,9},{9,8},{10,11... | collective-permute-start | bytes 1179656 | tf_op jit(solution)/shard_map/ppermute | solution.py:40
  70.6 32.5 %collective-permute-start.20 = (bf16[768,384]{1,0:T(8,128)(2,1)S(1)}, bf16[768,384]{1,0:T(8,128)(2,1)S(1)}, u32[]{:S(2)}, u32[]{:S(2)}) collective-permute-start(bf16[768,384]{1,0:T(8,128)(2,1)S(1)} %collective-permute-done.14.refs_6_), channel_id=1, source_target_pairs={{0,1},{1,0},{2,3},{3,2},{4,5},{5,4},{6,7},{7,6},{8,9},{9,8},{10,11... | collective-permute-start | bytes 1769480 | tf_op jit(solution)/shard_map/ppermute | solution.py:40
  82.3 5.7 %collective-permute-start.26 = (bf16[128,768]{1,0:T(8,128)(2,1)S(1)}, bf16[128,768]{1,0:T(8,128)(2,1)S(1)}, u32[]{:S(2)}, u32[]{:S(2)}) collective-permute-start(bf16[128,768]{1,0:T(8,128)(2,1)S(1)} %add_convert_fusion.3.refs_0_), channel_id=1, source_target_pairs={{0,6},{1,7},{2,0},{3,1},{4,2},{5,3},{6,4},{7,5},{8,14},{9,15},{10,... | collective-permute-start | bytes 589832 | tf_op jit(solution)/shard_map/ppermute | solution.py:40
  82.3 13.0 %collective-permute-start.23 = (bf16[128,768]{1,0:T(8,128)(2,1)S(1)}, bf16[128,768]{1,0:T(8,128)(2,1)S(1)}, u32[]{:S(2)}, u32[]{:S(2)}) collective-permute-start(bf16[128,768]{1,0:T(8,128)(2,1)S(1)} %add_convert_fusion.3.refs_0_), channel_id=1, source_target_pairs={{0,2},{1,3},{2,4},{3,5},{4,6},{5,7},{6,0},{7,1},{8,10},{9,11},{10,... | collective-permute-start | bytes 589832 | tf_op jit(solution)/shard_map/ppermute | solution.py:40
  84.3 17.2 %collective-permute-start.19 = (bf16[128,768]{1,0:T(8,128)(2,1)S(1)}, bf16[128,768]{1,0:T(8,128)(2,1)S(1)}, u32[]{:S(2)}, u32[]{:S(2)}) collective-permute-start(bf16[128,768]{1,0:T(8,128)(2,1)S(1)} %add_convert_fusion.3.refs_0_), channel_id=1, source_target_pairs={{0,4},{1,5},{2,6},{3,7},{4,0},{5,1},{6,2},{7,3},{8,12},{9,13},{10,... | collective-permute-start | bytes 589832 | tf_op jit(solution)/shard_map/ppermute | solution.py:40
  85.8 17.5 %collective-permute-start.22 = (bf16[128,768]{1,0:T(8,128)(2,1)S(1)}, bf16[128,768]{1,0:T(8,128)(2,1)S(1)}, u32[]{:S(2)}, u32[]{:S(2)}) collective-permute-start(bf16[128,768]{1,0:T(8,128)(2,1)S(1)} %add_convert_fusion.3.refs_0_), channel_id=1, source_target_pairs={{0,1},{1,0},{2,3},{3,2},{4,5},{5,4},{6,7},{7,6},{8,9},{9,8},{10,11... | collective-permute-start | bytes 589832 | tf_op jit(solution)/shard_map/ppermute | solution.py:40
  88.0 16.5 %collective-permute-start.27 = (bf16[128,768]{1,0:T(8,128)(2,1)S(1)}, bf16[128,768]{1,0:T(8,128)(2,1)S(1)}, u32[]{:S(2)}, u32[]{:S(2)}) collective-permute-start(bf16[128,768]{1,0:T(8,128)(2,1)S(1)} %collective-permute-done.26.refs_6_), channel_id=1, source_target_pairs={{0,1},{1,0},{2,3},{3,2},{4,5},{5,4},{6,7},{7,6},{8,9},{9,8},{10,11... | collective-permute-start | bytes 589832 | tf_op jit(solution)/shard_map/ppermute | solution.py:40
  95.3 14.7 %collective-permute-start.24 = (bf16[128,768]{1,0:T(8,128)(2,1)S(1)}, bf16[128,768]{1,0:T(8,128)(2,1)S(1)}, u32[]{:S(2)}, u32[]{:S(2)}) collective-permute-start(bf16[128,768]{1,0:T(8,128)(2,1)S(1)} %collective-permute-done.23.refs_2_), channel_id=1, source_target_pairs={{0,1},{1,0},{2,3},{3,2},{4,5},{5,4},{6,7},{7,6},{8,9},{9,8},{10,11... | collective-permute-start | bytes 589832 | tf_op jit(solution)/shard_map/ppermute | solution.py:40
  101.5 8.9 %collective-permute-start.25 = (bf16[128,768]{1,0:T(8,128)(2,1)S(1)}, bf16[128,768]{1,0:T(8,128)(2,1)S(1)}, u32[]{:S(2)}, u32[]{:S(2)}) collective-permute-start(bf16[128,768]{1,0:T(8,128)(2,1)S(1)} %collective-permute-done.19.refs_4_), channel_id=1, source_target_pairs={{0,1},{1,0},{2,3},{3,2},{4,5},{5,4},{6,7},{7,6},{8,9},{9,8},{10,11... | collective-permute-start | bytes 589832 | tf_op jit(solution)/shard_map/ppermute | solution.py:40
  103.2 12.2 %collective-permute-start.31 = (bf16[2,2,64,384]{3,2,1,0:T(8,128)(2,1)S(1)}, bf16[2,2,64,384]{3,2,1,0:T(8,128)(2,1)S(1)}, u32[]{:S(2)}, u32[]{:S(2)}) collective-permute-start(bf16[2,2,64,384]{3,2,1,0:T(8,128)(2,1)S(1)} %get-tuple-element.121), channel_id=1, source_target_pairs={{0,2},{1,3},{2,4},{3,5},{4,6},{5,7},{6,0},{7,1},{8,10},{9,11},{10,... | collective-permute-start | bytes 589832 | tf_op jit(solution)/shard_map/ppermute | solution.py:40
  103.3 16.4 %collective-permute-start.32 = (bf16[2,2,64,384]{3,2,1,0:T(8,128)(2,1)S(1)}, bf16[2,2,64,384]{3,2,1,0:T(8,128)(2,1)S(1)}, u32[]{:S(2)}, u32[]{:S(2)}) collective-permute-start(bf16[2,2,64,384]{3,2,1,0:T(8,128)(2,1)S(1)} %get-tuple-element.122), channel_id=1, source_target_pairs={{0,4},{1,5},{2,6},{3,7},{4,0},{5,1},{6,2},{7,3},{8,12},{9,13},{10,... | collective-permute-start | bytes 589832 | tf_op jit(solution)/shard_map/ppermute | solution.py:40
  104.5 15.3 %collective-permute-start.33 = (bf16[2,2,64,384]{3,2,1,0:T(8,128)(2,1)S(1)}, bf16[2,2,64,384]{3,2,1,0:T(8,128)(2,1)S(1)}, u32[]{:S(2)}, u32[]{:S(2)}) collective-permute-start(bf16[2,2,64,384]{3,2,1,0:T(8,128)(2,1)S(1)} %get-tuple-element.123), channel_id=1, source_target_pairs={{0,6},{1,7},{2,0},{3,1},{4,2},{5,3},{6,4},{7,5},{8,14},{9,15},{10,... | collective-permute-start | bytes 589832 | tf_op jit(solution)/shard_map/ppermute | solution.py:40
  113.3 38.0 %copy-start.26 = (bf16[2,256,384]{2,1,0:T(8,128)(2,1)}, bf16[2,256,384]{2,1,0:T(8,128)(2,1)S(1)}, u32[]{:S(2)}) copy-start(bf16[2,256,384]{2,1,0:T(8,128)(2,1)S(1)} %get-tuple-element.147.refs_4_) | copy-start | bytes 1179652
  113.3 43.5 %copy-start.16 = (bf16[3,128,768]{2,1,0:T(8,128)(2,1)}, bf16[3,128,768]{2,1,0:T(8,128)(2,1)S(1)}, u32[]{:S(2)}) copy-start(bf16[3,128,768]{2,1,0:T(8,128)(2,1)S(1)} %get-tuple-element.118.own_ref) | copy-start | bytes 1769476
  113.3 1.4 collective-permute-start.28
  119.9 21.9 %collective-permute-start.39 = (bf16[4,2,2,64,384]{4,3,2,1,0:T(8,128)(2,1)S(1)}, bf16[4,2,2,64,384]{4,3,2,1,0:T(8,128)(2,1)S(1)}, u32[]{:S(2)}, u32[]{:S(2)}) collective-permute-start(bf16[4,2,2,64,384]{4,3,2,1,0:T(8,128)(2,1)S(1)} %pad_maximum_fusion.1.refs_0_), channel_id=1, source_target_pairs={{0,16},{8,24},{16,0},{24,8},{1,17},{9,25},{17,1},{25,9},{2,18},{10... | collective-permute-start | bytes 2359304 | tf_op jit(solution)/shard_map/ppermute | solution.py:44
  121.4 17.8 %collective-permute-start.34 = (bf16[2,256,384]{2,1,0:T(8,128)(2,1)S(1)}, bf16[2,256,384]{2,1,0:T(8,128)(2,1)S(1)}, u32[]{:S(2)}, u32[]{:S(2)}) collective-permute-start(bf16[2,256,384]{2,1,0:T(8,128)(2,1)S(1)} %get-tuple-element.147.refs_4_), channel_id=1, source_target_pairs={{0,2},{1,3},{2,4},{3,5},{4,6},{5,7},{6,0},{7,1},{8,10},{9,11},{10,... | collective-permute-start | bytes 1179656 | tf_op jit(solution)/shard_map/ppermute | solution.py:40
  133.6 9.9 %collective-permute-start.29 = (bf16[3,128,768]{2,1,0:T(8,128)(2,1)S(1)}, bf16[3,128,768]{2,1,0:T(8,128)(2,1)S(1)}, u32[]{:S(2)}, u32[]{:S(2)}) collective-permute-start(bf16[3,128,768]{2,1,0:T(8,128)(2,1)S(1)} %get-tuple-element.118.own_ref), channel_id=1, source_target_pairs={{0,1},{1,0},{2,3},{3,2},{4,5},{5,4},{6,7},{7,6},{8,9},{9,8},{10,11... | collective-permute-start | bytes 1769480 | tf_op jit(solution)/shard_map/ppermute | solution.py:40
  134.1 16.4 %collective-permute-start.30 = (bf16[2,256,384]{2,1,0:T(8,128)(2,1)S(1)}, bf16[2,256,384]{2,1,0:T(8,128)(2,1)S(1)}, u32[]{:S(2)}, u32[]{:S(2)}) collective-permute-start(bf16[2,256,384]{2,1,0:T(8,128)(2,1)S(1)} %get-tuple-element.147.refs_4_), channel_id=1, source_target_pairs={{0,1},{1,0},{2,3},{3,2},{4,5},{5,4},{6,7},{7,6},{8,9},{9,8},{10,11... | collective-permute-start | bytes 1179656 | tf_op jit(solution)/shard_map/ppermute | solution.py:40
  139.2 17.6 %copy-start.28 = (bf16[2,256,384]{2,1,0:T(8,128)(2,1)}, bf16[2,256,384]{2,1,0:T(8,128)(2,1)S(1)}, u32[]{:S(2)}) copy-start(bf16[2,256,384]{2,1,0:T(8,128)(2,1)S(1)} %collective-permute-done.34.refs_5_) | copy-start | bytes 1179652
  139.2 12.0 %collective-permute-start.36 = (bf16[2,256,384]{2,1,0:T(8,128)(2,1)S(1)}, bf16[2,256,384]{2,1,0:T(8,128)(2,1)S(1)}, u32[]{:S(2)}, u32[]{:S(2)}) collective-permute-start(bf16[2,256,384]{2,1,0:T(8,128)(2,1)S(1)} %collective-permute-done.34.refs_5_), channel_id=1, source_target_pairs={{0,2},{1,3},{2,4},{3,5},{4,6},{5,7},{6,0},{7,1},{8,10},{9,11},{10,... | collective-permute-start | bytes 1179656 | tf_op jit(solution)/shard_map/ppermute | solution.py:40
  141.7 17.7 %collective-permute-start.38 = (bf16[4,2,2,64,384]{4,3,2,1,0:T(8,128)(2,1)S(1)}, bf16[4,2,2,64,384]{4,3,2,1,0:T(8,128)(2,1)S(1)}, u32[]{:S(2)}, u32[]{:S(2)}) collective-permute-start(bf16[4,2,2,64,384]{4,3,2,1,0:T(8,128)(2,1)S(1)} %pad_maximum_fusion.1.refs_0_), channel_id=1, source_target_pairs={{0,8},{8,0},{16,24},{24,16},{1,9},{9,1},{17,25},{25,17},{2,10},{10... | collective-permute-start | bytes 2359304 | tf_op jit(solution)/shard_map/ppermute | solution.py:44
  141.7 19.2 %collective-permute-start.40 = (bf16[4,2,2,64,384]{4,3,2,1,0:T(8,128)(2,1)S(1)}, bf16[4,2,2,64,384]{4,3,2,1,0:T(8,128)(2,1)S(1)}, u32[]{:S(2)}, u32[]{:S(2)}) collective-permute-start(bf16[4,2,2,64,384]{4,3,2,1,0:T(8,128)(2,1)S(1)} %collective-permute-done.39.refs_2_), channel_id=1, source_target_pairs={{0,8},{8,0},{16,24},{24,16},{1,9},{9,1},{17,25},{25,17},{2,10},{10... | collective-permute-start | bytes 2359304 | tf_op jit(solution)/shard_map/ppermute | solution.py:44
  143.5 13.3 %copy-start.18 = (bf16[3,128,768]{2,1,0:T(8,128)(2,1)}, bf16[3,128,768]{2,1,0:T(8,128)(2,1)S(1)}, u32[]{:S(2)}) copy-start(bf16[3,128,768]{2,1,0:T(8,128)(2,1)S(1)} %collective-permute-done.29.side_ref) | copy-start | bytes 1769476
  143.5 15.1 %collective-permute-start.35 = (bf16[2,256,384]{2,1,0:T(8,128)(2,1)S(1)}, bf16[2,256,384]{2,1,0:T(8,128)(2,1)S(1)}, u32[]{:S(2)}, u32[]{:S(2)}) collective-permute-start(bf16[2,256,384]{2,1,0:T(8,128)(2,1)S(1)} %collective-permute-done.34.refs_5_), channel_id=1, source_target_pairs={{0,1},{1,0},{2,3},{3,2},{4,5},{5,4},{6,7},{7,6},{8,9},{9,8},{10,11... | collective-permute-start | bytes 1179656 | tf_op jit(solution)/shard_map/ppermute | solution.py:40
  151.3 9.7 %collective-permute-start.37 = (bf16[2,256,384]{2,1,0:T(8,128)(2,1)S(1)}, bf16[2,256,384]{2,1,0:T(8,128)(2,1)}, u32[]{:S(2)}, u32[]{:S(2)}) collective-permute-start(bf16[2,256,384]{2,1,0:T(8,128)(2,1)S(1)} %collective-permute-done.36.refs_6_), channel_id=1, source_target_pairs={{0,2},{1,3},{2,4},{3,5},{4,6},{5,7},{6,0},{7,1},{8,10},{9,11},{10,... | collective-permute-start | bytes 1179656 | tf_op jit(solution)/shard_map/ppermute | solution.py:40
  159.4 12.2 %copy-start.10 = (bf16[2,256,384]{2,1,0:T(8,128)(2,1)S(1)}, bf16[2,256,384]{2,1,0:T(8,128)(2,1)}, u32[]{:S(2)}) copy-start(bf16[2,256,384]{2,1,0:T(8,128)(2,1)} %copy-done.9) | copy-start | bytes 1179652
  161.8 10.8 %collective-permute-start.41 = (bf16[2,256,1536]{2,1,0:T(8,128)(2,1)}, bf16[2,256,1536]{2,1,0:T(8,128)(2,1)}, u32[]{:S(2)}, u32[]{:S(2)}) collective-permute-start(bf16[2,256,1536]{2,1,0:T(8,128)(2,1)} %get-tuple-element.133), channel_id=1, source_target_pairs={{0,8},{8,0},{16,24},{24,16},{1,9},{9,1},{17,25},{25,17},{2,10},{10... | collective-permute-start | bytes 4718600 | tf_op jit(solution)/shard_map/ppermute | solution.py:44
  164.4 10.2 %collective-permute-start.42 = (f32[256,2]{1,0:T(8,128)}, f32[256,2]{1,0:T(8,128)S(1)}, u32[]{:S(2)}, u32[]{:S(2)}) collective-permute-start(f32[256,2]{1,0:T(8,128)} %add.57), channel_id=1, source_target_pairs={{0,16},{8,24},{16,0},{24,8},{1,17},{9,25},{17,1},{25,9},{2,18},{10... | collective-permute-start | bytes 6152 | tf_op jit(solution)/shard_map/ppermute | solution.py:44
  167.7 9.7 %collective-permute-start.45 = (bf16[128,768]{1,0:T(8,128)(2,1)S(1)}, bf16[128,768]{1,0:T(8,128)(2,1)S(1)}, u32[]{:S(2)}, u32[]{:S(2)}) collective-permute-start(bf16[128,768]{1,0:T(8,128)(2,1)S(1)} %get-tuple-element.159), channel_id=1, source_target_pairs={{0,2},{1,3},{2,4},{3,5},{4,6},{5,7},{6,0},{7,1},{8,10},{9,11},{10,... | collective-permute-start | bytes 589832 | tf_op jit(solution)/shard_map/ppermute | solution.py:40
  167.7 17.7 %collective-permute-start.46 = (bf16[128,768]{1,0:T(8,128)(2,1)S(1)}, bf16[128,768]{1,0:T(8,128)(2,1)S(1)}, u32[]{:S(2)}, u32[]{:S(2)}) collective-permute-start(bf16[128,768]{1,0:T(8,128)(2,1)S(1)} %get-tuple-element.160), channel_id=1, source_target_pairs={{0,4},{1,5},{2,6},{3,7},{4,0},{5,1},{6,2},{7,3},{8,12},{9,13},{10,... | collective-permute-start | bytes 589832 | tf_op jit(solution)/shard_map/ppermute | solution.py:40
  171.5 13.9 %collective-permute-start.47 = (bf16[128,768]{1,0:T(8,128)(2,1)S(1)}, bf16[128,768]{1,0:T(8,128)(2,1)S(1)}, u32[]{:S(2)}, u32[]{:S(2)}) collective-permute-start(bf16[128,768]{1,0:T(8,128)(2,1)S(1)} %get-tuple-element.161), channel_id=1, source_target_pairs={{0,6},{1,7},{2,0},{3,1},{4,2},{5,3},{6,4},{7,5},{8,14},{9,15},{10,... | collective-permute-start | bytes 589832 | tf_op jit(solution)/shard_map/ppermute | solution.py:40
  172.7 27.3 %collective-permute-start.44 = (bf16[4,256,384]{2,1,0:T(8,128)(2,1)S(1)}, bf16[4,256,384]{2,1,0:T(8,128)(2,1)S(1)}, u32[]{:S(2)}, u32[]{:S(2)}) collective-permute-start(bf16[4,256,384]{2,1,0:T(8,128)(2,1)S(1)} %bitcast.46), channel_id=1, source_target_pairs={{0,1},{1,0},{2,3},{3,2},{4,5},{5,4},{6,7},{7,6},{8,9},{9,8},{10,11... | collective-permute-start | bytes 2359304 | tf_op jit(solution)/shard_map/ppermute | solution.py:40
  173.2 20.6 %copy-start.29 = (bf16[2,256,384]{2,1,0:T(8,128)(2,1)S(1)}, bf16[2,256,384]{2,1,0:T(8,128)(2,1)}, u32[]{:S(2)}) copy-start(bf16[2,256,384]{2,1,0:T(8,128)(2,1)} %copy-done.28) | copy-start | bytes 1179652
  173.2 20.6 %copy-start.31 = (bf16[2,256,384]{2,1,0:T(8,128)(2,1)S(1)}, bf16[2,256,384]{2,1,0:T(8,128)(2,1)}, u32[]{:S(2)}) copy-start(bf16[2,256,384]{2,1,0:T(8,128)(2,1)} %copy-done.30) | copy-start | bytes 1179652
  173.2 20.6 %copy-start.33 = (bf16[2,256,384]{2,1,0:T(8,128)(2,1)S(1)}, bf16[2,256,384]{2,1,0:T(8,128)(2,1)}, u32[]{:S(2)}) copy-start(bf16[2,256,384]{2,1,0:T(8,128)(2,1)} %copy-done.32) | copy-start | bytes 1179652
  174.6 19.2 %copy-start.3 = (bf16[4,2,2,64,384]{4,3,2,1,0:T(8,128)(2,1)S(1)}, bf16[4,2,2,64,384]{4,3,2,1,0:T(8,128)(2,1)}, u32[]{:S(2)}) copy-start(bf16[4,2,2,64,384]{4,3,2,1,0:T(8,128)(2,1)} %copy-done.2) | copy-start | bytes 2359300
  174.6 19.2 %copy-start.5 = (bf16[4,2,2,64,384]{4,3,2,1,0:T(8,128)(2,1)S(1)}, bf16[4,2,2,64,384]{4,3,2,1,0:T(8,128)(2,1)}, u32[]{:S(2)}) copy-start(bf16[4,2,2,64,384]{4,3,2,1,0:T(8,128)(2,1)} %copy-done.4) | copy-start | bytes 2359300
  174.6 19.2 %copy-start.27 = (bf16[2,256,384]{2,1,0:T(8,128)(2,1)S(1)}, bf16[2,256,384]{2,1,0:T(8,128)(2,1)}, u32[]{:S(2)}) copy-start(bf16[2,256,384]{2,1,0:T(8,128)(2,1)} %copy-done.26) | copy-start | bytes 1179652
  174.7 19.2 %collective-permute-start.43 = (bf16[2,256,768]{2,1,0:T(8,128)(2,1)S(1)}, bf16[2,256,768]{2,1,0:T(8,128)(2,1)S(1)}, u32[]{:S(2)}, u32[]{:S(2)}) collective-permute-start(bf16[2,256,768]{2,1,0:T(8,128)(2,1)S(1)} %add_convert_fusion), channel_id=1, source_target_pairs={{0,16},{8,24},{16,0},{24,8},{1,17},{9,25},{17,1},{25,9},{2,18},{10... | collective-permute-start | bytes 2359304 | tf_op jit(solution)/shard_map/ppermute | solution.py:44
  (28 other events, 125.0 us)

commit v10 on v8

--- a/solution.py
+++ b/solution.py
@@ -836,7 +836,7 @@
     stage = (side_slots, side_mine, late, row_sums, tiles_x, tiles_core, away)
     side_slots, side_mine, late, row_sums, tiles_x, tiles_core, away = after(stage)
 
-    sides = [fsend(block, 0, 1) for block in late[1:3]]
+    joint = fsend(jnp.stack(late[1:3]).reshape(4, tokens, width_local), 0, 1)
     late = chain(list(late), pairs - 3)
     got = gsend(away, 1)
     width = model_width // 4
@@ -849,12 +849,12 @@
         after(slots, sent[0]), side_slots, place, video_counts, sample_caption, tokens, pairs
     )
     kv_parts = [fsend(terms[far], far, 0) for far in range(1, pairs, 2)]
-    stage = (sides, late, tiles_x, kv_parts, terms, far_out, sent[1])
-    sides, late, tiles_x, kv_parts, terms, far_out, sent_d = after(stage)
+    stage = (joint, late, tiles_x, kv_parts, terms, far_out, sent[1])
+    joint, late, tiles_x, kv_parts, terms, far_out, sent_d = after(stage)
 
     here = [((block, 0),) for block in late]
     tiles = [tiles, tiles_core, tiles_x, gsend(tiles_x, 1)]
-    there = [((block, 0),) for block in (side_mine, *sides)]
+    there = [((side_mine, 0),), ((joint, 0),), ((joint, 2),)]
     there += [((fsend(block, 0, 1), 0),) for block in late[3:]]
     known = weight_grads(tiles, here + there[:3], None, pairs)
     total = [

time: 198 us -> 193 us (0.975)
  waiting for transfers between devices: 86.2 us -> 78.3 us
  other arithmetic: 10.1 us -> 12.5 us
    ppermute x37 -> x36, waiting for transfers between devices: 72.2 us -> 62.8 us  [fsend(): return lax.ppermute(block, 'fsdp', perm)]
    another operation x0 -> x1, other arithmetic: none -> 2.3 us  [local(): joint = fsend(jnp.stack(late[1:3]).reshape(4, tokens, width_local), 0, 1)]
    ppermute x37 -> x36, starting transfers between devices: 52.2 us -> 51.8 us  [fsend(): return lax.ppermute(block, 'fsdp', perm)]
  transfers between devices with their start and end apart: 50 -> 49, of which waited for: 18 -> 20; matrix products, arithmetic and copies ran while one was open for 4% -> 6% of each run, Pallas kernels for 18% -> 18%
where the time goes in v10:
time: 193 us
  waiting for transfers between devices  78.3 us (41%)
  starting transfers between devices  59.6 us (31%)
  Pallas kernels  36.5 us (19%)
  other arithmetic  12.5 us (6%)
  local copies, waits for them, and re-layouts  4.9 us (3%)
    ppermute x36, waiting for transfers between devices, fsend(): return lax.ppermute(block, 'fsdp', perm)  62.8 us
    ppermute x36, starting transfers between devices, fsend(): return lax.ppermute(block, 'fsdp', perm)  51.8 us
    pallas_call x9, Pallas kernels, call(): pl.pallas_call(body, out_shape=out_shape, in_specs=specs, out_specs=jax.t...  21.4 us
    ppermute x13, waiting for transfers between devices, gsend(): lax.ppermute(block, 'grp', [(s, s ^ flip) for s in range(lax.axis_size('g...  15.5 us
    pallas_call x1, Pallas kernels, project_text(): pl.pallas_call(body, grid=(steps,), out_shape=shaped((rows, 3 * width)),...  7.96 us
    ppermute x13, starting transfers between devices, gsend(): lax.ppermute(block, 'grp', [(s, s ^ flip) for s in range(lax.axis_size('g...  7.82 us
    pallas_call x1, Pallas kernels, attend_text(): pl.pallas_call(body, grid=(steps,), out_shape=[shaped((rows // 2, depth))...  7.14 us
    unnamed x75, local copies, waits for them, and re-layouts  3.96 us
  transfers between devices with their start and end apart: 49, of which 20 were waited for; matrix products, arithmetic and copies ran while one was open for 6% of the time, Pallas kernels for 18%

profile of v10, /device:TPU:0, one launch (start us, length us, event | category | flops | bytes accessed | tf_op | source)
XLA Modules:
  0.0 192.9 jit_solution(15732317069722139223)
XLA Ops:
  0.6 3.0 %collective-permute-start.2 = (bf16[512,384]{1,0:T(8,128)(2,1)}, bf16[512,384]{1,0:T(8,128)(2,1)S(1)}, u32[]{:S(2)}, u32[]{:S(2)}) collective-permute-start(bf16[512,384]{1,0:T(8,128)(2,1)} %refs_4_.1), channel_id=1, source_target_pairs={{0,1},{1,0},{2,3},{3,2},{4,5},{5,4},{6,7},{7,6},{8,9},{9,8},{10,11... | collective-permute-start | bytes 1179656 | tf_op jit(solution)/shard_map/ppermute | solution.py:40
  3.7 2.0 %collective-permute-start = (bf16[384,384]{1,0:T(8,128)(2,1)}, bf16[384,384]{1,0:T(8,128)(2,1)S(1)}, u32[]{:S(2)}, u32[]{:S(2)}) collective-permute-start(bf16[384,384]{1,0:T(8,128)(2,1)} %refs_0_.3), channel_id=1, source_target_pairs={{0,2},{1,3},{2,4},{3,5},{4,6},{5,7},{6,0},{7,1},{8,10},{9,11},{10,... | collective-permute-start | bytes 884744 | tf_op jit(solution)/shard_map/ppermute | solution.py:40
  5.7 1.6 collective-permute-start.1
  7.3 8.0 %shard_map.208.qkv_ref = bf16[128,1536]{1,0:T(8,128)(2,1)} custom-call(bf16[128,4096]{1,0:T(8,128)(2,1)} %bitcast.43, f32[1,4096]{1,0:T(1,128)} %bitcast.57, bf16[4096,512]{1,0:T(8,128)(2,1)} %wq_ref.1, bf16[4096,512]{1,0:T(8,128)(2,1)} %wk_ref.1, bf16[4096,512]{1,0:T(8,128)(2,1)} %wv_ref.1), custom_call_target="tpu_custom_call" | custom-call | flops 1 | bytes 1 | tf_op jit(solution)/shard_map/pallas_call | solution.py:350
  16.0 7.1 %shard_map.209 = (bf16[64,4096]{1,0:T(8,128)(2,1)}, bf16[64,4096]{1,0:T(8,128)(2,1)}) custom-call(s32[3]{0:T(128)} %pad_add_fusion.place_ref, s32[8]{0:T(128)} %len_ref.3, bf16[128,1536]{1,0:T(8,128)(2,1)} %shard_map.208.qkv_ref, f32[8,128,128]{2,1,0:T(8,128)} %bias_ref.1, bf16[512,4096]{1,0:T(8,128)(2,1)} %out_ref.1), custom_call_target="tpu_custom_call" | custom-call | flops 1 | bytes 1 | tf_op jit(solution)/shard_map/pallas_call | solution.py:394
  24.2 1.6 collective-permute-start.9
  25.9 1.2 pad_maximum_fusion
  27.1 1.6 collective-permute-start.13
  28.7 1.6 collective-permute-start.5
  30.3 2.7 %shard_map.210 = (bf16[256,3072]{1,0:T(8,128)(2,1)S(1)}, f32[256,1]{1,0:T(8,128)S(1)}, f32[256,1]{1,0:T(8,128)S(1)}, bf16[4,2,64,384]{3,2,1,0:T(8,128)(2,1)S(1)}, bf16[4,2,64,384]{3,2,1,0:T(8,128)(2,1)S(1)}) custom-call(s32[3]{0:T(128)S(1)} %copy-done.25, bf16[256,3072]{1,0:T(8,128)(2,1)S(1)} %copy-done.6, bf16[256,3072]{1,0:T(8,128)(2,1)S(1)} %copy-done), custom_call_target="tpu_custom_call" | custom-call | flops 1 | bytes 1 | tf_op jit(solution)/shard_map/pallas_call | solution.py:307
  33.7 3.2 %collective-permute-done.5.far_ref = bf16[32,4096]{1,0:T(8,128)(2,1)S(1)} collective-permute-done((bf16[32,4096]{1,0:T(8,128)(2,1)S(1)}, bf16[32,4096]{1,0:T(8,128)(2,1)S(1)}, u32[]{:S(2)}, u32[]{:S(2)}) %collective-permute-start.5) | collective-permute-done | bytes 262176 | tf_op jit(solution)/shard_map/ppermute | solution.py:44
  36.9 0.8 shard_map.211
  38.2 2.4 %collective-permute-start.7 = (bf16[32,1024]{1,0:T(8,128)(2,1)S(1)}, bf16[32,1024]{1,0:T(8,128)(2,1)S(1)}, u32[]{:S(2)}, u32[]{:S(2)}) collective-permute-start(bf16[32,1024]{1,0:T(8,128)(2,1)S(1)} %get-tuple-element.97), channel_id=1, source_target_pairs={{0,4},{1,5},{2,6},{3,7},{4,0},{5,1},{6,2},{7,3},{8,12},{9,13},{10,... | collective-permute-start | bytes 196616 | tf_op jit(solution)/shard_map/ppermute | solution.py:40
  40.6 1.3 collective-permute-start.8
  41.9 2.7 %collective-permute-done.6 = bf16[32,1024]{1,0:T(8,128)(2,1)S(1)} collective-permute-done((bf16[32,1024]{1,0:T(8,128)(2,1)S(1)}, bf16[32,1024]{1,0:T(8,128)(2,1)S(1)}, u32[]{:S(2)}, u32[]{:S(2)}) %collective-permute-start.6) | collective-permute-done | bytes 65568 | tf_op jit(solution)/shard_map/ppermute | solution.py:40
  44.6 1.4 collective-permute-done.7
  46.1 1.9 collective-permute-start.14
  48.0 1.5 collective-permute-start.11
  49.5 6.5 %collective-permute-done.11.refs_2_ = bf16[4,32,1024]{2,1,0:T(8,128)(2,1)S(1)} collective-permute-done((bf16[4,32,1024]{2,1,0:T(8,128)(2,1)S(1)}, bf16[4,32,1024]{2,1,0:T(8,128)(2,1)S(1)}, u32[]{:S(2)}, u32[]{:S(2)}) %collective-permute-start.11) | collective-permute-done | bytes 262176 | tf_op jit(solution)/shard_map/ppermute | solution.py:44
  56.5 1.6 collective-permute-start.18
  58.1 1.8 shard_map.212
  59.9 3.2 %collective-permute-done.14.refs_6_ = bf16[768,384]{1,0:T(8,128)(2,1)S(1)} collective-permute-done((bf16[768,384]{1,0:T(8,128)(2,1)S(1)}, bf16[768,384]{1,0:T(8,128)(2,1)S(1)}, u32[]{:S(2)}, u32[]{:S(2)}) %collective-permute-start.14) | collective-permute-done | bytes 589856 | tf_op jit(solution)/shard_map/ppermute | solution.py:40
  63.1 1.6 collective-permute-start.16
  65.2 1.6 collective-permute-start.21
  66.7 3.1 %collective-permute-done.15 = bf16[128,768]{1,0:T(8,128)(2,1)S(1)} collective-permute-done((bf16[128,768]{1,0:T(8,128)(2,1)S(1)}, bf16[128,768]{1,0:T(8,128)(2,1)S(1)}, u32[]{:S(2)}, u32[]{:S(2)}) %collective-permute-start.15) | collective-permute-done | bytes 196640 | tf_op jit(solution)/shard_map/ppermute | solution.py:40
  69.8 1.6 collective-permute-start.20
  71.4 10.0 %collective-permute-done.16 = bf16[128,768]{1,0:T(8,128)(2,1)S(1)} collective-permute-done((bf16[128,768]{1,0:T(8,128)(2,1)S(1)}, bf16[128,768]{1,0:T(8,128)(2,1)S(1)}, u32[]{:S(2)}, u32[]{:S(2)}) %collective-permute-start.16) | collective-permute-done | bytes 196640 | tf_op jit(solution)/shard_map/ppermute | solution.py:40
  81.5 1.5 collective-permute-start.19
  83.1 2.8 %collective-permute-start.26 = (bf16[128,768]{1,0:T(8,128)(2,1)S(1)}, bf16[128,768]{1,0:T(8,128)(2,1)S(1)}, u32[]{:S(2)}, u32[]{:S(2)}) collective-permute-start(bf16[128,768]{1,0:T(8,128)(2,1)S(1)} %add_convert_fusion.4.refs_0_), channel_id=1, source_target_pairs={{0,6},{1,7},{2,0},{3,1},{4,2},{5,3},{6,4},{7,5},{8,14},{9,15},{10,... | collective-permute-start | bytes 589832 | tf_op jit(solution)/shard_map/ppermute | solution.py:40
  85.9 1.6 collective-permute-start.22
  87.5 3.7 %collective-permute-done.23.refs_2_ = bf16[128,768]{1,0:T(8,128)(2,1)S(1)} collective-permute-done((bf16[128,768]{1,0:T(8,128)(2,1)S(1)}, bf16[128,768]{1,0:T(8,128)(2,1)S(1)}, u32[]{:S(2)}, u32[]{:S(2)}) %collective-permute-start.23) | collective-permute-done | bytes 196640 | tf_op jit(solution)/shard_map/ppermute | solution.py:40
  91.2 1.6 collective-permute-start.24
  92.8 4.2 %collective-permute-done.19.refs_4_ = bf16[128,768]{1,0:T(8,128)(2,1)S(1)} collective-permute-done((bf16[128,768]{1,0:T(8,128)(2,1)S(1)}, bf16[128,768]{1,0:T(8,128)(2,1)S(1)}, u32[]{:S(2)}, u32[]{:S(2)}) %collective-permute-start.19) | collective-permute-done | bytes 196640 | tf_op jit(solution)/shard_map/ppermute | solution.py:40
  96.9 1.6 collective-permute-start.25
  99.1 6.5 %collective-permute-start.30 = (bf16[2,2,64,384]{3,2,1,0:T(8,128)(2,1)S(1)}, bf16[2,2,64,384]{3,2,1,0:T(8,128)(2,1)S(1)}, u32[]{:S(2)}, u32[]{:S(2)}) collective-permute-start(bf16[2,2,64,384]{3,2,1,0:T(8,128)(2,1)S(1)} %get-tuple-element.122), channel_id=1, source_target_pairs={{0,6},{1,7},{2,0},{3,1},{4,2},{5,3},{6,4},{7,5},{8,14},{9,15},{10,... | collective-permute-start | bytes 589832 | tf_op jit(solution)/shard_map/ppermute | solution.py:40
  106.3 2.8 %shard_map.213 = (bf16[256,384]{1,0:T(8,128)(2,1)S(1)}, bf16[256,384]{1,0:T(8,128)(2,1)S(1)}, f32[1,384]{1,0:T(1,128)S(1)}) custom-call(s32[3]{0:T(128)S(1)} %copy-done.25, bf16[256,3072]{1,0:T(8,128)(2,1)S(1)} %get-tuple-element.93.normed_ref, bf16[256,3072]{1,0:T(8,128)(2,1)S(1)} %copy-done, bf16[384,384]{1,0:T(8,128)(2,1)S(1)} %copy-done.4, ...), custom_call_target="tpu_custom_call" | custom-call | flops 1 | bytes 1 | tf_op jit(solution)/shard_map/pallas_call | solution.py:307
  109.7 2.8 %shard_map.214 = (bf16[2,256,384]{2,1,0:T(8,128)(2,1)S(1)}, bf16[256,384]{1,0:T(8,128)(2,1)S(1)}, bf16[256,384]{1,0:T(8,128)(2,1)S(1)}, f32[256,2]{1,0:T(8,128)S(1)}, bf16[3,128,768]{2,1,0:T(8,128)(2,1)S(1)}) custom-call(s32[3]{0:T(128)S(1)} %copy-done.25, s32[8]{0:T(128)S(1)} %copy-done.27, s32[8]{0:T(128)S(1)} %copy-done.28, s32[8]{0:T(128)S(1)} %copy-done.29, ...), custom_call_target="tpu_custom_call" | custom-call | flops 1 | bytes 1 | tf_op jit(solution)/shard_map/pallas_call | solution.py:307
  112.6 1.3 collective-permute-done.31
  114.0 8.0 %collective-permute-done.29 = bf16[2,2,64,384]{3,2,1,0:T(8,128)(2,1)S(1)} collective-permute-done((bf16[2,2,64,384]{3,2,1,0:T(8,128)(2,1)S(1)}, bf16[2,2,64,384]{3,2,1,0:T(8,128)(2,1)S(1)}, u32[]{:S(2)}, u32[]{:S(2)}) %collective-permute-start.29) | collective-permute-done | bytes 196640 | tf_op jit(solution)/shard_map/ppermute | solution.py:40
  122.1 1.6 collective-permute-start.36
  123.7 1.4 collective-permute-start.32
  125.7 9.4 %collective-permute-done.34.refs_5_ = bf16[2,256,384]{2,1,0:T(8,128)(2,1)S(1)} collective-permute-done((bf16[2,256,384]{2,1,0:T(8,128)(2,1)S(1)}, bf16[2,256,384]{2,1,0:T(8,128)(2,1)S(1)}, u32[]{:S(2)}, u32[]{:S(2)}) %collective-permute-start.34) | collective-permute-done | bytes 393248 | tf_op jit(solution)/shard_map/ppermute | solution.py:40
  135.1 4.4 %shard_map.215 = (bf16[2,256,768]{2,1,0:T(8,128)(2,1)S(1)}, bf16[2,256,768]{2,1,0:T(8,128)(2,1)S(1)}, bf16[2,256,1536]{2,1,0:T(8,128)(2,1)S(1)}) custom-call(s32[3]{0:T(128)S(1)} %copy-done.25, bf16[256,384]{1,0:T(8,128)(2,1)S(1)} %get-tuple-element.128.att_ref, bf16[256,384]{1,0:T(8,128)(2,1)S(1)} %get-tuple-element.129.dq_ref, ...), custom_call_target="tpu_custom_call" | custom-call | flops 1 | bytes 1 | tf_op jit(solution)/shard_map/pallas_call | solution.py:307
  139.4 8.4 %collective-permute-done.33.refs_8_ = bf16[2,256,384]{2,1,0:T(8,128)(2,1)S(1)} collective-permute-done((bf16[2,256,384]{2,1,0:T(8,128)(2,1)S(1)}, bf16[2,256,384]{2,1,0:T(8,128)(2,1)S(1)}, u32[]{:S(2)}, u32[]{:S(2)}) %collective-permute-start.33) | collective-permute-done | bytes 393248 | tf_op jit(solution)/shard_map/ppermute | solution.py:40
  148.0 2.3 %pad_maximum_fusion.2 = bf16[2,2,256,384]{3,2,1,0:T(8,128)(2,1)} fusion(bf16[1,2,256,384]{3,2,1,0:T(8,128)(2,1)} %bitcast.22, bf16[1,2,256,384]{3,2,1,0:T(8,128)(2,1)S(1)} %bitcast.45), kind=kLoop, calls=%fused_computation.17 | loop fusion | flops 393216 | bytes 1572864 | tf_op jit(solution)/shard_map/stack | solution.py:839
  150.3 1.4 collective-permute-start.39
  151.7 2.5 %collective-permute-start.40 = (bf16[2,256,384]{2,1,0:T(8,128)(2,1)}, bf16[2,256,384]{2,1,0:T(8,128)(2,1)}, u32[]{:S(2)}, u32[]{:S(2)}) collective-permute-start(bf16[2,256,384]{2,1,0:T(8,128)(2,1)} %collective-permute-done.35.refs_6_), channel_id=1, source_target_pairs={{0,2},{1,3},{2,4},{3,5},{4,6},{5,7},{6,0},{7,1},{8,10},{9,11},{10,... | collective-permute-start | bytes 1179656 | tf_op jit(solution)/shard_map/ppermute | solution.py:40
  154.7 1.2 fusion.9
  155.9 3.3 %collective-permute-done.43 = f32[256,2]{1,0:T(8,128)S(1)} collective-permute-done((f32[256,2]{1,0:T(8,128)S(1)}, f32[256,2]{1,0:T(8,128)S(1)}, u32[]{:S(2)}, u32[]{:S(2)}) %collective-permute-start.43) | collective-permute-done | bytes 2080 | tf_op jit(solution)/shard_map/ppermute | solution.py:44
  159.8 1.8 shard_map.216
  163.2 3.6 %collective-permute-start.42 = (bf16[128,768]{1,0:T(8,128)(2,1)}, bf16[128,768]{1,0:T(8,128)(2,1)}, u32[]{:S(2)}, u32[]{:S(2)}) collective-permute-start(bf16[128,768]{1,0:T(8,128)(2,1)} %get-tuple-element.144), channel_id=1, source_target_pairs={{0,6},{1,7},{2,0},{3,1},{4,2},{5,3},{6,4},{7,5},{8,14},{9,15},{10,... | collective-permute-start | bytes 589832 | tf_op jit(solution)/shard_map/ppermute | solution.py:40
  166.8 1.0 reduce
  167.8 1.0 reduce.2
  168.9 1.3 collective-permute-done.39.refs_9_
  170.2 2.4 %collective-permute-done.41 = bf16[128,768]{1,0:T(8,128)(2,1)} collective-permute-done((bf16[128,768]{1,0:T(8,128)(2,1)}, bf16[128,768]{1,0:T(8,128)(2,1)}, u32[]{:S(2)}, u32[]{:S(2)}) %collective-permute-start.41) | collective-permute-done | bytes 196640 | tf_op jit(solution)/shard_map/ppermute | solution.py:40
  173.2 2.1 %collective-permute-start.48 = (bf16[128,768]{1,0:T(8,128)(2,1)}, bf16[128,768]{1,0:T(8,128)(2,1)S(1)}, u32[]{:S(2)}, u32[]{:S(2)}) collective-permute-start(bf16[128,768]{1,0:T(8,128)(2,1)} %copy-done.30), channel_id=1, source_target_pairs={{0,4},{1,5},{2,6},{3,7},{4,0},{5,1},{6,2},{7,3},{8,12},{9,13},{10,... | collective-permute-start | bytes 589832 | tf_op jit(solution)/shard_map/ppermute | solution.py:40
  175.3 1.0 add_multiply_fusion
  176.9 1.5 collective-permute-start.45
  178.4 3.8 %collective-permute-done.48 = bf16[128,768]{1,0:T(8,128)(2,1)S(1)} collective-permute-done((bf16[128,768]{1,0:T(8,128)(2,1)}, bf16[128,768]{1,0:T(8,128)(2,1)S(1)}, u32[]{:S(2)}, u32[]{:S(2)}) %collective-permute-start.48) | collective-permute-done | bytes 196640 | tf_op jit(solution)/shard_map/ppermute | solution.py:40
  182.2 1.2 fusion.10
  184.2 3.0 %shard_map.217 = (f32[384,384]{1,0:T(8,128)S(1)}, f32[384,384]{1,0:T(8,128)S(1)}) custom-call(bf16[4,2,2,64,384]{4,3,2,1,0:T(8,128)(2,1)S(1)} %pad_maximum_fusion.1.refs_0_, bf16[4,2,2,64,384]{4,3,2,1,0:T(8,128)(2,1)S(1)} %copy-done.3, bf16[4,2,2,64,384]{4,3,2,1,0:T(8,128)(2,1)S(1)} %collective-permute-done.36.refs_2_, ...), custom_call_target="tpu_custom_call" | custom-call | flops 1 | bytes 1 | tf_op jit(solution)/shard_map/pallas_call | solution.py:307
  187.2 1.2 collective-permute-done.45
  188.4 1.3 shard_map.218
  190.5 2.5 %fusion.6 = (bf16[256,768]{1,0:T(8,128)(2,1)}, bf16[256,768]{1,0:T(8,128)(2,1)}) fusion(bf16[256,768]{1,0:T(8,128)(2,1)S(1)} %collective-permute-done.45, bf16[2,256,1536]{2,1,0:T(8,128)(2,1)S(1)} %copy-done.32, f32[256]{0:T(256)S(1)} %get-tuple-element.171, f32[256]{0:T(256)S(1)} %reduce.2, f32[256]{0:T(256)S(1)} %get-tuple-element.170, ...), kind=kLoop, calls=%fused_computation.15 | loop fusion | flops 4325376 | bytes 3936260 | tf_op jit(solution)/shard_map/convert_element_type | solution.py:871
  (138 shorter events, 12.4 us)
Async XLA Ops:
  0.6 22.5 %collective-permute-start.2 = (bf16[512,384]{1,0:T(8,128)(2,1)}, bf16[512,384]{1,0:T(8,128)(2,1)S(1)}, u32[]{:S(2)}, u32[]{:S(2)}) collective-permute-start(bf16[512,384]{1,0:T(8,128)(2,1)} %refs_4_.1), channel_id=1, source_target_pairs={{0,1},{1,0},{2,3},{3,2},{4,5},{5,4},{6,7},{7,6},{8,9},{9,8},{10,11... | collective-permute-start | bytes 1179656 | tf_op jit(solution)/shard_map/ppermute | solution.py:40
  3.7 19.5 %collective-permute-start.3 = (bf16[512,384]{1,0:T(8,128)(2,1)}, bf16[512,384]{1,0:T(8,128)(2,1)S(1)}, u32[]{:S(2)}, u32[]{:S(2)}) collective-permute-start(bf16[512,384]{1,0:T(8,128)(2,1)} %refs_5_.1), channel_id=1, source_target_pairs={{0,1},{1,0},{2,3},{3,2},{4,5},{5,4},{6,7},{7,6},{8,9},{9,8},{10,11... | collective-permute-start | bytes 1179656 | tf_op jit(solution)/shard_map/ppermute | solution.py:40
  3.7 19.4 %collective-permute-start = (bf16[384,384]{1,0:T(8,128)(2,1)}, bf16[384,384]{1,0:T(8,128)(2,1)S(1)}, u32[]{:S(2)}, u32[]{:S(2)}) collective-permute-start(bf16[384,384]{1,0:T(8,128)(2,1)} %refs_0_.3), channel_id=1, source_target_pairs={{0,2},{1,3},{2,4},{3,5},{4,6},{5,7},{6,0},{7,1},{8,10},{9,11},{10,... | collective-permute-start | bytes 884744 | tf_op jit(solution)/shard_map/ppermute | solution.py:40
  5.7 17.4 %collective-permute-start.1 = (bf16[384,384]{1,0:T(8,128)(2,1)}, bf16[384,384]{1,0:T(8,128)(2,1)S(1)}, u32[]{:S(2)}, u32[]{:S(2)}) collective-permute-start(bf16[384,384]{1,0:T(8,128)(2,1)} %refs_1_.3), channel_id=1, source_target_pairs={{0,2},{1,3},{2,4},{3,5},{4,6},{5,7},{6,0},{7,1},{8,10},{9,11},{10,... | collective-permute-start | bytes 884744 | tf_op jit(solution)/shard_map/ppermute | solution.py:40
  16.0 9.9 %copy-start.4 = (bf16[384,384]{1,0:T(8,128)(2,1)S(1)}, bf16[384,384]{1,0:T(8,128)(2,1)}, u32[]{:S(2)}) copy-start(bf16[384,384]{1,0:T(8,128)(2,1)} %refs_0_.3) | copy-start | bytes 884740
  16.0 9.9 %copy-start.5 = (bf16[384,384]{1,0:T(8,128)(2,1)S(1)}, bf16[384,384]{1,0:T(8,128)(2,1)}, u32[]{:S(2)}) copy-start(bf16[384,384]{1,0:T(8,128)(2,1)} %refs_1_.3) | copy-start | bytes 884740
  24.0 4.7 %collective-permute-start.4 = (bf16[64,4096]{1,0:T(8,128)(2,1)}, bf16[64,4096]{1,0:T(8,128)(2,1)S(1)}, u32[]{:S(2)}, u32[]{:S(2)}) collective-permute-start(bf16[64,4096]{1,0:T(8,128)(2,1)} %get-tuple-element.91), channel_id=1, source_target_pairs={{0,8},{8,0},{16,24},{24,16},{1,9},{9,1},{17,25},{25,17},{2,10},{10... | collective-permute-start | bytes 1572872 | tf_op jit(solution)/shard_map/ppermute | solution.py:44
  24.2 21.9 %collective-permute-start.9 = (bf16[768,384]{1,0:T(8,128)(2,1)S(1)}, bf16[768,384]{1,0:T(8,128)(2,1)S(1)}, u32[]{:S(2)}, u32[]{:S(2)}) collective-permute-start(bf16[768,384]{1,0:T(8,128)(2,1)S(1)} %constant_dynamic-update-slice_fusion.refs_3_), channel_id=1, source_target_pairs={{0,2},{1,3},{2,4},{3,5},{4,6},{5,7},{6,0},{7,1},{8,10},{9,11},{10,... | collective-permute-start | bytes 1769480 | tf_op jit(solution)/shard_map/ppermute | solution.py:40
  27.1 31.0 %collective-permute-start.13 = (bf16[1536,384]{1,0:T(8,128)(2,1)S(1)}, bf16[1536,384]{1,0:T(8,128)(2,1)S(1)}, u32[]{:S(2)}, u32[]{:S(2)}) collective-permute-start(bf16[1536,384]{1,0:T(8,128)(2,1)S(1)} %pad_maximum_fusion), channel_id=1, source_target_pairs={{0,1},{1,0},{2,3},{3,2},{4,5},{5,4},{6,7},{7,6},{8,9},{9,8},{10,11... | collective-permute-start | bytes 3538952 | tf_op jit(solution)/shard_map/ppermute | solution.py:40
  28.7 8.1 %collective-permute-start.5 = (bf16[32,4096]{1,0:T(8,128)(2,1)S(1)}, bf16[32,4096]{1,0:T(8,128)(2,1)S(1)}, u32[]{:S(2)}, u32[]{:S(2)}) collective-permute-start(bf16[32,4096]{1,0:T(8,128)(2,1)S(1)} %add_convert_fusion.2), channel_id=1, source_target_pairs={{0,16},{8,24},{16,0},{24,8},{1,17},{9,25},{17,1},{25,9},{2,18},{10... | collective-permute-start | bytes 786440 | tf_op jit(solution)/shard_map/ppermute | solution.py:44
  33.7 72.0 %copy-start.23 = (f32[256,1]{1,0:T(8,128)}, f32[256,1]{1,0:T(8,128)S(1)}, u32[]{:S(2)}) copy-start(f32[256,1]{1,0:T(8,128)S(1)} %get-tuple-element.163) | copy-start | bytes 3076
  33.7 24.4 %copy-start.17 = (bf16[512,384]{1,0:T(8,128)(2,1)S(1)}, bf16[512,384]{1,0:T(8,128)(2,1)}, u32[]{:S(2)}) copy-start(bf16[512,384]{1,0:T(8,128)(2,1)} %refs_4_.1) | copy-start | bytes 1179652
  33.7 24.4 %copy-start.18 = (bf16[512,384]{1,0:T(8,128)(2,1)S(1)}, bf16[512,384]{1,0:T(8,128)(2,1)}, u32[]{:S(2)}) copy-start(bf16[512,384]{1,0:T(8,128)(2,1)} %refs_5_.1) | copy-start | bytes 1179652
  33.7 24.4 %copy-start.20 = (bf16[512,384]{1,0:T(8,128)(2,1)S(1)}, bf16[512,384]{1,0:T(8,128)(2,1)}, u32[]{:S(2)}) copy-start(bf16[512,384]{1,0:T(8,128)(2,1)} %copy-done.19) | copy-start | bytes 1179652
  33.7 24.4 %copy-start.22 = (bf16[512,384]{1,0:T(8,128)(2,1)S(1)}, bf16[512,384]{1,0:T(8,128)(2,1)}, u32[]{:S(2)}) copy-start(bf16[512,384]{1,0:T(8,128)(2,1)} %copy-done.21) | copy-start | bytes 1179652
  37.7 6.9 %collective-permute-start.6 = (bf16[32,1024]{1,0:T(8,128)(2,1)S(1)}, bf16[32,1024]{1,0:T(8,128)(2,1)S(1)}, u32[]{:S(2)}, u32[]{:S(2)}) collective-permute-start(bf16[32,1024]{1,0:T(8,128)(2,1)S(1)} %get-tuple-element.96), channel_id=1, source_target_pairs={{0,2},{1,3},{2,4},{3,5},{4,6},{5,7},{6,0},{7,1},{8,10},{9,11},{10,... | collective-permute-start | bytes 196616 | tf_op jit(solution)/shard_map/ppermute | solution.py:40
  38.2 7.9 %collective-permute-start.7 = (bf16[32,1024]{1,0:T(8,128)(2,1)S(1)}, bf16[32,1024]{1,0:T(8,128)(2,1)S(1)}, u32[]{:S(2)}, u32[]{:S(2)}) collective-permute-start(bf16[32,1024]{1,0:T(8,128)(2,1)S(1)} %get-tuple-element.97), channel_id=1, source_target_pairs={{0,4},{1,5},{2,6},{3,7},{4,0},{5,1},{6,2},{7,3},{8,12},{9,13},{10,... | collective-permute-start | bytes 196616 | tf_op jit(solution)/shard_map/ppermute | solution.py:40
  40.6 5.5 %collective-permute-start.8 = (bf16[32,1024]{1,0:T(8,128)(2,1)S(1)}, bf16[32,1024]{1,0:T(8,128)(2,1)S(1)}, u32[]{:S(2)}, u32[]{:S(2)}) collective-permute-start(bf16[32,1024]{1,0:T(8,128)(2,1)S(1)} %get-tuple-element.98), channel_id=1, source_target_pairs={{0,6},{1,7},{2,0},{3,1},{4,2},{5,3},{6,4},{7,5},{8,14},{9,15},{10,... | collective-permute-start | bytes 196616 | tf_op jit(solution)/shard_map/ppermute | solution.py:40
  46.1 17.0 %collective-permute-start.14 = (bf16[768,384]{1,0:T(8,128)(2,1)S(1)}, bf16[768,384]{1,0:T(8,128)(2,1)S(1)}, u32[]{:S(2)}, u32[]{:S(2)}) collective-permute-start(bf16[768,384]{1,0:T(8,128)(2,1)S(1)} %collective-permute-done.9.refs_4_), channel_id=1, source_target_pairs={{0,2},{1,3},{2,4},{3,5},{4,6},{5,7},{6,0},{7,1},{8,10},{9,11},{10,... | collective-permute-start | bytes 1769480 | tf_op jit(solution)/shard_map/ppermute | solution.py:40
  48.0 7.9 %collective-permute-start.11 = (bf16[4,32,1024]{2,1,0:T(8,128)(2,1)S(1)}, bf16[4,32,1024]{2,1,0:T(8,128)(2,1)S(1)}, u32[]{:S(2)}, u32[]{:S(2)}) collective-permute-start(bf16[4,32,1024]{2,1,0:T(8,128)(2,1)S(1)} %pad_maximum_fusion.3.refs_0_), channel_id=1, source_target_pairs={{0,16},{8,24},{16,0},{24,8},{1,17},{9,25},{17,1},{25,9},{2,18},{10... | collective-permute-start | bytes 786440 | tf_op jit(solution)/shard_map/ppermute | solution.py:44
  56.0 2.1 %collective-permute-start.12 = (bf16[4,32,1024]{2,1,0:T(8,128)(2,1)S(1)}, bf16[4,32,1024]{2,1,0:T(8,128)(2,1)S(1)}, u32[]{:S(2)}, u32[]{:S(2)}) collective-permute-start(bf16[4,32,1024]{2,1,0:T(8,128)(2,1)S(1)} %collective-permute-done.11.refs_2_), channel_id=1, source_target_pairs={{0,8},{8,0},{16,24},{24,16},{1,9},{9,1},{17,25},{25,17},{2,10},{10... | collective-permute-start | bytes 786440 | tf_op jit(solution)/shard_map/ppermute | solution.py:44
  56.0 2.1 %collective-permute-start.10 = (bf16[4,32,1024]{2,1,0:T(8,128)(2,1)S(1)}, bf16[4,32,1024]{2,1,0:T(8,128)(2,1)S(1)}, u32[]{:S(2)}, u32[]{:S(2)}) collective-permute-start(bf16[4,32,1024]{2,1,0:T(8,128)(2,1)S(1)} %pad_maximum_fusion.3.refs_0_), channel_id=1, source_target_pairs={{0,8},{8,0},{16,24},{24,16},{1,9},{9,1},{17,25},{25,17},{2,10},{10... | collective-permute-start | bytes 786440 | tf_op jit(solution)/shard_map/ppermute | solution.py:44
  56.5 25.0 %collective-permute-start.18 = (bf16[768,384]{1,0:T(8,128)(2,1)S(1)}, bf16[768,384]{1,0:T(8,128)(2,1)S(1)}, u32[]{:S(2)}, u32[]{:S(2)}) collective-permute-start(bf16[768,384]{1,0:T(8,128)(2,1)S(1)} %collective-permute-done.9.refs_4_), channel_id=1, source_target_pairs={{0,1},{1,0},{2,3},{3,2},{4,5},{5,4},{6,7},{7,6},{8,9},{9,8},{10,11... | collective-permute-start | bytes 1769480 | tf_op jit(solution)/shard_map/ppermute | solution.py:40
  63.1 6.7 %collective-permute-start.15 = (bf16[128,768]{1,0:T(8,128)(2,1)S(1)}, bf16[128,768]{1,0:T(8,128)(2,1)S(1)}, u32[]{:S(2)}, u32[]{:S(2)}) collective-permute-start(bf16[128,768]{1,0:T(8,128)(2,1)S(1)} %get-tuple-element.107), channel_id=1, source_target_pairs={{0,6},{1,7},{2,0},{3,1},{4,2},{5,3},{6,4},{7,5},{8,14},{9,15},{10,... | collective-permute-start | bytes 589832 | tf_op jit(solution)/shard_map/ppermute | solution.py:40
  63.1 18.2 %collective-permute-start.16 = (bf16[128,768]{1,0:T(8,128)(2,1)S(1)}, bf16[128,768]{1,0:T(8,128)(2,1)S(1)}, u32[]{:S(2)}, u32[]{:S(2)}) collective-permute-start(bf16[128,768]{1,0:T(8,128)(2,1)S(1)} %get-tuple-element.108), channel_id=1, source_target_pairs={{0,4},{1,5},{2,6},{3,7},{4,0},{5,1},{6,2},{7,3},{8,12},{9,13},{10,... | collective-permute-start | bytes 589832 | tf_op jit(solution)/shard_map/ppermute | solution.py:40
  64.8 16.6 %collective-permute-start.17 = (bf16[128,768]{1,0:T(8,128)(2,1)S(1)}, bf16[128,768]{1,0:T(8,128)(2,1)S(1)}, u32[]{:S(2)}, u32[]{:S(2)}) collective-permute-start(bf16[128,768]{1,0:T(8,128)(2,1)S(1)} %get-tuple-element.109), channel_id=1, source_target_pairs={{0,2},{1,3},{2,4},{3,5},{4,6},{5,7},{6,0},{7,1},{8,10},{9,11},{10,... | collective-permute-start | bytes 589832 | tf_op jit(solution)/shard_map/ppermute | solution.py:40
  65.2 20.8 %collective-permute-start.21 = (bf16[4,2,64,384]{3,2,1,0:T(8,128)(2,1)S(1)}, bf16[4,2,64,384]{3,2,1,0:T(8,128)(2,1)S(1)}, u32[]{:S(2)}, u32[]{:S(2)}) collective-permute-start(bf16[4,2,64,384]{3,2,1,0:T(8,128)(2,1)S(1)} %get-tuple-element.111), channel_id=1, source_target_pairs={{0,1},{1,0},{2,3},{3,2},{4,5},{5,4},{6,7},{7,6},{8,9},{9,8},{10,11... | collective-permute-start | bytes 1179656 | tf_op jit(solution)/shard_map/ppermute | solution.py:40
  69.8 29.3 %collective-permute-start.20 = (bf16[768,384]{1,0:T(8,128)(2,1)S(1)}, bf16[768,384]{1,0:T(8,128)(2,1)S(1)}, u32[]{:S(2)}, u32[]{:S(2)}) collective-permute-start(bf16[768,384]{1,0:T(8,128)(2,1)S(1)} %collective-permute-done.14.refs_6_), channel_id=1, source_target_pairs={{0,1},{1,0},{2,3},{3,2},{4,5},{5,4},{6,7},{7,6},{8,9},{9,8},{10,11... | collective-permute-start | bytes 1769480 | tf_op jit(solution)/shard_map/ppermute | solution.py:40
  81.5 9.7 %collective-permute-start.23 = (bf16[128,768]{1,0:T(8,128)(2,1)S(1)}, bf16[128,768]{1,0:T(8,128)(2,1)S(1)}, u32[]{:S(2)}, u32[]{:S(2)}) collective-permute-start(bf16[128,768]{1,0:T(8,128)(2,1)S(1)} %add_convert_fusion.4.refs_0_), channel_id=1, source_target_pairs={{0,2},{1,3},{2,4},{3,5},{4,6},{5,7},{6,0},{7,1},{8,10},{9,11},{10,... | collective-permute-start | bytes 589832 | tf_op jit(solution)/shard_map/ppermute | solution.py:40
  81.5 15.4 %collective-permute-start.19 = (bf16[128,768]{1,0:T(8,128)(2,1)S(1)}, bf16[128,768]{1,0:T(8,128)(2,1)S(1)}, u32[]{:S(2)}, u32[]{:S(2)}) collective-permute-start(bf16[128,768]{1,0:T(8,128)(2,1)S(1)} %add_convert_fusion.4.refs_0_), channel_id=1, source_target_pairs={{0,4},{1,5},{2,6},{3,7},{4,0},{5,1},{6,2},{7,3},{8,12},{9,13},{10,... | collective-permute-start | bytes 589832 | tf_op jit(solution)/shard_map/ppermute | solution.py:40
  83.1 15.4 %collective-permute-start.26 = (bf16[128,768]{1,0:T(8,128)(2,1)S(1)}, bf16[128,768]{1,0:T(8,128)(2,1)S(1)}, u32[]{:S(2)}, u32[]{:S(2)}) collective-permute-start(bf16[128,768]{1,0:T(8,128)(2,1)S(1)} %add_convert_fusion.4.refs_0_), channel_id=1, source_target_pairs={{0,6},{1,7},{2,0},{3,1},{4,2},{5,3},{6,4},{7,5},{8,14},{9,15},{10,... | collective-permute-start | bytes 589832 | tf_op jit(solution)/shard_map/ppermute | solution.py:40
  85.9 19.6 %collective-permute-start.22 = (bf16[128,768]{1,0:T(8,128)(2,1)S(1)}, bf16[128,768]{1,0:T(8,128)(2,1)S(1)}, u32[]{:S(2)}, u32[]{:S(2)}) collective-permute-start(bf16[128,768]{1,0:T(8,128)(2,1)S(1)} %add_convert_fusion.4.refs_0_), channel_id=1, source_target_pairs={{0,1},{1,0},{2,3},{3,2},{4,5},{5,4},{6,7},{7,6},{8,9},{9,8},{10,11... | collective-permute-start | bytes 589832 | tf_op jit(solution)/shard_map/ppermute | solution.py:40
  91.2 14.4 %collective-permute-start.24 = (bf16[128,768]{1,0:T(8,128)(2,1)S(1)}, bf16[128,768]{1,0:T(8,128)(2,1)S(1)}, u32[]{:S(2)}, u32[]{:S(2)}) collective-permute-start(bf16[128,768]{1,0:T(8,128)(2,1)S(1)} %collective-permute-done.23.refs_2_), channel_id=1, source_target_pairs={{0,1},{1,0},{2,3},{3,2},{4,5},{5,4},{6,7},{7,6},{8,9},{9,8},{10,11... | collective-permute-start | bytes 589832 | tf_op jit(solution)/shard_map/ppermute | solution.py:40
  96.9 12.1 %collective-permute-start.25 = (bf16[128,768]{1,0:T(8,128)(2,1)S(1)}, bf16[128,768]{1,0:T(8,128)(2,1)S(1)}, u32[]{:S(2)}, u32[]{:S(2)}) collective-permute-start(bf16[128,768]{1,0:T(8,128)(2,1)S(1)} %collective-permute-done.19.refs_4_), channel_id=1, source_target_pairs={{0,1},{1,0},{2,3},{3,2},{4,5},{5,4},{6,7},{7,6},{8,9},{9,8},{10,11... | collective-permute-start | bytes 589832 | tf_op jit(solution)/shard_map/ppermute | solution.py:40
  98.5 11.2 %collective-permute-start.27 = (bf16[128,768]{1,0:T(8,128)(2,1)S(1)}, bf16[128,768]{1,0:T(8,128)(2,1)S(1)}, u32[]{:S(2)}, u32[]{:S(2)}) collective-permute-start(bf16[128,768]{1,0:T(8,128)(2,1)S(1)} %collective-permute-done.26.refs_6_), channel_id=1, source_target_pairs={{0,1},{1,0},{2,3},{3,2},{4,5},{5,4},{6,7},{7,6},{8,9},{9,8},{10,11... | collective-permute-start | bytes 589832 | tf_op jit(solution)/shard_map/ppermute | solution.py:40
  99.1 14.9 %collective-permute-start.30 = (bf16[2,2,64,384]{3,2,1,0:T(8,128)(2,1)S(1)}, bf16[2,2,64,384]{3,2,1,0:T(8,128)(2,1)S(1)}, u32[]{:S(2)}, u32[]{:S(2)}) collective-permute-start(bf16[2,2,64,384]{3,2,1,0:T(8,128)(2,1)S(1)} %get-tuple-element.122), channel_id=1, source_target_pairs={{0,6},{1,7},{2,0},{3,1},{4,2},{5,3},{6,4},{7,5},{8,14},{9,15},{10,... | collective-permute-start | bytes 589832 | tf_op jit(solution)/shard_map/ppermute | solution.py:40
  105.6 16.4 %collective-permute-start.29 = (bf16[2,2,64,384]{3,2,1,0:T(8,128)(2,1)S(1)}, bf16[2,2,64,384]{3,2,1,0:T(8,128)(2,1)S(1)}, u32[]{:S(2)}, u32[]{:S(2)}) collective-permute-start(bf16[2,2,64,384]{3,2,1,0:T(8,128)(2,1)S(1)} %get-tuple-element.121), channel_id=1, source_target_pairs={{0,4},{1,5},{2,6},{3,7},{4,0},{5,1},{6,2},{7,3},{8,12},{9,13},{10,... | collective-permute-start | bytes 589832 | tf_op jit(solution)/shard_map/ppermute | solution.py:40
  105.7 16.3 %collective-permute-start.28 = (bf16[2,2,64,384]{3,2,1,0:T(8,128)(2,1)S(1)}, bf16[2,2,64,384]{3,2,1,0:T(8,128)(2,1)S(1)}, u32[]{:S(2)}, u32[]{:S(2)}) collective-permute-start(bf16[2,2,64,384]{3,2,1,0:T(8,128)(2,1)S(1)} %get-tuple-element.120), channel_id=1, source_target_pairs={{0,2},{1,3},{2,4},{3,5},{4,6},{5,7},{6,0},{7,1},{8,10},{9,11},{10,... | collective-permute-start | bytes 589832 | tf_op jit(solution)/shard_map/ppermute | solution.py:40
  112.5 26.9 %copy-start.12 = (bf16[2,256,384]{2,1,0:T(8,128)(2,1)}, bf16[2,256,384]{2,1,0:T(8,128)(2,1)S(1)}, u32[]{:S(2)}) copy-start(bf16[2,256,384]{2,1,0:T(8,128)(2,1)S(1)} %get-tuple-element.154.refs_4_) | copy-start | bytes 1179652
  112.5 1.4 collective-permute-start.31
  113.9 40.3 %copy-start.35 = (f32[256,2]{1,0:T(8,128)}, f32[256,2]{1,0:T(8,128)S(1)}, u32[]{:S(2)}) copy-start(f32[256,2]{1,0:T(8,128)S(1)} %add.74) | copy-start | bytes 6148
  122.1 25.7 %collective-permute-start.36 = (bf16[4,2,2,64,384]{4,3,2,1,0:T(8,128)(2,1)S(1)}, bf16[4,2,2,64,384]{4,3,2,1,0:T(8,128)(2,1)S(1)}, u32[]{:S(2)}, u32[]{:S(2)}) collective-permute-start(bf16[4,2,2,64,384]{4,3,2,1,0:T(8,128)(2,1)S(1)} %pad_maximum_fusion.1.refs_0_), channel_id=1, source_target_pairs={{0,16},{8,24},{16,0},{24,8},{1,17},{9,25},{17,1},{25,9},{2,18},{10... | collective-permute-start | bytes 2359304 | tf_op jit(solution)/shard_map/ppermute | solution.py:44
  123.7 11.4 %collective-permute-start.34 = (bf16[2,256,384]{2,1,0:T(8,128)(2,1)S(1)}, bf16[2,256,384]{2,1,0:T(8,128)(2,1)S(1)}, u32[]{:S(2)}, u32[]{:S(2)}) collective-permute-start(bf16[2,256,384]{2,1,0:T(8,128)(2,1)S(1)} %get-tuple-element.154.refs_4_), channel_id=1, source_target_pairs={{0,2},{1,3},{2,4},{3,5},{4,6},{5,7},{6,0},{7,1},{8,10},{9,11},{10,... | collective-permute-start | bytes 1179656 | tf_op jit(solution)/shard_map/ppermute | solution.py:40
  123.7 24.2 %collective-permute-start.37 = (bf16[4,2,2,64,384]{4,3,2,1,0:T(8,128)(2,1)S(1)}, bf16[4,2,2,64,384]{4,3,2,1,0:T(8,128)(2,1)S(1)}, u32[]{:S(2)}, u32[]{:S(2)}) collective-permute-start(bf16[4,2,2,64,384]{4,3,2,1,0:T(8,128)(2,1)S(1)} %pad_maximum_fusion.1.refs_0_), channel_id=1, source_target_pairs={{0,8},{8,0},{16,24},{24,16},{1,9},{9,1},{17,25},{25,17},{2,10},{10... | collective-permute-start | bytes 2359304 | tf_op jit(solution)/shard_map/ppermute | solution.py:44
  123.7 24.2 %collective-permute-start.32 = (bf16[3,128,768]{2,1,0:T(8,128)(2,1)S(1)}, bf16[3,128,768]{2,1,0:T(8,128)(2,1)S(1)}, u32[]{:S(2)}, u32[]{:S(2)}) collective-permute-start(bf16[3,128,768]{2,1,0:T(8,128)(2,1)S(1)} %get-tuple-element.141.own_ref), channel_id=1, source_target_pairs={{0,1},{1,0},{2,3},{3,2},{4,5},{5,4},{6,7},{7,6},{8,9},{9,8},{10,11... | collective-permute-start | bytes 1769480 | tf_op jit(solution)/shard_map/ppermute | solution.py:40
  125.1 22.7 %collective-permute-start.33 = (bf16[2,256,384]{2,1,0:T(8,128)(2,1)S(1)}, bf16[2,256,384]{2,1,0:T(8,128)(2,1)S(1)}, u32[]{:S(2)}, u32[]{:S(2)}) collective-permute-start(bf16[2,256,384]{2,1,0:T(8,128)(2,1)S(1)} %get-tuple-element.154.refs_4_), channel_id=1, source_target_pairs={{0,1},{1,0},{2,3},{3,2},{4,5},{5,4},{6,7},{7,6},{8,9},{9,8},{10,11... | collective-permute-start | bytes 1179656 | tf_op jit(solution)/shard_map/ppermute | solution.py:40
  135.1 12.9 %copy-start.7 = (bf16[2,256,384]{2,1,0:T(8,128)(2,1)}, bf16[2,256,384]{2,1,0:T(8,128)(2,1)S(1)}, u32[]{:S(2)}) copy-start(bf16[2,256,384]{2,1,0:T(8,128)(2,1)S(1)} %collective-permute-done.34.refs_5_) | copy-start | bytes 1179652
  135.1 12.8 %collective-permute-start.35 = (bf16[2,256,384]{2,1,0:T(8,128)(2,1)S(1)}, bf16[2,256,384]{2,1,0:T(8,128)(2,1)}, u32[]{:S(2)}, u32[]{:S(2)}) collective-permute-start(bf16[2,256,384]{2,1,0:T(8,128)(2,1)S(1)} %collective-permute-done.34.refs_5_), channel_id=1, source_target_pairs={{0,2},{1,3},{2,4},{3,5},{4,6},{5,7},{6,0},{7,1},{8,10},{9,11},{10,... | collective-permute-start | bytes 1179656 | tf_op jit(solution)/shard_map/ppermute | solution.py:40
  139.4 16.5 %copy-start.10 = (bf16[2,256,768]{2,1,0:T(8,128)(2,1)}, bf16[2,256,768]{2,1,0:T(8,128)(2,1)S(1)}, u32[]{:S(2)}) copy-start(bf16[2,256,768]{2,1,0:T(8,128)(2,1)S(1)} %get-tuple-element.130) | copy-start | bytes 2359300
  147.9 6.8 %collective-permute-start.38 = (bf16[2,256,1536]{2,1,0:T(8,128)(2,1)S(1)}, bf16[2,256,1536]{2,1,0:T(8,128)(2,1)S(1)}, u32[]{:S(2)}, u32[]{:S(2)}) collective-permute-start(bf16[2,256,1536]{2,1,0:T(8,128)(2,1)S(1)} %get-tuple-element.135), channel_id=1, source_target_pairs={{0,8},{8,0},{16,24},{24,16},{1,9},{9,1},{17,25},{25,17},{2,10},{10... | collective-permute-start | bytes 4718600 | tf_op jit(solution)/shard_map/ppermute | solution.py:44
  150.3 19.9 %collective-permute-start.39 = (bf16[4,256,384]{2,1,0:T(8,128)(2,1)}, bf16[4,256,384]{2,1,0:T(8,128)(2,1)}, u32[]{:S(2)}, u32[]{:S(2)}) collective-permute-start(bf16[4,256,384]{2,1,0:T(8,128)(2,1)} %bitcast.23), channel_id=1, source_target_pairs={{0,1},{1,0},{2,3},{3,2},{4,5},{5,4},{6,7},{7,6},{8,9},{9,8},{10,11... | collective-permute-start | bytes 2359304 | tf_op jit(solution)/shard_map/ppermute | solution.py:40
  151.7 17.2 %collective-permute-start.40 = (bf16[2,256,384]{2,1,0:T(8,128)(2,1)}, bf16[2,256,384]{2,1,0:T(8,128)(2,1)}, u32[]{:S(2)}, u32[]{:S(2)}) collective-permute-start(bf16[2,256,384]{2,1,0:T(8,128)(2,1)} %collective-permute-done.35.refs_6_), channel_id=1, source_target_pairs={{0,2},{1,3},{2,4},{3,5},{4,6},{5,7},{6,0},{7,1},{8,10},{9,11},{10,... | collective-permute-start | bytes 1179656 | tf_op jit(solution)/shard_map/ppermute | solution.py:40
  154.2 5.0 %collective-permute-start.43 = (f32[256,2]{1,0:T(8,128)S(1)}, f32[256,2]{1,0:T(8,128)S(1)}, u32[]{:S(2)}, u32[]{:S(2)}) collective-permute-start(f32[256,2]{1,0:T(8,128)S(1)} %add.74), channel_id=1, source_target_pairs={{0,16},{8,24},{16,0},{24,8},{1,17},{9,25},{17,1},{25,9},{2,18},{10... | collective-permute-start | bytes 6152 | tf_op jit(solution)/shard_map/ppermute | solution.py:44
  159.2 25.0 %copy-start.8 = (bf16[2,256,384]{2,1,0:T(8,128)(2,1)S(1)}, bf16[2,256,384]{2,1,0:T(8,128)(2,1)}, u32[]{:S(2)}) copy-start(bf16[2,256,384]{2,1,0:T(8,128)(2,1)} %copy-done.7) | copy-start | bytes 1179652
  159.2 14.0 %collective-permute-start.44 = (bf16[256,768]{1,0:T(8,128)(2,1)}, bf16[256,768]{1,0:T(8,128)(2,1)}, u32[]{:S(2)}, u32[]{:S(2)}) collective-permute-start(bf16[256,768]{1,0:T(8,128)(2,1)} %get-tuple-element.148), channel_id=1, source_target_pairs={{0,16},{8,24},{16,0},{24,8},{1,17},{9,25},{17,1},{25,9},{2,18},{10... | collective-permute-start | bytes 1179656 | tf_op jit(solution)/shard_map/ppermute | solution.py:44
  163.0 9.7 %collective-permute-start.41 = (bf16[128,768]{1,0:T(8,128)(2,1)}, bf16[128,768]{1,0:T(8,128)(2,1)}, u32[]{:S(2)}, u32[]{:S(2)}) collective-permute-start(bf16[128,768]{1,0:T(8,128)(2,1)} %get-tuple-element.143), channel_id=1, source_target_pairs={{0,2},{1,3},{2,4},{3,5},{4,6},{5,7},{6,0},{7,1},{8,10},{9,11},{10,... | collective-permute-start | bytes 589832 | tf_op jit(solution)/shard_map/ppermute | solution.py:40
  163.2 9.9 %collective-permute-start.42 = (bf16[128,768]{1,0:T(8,128)(2,1)}, bf16[128,768]{1,0:T(8,128)(2,1)}, u32[]{:S(2)}, u32[]{:S(2)}) collective-permute-start(bf16[128,768]{1,0:T(8,128)(2,1)} %get-tuple-element.144), channel_id=1, source_target_pairs={{0,6},{1,7},{2,0},{3,1},{4,2},{5,3},{6,4},{7,5},{8,14},{9,15},{10,... | collective-permute-start | bytes 589832 | tf_op jit(solution)/shard_map/ppermute | solution.py:40
  168.8 15.3 %copy-start.3 = (bf16[4,2,2,64,384]{4,3,2,1,0:T(8,128)(2,1)S(1)}, bf16[4,2,2,64,384]{4,3,2,1,0:T(8,128)(2,1)}, u32[]{:S(2)}) copy-start(bf16[4,2,2,64,384]{4,3,2,1,0:T(8,128)(2,1)} %copy-done.2) | copy-start | bytes 2359300
  168.8 15.3 %copy-start.13 = (bf16[2,256,384]{2,1,0:T(8,128)(2,1)S(1)}, bf16[2,256,384]{2,1,0:T(8,128)(2,1)}, u32[]{:S(2)}) copy-start(bf16[2,256,384]{2,1,0:T(8,128)(2,1)} %copy-done.12) | copy-start | bytes 1179652
  168.9 15.3 %copy-start.15 = (bf16[2,256,384]{2,1,0:T(8,128)(2,1)S(1)}, bf16[2,256,384]{2,1,0:T(8,128)(2,1)}, u32[]{:S(2)}) copy-start(bf16[2,256,384]{2,1,0:T(8,128)(2,1)} %copy-done.14) | copy-start | bytes 1179652
  173.2 9.1 %collective-permute-start.48 = (bf16[128,768]{1,0:T(8,128)(2,1)}, bf16[128,768]{1,0:T(8,128)(2,1)S(1)}, u32[]{:S(2)}, u32[]{:S(2)}) collective-permute-start(bf16[128,768]{1,0:T(8,128)(2,1)} %copy-done.30), channel_id=1, source_target_pairs={{0,4},{1,5},{2,6},{3,7},{4,0},{5,1},{6,2},{7,3},{8,12},{9,13},{10,... | collective-permute-start | bytes 589832 | tf_op jit(solution)/shard_map/ppermute | solution.py:40
  175.3 8.9 %collective-permute-start.46 = (bf16[4,2,2,64,384]{4,3,2,1,0:T(8,128)(2,1)S(1)}, bf16[4,2,2,64,384]{4,3,2,1,0:T(8,128)(2,1)S(1)}, u32[]{:S(2)}, u32[]{:S(2)}) collective-permute-start(bf16[4,2,2,64,384]{4,3,2,1,0:T(8,128)(2,1)S(1)} %collective-permute-done.36.refs_2_), channel_id=1, source_target_pairs={{0,8},{8,0},{16,24},{24,16},{1,9},{9,1},{17,25},{25,17},{2,10},{10... | collective-permute-start | bytes 2359304 | tf_op jit(solution)/shard_map/ppermute | solution.py:44
  176.5 11.9 %collective-permute-start.47 = (bf16[2,256,384]{2,1,0:T(8,128)(2,1)}, bf16[2,256,384]{2,1,0:T(8,128)(2,1)S(1)}, u32[]{:S(2)}, u32[]{:S(2)}) collective-permute-start(bf16[2,256,384]{2,1,0:T(8,128)(2,1)} %collective-permute-done.40.refs_7_), channel_id=1, source_target_pairs={{0,1},{1,0},{2,3},{3,2},{4,5},{5,4},{6,7},{7,6},{8,9},{9,8},{10,11... | collective-permute-start | bytes 1179656 | tf_op jit(solution)/shard_map/ppermute | solution.py:40
  176.9 11.5 %collective-permute-start.45 = (bf16[256,768]{1,0:T(8,128)(2,1)}, bf16[256,768]{1,0:T(8,128)(2,1)S(1)}, u32[]{:S(2)}, u32[]{:S(2)}) collective-permute-start(bf16[256,768]{1,0:T(8,128)(2,1)} %get-tuple-element.151), channel_id=1, source_target_pairs={{0,16},{8,24},{16,0},{24,8},{1,17},{9,25},{17,1},{25,9},{2,18},{10... | collective-permute-start | bytes 1179656 | tf_op jit(solution)/shard_map/ppermute | solution.py:44
  (22 other events, 87.6 us)

commit v11 on v8

--- a/solution.py
+++ b/solution.py
@@ -848,7 +848,7 @@
     terms = caption_terms(
         after(slots, sent[0]), side_slots, place, video_counts, sample_caption, tokens, pairs
     )
-    kv_parts = [fsend(terms[far], far, 0) for far in range(1, pairs, 2)]
+    kv_parts = [fsend(terms[1], 1, 0)]
     stage = (sides, late, tiles_x, kv_parts, terms, far_out, sent[1])
     sides, late, tiles_x, kv_parts, terms, far_out, sent_d = after(stage)
 
@@ -869,7 +869,7 @@
         quarter(out_grad, g, 1).astype(F32)
         + inverse * (total[1] - row_sums[:, 0:1] - video_hat * row_sums[:, 1:2])
     ).astype(BF)
-    kv_parts += [fsend(terms[far], far, 0) for far in range(2, pairs, 2)]
+    kv_parts += [fsend(terms[far], far, 0) for far in range(2, pairs)]
     kv_grads = (terms[0] + sum(p.astype(F32) for p in kv_parts)).astype(BF)[None]
     key_grad = kv_grads[:, :, :width_local]
     value_grad = kv_grads[:, :, width_local:]

time: 198 us -> 192 us (0.970)
  waiting for transfers between devices: 86.2 us -> 80.2 us
    ppermute x37, waiting for transfers between devices: 72.2 us -> 65.6 us  [fsend(): return lax.ppermute(block, 'fsdp', perm)]
    unnamed x79 -> x73, local copies, waits for them, and re-layouts: 3.27 us -> 3.99 us
  transfers between devices with their start and end apart: 50 -> 50, of which waited for: 18 -> 19; matrix products, arithmetic and copies ran while one was open for 4% -> 4% of each run, Pallas kernels for 18% -> 18%
where the time goes in v11:
time: 192 us
  waiting for transfers between devices  80.2 us (42%)
  starting transfers between devices  59.1 us (31%)
  Pallas kernels  36.4 us (19%)
  other arithmetic  10.1 us (5%)
  local copies, waits for them, and re-layouts  4.93 us (3%)
    ppermute x37, waiting for transfers between devices, fsend(): return lax.ppermute(block, 'fsdp', perm)  65.6 us
    ppermute x37, starting transfers between devices, fsend(): return lax.ppermute(block, 'fsdp', perm)  52.3 us
    pallas_call x9, Pallas kernels, call(): pl.pallas_call(body, out_shape=out_shape, in_specs=specs, out_specs=jax.t...  21.3 us
    ppermute x13, waiting for transfers between devices, gsend(): lax.ppermute(block, 'grp', [(s, s ^ flip) for s in range(lax.axis_size('g...  14.6 us
    pallas_call x1, Pallas kernels, project_text(): pl.pallas_call(body, grid=(steps,), out_shape=shaped((rows, 3 * width)),...  7.96 us
    pallas_call x1, Pallas kernels, attend_text(): pl.pallas_call(body, grid=(steps,), out_shape=[shaped((rows // 2, depth))...  7.14 us
    ppermute x13, starting transfers between devices, gsend(): lax.ppermute(block, 'grp', [(s, s ^ flip) for s in range(lax.axis_size('g...  6.87 us
    unnamed x73, local copies, waits for them, and re-layouts  3.99 us
  transfers between devices with their start and end apart: 50, of which 19 were waited for; matrix products, arithmetic and copies ran while one was open for 4% of the time, Pallas kernels for 18%

profile of v11, /device:TPU:0, one launch (start us, length us, event | category | flops | bytes accessed | tf_op | source)
XLA Modules:
  0.0 191.9 jit_solution(12133401666714605129)
XLA Ops:
  0.6 3.0 %collective-permute-start.2 = (bf16[512,384]{1,0:T(8,128)(2,1)}, bf16[512,384]{1,0:T(8,128)(2,1)S(1)}, u32[]{:S(2)}, u32[]{:S(2)}) collective-permute-start(bf16[512,384]{1,0:T(8,128)(2,1)} %refs_4_.1), channel_id=1, source_target_pairs={{0,1},{1,0},{2,3},{3,2},{4,5},{5,4},{6,7},{7,6},{8,9},{9,8},{10,11... | collective-permute-start | bytes 1179656 | tf_op jit(solution)/shard_map/ppermute | solution.py:40
  3.7 2.0 %collective-permute-start = (bf16[384,384]{1,0:T(8,128)(2,1)}, bf16[384,384]{1,0:T(8,128)(2,1)S(1)}, u32[]{:S(2)}, u32[]{:S(2)}) collective-permute-start(bf16[384,384]{1,0:T(8,128)(2,1)} %refs_0_.3), channel_id=1, source_target_pairs={{0,2},{1,3},{2,4},{3,5},{4,6},{5,7},{6,0},{7,1},{8,10},{9,11},{10,... | collective-permute-start | bytes 884744 | tf_op jit(solution)/shard_map/ppermute | solution.py:40
  5.7 1.6 collective-permute-start.1
  7.3 8.0 %shard_map.208.qkv_ref = bf16[128,1536]{1,0:T(8,128)(2,1)} custom-call(bf16[128,4096]{1,0:T(8,128)(2,1)} %bitcast.40, f32[1,4096]{1,0:T(1,128)} %bitcast.53, bf16[4096,512]{1,0:T(8,128)(2,1)} %wq_ref.1, bf16[4096,512]{1,0:T(8,128)(2,1)} %wk_ref.1, bf16[4096,512]{1,0:T(8,128)(2,1)} %wv_ref.1), custom_call_target="tpu_custom_call" | custom-call | flops 1 | bytes 1 | tf_op jit(solution)/shard_map/pallas_call | solution.py:350
  16.0 7.1 %shard_map.209 = (bf16[64,4096]{1,0:T(8,128)(2,1)}, bf16[64,4096]{1,0:T(8,128)(2,1)}) custom-call(s32[3]{0:T(128)} %pad_add_fusion.place_ref, s32[8]{0:T(128)} %len_ref.3, bf16[128,1536]{1,0:T(8,128)(2,1)} %shard_map.208.qkv_ref, f32[8,128,128]{2,1,0:T(8,128)} %bias_ref.1, bf16[512,4096]{1,0:T(8,128)(2,1)} %out_ref.1), custom_call_target="tpu_custom_call" | custom-call | flops 1 | bytes 1 | tf_op jit(solution)/shard_map/pallas_call | solution.py:394
  23.2 0.8 copy-done.19
  24.2 1.6 collective-permute-start.9
  25.9 1.2 pad_maximum_fusion
  27.1 1.6 collective-permute-start.13
  28.7 1.6 collective-permute-start.5
  30.3 2.7 %shard_map.210 = (bf16[256,3072]{1,0:T(8,128)(2,1)S(1)}, f32[256,1]{1,0:T(8,128)S(1)}, f32[256,1]{1,0:T(8,128)S(1)}, bf16[4,2,64,384]{3,2,1,0:T(8,128)(2,1)S(1)}, bf16[4,2,64,384]{3,2,1,0:T(8,128)(2,1)S(1)}) custom-call(s32[3]{0:T(128)S(1)} %copy-done.23, bf16[256,3072]{1,0:T(8,128)(2,1)S(1)} %copy-done.6, bf16[256,3072]{1,0:T(8,128)(2,1)S(1)} %copy-done), custom_call_target="tpu_custom_call" | custom-call | flops 1 | bytes 1 | tf_op jit(solution)/shard_map/pallas_call | solution.py:307
  33.7 3.2 %collective-permute-done.5.far_ref = bf16[32,4096]{1,0:T(8,128)(2,1)S(1)} collective-permute-done((bf16[32,4096]{1,0:T(8,128)(2,1)S(1)}, bf16[32,4096]{1,0:T(8,128)(2,1)S(1)}, u32[]{:S(2)}, u32[]{:S(2)}) %collective-permute-start.5) | collective-permute-done | bytes 262176 | tf_op jit(solution)/shard_map/ppermute | solution.py:44
  36.9 0.8 shard_map.211
  38.2 2.4 %collective-permute-start.7 = (bf16[32,1024]{1,0:T(8,128)(2,1)S(1)}, bf16[32,1024]{1,0:T(8,128)(2,1)S(1)}, u32[]{:S(2)}, u32[]{:S(2)}) collective-permute-start(bf16[32,1024]{1,0:T(8,128)(2,1)S(1)} %get-tuple-element.98), channel_id=1, source_target_pairs={{0,4},{1,5},{2,6},{3,7},{4,0},{5,1},{6,2},{7,3},{8,12},{9,13},{10,... | collective-permute-start | bytes 196616 | tf_op jit(solution)/shard_map/ppermute | solution.py:40
  40.6 1.3 collective-permute-start.8
  41.9 2.7 %collective-permute-done.6 = bf16[32,1024]{1,0:T(8,128)(2,1)S(1)} collective-permute-done((bf16[32,1024]{1,0:T(8,128)(2,1)S(1)}, bf16[32,1024]{1,0:T(8,128)(2,1)S(1)}, u32[]{:S(2)}, u32[]{:S(2)}) %collective-permute-start.6) | collective-permute-done | bytes 65568 | tf_op jit(solution)/shard_map/ppermute | solution.py:40
  44.6 1.4 collective-permute-done.7
  46.1 1.9 %collective-permute-start.14 = (bf16[768,384]{1,0:T(8,128)(2,1)S(1)}, bf16[768,384]{1,0:T(8,128)(2,1)S(1)}, u32[]{:S(2)}, u32[]{:S(2)}) collective-permute-start(bf16[768,384]{1,0:T(8,128)(2,1)S(1)} %collective-permute-done.9.refs_4_), channel_id=1, source_target_pairs={{0,2},{1,3},{2,4},{3,5},{4,6},{5,7},{6,0},{7,1},{8,10},{9,11},{10,... | collective-permute-start | bytes 1769480 | tf_op jit(solution)/shard_map/ppermute | solution.py:40
  48.0 1.5 collective-permute-start.11
  49.5 6.5 %collective-permute-done.11.refs_2_ = bf16[4,32,1024]{2,1,0:T(8,128)(2,1)S(1)} collective-permute-done((bf16[4,32,1024]{2,1,0:T(8,128)(2,1)S(1)}, bf16[4,32,1024]{2,1,0:T(8,128)(2,1)S(1)}, u32[]{:S(2)}, u32[]{:S(2)}) %collective-permute-start.11) | collective-permute-done | bytes 262176 | tf_op jit(solution)/shard_map/ppermute | solution.py:44
  56.5 1.6 collective-permute-start.18
  58.1 1.8 shard_map.212
  59.9 3.2 %collective-permute-done.14.refs_6_ = bf16[768,384]{1,0:T(8,128)(2,1)S(1)} collective-permute-done((bf16[768,384]{1,0:T(8,128)(2,1)S(1)}, bf16[768,384]{1,0:T(8,128)(2,1)S(1)}, u32[]{:S(2)}, u32[]{:S(2)}) %collective-permute-start.14) | collective-permute-done | bytes 589856 | tf_op jit(solution)/shard_map/ppermute | solution.py:40
  63.1 1.6 collective-permute-start.16
  65.2 1.6 collective-permute-start.21
  66.7 3.1 %collective-permute-done.15 = bf16[128,768]{1,0:T(8,128)(2,1)S(1)} collective-permute-done((bf16[128,768]{1,0:T(8,128)(2,1)S(1)}, bf16[128,768]{1,0:T(8,128)(2,1)S(1)}, u32[]{:S(2)}, u32[]{:S(2)}) %collective-permute-start.15) | collective-permute-done | bytes 196640 | tf_op jit(solution)/shard_map/ppermute | solution.py:40
  69.8 1.6 collective-permute-start.20
  71.4 10.0 %collective-permute-done.16 = bf16[128,768]{1,0:T(8,128)(2,1)S(1)} collective-permute-done((bf16[128,768]{1,0:T(8,128)(2,1)S(1)}, bf16[128,768]{1,0:T(8,128)(2,1)S(1)}, u32[]{:S(2)}, u32[]{:S(2)}) %collective-permute-start.16) | collective-permute-done | bytes 196640 | tf_op jit(solution)/shard_map/ppermute | solution.py:40
  81.5 1.5 collective-permute-start.19
  83.1 2.8 %collective-permute-start.26 = (bf16[128,768]{1,0:T(8,128)(2,1)S(1)}, bf16[128,768]{1,0:T(8,128)(2,1)S(1)}, u32[]{:S(2)}, u32[]{:S(2)}) collective-permute-start(bf16[128,768]{1,0:T(8,128)(2,1)S(1)} %add_convert_fusion.4.refs_0_), channel_id=1, source_target_pairs={{0,6},{1,7},{2,0},{3,1},{4,2},{5,3},{6,4},{7,5},{8,14},{9,15},{10,... | collective-permute-start | bytes 589832 | tf_op jit(solution)/shard_map/ppermute | solution.py:40
  85.9 1.6 collective-permute-start.22
  87.5 3.7 %collective-permute-done.23.refs_2_ = bf16[128,768]{1,0:T(8,128)(2,1)S(1)} collective-permute-done((bf16[128,768]{1,0:T(8,128)(2,1)S(1)}, bf16[128,768]{1,0:T(8,128)(2,1)S(1)}, u32[]{:S(2)}, u32[]{:S(2)}) %collective-permute-start.23) | collective-permute-done | bytes 196640 | tf_op jit(solution)/shard_map/ppermute | solution.py:40
  91.2 1.6 collective-permute-start.24
  92.8 4.2 %collective-permute-done.19.refs_4_ = bf16[128,768]{1,0:T(8,128)(2,1)S(1)} collective-permute-done((bf16[128,768]{1,0:T(8,128)(2,1)S(1)}, bf16[128,768]{1,0:T(8,128)(2,1)S(1)}, u32[]{:S(2)}, u32[]{:S(2)}) %collective-permute-start.19) | collective-permute-done | bytes 196640 | tf_op jit(solution)/shard_map/ppermute | solution.py:40
  96.9 1.6 collective-permute-start.25
  99.1 6.5 %collective-permute-start.30 = (bf16[2,2,64,384]{3,2,1,0:T(8,128)(2,1)S(1)}, bf16[2,2,64,384]{3,2,1,0:T(8,128)(2,1)S(1)}, u32[]{:S(2)}, u32[]{:S(2)}) collective-permute-start(bf16[2,2,64,384]{3,2,1,0:T(8,128)(2,1)S(1)} %get-tuple-element.123), channel_id=1, source_target_pairs={{0,6},{1,7},{2,0},{3,1},{4,2},{5,3},{6,4},{7,5},{8,14},{9,15},{10,... | collective-permute-start | bytes 589832 | tf_op jit(solution)/shard_map/ppermute | solution.py:40
  106.2 2.8 %shard_map.213 = (bf16[256,384]{1,0:T(8,128)(2,1)S(1)}, bf16[256,384]{1,0:T(8,128)(2,1)S(1)}, f32[1,384]{1,0:T(1,128)S(1)}) custom-call(s32[3]{0:T(128)S(1)} %copy-done.23, bf16[256,3072]{1,0:T(8,128)(2,1)S(1)} %get-tuple-element.94.normed_ref, bf16[256,3072]{1,0:T(8,128)(2,1)S(1)} %copy-done, bf16[384,384]{1,0:T(8,128)(2,1)S(1)} %copy-done.4, ...), custom_call_target="tpu_custom_call" | custom-call | flops 1 | bytes 1 | tf_op jit(solution)/shard_map/pallas_call | solution.py:307
  109.7 2.8 %shard_map.214 = (bf16[2,256,384]{2,1,0:T(8,128)(2,1)S(1)}, bf16[256,384]{1,0:T(8,128)(2,1)S(1)}, bf16[256,384]{1,0:T(8,128)(2,1)S(1)}, f32[256,2]{1,0:T(8,128)S(1)}, bf16[3,128,768]{2,1,0:T(8,128)(2,1)S(1)}) custom-call(s32[3]{0:T(128)S(1)} %copy-done.23, s32[8]{0:T(128)S(1)} %copy-done.25, s32[8]{0:T(128)S(1)} %copy-done.26, s32[8]{0:T(128)S(1)} %copy-done.27, ...), custom_call_target="tpu_custom_call" | custom-call | flops 1 | bytes 1 | tf_op jit(solution)/shard_map/pallas_call | solution.py:307
  112.6 1.3 collective-permute-done.31
  114.0 8.0 %collective-permute-done.29 = bf16[2,2,64,384]{3,2,1,0:T(8,128)(2,1)S(1)} collective-permute-done((bf16[2,2,64,384]{3,2,1,0:T(8,128)(2,1)S(1)}, bf16[2,2,64,384]{3,2,1,0:T(8,128)(2,1)S(1)}, u32[]{:S(2)}, u32[]{:S(2)}) %collective-permute-start.29) | collective-permute-done | bytes 196640 | tf_op jit(solution)/shard_map/ppermute | solution.py:40
  122.1 1.6 collective-permute-start.36
  123.7 1.4 collective-permute-start.32
  125.7 9.5 %collective-permute-done.34.refs_5_ = bf16[2,256,384]{2,1,0:T(8,128)(2,1)} collective-permute-done((bf16[2,256,384]{2,1,0:T(8,128)(2,1)S(1)}, bf16[2,256,384]{2,1,0:T(8,128)(2,1)}, u32[]{:S(2)}, u32[]{:S(2)}) %collective-permute-start.34) | collective-permute-done | bytes 393248 | tf_op jit(solution)/shard_map/ppermute | solution.py:40
  135.2 4.4 %shard_map.215 = (bf16[2,256,768]{2,1,0:T(8,128)(2,1)S(1)}, bf16[2,256,768]{2,1,0:T(8,128)(2,1)S(1)}, bf16[2,256,1536]{2,1,0:T(8,128)(2,1)S(1)}) custom-call(s32[3]{0:T(128)S(1)} %copy-done.23, bf16[256,384]{1,0:T(8,128)(2,1)S(1)} %get-tuple-element.129.att_ref, bf16[256,384]{1,0:T(8,128)(2,1)S(1)} %get-tuple-element.130.dq_ref, ...), custom_call_target="tpu_custom_call" | custom-call | flops 1 | bytes 1 | tf_op jit(solution)/shard_map/pallas_call | solution.py:307
  139.5 8.3 %collective-permute-done.33.refs_8_ = bf16[2,256,384]{2,1,0:T(8,128)(2,1)S(1)} collective-permute-done((bf16[2,256,384]{2,1,0:T(8,128)(2,1)S(1)}, bf16[2,256,384]{2,1,0:T(8,128)(2,1)S(1)}, u32[]{:S(2)}, u32[]{:S(2)}) %collective-permute-start.33) | collective-permute-done | bytes 393248 | tf_op jit(solution)/shard_map/ppermute | solution.py:40
  148.0 1.5 collective-permute-start.40
  149.5 2.5 %collective-permute-start.41 = (bf16[2,256,384]{2,1,0:T(8,128)(2,1)}, bf16[2,256,384]{2,1,0:T(8,128)(2,1)}, u32[]{:S(2)}, u32[]{:S(2)}) collective-permute-start(bf16[2,256,384]{2,1,0:T(8,128)(2,1)} %collective-permute-done.35.refs_6_), channel_id=1, source_target_pairs={{0,2},{1,3},{2,4},{3,5},{4,6},{5,7},{6,0},{7,1},{8,10},{9,11},{10,... | collective-permute-start | bytes 1179656 | tf_op jit(solution)/shard_map/ppermute | solution.py:40
  152.9 1.2 fusion.9
  154.1 3.1 %collective-permute-done.43 = f32[256,2]{1,0:T(8,128)S(1)} collective-permute-done((f32[256,2]{1,0:T(8,128)S(1)}, f32[256,2]{1,0:T(8,128)S(1)}, u32[]{:S(2)}, u32[]{:S(2)}) %collective-permute-start.43) | collective-permute-done | bytes 2080 | tf_op jit(solution)/shard_map/ppermute | solution.py:44
  157.8 1.6 shard_map.216
  160.1 0.8 copy-done.14
  161.2 1.0 reduce
  162.2 1.0 reduce.2
  163.3 5.0 %collective-permute-done.39.refs_9_ = bf16[2,256,384]{2,1,0:T(8,128)(2,1)} collective-permute-done((bf16[2,256,384]{2,1,0:T(8,128)(2,1)}, bf16[2,256,384]{2,1,0:T(8,128)(2,1)}, u32[]{:S(2)}, u32[]{:S(2)}) %collective-permute-start.39) | collective-permute-done | bytes 393248 | tf_op jit(solution)/shard_map/ppermute | solution.py:40
  168.7 1.4 collective-permute-start.48
  170.1 2.9 %collective-permute-start.49 = (bf16[128,768]{1,0:T(8,128)(2,1)}, bf16[128,768]{1,0:T(8,128)(2,1)S(1)}, u32[]{:S(2)}, u32[]{:S(2)}) collective-permute-start(bf16[128,768]{1,0:T(8,128)(2,1)} %copy-done.28), channel_id=1, source_target_pairs={{0,6},{1,7},{2,0},{3,1},{4,2},{5,3},{6,4},{7,5},{8,14},{9,15},{10,... | collective-permute-start | bytes 589832 | tf_op jit(solution)/shard_map/ppermute | solution.py:40
  173.0 1.0 add_multiply_fusion
  174.2 1.6 collective-permute-start.47
  176.4 5.4 %collective-permute-done.48 = bf16[128,768]{1,0:T(8,128)(2,1)S(1)} collective-permute-done((bf16[128,768]{1,0:T(8,128)(2,1)}, bf16[128,768]{1,0:T(8,128)(2,1)S(1)}, u32[]{:S(2)}, u32[]{:S(2)}) %collective-permute-start.48) | collective-permute-done | bytes 196640 | tf_op jit(solution)/shard_map/ppermute | solution.py:40
  181.8 1.1 fusion.10
  183.7 3.1 %shard_map.217 = (f32[384,384]{1,0:T(8,128)S(1)}, f32[384,384]{1,0:T(8,128)S(1)}) custom-call(bf16[4,2,2,64,384]{4,3,2,1,0:T(8,128)(2,1)S(1)} %pad_maximum_fusion.1.refs_0_, bf16[4,2,2,64,384]{4,3,2,1,0:T(8,128)(2,1)S(1)} %copy-done.3, bf16[4,2,2,64,384]{4,3,2,1,0:T(8,128)(2,1)S(1)} %collective-permute-done.36.refs_2_, ...), custom_call_target="tpu_custom_call" | custom-call | flops 1 | bytes 1 | tf_op jit(solution)/shard_map/pallas_call | solution.py:307
  187.3 1.3 shard_map.218
  188.6 0.8 copy-done.31
  189.4 2.5 %fusion.6 = (bf16[256,768]{1,0:T(8,128)(2,1)}, bf16[256,768]{1,0:T(8,128)(2,1)}) fusion(bf16[256,768]{1,0:T(8,128)(2,1)S(1)} %collective-permute-done.45, bf16[2,256,1536]{2,1,0:T(8,128)(2,1)S(1)} %copy-done.31, f32[256]{0:T(256)S(1)} %get-tuple-element.173, f32[256]{0:T(256)S(1)} %reduce.2, f32[256]{0:T(256)S(1)} %get-tuple-element.172, ...), kind=kLoop, calls=%fused_computation.15 | loop fusion | flops 4325376 | bytes 3936260 | tf_op jit(solution)/shard_map/convert_element_type | solution.py:871
  (137 shorter events, 11.2 us)
Async XLA Ops:
  0.6 22.5 %collective-permute-start.2 = (bf16[512,384]{1,0:T(8,128)(2,1)}, bf16[512,384]{1,0:T(8,128)(2,1)S(1)}, u32[]{:S(2)}, u32[]{:S(2)}) collective-permute-start(bf16[512,384]{1,0:T(8,128)(2,1)} %refs_4_.1), channel_id=1, source_target_pairs={{0,1},{1,0},{2,3},{3,2},{4,5},{5,4},{6,7},{7,6},{8,9},{9,8},{10,11... | collective-permute-start | bytes 1179656 | tf_op jit(solution)/shard_map/ppermute | solution.py:40
  3.7 19.5 %collective-permute-start.3 = (bf16[512,384]{1,0:T(8,128)(2,1)}, bf16[512,384]{1,0:T(8,128)(2,1)S(1)}, u32[]{:S(2)}, u32[]{:S(2)}) collective-permute-start(bf16[512,384]{1,0:T(8,128)(2,1)} %refs_5_.1), channel_id=1, source_target_pairs={{0,1},{1,0},{2,3},{3,2},{4,5},{5,4},{6,7},{7,6},{8,9},{9,8},{10,11... | collective-permute-start | bytes 1179656 | tf_op jit(solution)/shard_map/ppermute | solution.py:40
  3.7 19.4 %collective-permute-start = (bf16[384,384]{1,0:T(8,128)(2,1)}, bf16[384,384]{1,0:T(8,128)(2,1)S(1)}, u32[]{:S(2)}, u32[]{:S(2)}) collective-permute-start(bf16[384,384]{1,0:T(8,128)(2,1)} %refs_0_.3), channel_id=1, source_target_pairs={{0,2},{1,3},{2,4},{3,5},{4,6},{5,7},{6,0},{7,1},{8,10},{9,11},{10,... | collective-permute-start | bytes 884744 | tf_op jit(solution)/shard_map/ppermute | solution.py:40
  5.7 17.4 %collective-permute-start.1 = (bf16[384,384]{1,0:T(8,128)(2,1)}, bf16[384,384]{1,0:T(8,128)(2,1)S(1)}, u32[]{:S(2)}, u32[]{:S(2)}) collective-permute-start(bf16[384,384]{1,0:T(8,128)(2,1)} %refs_1_.3), channel_id=1, source_target_pairs={{0,2},{1,3},{2,4},{3,5},{4,6},{5,7},{6,0},{7,1},{8,10},{9,11},{10,... | collective-permute-start | bytes 884744 | tf_op jit(solution)/shard_map/ppermute | solution.py:40
  16.0 9.9 %copy-start.5 = (bf16[384,384]{1,0:T(8,128)(2,1)S(1)}, bf16[384,384]{1,0:T(8,128)(2,1)}, u32[]{:S(2)}) copy-start(bf16[384,384]{1,0:T(8,128)(2,1)} %refs_1_.3) | copy-start | bytes 884740
  24.0 4.7 %collective-permute-start.4 = (bf16[64,4096]{1,0:T(8,128)(2,1)}, bf16[64,4096]{1,0:T(8,128)(2,1)S(1)}, u32[]{:S(2)}, u32[]{:S(2)}) collective-permute-start(bf16[64,4096]{1,0:T(8,128)(2,1)} %get-tuple-element.92), channel_id=1, source_target_pairs={{0,8},{8,0},{16,24},{24,16},{1,9},{9,1},{17,25},{25,17},{2,10},{10... | collective-permute-start | bytes 1572872 | tf_op jit(solution)/shard_map/ppermute | solution.py:44
  24.2 21.9 %collective-permute-start.9 = (bf16[768,384]{1,0:T(8,128)(2,1)S(1)}, bf16[768,384]{1,0:T(8,128)(2,1)S(1)}, u32[]{:S(2)}, u32[]{:S(2)}) collective-permute-start(bf16[768,384]{1,0:T(8,128)(2,1)S(1)} %constant_dynamic-update-slice_fusion.refs_3_), channel_id=1, source_target_pairs={{0,2},{1,3},{2,4},{3,5},{4,6},{5,7},{6,0},{7,1},{8,10},{9,11},{10,... | collective-permute-start | bytes 1769480 | tf_op jit(solution)/shard_map/ppermute | solution.py:40
  27.1 31.0 %collective-permute-start.13 = (bf16[1536,384]{1,0:T(8,128)(2,1)S(1)}, bf16[1536,384]{1,0:T(8,128)(2,1)S(1)}, u32[]{:S(2)}, u32[]{:S(2)}) collective-permute-start(bf16[1536,384]{1,0:T(8,128)(2,1)S(1)} %pad_maximum_fusion), channel_id=1, source_target_pairs={{0,1},{1,0},{2,3},{3,2},{4,5},{5,4},{6,7},{7,6},{8,9},{9,8},{10,11... | collective-permute-start | bytes 3538952 | tf_op jit(solution)/shard_map/ppermute | solution.py:40
  28.7 8.1 %collective-permute-start.5 = (bf16[32,4096]{1,0:T(8,128)(2,1)S(1)}, bf16[32,4096]{1,0:T(8,128)(2,1)S(1)}, u32[]{:S(2)}, u32[]{:S(2)}) collective-permute-start(bf16[32,4096]{1,0:T(8,128)(2,1)S(1)} %add_convert_fusion.2), channel_id=1, source_target_pairs={{0,16},{8,24},{16,0},{24,8},{1,17},{9,25},{17,1},{25,9},{2,18},{10... | collective-permute-start | bytes 786440 | tf_op jit(solution)/shard_map/ppermute | solution.py:44
  33.7 72.0 %copy-start.21 = (f32[256,1]{1,0:T(8,128)}, f32[256,1]{1,0:T(8,128)S(1)}, u32[]{:S(2)}) copy-start(f32[256,1]{1,0:T(8,128)S(1)} %get-tuple-element.165) | copy-start | bytes 3076
  33.7 24.4 %copy-start.15 = (bf16[512,384]{1,0:T(8,128)(2,1)S(1)}, bf16[512,384]{1,0:T(8,128)(2,1)}, u32[]{:S(2)}) copy-start(bf16[512,384]{1,0:T(8,128)(2,1)} %refs_4_.1) | copy-start | bytes 1179652
  33.7 24.4 %copy-start.16 = (bf16[512,384]{1,0:T(8,128)(2,1)S(1)}, bf16[512,384]{1,0:T(8,128)(2,1)}, u32[]{:S(2)}) copy-start(bf16[512,384]{1,0:T(8,128)(2,1)} %refs_5_.1) | copy-start | bytes 1179652
  33.7 24.4 %copy-start.18 = (bf16[512,384]{1,0:T(8,128)(2,1)S(1)}, bf16[512,384]{1,0:T(8,128)(2,1)}, u32[]{:S(2)}) copy-start(bf16[512,384]{1,0:T(8,128)(2,1)} %copy-done.17) | copy-start | bytes 1179652
  33.7 24.4 %copy-start.20 = (bf16[512,384]{1,0:T(8,128)(2,1)S(1)}, bf16[512,384]{1,0:T(8,128)(2,1)}, u32[]{:S(2)}) copy-start(bf16[512,384]{1,0:T(8,128)(2,1)} %copy-done.19) | copy-start | bytes 1179652
  37.7 6.9 %collective-permute-start.6 = (bf16[32,1024]{1,0:T(8,128)(2,1)S(1)}, bf16[32,1024]{1,0:T(8,128)(2,1)S(1)}, u32[]{:S(2)}, u32[]{:S(2)}) collective-permute-start(bf16[32,1024]{1,0:T(8,128)(2,1)S(1)} %get-tuple-element.97), channel_id=1, source_target_pairs={{0,2},{1,3},{2,4},{3,5},{4,6},{5,7},{6,0},{7,1},{8,10},{9,11},{10,... | collective-permute-start | bytes 196616 | tf_op jit(solution)/shard_map/ppermute | solution.py:40
  38.2 7.9 %collective-permute-start.7 = (bf16[32,1024]{1,0:T(8,128)(2,1)S(1)}, bf16[32,1024]{1,0:T(8,128)(2,1)S(1)}, u32[]{:S(2)}, u32[]{:S(2)}) collective-permute-start(bf16[32,1024]{1,0:T(8,128)(2,1)S(1)} %get-tuple-element.98), channel_id=1, source_target_pairs={{0,4},{1,5},{2,6},{3,7},{4,0},{5,1},{6,2},{7,3},{8,12},{9,13},{10,... | collective-permute-start | bytes 196616 | tf_op jit(solution)/shard_map/ppermute | solution.py:40
  40.6 5.5 %collective-permute-start.8 = (bf16[32,1024]{1,0:T(8,128)(2,1)S(1)}, bf16[32,1024]{1,0:T(8,128)(2,1)S(1)}, u32[]{:S(2)}, u32[]{:S(2)}) collective-permute-start(bf16[32,1024]{1,0:T(8,128)(2,1)S(1)} %get-tuple-element.99), channel_id=1, source_target_pairs={{0,6},{1,7},{2,0},{3,1},{4,2},{5,3},{6,4},{7,5},{8,14},{9,15},{10,... | collective-permute-start | bytes 196616 | tf_op jit(solution)/shard_map/ppermute | solution.py:40
  46.1 17.0 %collective-permute-start.14 = (bf16[768,384]{1,0:T(8,128)(2,1)S(1)}, bf16[768,384]{1,0:T(8,128)(2,1)S(1)}, u32[]{:S(2)}, u32[]{:S(2)}) collective-permute-start(bf16[768,384]{1,0:T(8,128)(2,1)S(1)} %collective-permute-done.9.refs_4_), channel_id=1, source_target_pairs={{0,2},{1,3},{2,4},{3,5},{4,6},{5,7},{6,0},{7,1},{8,10},{9,11},{10,... | collective-permute-start | bytes 1769480 | tf_op jit(solution)/shard_map/ppermute | solution.py:40
  48.0 7.9 %collective-permute-start.11 = (bf16[4,32,1024]{2,1,0:T(8,128)(2,1)S(1)}, bf16[4,32,1024]{2,1,0:T(8,128)(2,1)S(1)}, u32[]{:S(2)}, u32[]{:S(2)}) collective-permute-start(bf16[4,32,1024]{2,1,0:T(8,128)(2,1)S(1)} %pad_maximum_fusion.2.refs_0_), channel_id=1, source_target_pairs={{0,16},{8,24},{16,0},{24,8},{1,17},{9,25},{17,1},{25,9},{2,18},{10... | collective-permute-start | bytes 786440 | tf_op jit(solution)/shard_map/ppermute | solution.py:44
  56.0 2.1 %collective-permute-start.12 = (bf16[4,32,1024]{2,1,0:T(8,128)(2,1)S(1)}, bf16[4,32,1024]{2,1,0:T(8,128)(2,1)S(1)}, u32[]{:S(2)}, u32[]{:S(2)}) collective-permute-start(bf16[4,32,1024]{2,1,0:T(8,128)(2,1)S(1)} %collective-permute-done.11.refs_2_), channel_id=1, source_target_pairs={{0,8},{8,0},{16,24},{24,16},{1,9},{9,1},{17,25},{25,17},{2,10},{10... | collective-permute-start | bytes 786440 | tf_op jit(solution)/shard_map/ppermute | solution.py:44
  56.0 2.1 %collective-permute-start.10 = (bf16[4,32,1024]{2,1,0:T(8,128)(2,1)S(1)}, bf16[4,32,1024]{2,1,0:T(8,128)(2,1)S(1)}, u32[]{:S(2)}, u32[]{:S(2)}) collective-permute-start(bf16[4,32,1024]{2,1,0:T(8,128)(2,1)S(1)} %pad_maximum_fusion.2.refs_0_), channel_id=1, source_target_pairs={{0,8},{8,0},{16,24},{24,16},{1,9},{9,1},{17,25},{25,17},{2,10},{10... | collective-permute-start | bytes 786440 | tf_op jit(solution)/shard_map/ppermute | solution.py:44
  56.5 25.0 %collective-permute-start.18 = (bf16[768,384]{1,0:T(8,128)(2,1)S(1)}, bf16[768,384]{1,0:T(8,128)(2,1)S(1)}, u32[]{:S(2)}, u32[]{:S(2)}) collective-permute-start(bf16[768,384]{1,0:T(8,128)(2,1)S(1)} %collective-permute-done.9.refs_4_), channel_id=1, source_target_pairs={{0,1},{1,0},{2,3},{3,2},{4,5},{5,4},{6,7},{7,6},{8,9},{9,8},{10,11... | collective-permute-start | bytes 1769480 | tf_op jit(solution)/shard_map/ppermute | solution.py:40
  63.1 6.7 %collective-permute-start.15 = (bf16[128,768]{1,0:T(8,128)(2,1)S(1)}, bf16[128,768]{1,0:T(8,128)(2,1)S(1)}, u32[]{:S(2)}, u32[]{:S(2)}) collective-permute-start(bf16[128,768]{1,0:T(8,128)(2,1)S(1)} %get-tuple-element.108), channel_id=1, source_target_pairs={{0,6},{1,7},{2,0},{3,1},{4,2},{5,3},{6,4},{7,5},{8,14},{9,15},{10,... | collective-permute-start | bytes 589832 | tf_op jit(solution)/shard_map/ppermute | solution.py:40
  63.1 18.2 %collective-permute-start.16 = (bf16[128,768]{1,0:T(8,128)(2,1)S(1)}, bf16[128,768]{1,0:T(8,128)(2,1)S(1)}, u32[]{:S(2)}, u32[]{:S(2)}) collective-permute-start(bf16[128,768]{1,0:T(8,128)(2,1)S(1)} %get-tuple-element.109), channel_id=1, source_target_pairs={{0,4},{1,5},{2,6},{3,7},{4,0},{5,1},{6,2},{7,3},{8,12},{9,13},{10,... | collective-permute-start | bytes 589832 | tf_op jit(solution)/shard_map/ppermute | solution.py:40
  64.8 16.6 %collective-permute-start.17 = (bf16[128,768]{1,0:T(8,128)(2,1)S(1)}, bf16[128,768]{1,0:T(8,128)(2,1)S(1)}, u32[]{:S(2)}, u32[]{:S(2)}) collective-permute-start(bf16[128,768]{1,0:T(8,128)(2,1)S(1)} %get-tuple-element.110), channel_id=1, source_target_pairs={{0,2},{1,3},{2,4},{3,5},{4,6},{5,7},{6,0},{7,1},{8,10},{9,11},{10,... | collective-permute-start | bytes 589832 | tf_op jit(solution)/shard_map/ppermute | solution.py:40
  65.2 20.8 %collective-permute-start.21 = (bf16[4,2,64,384]{3,2,1,0:T(8,128)(2,1)S(1)}, bf16[4,2,64,384]{3,2,1,0:T(8,128)(2,1)S(1)}, u32[]{:S(2)}, u32[]{:S(2)}) collective-permute-start(bf16[4,2,64,384]{3,2,1,0:T(8,128)(2,1)S(1)} %get-tuple-element.112), channel_id=1, source_target_pairs={{0,1},{1,0},{2,3},{3,2},{4,5},{5,4},{6,7},{7,6},{8,9},{9,8},{10,11... | collective-permute-start | bytes 1179656 | tf_op jit(solution)/shard_map/ppermute | solution.py:40
  69.8 29.2 %collective-permute-start.20 = (bf16[768,384]{1,0:T(8,128)(2,1)S(1)}, bf16[768,384]{1,0:T(8,128)(2,1)S(1)}, u32[]{:S(2)}, u32[]{:S(2)}) collective-permute-start(bf16[768,384]{1,0:T(8,128)(2,1)S(1)} %collective-permute-done.14.refs_6_), channel_id=1, source_target_pairs={{0,1},{1,0},{2,3},{3,2},{4,5},{5,4},{6,7},{7,6},{8,9},{9,8},{10,11... | collective-permute-start | bytes 1769480 | tf_op jit(solution)/shard_map/ppermute | solution.py:40
  81.5 9.7 %collective-permute-start.23 = (bf16[128,768]{1,0:T(8,128)(2,1)S(1)}, bf16[128,768]{1,0:T(8,128)(2,1)S(1)}, u32[]{:S(2)}, u32[]{:S(2)}) collective-permute-start(bf16[128,768]{1,0:T(8,128)(2,1)S(1)} %add_convert_fusion.4.refs_0_), channel_id=1, source_target_pairs={{0,2},{1,3},{2,4},{3,5},{4,6},{5,7},{6,0},{7,1},{8,10},{9,11},{10,... | collective-permute-start | bytes 589832 | tf_op jit(solution)/shard_map/ppermute | solution.py:40
  81.5 15.4 %collective-permute-start.19 = (bf16[128,768]{1,0:T(8,128)(2,1)S(1)}, bf16[128,768]{1,0:T(8,128)(2,1)S(1)}, u32[]{:S(2)}, u32[]{:S(2)}) collective-permute-start(bf16[128,768]{1,0:T(8,128)(2,1)S(1)} %add_convert_fusion.4.refs_0_), channel_id=1, source_target_pairs={{0,4},{1,5},{2,6},{3,7},{4,0},{5,1},{6,2},{7,3},{8,12},{9,13},{10,... | collective-permute-start | bytes 589832 | tf_op jit(solution)/shard_map/ppermute | solution.py:40
  83.1 15.4 %collective-permute-start.26 = (bf16[128,768]{1,0:T(8,128)(2,1)S(1)}, bf16[128,768]{1,0:T(8,128)(2,1)S(1)}, u32[]{:S(2)}, u32[]{:S(2)}) collective-permute-start(bf16[128,768]{1,0:T(8,128)(2,1)S(1)} %add_convert_fusion.4.refs_0_), channel_id=1, source_target_pairs={{0,6},{1,7},{2,0},{3,1},{4,2},{5,3},{6,4},{7,5},{8,14},{9,15},{10,... | collective-permute-start | bytes 589832 | tf_op jit(solution)/shard_map/ppermute | solution.py:40
  85.9 19.6 %collective-permute-start.22 = (bf16[128,768]{1,0:T(8,128)(2,1)S(1)}, bf16[128,768]{1,0:T(8,128)(2,1)S(1)}, u32[]{:S(2)}, u32[]{:S(2)}) collective-permute-start(bf16[128,768]{1,0:T(8,128)(2,1)S(1)} %add_convert_fusion.4.refs_0_), channel_id=1, source_target_pairs={{0,1},{1,0},{2,3},{3,2},{4,5},{5,4},{6,7},{7,6},{8,9},{9,8},{10,11... | collective-permute-start | bytes 589832 | tf_op jit(solution)/shard_map/ppermute | solution.py:40
  91.2 14.4 %collective-permute-start.24 = (bf16[128,768]{1,0:T(8,128)(2,1)S(1)}, bf16[128,768]{1,0:T(8,128)(2,1)S(1)}, u32[]{:S(2)}, u32[]{:S(2)}) collective-permute-start(bf16[128,768]{1,0:T(8,128)(2,1)S(1)} %collective-permute-done.23.refs_2_), channel_id=1, source_target_pairs={{0,1},{1,0},{2,3},{3,2},{4,5},{5,4},{6,7},{7,6},{8,9},{9,8},{10,11... | collective-permute-start | bytes 589832 | tf_op jit(solution)/shard_map/ppermute | solution.py:40
  96.9 12.1 %collective-permute-start.25 = (bf16[128,768]{1,0:T(8,128)(2,1)S(1)}, bf16[128,768]{1,0:T(8,128)(2,1)S(1)}, u32[]{:S(2)}, u32[]{:S(2)}) collective-permute-start(bf16[128,768]{1,0:T(8,128)(2,1)S(1)} %collective-permute-done.19.refs_4_), channel_id=1, source_target_pairs={{0,1},{1,0},{2,3},{3,2},{4,5},{5,4},{6,7},{7,6},{8,9},{9,8},{10,11... | collective-permute-start | bytes 589832 | tf_op jit(solution)/shard_map/ppermute | solution.py:40
  98.5 11.2 %collective-permute-start.27 = (bf16[128,768]{1,0:T(8,128)(2,1)S(1)}, bf16[128,768]{1,0:T(8,128)(2,1)S(1)}, u32[]{:S(2)}, u32[]{:S(2)}) collective-permute-start(bf16[128,768]{1,0:T(8,128)(2,1)S(1)} %collective-permute-done.26.refs_6_), channel_id=1, source_target_pairs={{0,1},{1,0},{2,3},{3,2},{4,5},{5,4},{6,7},{7,6},{8,9},{9,8},{10,11... | collective-permute-start | bytes 589832 | tf_op jit(solution)/shard_map/ppermute | solution.py:40
  99.1 14.9 %collective-permute-start.30 = (bf16[2,2,64,384]{3,2,1,0:T(8,128)(2,1)S(1)}, bf16[2,2,64,384]{3,2,1,0:T(8,128)(2,1)S(1)}, u32[]{:S(2)}, u32[]{:S(2)}) collective-permute-start(bf16[2,2,64,384]{3,2,1,0:T(8,128)(2,1)S(1)} %get-tuple-element.123), channel_id=1, source_target_pairs={{0,6},{1,7},{2,0},{3,1},{4,2},{5,3},{6,4},{7,5},{8,14},{9,15},{10,... | collective-permute-start | bytes 589832 | tf_op jit(solution)/shard_map/ppermute | solution.py:40
  105.6 16.4 %collective-permute-start.29 = (bf16[2,2,64,384]{3,2,1,0:T(8,128)(2,1)S(1)}, bf16[2,2,64,384]{3,2,1,0:T(8,128)(2,1)S(1)}, u32[]{:S(2)}, u32[]{:S(2)}) collective-permute-start(bf16[2,2,64,384]{3,2,1,0:T(8,128)(2,1)S(1)} %get-tuple-element.122), channel_id=1, source_target_pairs={{0,4},{1,5},{2,6},{3,7},{4,0},{5,1},{6,2},{7,3},{8,12},{9,13},{10,... | collective-permute-start | bytes 589832 | tf_op jit(solution)/shard_map/ppermute | solution.py:40
  105.7 16.3 %collective-permute-start.28 = (bf16[2,2,64,384]{3,2,1,0:T(8,128)(2,1)S(1)}, bf16[2,2,64,384]{3,2,1,0:T(8,128)(2,1)S(1)}, u32[]{:S(2)}, u32[]{:S(2)}) collective-permute-start(bf16[2,2,64,384]{3,2,1,0:T(8,128)(2,1)S(1)} %get-tuple-element.121), channel_id=1, source_target_pairs={{0,2},{1,3},{2,4},{3,5},{4,6},{5,7},{6,0},{7,1},{8,10},{9,11},{10,... | collective-permute-start | bytes 589832 | tf_op jit(solution)/shard_map/ppermute | solution.py:40
  112.5 27.0 %copy-start.10 = (bf16[2,256,384]{2,1,0:T(8,128)(2,1)}, bf16[2,256,384]{2,1,0:T(8,128)(2,1)S(1)}, u32[]{:S(2)}) copy-start(bf16[2,256,384]{2,1,0:T(8,128)(2,1)S(1)} %get-tuple-element.155.refs_4_) | copy-start | bytes 1179652
  112.5 1.4 collective-permute-start.31
  113.9 38.0 %copy-start.34 = (f32[256,2]{1,0:T(8,128)}, f32[256,2]{1,0:T(8,128)S(1)}, u32[]{:S(2)}) copy-start(f32[256,2]{1,0:T(8,128)S(1)} %add.74) | copy-start | bytes 6148
  122.1 25.7 %collective-permute-start.36 = (bf16[4,2,2,64,384]{4,3,2,1,0:T(8,128)(2,1)S(1)}, bf16[4,2,2,64,384]{4,3,2,1,0:T(8,128)(2,1)S(1)}, u32[]{:S(2)}, u32[]{:S(2)}) collective-permute-start(bf16[4,2,2,64,384]{4,3,2,1,0:T(8,128)(2,1)S(1)} %pad_maximum_fusion.1.refs_0_), channel_id=1, source_target_pairs={{0,16},{8,24},{16,0},{24,8},{1,17},{9,25},{17,1},{25,9},{2,18},{10... | collective-permute-start | bytes 2359304 | tf_op jit(solution)/shard_map/ppermute | solution.py:44
  123.7 11.5 %collective-permute-start.34 = (bf16[2,256,384]{2,1,0:T(8,128)(2,1)S(1)}, bf16[2,256,384]{2,1,0:T(8,128)(2,1)}, u32[]{:S(2)}, u32[]{:S(2)}) collective-permute-start(bf16[2,256,384]{2,1,0:T(8,128)(2,1)S(1)} %get-tuple-element.155.refs_4_), channel_id=1, source_target_pairs={{0,2},{1,3},{2,4},{3,5},{4,6},{5,7},{6,0},{7,1},{8,10},{9,11},{10,... | collective-permute-start | bytes 1179656 | tf_op jit(solution)/shard_map/ppermute | solution.py:40
  123.7 24.2 %collective-permute-start.37 = (bf16[4,2,2,64,384]{4,3,2,1,0:T(8,128)(2,1)S(1)}, bf16[4,2,2,64,384]{4,3,2,1,0:T(8,128)(2,1)S(1)}, u32[]{:S(2)}, u32[]{:S(2)}) collective-permute-start(bf16[4,2,2,64,384]{4,3,2,1,0:T(8,128)(2,1)S(1)} %pad_maximum_fusion.1.refs_0_), channel_id=1, source_target_pairs={{0,8},{8,0},{16,24},{24,16},{1,9},{9,1},{17,25},{25,17},{2,10},{10... | collective-permute-start | bytes 2359304 | tf_op jit(solution)/shard_map/ppermute | solution.py:44
  123.7 24.2 %collective-permute-start.32 = (bf16[3,128,768]{2,1,0:T(8,128)(2,1)S(1)}, bf16[3,128,768]{2,1,0:T(8,128)(2,1)S(1)}, u32[]{:S(2)}, u32[]{:S(2)}) collective-permute-start(bf16[3,128,768]{2,1,0:T(8,128)(2,1)S(1)} %get-tuple-element.142.own_ref), channel_id=1, source_target_pairs={{0,1},{1,0},{2,3},{3,2},{4,5},{5,4},{6,7},{7,6},{8,9},{9,8},{10,11... | collective-permute-start | bytes 1769480 | tf_op jit(solution)/shard_map/ppermute | solution.py:40
  125.1 22.7 %collective-permute-start.33 = (bf16[2,256,384]{2,1,0:T(8,128)(2,1)S(1)}, bf16[2,256,384]{2,1,0:T(8,128)(2,1)S(1)}, u32[]{:S(2)}, u32[]{:S(2)}) collective-permute-start(bf16[2,256,384]{2,1,0:T(8,128)(2,1)S(1)} %get-tuple-element.155.refs_4_), channel_id=1, source_target_pairs={{0,1},{1,0},{2,3},{3,2},{4,5},{5,4},{6,7},{7,6},{8,9},{9,8},{10,11... | collective-permute-start | bytes 1179656 | tf_op jit(solution)/shard_map/ppermute | solution.py:40
  135.2 12.7 %collective-permute-start.35 = (bf16[2,256,384]{2,1,0:T(8,128)(2,1)}, bf16[2,256,384]{2,1,0:T(8,128)(2,1)}, u32[]{:S(2)}, u32[]{:S(2)}) collective-permute-start(bf16[2,256,384]{2,1,0:T(8,128)(2,1)} %collective-permute-done.34.refs_5_), channel_id=1, source_target_pairs={{0,2},{1,3},{2,4},{3,5},{4,6},{5,7},{6,0},{7,1},{8,10},{9,11},{10,... | collective-permute-start | bytes 1179656 | tf_op jit(solution)/shard_map/ppermute | solution.py:40
  139.5 19.8 %copy-start.8 = (bf16[2,256,768]{2,1,0:T(8,128)(2,1)}, bf16[2,256,768]{2,1,0:T(8,128)(2,1)S(1)}, u32[]{:S(2)}) copy-start(bf16[2,256,768]{2,1,0:T(8,128)(2,1)S(1)} %get-tuple-element.131) | copy-start | bytes 2359300
  147.8 11.5 %copy-start.12 = (bf16[2,256,384]{2,1,0:T(8,128)(2,1)}, bf16[2,256,384]{2,1,0:T(8,128)(2,1)S(1)}, u32[]{:S(2)}) copy-start(bf16[2,256,384]{2,1,0:T(8,128)(2,1)S(1)} %collective-permute-done.33.refs_8_) | copy-start | bytes 1179652
  147.9 11.5 %copy-start.2 = (bf16[4,2,2,64,384]{4,3,2,1,0:T(8,128)(2,1)}, bf16[4,2,2,64,384]{4,3,2,1,0:T(8,128)(2,1)S(1)}, u32[]{:S(2)}) copy-start(bf16[4,2,2,64,384]{4,3,2,1,0:T(8,128)(2,1)S(1)} %collective-permute-done.37.refs_1_) | copy-start | bytes 2359300
  147.9 5.1 %collective-permute-start.38 = (bf16[2,256,1536]{2,1,0:T(8,128)(2,1)S(1)}, bf16[2,256,1536]{2,1,0:T(8,128)(2,1)S(1)}, u32[]{:S(2)}, u32[]{:S(2)}) collective-permute-start(bf16[2,256,1536]{2,1,0:T(8,128)(2,1)S(1)} %get-tuple-element.136), channel_id=1, source_target_pairs={{0,8},{8,0},{16,24},{24,16},{1,9},{9,1},{17,25},{25,17},{2,10},{10... | collective-permute-start | bytes 4718600 | tf_op jit(solution)/shard_map/ppermute | solution.py:44
  148.0 20.3 %collective-permute-start.40 = (bf16[2,256,384]{2,1,0:T(8,128)(2,1)}, bf16[2,256,384]{2,1,0:T(8,128)(2,1)}, u32[]{:S(2)}, u32[]{:S(2)}) collective-permute-start(bf16[2,256,384]{2,1,0:T(8,128)(2,1)} %collective-permute-done.35.refs_6_), channel_id=1, source_target_pairs={{0,1},{1,0},{2,3},{3,2},{4,5},{5,4},{6,7},{7,6},{8,9},{9,8},{10,11... | collective-permute-start | bytes 1179656 | tf_op jit(solution)/shard_map/ppermute | solution.py:40
  149.5 18.8 %collective-permute-start.41 = (bf16[2,256,384]{2,1,0:T(8,128)(2,1)}, bf16[2,256,384]{2,1,0:T(8,128)(2,1)}, u32[]{:S(2)}, u32[]{:S(2)}) collective-permute-start(bf16[2,256,384]{2,1,0:T(8,128)(2,1)} %collective-permute-done.35.refs_6_), channel_id=1, source_target_pairs={{0,2},{1,3},{2,4},{3,5},{4,6},{5,7},{6,0},{7,1},{8,10},{9,11},{10,... | collective-permute-start | bytes 1179656 | tf_op jit(solution)/shard_map/ppermute | solution.py:40
  151.9 5.3 %collective-permute-start.43 = (f32[256,2]{1,0:T(8,128)S(1)}, f32[256,2]{1,0:T(8,128)S(1)}, u32[]{:S(2)}, u32[]{:S(2)}) collective-permute-start(f32[256,2]{1,0:T(8,128)S(1)} %add.74), channel_id=1, source_target_pairs={{0,16},{8,24},{16,0},{24,8},{1,17},{9,25},{17,1},{25,9},{2,18},{10... | collective-permute-start | bytes 6152 | tf_op jit(solution)/shard_map/ppermute | solution.py:44
  152.5 15.8 %collective-permute-start.39 = (bf16[2,256,384]{2,1,0:T(8,128)(2,1)}, bf16[2,256,384]{2,1,0:T(8,128)(2,1)}, u32[]{:S(2)}, u32[]{:S(2)}) collective-permute-start(bf16[2,256,384]{2,1,0:T(8,128)(2,1)} %collective-permute-done.34.refs_5_), channel_id=1, source_target_pairs={{0,1},{1,0},{2,3},{3,2},{4,5},{5,4},{6,7},{7,6},{8,9},{9,8},{10,11... | collective-permute-start | bytes 1179656 | tf_op jit(solution)/shard_map/ppermute | solution.py:40
  157.2 26.4 %copy-start.11 = (bf16[2,256,384]{2,1,0:T(8,128)(2,1)S(1)}, bf16[2,256,384]{2,1,0:T(8,128)(2,1)}, u32[]{:S(2)}) copy-start(bf16[2,256,384]{2,1,0:T(8,128)(2,1)} %copy-done.10) | copy-start | bytes 1179652
  157.2 11.4 %collective-permute-start.44 = (bf16[256,768]{1,0:T(8,128)(2,1)}, bf16[256,768]{1,0:T(8,128)(2,1)}, u32[]{:S(2)}, u32[]{:S(2)}) collective-permute-start(bf16[256,768]{1,0:T(8,128)(2,1)} %get-tuple-element.149), channel_id=1, source_target_pairs={{0,16},{8,24},{16,0},{24,8},{1,17},{9,25},{17,1},{25,9},{2,18},{10... | collective-permute-start | bytes 1179656 | tf_op jit(solution)/shard_map/ppermute | solution.py:44
  160.9 7.8 %collective-permute-start.42 = (bf16[128,768]{1,0:T(8,128)(2,1)}, bf16[128,768]{1,0:T(8,128)(2,1)}, u32[]{:S(2)}, u32[]{:S(2)}) collective-permute-start(bf16[128,768]{1,0:T(8,128)(2,1)} %get-tuple-element.144), channel_id=1, source_target_pairs={{0,2},{1,3},{2,4},{3,5},{4,6},{5,7},{6,0},{7,1},{8,10},{9,11},{10,... | collective-permute-start | bytes 589832 | tf_op jit(solution)/shard_map/ppermute | solution.py:40
  163.2 20.4 %copy-start.3 = (bf16[4,2,2,64,384]{4,3,2,1,0:T(8,128)(2,1)S(1)}, bf16[4,2,2,64,384]{4,3,2,1,0:T(8,128)(2,1)}, u32[]{:S(2)}) copy-start(bf16[4,2,2,64,384]{4,3,2,1,0:T(8,128)(2,1)} %copy-done.2) | copy-start | bytes 2359300
  163.2 20.4 %copy-start.13 = (bf16[2,256,384]{2,1,0:T(8,128)(2,1)S(1)}, bf16[2,256,384]{2,1,0:T(8,128)(2,1)}, u32[]{:S(2)}) copy-start(bf16[2,256,384]{2,1,0:T(8,128)(2,1)} %copy-done.12) | copy-start | bytes 1179652
  168.7 13.2 %collective-permute-start.48 = (bf16[128,768]{1,0:T(8,128)(2,1)}, bf16[128,768]{1,0:T(8,128)(2,1)S(1)}, u32[]{:S(2)}, u32[]{:S(2)}) collective-permute-start(bf16[128,768]{1,0:T(8,128)(2,1)} %copy-done.29), channel_id=1, source_target_pairs={{0,4},{1,5},{2,6},{3,7},{4,0},{5,1},{6,2},{7,3},{8,12},{9,13},{10,... | collective-permute-start | bytes 589832 | tf_op jit(solution)/shard_map/ppermute | solution.py:40
  170.1 11.7 %collective-permute-start.49 = (bf16[128,768]{1,0:T(8,128)(2,1)}, bf16[128,768]{1,0:T(8,128)(2,1)S(1)}, u32[]{:S(2)}, u32[]{:S(2)}) collective-permute-start(bf16[128,768]{1,0:T(8,128)(2,1)} %copy-done.28), channel_id=1, source_target_pairs={{0,6},{1,7},{2,0},{3,1},{4,2},{5,3},{6,4},{7,5},{8,14},{9,15},{10,... | collective-permute-start | bytes 589832 | tf_op jit(solution)/shard_map/ppermute | solution.py:40
  173.0 10.6 %collective-permute-start.46 = (bf16[4,2,2,64,384]{4,3,2,1,0:T(8,128)(2,1)S(1)}, bf16[4,2,2,64,384]{4,3,2,1,0:T(8,128)(2,1)S(1)}, u32[]{:S(2)}, u32[]{:S(2)}) collective-permute-start(bf16[4,2,2,64,384]{4,3,2,1,0:T(8,128)(2,1)S(1)} %collective-permute-done.36.refs_2_), channel_id=1, source_target_pairs={{0,8},{8,0},{16,24},{24,16},{1,9},{9,1},{17,25},{25,17},{2,10},{10... | collective-permute-start | bytes 2359304 | tf_op jit(solution)/shard_map/ppermute | solution.py:44
  174.2 13.1 %collective-permute-start.47 = (bf16[2,256,384]{2,1,0:T(8,128)(2,1)}, bf16[2,256,384]{2,1,0:T(8,128)(2,1)S(1)}, u32[]{:S(2)}, u32[]{:S(2)}) collective-permute-start(bf16[2,256,384]{2,1,0:T(8,128)(2,1)} %collective-permute-done.41.refs_7_), channel_id=1, source_target_pairs={{0,1},{1,0},{2,3},{3,2},{4,5},{5,4},{6,7},{7,6},{8,9},{9,8},{10,11... | collective-permute-start | bytes 1179656 | tf_op jit(solution)/shard_map/ppermute | solution.py:40
  175.9 11.5 %collective-permute-start.45 = (bf16[256,768]{1,0:T(8,128)(2,1)}, bf16[256,768]{1,0:T(8,128)(2,1)S(1)}, u32[]{:S(2)}, u32[]{:S(2)}) collective-permute-start(bf16[256,768]{1,0:T(8,128)(2,1)} %get-tuple-element.152), channel_id=1, source_target_pairs={{0,16},{8,24},{16,0},{24,8},{1,17},{9,25},{17,1},{25,9},{2,18},{10... | collective-permute-start | bytes 1179656 | tf_op jit(solution)/shard_map/ppermute | solution.py:44
  (22 other events, 80.7 us)

commit v12 on v11

--- a/solution.py
+++ b/solution.py
@@ -758,7 +758,8 @@
     kept, away = after((kept, away), first, side_key, side_value)
     got = gsend(away, 1)
     ring = [None, jnp.concatenate(first, axis=0)]
-    side_first = fsend(jnp.concatenate([cross_query, cross_out, *first], axis=0), 0, 1)
+    side_own = [fsend(w, 0, 1) for w in (cross_query, cross_out)]
+    side_first = fsend(ring[1], 0, 1)
     ring.append(fsend(ring[1], 1, 0))
     sent = (kept[quarter_rows:].astype(F32) + got[quarter_rows:].astype(F32)).astype(BF)
     over_x = gsend(sent, 2)
@@ -766,18 +767,17 @@
         after(video_states, sent), out_grad, place, pairs, part
     )
     pieces = encode_rows(
-        states, kept, got, after(over_x, normed), final_gain, place, pairs
+        states, kept, got, after(over_x, normed, *side_own), final_gain, place, pairs
     )
 
     mine = jnp.stack([fsend(p, far, 0) if far else p for far, p in enumerate(pieces)])
-    mine = after(mine, ring[2])
+    mine = after(mine, ring[2], side_first)
     over_x = gsend(mine, 2)
     parts = [mine, gsend(mine, 1), over_x, gsend(over_x, 1)]
     current = after(ring[2], mine)
     for far in range(3, pairs):
         current = fsend(current, 1, 0)
         ring.append(current)
-    parts[3] = after(parts[3], side_first)
     kv_partial = project_captions(
         parts, cross_key, cross_value, side_key, side_value, place, pairs
     )
@@ -791,12 +791,9 @@
     kv_blocks = gather_direct(kv_sum)
     kv_blocks[4] = after(kv_blocks[4], side_later, other_tiles)
 
-    step = part + width_local
-    blocks = []
-    for far, held in enumerate(ring):
-        side, start = (side_first, far * step) if far < 2 else (side_later[far - 2], 0)
-        here = ((held, 0), (held, part)) if far else ((cross_query, 0), (cross_out, 0))
-        blocks += [here, ((side, start), (side, start + part))]
+    blocks = [((cross_query, 0), (cross_out, 0)), ((side_own[0], 0), (side_own[1], 0))]
+    for held, side in zip(ring[1:], [side_first, *side_later]):
+        blocks += [((held, 0), (held, part)), ((side, 0), (side, part))]
     queries, d_attended, column_sum = project_rows(
         normed, after(out_grad, kv_blocks[4]), blocks, place, pairs, part
     )
@@ -870,9 +867,11 @@
         + inverse * (total[1] - row_sums[:, 0:1] - video_hat * row_sums[:, 1:2])
     ).astype(BF)
     kv_parts += [fsend(terms[far], far, 0) for far in range(2, pairs)]
+    kv_parts = after(kv_parts, known)
     kv_grads = (terms[0] + sum(p.astype(F32) for p in kv_parts)).astype(BF)[None]
     key_grad = kv_grads[:, :, :width_local]
     value_grad = kv_grads[:, :, width_local:]
+    known = after(known, updated, input_grad)
     query_grad, out_weight_grad = weight_grads(
         tiles, [None] * (pairs + 3) + there[3:], known, pairs
     )

time: 192 us -> 208 us (1.083)
  starting transfers between devices: 59.1 us -> 68 us
  local copies, waits for them, and re-layouts: 4.93 us -> 11.8 us
    ppermute x37 -> x39, starting transfers between devices: 52.3 us -> 61.5 us  [fsend(): return lax.ppermute(block, 'fsdp', perm)]
    unnamed x73 -> x83, local copies, waits for them, and re-layouts: 3.99 us -> 9.86 us
    ppermute x13, waiting for transfers between devices: 14.6 us -> 9.74 us  [gsend(): lax.ppermute(block, 'grp', [(s, s ^ flip) for s in range(lax.axis_size('g...]
    ppermute x37 -> x39, waiting for transfers between devices: 65.6 us -> 69 us  [fsend(): return lax.ppermute(block, 'fsdp', perm)]
  transfers between devices with their start and end apart: 50 -> 52, of which waited for: 19 -> 18; matrix products, arithmetic and copies ran while one was open for 4% -> 6% of each run, Pallas kernels for 18% -> 17%
where the time goes in v12:
time: 208 us; the launch traced here: 207 us
  waiting for transfers between devices  78.8 us (38%)
  starting transfers between devices  68 us (33%)
  Pallas kernels  38 us (18%)
  local copies, waits for them, and re-layouts  11.8 us (6%)
  other arithmetic  8.74 us (4%)
    ppermute x39, waiting for transfers between devices, fsend(): return lax.ppermute(block, 'fsdp', perm)  69 us
    ppermute x39, starting transfers between devices, fsend(): return lax.ppermute(block, 'fsdp', perm)  61.5 us
    pallas_call x9, Pallas kernels, call(): pl.pallas_call(body, out_shape=out_shape, in_specs=specs, out_specs=jax.t...  22.8 us
    unnamed x83, local copies, waits for them, and re-layouts  9.86 us
    ppermute x13, waiting for transfers between devices, gsend(): lax.ppermute(block, 'grp', [(s, s ^ flip) for s in range(lax.axis_size('g...  9.74 us
    pallas_call x1, Pallas kernels, project_text(): pl.pallas_call(body, grid=(steps,), out_shape=shaped((rows, 3 * width)),...  7.96 us
    pallas_call x1, Pallas kernels, attend_text(): pl.pallas_call(body, grid=(steps,), out_shape=[shaped((rows // 2, depth))...  7.23 us
    ppermute x13, starting transfers between devices, gsend(): lax.ppermute(block, 'grp', [(s, s ^ flip) for s in range(lax.axis_size('g...  6.5 us
  transfers between devices with their start and end apart: 52, of which 18 were waited for; matrix products, arithmetic and copies ran while one was open for 6% of the time, Pallas kernels for 17%

profile of v12, /device:TPU:0, one launch (start us, length us, event | category | flops | bytes accessed | tf_op | source)
XLA Modules:
  0.0 206.5 jit_solution(8471094941014869528)
XLA Ops:
  0.6 3.0 %collective-permute-start.2 = (bf16[512,384]{1,0:T(8,128)(2,1)}, bf16[512,384]{1,0:T(8,128)(2,1)}, u32[]{:S(2)}, u32[]{:S(2)}) collective-permute-start(bf16[512,384]{1,0:T(8,128)(2,1)} %refs_4_.1), channel_id=1, source_target_pairs={{0,1},{1,0},{2,3},{3,2},{4,5},{5,4},{6,7},{7,6},{8,9},{9,8},{10,11... | collective-permute-start | bytes 1179656 | tf_op jit(solution)/shard_map/ppermute | solution.py:40
  3.7 2.0 collective-permute-start
  5.7 1.6 collective-permute-start.1
  7.3 8.0 %shard_map.208.qkv_ref = bf16[128,1536]{1,0:T(8,128)(2,1)} custom-call(bf16[128,4096]{1,0:T(8,128)(2,1)} %bitcast.40, f32[1,4096]{1,0:T(1,128)} %bitcast.53, bf16[4096,512]{1,0:T(8,128)(2,1)} %wq_ref.1, bf16[4096,512]{1,0:T(8,128)(2,1)} %wk_ref.1, bf16[4096,512]{1,0:T(8,128)(2,1)} %wv_ref.1), custom_call_target="tpu_custom_call" | custom-call | flops 1 | bytes 1 | tf_op jit(solution)/shard_map/pallas_call | solution.py:350
  15.9 7.2 %shard_map.209 = (bf16[64,4096]{1,0:T(8,128)(2,1)}, bf16[64,4096]{1,0:T(8,128)(2,1)}) custom-call(s32[3]{0:T(128)} %pad_add_fusion.place_ref, s32[8]{0:T(128)} %len_ref.3, bf16[128,1536]{1,0:T(8,128)(2,1)} %shard_map.208.qkv_ref, f32[8,128,128]{2,1,0:T(8,128)} %bias_ref.1, bf16[512,4096]{1,0:T(8,128)(2,1)} %out_ref.1), custom_call_target="tpu_custom_call" | custom-call | flops 1 | bytes 1 | tf_op jit(solution)/shard_map/pallas_call | solution.py:394
  23.3 1.6 collective-permute-start.6
  26.4 1.0 constant_dynamic-update-slice_fusion.refs_4_
  27.4 1.6 collective-permute-start.12
  29.0 1.6 collective-permute-start.11
  30.5 1.0 add_convert_fusion.2
  31.6 1.6 collective-permute-start.5
  33.2 2.7 %shard_map.210 = (bf16[256,3072]{1,0:T(8,128)(2,1)S(1)}, f32[256,1]{1,0:T(8,128)S(1)}, f32[256,1]{1,0:T(8,128)S(1)}, bf16[4,2,64,384]{3,2,1,0:T(8,128)(2,1)S(1)}, bf16[4,2,64,384]{3,2,1,0:T(8,128)(2,1)S(1)}) custom-call(s32[3]{0:T(128)S(1)} %copy-done.26, bf16[256,3072]{1,0:T(8,128)(2,1)S(1)} %copy-done.2, bf16[256,3072]{1,0:T(8,128)(2,1)S(1)} %copy-done), custom_call_target="tpu_custom_call" | custom-call | flops 1 | bytes 1 | tf_op jit(solution)/shard_map/pallas_call | solution.py:307
  36.0 3.5 %collective-permute-done.7.refs_3_ = bf16[384,384]{1,0:T(8,128)(2,1)S(1)} collective-permute-done((bf16[384,384]{1,0:T(8,128)(2,1)S(1)}, bf16[384,384]{1,0:T(8,128)(2,1)S(1)}, u32[]{:S(2)}, u32[]{:S(2)}) %collective-permute-start.7) | collective-permute-done | bytes 294944 | tf_op jit(solution)/shard_map/ppermute | solution.py:40
  40.3 1.6 collective-permute-start.8
  42.0 1.2 collective-permute-start.9
  43.2 1.2 collective-permute-start.10
  44.4 4.1 %collective-permute-done.8 = bf16[32,1024]{1,0:T(8,128)(2,1)S(1)} collective-permute-done((bf16[32,1024]{1,0:T(8,128)(2,1)S(1)}, bf16[32,1024]{1,0:T(8,128)(2,1)S(1)}, u32[]{:S(2)}, u32[]{:S(2)}) %collective-permute-start.8) | collective-permute-done | bytes 65568 | tf_op jit(solution)/shard_map/ppermute | solution.py:40
  48.5 1.4 collective-permute-done.9
  49.9 1.7 collective-permute-done.12.refs_5_
  51.7 1.6 collective-permute-start.16
  53.2 1.5 collective-permute-start.14
  54.7 6.1 %collective-permute-done.14.refs_2_ = bf16[4,32,1024]{2,1,0:T(8,128)(2,1)S(1)} collective-permute-done((bf16[4,32,1024]{2,1,0:T(8,128)(2,1)S(1)}, bf16[4,32,1024]{2,1,0:T(8,128)(2,1)S(1)}, u32[]{:S(2)}, u32[]{:S(2)}) %collective-permute-start.14) | collective-permute-done | bytes 262176 | tf_op jit(solution)/shard_map/ppermute | solution.py:44
  60.8 1.5 collective-permute-start.20
  62.4 2.4 %shard_map.212 = (bf16[128,768]{1,0:T(8,128)(2,1)S(1)}, bf16[128,768]{1,0:T(8,128)(2,1)S(1)}, bf16[128,768]{1,0:T(8,128)(2,1)S(1)}, bf16[128,768]{1,0:T(8,128)(2,1)S(1)}) custom-call(s32[3]{0:T(128)S(1)} %copy-done.26, bf16[4,32,1024]{2,1,0:T(8,128)(2,1)S(1)} %pad_maximum_fusion.1.refs_0_, bf16[4,32,1024]{2,1,0:T(8,128)(2,1)S(1)} %collective-permute-done.13.refs_1_, ...), custom_call_target="tpu_custom_call" | custom-call | flops 1 | bytes 1 | tf_op jit(solution)/shard_map/pallas_call | solution.py:307
  64.8 3.6 %collective-permute-done.16.refs_8_ = bf16[768,384]{1,0:T(8,128)(2,1)S(1)} collective-permute-done((bf16[768,384]{1,0:T(8,128)(2,1)S(1)}, bf16[768,384]{1,0:T(8,128)(2,1)S(1)}, u32[]{:S(2)}, u32[]{:S(2)}) %collective-permute-start.16) | collective-permute-done | bytes 589856 | tf_op jit(solution)/shard_map/ppermute | solution.py:40
  70.4 1.5 collective-permute-start.23
  71.9 3.1 %collective-permute-done.17 = bf16[128,768]{1,0:T(8,128)(2,1)S(1)} collective-permute-done((bf16[128,768]{1,0:T(8,128)(2,1)S(1)}, bf16[128,768]{1,0:T(8,128)(2,1)S(1)}, u32[]{:S(2)}, u32[]{:S(2)}) %collective-permute-start.17) | collective-permute-done | bytes 196640 | tf_op jit(solution)/shard_map/ppermute | solution.py:40
  75.0 1.4 collective-permute-start.22
  76.5 9.3 %collective-permute-done.18 = bf16[128,768]{1,0:T(8,128)(2,1)S(1)} collective-permute-done((bf16[128,768]{1,0:T(8,128)(2,1)S(1)}, bf16[128,768]{1,0:T(8,128)(2,1)S(1)}, u32[]{:S(2)}, u32[]{:S(2)}) %collective-permute-start.18) | collective-permute-done | bytes 196640 | tf_op jit(solution)/shard_map/ppermute | solution.py:40
  85.9 2.0 collective-permute-start.25
  88.0 2.1 %collective-permute-start.21 = (bf16[128,768]{1,0:T(8,128)(2,1)S(1)}, bf16[128,768]{1,0:T(8,128)(2,1)S(1)}, u32[]{:S(2)}, u32[]{:S(2)}) collective-permute-start(bf16[128,768]{1,0:T(8,128)(2,1)S(1)} %add_convert_fusion.4.refs_0_), channel_id=1, source_target_pairs={{0,4},{1,5},{2,6},{3,7},{4,0},{5,1},{6,2},{7,3},{8,12},{9,13},{10,... | collective-permute-start | bytes 589832 | tf_op jit(solution)/shard_map/ppermute | solution.py:40
  90.1 1.5 collective-permute-start.24
  91.6 1.5 collective-permute-start.29
  93.1 6.5 %collective-permute-done.25.refs_2_ = bf16[128,768]{1,0:T(8,128)(2,1)S(1)} collective-permute-done((bf16[128,768]{1,0:T(8,128)(2,1)S(1)}, bf16[128,768]{1,0:T(8,128)(2,1)S(1)}, u32[]{:S(2)}, u32[]{:S(2)}) %collective-permute-start.25) | collective-permute-done | bytes 196640 | tf_op jit(solution)/shard_map/ppermute | solution.py:40
  99.6 1.5 collective-permute-start.26
  101.1 4.7 %collective-permute-done.21.refs_4_ = bf16[128,768]{1,0:T(8,128)(2,1)S(1)} collective-permute-done((bf16[128,768]{1,0:T(8,128)(2,1)S(1)}, bf16[128,768]{1,0:T(8,128)(2,1)S(1)}, u32[]{:S(2)}, u32[]{:S(2)}) %collective-permute-start.21) | collective-permute-done | bytes 196640 | tf_op jit(solution)/shard_map/ppermute | solution.py:40
  105.8 1.5 collective-permute-start.27
  107.5 1.0 collective-permute-start.31
  108.5 2.9 %collective-permute-start.32 = (bf16[2,2,64,384]{3,2,1,0:T(8,128)(2,1)S(1)}, bf16[2,2,64,384]{3,2,1,0:T(8,128)(2,1)S(1)}, u32[]{:S(2)}, u32[]{:S(2)}) collective-permute-start(bf16[2,2,64,384]{3,2,1,0:T(8,128)(2,1)S(1)} %get-tuple-element.126), channel_id=1, source_target_pairs={{0,6},{1,7},{2,0},{3,1},{4,2},{5,3},{6,4},{7,5},{8,14},{9,15},{10,... | collective-permute-start | bytes 589832 | tf_op jit(solution)/shard_map/ppermute | solution.py:40
  111.4 2.8 %shard_map.213 = (bf16[256,384]{1,0:T(8,128)(2,1)S(1)}, bf16[256,384]{1,0:T(8,128)(2,1)S(1)}, f32[1,384]{1,0:T(1,128)S(1)}) custom-call(s32[3]{0:T(128)S(1)} %copy-done.26, bf16[256,3072]{1,0:T(8,128)(2,1)S(1)} %get-tuple-element.98.normed_ref, bf16[256,3072]{1,0:T(8,128)(2,1)S(1)} %copy-done, bf16[384,384]{1,0:T(8,128)(2,1)S(1)} %copy-done.4, ...), custom_call_target="tpu_custom_call" | custom-call | flops 1 | bytes 1 | tf_op jit(solution)/shard_map/pallas_call | solution.py:307
  114.5 2.8 %shard_map.214 = (bf16[2,256,384]{2,1,0:T(8,128)(2,1)S(1)}, bf16[256,384]{1,0:T(8,128)(2,1)S(1)}, bf16[256,384]{1,0:T(8,128)(2,1)S(1)}, f32[256,2]{1,0:T(8,128)S(1)}, bf16[3,128,768]{2,1,0:T(8,128)(2,1)S(1)}) custom-call(s32[3]{0:T(128)S(1)} %copy-done.26, s32[8]{0:T(128)S(1)} %copy-done.28, s32[8]{0:T(128)S(1)} %copy-done.29, s32[8]{0:T(128)S(1)} %copy-done.30, ...), custom_call_target="tpu_custom_call" | custom-call | flops 1 | bytes 1 | tf_op jit(solution)/shard_map/pallas_call | solution.py:307
  117.4 1.3 collective-permute-done.33
  118.8 5.2 %collective-permute-done.31 = bf16[2,2,64,384]{3,2,1,0:T(8,128)(2,1)S(1)} collective-permute-done((bf16[2,2,64,384]{3,2,1,0:T(8,128)(2,1)S(1)}, bf16[2,2,64,384]{3,2,1,0:T(8,128)(2,1)S(1)}, u32[]{:S(2)}, u32[]{:S(2)}) %collective-permute-start.31) | collective-permute-done | bytes 196640 | tf_op jit(solution)/shard_map/ppermute | solution.py:40
  124.0 12.2 %collective-permute-start.36 = (bf16[2,256,384]{2,1,0:T(8,128)(2,1)S(1)}, bf16[2,256,384]{2,1,0:T(8,128)(2,1)S(1)}, u32[]{:S(2)}, u32[]{:S(2)}) collective-permute-start(bf16[2,256,384]{2,1,0:T(8,128)(2,1)S(1)} %get-tuple-element.158.refs_4_), channel_id=1, source_target_pairs={{0,2},{1,3},{2,4},{3,5},{4,6},{5,7},{6,0},{7,1},{8,10},{9,11},{10,... | collective-permute-start | bytes 1179656 | tf_op jit(solution)/shard_map/ppermute | solution.py:40
  136.4 1.6 collective-permute-start.38
  138.5 1.6 collective-permute-start.35
  140.0 2.9 %collective-permute-done.36.refs_5_ = bf16[2,256,384]{2,1,0:T(8,128)(2,1)S(1)} collective-permute-done((bf16[2,256,384]{2,1,0:T(8,128)(2,1)S(1)}, bf16[2,256,384]{2,1,0:T(8,128)(2,1)S(1)}, u32[]{:S(2)}, u32[]{:S(2)}) %collective-permute-start.36) | collective-permute-done | bytes 393248 | tf_op jit(solution)/shard_map/ppermute | solution.py:40
  142.9 2.5 %collective-permute-start.37 = (bf16[2,256,384]{2,1,0:T(8,128)(2,1)S(1)}, bf16[2,256,384]{2,1,0:T(8,128)(2,1)S(1)}, u32[]{:S(2)}, u32[]{:S(2)}) collective-permute-start(bf16[2,256,384]{2,1,0:T(8,128)(2,1)S(1)} %collective-permute-done.36.refs_5_), channel_id=1, source_target_pairs={{0,2},{1,3},{2,4},{3,5},{4,6},{5,7},{6,0},{7,1},{8,10},{9,11},{10,... | collective-permute-start | bytes 1179656 | tf_op jit(solution)/shard_map/ppermute | solution.py:40
  145.4 4.4 %shard_map.215 = (bf16[2,256,768]{2,1,0:T(8,128)(2,1)S(1)}, bf16[2,256,768]{2,1,0:T(8,128)(2,1)S(1)}, bf16[2,256,1536]{2,1,0:T(8,128)(2,1)S(1)}) custom-call(s32[3]{0:T(128)S(1)} %copy-done.26, bf16[256,384]{1,0:T(8,128)(2,1)S(1)} %get-tuple-element.132.att_ref, bf16[256,384]{1,0:T(8,128)(2,1)S(1)} %get-tuple-element.133.dq_ref, ...), custom_call_target="tpu_custom_call" | custom-call | flops 1 | bytes 1 | tf_op jit(solution)/shard_map/pallas_call | solution.py:307
  149.8 12.0 %collective-permute-done.35.refs_8_ = bf16[2,256,384]{2,1,0:T(8,128)(2,1)S(1)} collective-permute-done((bf16[2,256,384]{2,1,0:T(8,128)(2,1)S(1)}, bf16[2,256,384]{2,1,0:T(8,128)(2,1)S(1)}, u32[]{:S(2)}, u32[]{:S(2)}) %collective-permute-start.35) | collective-permute-done | bytes 393248 | tf_op jit(solution)/shard_map/ppermute | solution.py:40
  163.1 1.5 collective-permute-start.41
  165.3 1.1 fusion.9
  166.4 1.6 collective-permute-done.45
  171.1 10.8 %collective-permute-done.41.refs_9_ = bf16[2,256,384]{2,1,0:T(8,128)(2,1)S(1)} collective-permute-done((bf16[2,256,384]{2,1,0:T(8,128)(2,1)S(1)}, bf16[2,256,384]{2,1,0:T(8,128)(2,1)S(1)}, u32[]{:S(2)}, u32[]{:S(2)}) %collective-permute-start.41) | collective-permute-done | bytes 393248 | tf_op jit(solution)/shard_map/ppermute | solution.py:40
  184.8 1.0 reduce
  185.8 1.0 reduce.2
  186.9 3.6 %collective-permute-start.51 = (bf16[128,768]{1,0:T(8,128)(2,1)}, bf16[128,768]{1,0:T(8,128)(2,1)S(1)}, u32[]{:S(2)}, u32[]{:S(2)}) collective-permute-start(bf16[128,768]{1,0:T(8,128)(2,1)} %copy-done.31), channel_id=1, source_target_pairs={{0,6},{1,7},{2,0},{3,1},{4,2},{5,3},{6,4},{7,5},{8,14},{9,15},{10,... | collective-permute-start | bytes 589832 | tf_op jit(solution)/shard_map/ppermute | solution.py:40
  192.3 1.0 copy-done.11
  193.3 1.0 copy-done.13
  194.2 1.0 copy-done.15
  196.2 1.0 copy-done.19
  197.2 3.2 %shard_map.217 = (f32[384,384]{1,0:T(8,128)S(1)}, f32[384,384]{1,0:T(8,128)S(1)}) custom-call(bf16[4,2,2,64,384]{4,3,2,1,0:T(8,128)(2,1)S(1)} %pad_maximum_fusion.refs_0_, bf16[4,2,2,64,384]{4,3,2,1,0:T(8,128)(2,1)S(1)} %collective-permute-done.39.refs_1_, bf16[4,2,2,64,384]{4,3,2,1,0:T(8,128)(2,1)} %collective-permute-done.38.refs_2_, ...), custom_call_target="tpu_custom_call" | custom-call | flops 1 | bytes 1 | tf_op jit(solution)/shard_map/pallas_call | solution.py:307
  200.5 2.5 %fusion.6 = (bf16[256,768]{1,0:T(8,128)(2,1)}, bf16[256,768]{1,0:T(8,128)(2,1)}) fusion(bf16[256,768]{1,0:T(8,128)(2,1)} %collective-permute-done.47, bf16[2,256,1536]{2,1,0:T(8,128)(2,1)S(1)} %copy-done.34, f32[256]{0:T(256)S(1)} %get-tuple-element.181, f32[256]{0:T(256)S(1)} %reduce.2, f32[256]{0:T(256)S(1)} %get-tuple-element.180, ...), kind=kLoop, calls=%fused_computation.14 | loop fusion | flops 4325376 | bytes 3936260 | tf_op jit(solution)/shard_map/convert_element_type | solution.py:868
  203.9 2.7 %shard_map.218 = (f32[384,384]{1,0:T(8,128)}, f32[384,384]{1,0:T(8,128)}) custom-call(bf16[4,2,2,64,384]{4,3,2,1,0:T(8,128)(2,1)S(1)} %pad_maximum_fusion.refs_0_, bf16[4,2,2,64,384]{4,3,2,1,0:T(8,128)(2,1)S(1)} %collective-permute-done.39.refs_1_, bf16[4,2,2,64,384]{4,3,2,1,0:T(8,128)(2,1)} %collective-permute-done.38.refs_2_, ...), custom_call_target="tpu_custom_call" | custom-call | flops 1 | bytes 1 | tf_op jit(solution)/shard_map/pallas_call | solution.py:307
  (150 shorter events, 18.2 us)
Async XLA Ops:
  0.6 22.5 %collective-permute-start.2 = (bf16[512,384]{1,0:T(8,128)(2,1)}, bf16[512,384]{1,0:T(8,128)(2,1)}, u32[]{:S(2)}, u32[]{:S(2)}) collective-permute-start(bf16[512,384]{1,0:T(8,128)(2,1)} %refs_4_.1), channel_id=1, source_target_pairs={{0,1},{1,0},{2,3},{3,2},{4,5},{5,4},{6,7},{7,6},{8,9},{9,8},{10,11... | collective-permute-start | bytes 1179656 | tf_op jit(solution)/shard_map/ppermute | solution.py:40
  3.7 19.5 %collective-permute-start.3 = (bf16[512,384]{1,0:T(8,128)(2,1)}, bf16[512,384]{1,0:T(8,128)(2,1)}, u32[]{:S(2)}, u32[]{:S(2)}) collective-permute-start(bf16[512,384]{1,0:T(8,128)(2,1)} %refs_5_.1), channel_id=1, source_target_pairs={{0,1},{1,0},{2,3},{3,2},{4,5},{5,4},{6,7},{7,6},{8,9},{9,8},{10,11... | collective-permute-start | bytes 1179656 | tf_op jit(solution)/shard_map/ppermute | solution.py:40
  3.7 19.4 %collective-permute-start = (bf16[384,384]{1,0:T(8,128)(2,1)}, bf16[384,384]{1,0:T(8,128)(2,1)}, u32[]{:S(2)}, u32[]{:S(2)}) collective-permute-start(bf16[384,384]{1,0:T(8,128)(2,1)} %refs_0_.3), channel_id=1, source_target_pairs={{0,2},{1,3},{2,4},{3,5},{4,6},{5,7},{6,0},{7,1},{8,10},{9,11},{10,... | collective-permute-start | bytes 884744 | tf_op jit(solution)/shard_map/ppermute | solution.py:40
  5.7 17.4 %collective-permute-start.1 = (bf16[384,384]{1,0:T(8,128)(2,1)}, bf16[384,384]{1,0:T(8,128)(2,1)}, u32[]{:S(2)}, u32[]{:S(2)}) collective-permute-start(bf16[384,384]{1,0:T(8,128)(2,1)} %refs_1_.3), channel_id=1, source_target_pairs={{0,2},{1,3},{2,4},{3,5},{4,6},{5,7},{6,0},{7,1},{8,10},{9,11},{10,... | collective-permute-start | bytes 884744 | tf_op jit(solution)/shard_map/ppermute | solution.py:40
  15.9 17.3 %copy-start.2 = (bf16[256,3072]{1,0:T(8,128)(2,1)S(1)}, bf16[256,3072]{1,0:T(8,128)(2,1)}, u32[]{:S(2)}) copy-start(bf16[256,3072]{1,0:T(8,128)(2,1)} %video_ref) | copy-start | bytes 4718596
  23.2 7.4 %collective-permute-start.4 = (bf16[64,4096]{1,0:T(8,128)(2,1)}, bf16[64,4096]{1,0:T(8,128)(2,1)S(1)}, u32[]{:S(2)}, u32[]{:S(2)}) collective-permute-start(bf16[64,4096]{1,0:T(8,128)(2,1)} %get-tuple-element.96), channel_id=1, source_target_pairs={{0,8},{8,0},{16,24},{24,16},{1,9},{9,1},{17,25},{25,17},{2,10},{10... | collective-permute-start | bytes 1572872 | tf_op jit(solution)/shard_map/ppermute | solution.py:44
  23.3 12.7 %collective-permute-start.6 = (bf16[384,384]{1,0:T(8,128)(2,1)S(1)}, bf16[384,384]{1,0:T(8,128)(2,1)S(1)}, u32[]{:S(2)}, u32[]{:S(2)}) collective-permute-start(bf16[384,384]{1,0:T(8,128)(2,1)S(1)} %copy-done.4), channel_id=1, source_target_pairs={{0,1},{1,0},{2,3},{3,2},{4,5},{5,4},{6,7},{7,6},{8,9},{9,8},{10,11... | collective-permute-start | bytes 884744 | tf_op jit(solution)/shard_map/ppermute | solution.py:40
  24.9 14.6 %collective-permute-start.7 = (bf16[384,384]{1,0:T(8,128)(2,1)S(1)}, bf16[384,384]{1,0:T(8,128)(2,1)S(1)}, u32[]{:S(2)}, u32[]{:S(2)}) collective-permute-start(bf16[384,384]{1,0:T(8,128)(2,1)S(1)} %copy-done.5), channel_id=1, source_target_pairs={{0,1},{1,0},{2,3},{3,2},{4,5},{5,4},{6,7},{7,6},{8,9},{9,8},{10,11... | collective-permute-start | bytes 884744 | tf_op jit(solution)/shard_map/ppermute | solution.py:40
  27.4 24.3 %collective-permute-start.12 = (bf16[768,384]{1,0:T(8,128)(2,1)S(1)}, bf16[768,384]{1,0:T(8,128)(2,1)S(1)}, u32[]{:S(2)}, u32[]{:S(2)}) collective-permute-start(bf16[768,384]{1,0:T(8,128)(2,1)S(1)} %constant_dynamic-update-slice_fusion.refs_4_), channel_id=1, source_target_pairs={{0,1},{1,0},{2,3},{3,2},{4,5},{5,4},{6,7},{7,6},{8,9},{9,8},{10,11... | collective-permute-start | bytes 1769480 | tf_op jit(solution)/shard_map/ppermute | solution.py:40
  29.0 22.7 %collective-permute-start.11 = (bf16[768,384]{1,0:T(8,128)(2,1)S(1)}, bf16[768,384]{1,0:T(8,128)(2,1)S(1)}, u32[]{:S(2)}, u32[]{:S(2)}) collective-permute-start(bf16[768,384]{1,0:T(8,128)(2,1)S(1)} %constant_dynamic-update-slice_fusion.refs_4_), channel_id=1, source_target_pairs={{0,2},{1,3},{2,4},{3,5},{4,6},{5,7},{6,0},{7,1},{8,10},{9,11},{10,... | collective-permute-start | bytes 1769480 | tf_op jit(solution)/shard_map/ppermute | solution.py:40
  31.6 7.9 %collective-permute-start.5 = (bf16[32,4096]{1,0:T(8,128)(2,1)S(1)}, bf16[32,4096]{1,0:T(8,128)(2,1)S(1)}, u32[]{:S(2)}, u32[]{:S(2)}) collective-permute-start(bf16[32,4096]{1,0:T(8,128)(2,1)S(1)} %add_convert_fusion.2), channel_id=1, source_target_pairs={{0,16},{8,24},{16,0},{24,8},{1,17},{9,25},{17,1},{25,9},{2,18},{10... | collective-permute-start | bytes 786440 | tf_op jit(solution)/shard_map/ppermute | solution.py:44
  35.9 50.0 %copy-start.25 = (f32[256,1]{1,0:T(8,128)}, f32[256,1]{1,0:T(8,128)S(1)}, u32[]{:S(2)}) copy-start(f32[256,1]{1,0:T(8,128)S(1)} %get-tuple-element.154) | copy-start | bytes 3076
  35.9 72.6 %copy-start.24 = (f32[256,1]{1,0:T(8,128)}, f32[256,1]{1,0:T(8,128)S(1)}, u32[]{:S(2)}) copy-start(f32[256,1]{1,0:T(8,128)S(1)} %get-tuple-element.168) | copy-start | bytes 3076
  35.9 26.4 %copy-start.22 = (bf16[512,384]{1,0:T(8,128)(2,1)S(1)}, bf16[512,384]{1,0:T(8,128)(2,1)}, u32[]{:S(2)}) copy-start(bf16[512,384]{1,0:T(8,128)(2,1)} %refs_4_.1) | copy-start | bytes 1179652
  35.9 26.4 %copy-start.23 = (bf16[512,384]{1,0:T(8,128)(2,1)S(1)}, bf16[512,384]{1,0:T(8,128)(2,1)}, u32[]{:S(2)}) copy-start(bf16[512,384]{1,0:T(8,128)(2,1)} %refs_5_.1) | copy-start | bytes 1179652
  40.3 8.2 %collective-permute-start.8 = (bf16[32,1024]{1,0:T(8,128)(2,1)S(1)}, bf16[32,1024]{1,0:T(8,128)(2,1)S(1)}, u32[]{:S(2)}, u32[]{:S(2)}) collective-permute-start(bf16[32,1024]{1,0:T(8,128)(2,1)S(1)} %get-tuple-element.101), channel_id=1, source_target_pairs={{0,2},{1,3},{2,4},{3,5},{4,6},{5,7},{6,0},{7,1},{8,10},{9,11},{10,... | collective-permute-start | bytes 196616 | tf_op jit(solution)/shard_map/ppermute | solution.py:40
  42.0 7.9 %collective-permute-start.9 = (bf16[32,1024]{1,0:T(8,128)(2,1)S(1)}, bf16[32,1024]{1,0:T(8,128)(2,1)S(1)}, u32[]{:S(2)}, u32[]{:S(2)}) collective-permute-start(bf16[32,1024]{1,0:T(8,128)(2,1)S(1)} %get-tuple-element.102), channel_id=1, source_target_pairs={{0,4},{1,5},{2,6},{3,7},{4,0},{5,1},{6,2},{7,3},{8,12},{9,13},{10,... | collective-permute-start | bytes 196616 | tf_op jit(solution)/shard_map/ppermute | solution.py:40
  43.2 6.7 %collective-permute-start.10 = (bf16[32,1024]{1,0:T(8,128)(2,1)S(1)}, bf16[32,1024]{1,0:T(8,128)(2,1)S(1)}, u32[]{:S(2)}, u32[]{:S(2)}) collective-permute-start(bf16[32,1024]{1,0:T(8,128)(2,1)S(1)} %get-tuple-element.103), channel_id=1, source_target_pairs={{0,6},{1,7},{2,0},{3,1},{4,2},{5,3},{6,4},{7,5},{8,14},{9,15},{10,... | collective-permute-start | bytes 196616 | tf_op jit(solution)/shard_map/ppermute | solution.py:40
  51.7 16.7 %collective-permute-start.16 = (bf16[768,384]{1,0:T(8,128)(2,1)S(1)}, bf16[768,384]{1,0:T(8,128)(2,1)S(1)}, u32[]{:S(2)}, u32[]{:S(2)}) collective-permute-start(bf16[768,384]{1,0:T(8,128)(2,1)S(1)} %collective-permute-done.11.refs_6_), channel_id=1, source_target_pairs={{0,2},{1,3},{2,4},{3,5},{4,6},{5,7},{6,0},{7,1},{8,10},{9,11},{10,... | collective-permute-start | bytes 1769480 | tf_op jit(solution)/shard_map/ppermute | solution.py:40
  53.2 7.6 %collective-permute-start.14 = (bf16[4,32,1024]{2,1,0:T(8,128)(2,1)S(1)}, bf16[4,32,1024]{2,1,0:T(8,128)(2,1)S(1)}, u32[]{:S(2)}, u32[]{:S(2)}) collective-permute-start(bf16[4,32,1024]{2,1,0:T(8,128)(2,1)S(1)} %pad_maximum_fusion.1.refs_0_), channel_id=1, source_target_pairs={{0,16},{8,24},{16,0},{24,8},{1,17},{9,25},{17,1},{25,9},{2,18},{10... | collective-permute-start | bytes 786440 | tf_op jit(solution)/shard_map/ppermute | solution.py:44
  54.7 7.6 %collective-permute-start.13 = (bf16[4,32,1024]{2,1,0:T(8,128)(2,1)S(1)}, bf16[4,32,1024]{2,1,0:T(8,128)(2,1)S(1)}, u32[]{:S(2)}, u32[]{:S(2)}) collective-permute-start(bf16[4,32,1024]{2,1,0:T(8,128)(2,1)S(1)} %pad_maximum_fusion.1.refs_0_), channel_id=1, source_target_pairs={{0,8},{8,0},{16,24},{24,16},{1,9},{9,1},{17,25},{25,17},{2,10},{10... | collective-permute-start | bytes 786440 | tf_op jit(solution)/shard_map/ppermute | solution.py:44
  60.8 1.5 collective-permute-start.15
  60.8 25.1 %collective-permute-start.20 = (bf16[768,384]{1,0:T(8,128)(2,1)S(1)}, bf16[768,384]{1,0:T(8,128)(2,1)S(1)}, u32[]{:S(2)}, u32[]{:S(2)}) collective-permute-start(bf16[768,384]{1,0:T(8,128)(2,1)S(1)} %collective-permute-done.11.refs_6_), channel_id=1, source_target_pairs={{0,1},{1,0},{2,3},{3,2},{4,5},{5,4},{6,7},{7,6},{8,9},{9,8},{10,11... | collective-permute-start | bytes 1769480 | tf_op jit(solution)/shard_map/ppermute | solution.py:40
  68.3 6.7 %collective-permute-start.17 = (bf16[128,768]{1,0:T(8,128)(2,1)S(1)}, bf16[128,768]{1,0:T(8,128)(2,1)S(1)}, u32[]{:S(2)}, u32[]{:S(2)}) collective-permute-start(bf16[128,768]{1,0:T(8,128)(2,1)S(1)} %get-tuple-element.111), channel_id=1, source_target_pairs={{0,6},{1,7},{2,0},{3,1},{4,2},{5,3},{6,4},{7,5},{8,14},{9,15},{10,... | collective-permute-start | bytes 589832 | tf_op jit(solution)/shard_map/ppermute | solution.py:40
  68.8 17.0 %collective-permute-start.18 = (bf16[128,768]{1,0:T(8,128)(2,1)S(1)}, bf16[128,768]{1,0:T(8,128)(2,1)S(1)}, u32[]{:S(2)}, u32[]{:S(2)}) collective-permute-start(bf16[128,768]{1,0:T(8,128)(2,1)S(1)} %get-tuple-element.112), channel_id=1, source_target_pairs={{0,4},{1,5},{2,6},{3,7},{4,0},{5,1},{6,2},{7,3},{8,12},{9,13},{10,... | collective-permute-start | bytes 589832 | tf_op jit(solution)/shard_map/ppermute | solution.py:40
  69.6 16.2 %collective-permute-start.19 = (bf16[128,768]{1,0:T(8,128)(2,1)S(1)}, bf16[128,768]{1,0:T(8,128)(2,1)S(1)}, u32[]{:S(2)}, u32[]{:S(2)}) collective-permute-start(bf16[128,768]{1,0:T(8,128)(2,1)S(1)} %get-tuple-element.113), channel_id=1, source_target_pairs={{0,2},{1,3},{2,4},{3,5},{4,6},{5,7},{6,0},{7,1},{8,10},{9,11},{10,... | collective-permute-start | bytes 589832 | tf_op jit(solution)/shard_map/ppermute | solution.py:40
  70.4 19.7 %collective-permute-start.23 = (bf16[4,2,64,384]{3,2,1,0:T(8,128)(2,1)S(1)}, bf16[4,2,64,384]{3,2,1,0:T(8,128)(2,1)S(1)}, u32[]{:S(2)}, u32[]{:S(2)}) collective-permute-start(bf16[4,2,64,384]{3,2,1,0:T(8,128)(2,1)S(1)} %get-tuple-element.115), channel_id=1, source_target_pairs={{0,1},{1,0},{2,3},{3,2},{4,5},{5,4},{6,7},{7,6},{8,9},{9,8},{10,11... | collective-permute-start | bytes 1179656 | tf_op jit(solution)/shard_map/ppermute | solution.py:40
  75.0 32.4 %collective-permute-start.22 = (bf16[768,384]{1,0:T(8,128)(2,1)S(1)}, bf16[768,384]{1,0:T(8,128)(2,1)S(1)}, u32[]{:S(2)}, u32[]{:S(2)}) collective-permute-start(bf16[768,384]{1,0:T(8,128)(2,1)S(1)} %collective-permute-done.16.refs_8_), channel_id=1, source_target_pairs={{0,1},{1,0},{2,3},{3,2},{4,5},{5,4},{6,7},{7,6},{8,9},{9,8},{10,11... | collective-permute-start | bytes 1769480 | tf_op jit(solution)/shard_map/ppermute | solution.py:40
  85.9 5.7 %collective-permute-start.28 = (bf16[128,768]{1,0:T(8,128)(2,1)S(1)}, bf16[128,768]{1,0:T(8,128)(2,1)S(1)}, u32[]{:S(2)}, u32[]{:S(2)}) collective-permute-start(bf16[128,768]{1,0:T(8,128)(2,1)S(1)} %add_convert_fusion.4.refs_0_), channel_id=1, source_target_pairs={{0,6},{1,7},{2,0},{3,1},{4,2},{5,3},{6,4},{7,5},{8,14},{9,15},{10,... | collective-permute-start | bytes 589832 | tf_op jit(solution)/shard_map/ppermute | solution.py:40
  85.9 13.6 %collective-permute-start.25 = (bf16[128,768]{1,0:T(8,128)(2,1)S(1)}, bf16[128,768]{1,0:T(8,128)(2,1)S(1)}, u32[]{:S(2)}, u32[]{:S(2)}) collective-permute-start(bf16[128,768]{1,0:T(8,128)(2,1)S(1)} %add_convert_fusion.4.refs_0_), channel_id=1, source_target_pairs={{0,2},{1,3},{2,4},{3,5},{4,6},{5,7},{6,0},{7,1},{8,10},{9,11},{10,... | collective-permute-start | bytes 589832 | tf_op jit(solution)/shard_map/ppermute | solution.py:40
  88.0 17.8 %collective-permute-start.21 = (bf16[128,768]{1,0:T(8,128)(2,1)S(1)}, bf16[128,768]{1,0:T(8,128)(2,1)S(1)}, u32[]{:S(2)}, u32[]{:S(2)}) collective-permute-start(bf16[128,768]{1,0:T(8,128)(2,1)S(1)} %add_convert_fusion.4.refs_0_), channel_id=1, source_target_pairs={{0,4},{1,5},{2,6},{3,7},{4,0},{5,1},{6,2},{7,3},{8,12},{9,13},{10,... | collective-permute-start | bytes 589832 | tf_op jit(solution)/shard_map/ppermute | solution.py:40
  90.1 17.4 %collective-permute-start.24 = (bf16[128,768]{1,0:T(8,128)(2,1)S(1)}, bf16[128,768]{1,0:T(8,128)(2,1)S(1)}, u32[]{:S(2)}, u32[]{:S(2)}) collective-permute-start(bf16[128,768]{1,0:T(8,128)(2,1)S(1)} %add_convert_fusion.4.refs_0_), channel_id=1, source_target_pairs={{0,1},{1,0},{2,3},{3,2},{4,5},{5,4},{6,7},{7,6},{8,9},{9,8},{10,11... | collective-permute-start | bytes 589832 | tf_op jit(solution)/shard_map/ppermute | solution.py:40
  91.6 16.9 %collective-permute-start.29 = (bf16[128,768]{1,0:T(8,128)(2,1)S(1)}, bf16[128,768]{1,0:T(8,128)(2,1)S(1)}, u32[]{:S(2)}, u32[]{:S(2)}) collective-permute-start(bf16[128,768]{1,0:T(8,128)(2,1)S(1)} %collective-permute-done.28.refs_6_), channel_id=1, source_target_pairs={{0,1},{1,0},{2,3},{3,2},{4,5},{5,4},{6,7},{7,6},{8,9},{9,8},{10,11... | collective-permute-start | bytes 589832 | tf_op jit(solution)/shard_map/ppermute | solution.py:40
  99.6 14.6 %collective-permute-start.26 = (bf16[128,768]{1,0:T(8,128)(2,1)S(1)}, bf16[128,768]{1,0:T(8,128)(2,1)S(1)}, u32[]{:S(2)}, u32[]{:S(2)}) collective-permute-start(bf16[128,768]{1,0:T(8,128)(2,1)S(1)} %collective-permute-done.25.refs_2_), channel_id=1, source_target_pairs={{0,1},{1,0},{2,3},{3,2},{4,5},{5,4},{6,7},{7,6},{8,9},{9,8},{10,11... | collective-permute-start | bytes 589832 | tf_op jit(solution)/shard_map/ppermute | solution.py:40
  105.8 8.7 %collective-permute-start.27 = (bf16[128,768]{1,0:T(8,128)(2,1)S(1)}, bf16[128,768]{1,0:T(8,128)(2,1)S(1)}, u32[]{:S(2)}, u32[]{:S(2)}) collective-permute-start(bf16[128,768]{1,0:T(8,128)(2,1)S(1)} %collective-permute-done.21.refs_4_), channel_id=1, source_target_pairs={{0,1},{1,0},{2,3},{3,2},{4,5},{5,4},{6,7},{7,6},{8,9},{9,8},{10,11... | collective-permute-start | bytes 589832 | tf_op jit(solution)/shard_map/ppermute | solution.py:40
  107.5 11.3 %collective-permute-start.30 = (bf16[2,2,64,384]{3,2,1,0:T(8,128)(2,1)S(1)}, bf16[2,2,64,384]{3,2,1,0:T(8,128)(2,1)S(1)}, u32[]{:S(2)}, u32[]{:S(2)}) collective-permute-start(bf16[2,2,64,384]{3,2,1,0:T(8,128)(2,1)S(1)} %get-tuple-element.124), channel_id=1, source_target_pairs={{0,2},{1,3},{2,4},{3,5},{4,6},{5,7},{6,0},{7,1},{8,10},{9,11},{10,... | collective-permute-start | bytes 589832 | tf_op jit(solution)/shard_map/ppermute | solution.py:40
  107.5 16.4 %collective-permute-start.31 = (bf16[2,2,64,384]{3,2,1,0:T(8,128)(2,1)S(1)}, bf16[2,2,64,384]{3,2,1,0:T(8,128)(2,1)S(1)}, u32[]{:S(2)}, u32[]{:S(2)}) collective-permute-start(bf16[2,2,64,384]{3,2,1,0:T(8,128)(2,1)S(1)} %get-tuple-element.125), channel_id=1, source_target_pairs={{0,4},{1,5},{2,6},{3,7},{4,0},{5,1},{6,2},{7,3},{8,12},{9,13},{10,... | collective-permute-start | bytes 589832 | tf_op jit(solution)/shard_map/ppermute | solution.py:40
  108.5 15.4 %collective-permute-start.32 = (bf16[2,2,64,384]{3,2,1,0:T(8,128)(2,1)S(1)}, bf16[2,2,64,384]{3,2,1,0:T(8,128)(2,1)S(1)}, u32[]{:S(2)}, u32[]{:S(2)}) collective-permute-start(bf16[2,2,64,384]{3,2,1,0:T(8,128)(2,1)S(1)} %get-tuple-element.126), channel_id=1, source_target_pairs={{0,6},{1,7},{2,0},{3,1},{4,2},{5,3},{6,4},{7,5},{8,14},{9,15},{10,... | collective-permute-start | bytes 589832 | tf_op jit(solution)/shard_map/ppermute | solution.py:40
  117.3 32.5 %copy-start.8 = (bf16[2,256,384]{2,1,0:T(8,128)(2,1)}, bf16[2,256,384]{2,1,0:T(8,128)(2,1)S(1)}, u32[]{:S(2)}) copy-start(bf16[2,256,384]{2,1,0:T(8,128)(2,1)S(1)} %get-tuple-element.158.refs_4_) | copy-start | bytes 1179652
  117.3 1.4 collective-permute-start.33
  118.8 43.8 %copy-start.35 = (f32[256,2]{1,0:T(8,128)}, f32[256,2]{1,0:T(8,128)S(1)}, u32[]{:S(2)}) copy-start(f32[256,2]{1,0:T(8,128)S(1)} %add.74) | copy-start | bytes 6148
  124.0 19.0 %collective-permute-start.36 = (bf16[2,256,384]{2,1,0:T(8,128)(2,1)S(1)}, bf16[2,256,384]{2,1,0:T(8,128)(2,1)S(1)}, u32[]{:S(2)}, u32[]{:S(2)}) collective-permute-start(bf16[2,256,384]{2,1,0:T(8,128)(2,1)S(1)} %get-tuple-element.158.refs_4_), channel_id=1, source_target_pairs={{0,2},{1,3},{2,4},{3,5},{4,6},{5,7},{6,0},{7,1},{8,10},{9,11},{10,... | collective-permute-start | bytes 1179656 | tf_op jit(solution)/shard_map/ppermute | solution.py:40
  136.3 25.5 %collective-permute-start.39 = (bf16[4,2,2,64,384]{4,3,2,1,0:T(8,128)(2,1)S(1)}, bf16[4,2,2,64,384]{4,3,2,1,0:T(8,128)(2,1)S(1)}, u32[]{:S(2)}, u32[]{:S(2)}) collective-permute-start(bf16[4,2,2,64,384]{4,3,2,1,0:T(8,128)(2,1)S(1)} %pad_maximum_fusion.refs_0_), channel_id=1, source_target_pairs={{0,8},{8,0},{16,24},{24,16},{1,9},{9,1},{17,25},{25,17},{2,10},{10... | collective-permute-start | bytes 2359304 | tf_op jit(solution)/shard_map/ppermute | solution.py:44
  136.4 25.4 %collective-permute-start.38 = (bf16[4,2,2,64,384]{4,3,2,1,0:T(8,128)(2,1)S(1)}, bf16[4,2,2,64,384]{4,3,2,1,0:T(8,128)(2,1)}, u32[]{:S(2)}, u32[]{:S(2)}) collective-permute-start(bf16[4,2,2,64,384]{4,3,2,1,0:T(8,128)(2,1)S(1)} %pad_maximum_fusion.refs_0_), channel_id=1, source_target_pairs={{0,16},{8,24},{16,0},{24,8},{1,17},{9,25},{17,1},{25,9},{2,18},{10... | collective-permute-start | bytes 2359304 | tf_op jit(solution)/shard_map/ppermute | solution.py:44
  138.0 23.8 %collective-permute-start.34 = (bf16[3,128,768]{2,1,0:T(8,128)(2,1)S(1)}, bf16[3,128,768]{2,1,0:T(8,128)(2,1)S(1)}, u32[]{:S(2)}, u32[]{:S(2)}) collective-permute-start(bf16[3,128,768]{2,1,0:T(8,128)(2,1)S(1)} %get-tuple-element.145.own_ref), channel_id=1, source_target_pairs={{0,1},{1,0},{2,3},{3,2},{4,5},{5,4},{6,7},{7,6},{8,9},{9,8},{10,11... | collective-permute-start | bytes 1769480 | tf_op jit(solution)/shard_map/ppermute | solution.py:40
  138.5 23.3 %collective-permute-start.35 = (bf16[2,256,384]{2,1,0:T(8,128)(2,1)S(1)}, bf16[2,256,384]{2,1,0:T(8,128)(2,1)S(1)}, u32[]{:S(2)}, u32[]{:S(2)}) collective-permute-start(bf16[2,256,384]{2,1,0:T(8,128)(2,1)S(1)} %get-tuple-element.158.refs_4_), channel_id=1, source_target_pairs={{0,1},{1,0},{2,3},{3,2},{4,5},{5,4},{6,7},{7,6},{8,9},{9,8},{10,11... | collective-permute-start | bytes 1179656 | tf_op jit(solution)/shard_map/ppermute | solution.py:40
  142.9 20.2 %copy-start.10 = (bf16[2,256,384]{2,1,0:T(8,128)(2,1)}, bf16[2,256,384]{2,1,0:T(8,128)(2,1)S(1)}, u32[]{:S(2)}) copy-start(bf16[2,256,384]{2,1,0:T(8,128)(2,1)S(1)} %collective-permute-done.36.refs_5_) | copy-start | bytes 1179652
  142.9 18.9 %collective-permute-start.37 = (bf16[2,256,384]{2,1,0:T(8,128)(2,1)S(1)}, bf16[2,256,384]{2,1,0:T(8,128)(2,1)S(1)}, u32[]{:S(2)}, u32[]{:S(2)}) collective-permute-start(bf16[2,256,384]{2,1,0:T(8,128)(2,1)S(1)} %collective-permute-done.36.refs_5_), channel_id=1, source_target_pairs={{0,2},{1,3},{2,4},{3,5},{4,6},{5,7},{6,0},{7,1},{8,10},{9,11},{10,... | collective-permute-start | bytes 1179656 | tf_op jit(solution)/shard_map/ppermute | solution.py:40
  149.8 20.4 %copy-start.6 = (bf16[2,256,768]{2,1,0:T(8,128)(2,1)}, bf16[2,256,768]{2,1,0:T(8,128)(2,1)S(1)}, u32[]{:S(2)}) copy-start(bf16[2,256,768]{2,1,0:T(8,128)(2,1)S(1)} %get-tuple-element.134) | copy-start | bytes 2359300
  161.8 3.5 %collective-permute-start.40 = (bf16[2,256,1536]{2,1,0:T(8,128)(2,1)S(1)}, bf16[2,256,1536]{2,1,0:T(8,128)(2,1)S(1)}, u32[]{:S(2)}, u32[]{:S(2)}) collective-permute-start(bf16[2,256,1536]{2,1,0:T(8,128)(2,1)S(1)} %get-tuple-element.139), channel_id=1, source_target_pairs={{0,8},{8,0},{16,24},{24,16},{1,9},{9,1},{17,25},{25,17},{2,10},{10... | collective-permute-start | bytes 4718600 | tf_op jit(solution)/shard_map/ppermute | solution.py:44
  161.9 20.7 %collective-permute-start.43 = (bf16[2,256,384]{2,1,0:T(8,128)(2,1)S(1)}, bf16[2,256,384]{2,1,0:T(8,128)(2,1)}, u32[]{:S(2)}, u32[]{:S(2)}) collective-permute-start(bf16[2,256,384]{2,1,0:T(8,128)(2,1)S(1)} %collective-permute-done.37.refs_6_), channel_id=1, source_target_pairs={{0,2},{1,3},{2,4},{3,5},{4,6},{5,7},{6,0},{7,1},{8,10},{9,11},{10,... | collective-permute-start | bytes 1179656 | tf_op jit(solution)/shard_map/ppermute | solution.py:40
  162.0 20.6 %collective-permute-start.42 = (bf16[2,256,384]{2,1,0:T(8,128)(2,1)S(1)}, bf16[2,256,384]{2,1,0:T(8,128)(2,1)S(1)}, u32[]{:S(2)}, u32[]{:S(2)}) collective-permute-start(bf16[2,256,384]{2,1,0:T(8,128)(2,1)S(1)} %collective-permute-done.37.refs_6_), channel_id=1, source_target_pairs={{0,1},{1,0},{2,3},{3,2},{4,5},{5,4},{6,7},{7,6},{8,9},{9,8},{10,11... | collective-permute-start | bytes 1179656 | tf_op jit(solution)/shard_map/ppermute | solution.py:40
  162.6 5.5 %collective-permute-start.45 = (f32[256,2]{1,0:T(8,128)S(1)}, f32[256,2]{1,0:T(8,128)S(1)}, u32[]{:S(2)}, u32[]{:S(2)}) collective-permute-start(f32[256,2]{1,0:T(8,128)S(1)} %add.74), channel_id=1, source_target_pairs={{0,16},{8,24},{16,0},{24,8},{1,17},{9,25},{17,1},{25,9},{2,18},{10... | collective-permute-start | bytes 6152 | tf_op jit(solution)/shard_map/ppermute | solution.py:44
  163.1 18.8 %collective-permute-start.41 = (bf16[2,256,384]{2,1,0:T(8,128)(2,1)S(1)}, bf16[2,256,384]{2,1,0:T(8,128)(2,1)S(1)}, u32[]{:S(2)}, u32[]{:S(2)}) collective-permute-start(bf16[2,256,384]{2,1,0:T(8,128)(2,1)S(1)} %collective-permute-done.36.refs_5_), channel_id=1, source_target_pairs={{0,1},{1,0},{2,3},{3,2},{4,5},{5,4},{6,7},{7,6},{8,9},{9,8},{10,11... | collective-permute-start | bytes 1179656 | tf_op jit(solution)/shard_map/ppermute | solution.py:40
  166.4 25.8 %copy-start.9 = (bf16[2,256,384]{2,1,0:T(8,128)(2,1)S(1)}, bf16[2,256,384]{2,1,0:T(8,128)(2,1)}, u32[]{:S(2)}) copy-start(bf16[2,256,384]{2,1,0:T(8,128)(2,1)} %copy-done.8) | copy-start | bytes 1179652
  168.7 14.7 %collective-permute-start.46 = (bf16[256,768]{1,0:T(8,128)(2,1)S(1)}, bf16[256,768]{1,0:T(8,128)(2,1)S(1)}, u32[]{:S(2)}, u32[]{:S(2)}) collective-permute-start(bf16[256,768]{1,0:T(8,128)(2,1)S(1)} %get-tuple-element.152), channel_id=1, source_target_pairs={{0,16},{8,24},{16,0},{24,8},{1,17},{9,25},{17,1},{25,9},{2,18},{10... | collective-permute-start | bytes 1179656 | tf_op jit(solution)/shard_map/ppermute | solution.py:44
  171.0 11.6 %copy-start.31 = (bf16[128,768]{1,0:T(8,128)(2,1)}, bf16[128,768]{1,0:T(8,128)(2,1)S(1)}, u32[]{:S(2)}) copy-start(bf16[128,768]{1,0:T(8,128)(2,1)S(1)} %get-tuple-element.176) | copy-start | bytes 589828
  171.0 12.3 %copy-start.32 = (bf16[128,768]{1,0:T(8,128)(2,1)}, bf16[128,768]{1,0:T(8,128)(2,1)S(1)}, u32[]{:S(2)}) copy-start(bf16[128,768]{1,0:T(8,128)(2,1)S(1)} %get-tuple-element.175) | copy-start | bytes 589828
  171.0 12.3 %collective-permute-start.44 = (bf16[128,768]{1,0:T(8,128)(2,1)S(1)}, bf16[128,768]{1,0:T(8,128)(2,1)S(1)}, u32[]{:S(2)}, u32[]{:S(2)}) collective-permute-start(bf16[128,768]{1,0:T(8,128)(2,1)S(1)} %get-tuple-element.147), channel_id=1, source_target_pairs={{0,2},{1,3},{2,4},{3,5},{4,6},{5,7},{6,0},{7,1},{8,10},{9,11},{10,... | collective-permute-start | bytes 589832 | tf_op jit(solution)/shard_map/ppermute | solution.py:40
  184.2 8.0 %collective-permute-start.48 = (bf16[4,2,2,64,384]{4,3,2,1,0:T(8,128)(2,1)}, bf16[4,2,2,64,384]{4,3,2,1,0:T(8,128)(2,1)}, u32[]{:S(2)}, u32[]{:S(2)}) collective-permute-start(bf16[4,2,2,64,384]{4,3,2,1,0:T(8,128)(2,1)} %collective-permute-done.38.refs_2_), channel_id=1, source_target_pairs={{0,8},{8,0},{16,24},{24,16},{1,9},{9,1},{17,25},{25,17},{2,10},{10... | collective-permute-start | bytes 2359304 | tf_op jit(solution)/shard_map/ppermute | solution.py:44
  184.2 16.2 %collective-permute-start.47 = (bf16[256,768]{1,0:T(8,128)(2,1)}, bf16[256,768]{1,0:T(8,128)(2,1)}, u32[]{:S(2)}, u32[]{:S(2)}) collective-permute-start(bf16[256,768]{1,0:T(8,128)(2,1)} %get-tuple-element.155), channel_id=1, source_target_pairs={{0,16},{8,24},{16,0},{24,8},{1,17},{9,25},{17,1},{25,9},{2,18},{10... | collective-permute-start | bytes 1179656 | tf_op jit(solution)/shard_map/ppermute | solution.py:44
  186.8 13.7 %collective-permute-start.50 = (bf16[128,768]{1,0:T(8,128)(2,1)}, bf16[128,768]{1,0:T(8,128)(2,1)S(1)}, u32[]{:S(2)}, u32[]{:S(2)}) collective-permute-start(bf16[128,768]{1,0:T(8,128)(2,1)} %copy-done.32), channel_id=1, source_target_pairs={{0,4},{1,5},{2,6},{3,7},{4,0},{5,1},{6,2},{7,3},{8,12},{9,13},{10,... | collective-permute-start | bytes 589832 | tf_op jit(solution)/shard_map/ppermute | solution.py:40
  186.9 13.6 %collective-permute-start.51 = (bf16[128,768]{1,0:T(8,128)(2,1)}, bf16[128,768]{1,0:T(8,128)(2,1)S(1)}, u32[]{:S(2)}, u32[]{:S(2)}) collective-permute-start(bf16[128,768]{1,0:T(8,128)(2,1)} %copy-done.31), channel_id=1, source_target_pairs={{0,6},{1,7},{2,0},{3,1},{4,2},{5,3},{6,4},{7,5},{8,14},{9,15},{10,... | collective-permute-start | bytes 589832 | tf_op jit(solution)/shard_map/ppermute | solution.py:40
  191.7 12.2 %collective-permute-start.49 = (bf16[2,256,384]{2,1,0:T(8,128)(2,1)}, bf16[2,256,384]{2,1,0:T(8,128)(2,1)S(1)}, u32[]{:S(2)}, u32[]{:S(2)}) collective-permute-start(bf16[2,256,384]{2,1,0:T(8,128)(2,1)} %collective-permute-done.43.refs_7_), channel_id=1, source_target_pairs={{0,1},{1,0},{2,3},{3,2},{4,5},{5,4},{6,7},{7,6},{8,9},{9,8},{10,11... | collective-permute-start | bytes 1179656 | tf_op jit(solution)/shard_map/ppermute | solution.py:40
  (29 other events, 130.9 us)

commit v13 on v11

--- a/solution.py
+++ b/solution.py
@@ -870,12 +870,14 @@
         + inverse * (total[1] - row_sums[:, 0:1] - video_hat * row_sums[:, 1:2])
     ).astype(BF)
     kv_parts += [fsend(terms[far], far, 0) for far in range(2, pairs)]
+    known = after(known, updated, input_grad)
+    query_grad, out_weight_grad = weight_grads(
+        tiles, [None] * (pairs + 3) + there[3:], known, pairs
+    )
+    kv_parts = after(kv_parts, query_grad)
     kv_grads = (terms[0] + sum(p.astype(F32) for p in kv_parts)).astype(BF)[None]
     key_grad = kv_grads[:, :, :width_local]
     value_grad = kv_grads[:, :, width_local:]
-    query_grad, out_weight_grad = weight_grads(
-        tiles, [None] * (pairs + 3) + there[3:], known, pairs
-    )
     return (updated, input_grad, query_grad, out_weight_grad, key_grad, value_grad)
 
 

time: 192 us -> 196 us (1.021)
  local copies, waits for them, and re-layouts: 4.93 us -> 14 us
  waiting for transfers between devices: 80.2 us -> 76.2 us
  other arithmetic: 10.1 us -> 7.89 us
    unnamed x73 -> x93, local copies, waits for them, and re-layouts: 3.99 us -> 13.1 us
    ppermute x37, waiting for transfers between devices: 65.6 us -> 62.7 us  [fsend(): return lax.ppermute(block, 'fsdp', perm)]
  transfers between devices with their start and end apart: 50 -> 50, of which waited for: 19 -> 16; matrix products, arithmetic and copies ran while one was open for 4% -> 4% of each run, Pallas kernels for 18% -> 19%
where the time goes in v13:
time: 196 us
  waiting for transfers between devices  76.2 us (39%)
  starting transfers between devices  59.4 us (30%)
  Pallas kernels  36.9 us (19%)
  local copies, waits for them, and re-layouts  14 us (7%)
  other arithmetic  7.89 us (4%)
    ppermute x37, waiting for transfers between devices, fsend(): return lax.ppermute(block, 'fsdp', perm)  62.7 us
    ppermute x37, starting transfers between devices, fsend(): return lax.ppermute(block, 'fsdp', perm)  52.4 us
    pallas_call x9, Pallas kernels, call(): pl.pallas_call(body, out_shape=out_shape, in_specs=specs, out_specs=jax.t...  21.8 us
    ppermute x13, waiting for transfers between devices, gsend(): lax.ppermute(block, 'grp', [(s, s ^ flip) for s in range(lax.axis_size('g...  13.5 us
    unnamed x93, local copies, waits for them, and re-layouts  13.1 us
    pallas_call x1, Pallas kernels, project_text(): pl.pallas_call(body, grid=(steps,), out_shape=shaped((rows, 3 * width)),...  7.96 us
    pallas_call x1, Pallas kernels, attend_text(): pl.pallas_call(body, grid=(steps,), out_shape=[shaped((rows // 2, depth))...  7.14 us
    ppermute x13, starting transfers between devices, gsend(): lax.ppermute(block, 'grp', [(s, s ^ flip) for s in range(lax.axis_size('g...  6.94 us
  transfers between devices with their start and end apart: 50, of which 16 were waited for; matrix products, arithmetic and copies ran while one was open for 4% of the time, Pallas kernels for 19%

profile of v13, /device:TPU:0, one launch (start us, length us, event | category | flops | bytes accessed | tf_op | source)
XLA Modules:
  0.0 195.6 jit_solution(6014261035497208953)
XLA Ops:
  0.6 3.0 %collective-permute-start.2 = (bf16[512,384]{1,0:T(8,128)(2,1)}, bf16[512,384]{1,0:T(8,128)(2,1)S(1)}, u32[]{:S(2)}, u32[]{:S(2)}) collective-permute-start(bf16[512,384]{1,0:T(8,128)(2,1)} %refs_4_.1), channel_id=1, source_target_pairs={{0,1},{1,0},{2,3},{3,2},{4,5},{5,4},{6,7},{7,6},{8,9},{9,8},{10,11... | collective-permute-start | bytes 1179656 | tf_op jit(solution)/shard_map/ppermute | solution.py:40
  3.7 2.0 %collective-permute-start = (bf16[384,384]{1,0:T(8,128)(2,1)}, bf16[384,384]{1,0:T(8,128)(2,1)S(1)}, u32[]{:S(2)}, u32[]{:S(2)}) collective-permute-start(bf16[384,384]{1,0:T(8,128)(2,1)} %refs_0_.3), channel_id=1, source_target_pairs={{0,2},{1,3},{2,4},{3,5},{4,6},{5,7},{6,0},{7,1},{8,10},{9,11},{10,... | collective-permute-start | bytes 884744 | tf_op jit(solution)/shard_map/ppermute | solution.py:40
  5.7 1.6 collective-permute-start.1
  7.3 8.0 %shard_map.208.qkv_ref = bf16[128,1536]{1,0:T(8,128)(2,1)} custom-call(bf16[128,4096]{1,0:T(8,128)(2,1)} %bitcast.40, f32[1,4096]{1,0:T(1,128)} %bitcast.53, bf16[4096,512]{1,0:T(8,128)(2,1)} %wq_ref.1, bf16[4096,512]{1,0:T(8,128)(2,1)} %wk_ref.1, bf16[4096,512]{1,0:T(8,128)(2,1)} %wv_ref.1), custom_call_target="tpu_custom_call" | custom-call | flops 1 | bytes 1 | tf_op jit(solution)/shard_map/pallas_call | solution.py:350
  15.8 7.1 %shard_map.209 = (bf16[64,4096]{1,0:T(8,128)(2,1)}, bf16[64,4096]{1,0:T(8,128)(2,1)}) custom-call(s32[3]{0:T(128)} %pad_add_fusion.place_ref, s32[8]{0:T(128)} %len_ref.3, bf16[128,1536]{1,0:T(8,128)(2,1)} %shard_map.208.qkv_ref, f32[8,128,128]{2,1,0:T(8,128)} %bias_ref.1, bf16[512,4096]{1,0:T(8,128)(2,1)} %out_ref.1), custom_call_target="tpu_custom_call" | custom-call | flops 1 | bytes 1 | tf_op jit(solution)/shard_map/pallas_call | solution.py:394
  23.2 1.6 collective-permute-start.9
  25.0 1.6 collective-permute-start.13
  26.7 1.6 collective-permute-start.5
  28.2 2.7 %shard_map.210 = (bf16[256,3072]{1,0:T(8,128)(2,1)S(1)}, f32[256,1]{1,0:T(8,128)S(1)}, f32[256,1]{1,0:T(8,128)S(1)}, bf16[4,2,64,384]{3,2,1,0:T(8,128)(2,1)S(1)}, bf16[4,2,64,384]{3,2,1,0:T(8,128)(2,1)S(1)}) custom-call(s32[3]{0:T(128)S(1)} %copy-done.31, bf16[256,3072]{1,0:T(8,128)(2,1)S(1)} %copy-done.7, bf16[256,3072]{1,0:T(8,128)(2,1)S(1)} %copy-done), custom_call_target="tpu_custom_call" | custom-call | flops 1 | bytes 1 | tf_op jit(solution)/shard_map/pallas_call | solution.py:307
  32.3 2.6 %collective-permute-done.5.far_ref = bf16[32,4096]{1,0:T(8,128)(2,1)S(1)} collective-permute-done((bf16[32,4096]{1,0:T(8,128)(2,1)S(1)}, bf16[32,4096]{1,0:T(8,128)(2,1)S(1)}, u32[]{:S(2)}, u32[]{:S(2)}) %collective-permute-start.5) | collective-permute-done | bytes 262176 | tf_op jit(solution)/shard_map/ppermute | solution.py:44
  36.2 2.4 %collective-permute-start.7 = (bf16[32,1024]{1,0:T(8,128)(2,1)S(1)}, bf16[32,1024]{1,0:T(8,128)(2,1)S(1)}, u32[]{:S(2)}, u32[]{:S(2)}) collective-permute-start(bf16[32,1024]{1,0:T(8,128)(2,1)S(1)} %get-tuple-element.103), channel_id=1, source_target_pairs={{0,4},{1,5},{2,6},{3,7},{4,0},{5,1},{6,2},{7,3},{8,12},{9,13},{10,... | collective-permute-start | bytes 196616 | tf_op jit(solution)/shard_map/ppermute | solution.py:40
  38.6 1.3 collective-permute-start.8
  39.9 2.8 %collective-permute-done.6 = bf16[32,1024]{1,0:T(8,128)(2,1)S(1)} collective-permute-done((bf16[32,1024]{1,0:T(8,128)(2,1)S(1)}, bf16[32,1024]{1,0:T(8,128)(2,1)S(1)}, u32[]{:S(2)}, u32[]{:S(2)}) %collective-permute-start.6) | collective-permute-done | bytes 65568 | tf_op jit(solution)/shard_map/ppermute | solution.py:40
  42.8 2.4 %collective-permute-done.7 = bf16[32,1024]{1,0:T(8,128)(2,1)S(1)} collective-permute-done((bf16[32,1024]{1,0:T(8,128)(2,1)S(1)}, bf16[32,1024]{1,0:T(8,128)(2,1)S(1)}, u32[]{:S(2)}, u32[]{:S(2)}) %collective-permute-start.7) | collective-permute-done | bytes 65568 | tf_op jit(solution)/shard_map/ppermute | solution.py:40
  45.2 1.9 collective-permute-start.14
  47.1 1.5 collective-permute-start.11
  48.6 6.5 %collective-permute-done.11.refs_2_ = bf16[4,32,1024]{2,1,0:T(8,128)(2,1)S(1)} collective-permute-done((bf16[4,32,1024]{2,1,0:T(8,128)(2,1)S(1)}, bf16[4,32,1024]{2,1,0:T(8,128)(2,1)S(1)}, u32[]{:S(2)}, u32[]{:S(2)}) %collective-permute-start.11) | collective-permute-done | bytes 262176 | tf_op jit(solution)/shard_map/ppermute | solution.py:44
  55.6 1.5 collective-permute-start.18
  57.2 1.8 shard_map.212
  59.0 3.3 %collective-permute-done.14.refs_6_ = bf16[768,384]{1,0:T(8,128)(2,1)S(1)} collective-permute-done((bf16[768,384]{1,0:T(8,128)(2,1)S(1)}, bf16[768,384]{1,0:T(8,128)(2,1)S(1)}, u32[]{:S(2)}, u32[]{:S(2)}) %collective-permute-start.14) | collective-permute-done | bytes 589856 | tf_op jit(solution)/shard_map/ppermute | solution.py:40
  62.2 1.6 collective-permute-start.16
  64.3 1.5 collective-permute-start.21
  65.8 3.2 %collective-permute-done.15 = bf16[128,768]{1,0:T(8,128)(2,1)S(1)} collective-permute-done((bf16[128,768]{1,0:T(8,128)(2,1)S(1)}, bf16[128,768]{1,0:T(8,128)(2,1)S(1)}, u32[]{:S(2)}, u32[]{:S(2)}) %collective-permute-start.15) | collective-permute-done | bytes 196640 | tf_op jit(solution)/shard_map/ppermute | solution.py:40
  68.9 1.5 collective-permute-start.20
  70.4 10.0 %collective-permute-done.16 = bf16[128,768]{1,0:T(8,128)(2,1)S(1)} collective-permute-done((bf16[128,768]{1,0:T(8,128)(2,1)S(1)}, bf16[128,768]{1,0:T(8,128)(2,1)S(1)}, u32[]{:S(2)}, u32[]{:S(2)}) %collective-permute-start.16) | collective-permute-done | bytes 196640 | tf_op jit(solution)/shard_map/ppermute | solution.py:40
  80.6 1.5 collective-permute-start.19
  82.2 2.8 %collective-permute-start.26 = (bf16[128,768]{1,0:T(8,128)(2,1)S(1)}, bf16[128,768]{1,0:T(8,128)(2,1)S(1)}, u32[]{:S(2)}, u32[]{:S(2)}) collective-permute-start(bf16[128,768]{1,0:T(8,128)(2,1)S(1)} %add_convert_fusion.4.refs_0_), channel_id=1, source_target_pairs={{0,6},{1,7},{2,0},{3,1},{4,2},{5,3},{6,4},{7,5},{8,14},{9,15},{10,... | collective-permute-start | bytes 589832 | tf_op jit(solution)/shard_map/ppermute | solution.py:40
  85.0 1.5 collective-permute-start.22
  86.5 3.8 %collective-permute-done.23.refs_2_ = bf16[128,768]{1,0:T(8,128)(2,1)S(1)} collective-permute-done((bf16[128,768]{1,0:T(8,128)(2,1)S(1)}, bf16[128,768]{1,0:T(8,128)(2,1)S(1)}, u32[]{:S(2)}, u32[]{:S(2)}) %collective-permute-start.23) | collective-permute-done | bytes 196640 | tf_op jit(solution)/shard_map/ppermute | solution.py:40
  90.3 1.5 collective-permute-start.24
  91.8 4.2 %collective-permute-done.19.refs_4_ = bf16[128,768]{1,0:T(8,128)(2,1)S(1)} collective-permute-done((bf16[128,768]{1,0:T(8,128)(2,1)S(1)}, bf16[128,768]{1,0:T(8,128)(2,1)S(1)}, u32[]{:S(2)}, u32[]{:S(2)}) %collective-permute-start.19) | collective-permute-done | bytes 196640 | tf_op jit(solution)/shard_map/ppermute | solution.py:40
  96.0 1.5 collective-permute-start.25
  98.2 6.5 %collective-permute-start.30 = (bf16[2,2,64,384]{3,2,1,0:T(8,128)(2,1)S(1)}, bf16[2,2,64,384]{3,2,1,0:T(8,128)(2,1)S(1)}, u32[]{:S(2)}, u32[]{:S(2)}) collective-permute-start(bf16[2,2,64,384]{3,2,1,0:T(8,128)(2,1)S(1)} %get-tuple-element.128), channel_id=1, source_target_pairs={{0,6},{1,7},{2,0},{3,1},{4,2},{5,3},{6,4},{7,5},{8,14},{9,15},{10,... | collective-permute-start | bytes 589832 | tf_op jit(solution)/shard_map/ppermute | solution.py:40
  105.3 2.8 %shard_map.213 = (bf16[256,384]{1,0:T(8,128)(2,1)S(1)}, bf16[256,384]{1,0:T(8,128)(2,1)S(1)}, f32[1,384]{1,0:T(1,128)S(1)}) custom-call(s32[3]{0:T(128)S(1)} %copy-done.31, bf16[256,3072]{1,0:T(8,128)(2,1)S(1)} %get-tuple-element.99.normed_ref, bf16[256,3072]{1,0:T(8,128)(2,1)S(1)} %copy-done, bf16[384,384]{1,0:T(8,128)(2,1)S(1)} %copy-done.5, ...), custom_call_target="tpu_custom_call" | custom-call | flops 1 | bytes 1 | tf_op jit(solution)/shard_map/pallas_call | solution.py:307
  108.8 2.8 %shard_map.214 = (bf16[2,256,384]{2,1,0:T(8,128)(2,1)S(1)}, bf16[256,384]{1,0:T(8,128)(2,1)S(1)}, bf16[256,384]{1,0:T(8,128)(2,1)S(1)}, f32[256,2]{1,0:T(8,128)S(1)}, bf16[3,128,768]{2,1,0:T(8,128)(2,1)S(1)}) custom-call(s32[3]{0:T(128)S(1)} %copy-done.31, s32[8]{0:T(128)S(1)} %copy-done.33, s32[8]{0:T(128)S(1)} %copy-done.34, s32[8]{0:T(128)S(1)} %copy-done.35, ...), custom_call_target="tpu_custom_call" | custom-call | flops 1 | bytes 1 | tf_op jit(solution)/shard_map/pallas_call | solution.py:307
  111.7 1.3 collective-permute-done.31
  113.0 8.0 %collective-permute-done.29 = bf16[2,2,64,384]{3,2,1,0:T(8,128)(2,1)S(1)} collective-permute-done((bf16[2,2,64,384]{3,2,1,0:T(8,128)(2,1)S(1)}, bf16[2,2,64,384]{3,2,1,0:T(8,128)(2,1)S(1)}, u32[]{:S(2)}, u32[]{:S(2)}) %collective-permute-start.29) | collective-permute-done | bytes 196640 | tf_op jit(solution)/shard_map/ppermute | solution.py:40
  121.2 1.6 collective-permute-start.36
  122.7 1.4 collective-permute-start.32
  124.7 9.4 %collective-permute-done.34.refs_5_ = bf16[2,256,384]{2,1,0:T(8,128)(2,1)S(1)} collective-permute-done((bf16[2,256,384]{2,1,0:T(8,128)(2,1)S(1)}, bf16[2,256,384]{2,1,0:T(8,128)(2,1)S(1)}, u32[]{:S(2)}, u32[]{:S(2)}) %collective-permute-start.34) | collective-permute-done | bytes 393248 | tf_op jit(solution)/shard_map/ppermute | solution.py:40
  134.1 4.4 %shard_map.215 = (bf16[2,256,768]{2,1,0:T(8,128)(2,1)S(1)}, bf16[2,256,768]{2,1,0:T(8,128)(2,1)S(1)}, bf16[2,256,1536]{2,1,0:T(8,128)(2,1)S(1)}) custom-call(s32[3]{0:T(128)S(1)} %copy-done.31, bf16[256,384]{1,0:T(8,128)(2,1)S(1)} %get-tuple-element.134.att_ref, bf16[256,384]{1,0:T(8,128)(2,1)S(1)} %get-tuple-element.135.dq_ref, ...), custom_call_target="tpu_custom_call" | custom-call | flops 1 | bytes 1 | tf_op jit(solution)/shard_map/pallas_call | solution.py:307
  138.5 8.4 %collective-permute-done.33.refs_8_ = bf16[2,256,384]{2,1,0:T(8,128)(2,1)S(1)} collective-permute-done((bf16[2,256,384]{2,1,0:T(8,128)(2,1)S(1)}, bf16[2,256,384]{2,1,0:T(8,128)(2,1)S(1)}, u32[]{:S(2)}, u32[]{:S(2)}) %collective-permute-start.33) | collective-permute-done | bytes 393248 | tf_op jit(solution)/shard_map/ppermute | solution.py:40
  147.0 1.5 collective-permute-start.40
  148.5 2.5 %collective-permute-start.41 = (bf16[2,256,384]{2,1,0:T(8,128)(2,1)S(1)}, bf16[2,256,384]{2,1,0:T(8,128)(2,1)S(1)}, u32[]{:S(2)}, u32[]{:S(2)}) collective-permute-start(bf16[2,256,384]{2,1,0:T(8,128)(2,1)S(1)} %collective-permute-done.35.refs_6_), channel_id=1, source_target_pairs={{0,2},{1,3},{2,4},{3,5},{4,6},{5,7},{6,0},{7,1},{8,10},{9,11},{10,... | collective-permute-start | bytes 1179656 | tf_op jit(solution)/shard_map/ppermute | solution.py:40
  152.1 1.1 fusion.9
  153.2 3.1 %collective-permute-done.43 = f32[256,2]{1,0:T(8,128)S(1)} collective-permute-done((f32[256,2]{1,0:T(8,128)S(1)}, f32[256,2]{1,0:T(8,128)S(1)}, u32[]{:S(2)}, u32[]{:S(2)}) %collective-permute-start.43) | collective-permute-done | bytes 2080 | tf_op jit(solution)/shard_map/ppermute | solution.py:44
  157.5 1.1 shard_map.216
  160.3 6.7 %collective-permute-done.39.refs_9_ = bf16[2,256,384]{2,1,0:T(8,128)(2,1)S(1)} collective-permute-done((bf16[2,256,384]{2,1,0:T(8,128)(2,1)S(1)}, bf16[2,256,384]{2,1,0:T(8,128)(2,1)S(1)}, u32[]{:S(2)}, u32[]{:S(2)}) %collective-permute-start.39) | collective-permute-done | bytes 393248 | tf_op jit(solution)/shard_map/ppermute | solution.py:40
  170.0 1.0 reduce
  171.0 1.0 reduce.2
  172.0 1.0 add_multiply_fusion
  173.0 1.5 collective-permute-start.47
  174.7 2.0 %collective-permute-start.48 = (bf16[128,768]{1,0:T(8,128)(2,1)}, bf16[128,768]{1,0:T(8,128)(2,1)S(1)}, u32[]{:S(2)}, u32[]{:S(2)}) collective-permute-start(bf16[128,768]{1,0:T(8,128)(2,1)} %copy-done.37), channel_id=1, source_target_pairs={{0,4},{1,5},{2,6},{3,7},{4,0},{5,1},{6,2},{7,3},{8,12},{9,13},{10,... | collective-permute-start | bytes 589832 | tf_op jit(solution)/shard_map/ppermute | solution.py:40
  176.7 2.9 %collective-permute-start.49 = (bf16[128,768]{1,0:T(8,128)(2,1)}, bf16[128,768]{1,0:T(8,128)(2,1)S(1)}, u32[]{:S(2)}, u32[]{:S(2)}) collective-permute-start(bf16[128,768]{1,0:T(8,128)(2,1)} %copy-done.36), channel_id=1, source_target_pairs={{0,6},{1,7},{2,0},{3,1},{4,2},{5,3},{6,4},{7,5},{8,14},{9,15},{10,... | collective-permute-start | bytes 589832 | tf_op jit(solution)/shard_map/ppermute | solution.py:40
  179.6 1.1 copy-done.3
  180.8 1.0 copy-done.14
  181.8 1.0 copy-done.16
  182.8 1.0 copy-done.18
  183.8 1.0 copy-done.20
  184.7 1.0 copy-done.22
  185.7 1.0 copy-done.24
  186.7 2.9 %shard_map.217 = (f32[384,384]{1,0:T(8,128)S(1)}, f32[384,384]{1,0:T(8,128)S(1)}) custom-call(bf16[4,2,2,64,384]{4,3,2,1,0:T(8,128)(2,1)S(1)} %pad_maximum_fusion.1.refs_0_, bf16[4,2,2,64,384]{4,3,2,1,0:T(8,128)(2,1)S(1)} %copy-done.3, bf16[4,2,2,64,384]{4,3,2,1,0:T(8,128)(2,1)S(1)} %collective-permute-done.36.refs_2_, ...), custom_call_target="tpu_custom_call" | custom-call | flops 1 | bytes 1 | tf_op jit(solution)/shard_map/pallas_call | solution.py:307
  189.7 2.5 %fusion.6 = (bf16[256,768]{1,0:T(8,128)(2,1)}, bf16[256,768]{1,0:T(8,128)(2,1)}) fusion(bf16[256,768]{1,0:T(8,128)(2,1)} %collective-permute-done.45, bf16[2,256,1536]{2,1,0:T(8,128)(2,1)S(1)} %copy-done.39, f32[256]{0:T(256)S(1)} %get-tuple-element.183, f32[256]{0:T(256)S(1)} %reduce.2, f32[256]{0:T(256)S(1)} %get-tuple-element.182, ...), kind=kLoop, calls=%fused_computation.15 | loop fusion | flops 4325376 | bytes 3936260 | tf_op jit(solution)/shard_map/convert_element_type | solution.py:871
  192.3 2.5 %shard_map.218 = (f32[384,384]{1,0:T(8,128)}, f32[384,384]{1,0:T(8,128)}) custom-call(bf16[4,2,2,64,384]{4,3,2,1,0:T(8,128)(2,1)S(1)} %pad_maximum_fusion.1.refs_0_, bf16[4,2,2,64,384]{4,3,2,1,0:T(8,128)(2,1)S(1)} %copy-done.4, bf16[4,2,2,64,384]{4,3,2,1,0:T(8,128)(2,1)S(1)} %collective-permute-done.36.refs_2_, ...), custom_call_target="tpu_custom_call" | custom-call | flops 1 | bytes 1 | tf_op jit(solution)/shard_map/pallas_call | solution.py:307
  (157 shorter events, 15.4 us)
Async XLA Ops:
  0.6 22.4 %collective-permute-start.2 = (bf16[512,384]{1,0:T(8,128)(2,1)}, bf16[512,384]{1,0:T(8,128)(2,1)S(1)}, u32[]{:S(2)}, u32[]{:S(2)}) collective-permute-start(bf16[512,384]{1,0:T(8,128)(2,1)} %refs_4_.1), channel_id=1, source_target_pairs={{0,1},{1,0},{2,3},{3,2},{4,5},{5,4},{6,7},{7,6},{8,9},{9,8},{10,11... | collective-permute-start | bytes 1179656 | tf_op jit(solution)/shard_map/ppermute | solution.py:40
  3.7 19.3 %collective-permute-start.3 = (bf16[512,384]{1,0:T(8,128)(2,1)}, bf16[512,384]{1,0:T(8,128)(2,1)S(1)}, u32[]{:S(2)}, u32[]{:S(2)}) collective-permute-start(bf16[512,384]{1,0:T(8,128)(2,1)} %refs_5_.1), channel_id=1, source_target_pairs={{0,1},{1,0},{2,3},{3,2},{4,5},{5,4},{6,7},{7,6},{8,9},{9,8},{10,11... | collective-permute-start | bytes 1179656 | tf_op jit(solution)/shard_map/ppermute | solution.py:40
  3.7 19.2 %collective-permute-start = (bf16[384,384]{1,0:T(8,128)(2,1)}, bf16[384,384]{1,0:T(8,128)(2,1)S(1)}, u32[]{:S(2)}, u32[]{:S(2)}) collective-permute-start(bf16[384,384]{1,0:T(8,128)(2,1)} %refs_0_.3), channel_id=1, source_target_pairs={{0,2},{1,3},{2,4},{3,5},{4,6},{5,7},{6,0},{7,1},{8,10},{9,11},{10,... | collective-permute-start | bytes 884744 | tf_op jit(solution)/shard_map/ppermute | solution.py:40
  5.7 17.2 %collective-permute-start.1 = (bf16[384,384]{1,0:T(8,128)(2,1)}, bf16[384,384]{1,0:T(8,128)(2,1)S(1)}, u32[]{:S(2)}, u32[]{:S(2)}) collective-permute-start(bf16[384,384]{1,0:T(8,128)(2,1)} %refs_1_.3), channel_id=1, source_target_pairs={{0,2},{1,3},{2,4},{3,5},{4,6},{5,7},{6,0},{7,1},{8,10},{9,11},{10,... | collective-permute-start | bytes 884744 | tf_op jit(solution)/shard_map/ppermute | solution.py:40
  15.8 9.0 %copy-start.5 = (bf16[384,384]{1,0:T(8,128)(2,1)S(1)}, bf16[384,384]{1,0:T(8,128)(2,1)}, u32[]{:S(2)}) copy-start(bf16[384,384]{1,0:T(8,128)(2,1)} %refs_0_.3) | copy-start | bytes 884740
  15.8 9.0 %copy-start.6 = (bf16[384,384]{1,0:T(8,128)(2,1)S(1)}, bf16[384,384]{1,0:T(8,128)(2,1)}, u32[]{:S(2)}) copy-start(bf16[384,384]{1,0:T(8,128)(2,1)} %refs_1_.3) | copy-start | bytes 884740
  23.0 3.6 %collective-permute-start.4 = (bf16[64,4096]{1,0:T(8,128)(2,1)}, bf16[64,4096]{1,0:T(8,128)(2,1)S(1)}, u32[]{:S(2)}, u32[]{:S(2)}) collective-permute-start(bf16[64,4096]{1,0:T(8,128)(2,1)} %get-tuple-element.97), channel_id=1, source_target_pairs={{0,8},{8,0},{16,24},{24,16},{1,9},{9,1},{17,25},{25,17},{2,10},{10... | collective-permute-start | bytes 1572872 | tf_op jit(solution)/shard_map/ppermute | solution.py:44
  23.2 22.0 %collective-permute-start.9 = (bf16[768,384]{1,0:T(8,128)(2,1)S(1)}, bf16[768,384]{1,0:T(8,128)(2,1)S(1)}, u32[]{:S(2)}, u32[]{:S(2)}) collective-permute-start(bf16[768,384]{1,0:T(8,128)(2,1)S(1)} %constant_dynamic-update-slice_fusion.refs_3_), channel_id=1, source_target_pairs={{0,2},{1,3},{2,4},{3,5},{4,6},{5,7},{6,0},{7,1},{8,10},{9,11},{10,... | collective-permute-start | bytes 1769480 | tf_op jit(solution)/shard_map/ppermute | solution.py:40
  25.0 32.1 %collective-permute-start.13 = (bf16[1536,384]{1,0:T(8,128)(2,1)S(1)}, bf16[1536,384]{1,0:T(8,128)(2,1)S(1)}, u32[]{:S(2)}, u32[]{:S(2)}) collective-permute-start(bf16[1536,384]{1,0:T(8,128)(2,1)S(1)} %pad_maximum_fusion), channel_id=1, source_target_pairs={{0,1},{1,0},{2,3},{3,2},{4,5},{5,4},{6,7},{7,6},{8,9},{9,8},{10,11... | collective-permute-start | bytes 3538952 | tf_op jit(solution)/shard_map/ppermute | solution.py:40
  26.7 8.2 %collective-permute-start.5 = (bf16[32,4096]{1,0:T(8,128)(2,1)S(1)}, bf16[32,4096]{1,0:T(8,128)(2,1)S(1)}, u32[]{:S(2)}, u32[]{:S(2)}) collective-permute-start(bf16[32,4096]{1,0:T(8,128)(2,1)S(1)} %add_convert_fusion.2), channel_id=1, source_target_pairs={{0,16},{8,24},{16,0},{24,8},{1,17},{9,25},{17,1},{25,9},{2,18},{10... | collective-permute-start | bytes 786440 | tf_op jit(solution)/shard_map/ppermute | solution.py:44
  32.3 24.8 %copy-start.27 = (bf16[512,384]{1,0:T(8,128)(2,1)S(1)}, bf16[512,384]{1,0:T(8,128)(2,1)}, u32[]{:S(2)}) copy-start(bf16[512,384]{1,0:T(8,128)(2,1)} %refs_4_.1) | copy-start | bytes 1179652
  32.3 24.9 %copy-start.28 = (bf16[512,384]{1,0:T(8,128)(2,1)S(1)}, bf16[512,384]{1,0:T(8,128)(2,1)}, u32[]{:S(2)}) copy-start(bf16[512,384]{1,0:T(8,128)(2,1)} %refs_5_.1) | copy-start | bytes 1179652
  35.7 7.0 %collective-permute-start.6 = (bf16[32,1024]{1,0:T(8,128)(2,1)S(1)}, bf16[32,1024]{1,0:T(8,128)(2,1)S(1)}, u32[]{:S(2)}, u32[]{:S(2)}) collective-permute-start(bf16[32,1024]{1,0:T(8,128)(2,1)S(1)} %get-tuple-element.102), channel_id=1, source_target_pairs={{0,2},{1,3},{2,4},{3,5},{4,6},{5,7},{6,0},{7,1},{8,10},{9,11},{10,... | collective-permute-start | bytes 196616 | tf_op jit(solution)/shard_map/ppermute | solution.py:40
  36.2 9.0 %collective-permute-start.7 = (bf16[32,1024]{1,0:T(8,128)(2,1)S(1)}, bf16[32,1024]{1,0:T(8,128)(2,1)S(1)}, u32[]{:S(2)}, u32[]{:S(2)}) collective-permute-start(bf16[32,1024]{1,0:T(8,128)(2,1)S(1)} %get-tuple-element.103), channel_id=1, source_target_pairs={{0,4},{1,5},{2,6},{3,7},{4,0},{5,1},{6,2},{7,3},{8,12},{9,13},{10,... | collective-permute-start | bytes 196616 | tf_op jit(solution)/shard_map/ppermute | solution.py:40
  38.6 6.6 %collective-permute-start.8 = (bf16[32,1024]{1,0:T(8,128)(2,1)S(1)}, bf16[32,1024]{1,0:T(8,128)(2,1)S(1)}, u32[]{:S(2)}, u32[]{:S(2)}) collective-permute-start(bf16[32,1024]{1,0:T(8,128)(2,1)S(1)} %get-tuple-element.104), channel_id=1, source_target_pairs={{0,6},{1,7},{2,0},{3,1},{4,2},{5,3},{6,4},{7,5},{8,14},{9,15},{10,... | collective-permute-start | bytes 196616 | tf_op jit(solution)/shard_map/ppermute | solution.py:40
  45.2 17.0 %collective-permute-start.14 = (bf16[768,384]{1,0:T(8,128)(2,1)S(1)}, bf16[768,384]{1,0:T(8,128)(2,1)S(1)}, u32[]{:S(2)}, u32[]{:S(2)}) collective-permute-start(bf16[768,384]{1,0:T(8,128)(2,1)S(1)} %collective-permute-done.9.refs_4_), channel_id=1, source_target_pairs={{0,2},{1,3},{2,4},{3,5},{4,6},{5,7},{6,0},{7,1},{8,10},{9,11},{10,... | collective-permute-start | bytes 1769480 | tf_op jit(solution)/shard_map/ppermute | solution.py:40
  47.1 7.9 %collective-permute-start.11 = (bf16[4,32,1024]{2,1,0:T(8,128)(2,1)S(1)}, bf16[4,32,1024]{2,1,0:T(8,128)(2,1)S(1)}, u32[]{:S(2)}, u32[]{:S(2)}) collective-permute-start(bf16[4,32,1024]{2,1,0:T(8,128)(2,1)S(1)} %pad_maximum_fusion.2.refs_0_), channel_id=1, source_target_pairs={{0,16},{8,24},{16,0},{24,8},{1,17},{9,25},{17,1},{25,9},{2,18},{10... | collective-permute-start | bytes 786440 | tf_op jit(solution)/shard_map/ppermute | solution.py:44
  55.1 2.0 %collective-permute-start.12 = (bf16[4,32,1024]{2,1,0:T(8,128)(2,1)S(1)}, bf16[4,32,1024]{2,1,0:T(8,128)(2,1)S(1)}, u32[]{:S(2)}, u32[]{:S(2)}) collective-permute-start(bf16[4,32,1024]{2,1,0:T(8,128)(2,1)S(1)} %collective-permute-done.11.refs_2_), channel_id=1, source_target_pairs={{0,8},{8,0},{16,24},{24,16},{1,9},{9,1},{17,25},{25,17},{2,10},{10... | collective-permute-start | bytes 786440 | tf_op jit(solution)/shard_map/ppermute | solution.py:44
  55.1 2.0 %collective-permute-start.10 = (bf16[4,32,1024]{2,1,0:T(8,128)(2,1)S(1)}, bf16[4,32,1024]{2,1,0:T(8,128)(2,1)S(1)}, u32[]{:S(2)}, u32[]{:S(2)}) collective-permute-start(bf16[4,32,1024]{2,1,0:T(8,128)(2,1)S(1)} %pad_maximum_fusion.2.refs_0_), channel_id=1, source_target_pairs={{0,8},{8,0},{16,24},{24,16},{1,9},{9,1},{17,25},{25,17},{2,10},{10... | collective-permute-start | bytes 786440 | tf_op jit(solution)/shard_map/ppermute | solution.py:44
  55.6 25.0 %collective-permute-start.18 = (bf16[768,384]{1,0:T(8,128)(2,1)S(1)}, bf16[768,384]{1,0:T(8,128)(2,1)S(1)}, u32[]{:S(2)}, u32[]{:S(2)}) collective-permute-start(bf16[768,384]{1,0:T(8,128)(2,1)S(1)} %collective-permute-done.9.refs_4_), channel_id=1, source_target_pairs={{0,1},{1,0},{2,3},{3,2},{4,5},{5,4},{6,7},{7,6},{8,9},{9,8},{10,11... | collective-permute-start | bytes 1769480 | tf_op jit(solution)/shard_map/ppermute | solution.py:40
  62.2 6.7 %collective-permute-start.15 = (bf16[128,768]{1,0:T(8,128)(2,1)S(1)}, bf16[128,768]{1,0:T(8,128)(2,1)S(1)}, u32[]{:S(2)}, u32[]{:S(2)}) collective-permute-start(bf16[128,768]{1,0:T(8,128)(2,1)S(1)} %get-tuple-element.113), channel_id=1, source_target_pairs={{0,6},{1,7},{2,0},{3,1},{4,2},{5,3},{6,4},{7,5},{8,14},{9,15},{10,... | collective-permute-start | bytes 589832 | tf_op jit(solution)/shard_map/ppermute | solution.py:40
  62.2 18.2 %collective-permute-start.16 = (bf16[128,768]{1,0:T(8,128)(2,1)S(1)}, bf16[128,768]{1,0:T(8,128)(2,1)S(1)}, u32[]{:S(2)}, u32[]{:S(2)}) collective-permute-start(bf16[128,768]{1,0:T(8,128)(2,1)S(1)} %get-tuple-element.114), channel_id=1, source_target_pairs={{0,4},{1,5},{2,6},{3,7},{4,0},{5,1},{6,2},{7,3},{8,12},{9,13},{10,... | collective-permute-start | bytes 589832 | tf_op jit(solution)/shard_map/ppermute | solution.py:40
  63.9 16.6 %collective-permute-start.17 = (bf16[128,768]{1,0:T(8,128)(2,1)S(1)}, bf16[128,768]{1,0:T(8,128)(2,1)S(1)}, u32[]{:S(2)}, u32[]{:S(2)}) collective-permute-start(bf16[128,768]{1,0:T(8,128)(2,1)S(1)} %get-tuple-element.115), channel_id=1, source_target_pairs={{0,2},{1,3},{2,4},{3,5},{4,6},{5,7},{6,0},{7,1},{8,10},{9,11},{10,... | collective-permute-start | bytes 589832 | tf_op jit(solution)/shard_map/ppermute | solution.py:40
  64.3 20.8 %collective-permute-start.21 = (bf16[4,2,64,384]{3,2,1,0:T(8,128)(2,1)S(1)}, bf16[4,2,64,384]{3,2,1,0:T(8,128)(2,1)S(1)}, u32[]{:S(2)}, u32[]{:S(2)}) collective-permute-start(bf16[4,2,64,384]{3,2,1,0:T(8,128)(2,1)S(1)} %get-tuple-element.117), channel_id=1, source_target_pairs={{0,1},{1,0},{2,3},{3,2},{4,5},{5,4},{6,7},{7,6},{8,9},{9,8},{10,11... | collective-permute-start | bytes 1179656 | tf_op jit(solution)/shard_map/ppermute | solution.py:40
  68.9 29.2 %collective-permute-start.20 = (bf16[768,384]{1,0:T(8,128)(2,1)S(1)}, bf16[768,384]{1,0:T(8,128)(2,1)S(1)}, u32[]{:S(2)}, u32[]{:S(2)}) collective-permute-start(bf16[768,384]{1,0:T(8,128)(2,1)S(1)} %collective-permute-done.14.refs_6_), channel_id=1, source_target_pairs={{0,1},{1,0},{2,3},{3,2},{4,5},{5,4},{6,7},{7,6},{8,9},{9,8},{10,11... | collective-permute-start | bytes 1769480 | tf_op jit(solution)/shard_map/ppermute | solution.py:40
  80.6 9.7 %collective-permute-start.23 = (bf16[128,768]{1,0:T(8,128)(2,1)S(1)}, bf16[128,768]{1,0:T(8,128)(2,1)S(1)}, u32[]{:S(2)}, u32[]{:S(2)}) collective-permute-start(bf16[128,768]{1,0:T(8,128)(2,1)S(1)} %add_convert_fusion.4.refs_0_), channel_id=1, source_target_pairs={{0,2},{1,3},{2,4},{3,5},{4,6},{5,7},{6,0},{7,1},{8,10},{9,11},{10,... | collective-permute-start | bytes 589832 | tf_op jit(solution)/shard_map/ppermute | solution.py:40
  80.6 15.4 %collective-permute-start.19 = (bf16[128,768]{1,0:T(8,128)(2,1)S(1)}, bf16[128,768]{1,0:T(8,128)(2,1)S(1)}, u32[]{:S(2)}, u32[]{:S(2)}) collective-permute-start(bf16[128,768]{1,0:T(8,128)(2,1)S(1)} %add_convert_fusion.4.refs_0_), channel_id=1, source_target_pairs={{0,4},{1,5},{2,6},{3,7},{4,0},{5,1},{6,2},{7,3},{8,12},{9,13},{10,... | collective-permute-start | bytes 589832 | tf_op jit(solution)/shard_map/ppermute | solution.py:40
  82.2 15.4 %collective-permute-start.26 = (bf16[128,768]{1,0:T(8,128)(2,1)S(1)}, bf16[128,768]{1,0:T(8,128)(2,1)S(1)}, u32[]{:S(2)}, u32[]{:S(2)}) collective-permute-start(bf16[128,768]{1,0:T(8,128)(2,1)S(1)} %add_convert_fusion.4.refs_0_), channel_id=1, source_target_pairs={{0,6},{1,7},{2,0},{3,1},{4,2},{5,3},{6,4},{7,5},{8,14},{9,15},{10,... | collective-permute-start | bytes 589832 | tf_op jit(solution)/shard_map/ppermute | solution.py:40
  85.0 19.6 %collective-permute-start.22 = (bf16[128,768]{1,0:T(8,128)(2,1)S(1)}, bf16[128,768]{1,0:T(8,128)(2,1)S(1)}, u32[]{:S(2)}, u32[]{:S(2)}) collective-permute-start(bf16[128,768]{1,0:T(8,128)(2,1)S(1)} %add_convert_fusion.4.refs_0_), channel_id=1, source_target_pairs={{0,1},{1,0},{2,3},{3,2},{4,5},{5,4},{6,7},{7,6},{8,9},{9,8},{10,11... | collective-permute-start | bytes 589832 | tf_op jit(solution)/shard_map/ppermute | solution.py:40
  90.3 14.4 %collective-permute-start.24 = (bf16[128,768]{1,0:T(8,128)(2,1)S(1)}, bf16[128,768]{1,0:T(8,128)(2,1)S(1)}, u32[]{:S(2)}, u32[]{:S(2)}) collective-permute-start(bf16[128,768]{1,0:T(8,128)(2,1)S(1)} %collective-permute-done.23.refs_2_), channel_id=1, source_target_pairs={{0,1},{1,0},{2,3},{3,2},{4,5},{5,4},{6,7},{7,6},{8,9},{9,8},{10,11... | collective-permute-start | bytes 589832 | tf_op jit(solution)/shard_map/ppermute | solution.py:40
  96.0 12.1 %collective-permute-start.25 = (bf16[128,768]{1,0:T(8,128)(2,1)S(1)}, bf16[128,768]{1,0:T(8,128)(2,1)S(1)}, u32[]{:S(2)}, u32[]{:S(2)}) collective-permute-start(bf16[128,768]{1,0:T(8,128)(2,1)S(1)} %collective-permute-done.19.refs_4_), channel_id=1, source_target_pairs={{0,1},{1,0},{2,3},{3,2},{4,5},{5,4},{6,7},{7,6},{8,9},{9,8},{10,11... | collective-permute-start | bytes 589832 | tf_op jit(solution)/shard_map/ppermute | solution.py:40
  97.6 11.2 %collective-permute-start.27 = (bf16[128,768]{1,0:T(8,128)(2,1)S(1)}, bf16[128,768]{1,0:T(8,128)(2,1)S(1)}, u32[]{:S(2)}, u32[]{:S(2)}) collective-permute-start(bf16[128,768]{1,0:T(8,128)(2,1)S(1)} %collective-permute-done.26.refs_6_), channel_id=1, source_target_pairs={{0,1},{1,0},{2,3},{3,2},{4,5},{5,4},{6,7},{7,6},{8,9},{9,8},{10,11... | collective-permute-start | bytes 589832 | tf_op jit(solution)/shard_map/ppermute | solution.py:40
  98.2 14.9 %collective-permute-start.30 = (bf16[2,2,64,384]{3,2,1,0:T(8,128)(2,1)S(1)}, bf16[2,2,64,384]{3,2,1,0:T(8,128)(2,1)S(1)}, u32[]{:S(2)}, u32[]{:S(2)}) collective-permute-start(bf16[2,2,64,384]{3,2,1,0:T(8,128)(2,1)S(1)} %get-tuple-element.128), channel_id=1, source_target_pairs={{0,6},{1,7},{2,0},{3,1},{4,2},{5,3},{6,4},{7,5},{8,14},{9,15},{10,... | collective-permute-start | bytes 589832 | tf_op jit(solution)/shard_map/ppermute | solution.py:40
  104.7 16.4 %collective-permute-start.29 = (bf16[2,2,64,384]{3,2,1,0:T(8,128)(2,1)S(1)}, bf16[2,2,64,384]{3,2,1,0:T(8,128)(2,1)S(1)}, u32[]{:S(2)}, u32[]{:S(2)}) collective-permute-start(bf16[2,2,64,384]{3,2,1,0:T(8,128)(2,1)S(1)} %get-tuple-element.127), channel_id=1, source_target_pairs={{0,4},{1,5},{2,6},{3,7},{4,0},{5,1},{6,2},{7,3},{8,12},{9,13},{10,... | collective-permute-start | bytes 589832 | tf_op jit(solution)/shard_map/ppermute | solution.py:40
  104.7 16.3 %collective-permute-start.28 = (bf16[2,2,64,384]{3,2,1,0:T(8,128)(2,1)S(1)}, bf16[2,2,64,384]{3,2,1,0:T(8,128)(2,1)S(1)}, u32[]{:S(2)}, u32[]{:S(2)}) collective-permute-start(bf16[2,2,64,384]{3,2,1,0:T(8,128)(2,1)S(1)} %get-tuple-element.126), channel_id=1, source_target_pairs={{0,2},{1,3},{2,4},{3,5},{4,6},{5,7},{6,0},{7,1},{8,10},{9,11},{10,... | collective-permute-start | bytes 589832 | tf_op jit(solution)/shard_map/ppermute | solution.py:40
  111.6 26.9 %copy-start.11 = (bf16[2,256,384]{2,1,0:T(8,128)(2,1)}, bf16[2,256,384]{2,1,0:T(8,128)(2,1)S(1)}, u32[]{:S(2)}) copy-start(bf16[2,256,384]{2,1,0:T(8,128)(2,1)S(1)} %get-tuple-element.160.refs_4_) | copy-start | bytes 1179652
  111.6 1.4 collective-permute-start.31
  113.0 38.0 %copy-start.40 = (f32[256,2]{1,0:T(8,128)}, f32[256,2]{1,0:T(8,128)S(1)}, u32[]{:S(2)}) copy-start(f32[256,2]{1,0:T(8,128)S(1)} %add.74) | copy-start | bytes 6148
  121.2 25.7 %collective-permute-start.36 = (bf16[4,2,2,64,384]{4,3,2,1,0:T(8,128)(2,1)S(1)}, bf16[4,2,2,64,384]{4,3,2,1,0:T(8,128)(2,1)S(1)}, u32[]{:S(2)}, u32[]{:S(2)}) collective-permute-start(bf16[4,2,2,64,384]{4,3,2,1,0:T(8,128)(2,1)S(1)} %pad_maximum_fusion.1.refs_0_), channel_id=1, source_target_pairs={{0,16},{8,24},{16,0},{24,8},{1,17},{9,25},{17,1},{25,9},{2,18},{10... | collective-permute-start | bytes 2359304 | tf_op jit(solution)/shard_map/ppermute | solution.py:44
  122.7 11.4 %collective-permute-start.34 = (bf16[2,256,384]{2,1,0:T(8,128)(2,1)S(1)}, bf16[2,256,384]{2,1,0:T(8,128)(2,1)S(1)}, u32[]{:S(2)}, u32[]{:S(2)}) collective-permute-start(bf16[2,256,384]{2,1,0:T(8,128)(2,1)S(1)} %get-tuple-element.160.refs_4_), channel_id=1, source_target_pairs={{0,2},{1,3},{2,4},{3,5},{4,6},{5,7},{6,0},{7,1},{8,10},{9,11},{10,... | collective-permute-start | bytes 1179656 | tf_op jit(solution)/shard_map/ppermute | solution.py:40
  122.7 24.2 %collective-permute-start.37 = (bf16[4,2,2,64,384]{4,3,2,1,0:T(8,128)(2,1)S(1)}, bf16[4,2,2,64,384]{4,3,2,1,0:T(8,128)(2,1)S(1)}, u32[]{:S(2)}, u32[]{:S(2)}) collective-permute-start(bf16[4,2,2,64,384]{4,3,2,1,0:T(8,128)(2,1)S(1)} %pad_maximum_fusion.1.refs_0_), channel_id=1, source_target_pairs={{0,8},{8,0},{16,24},{24,16},{1,9},{9,1},{17,25},{25,17},{2,10},{10... | collective-permute-start | bytes 2359304 | tf_op jit(solution)/shard_map/ppermute | solution.py:44
  122.7 24.2 %collective-permute-start.32 = (bf16[3,128,768]{2,1,0:T(8,128)(2,1)S(1)}, bf16[3,128,768]{2,1,0:T(8,128)(2,1)S(1)}, u32[]{:S(2)}, u32[]{:S(2)}) collective-permute-start(bf16[3,128,768]{2,1,0:T(8,128)(2,1)S(1)} %get-tuple-element.147.own_ref), channel_id=1, source_target_pairs={{0,1},{1,0},{2,3},{3,2},{4,5},{5,4},{6,7},{7,6},{8,9},{9,8},{10,11... | collective-permute-start | bytes 1769480 | tf_op jit(solution)/shard_map/ppermute | solution.py:40
  124.2 22.7 %collective-permute-start.33 = (bf16[2,256,384]{2,1,0:T(8,128)(2,1)S(1)}, bf16[2,256,384]{2,1,0:T(8,128)(2,1)S(1)}, u32[]{:S(2)}, u32[]{:S(2)}) collective-permute-start(bf16[2,256,384]{2,1,0:T(8,128)(2,1)S(1)} %get-tuple-element.160.refs_4_), channel_id=1, source_target_pairs={{0,1},{1,0},{2,3},{3,2},{4,5},{5,4},{6,7},{7,6},{8,9},{9,8},{10,11... | collective-permute-start | bytes 1179656 | tf_op jit(solution)/shard_map/ppermute | solution.py:40
  134.1 17.5 %copy-start.13 = (bf16[2,256,384]{2,1,0:T(8,128)(2,1)}, bf16[2,256,384]{2,1,0:T(8,128)(2,1)S(1)}, u32[]{:S(2)}) copy-start(bf16[2,256,384]{2,1,0:T(8,128)(2,1)S(1)} %collective-permute-done.34.refs_5_) | copy-start | bytes 1179652
  134.1 12.8 %collective-permute-start.35 = (bf16[2,256,384]{2,1,0:T(8,128)(2,1)S(1)}, bf16[2,256,384]{2,1,0:T(8,128)(2,1)S(1)}, u32[]{:S(2)}, u32[]{:S(2)}) collective-permute-start(bf16[2,256,384]{2,1,0:T(8,128)(2,1)S(1)} %collective-permute-done.34.refs_5_), channel_id=1, source_target_pairs={{0,2},{1,3},{2,4},{3,5},{4,6},{5,7},{6,0},{7,1},{8,10},{9,11},{10,... | collective-permute-start | bytes 1179656 | tf_op jit(solution)/shard_map/ppermute | solution.py:40
  138.5 20.1 %copy-start.9 = (bf16[2,256,768]{2,1,0:T(8,128)(2,1)}, bf16[2,256,768]{2,1,0:T(8,128)(2,1)S(1)}, u32[]{:S(2)}) copy-start(bf16[2,256,768]{2,1,0:T(8,128)(2,1)S(1)} %get-tuple-element.136) | copy-start | bytes 2359300
  146.9 11.7 %copy-start.15 = (bf16[2,256,384]{2,1,0:T(8,128)(2,1)}, bf16[2,256,384]{2,1,0:T(8,128)(2,1)S(1)}, u32[]{:S(2)}) copy-start(bf16[2,256,384]{2,1,0:T(8,128)(2,1)S(1)} %collective-permute-done.33.refs_8_) | copy-start | bytes 1179652
  146.9 11.7 %copy-start.2 = (bf16[4,2,2,64,384]{4,3,2,1,0:T(8,128)(2,1)}, bf16[4,2,2,64,384]{4,3,2,1,0:T(8,128)(2,1)S(1)}, u32[]{:S(2)}) copy-start(bf16[4,2,2,64,384]{4,3,2,1,0:T(8,128)(2,1)S(1)} %collective-permute-done.37.refs_1_) | copy-start | bytes 2359300
  146.9 11.7 %copy-start.17 = (bf16[2,256,384]{2,1,0:T(8,128)(2,1)}, bf16[2,256,384]{2,1,0:T(8,128)(2,1)S(1)}, u32[]{:S(2)}) copy-start(bf16[2,256,384]{2,1,0:T(8,128)(2,1)S(1)} %collective-permute-done.35.refs_6_) | copy-start | bytes 1179652
  146.9 5.1 %collective-permute-start.38 = (bf16[2,256,1536]{2,1,0:T(8,128)(2,1)S(1)}, bf16[2,256,1536]{2,1,0:T(8,128)(2,1)S(1)}, u32[]{:S(2)}, u32[]{:S(2)}) collective-permute-start(bf16[2,256,1536]{2,1,0:T(8,128)(2,1)S(1)} %get-tuple-element.141), channel_id=1, source_target_pairs={{0,8},{8,0},{16,24},{24,16},{1,9},{9,1},{17,25},{25,17},{2,10},{10... | collective-permute-start | bytes 4718600 | tf_op jit(solution)/shard_map/ppermute | solution.py:44
  147.0 20.7 %collective-permute-start.40 = (bf16[2,256,384]{2,1,0:T(8,128)(2,1)S(1)}, bf16[2,256,384]{2,1,0:T(8,128)(2,1)S(1)}, u32[]{:S(2)}, u32[]{:S(2)}) collective-permute-start(bf16[2,256,384]{2,1,0:T(8,128)(2,1)S(1)} %collective-permute-done.35.refs_6_), channel_id=1, source_target_pairs={{0,1},{1,0},{2,3},{3,2},{4,5},{5,4},{6,7},{7,6},{8,9},{9,8},{10,11... | collective-permute-start | bytes 1179656 | tf_op jit(solution)/shard_map/ppermute | solution.py:40
  148.5 20.0 %collective-permute-start.41 = (bf16[2,256,384]{2,1,0:T(8,128)(2,1)S(1)}, bf16[2,256,384]{2,1,0:T(8,128)(2,1)S(1)}, u32[]{:S(2)}, u32[]{:S(2)}) collective-permute-start(bf16[2,256,384]{2,1,0:T(8,128)(2,1)S(1)} %collective-permute-done.35.refs_6_), channel_id=1, source_target_pairs={{0,2},{1,3},{2,4},{3,5},{4,6},{5,7},{6,0},{7,1},{8,10},{9,11},{10,... | collective-permute-start | bytes 1179656 | tf_op jit(solution)/shard_map/ppermute | solution.py:40
  151.0 5.3 %collective-permute-start.43 = (f32[256,2]{1,0:T(8,128)S(1)}, f32[256,2]{1,0:T(8,128)S(1)}, u32[]{:S(2)}, u32[]{:S(2)}) collective-permute-start(f32[256,2]{1,0:T(8,128)S(1)} %add.74), channel_id=1, source_target_pairs={{0,16},{8,24},{16,0},{24,8},{1,17},{9,25},{17,1},{25,9},{2,18},{10... | collective-permute-start | bytes 6152 | tf_op jit(solution)/shard_map/ppermute | solution.py:44
  151.6 15.4 %collective-permute-start.39 = (bf16[2,256,384]{2,1,0:T(8,128)(2,1)S(1)}, bf16[2,256,384]{2,1,0:T(8,128)(2,1)S(1)}, u32[]{:S(2)}, u32[]{:S(2)}) collective-permute-start(bf16[2,256,384]{2,1,0:T(8,128)(2,1)S(1)} %collective-permute-done.34.refs_5_), channel_id=1, source_target_pairs={{0,1},{1,0},{2,3},{3,2},{4,5},{5,4},{6,7},{7,6},{8,9},{9,8},{10,11... | collective-permute-start | bytes 1179656 | tf_op jit(solution)/shard_map/ppermute | solution.py:40
  152.1 17.2 %copy-start.38 = (bf16[2,256,1536]{2,1,0:T(8,128)(2,1)}, bf16[2,256,1536]{2,1,0:T(8,128)(2,1)S(1)}, u32[]{:S(2)}) copy-start(bf16[2,256,1536]{2,1,0:T(8,128)(2,1)S(1)} %collective-permute-done.38) | copy-start | bytes 4718596
  153.2 26.5 %copy-start.12 = (bf16[2,256,384]{2,1,0:T(8,128)(2,1)S(1)}, bf16[2,256,384]{2,1,0:T(8,128)(2,1)}, u32[]{:S(2)}) copy-start(bf16[2,256,384]{2,1,0:T(8,128)(2,1)} %copy-done.11) | copy-start | bytes 1179652
  157.0 11.6 %collective-permute-start.44 = (bf16[256,768]{1,0:T(8,128)(2,1)S(1)}, bf16[256,768]{1,0:T(8,128)(2,1)S(1)}, u32[]{:S(2)}, u32[]{:S(2)}) collective-permute-start(bf16[256,768]{1,0:T(8,128)(2,1)S(1)} %get-tuple-element.154), channel_id=1, source_target_pairs={{0,16},{8,24},{16,0},{24,8},{1,17},{9,25},{17,1},{25,9},{2,18},{10... | collective-permute-start | bytes 1179656 | tf_op jit(solution)/shard_map/ppermute | solution.py:44
  160.1 9.2 %copy-start.36 = (bf16[128,768]{1,0:T(8,128)(2,1)}, bf16[128,768]{1,0:T(8,128)(2,1)S(1)}, u32[]{:S(2)}) copy-start(bf16[128,768]{1,0:T(8,128)(2,1)S(1)} %get-tuple-element.178) | copy-start | bytes 589828
  160.1 8.4 %collective-permute-start.42 = (bf16[128,768]{1,0:T(8,128)(2,1)S(1)}, bf16[128,768]{1,0:T(8,128)(2,1)S(1)}, u32[]{:S(2)}, u32[]{:S(2)}) collective-permute-start(bf16[128,768]{1,0:T(8,128)(2,1)S(1)} %get-tuple-element.149), channel_id=1, source_target_pairs={{0,2},{1,3},{2,4},{3,5},{4,6},{5,7},{6,0},{7,1},{8,10},{9,11},{10,... | collective-permute-start | bytes 589832 | tf_op jit(solution)/shard_map/ppermute | solution.py:40
  169.2 10.4 %collective-permute-start.46 = (bf16[4,2,2,64,384]{4,3,2,1,0:T(8,128)(2,1)S(1)}, bf16[4,2,2,64,384]{4,3,2,1,0:T(8,128)(2,1)}, u32[]{:S(2)}, u32[]{:S(2)}) collective-permute-start(bf16[4,2,2,64,384]{4,3,2,1,0:T(8,128)(2,1)S(1)} %collective-permute-done.36.refs_2_), channel_id=1, source_target_pairs={{0,8},{8,0},{16,24},{24,16},{1,9},{9,1},{17,25},{25,17},{2,10},{10... | collective-permute-start | bytes 2359304 | tf_op jit(solution)/shard_map/ppermute | solution.py:44
  169.4 20.2 %collective-permute-start.45 = (bf16[256,768]{1,0:T(8,128)(2,1)}, bf16[256,768]{1,0:T(8,128)(2,1)}, u32[]{:S(2)}, u32[]{:S(2)}) collective-permute-start(bf16[256,768]{1,0:T(8,128)(2,1)} %get-tuple-element.157), channel_id=1, source_target_pairs={{0,16},{8,24},{16,0},{24,8},{1,17},{9,25},{17,1},{25,9},{2,18},{10... | collective-permute-start | bytes 1179656 | tf_op jit(solution)/shard_map/ppermute | solution.py:44
  173.0 19.2 %collective-permute-start.47 = (bf16[2,256,384]{2,1,0:T(8,128)(2,1)}, bf16[2,256,384]{2,1,0:T(8,128)(2,1)S(1)}, u32[]{:S(2)}, u32[]{:S(2)}) collective-permute-start(bf16[2,256,384]{2,1,0:T(8,128)(2,1)} %copy-done.19), channel_id=1, source_target_pairs={{0,1},{1,0},{2,3},{3,2},{4,5},{5,4},{6,7},{7,6},{8,9},{9,8},{10,11... | collective-permute-start | bytes 1179656 | tf_op jit(solution)/shard_map/ppermute | solution.py:40
  174.7 20.1 %collective-permute-start.48 = (bf16[128,768]{1,0:T(8,128)(2,1)}, bf16[128,768]{1,0:T(8,128)(2,1)S(1)}, u32[]{:S(2)}, u32[]{:S(2)}) collective-permute-start(bf16[128,768]{1,0:T(8,128)(2,1)} %copy-done.37), channel_id=1, source_target_pairs={{0,4},{1,5},{2,6},{3,7},{4,0},{5,1},{6,2},{7,3},{8,12},{9,13},{10,... | collective-permute-start | bytes 589832 | tf_op jit(solution)/shard_map/ppermute | solution.py:40
  176.7 18.1 %collective-permute-start.49 = (bf16[128,768]{1,0:T(8,128)(2,1)}, bf16[128,768]{1,0:T(8,128)(2,1)S(1)}, u32[]{:S(2)}, u32[]{:S(2)}) collective-permute-start(bf16[128,768]{1,0:T(8,128)(2,1)} %copy-done.36), channel_id=1, source_target_pairs={{0,6},{1,7},{2,0},{3,1},{4,2},{5,3},{6,4},{7,5},{8,14},{9,15},{10,... | collective-permute-start | bytes 589832 | tf_op jit(solution)/shard_map/ppermute | solution.py:40
  (32 other events, 78.3 us)
